TPU v7x, 32 devices: a whole 2x2x4 slice. The times are simulated.
32 devices in a mesh: groups: 1, wide: 16 (over z, y, core), mp: 2 (over x), sub: 1.
Axes of the slice: x: 2, y: 2, z: 4, core: 2. Of those that a mesh axis runs over, the one named last changes fastest.
Arguments:
- gate_activation: bfloat16 [512, 28672], P(('groups', 'wide'), ('mp', 'sub')), may hold values from -6 to 6
- up_activation: bfloat16 [512, 28672], P(('groups', 'wide'), ('mp', 'sub')), may hold values from -6 to 6
- down_base_weight: bfloat16 [28672, 8192], P(('mp', 'sub'), 'wide'), may hold values from -0.03125 to 0.03125
- first_factor_table: bfloat16 [16, 64, 28672], P('wide', None, ('mp', 'sub')), may hold values from -0.03125 to 0.03125
- second_factor_table: bfloat16 [16, 64, 8192], P(None, ('mp', 'sub'), 'wide'), may hold values from -0.75 to 0.75
- row_adapter_index: int32 [512, 1], P('groups'), may hold values from 0 to 15; in each aligned block of 32 rows (0 to 31, 32 to 63, ...) at most 2 rows name the same one
- adapter_storage_slot: int32 [16], replicated, may hold values from 0 to 15, each once
Outputs:
- mixed: bfloat16 [512, 8192], P(('groups', 'mp', 'sub'), 'wide')
Inputs may be any that keep to these rules, and one draw needn't show every extreme that they name: `row_adapter_index`: in each aligned block of 32 rows no adapter is named by more than 2 rows; every adapter is named somewhere. `adapter_storage_slot`: each slot once.
All inputs are finite; a program needn't handle non-finite values.
Results may differ from a plain program's by a relative error of at most 0.0055.
Values may be sent and summed in bfloat16 or wider, within the bound.
No kernel may reach another device: no remote copies, remote signals or barrier semaphores. Data moves between devices by JAX's collectives and lax.ppermute only.
A program may use at most 64 MiB of HBM per device.

v0:
```python
import jax
import jax.numpy as jnp
from jax import lax
from jax.sharding import PartitionSpec as P

MOST = 2


def on_device(
    gate_activation,
    up_activation,
    down_base_weight,
    first_factor_table,
    second_factor_table,
    row_adapter_index,
    adapter_storage_slot,
):
    hidden = (
        jax.nn.silu(gate_activation.astype(jnp.float32)) * up_activation.astype(jnp.float32)
    ).astype(jnp.bfloat16)
    row_count = hidden.shape[0]
    owners = lax.axis_size("wide")
    local_adapter = first_factor_table.shape[0]
    adapter_list = local_adapter * owners
    rank_portion = second_factor_table.shape[1]
    width_part = hidden.shape[1]
    home = lax.axis_index("wide")
    ids = row_adapter_index[:, 0]
    table = jnp.arange(adapter_list, dtype=jnp.int32)
    slot_all = jnp.sum(
        jnp.where(ids[:, None] == table[None, :], adapter_storage_slot[None, :], 0), axis=1
    )
    second_factor = second_factor_table.reshape(
        adapter_list * rank_portion, second_factor_table.shape[2]
    )
    own_slots = lax.dynamic_slice_in_dim(slot_all, home * row_count, row_count)
    order = jnp.arange(row_count, dtype=jnp.int32)
    earlier = (own_slots[:, None] == own_slots[None, :]) & (order[None, :] < order[:, None])
    position = jnp.sum(earlier.astype(jnp.int32), axis=1)
    target = own_slots * MOST + position
    outgoing = jnp.zeros((adapter_list * MOST, width_part), jnp.bfloat16).at[target].set(hidden)
    outgoing = outgoing.reshape(adapter_list, MOST, width_part)
    received = lax.all_to_all(outgoing, "wide", split_axis=0, concat_axis=0, tiled=True)
    items = received.shape[1]
    block_list = received.reshape(owners, local_adapter, items, width_part)
    partial_output_value = jnp.einsum(
        "dnle,nqe->dnlq", block_list, first_factor_table, preferred_element_type=jnp.float32
    )
    summed = lax.psum(partial_output_value, ("mp", "sub"))
    lowered = summed.astype(jnp.bfloat16).reshape(owners * local_adapter, items, summed.shape[3])
    returned = lax.all_to_all(lowered, "wide", split_axis=0, concat_axis=0, tiled=True)
    flat = returned.reshape(adapter_list * MOST, returned.shape[2])
    mine = flat[target]
    mine = lax.dynamic_slice_in_dim(
        mine, lax.axis_index(("mp", "sub")) * rank_portion, rank_portion, 1
    )
    base = jnp.dot(
        lax.all_gather(hidden, "wide", axis=0, tiled=True),
        down_base_weight,
        preferred_element_type=jnp.float32,
    )
    low_all = lax.all_gather(mine, "wide", axis=0, tiled=True)
    count = low_all.shape[0]
    picks = (slot_all[:, None] == table[None, :]).astype(jnp.bfloat16)
    spread = (picks[:, :, None] * low_all[:, None, :]).reshape(count, adapter_list * rank_portion)
    total = base + jnp.dot(spread, second_factor, preferred_element_type=jnp.float32)
    return lax.psum_scatter(total, ("mp", "sub"), scatter_dimension=0, tiled=True).astype(
        jnp.bfloat16
    )


def solution(mesh):
    return jax.shard_map(
        on_device,
        mesh=mesh,
        in_specs=(
            P(("groups", "wide"), ("mp", "sub")),
            P(("groups", "wide"), ("mp", "sub")),
            P(("mp", "sub"), "wide"),
            P("wide", None, ("mp", "sub")),
            P(None, ("mp", "sub"), "wide"),
            P("groups", None),
            P(),
        ),
        out_specs=P(("groups", "mp", "sub"), "wide"),
        check_vma=False,
    )
```

profile of v0, /device:TPU:0, one launch (start us, length us, event | category | flops | bytes accessed | tf_op | source)
XLA Modules:
  0.0 190.6 jit_solution(4876248001921240908)
XLA Ops:
  6.5 0.0 copy-start
  6.5 0.0 copy-start.2
  6.5 0.0 copy-start.1
  6.5 0.0 all-gather.2.cloned.1.call-start
  6.5 3.0 %fusion.6 = bf16[32,14336]{1,0:T(8,128)(2,1)} fusion(bf16[32,14336]{1,0:T(8,128)(2,1)} %param.8, bf16[32,14336]{1,0:T(8,128)(2,1)} %param.7), kind=kLoop, calls=%fused_computation.10 | loop fusion | flops 3670016 | bytes 2752512 | tf_op jit(solution)/shard_map/convert_element_type | solution.py:20
  9.6 0.0 all-gather.2.cloned.1.call-update
  9.6 0.0 copy-done.2
  9.6 0.0 copy-done.1
  9.6 0.1 select_reduce_fusion
  9.7 0.1 dynamic_slice.6
  9.8 0.2 convert_reduce_fusion
  10.0 0.1 compare_select_fusion
  10.1 2.7 %scatter_custom_fusion = bf16[32,14336]{1,0:T(8,128)(2,1)S(1)} fusion(s32[32]{0:T(128)S(1)} %compare_select_fusion, bf16[32,14336]{1,0:T(8,128)(2,1)} %fusion.6, bf16[]{:T(256)} %constant.11.clone.1), kind=kCustom, calls=%fused_computation.16 | custom fusion | bytes 918016 | tf_op jit(solution)/shard_map/scatter | solution.py:41
  12.8 1.5 reshape.44
  14.3 7.4 %all-to-all-start = ((bf16[16,2,14336]{2,1,0:T(2,128)(2,1)}), bf16[16,2,14336]{2,1,0:T(2,128)(2,1)S(1)}, u32[]{:S(2)}, u32[]{:S(2)}) async-start(bf16[16,2,14336]{2,1,0:T(2,128)(2,1)} %reshape.44), calls=%async_computation | async-start | bytes 1835008 | tf_op jit(solution)/shard_map/all_to_all | solution.py:43
  21.7 0.0 copy-start.3
  21.7 35.3 %all-to-all-done = bf16[16,2,14336]{2,1,0:T(2,128)(2,1)S(1)} async-done(((bf16[16,2,14336]{2,1,0:T(2,128)(2,1)}), bf16[16,2,14336]{2,1,0:T(2,128)(2,1)S(1)}, u32[]{:S(2)}, u32[]{:S(2)}) %all-to-all-start) | async-done | bytes 917536 | tf_op jit(solution)/shard_map/all_to_all | solution.py:43
  57.0 0.0 copy-done
  57.0 0.6 fusion.7
  57.6 8.2 %psum.7 = bf16[16,1,2,64]{3,0,2,1:T(8,128)(2,1)S(1)} all-reduce(f32[16,1,2,64]{3,0,2,1:T(8,128)S(1)} %fusion.7), channel_id=1, replica_groups=mesh['groups'=1,'wide'=16,'mp'=2,'sub'=1] {'mp','sub'}, use_global_device_ids=true, to_apply=%region_3.4 | all-reduce | flops 2048 | bytes 12288 | tf_op jit(solution)/shard_map/psum | solution.py:49
  65.8 0.6 copy.16
  66.4 15.1 %all-to-all-start.1 = ((bf16[16,2,64]{2,1,0:T(2,128)(2,1)}), bf16[16,2,64]{2,1,0:T(2,128)(2,1)S(1)}, u32[]{:S(2)}, u32[]{:S(2)}) async-start(bf16[16,2,64]{2,1,0:T(2,128)(2,1)} %copy.16), calls=%async_computation.1 | async-start | bytes 16384 | tf_op jit(solution)/shard_map/all_to_all | solution.py:51
  81.5 0.0 reduce-scatter.2.cloned.1.call-start
  81.6 6.4 %all-to-all-done.1 = bf16[16,2,64]{2,1,0:T(2,128)(2,1)S(1)} async-done(((bf16[16,2,64]{2,1,0:T(2,128)(2,1)}), bf16[16,2,64]{2,1,0:T(2,128)(2,1)S(1)}, u32[]{:S(2)}, u32[]{:S(2)}) %all-to-all-start.1) | async-done | bytes 4128 | tf_op jit(solution)/shard_map/all_to_all | solution.py:51
  88.0 0.6 gather_fusion
  88.6 0.1 constant_dynamic-slice_fusion
  88.6 19.3 %all_gather.7 = bf16[512,32]{1,0:T(8,128)(2,1)S(1)} all-gather(bf16[32,32]{1,0:T(8,128)(2,1)S(1)} %constant_dynamic-slice_fusion), channel_id=1, replica_groups=mesh['groups'=1,'wide'=16,'mp'=2,'sub'=1] {'wide'}, dimensions={0}, use_global_device_ids=true | all-gather | bytes 34816 | tf_op jit(solution)/shard_map/all_gather | solution.py:62
  108.0 0.1 copy.17
  108.0 0.0 copy-done.3
  108.1 1.5 convolution_bitcast_fusion
  109.5 37.7 %all-gather.2.cloned.1.call-done = bf16[512,14336]{1,0:T(8,128)(2,1)} async-done(((bf16[32,14336]{1,0:T(8,128)(2,1)}), bf16[512,14336]{1,0:T(8,128)(2,1)}) %all-gather.2.cloned.1.call-update) | async-done | bytes 14680080 | tf_op jit(solution)/shard_map/all_gather | solution.py:58
  147.2 16.2 %convolution_add_fusion = f32[512,512]{1,0:T(8,128)} fusion(f32[512,512]{1,0:T(8,128)} %convolution_bitcast_fusion, bf16[512,14336]{1,0:T(8,128)(2,1)} %all-gather.2.cloned.1.call-done, bf16[14336,512]{1,0:T(8,128)(2,1)} %param.9), kind=kOutput, calls=%fused_computation.11 | convolution fusion | flops 7516454912 | bytes 31457280 | tf_op jit(solution)/shard_map/dot_general | solution.py:57
  163.4 0.0 reduce-scatter.2.cloned.1.call-update
  163.4 18.6 %reduce-scatter.2.cloned.1.call-done = f32[256,512]{1,0:T(8,128)} async-done(((f32[512,512]{1,0:T(8,128)}), f32[256,512]{1,0:T(8,128)}) %reduce-scatter.2.cloned.1.call-update) | async-done | bytes 524304 | tf_op jit(solution)/shard_map/reduce_scatter | solution.py:67
  182.0 1.8 convert_element_type.31
  (2 shorter events, 0.0 us)
Async XLA Ops:
  6.5 50.5 %copy-start = (bf16[1,64,14336]{2,1,0:T(8,128)(2,1)S(1)}, bf16[1,64,14336]{2,1,0:T(8,128)(2,1)}, u32[]{:S(2)}) copy-start(bf16[1,64,14336]{2,1,0:T(8,128)(2,1)} %param.10) | copy-start | bytes 5505028
  6.5 3.1 %copy-start.2 = (s32[16]{0:T(128)S(1)}, s32[16]{0:T(128)}, u32[]{:S(2)}) copy-start(s32[16]{0:T(128)} %param.13) | copy-start | bytes 196
  6.5 3.1 %copy-start.1 = (s32[512,1]{0,1:T(1,128)S(1)}, s32[512,1]{0,1:T(1,128)}, u32[]{:S(2)}) copy-start(s32[512,1]{0,1:T(1,128)} %param.12) | copy-start | bytes 6148
  6.5 140.6 %all-gather.2.cloned.1.call-start = ((), (), s32[]{:S(2)}) async-start(), calls=%async_computation.3 | async-start | bytes 15597568 | tf_op jit(solution)/shard_map/all_gather | solution.py:58
  14.3 42.8 %all-to-all-start = ((bf16[16,2,14336]{2,1,0:T(2,128)(2,1)}), bf16[16,2,14336]{2,1,0:T(2,128)(2,1)S(1)}, u32[]{:S(2)}, u32[]{:S(2)}) async-start(bf16[16,2,14336]{2,1,0:T(2,128)(2,1)} %reshape.44), calls=%async_computation | async-start | bytes 1835008 | tf_op jit(solution)/shard_map/all_to_all | solution.py:43
  21.7 86.4 %copy-start.3 = (bf16[16,32,512]{2,1,0:T(8,128)(2,1)S(1)}, bf16[16,32,512]{2,1,0:T(8,128)(2,1)}, u32[]{:S(2)}) copy-start(bf16[16,32,512]{2,1,0:T(8,128)(2,1)} %param.11) | copy-start | bytes 1572868
  66.4 21.6 %all-to-all-start.1 = ((bf16[16,2,64]{2,1,0:T(2,128)(2,1)}), bf16[16,2,64]{2,1,0:T(2,128)(2,1)S(1)}, u32[]{:S(2)}, u32[]{:S(2)}) async-start(bf16[16,2,64]{2,1,0:T(2,128)(2,1)} %copy.16), calls=%async_computation.1 | async-start | bytes 16384 | tf_op jit(solution)/shard_map/all_to_all | solution.py:51
  81.5 100.5 %reduce-scatter.2.cloned.1.call-start = ((), (), s32[]{:S(2)}) async-start(), calls=%async_computation.4 | async-start | bytes 1572864 | tf_op jit(solution)/shard_map/reduce_scatter | solution.py:67
Sparse Core Ops, SparseCore 0:
  9.7 137.4 all-gather.1
  163.5 18.4 reduce-scatter.1
where the time goes:
time: 191 us
  waiting for transfers between devices  98.1 us (51%)
  blocking collectives  27.5 us (14%)
  starting transfers between devices  22.5 us (12%)
  matrix products  18.3 us (10%)
  between operations  13.5 us (7%)
  local copies, waits for them, and re-layouts  5.65 us (3%)
  other arithmetic  5.18 us (3%)
    all_gather x1, waiting for transfers between devices, on_device(): lax.all_gather(hidden, 'wide', axis=0, tiled=True)  37.7 us
    all_to_all x1, waiting for transfers between devices, on_device(): lax.all_to_all(outgoing, 'wide', split_axis=0, concat_axis=0, tiled=True)  35.3 us
    all_gather x1, blocking collectives, on_device(): low_all = lax.all_gather(mine, 'wide', axis=0, tiled=True)  19.3 us
    reduce_scatter x1, waiting for transfers between devices, on_device(): lax.psum_scatter(total, ('mp', 'sub'), scatter_dimension=0, tiled=True)  18.6 us
    dot_general x1, matrix products, on_device(): jnp.dot(lax.all_gather(hidden, 'wide', axis=0, tiled=True), down_base_wei...  16.2 us
    all_to_all x1, starting transfers between devices, on_device(): lax.all_to_all(lowered, 'wide', split_axis=0, concat_axis=0, tiled=True)  15.1 us
    psum x1, blocking collectives, on_device(): summed = lax.psum(partial_output_value, ('mp', 'sub'))  8.17 us
    all_to_all x1, starting transfers between devices, on_device(): lax.all_to_all(outgoing, 'wide', split_axis=0, concat_axis=0, tiled=True)  7.39 us
  transfers between devices with their start and end apart: 4, of which 4 were waited for; matrix products, arithmetic and copies ran while one was open for 4% of the time, Pallas kernels for 0%

commit v1 on v0

v1 whole, which is shorter than its diff:
```python
import functools

import jax
import jax.numpy as jnp
from jax import lax
from jax.experimental import pallas as pl
from jax.experimental.pallas import tpu as pltpu
from jax.sharding import PartitionSpec as P

MOST = 2
CHUNKS = 2
INNER = ("mp", "sub")


def tile_of(depth, most=1792):
    parts = 1
    while depth % parts or (depth // parts) % 128 or depth // parts > most:
        parts += 1
    return depth // parts


def rows_kernel(per_chunk, tiles, *refs):
    count = CHUNKS * per_chunk
    pieces, (weight, first, base, low) = refs[:count], refs[count:]
    step = pl.program_id(0)

    @pl.when(step == 0)
    def _():
        base[...] = jnp.zeros_like(base)
        low[...] = jnp.zeros_like(low)

    for chunk in range(CHUNKS):

        @pl.when(step // tiles == chunk)
        def _():
            held = pieces[chunk * per_chunk : (chunk + 1) * per_chunk]
            rows = jnp.concatenate([piece[...] for piece in held], axis=0)
            base[...] += jnp.dot(rows, weight[...], preferred_element_type=jnp.float32)
            low[...] += lax.dot_general(
                rows, first[...], (((1,), (1,)), ((), ())), preferred_element_type=jnp.float32
            )


def rows_product(pieces, weight, first):
    per_chunk = len(pieces[0])
    row_count, depth = pieces[0][0].shape
    tile = tile_of(depth)
    tiles = depth // tile
    total = per_chunk * row_count
    width, rank = weight.shape[1], first.shape[0]
    specs = []
    for chunk in range(CHUNKS):
        for _ in range(per_chunk):
            specs.append(
                pl.BlockSpec(
                    (row_count, tile),
                    lambda i, chunk=chunk: (0, jnp.clip(i - chunk * tiles, 0, tiles - 1)),
                )
            )
    specs.append(pl.BlockSpec((tile, width), lambda i: (i, 0)))
    specs.append(pl.BlockSpec((rank, tile), lambda i: (0, i)))
    return pl.pallas_call(
        functools.partial(rows_kernel, per_chunk, tiles),
        grid=(CHUNKS * tiles,),
        in_specs=specs,
        out_specs=[
            pl.BlockSpec((total, width), lambda i: (0, 0)),
            pl.BlockSpec((total, rank), lambda i: (0, 0)),
        ],
        out_shape=[
            jax.ShapeDtypeStruct((total, width), jnp.float32),
            jax.ShapeDtypeStruct((total, rank), jnp.float32),
        ],
        compiler_params=pltpu.CompilerParams(vmem_limit_bytes=24 * 2**20),
        cost_estimate=pl.CostEstimate(
            flops=2 * total * depth * CHUNKS * (width + rank),
            bytes_accessed=2 * depth * CHUNKS * (width + rank + total),
            transcendentals=0,
        ),
    )(*pieces[0], *pieces[1], weight, first)


def ring_order(nodes, lanes):
    if lanes == 1:
        return list(range(nodes))
    return list(range(0, nodes, 2)) + list(range(nodes - 1, 0, -2))


def on_device(
    gate_activation,
    up_activation,
    down_base_weight,
    first_factor_table,
    second_factor_table,
    row_adapter_index,
    adapter_storage_slot,
):
    f32, bf16 = jnp.float32, jnp.bfloat16
    row_count, width_part = gate_activation.shape
    owners = lax.axis_size("wide")
    inner = lax.axis_size(INNER)
    slots = first_factor_table.shape[0] * owners
    lanes = 2 if lax.axis_size("sub") == 1 and owners % 4 == 0 else 1
    nodes = owners // lanes
    order = ring_order(nodes, lanes)
    place = [order.index(node) for node in range(nodes)]
    steps = (nodes - 1) // 2
    far = nodes // 2

    home = lax.axis_index("wide")
    lane = home % lanes
    my_place = jnp.asarray(place, jnp.int32)[home // lanes]
    part = lax.axis_index(INNER)

    def moved(shift, cross=False):
        return [
            (order[p] * lanes + c, order[(p + shift) % nodes] * lanes + (c ^ int(cross)))
            for p in range(nodes)
            for c in range(lanes)
        ]

    def node_at(shift):
        return jnp.asarray(order, jnp.int32)[(my_place + shift) % nodes]

    def sibling(piece):
        return lax.ppermute(piece, "wide", moved(0, True))

    def both(piece):
        return [piece, sibling(piece)] if lanes == 2 else [piece]

    ids = row_adapter_index[:, 0]
    names = jnp.arange(slots, dtype=jnp.int32)
    slot_all = jnp.sum(
        jnp.where(ids[:, None] == names[None, :], adapter_storage_slot[None, :], 0), axis=1
    ).reshape(owners, row_count)
    ranks = jnp.arange(row_count, dtype=jnp.int32)
    earlier = (slot_all[:, :, None] == slot_all[:, None, :]) & (ranks[None, :] < ranks[:, None])[None]
    position = jnp.sum(earlier.astype(jnp.int32), axis=2)

    depth = width_part // CHUNKS
    hidden = []
    for chunk in range(CHUNKS):
        gate = gate_activation[:, chunk * depth : (chunk + 1) * depth].astype(f32)
        up = up_activation[:, chunk * depth : (chunk + 1) * depth].astype(f32)
        hidden.append((jax.nn.silu(gate) * up).astype(bf16))

    first = first_factor_table[0]

    my_slot = lax.dynamic_index_in_dim(slot_all, home, 0, keepdims=False)
    my_position = lax.dynamic_index_in_dim(position, home, 0, keepdims=False)
    far_rows = []
    for cross in range(lanes):
        target = node_at(far) * lanes + (lane ^ cross)
        pick = (my_slot[None, :] == target) & (my_position[None, :] == jnp.arange(MOST)[:, None])
        sent = jnp.concatenate(
            [
                jnp.dot(pick.astype(bf16), block, preferred_element_type=f32).astype(bf16)
                for block in hidden
            ],
            axis=1,
        )
        far_rows.append(lax.ppermute(sent, "wide", moved(far, bool(cross))))

    right, left = list(hidden), list(hidden)
    groups = [(0, [both(block) for block in hidden])]
    for step in range(1, steps + 1):
        right = [lax.ppermute(block, "wide", moved(1)) for block in right]
        left = [lax.ppermute(block, "wide", moved(-1)) for block in left]
        groups.append((step, [both(r) + both(l) for r, l in zip(right, left)]))
    last = [
        lax.ppermute(right[0], "wide", moved(1)),
        lax.ppermute(left[1], "wide", moved(-1)),
    ]
    groups.append((far, [both(block) for block in last]))

    base, low, where = {}, [], []
    for step, pieces in groups:
        total, lowered = rows_product(pieces, down_base_weight, first)
        total = total.reshape(-1, lanes * row_count, total.shape[1])
        shifts = [step] if step in (0, far) else [-step, step]
        for index, shift in enumerate(shifts):
            base[shift % nodes] = total[index]
        if step != far:
            low.append(lowered)
            for shift in shifts:
                where += [node_at(shift) * lanes + (lane ^ c) for c in range(lanes)]
    far_where = [node_at(far) * lanes + (lane ^ c) for c in range(lanes)]
    low.append(
        lax.dot_general(
            jnp.concatenate(far_rows, axis=0),
            first,
            (((1,), (1,)), ((), ())),
            preferred_element_type=f32,
        )
    )
    low = jnp.concatenate(low, axis=0)

    blocks = jnp.arange(owners, dtype=jnp.int32)
    items = jnp.arange(MOST, dtype=jnp.int32)
    where = jnp.stack(where)
    chosen = (
        (where[None, None, :, None] == blocks[:, None, None, None])
        & (slot_all == home)[:, None, None, :]
        & (position[:, None, None, :] == items[None, :, None, None])
    ).reshape(owners * MOST, -1)
    far_chosen = (
        (jnp.stack(far_where)[None, None, :, None] == blocks[:, None, None, None])
        & (items[:, None] == items[None, :])[None, :, None, :]
    ).reshape(owners * MOST, -1)
    chosen = jnp.concatenate([chosen, far_chosen], axis=1).astype(f32)
    low = jnp.dot(chosen, low, precision=lax.Precision.HIGHEST)

    half = owners * MOST // inner
    if inner == 2:
        kept = jnp.where(part == 0, low[:half], low[half:])
        sent = jnp.where(part == 0, low[half:], low[:half])
        low = kept + lax.ppermute(sent, INNER, [(0, 1), (1, 0)])
    else:
        low = lax.psum_scatter(low, INNER, scatter_dimension=0, tiled=True)
    low = low.astype(bf16)[None]
    if owners & (owners - 1) == 0:
        gap = 1
        while gap < owners:
            other = lax.ppermute(low, "wide", [(w, w ^ gap) for w in range(owners)])
            low = jnp.where(
                home & gap == 0,
                jnp.concatenate([low, other], axis=0),
                jnp.concatenate([other, low], axis=0),
            )
            gap *= 2
    else:
        low = lax.all_gather(low, "wide", axis=0, tiled=True)
    own_blocks = owners // inner
    low = low.reshape(slots, own_blocks, MOST, -1)

    if inner == 2:
        other = lax.ppermute(second_factor_table, INNER, [(0, 1), (1, 0)])
        second = jnp.where(
            part == 0,
            jnp.concatenate([second_factor_table, other], axis=1),
            jnp.concatenate([other, second_factor_table], axis=1),
        )
    else:
        second = lax.all_gather(second_factor_table, INNER, axis=1, tiled=True)
    width = second.shape[2]
    own_slot = lax.dynamic_slice_in_dim(slot_all, part * own_blocks, own_blocks)
    own_position = lax.dynamic_slice_in_dim(position, part * own_blocks, own_blocks)
    spread = 0
    for item in range(MOST):
        mask = (own_slot[:, :, None] == names) & (own_position == item)[:, :, None]
        spread += jnp.where(mask[..., None], jnp.swapaxes(low[:, :, item], 0, 1)[:, None], 0)
    delta = jnp.dot(
        spread.reshape(own_blocks * row_count, -1).astype(bf16),
        second.reshape(-1, width),
        preferred_element_type=f32,
    )

    half_nodes = nodes // inner if nodes % inner == 0 else 0
    opposite = (
        inner == 2
        and nodes % 2 == 0
        and all((order[p] < half_nodes) != (order[(p + far) % nodes] < half_nodes) for p in range(nodes))
    )
    group_rows = lanes * row_count
    if opposite:
        sums, targets = [], []
        for shift in range(far):
            mine = node_at(shift) // half_nodes == part
            kept = jnp.where(mine, base[shift], base[shift + far])
            sent = jnp.where(mine, base[shift + far], base[shift])
            sums.append(kept + lax.ppermute(sent, INNER, [(0, 1), (1, 0)]))
            targets.append(jnp.where(mine, node_at(shift), node_at(shift + far)) % half_nodes)
    else:
        sums = [base[shift] for shift in range(nodes)]
        targets = [node_at(shift) for shift in range(nodes)]
    out = []
    for index in range(len(sums)):
        rows = sums[0]
        for target, value in zip(targets[1:], sums[1:]):
            rows = jnp.where(target == index, value, rows)
        out.append(rows)
    out = jnp.stack(out).reshape(-1, lanes, row_count, width)
    if lanes == 2:
        out = jnp.where(lane == 0, out, out[:, ::-1])
    out = out.reshape(-1, width)
    if not opposite:
        out = lax.psum_scatter(out, INNER, scatter_dimension=0, tiled=True)
    return (out + delta).astype(bf16)


def solution(mesh):
    return jax.shard_map(
        on_device,
        mesh=mesh,
        in_specs=(
            P(("groups", "wide"), ("mp", "sub")),
            P(("groups", "wide"), ("mp", "sub")),
            P(("mp", "sub"), "wide"),
            P("wide", None, ("mp", "sub")),
            P(None, ("mp", "sub"), "wide"),
            P("groups", None),
            P(),
        ),
        out_specs=P(("groups", "mp", "sub"), "wide"),
        check_vma=False,
    )
```

time: 191 us -> 161 us (0.84)
  waiting for transfers between devices: 98.1 us -> 34.9 us
  Pallas kernels: 0 us -> 33.5 us
  blocking collectives: 27.5 us -> 0 us
  starting transfers between devices: 22.5 us -> 39 us
  matrix products: 18.3 us -> 2.66 us
  between operations: 13.5 us -> 28.3 us
  local copies, waits for them, and re-layouts: 5.65 us -> 11.9 us
  other arithmetic: 5.18 us -> 9.47 us
    all_to_all x2 -> x0, waiting for transfers between devices: 41.7 us -> none  [the longest x1 35.3 us: on_device(): lax.all_to_all(outgoing, 'wide', split_axis=0, concat_axis=0, tiled=True)]
    ppermute x0 -> x42, starting transfers between devices: none -> 39 us  [the longest x6 11.9 us: on_device(): right = [lax.ppermute(block, 'wide', moved(1)) for block in right]]
    all_gather x1 -> x0, waiting for transfers between devices: 37.7 us -> none  [on_device(): lax.all_gather(hidden, 'wide', axis=0, tiled=True)]
    ppermute x0 -> x42, waiting for transfers between devices: none -> 34.9 us  [the longest x1 9.08 us: on_device(): other = lax.ppermute(second_factor_table, INNER, [(0, 1), (1, 0)])]
    pallas_call x0 -> x5, Pallas kernels: none -> 33.5 us  [rows_product(): pl.pallas_call(functools.partial(rows_kernel, per_chunk, tiles), grid=(CH...]
    all_to_all x2 -> x0, starting transfers between devices: 22.5 us -> none  [the longest x1 15.1 us: on_device(): lax.all_to_all(lowered, 'wide', split_axis=0, concat_axis=0, tiled=True)]
    all_gather x1 -> x0, blocking collectives: 19.3 us -> none  [on_device(): low_all = lax.all_gather(mine, 'wide', axis=0, tiled=True)]
    reduce_scatter x1 -> x0, waiting for transfers between devices: 18.6 us -> none  [on_device(): lax.psum_scatter(total, ('mp', 'sub'), scatter_dimension=0, tiled=True)]
  transfers between devices with their start and end apart: 4 -> 42, of which waited for: 4 -> 9; matrix products, arithmetic and copies ran while one was open for 4% -> 6% of each run, Pallas kernels for 0% -> 21%
where the time goes in v1:
time: 161 us; the launch traced here: 160 us
  starting transfers between devices  39 us (24%)
  waiting for transfers between devices  34.9 us (22%)
  Pallas kernels  33.5 us (21%)
  between operations  28.3 us (18%)
  local copies, waits for them, and re-layouts  11.9 us (7%)
  other arithmetic  9.47 us (6%)
  matrix products  2.66 us (2%)
    pallas_call x5, Pallas kernels, rows_product(): pl.pallas_call(functools.partial(rows_kernel, per_chunk, tiles), grid=(CH...  33.5 us
    ppermute x6, starting transfers between devices, on_device(): right = [lax.ppermute(block, 'wide', moved(1)) for block in right]  11.9 us
    unnamed x44, local copies, waits for them, and re-layouts  9.36 us
    ppermute x1, waiting for transfers between devices, on_device(): other = lax.ppermute(second_factor_table, INNER, [(0, 1), (1, 0)])  9.08 us
    ppermute x6, waiting for transfers between devices, on_device(): right = [lax.ppermute(block, 'wide', moved(1)) for block in right]  8.73 us
    ppermute x1, waiting for transfers between devices, on_device(): lax.ppermute(right[0], 'wide', moved(1))  8.19 us
    ppermute x4, starting transfers between devices, on_device(): other = lax.ppermute(low, 'wide', [(w, w ^ gap) for w in range(owners)])  6.44 us
    ppermute x4, waiting for transfers between devices, on_device(): other = lax.ppermute(low, 'wide', [(w, w ^ gap) for w in range(owners)])  5.99 us
  transfers between devices with their start and end apart: 42, of which 9 were waited for; matrix products, arithmetic and copies ran while one was open for 6% of the time, Pallas kernels for 21%

profile of v1, /device:TPU:0, one launch (start us, length us, event | category | flops | bytes accessed | tf_op | source)
XLA Modules:
  0.0 159.8 jit_solution(4555805128502079836)
XLA Ops:
  0.0 2.0 %fusion.9 = (bf16[32,7168]{1,0:T(8,128)(2,1)S(1)}, bf16[32,7168]{1,0:T(8,128)(2,1)S(1)}) fusion(bf16[32,14336]{1,0:T(8,128)(2,1)} %param.37, bf16[32,14336]{1,0:T(8,128)(2,1)} %param.36), kind=kLoop, calls=%fused_computation.21 | loop fusion | flops 3670016 | bytes 2752512 | tf_op jit(solution)/shard_map/convert_element_type | solution.py:145
  2.0 3.1 %collective-permute-start = (bf16[32,7168]{1,0:T(8,128)(2,1)S(1)}, bf16[32,7168]{1,0:T(8,128)(2,1)S(1)}, u32[]{:S(2)}, u32[]{:S(2)}) collective-permute-start(bf16[32,7168]{1,0:T(8,128)(2,1)S(1)} %get-tuple-element.29.refs_0_), channel_id=1, source_target_pairs={{0,8},{2,10},{8,16},{10,18},{16,24},{18,26},{24,28},{26,30},{28,20... | collective-permute-start | bytes 1376264 | tf_op jit(solution)/shard_map/ppermute | solution.py:167
  5.1 2.0 %collective-permute-start.8 = (bf16[32,7168]{1,0:T(8,128)(2,1)S(1)}, bf16[32,7168]{1,0:T(8,128)(2,1)}, u32[]{:S(2)}, u32[]{:S(2)}) collective-permute-start(bf16[32,7168]{1,0:T(8,128)(2,1)S(1)} %get-tuple-element.28.refs_2_), channel_id=1, source_target_pairs={{0,8},{2,10},{8,16},{10,18},{16,24},{18,26},{24,28},{26,30},{28,20... | collective-permute-start | bytes 1376264 | tf_op jit(solution)/shard_map/ppermute | solution.py:167
  7.2 0.6 dynamic_slice.100
  16.5 0.7 fusion.36
  23.9 0.6 collective-permute-start.28
  24.5 1.9 %collective-permute-start.41 = (bf16[16,32,512]{2,1,0:T(8,128)(2,1)}, bf16[16,32,512]{2,1,0:T(8,128)(2,1)}, u32[]{:S(2)}, u32[]{:S(2)}) collective-permute-start(bf16[16,32,512]{2,1,0:T(8,128)(2,1)} %param.40), channel_id=1, source_target_pairs={{0,1},{1,0},{2,3},{3,2},{4,5},{5,4},{6,7},{7,6},{8,9},{9,8},{10,11... | collective-permute-start | bytes 1572872 | tf_op jit(solution)/shard_map/ppermute | solution.py:237
  27.0 1.6 collective-permute-start.1
  28.6 0.8 copy-done.2
  29.8 9.1 %collective-permute-done.41 = bf16[16,32,512]{2,1,0:T(8,128)(2,1)} collective-permute-done((bf16[16,32,512]{2,1,0:T(8,128)(2,1)}, bf16[16,32,512]{2,1,0:T(8,128)(2,1)}, u32[]{:S(2)}, u32[]{:S(2)}) %collective-permute-start.41) | collective-permute-done | bytes 524320 | tf_op jit(solution)/shard_map/ppermute | solution.py:237
  39.0 1.9 %collective-permute-start.9 = (bf16[32,7168]{1,0:T(8,128)(2,1)}, bf16[32,7168]{1,0:T(8,128)(2,1)}, u32[]{:S(2)}, u32[]{:S(2)}) collective-permute-start(bf16[32,7168]{1,0:T(8,128)(2,1)} %collective-permute-done.8.refs_4_), channel_id=1, source_target_pairs={{0,8},{2,10},{8,16},{10,18},{16,24},{18,26},{24,28},{26,30},{28,20... | collective-permute-start | bytes 1376264 | tf_op jit(solution)/shard_map/ppermute | solution.py:167
  41.2 1.7 %collective-permute-start.13 = (bf16[32,7168]{1,0:T(8,128)(2,1)}, bf16[32,7168]{1,0:T(8,128)(2,1)}, u32[]{:S(2)}, u32[]{:S(2)}) collective-permute-start(bf16[32,7168]{1,0:T(8,128)(2,1)} %collective-permute-done.12.refs_6_), channel_id=1, source_target_pairs={{0,4},{2,6},{8,0},{10,2},{16,8},{18,10},{24,16},{26,18},{28,24},{3... | collective-permute-start | bytes 1376264 | tf_op jit(solution)/shard_map/ppermute | solution.py:168
  43.6 8.7 %collective-permute-done.9.refs_4_ = bf16[32,7168]{1,0:T(8,128)(2,1)} collective-permute-done((bf16[32,7168]{1,0:T(8,128)(2,1)}, bf16[32,7168]{1,0:T(8,128)(2,1)}, u32[]{:S(2)}, u32[]{:S(2)}) %collective-permute-start.9) | collective-permute-done | bytes 458784 | tf_op jit(solution)/shard_map/ppermute | solution.py:167
  52.4 0.8 copy-done.6
  53.2 1.8 %collective-permute-start.2 = (bf16[32,7168]{1,0:T(8,128)(2,1)}, bf16[32,7168]{1,0:T(8,128)(2,1)}, u32[]{:S(2)}, u32[]{:S(2)}) collective-permute-start(bf16[32,7168]{1,0:T(8,128)(2,1)} %collective-permute-done.1.refs_0_), channel_id=1, source_target_pairs={{0,8},{2,10},{8,16},{10,18},{16,24},{18,26},{24,28},{26,30},{28,20... | collective-permute-start | bytes 1376264 | tf_op jit(solution)/shard_map/ppermute | solution.py:167
  55.0 1.6 collective-permute-start.10
  56.6 0.8 copy-done.4
  57.8 0.8 copy-done.8
  58.6 0.7 collective-permute-start.14
  73.6 5.2 %copy-done = bf16[14336,512]{1,0:T(8,128)(2,1)S(1)} copy-done((bf16[14336,512]{1,0:T(8,128)(2,1)S(1)}, bf16[14336,512]{1,0:T(8,128)(2,1)}, u32[]{:S(2)}) %copy-start) | copy-done | bytes 14680088
  78.8 1.0 copy-done.3
  79.8 5.9 %shard_map.337 = (f32[64,512]{1,0:T(8,128)S(1)}, f32[64,64]{1,0:T(8,128)S(1)}) custom-call(bf16[32,7168]{1,0:T(8,128)(2,1)S(1)} %get-tuple-element.29.refs_0_, bf16[32,7168]{1,0:T(8,128)(2,1)} %collective-permute-done.27.refs_1_, bf16[32,7168]{1,0:T(8,128)(2,1)S(1)} %get-tuple-element.28.refs_2_, bf16[32,7168]{1,0:T(8,128)(2,1)S(1)} %copy-done.3, ...), custom_call_target="tpu_custom_call" | custom-call | flops 1056964608 | bytes 18350080 | tf_op jit(solution)/shard_map/pallas_call | solution.py:62
  85.8 2.6 %maximum_select_fusion = bf16[16,64,512]{2,1,0:T(8,128)(2,1)} fusion(bf16[16,32,512]{2,1,0:T(8,128)(2,1)} %collective-permute-done.41, bf16[16,32,512]{2,1,0:T(8,128)(2,1)S(1)} %copy-done.11, pred[]{:T(512)S(6)} %eq.316), kind=kLoop, calls=%fused_computation.11 | loop fusion | flops 4718592 | bytes 2097153 | tf_op jit(solution)/shard_map/jit(_where)/select_n | solution.py:238
  89.6 7.2 %shard_map.335 = (f32[128,512]{1,0:T(8,128)S(1)}, f32[128,64]{1,0:T(8,128)S(1)}) custom-call(bf16[32,7168]{1,0:T(8,128)(2,1)S(1)} %collective-permute-done.refs_0_, bf16[32,7168]{1,0:T(8,128)(2,1)} %collective-permute-done.16.refs_1_, bf16[32,7168]{1,0:T(8,128)(2,1)} %collective-permute-done.4.refs_2_, bf16[32,7168]{1,0:T(8,128)(2,1)} %collective-permute-done.17.refs_3_, ...), custom_call_target="tpu_custom_call" | custom-call | flops 2113929216 | bytes 20185088 | tf_op jit(solution)/shard_map/pallas_call | solution.py:62
  96.8 4.4 %collective-permute-start.34 = (bf16[2,14336]{1,0:T(2,128)(2,1)S(1)}, bf16[2,14336]{1,0:T(2,128)(2,1)S(1)}, u32[]{:S(2)}, u32[]{:S(2)}) collective-permute-start(bf16[2,14336]{1,0:T(2,128)(2,1)S(1)} %pad_maximum_fusion.1), channel_id=1, source_target_pairs={{0,28},{2,30},{8,20},{10,22},{16,12},{18,14},{24,4},{26,6},{28,0},... | collective-permute-start | bytes 172040 | tf_op jit(solution)/shard_map/ppermute | solution.py:162
  101.2 7.9 %shard_map.336 = (f32[128,512]{1,0:T(8,128)S(1)}, f32[128,64]{1,0:T(8,128)S(1)}) custom-call(bf16[32,7168]{1,0:T(8,128)(2,1)} %collective-permute-done.1.refs_0_, bf16[32,7168]{1,0:T(8,128)(2,1)S(1)} %copy-done.5, bf16[32,7168]{1,0:T(8,128)(2,1)} %collective-permute-done.5.refs_2_, bf16[32,7168]{1,0:T(8,128)(2,1)S(1)} %copy-done.9, ...), custom_call_target="tpu_custom_call" | custom-call | flops 2113929216 | bytes 20185088 | tf_op jit(solution)/shard_map/pallas_call | solution.py:62
  109.4 7.1 %shard_map.334 = (f32[128,512]{1,0:T(8,128)S(1)}, f32[128,64]{1,0:T(8,128)S(1)}) custom-call(bf16[32,7168]{1,0:T(8,128)(2,1)} %collective-permute-done.2.refs_0_, bf16[32,7168]{1,0:T(8,128)(2,1)S(1)} %collective-permute-done.3.refs_1_, bf16[32,7168]{1,0:T(8,128)(2,1)} %collective-permute-done.6.refs_2_, bf16[32,7168]{1,0:T(8,128)(2,1)S(1)} %collective-permute-done.7.refs_3_, ...), custom_call_target="tpu_custom_call" | custom-call | flops 2113929216 | bytes 20185088 | tf_op jit(solution)/shard_map/pallas_call | solution.py:62
  116.6 0.6 convolution_dynamic-update-slice_fusion
  117.4 1.6 collective-permute-start.36
  119.0 0.6 collective-permute-start.25
  119.6 2.0 %collective-permute-start.31 = (bf16[32,7168]{1,0:T(8,128)(2,1)}, bf16[32,7168]{1,0:T(8,128)(2,1)S(1)}, u32[]{:S(2)}, u32[]{:S(2)}) collective-permute-start(bf16[32,7168]{1,0:T(8,128)(2,1)} %collective-permute-done.14.refs_6_), channel_id=1, source_target_pairs={{0,4},{2,6},{8,0},{10,2},{16,8},{18,10},{24,16},{26,18},{28,24},{3... | collective-permute-start | bytes 1376264 | tf_op jit(solution)/shard_map/ppermute | solution.py:172
  121.7 0.7 slice_select_fusion.2
  122.4 1.5 collective-permute-start.20
  123.9 8.2 %collective-permute-done.29.refs_0_ = bf16[32,7168]{1,0:T(8,128)(2,1)S(1)} collective-permute-done((bf16[32,7168]{1,0:T(8,128)(2,1)}, bf16[32,7168]{1,0:T(8,128)(2,1)S(1)}, u32[]{:S(2)}, u32[]{:S(2)}) %collective-permute-start.29) | collective-permute-done | bytes 458784 | tf_op jit(solution)/shard_map/ppermute | solution.py:171
  132.7 1.7 %collective-permute-start.38 = (bf16[2,16,64]{2,1,0:T(8,128)(2,1)S(1)}, bf16[2,16,64]{2,1,0:T(8,128)(2,1)S(1)}, u32[]{:S(2)}, u32[]{:S(2)}) collective-permute-start(bf16[2,16,64]{2,1,0:T(8,128)(2,1)S(1)} %maximum_select_fusion.7), channel_id=1, source_target_pairs={{0,4},{2,6},{4,0},{6,2},{8,12},{10,14},{12,8},{14,10},{16,20},{18,... | collective-permute-start | bytes 12296 | tf_op jit(solution)/shard_map/ppermute | solution.py:224
  134.3 2.0 %collective-permute-done.38 = bf16[2,16,64]{2,1,0:T(8,128)(2,1)S(1)} collective-permute-done((bf16[2,16,64]{2,1,0:T(8,128)(2,1)S(1)}, bf16[2,16,64]{2,1,0:T(8,128)(2,1)S(1)}, u32[]{:S(2)}, u32[]{:S(2)}) %collective-permute-start.38) | collective-permute-done | bytes 4128 | tf_op jit(solution)/shard_map/ppermute | solution.py:224
  136.4 1.8 %collective-permute-start.39 = (bf16[4,16,64]{2,1,0:T(8,128)(2,1)S(1)}, bf16[4,16,64]{2,1,0:T(8,128)(2,1)S(1)}, u32[]{:S(2)}, u32[]{:S(2)}) collective-permute-start(bf16[4,16,64]{2,1,0:T(8,128)(2,1)S(1)} %maximum_select_fusion.5), channel_id=1, source_target_pairs={{0,8},{2,10},{4,12},{6,14},{8,0},{10,2},{12,4},{14,6},{16,24},{18,... | collective-permute-start | bytes 24584 | tf_op jit(solution)/shard_map/ppermute | solution.py:224
  138.2 2.0 %collective-permute-done.39 = bf16[4,16,64]{2,1,0:T(8,128)(2,1)S(1)} collective-permute-done((bf16[4,16,64]{2,1,0:T(8,128)(2,1)S(1)}, bf16[4,16,64]{2,1,0:T(8,128)(2,1)S(1)}, u32[]{:S(2)}, u32[]{:S(2)}) %collective-permute-start.39) | collective-permute-done | bytes 8224 | tf_op jit(solution)/shard_map/ppermute | solution.py:224
  140.2 2.9 %collective-permute-start.40 = (bf16[8,16,64]{2,1,0:T(8,128)(2,1)S(1)}, bf16[8,16,64]{2,1,0:T(8,128)(2,1)S(1)}, u32[]{:S(2)}, u32[]{:S(2)}) collective-permute-start(bf16[8,16,64]{2,1,0:T(8,128)(2,1)S(1)} %maximum_select_fusion.3), channel_id=1, source_target_pairs={{0,16},{2,18},{4,20},{6,22},{8,24},{10,26},{12,28},{14,30},{16,0},... | collective-permute-start | bytes 49160 | tf_op jit(solution)/shard_map/ppermute | solution.py:224
  143.2 1.9 %collective-permute-done.40 = bf16[8,16,64]{2,1,0:T(8,128)(2,1)S(1)} collective-permute-done((bf16[8,16,64]{2,1,0:T(8,128)(2,1)S(1)}, bf16[8,16,64]{2,1,0:T(8,128)(2,1)S(1)}, u32[]{:S(2)}, u32[]{:S(2)}) %collective-permute-start.40) | collective-permute-done | bytes 16416 | tf_op jit(solution)/shard_map/ppermute | solution.py:224
  145.1 1.5 collective-permute-start.26
  146.8 5.4 %shard_map.338 = (f32[64,512]{1,0:T(8,128)S(1)}, f32[64,64]{1,0:T(8,128)}) custom-call(bf16[32,7168]{1,0:T(8,128)(2,1)S(1)} %collective-permute-done.29.refs_0_, bf16[32,7168]{1,0:T(8,128)(2,1)S(1)} %collective-permute-done.30.refs_1_, bf16[32,7168]{1,0:T(8,128)(2,1)S(1)} %collective-permute-done.31.refs_2_, ...), custom_call_target="tpu_custom_call" | custom-call | flops 1056964608 | bytes 18350080 | tf_op jit(solution)/shard_map/pallas_call | solution.py:62
  152.2 0.6 collective-permute-start.33
  152.7 1.4 select_add_fusion
  154.1 0.7 add.333
  154.9 2.3 %collective-permute-done.33 = f32[64,512]{1,0:T(8,128)S(1)} collective-permute-done((f32[64,512]{1,0:T(8,128)S(1)}, f32[64,512]{1,0:T(8,128)S(1)}, u32[]{:S(2)}, u32[]{:S(2)}) %collective-permute-start.33) | collective-permute-done | bytes 131104 | tf_op jit(solution)/shard_map/ppermute | solution.py:271
  157.2 1.2 select_select_fusion.3
  158.6 1.1 fusion
  (147 shorter events, 7.4 us)
Async XLA Ops:
  0.0 17.8 %copy-start.14 = (s32[16]{0:T(128)S(1)}, s32[16]{0:T(128)}, u32[]{:S(2)}) copy-start(s32[16]{0:T(128)} %param.42) | copy-start | bytes 196
  2.0 71.5 %copy-start.1 = (bf16[1,64,14336]{2,1,0:T(8,128)(2,1)S(1)}, bf16[1,64,14336]{2,1,0:T(8,128)(2,1)}, u32[]{:S(2)}) copy-start(bf16[1,64,14336]{2,1,0:T(8,128)(2,1)} %param.39) | copy-start | bytes 5505028
  2.0 21.9 %collective-permute-start = (bf16[32,7168]{1,0:T(8,128)(2,1)S(1)}, bf16[32,7168]{1,0:T(8,128)(2,1)S(1)}, u32[]{:S(2)}, u32[]{:S(2)}) collective-permute-start(bf16[32,7168]{1,0:T(8,128)(2,1)S(1)} %get-tuple-element.29.refs_0_), channel_id=1, source_target_pairs={{0,8},{2,10},{8,16},{10,18},{16,24},{18,26},{24,28},{26,30},{28,20... | collective-permute-start | bytes 1376264 | tf_op jit(solution)/shard_map/ppermute | solution.py:167
  5.1 19.4 %collective-permute-start.4 = (bf16[32,7168]{1,0:T(8,128)(2,1)S(1)}, bf16[32,7168]{1,0:T(8,128)(2,1)}, u32[]{:S(2)}, u32[]{:S(2)}) collective-permute-start(bf16[32,7168]{1,0:T(8,128)(2,1)S(1)} %get-tuple-element.29.refs_0_), channel_id=1, source_target_pairs={{0,4},{2,6},{8,0},{10,2},{16,8},{18,10},{24,16},{26,18},{28,24},{3... | collective-permute-start | bytes 1376264 | tf_op jit(solution)/shard_map/ppermute | solution.py:168
  5.1 21.3 %collective-permute-start.8 = (bf16[32,7168]{1,0:T(8,128)(2,1)S(1)}, bf16[32,7168]{1,0:T(8,128)(2,1)}, u32[]{:S(2)}, u32[]{:S(2)}) collective-permute-start(bf16[32,7168]{1,0:T(8,128)(2,1)S(1)} %get-tuple-element.28.refs_2_), channel_id=1, source_target_pairs={{0,8},{2,10},{8,16},{10,18},{16,24},{18,26},{24,28},{26,30},{28,20... | collective-permute-start | bytes 1376264 | tf_op jit(solution)/shard_map/ppermute | solution.py:167
  7.1 19.9 %collective-permute-start.12 = (bf16[32,7168]{1,0:T(8,128)(2,1)S(1)}, bf16[32,7168]{1,0:T(8,128)(2,1)}, u32[]{:S(2)}, u32[]{:S(2)}) collective-permute-start(bf16[32,7168]{1,0:T(8,128)(2,1)S(1)} %get-tuple-element.28.refs_2_), channel_id=1, source_target_pairs={{0,4},{2,6},{8,0},{10,2},{16,8},{18,10},{24,16},{26,18},{28,24},{3... | collective-permute-start | bytes 1376264 | tf_op jit(solution)/shard_map/ppermute | solution.py:168
  7.2 21.5 %collective-permute-start.27 = (bf16[32,7168]{1,0:T(8,128)(2,1)S(1)}, bf16[32,7168]{1,0:T(8,128)(2,1)}, u32[]{:S(2)}, u32[]{:S(2)}) collective-permute-start(bf16[32,7168]{1,0:T(8,128)(2,1)S(1)} %get-tuple-element.29.refs_0_), channel_id=1, source_target_pairs={{0,2},{2,0},{8,10},{10,8},{16,18},{18,16},{24,26},{26,24},{28,30},... | collective-permute-start | bytes 1376264 | tf_op jit(solution)/shard_map/ppermute | solution.py:126
  23.9 4.7 %collective-permute-start.28 = (bf16[32,7168]{1,0:T(8,128)(2,1)S(1)}, bf16[32,7168]{1,0:T(8,128)(2,1)S(1)}, u32[]{:S(2)}, u32[]{:S(2)}) collective-permute-start(bf16[32,7168]{1,0:T(8,128)(2,1)S(1)} %get-tuple-element.28.refs_2_), channel_id=1, source_target_pairs={{0,2},{2,0},{8,10},{10,8},{16,18},{18,16},{24,26},{26,24},{28,30},... | collective-permute-start | bytes 1376264 | tf_op jit(solution)/shard_map/ppermute | solution.py:126
  24.5 14.4 %collective-permute-start.41 = (bf16[16,32,512]{2,1,0:T(8,128)(2,1)}, bf16[16,32,512]{2,1,0:T(8,128)(2,1)}, u32[]{:S(2)}, u32[]{:S(2)}) collective-permute-start(bf16[16,32,512]{2,1,0:T(8,128)(2,1)} %param.40), channel_id=1, source_target_pairs={{0,1},{1,0},{2,3},{3,2},{4,5},{5,4},{6,7},{7,6},{8,9},{9,8},{10,11... | collective-permute-start | bytes 1572872 | tf_op jit(solution)/shard_map/ppermute | solution.py:237
  26.5 12.5 %collective-permute-start.16 = (bf16[32,7168]{1,0:T(8,128)(2,1)S(1)}, bf16[32,7168]{1,0:T(8,128)(2,1)}, u32[]{:S(2)}, u32[]{:S(2)}) collective-permute-start(bf16[32,7168]{1,0:T(8,128)(2,1)S(1)} %collective-permute-done.refs_0_), channel_id=1, source_target_pairs={{0,2},{2,0},{8,10},{10,8},{16,18},{18,16},{24,26},{26,24},{28,30},... | collective-permute-start | bytes 1376264 | tf_op jit(solution)/shard_map/ppermute | solution.py:126
  27.0 15.8 %collective-permute-start.1 = (bf16[32,7168]{1,0:T(8,128)(2,1)S(1)}, bf16[32,7168]{1,0:T(8,128)(2,1)}, u32[]{:S(2)}, u32[]{:S(2)}) collective-permute-start(bf16[32,7168]{1,0:T(8,128)(2,1)S(1)} %collective-permute-done.refs_0_), channel_id=1, source_target_pairs={{0,8},{2,10},{8,16},{10,18},{16,24},{18,26},{24,28},{26,30},{28,20... | collective-permute-start | bytes 1376264 | tf_op jit(solution)/shard_map/ppermute | solution.py:167
  28.6 12.3 %collective-permute-start.17 = (bf16[32,7168]{1,0:T(8,128)(2,1)}, bf16[32,7168]{1,0:T(8,128)(2,1)}, u32[]{:S(2)}, u32[]{:S(2)}) collective-permute-start(bf16[32,7168]{1,0:T(8,128)(2,1)} %collective-permute-done.4.refs_2_), channel_id=1, source_target_pairs={{0,2},{2,0},{8,10},{10,8},{16,18},{18,16},{24,26},{26,24},{28,30},... | collective-permute-start | bytes 1376264 | tf_op jit(solution)/shard_map/ppermute | solution.py:126
  29.4 13.5 %collective-permute-start.5 = (bf16[32,7168]{1,0:T(8,128)(2,1)}, bf16[32,7168]{1,0:T(8,128)(2,1)}, u32[]{:S(2)}, u32[]{:S(2)}) collective-permute-start(bf16[32,7168]{1,0:T(8,128)(2,1)} %collective-permute-done.4.refs_2_), channel_id=1, source_target_pairs={{0,4},{2,6},{8,0},{10,2},{16,8},{18,10},{24,16},{26,18},{28,24},{3... | collective-permute-start | bytes 1376264 | tf_op jit(solution)/shard_map/ppermute | solution.py:168
  38.9 2.3 %collective-permute-start.18 = (bf16[32,7168]{1,0:T(8,128)(2,1)}, bf16[32,7168]{1,0:T(8,128)(2,1)}, u32[]{:S(2)}, u32[]{:S(2)}) collective-permute-start(bf16[32,7168]{1,0:T(8,128)(2,1)} %collective-permute-done.8.refs_4_), channel_id=1, source_target_pairs={{0,2},{2,0},{8,10},{10,8},{16,18},{18,16},{24,26},{26,24},{28,30},... | collective-permute-start | bytes 1376264 | tf_op jit(solution)/shard_map/ppermute | solution.py:126
  39.0 13.3 %collective-permute-start.9 = (bf16[32,7168]{1,0:T(8,128)(2,1)}, bf16[32,7168]{1,0:T(8,128)(2,1)}, u32[]{:S(2)}, u32[]{:S(2)}) collective-permute-start(bf16[32,7168]{1,0:T(8,128)(2,1)} %collective-permute-done.8.refs_4_), channel_id=1, source_target_pairs={{0,8},{2,10},{8,16},{10,18},{16,24},{18,26},{24,28},{26,30},{28,20... | collective-permute-start | bytes 1376264 | tf_op jit(solution)/shard_map/ppermute | solution.py:167
  40.9 11.5 %collective-permute-start.19 = (bf16[32,7168]{1,0:T(8,128)(2,1)}, bf16[32,7168]{1,0:T(8,128)(2,1)S(1)}, u32[]{:S(2)}, u32[]{:S(2)}) collective-permute-start(bf16[32,7168]{1,0:T(8,128)(2,1)} %collective-permute-done.12.refs_6_), channel_id=1, source_target_pairs={{0,2},{2,0},{8,10},{10,8},{16,18},{18,16},{24,26},{26,24},{28,30},... | collective-permute-start | bytes 1376264 | tf_op jit(solution)/shard_map/ppermute | solution.py:126
  41.2 13.8 %collective-permute-start.13 = (bf16[32,7168]{1,0:T(8,128)(2,1)}, bf16[32,7168]{1,0:T(8,128)(2,1)}, u32[]{:S(2)}, u32[]{:S(2)}) collective-permute-start(bf16[32,7168]{1,0:T(8,128)(2,1)} %collective-permute-done.12.refs_6_), channel_id=1, source_target_pairs={{0,4},{2,6},{8,0},{10,2},{16,8},{18,10},{24,16},{26,18},{28,24},{3... | collective-permute-start | bytes 1376264 | tf_op jit(solution)/shard_map/ppermute | solution.py:168
  42.9 13.7 %collective-permute-start.21 = (bf16[32,7168]{1,0:T(8,128)(2,1)}, bf16[32,7168]{1,0:T(8,128)(2,1)S(1)}, u32[]{:S(2)}, u32[]{:S(2)}) collective-permute-start(bf16[32,7168]{1,0:T(8,128)(2,1)} %collective-permute-done.1.refs_0_), channel_id=1, source_target_pairs={{0,2},{2,0},{8,10},{10,8},{16,18},{18,16},{24,26},{26,24},{28,30},... | collective-permute-start | bytes 1376264 | tf_op jit(solution)/shard_map/ppermute | solution.py:126
  42.9 15.0 %collective-permute-start.22 = (bf16[32,7168]{1,0:T(8,128)(2,1)}, bf16[32,7168]{1,0:T(8,128)(2,1)S(1)}, u32[]{:S(2)}, u32[]{:S(2)}) collective-permute-start(bf16[32,7168]{1,0:T(8,128)(2,1)} %collective-permute-done.5.refs_2_), channel_id=1, source_target_pairs={{0,2},{2,0},{8,10},{10,8},{16,18},{18,16},{24,26},{26,24},{28,30},... | collective-permute-start | bytes 1376264 | tf_op jit(solution)/shard_map/ppermute | solution.py:126
  52.3 33.4 %collective-permute-start.23 = (bf16[32,7168]{1,0:T(8,128)(2,1)}, bf16[32,7168]{1,0:T(8,128)(2,1)}, u32[]{:S(2)}, u32[]{:S(2)}) collective-permute-start(bf16[32,7168]{1,0:T(8,128)(2,1)} %collective-permute-done.9.refs_4_), channel_id=1, source_target_pairs={{0,2},{2,0},{8,10},{10,8},{16,18},{18,16},{24,26},{26,24},{28,30},... | collective-permute-start | bytes 1376264 | tf_op jit(solution)/shard_map/ppermute | solution.py:126
  53.2 35.8 %collective-permute-start.2 = (bf16[32,7168]{1,0:T(8,128)(2,1)}, bf16[32,7168]{1,0:T(8,128)(2,1)}, u32[]{:S(2)}, u32[]{:S(2)}) collective-permute-start(bf16[32,7168]{1,0:T(8,128)(2,1)} %collective-permute-done.1.refs_0_), channel_id=1, source_target_pairs={{0,8},{2,10},{8,16},{10,18},{16,24},{18,26},{24,28},{26,30},{28,20... | collective-permute-start | bytes 1376264 | tf_op jit(solution)/shard_map/ppermute | solution.py:167
  55.0 34.1 %collective-permute-start.10 = (bf16[32,7168]{1,0:T(8,128)(2,1)}, bf16[32,7168]{1,0:T(8,128)(2,1)}, u32[]{:S(2)}, u32[]{:S(2)}) collective-permute-start(bf16[32,7168]{1,0:T(8,128)(2,1)} %collective-permute-done.9.refs_4_), channel_id=1, source_target_pairs={{0,8},{2,10},{8,16},{10,18},{16,24},{18,26},{24,28},{26,30},{28,20... | collective-permute-start | bytes 1376264 | tf_op jit(solution)/shard_map/ppermute | solution.py:167
  57.4 32.1 %collective-permute-start.6 = (bf16[32,7168]{1,0:T(8,128)(2,1)}, bf16[32,7168]{1,0:T(8,128)(2,1)}, u32[]{:S(2)}, u32[]{:S(2)}) collective-permute-start(bf16[32,7168]{1,0:T(8,128)(2,1)} %collective-permute-done.5.refs_2_), channel_id=1, source_target_pairs={{0,4},{2,6},{8,0},{10,2},{16,8},{18,10},{24,16},{26,18},{28,24},{3... | collective-permute-start | bytes 1376264 | tf_op jit(solution)/shard_map/ppermute | solution.py:168
  58.6 29.9 %collective-permute-start.14 = (bf16[32,7168]{1,0:T(8,128)(2,1)}, bf16[32,7168]{1,0:T(8,128)(2,1)}, u32[]{:S(2)}, u32[]{:S(2)}) collective-permute-start(bf16[32,7168]{1,0:T(8,128)(2,1)} %collective-permute-done.13.refs_6_), channel_id=1, source_target_pairs={{0,4},{2,6},{8,0},{10,2},{16,8},{18,10},{24,16},{26,18},{28,24},{3... | collective-permute-start | bytes 1376264 | tf_op jit(solution)/shard_map/ppermute | solution.py:168
  85.7 11.1 %collective-permute-start.24 = (bf16[32,7168]{1,0:T(8,128)(2,1)}, bf16[32,7168]{1,0:T(8,128)(2,1)S(1)}, u32[]{:S(2)}, u32[]{:S(2)}) collective-permute-start(bf16[32,7168]{1,0:T(8,128)(2,1)} %collective-permute-done.13.refs_6_), channel_id=1, source_target_pairs={{0,2},{2,0},{8,10},{10,8},{16,18},{18,16},{24,26},{26,24},{28,30},... | collective-permute-start | bytes 1376264 | tf_op jit(solution)/shard_map/ppermute | solution.py:126
  88.5 20.7 %collective-permute-start.15 = (bf16[32,7168]{1,0:T(8,128)(2,1)}, bf16[32,7168]{1,0:T(8,128)(2,1)S(1)}, u32[]{:S(2)}, u32[]{:S(2)}) collective-permute-start(bf16[32,7168]{1,0:T(8,128)(2,1)} %collective-permute-done.14.refs_6_), channel_id=1, source_target_pairs={{0,2},{2,0},{8,10},{10,8},{16,18},{18,16},{24,26},{26,24},{28,30},... | collective-permute-start | bytes 1376264 | tf_op jit(solution)/shard_map/ppermute | solution.py:126
  89.0 20.5 %collective-permute-start.3 = (bf16[32,7168]{1,0:T(8,128)(2,1)}, bf16[32,7168]{1,0:T(8,128)(2,1)S(1)}, u32[]{:S(2)}, u32[]{:S(2)}) collective-permute-start(bf16[32,7168]{1,0:T(8,128)(2,1)} %collective-permute-done.2.refs_0_), channel_id=1, source_target_pairs={{0,2},{2,0},{8,10},{10,8},{16,18},{18,16},{24,26},{26,24},{28,30},... | collective-permute-start | bytes 1376264 | tf_op jit(solution)/shard_map/ppermute | solution.py:126
  89.1 20.4 %collective-permute-start.11 = (bf16[32,7168]{1,0:T(8,128)(2,1)}, bf16[32,7168]{1,0:T(8,128)(2,1)S(1)}, u32[]{:S(2)}, u32[]{:S(2)}) collective-permute-start(bf16[32,7168]{1,0:T(8,128)(2,1)} %collective-permute-done.10.refs_4_), channel_id=1, source_target_pairs={{0,2},{2,0},{8,10},{10,8},{16,18},{18,16},{24,26},{26,24},{28,30},... | collective-permute-start | bytes 1376264 | tf_op jit(solution)/shard_map/ppermute | solution.py:126
  89.5 19.9 %collective-permute-start.7 = (bf16[32,7168]{1,0:T(8,128)(2,1)}, bf16[32,7168]{1,0:T(8,128)(2,1)S(1)}, u32[]{:S(2)}, u32[]{:S(2)}) collective-permute-start(bf16[32,7168]{1,0:T(8,128)(2,1)} %collective-permute-done.6.refs_2_), channel_id=1, source_target_pairs={{0,2},{2,0},{8,10},{10,8},{16,18},{18,16},{24,26},{26,24},{28,30},... | collective-permute-start | bytes 1376264 | tf_op jit(solution)/shard_map/ppermute | solution.py:126
  96.8 19.8 %collective-permute-start.34 = (bf16[2,14336]{1,0:T(2,128)(2,1)S(1)}, bf16[2,14336]{1,0:T(2,128)(2,1)S(1)}, u32[]{:S(2)}, u32[]{:S(2)}) collective-permute-start(bf16[2,14336]{1,0:T(2,128)(2,1)S(1)} %pad_maximum_fusion.1), channel_id=1, source_target_pairs={{0,28},{2,30},{8,20},{10,22},{16,12},{18,14},{24,4},{26,6},{28,0},... | collective-permute-start | bytes 172040 | tf_op jit(solution)/shard_map/ppermute | solution.py:162
  101.2 45.5 %slice-start = ((s8[14680064]{0:T(1024)(128)(4,1)}), s8[4194304]{0:T(1024)(128)(4,1)S(1)}, s32[]{:S(2)}) async-start(s8[14680064]{0:T(1024)(128)(4,1)} %bitcast.75), calls=%async_computation | async-start | bytes 8388608
  101.2 45.5 %slice-start.1 = ((s8[14680064]{0:T(1024)(128)(4,1)}), s8[4194304]{0:T(1024)(128)(4,1)S(1)}, s32[]{:S(2)}) async-start(s8[14680064]{0:T(1024)(128)(4,1)} %bitcast.75), calls=%async_computation.1 | async-start | bytes 8388608
  109.2 37.6 %slice-start.2 = ((s8[14680064]{0:T(1024)(128)(4,1)}), s8[4194304]{0:T(1024)(128)(4,1)S(1)}, s32[]{:S(2)}) async-start(s8[14680064]{0:T(1024)(128)(4,1)} %bitcast.75), calls=%async_computation.2 | async-start | bytes 8388608
  109.2 37.6 %slice-start.3 = ((s8[14680064]{0:T(1024)(128)(4,1)}), s8[2097152]{0:T(1024)(128)(4,1)S(1)}, s32[]{:S(2)}) async-start(s8[14680064]{0:T(1024)(128)(4,1)} %bitcast.75), calls=%async_computation.3 | async-start | bytes 4194304
  109.2 7.4 %collective-permute-start.35 = (bf16[2,14336]{1,0:T(2,128)(2,1)S(1)}, bf16[2,14336]{1,0:T(2,128)(2,1)S(1)}, u32[]{:S(2)}, u32[]{:S(2)}) collective-permute-start(bf16[2,14336]{1,0:T(2,128)(2,1)S(1)} %pad_maximum_fusion.2), channel_id=1, source_target_pairs={{0,30},{2,28},{8,22},{10,20},{16,14},{18,12},{24,6},{26,4},{28,2},... | collective-permute-start | bytes 172040 | tf_op jit(solution)/shard_map/ppermute | solution.py:162
  117.4 4.2 %collective-permute-start.36 = (f32[16,64]{1,0:T(8,128)S(1)}, f32[16,64]{1,0:T(8,128)S(1)}, u32[]{:S(2)}, u32[]{:S(2)}) collective-permute-start(f32[16,64]{1,0:T(8,128)S(1)} %slice_select_fusion.3), channel_id=1, source_target_pairs={{0,1},{1,0},{2,3},{3,2},{4,5},{5,4},{6,7},{7,6},{8,9},{9,8},{10,11... | collective-permute-start | bytes 12296 | tf_op jit(solution)/shard_map/ppermute | solution.py:217
  119.0 35.8 %collective-permute-start.25 = (f32[64,512]{1,0:T(8,128)S(1)}, f32[64,512]{1,0:T(8,128)}, u32[]{:S(2)}, u32[]{:S(2)}) collective-permute-start(f32[64,512]{1,0:T(8,128)S(1)} %slice_select_fusion.1), channel_id=1, source_target_pairs={{0,1},{1,0},{2,3},{3,2},{4,5},{5,4},{6,7},{7,6},{8,9},{9,8},{10,11... | collective-permute-start | bytes 393224 | tf_op jit(solution)/shard_map/ppermute | solution.py:271
  119.6 12.5 %collective-permute-start.29 = (bf16[32,7168]{1,0:T(8,128)(2,1)}, bf16[32,7168]{1,0:T(8,128)(2,1)S(1)}, u32[]{:S(2)}, u32[]{:S(2)}) collective-permute-start(bf16[32,7168]{1,0:T(8,128)(2,1)} %collective-permute-done.2.refs_0_), channel_id=1, source_target_pairs={{0,8},{2,10},{8,16},{10,18},{16,24},{18,26},{24,28},{26,30},{28,20... | collective-permute-start | bytes 1376264 | tf_op jit(solution)/shard_map/ppermute | solution.py:171
  119.6 12.6 %collective-permute-start.31 = (bf16[32,7168]{1,0:T(8,128)(2,1)}, bf16[32,7168]{1,0:T(8,128)(2,1)S(1)}, u32[]{:S(2)}, u32[]{:S(2)}) collective-permute-start(bf16[32,7168]{1,0:T(8,128)(2,1)} %collective-permute-done.14.refs_6_), channel_id=1, source_target_pairs={{0,4},{2,6},{8,0},{10,2},{16,8},{18,10},{24,16},{26,18},{28,24},{3... | collective-permute-start | bytes 1376264 | tf_op jit(solution)/shard_map/ppermute | solution.py:172
  121.7 11.0 %collective-permute-start.37 = (bf16[1,16,64]{2,1,0:T(8,128)(2,1)S(1)}, bf16[1,16,64]{2,1,0:T(8,128)(2,1)S(1)}, u32[]{:S(2)}, u32[]{:S(2)}) collective-permute-start(bf16[1,16,64]{2,1,0:T(8,128)(2,1)S(1)} %bitcast.89), channel_id=1, source_target_pairs={{0,2},{2,0},{4,6},{6,4},{8,10},{10,8},{12,14},{14,12},{16,18},{18,... | collective-permute-start | bytes 6152 | tf_op jit(solution)/shard_map/ppermute | solution.py:224
  122.4 32.4 %collective-permute-start.20 = (f32[64,512]{1,0:T(8,128)}, f32[64,512]{1,0:T(8,128)}, u32[]{:S(2)}, u32[]{:S(2)}) collective-permute-start(f32[64,512]{1,0:T(8,128)} %get-tuple-element.33), channel_id=1, source_target_pairs={{0,1},{1,0},{2,3},{3,2},{4,5},{5,4},{6,7},{7,6},{8,9},{9,8},{10,11... | collective-permute-start | bytes 393224 | tf_op jit(solution)/shard_map/ppermute | solution.py:271
  132.1 14.6 %collective-permute-start.30 = (bf16[32,7168]{1,0:T(8,128)(2,1)S(1)}, bf16[32,7168]{1,0:T(8,128)(2,1)S(1)}, u32[]{:S(2)}, u32[]{:S(2)}) collective-permute-start(bf16[32,7168]{1,0:T(8,128)(2,1)S(1)} %collective-permute-done.29.refs_0_), channel_id=1, source_target_pairs={{0,2},{2,0},{8,10},{10,8},{16,18},{18,16},{24,26},{26,24},{28,30},... | collective-permute-start | bytes 1376264 | tf_op jit(solution)/shard_map/ppermute | solution.py:126
  132.2 14.5 %collective-permute-start.32 = (bf16[32,7168]{1,0:T(8,128)(2,1)S(1)}, bf16[32,7168]{1,0:T(8,128)(2,1)S(1)}, u32[]{:S(2)}, u32[]{:S(2)}) collective-permute-start(bf16[32,7168]{1,0:T(8,128)(2,1)S(1)} %collective-permute-done.31.refs_2_), channel_id=1, source_target_pairs={{0,2},{2,0},{8,10},{10,8},{16,18},{18,16},{24,26},{26,24},{28,30},... | collective-permute-start | bytes 1376264 | tf_op jit(solution)/shard_map/ppermute | solution.py:126
  132.7 3.7 %collective-permute-start.38 = (bf16[2,16,64]{2,1,0:T(8,128)(2,1)S(1)}, bf16[2,16,64]{2,1,0:T(8,128)(2,1)S(1)}, u32[]{:S(2)}, u32[]{:S(2)}) collective-permute-start(bf16[2,16,64]{2,1,0:T(8,128)(2,1)S(1)} %maximum_select_fusion.7), channel_id=1, source_target_pairs={{0,4},{2,6},{4,0},{6,2},{8,12},{10,14},{12,8},{14,10},{16,20},{18,... | collective-permute-start | bytes 12296 | tf_op jit(solution)/shard_map/ppermute | solution.py:224
  136.4 3.8 %collective-permute-start.39 = (bf16[4,16,64]{2,1,0:T(8,128)(2,1)S(1)}, bf16[4,16,64]{2,1,0:T(8,128)(2,1)S(1)}, u32[]{:S(2)}, u32[]{:S(2)}) collective-permute-start(bf16[4,16,64]{2,1,0:T(8,128)(2,1)S(1)} %maximum_select_fusion.5), channel_id=1, source_target_pairs={{0,8},{2,10},{4,12},{6,14},{8,0},{10,2},{12,4},{14,6},{16,24},{18,... | collective-permute-start | bytes 24584 | tf_op jit(solution)/shard_map/ppermute | solution.py:224
  140.2 4.9 %collective-permute-start.40 = (bf16[8,16,64]{2,1,0:T(8,128)(2,1)S(1)}, bf16[8,16,64]{2,1,0:T(8,128)(2,1)S(1)}, u32[]{:S(2)}, u32[]{:S(2)}) collective-permute-start(bf16[8,16,64]{2,1,0:T(8,128)(2,1)S(1)} %maximum_select_fusion.3), channel_id=1, source_target_pairs={{0,16},{2,18},{4,20},{6,22},{8,24},{10,26},{12,28},{14,30},{16,0},... | collective-permute-start | bytes 49160 | tf_op jit(solution)/shard_map/ppermute | solution.py:224
  145.1 9.8 %collective-permute-start.26 = (f32[64,512]{1,0:T(8,128)S(1)}, f32[64,512]{1,0:T(8,128)}, u32[]{:S(2)}, u32[]{:S(2)}) collective-permute-start(f32[64,512]{1,0:T(8,128)S(1)} %get-tuple-element.34), channel_id=1, source_target_pairs={{0,1},{1,0},{2,3},{3,2},{4,5},{5,4},{6,7},{7,6},{8,9},{9,8},{10,11... | collective-permute-start | bytes 393224 | tf_op jit(solution)/shard_map/ppermute | solution.py:271
  152.2 5.0 %collective-permute-start.33 = (f32[64,512]{1,0:T(8,128)S(1)}, f32[64,512]{1,0:T(8,128)S(1)}, u32[]{:S(2)}, u32[]{:S(2)}) collective-permute-start(f32[64,512]{1,0:T(8,128)S(1)} %broadcast_select_fusion), channel_id=1, source_target_pairs={{0,1},{1,0},{2,3},{3,2},{4,5},{5,4},{6,7},{7,6},{8,9},{9,8},{10,11... | collective-permute-start | bytes 393224 | tf_op jit(solution)/shard_map/ppermute | solution.py:271
  (14 other events, 89.9 us)

commit v2 on v0

v2 whole, which is shorter than its diff:
```python
import functools

import jax
import jax.numpy as jnp
import numpy as np
from jax import lax
from jax.experimental import pallas as pl
from jax.experimental.pallas import tpu as pltpu
from jax.sharding import PartitionSpec as P

MOST = 2
INNER = ("mp", "sub")
SWAP = [(0, 1), (1, 0)]


def tile_of(depth, most=1792):
    parts = 1
    while depth % parts or (depth // parts) % 128 or depth // parts > most:
        parts += 1
    return depth // parts


def rows_kernel(count, lane_ref, *refs):
    pieces, rest = refs[:count], refs[count:]
    weight, weight_sib, first, first_sib, mine, sib, low, acc, acc_sib, acc_low = rest
    step = pl.program_id(0)

    @pl.when(step == 0)
    def _():
        acc[...] = jnp.zeros_like(acc)
        acc_sib[...] = jnp.zeros_like(acc_sib)
        acc_low[...] = jnp.zeros_like(acc_low)

    rows = jnp.concatenate([piece[...] for piece in pieces], axis=0)
    factors = jnp.concatenate([first[...], first_sib[...]], axis=0)
    acc[...] += jnp.dot(rows, weight[...], preferred_element_type=jnp.float32)
    acc_sib[...] += jnp.dot(rows, weight_sib[...], preferred_element_type=jnp.float32)
    acc_low[...] += lax.dot_general(
        rows, factors, (((1,), (1,)), ((), ())), preferred_element_type=jnp.float32
    )

    @pl.when(step == pl.num_programs(0) - 1)
    def _():
        height = pieces[0].shape[0]
        for index in range(count):
            lane = jnp.bitwise_xor(lane_ref[0], index % 2)
            block = slice(index * height, (index + 1) * height)
            mine[index // 2, lane] = acc[block, :]
            sib[index // 2, lane] = acc_sib[block, :]
            low[index // 2, lane] = acc_low[block, :]


def rows_product(lane, pieces, weight, weight_sib, first, first_sib):
    count = len(pieces)
    row_count, depth = pieces[0].shape
    tile = tile_of(depth)
    tiles = depth // tile
    width, rank = weight.shape[1], first.shape[0]
    total = count * row_count
    grid_spec = pltpu.PrefetchScalarGridSpec(
        num_scalar_prefetch=1,
        grid=(tiles,),
        in_specs=[pl.BlockSpec((row_count, tile), lambda i, lane: (0, i))] * count
        + [
            pl.BlockSpec((tile, width), lambda i, lane: (lane[0] * tiles + i, 0)),
            pl.BlockSpec((tile, width), lambda i, lane: (i, 0)),
            pl.BlockSpec((rank, tile), lambda i, lane: (0, lane[0] * tiles + i)),
            pl.BlockSpec((rank, tile), lambda i, lane: (0, i)),
        ],
        out_specs=[
            pl.BlockSpec((count // 2, 2, row_count, size), lambda i, lane: (0, 0, 0, 0))
            for size in (width, width, 2 * rank)
        ],
        scratch_shapes=[
            pltpu.VMEM((total, size), jnp.float32) for size in (width, width, 2 * rank)
        ],
    )
    return pl.pallas_call(
        functools.partial(rows_kernel, count),
        grid_spec=grid_spec,
        out_shape=[
            jax.ShapeDtypeStruct((count // 2, 2, row_count, size), jnp.float32)
            for size in (width, width, 2 * rank)
        ],
        compiler_params=pltpu.CompilerParams(vmem_limit_bytes=40 * 2**20),
        cost_estimate=pl.CostEstimate(
            flops=4 * total * depth * (width + rank),
            bytes_accessed=2 * depth * (2 * width + 2 * rank + total),
            transcendentals=0,
        ),
    )(lane, *pieces, weight, weight_sib, first, first_sib)


def hidden_of(gate, up):
    return (jax.nn.silu(gate.astype(jnp.float32)) * up.astype(jnp.float32)).astype(jnp.bfloat16)


def slots_of(row_adapter_index, adapter_storage_slot):
    names = jnp.arange(adapter_storage_slot.shape[0], dtype=jnp.int32)
    same = row_adapter_index == names[None, :]
    return jnp.sum(jnp.where(same, adapter_storage_slot[None, :], 0), axis=1)


def gathered(
    gate_activation,
    up_activation,
    down_base_weight,
    first_factor_table,
    second_factor_table,
    row_adapter_index,
    adapter_storage_slot,
):
    hidden = hidden_of(gate_activation, up_activation)
    row_count = hidden.shape[0]
    owners = lax.axis_size("wide")
    local_adapter = first_factor_table.shape[0]
    slots = local_adapter * owners
    rank_portion = second_factor_table.shape[1]
    home = lax.axis_index("wide")
    slot_all = slots_of(row_adapter_index, adapter_storage_slot)
    blocks = slot_all.reshape(owners, row_count)
    order = jnp.arange(row_count, dtype=jnp.int32)
    earlier = (blocks[:, :, None] == blocks[:, None, :]) & (order[None, :] < order[:, None])
    position = jnp.sum(earlier.astype(jnp.int32), axis=2)
    rows = lax.all_gather(hidden, "wide", axis=0, tiled=True)
    base = jnp.dot(rows, down_base_weight, preferred_element_type=jnp.float32)
    low = jnp.einsum("re,nqe->nrq", rows, first_factor_table, preferred_element_type=jnp.float32)
    low = low.reshape(local_adapter, owners, row_count, low.shape[2])
    own = home * local_adapter + jnp.arange(local_adapter, dtype=jnp.int32)
    kept = []
    for item in range(MOST):
        mask = (blocks[None] == own[:, None, None]) & (position == item)[None]
        kept.append(jnp.sum(jnp.where(mask[..., None], low, 0), axis=2))
    low = lax.psum_scatter(jnp.stack(kept, axis=2), INNER, scatter_dimension=3, tiled=True)
    low = lax.all_gather(low.astype(jnp.bfloat16), "wide", axis=0, tiled=True)
    spread = 0
    for item in range(MOST):
        mask = (blocks[None] == jnp.arange(slots, dtype=jnp.int32)[:, None, None]) & (position == item)
        spread += jnp.where(mask[..., None], low[:, :, item][:, :, None], 0)
    spread = spread.reshape(slots, owners * row_count, rank_portion)
    delta = jnp.einsum("srq,sqw->rw", spread, second_factor_table, preferred_element_type=jnp.float32)
    total = base + delta
    return lax.psum_scatter(total, INNER, scatter_dimension=0, tiled=True).astype(jnp.bfloat16)


def ring_order(nodes):
    return list(range(0, nodes, 2)) + list(range(nodes - 1, 0, -2))


def ringed(
    gate_activation,
    up_activation,
    down_base_weight,
    first_factor_table,
    second_factor_table,
    row_adapter_index,
    adapter_storage_slot,
):
    f32, bf16 = jnp.float32, jnp.bfloat16
    row_count, width_part = gate_activation.shape
    owners = lax.axis_size("wide")
    nodes = owners // 2
    far = nodes // 2
    steps = far - 1
    own_nodes = nodes // 2
    own_blocks = owners // 2
    order = ring_order(nodes)
    depth = width_part // 2

    table = []
    for w in range(owners):
        p, lane = order.index(w // 2), w % 2
        at = lambda shift: order[(p + shift) % nodes]
        arrivals = [at(0)] + [at(s * k) for k in range(1, far) for s in (-1, 1)]
        row = [lane]
        row += [2 * node + side for node in arrivals for side in (0, 1)]
        row += [2 * at(far) + (lane ^ side) for side in (0, 1)]
        row += [int(at(s) < own_nodes) for s in range(far)]
        row += [at(s) % own_nodes for s in range(far)]
        row += [at(s + far) % own_nodes for s in range(far)]
        table.append(row)
    home = lax.axis_index("wide")
    part = lax.axis_index(INNER)
    facts = lax.dynamic_index_in_dim(jnp.asarray(np.array(table, np.int32)), home, 0, keepdims=False)
    edges = np.cumsum([0, 1, 2 * (nodes - 1), 2, far, far, far])
    lane, arrived, far_wide, in_first, near_target, far_target = [
        facts[a:b] for a, b in zip(edges[:-1], edges[1:])
    ]
    side = lane[0]
    mine = (in_first == 1) == (part == 0)
    target = jnp.where(mine, near_target, far_target)

    def moved(shift, cross=0):
        return [
            (order[p] * 2 + c, order[(p + shift) % nodes] * 2 + (c ^ cross))
            for p in range(nodes)
            for c in (0, 1)
        ]

    def send(value, shift, cross=0):
        return lax.ppermute(value, "wide", moved(shift, cross))

    def half_of(value, which, axis):
        return lax.dynamic_slice_in_dim(value, which * depth, depth, axis)

    keep = hidden_of(half_of(gate_activation, side, 1), half_of(up_activation, side, 1))
    right, left = [send(keep, 1)], [send(keep, -1)]
    give = hidden_of(half_of(gate_activation, 1 - side, 1), half_of(up_activation, 1 - side, 1))
    twin = send(give, 0, 1)
    right.append(send(twin, 1))
    left.append(send(twin, -1))

    first = first_factor_table[0]
    weight_sib = send(half_of(down_base_weight, 1 - side, 0), 0, 1)
    first_sib = send(half_of(first, 1 - side, 1), 0, 1)
    product = lambda pieces: rows_product(
        lane, pieces, down_base_weight, weight_sib, first, first_sib
    )

    slot_all = slots_of(row_adapter_index, adapter_storage_slot).reshape(owners, row_count)
    ranks = jnp.arange(row_count, dtype=jnp.int32)
    earlier = (slot_all[:, :, None] == slot_all[:, None, :]) & (ranks[None, :] < ranks[:, None])
    position = jnp.sum(earlier.astype(jnp.int32), axis=2)
    items = jnp.arange(MOST, dtype=jnp.int32)

    sides = jnp.arange(2, dtype=jnp.int32)
    own_wide = jnp.bitwise_xor(home, sides)
    blocks = jnp.arange(owners, dtype=jnp.int32)
    own_is = own_wide[:, None, None] == blocks[None, :, None]
    own_slot = jnp.sum(jnp.where(own_is, slot_all[None], 0), axis=1)
    own_position = jnp.sum(jnp.where(own_is, position[None], 0), axis=1)
    pick = (own_slot[None, :, None, :] == far_wide[:, None, None, None]) & (
        own_position[None, :, None, :] == items[None, None, :, None]
    )
    pick = jnp.where(
        (sides[:, None] == sides[None, :])[None, :, None, :, None], pick[:, :, :, None, :], False
    ).reshape(4 * MOST, 2 * row_count)
    both = jnp.concatenate([keep, twin], axis=0)
    picked = jnp.dot(pick.astype(bf16), both, preferred_element_type=f32).astype(bf16)
    far_rows = send(picked, far)

    mine_sums, sib_sums, lows = [], [], []

    def add(result):
        mine_sums.append(result[0])
        sib_sums.append(send(result[1], 0, 1))
        lows.append(result[2].reshape(-1, result[2].shape[3]))

    pieces = [keep, twin]
    result = None
    for step in range(1, steps + 1):
        pieces += right + left
        if result is not None:
            right[0], left[0], result = lax.optimization_barrier((right[0], left[0], result))
            add(result)
        if step < steps:
            right = [send(block, 1) for block in right]
            left = [send(block, -1) for block in left]
        else:
            last = [send(right[0], 1), send(left[1], -1)]
        result = product(pieces)
        pieces = []
    last[0], last[1], result = lax.optimization_barrier((last[0], last[1], result))
    add(result)

    far_low = lax.dot_general(
        far_rows,
        jnp.concatenate([first_half(first, side, depth), first_sib], axis=0),
        (((1,), (1,)), ((), ())),
        preferred_element_type=f32,
    )
    rank = first.shape[0]
    low = jnp.concatenate(lows, axis=0)

    def chosen(slot, far_part):
        near = (
            (arrived[None, None, :, None] == blocks[:, None, None, None])
            & (slot_all == slot)[:, None, None, :]
            & (position[:, None, None, :] == items[None, :, None, None])
        ).reshape(owners * MOST, -1)
        there = (
            (far_wide[None, None, :, None] == blocks[:, None, None, None])
            & (items[:, None] == items[None, :])[None, :, None, :]
        ).reshape(owners * MOST, -1)
        return jnp.concatenate([near, there], axis=1).astype(f32)

    def compact(slot, values, far_values):
        return jnp.dot(
            chosen(slot, far_values),
            jnp.concatenate([values, far_values], axis=0),
            precision=lax.Precision.HIGHEST,
        )

    count = 2 * MOST
    low_sib = compact(jnp.bitwise_xor(home, 1), low[:, rank:], far_low[count:, rank:])
    low_mine = compact(home, low[:, :rank], far_low[:count, :rank])
    low = low_mine + send(low_sib, 0, 1)

    half = owners * MOST // 2
    kept = jnp.where(part == 0, low[:half], low[half:])
    sent = jnp.where(part == 0, low[half:], low[:half])
    low = (kept + lax.ppermute(sent, INNER, SWAP)).astype(bf16)[None]
    gap = 1
    while gap < owners:
        other = lax.ppermute(low, "wide", [(w, w ^ gap) for w in range(owners)])
        low = jnp.where(
            home & gap == 0,
            jnp.concatenate([low, other], axis=0),
            jnp.concatenate([other, low], axis=0),
        )
        gap *= 2
    low = low.reshape(owners, own_blocks, MOST, rank)

    other = lax.ppermute(second_factor_table, INNER, SWAP)
    second = jnp.where(
        part == 0,
        jnp.concatenate([second_factor_table, other], axis=1),
        jnp.concatenate([other, second_factor_table], axis=1),
    )
    width = second.shape[2]
    slot_here = lax.dynamic_slice_in_dim(slot_all, part * own_blocks, own_blocks)
    position_here = lax.dynamic_slice_in_dim(position, part * own_blocks, own_blocks)
    spread = 0
    for item in range(MOST):
        mask = (slot_here[:, :, None] == blocks) & (position_here == item)[:, :, None]
        spread += jnp.where(mask[..., None], jnp.swapaxes(low[:, :, item], 0, 1)[:, None], 0)
    delta = jnp.dot(
        spread.reshape(own_blocks * row_count, -1).astype(bf16),
        second.reshape(-1, width),
        preferred_element_type=f32,
    )

    result = product(last)
    add(result)
    sums = [a + b for a, b in zip(mine_sums, sib_sums)]
    group_rows = 2 * row_count
    by_shift = {0: sums[0][0], far: sums[-1][0]}
    for step in range(1, far):
        extra = 1 if step == 1 else 0
        by_shift[nodes - step] = sums[step - 1][extra]
        by_shift[step] = sums[step - 1][extra + 1]

    def over_mp(shifts):
        near = jnp.stack([by_shift[s] for s in shifts])
        away = jnp.stack([by_shift[s + far] for s in shifts])
        pred = mine[shifts[0] : shifts[-1] + 1][:, None, None, None]
        kept = jnp.where(pred, near, away)
        sent = jnp.where(pred, away, near).astype(bf16)
        return kept + lax.ppermute(sent, INNER, SWAP).astype(f32)

    values = jnp.concatenate([over_mp([0]), over_mp(list(range(1, far)))], axis=0)
    delta = delta.reshape(own_nodes, group_rows, width)
    out = []
    for index in range(own_nodes):
        rows = delta[index]
        for pair in range(far):
            rows = rows + jnp.where(
                target[pair] == index, values[pair].reshape(group_rows, width), 0
            )
        out.append(rows)
    return jnp.stack(out).reshape(-1, width).astype(bf16)


def first_half(first, side, depth):
    return lax.dynamic_slice_in_dim(first, side * depth, depth, 1)


def solution(mesh):
    shape = dict(mesh.shape)
    wide, inner = shape["wide"], shape["mp"] * shape["sub"]
    paired = shape["sub"] == 1 and inner == 2 and wide % 8 == 0 and wide & (wide - 1) == 0
    if paired:
        nodes = wide // 2
        order = ring_order(nodes)
        paired = all(
            (order[p] < nodes // 2) != (order[(p + nodes // 2) % nodes] < nodes // 2)
            for p in range(nodes)
        )
    return jax.shard_map(
        ringed if paired else gathered,
        mesh=mesh,
        in_specs=(
            P(("groups", "wide"), ("mp", "sub")),
            P(("groups", "wide"), ("mp", "sub")),
            P(("mp", "sub"), "wide"),
            P("wide", None, ("mp", "sub")),
            P(None, ("mp", "sub"), "wide"),
            P("groups", None),
            P(),
        ),
        out_specs=P(("groups", "mp", "sub"), "wide"),
        check_vma=False,
    )
```

time: 191 us -> 145 us (0.76)
  waiting for transfers between devices: 98.1 us -> 36.9 us
  Pallas kernels: 0 us -> 32.3 us
  blocking collectives: 27.5 us -> 0 us
  matrix products: 18.3 us -> 2.67 us
  starting transfers between devices: 22.5 us -> 37.7 us
  local copies, waits for them, and re-layouts: 5.65 us -> 12.8 us
  other arithmetic: 5.18 us -> 12.1 us
  between operations: 13.5 us -> 10.2 us
    all_to_all x2 -> x0, waiting for transfers between devices: 41.7 us -> none  [the longest x1 35.3 us: on_device(): lax.all_to_all(outgoing, 'wide', split_axis=0, concat_axis=0, tiled=True)]
    ppermute x0 -> x31, starting transfers between devices: none -> 37.7 us  [the longest x23 22.5 us: send(): return lax.ppermute(value, 'wide', moved(shift, cross))]
    all_gather x1 -> x0, waiting for transfers between devices: 37.7 us -> none  [on_device(): lax.all_gather(hidden, 'wide', axis=0, tiled=True)]
    ppermute x0 -> x31, waiting for transfers between devices: none -> 36.9 us  [the longest x23 23.4 us: send(): return lax.ppermute(value, 'wide', moved(shift, cross))]
    pallas_call x0 -> x4, Pallas kernels: none -> 32.3 us  [rows_product(): pl.pallas_call(functools.partial(rows_kernel, count), grid_spec=grid_spec...]
    all_to_all x2 -> x0, starting transfers between devices: 22.5 us -> none  [the longest x1 15.1 us: on_device(): lax.all_to_all(lowered, 'wide', split_axis=0, concat_axis=0, tiled=True)]
    all_gather x1 -> x0, blocking collectives: 19.3 us -> none  [on_device(): low_all = lax.all_gather(mine, 'wide', axis=0, tiled=True)]
    reduce_scatter x1 -> x0, waiting for transfers between devices: 18.6 us -> none  [on_device(): lax.psum_scatter(total, ('mp', 'sub'), scatter_dimension=0, tiled=True)]
  transfers between devices with their start and end apart: 4 -> 31, of which waited for: 4 -> 9; matrix products, arithmetic and copies ran while one was open for 4% -> 11% of each run, Pallas kernels for 0% -> 22%
where the time goes in v2:
time: 145 us
  starting transfers between devices  37.7 us (26%)
  waiting for transfers between devices  36.9 us (25%)
  Pallas kernels  32.3 us (22%)
  local copies, waits for them, and re-layouts  12.8 us (9%)
  other arithmetic  12.1 us (8%)
  between operations  10.2 us (7%)
  matrix products  2.67 us (2%)
    pallas_call x4, Pallas kernels, rows_product(): pl.pallas_call(functools.partial(rows_kernel, count), grid_spec=grid_spec...  32.3 us
    ppermute x23, waiting for transfers between devices, send(): return lax.ppermute(value, 'wide', moved(shift, cross))  23.4 us
    ppermute x23, starting transfers between devices, send(): return lax.ppermute(value, 'wide', moved(shift, cross))  22.5 us
    ppermute x4, starting transfers between devices, ringed(): other = lax.ppermute(low, 'wide', [(w, w ^ gap) for w in range(owners)])  8.13 us
    dynamic_slice x1, local copies, waits for them, and re-layouts, half_of(): return lax.dynamic_slice_in_dim(value, which * depth, depth, axis)  6.65 us
    ppermute x2, waiting for transfers between devices, over_mp(): return kept + lax.ppermute(sent, INNER, SWAP).astype(f32)  5.6 us
    ppermute x4, waiting for transfers between devices, ringed(): other = lax.ppermute(low, 'wide', [(w, w ^ gap) for w in range(owners)])  5.4 us
    ppermute x2, starting transfers between devices, over_mp(): return kept + lax.ppermute(sent, INNER, SWAP).astype(f32)  4.39 us
  transfers between devices with their start and end apart: 31, of which 9 were waited for; matrix products, arithmetic and copies ran while one was open for 11% of the time, Pallas kernels for 22%

profile of v2, /device:TPU:0, one launch (start us, length us, event | category | flops | bytes accessed | tf_op | source)
XLA Modules:
  0.0 144.8 jit_solution(7187519998430718763)
XLA Ops:
  0.0 0.7 constant_dynamic-slice_fusion.1
  0.8 6.6 %constant_dynamic-slice_fusion = bf16[7168,512]{1,0:T(8,128)(2,1)} fusion(bf16[14336,512]{1,0:T(8,128)(2,1)} %refs_2_.1, s32[]{:T(128)S(6)} %select_n.345), kind=kLoop, calls=%fused_computation.115 | loop fusion | bytes 14680068 | tf_op jit(solution)/shard_map/dynamic_slice | solution.py:204
  7.9 2.5 %fusion.16 = (bf16[32,7168]{1,0:T(8,128)(2,1)S(1)}, bf16[32,7168]{1,0:T(8,128)(2,1)}) fusion(bf16[32,14336]{1,0:T(8,128)(2,1)S(1)} %copy-done.7, s32[]{:T(128)S(6)} %select_n.344, bf16[32,14336]{1,0:T(8,128)(2,1)} %param.8, s32[]{:T(128)S(6)} %select_n.345), kind=kLoop, calls=%fused_computation.26 | loop fusion | flops 3670016 | bytes 2752520 | tf_op jit(solution)/shard_map/convert_element_type | solution.py:95
  10.4 2.7 %collective-permute-start = (bf16[32,7168]{1,0:T(8,128)(2,1)S(1)}, bf16[32,7168]{1,0:T(8,128)(2,1)}, u32[]{:S(2)}, u32[]{:S(2)}) collective-permute-start(bf16[32,7168]{1,0:T(8,128)(2,1)S(1)} %get-tuple-element.63.refs_0_), channel_id=1, source_target_pairs={{0,8},{2,10},{8,16},{10,18},{16,24},{18,26},{24,28},{26,30},{28,20... | collective-permute-start | bytes 1376264 | tf_op jit(solution)/shard_map/ppermute | solution.py:201
  13.1 1.4 dynamic-slice_bitcast_fusion
  16.4 4.4 %collective-permute-done.4.refs_1_ = bf16[32,7168]{1,0:T(8,128)(2,1)} collective-permute-done((bf16[32,7168]{1,0:T(8,128)(2,1)}, bf16[32,7168]{1,0:T(8,128)(2,1)}, u32[]{:S(2)}, u32[]{:S(2)}) %collective-permute-start.4) | collective-permute-done | bytes 458784 | tf_op jit(solution)/shard_map/ppermute | solution.py:201
  20.8 2.9 %collective-permute-start.6 = (bf16[32,7168]{1,0:T(8,128)(2,1)}, bf16[32,7168]{1,0:T(8,128)(2,1)}, u32[]{:S(2)}, u32[]{:S(2)}) collective-permute-start(bf16[32,7168]{1,0:T(8,128)(2,1)} %collective-permute-done.4.refs_1_), channel_id=1, source_target_pairs={{0,4},{2,6},{8,0},{10,2},{16,8},{18,10},{24,16},{26,18},{28,24},{3... | collective-permute-start | bytes 1376264 | tf_op jit(solution)/shard_map/ppermute | solution.py:201
  23.8 0.8 fusion.41
  24.7 1.3 collective-permute-start.5
  26.0 9.6 %collective-permute-done.6.refs_5_ = bf16[32,7168]{1,0:T(8,128)(2,1)} collective-permute-done((bf16[32,7168]{1,0:T(8,128)(2,1)}, bf16[32,7168]{1,0:T(8,128)(2,1)}, u32[]{:S(2)}, u32[]{:S(2)}) %collective-permute-start.6) | collective-permute-done | bytes 458784 | tf_op jit(solution)/shard_map/ppermute | solution.py:201
  35.6 1.0 collective-permute-start.12
  36.7 1.1 collective-permute-start.1
  37.8 1.0 collective-permute-start.3
  38.9 1.0 collective-permute-start.11
  39.9 9.4 %collective-permute-done.12.refs_3_ = bf16[32,7168]{1,0:T(8,128)(2,1)} collective-permute-done((bf16[32,7168]{1,0:T(8,128)(2,1)}, bf16[32,7168]{1,0:T(8,128)(2,1)}, u32[]{:S(2)}, u32[]{:S(2)}) %collective-permute-start.12) | collective-permute-done | bytes 458784 | tf_op jit(solution)/shard_map/ppermute | solution.py:201
  49.3 1.0 collective-permute-start.14
  50.3 8.4 %shard_map.82 = (f32[3,2,32,512]{3,2,1,0:T(8,128)S(1)}, f32[3,2,32,512]{3,2,1,0:T(8,128)S(1)}, f32[3,2,32,128]{3,2,1,0:T(8,128)S(1)}) custom-call(s32[1]{0:T(128)S(1)} %bitcast.108, bf16[32,7168]{1,0:T(8,128)(2,1)S(1)} %get-tuple-element.63.refs_0_, bf16[32,7168]{1,0:T(8,128)(2,1)} %collective-permute-done.4.refs_1_, ...), custom_call_target="tpu_custom_call" | custom-call | flops 3170893824 | bytes 19267584 | tf_op jit(solution)/shard_map/pallas_call | solution.py:78
  58.7 0.8 copy-done.1
  59.5 0.8 copy-done.3
  60.3 1.6 %collective-permute-start.10 = (bf16[32,7168]{1,0:T(8,128)(2,1)}, bf16[32,7168]{1,0:T(8,128)(2,1)}, u32[]{:S(2)}, u32[]{:S(2)}) collective-permute-start(bf16[32,7168]{1,0:T(8,128)(2,1)} %collective-permute-done.3.refs_2_), channel_id=1, source_target_pairs={{0,4},{2,6},{8,0},{10,2},{16,8},{18,10},{24,16},{26,18},{28,24},{3... | collective-permute-start | bytes 1376264 | tf_op jit(solution)/shard_map/ppermute | solution.py:201
  62.3 0.6 fusion.54
  73.1 1.2 convolution_convert_fusion
  74.4 4.0 %collective-permute-start.17 = (bf16[8,7168]{1,0:T(8,128)(2,1)S(1)}, bf16[8,7168]{1,0:T(8,128)(2,1)S(1)}, u32[]{:S(2)}, u32[]{:S(2)}) collective-permute-start(bf16[8,7168]{1,0:T(8,128)(2,1)S(1)} %convolution_convert_fusion), channel_id=1, source_target_pairs={{0,28},{2,30},{8,20},{10,22},{16,12},{18,14},{24,4},{26,6},{28,0},... | collective-permute-start | bytes 344072 | tf_op jit(solution)/shard_map/ppermute | solution.py:201
  78.7 7.7 %shard_map.83 = (f32[2,2,32,512]{3,2,1,0:T(8,128)S(1)}, f32[2,2,32,512]{3,2,1,0:T(8,128)S(1)}, f32[2,2,32,128]{3,2,1,0:T(8,128)S(1)}) custom-call(s32[1]{0:T(128)S(1)} %bitcast.109, bf16[32,7168]{1,0:T(8,128)(2,1)} %collective-permute-done.1.refs_0_, bf16[32,7168]{1,0:T(8,128)(2,1)} %collective-permute-done.11.refs_1_, ...), custom_call_target="tpu_custom_call" | custom-call | flops 2113929216 | bytes 18350080 | tf_op jit(solution)/shard_map/pallas_call | solution.py:78
  86.4 1.6 %collective-permute-start.24 = (bf16[16,32,512]{2,1,0:T(8,128)(2,1)S(1)}, bf16[16,32,512]{2,1,0:T(8,128)(2,1)S(1)}, u32[]{:S(2)}, u32[]{:S(2)}) collective-permute-start(bf16[16,32,512]{2,1,0:T(8,128)(2,1)S(1)} %copy-done.9), channel_id=1, source_target_pairs={{0,1},{1,0},{2,3},{3,2},{4,5},{5,4},{6,7},{7,6},{8,9},{9,8},{10,11... | collective-permute-start | bytes 1572872 | tf_op jit(solution)/shard_map/ppermute | solution.py:314
  87.9 1.8 %collective-permute-start.15 = (bf16[32,7168]{1,0:T(8,128)(2,1)}, bf16[32,7168]{1,0:T(8,128)(2,1)S(1)}, u32[]{:S(2)}, u32[]{:S(2)}) collective-permute-start(bf16[32,7168]{1,0:T(8,128)(2,1)} %collective-permute-done.14.refs_3_), channel_id=1, source_target_pairs={{0,4},{2,6},{8,0},{10,2},{16,8},{18,10},{24,16},{26,18},{28,24},{3... | collective-permute-start | bytes 1376264 | tf_op jit(solution)/shard_map/ppermute | solution.py:201
  89.9 0.6 fusion
  91.1 8.2 %shard_map.84 = (f32[2,2,32,512]{3,2,1,0:T(8,128)S(1)}, f32[2,2,32,512]{3,2,1,0:T(8,128)}, f32[2,2,32,128]{3,2,1,0:T(8,128)S(1)}) custom-call(s32[1]{0:T(128)S(1)} %bitcast.110, bf16[32,7168]{1,0:T(8,128)(2,1)} %collective-permute-done.9.refs_0_, bf16[32,7168]{1,0:T(8,128)(2,1)S(1)} %collective-permute-done.16.refs_1_, ...), custom_call_target="tpu_custom_call" | custom-call | flops 2113929216 | bytes 18350080 | tf_op jit(solution)/shard_map/pallas_call | solution.py:78
  99.9 1.5 %maximum_select_fusion = bf16[16,64,512]{2,1,0:T(8,128)(2,1)} fusion(bf16[16,32,512]{2,1,0:T(8,128)(2,1)S(1)} %collective-permute-done.24, bf16[16,32,512]{2,1,0:T(8,128)(2,1)S(1)} %copy-done.9, pred[]{:T(512)S(6)} %eq.418), kind=kLoop, calls=%fused_computation.10 | loop fusion | flops 4718592 | bytes 2097153 | tf_op jit(solution)/shard_map/jit(_where)/select_n | solution.py:315
  101.4 0.8 add.162
  102.5 1.1 collective-permute-start.19
  103.8 2.5 %collective-permute-done.19 = f32[16,64]{1,0:T(8,128)S(1)} collective-permute-done((f32[16,64]{1,0:T(8,128)S(1)}, f32[16,64]{1,0:T(8,128)S(1)}, u32[]{:S(2)}, u32[]{:S(2)}) %collective-permute-start.19) | collective-permute-done | bytes 4128 | tf_op jit(solution)/shard_map/ppermute | solution.py:302
  106.4 8.0 %shard_map.85 = (f32[1,2,32,512]{3,2,1,0:T(8,128)S(1)}, f32[1,2,32,512]{3,2,1,0:T(8,128)S(1)}, f32[1,2,32,128]{3,2,1,0:T(8,128)}) custom-call(s32[1]{0:T(128)S(1)} %bitcast.111, bf16[32,7168]{1,0:T(8,128)(2,1)S(1)} %collective-permute-done.13.refs_0_, bf16[32,7168]{1,0:T(8,128)(2,1)S(1)} %collective-permute-done.15.refs_1_, bf16[14336,512]{1,0:T(8,128)(2,1)} %refs_2_.1, ...), custom_call_target="tpu_custom_call" | custom-call | flops 1056964608 | bytes 17432576 | tf_op jit(solution)/shard_map/pallas_call | solution.py:78
  114.9 1.9 %collective-permute-start.21 = (bf16[2,16,64]{2,1,0:T(8,128)(2,1)S(1)}, bf16[2,16,64]{2,1,0:T(8,128)(2,1)S(1)}, u32[]{:S(2)}, u32[]{:S(2)}) collective-permute-start(bf16[2,16,64]{2,1,0:T(8,128)(2,1)S(1)} %maximum_select_fusion.7), channel_id=1, source_target_pairs={{0,4},{2,6},{4,0},{6,2},{8,12},{10,14},{12,8},{14,10},{16,20},{18,... | collective-permute-start | bytes 12296 | tf_op jit(solution)/shard_map/ppermute | solution.py:305
  116.8 1.8 %collective-permute-done.21 = bf16[2,16,64]{2,1,0:T(8,128)(2,1)S(1)} collective-permute-done((bf16[2,16,64]{2,1,0:T(8,128)(2,1)S(1)}, bf16[2,16,64]{2,1,0:T(8,128)(2,1)S(1)}, u32[]{:S(2)}, u32[]{:S(2)}) %collective-permute-start.21) | collective-permute-done | bytes 4128 | tf_op jit(solution)/shard_map/ppermute | solution.py:305
  118.6 2.3 %collective-permute-start.22 = (bf16[4,16,64]{2,1,0:T(8,128)(2,1)S(1)}, bf16[4,16,64]{2,1,0:T(8,128)(2,1)S(1)}, u32[]{:S(2)}, u32[]{:S(2)}) collective-permute-start(bf16[4,16,64]{2,1,0:T(8,128)(2,1)S(1)} %maximum_select_fusion.5), channel_id=1, source_target_pairs={{0,8},{2,10},{4,12},{6,14},{8,0},{10,2},{12,4},{14,6},{16,24},{18,... | collective-permute-start | bytes 24584 | tf_op jit(solution)/shard_map/ppermute | solution.py:305
  120.9 1.7 %collective-permute-done.22 = bf16[4,16,64]{2,1,0:T(8,128)(2,1)S(1)} collective-permute-done((bf16[4,16,64]{2,1,0:T(8,128)(2,1)S(1)}, bf16[4,16,64]{2,1,0:T(8,128)(2,1)S(1)}, u32[]{:S(2)}, u32[]{:S(2)}) %collective-permute-start.22) | collective-permute-done | bytes 8224 | tf_op jit(solution)/shard_map/ppermute | solution.py:305
  122.6 3.9 %collective-permute-start.23 = (bf16[8,16,64]{2,1,0:T(8,128)(2,1)S(1)}, bf16[8,16,64]{2,1,0:T(8,128)(2,1)S(1)}, u32[]{:S(2)}, u32[]{:S(2)}) collective-permute-start(bf16[8,16,64]{2,1,0:T(8,128)(2,1)S(1)} %maximum_select_fusion.3), channel_id=1, source_target_pairs={{0,16},{2,18},{4,20},{6,22},{8,24},{10,26},{12,28},{14,30},{16,0},... | collective-permute-start | bytes 49160 | tf_op jit(solution)/shard_map/ppermute | solution.py:305
  126.6 1.9 %collective-permute-done.23 = bf16[8,16,64]{2,1,0:T(8,128)(2,1)S(1)} collective-permute-done((bf16[8,16,64]{2,1,0:T(8,128)(2,1)S(1)}, bf16[8,16,64]{2,1,0:T(8,128)(2,1)S(1)}, u32[]{:S(2)}, u32[]{:S(2)}) %collective-permute-start.23) | collective-permute-done | bytes 16416 | tf_op jit(solution)/shard_map/ppermute | solution.py:305
  128.5 1.4 select_add_fusion
  129.9 0.7 add.161
  130.7 1.0 select_convert_fusion.1
  131.7 2.1 %collective-permute-start.27 = (bf16[1,2,32,512]{3,2,1,0:T(8,128)(2,1)S(1)}, bf16[1,2,32,512]{3,2,1,0:T(8,128)(2,1)S(1)}, u32[]{:S(2)}, u32[]{:S(2)}) collective-permute-start(bf16[1,2,32,512]{3,2,1,0:T(8,128)(2,1)S(1)} %select_convert_fusion.1), channel_id=1, source_target_pairs={{0,1},{1,0},{2,3},{3,2},{4,5},{5,4},{6,7},{7,6},{8,9},{9,8},{10,11... | collective-permute-start | bytes 196616 | tf_op jit(solution)/shard_map/ppermute | solution.py:349
  134.2 2.0 %collective-permute-done.27 = bf16[1,2,32,512]{3,2,1,0:T(8,128)(2,1)S(1)} collective-permute-done((bf16[1,2,32,512]{3,2,1,0:T(8,128)(2,1)S(1)}, bf16[1,2,32,512]{3,2,1,0:T(8,128)(2,1)S(1)}, u32[]{:S(2)}, u32[]{:S(2)}) %collective-permute-start.27) | collective-permute-done | bytes 65568 | tf_op jit(solution)/shard_map/ppermute | solution.py:349
  136.3 1.0 add.167
  137.4 2.3 %collective-permute-start.30 = (bf16[3,2,32,512]{3,2,1,0:T(8,128)(2,1)S(1)}, bf16[3,2,32,512]{3,2,1,0:T(8,128)(2,1)S(1)}, u32[]{:S(2)}, u32[]{:S(2)}) collective-permute-start(bf16[3,2,32,512]{3,2,1,0:T(8,128)(2,1)S(1)} %select_convert_fusion), channel_id=1, source_target_pairs={{0,1},{1,0},{2,3},{3,2},{4,5},{5,4},{6,7},{7,6},{8,9},{9,8},{10,11... | collective-permute-start | bytes 589832 | tf_op jit(solution)/shard_map/ppermute | solution.py:349
  139.8 3.6 %collective-permute-done.30 = bf16[3,2,32,512]{3,2,1,0:T(8,128)(2,1)S(1)} collective-permute-done((bf16[3,2,32,512]{3,2,1,0:T(8,128)(2,1)S(1)}, bf16[3,2,32,512]{3,2,1,0:T(8,128)(2,1)S(1)}, u32[]{:S(2)}, u32[]{:S(2)}) %collective-permute-start.30) | collective-permute-done | bytes 196640 | tf_op jit(solution)/shard_map/ppermute | solution.py:349
  144.0 0.7 pad_maximum_fusion.2
  (125 shorter events, 7.6 us)
Async XLA Ops:
  0.7 7.2 %copy-start.7 = (bf16[32,14336]{1,0:T(8,128)(2,1)S(1)}, bf16[32,14336]{1,0:T(8,128)(2,1)}, u32[]{:S(2)}) copy-start(bf16[32,14336]{1,0:T(8,128)(2,1)} %param.9) | copy-start | bytes 2752516
  7.4 5.7 %copy-start = (bf16[1,64,14336]{2,1,0:T(8,128)(2,1)S(1)}, bf16[1,64,14336]{2,1,0:T(8,128)(2,1)}, u32[]{:S(2)}) copy-start(bf16[1,64,14336]{2,1,0:T(8,128)(2,1)} %param.11) | copy-start | bytes 5505028
  7.4 42.9 %collective-permute-start.7 = (bf16[7168,512]{1,0:T(8,128)(2,1)}, bf16[7168,512]{1,0:T(8,128)(2,1)}, u32[]{:S(2)}, u32[]{:S(2)}) collective-permute-start(bf16[7168,512]{1,0:T(8,128)(2,1)} %constant_dynamic-slice_fusion), channel_id=1, source_target_pairs={{0,2},{2,0},{8,10},{10,8},{16,18},{18,16},{24,26},{26,24},{28,30},... | collective-permute-start | bytes 22020104 | tf_op jit(solution)/shard_map/ppermute | solution.py:201
  10.4 4.6 %copy-start.12 = (s32[512,1]{0,1:T(1,128)S(1)}, s32[512,1]{0,1:T(1,128)}, u32[]{:S(2)}) copy-start(s32[512,1]{0,1:T(1,128)} %param.13) | copy-start | bytes 6148
  10.4 4.6 %copy-start.13 = (s32[16]{0:T(128)S(1)}, s32[16]{0:T(128)}, u32[]{:S(2)}) copy-start(s32[16]{0:T(128)} %param.14) | copy-start | bytes 196
  10.4 14.2 %collective-permute-start = (bf16[32,7168]{1,0:T(8,128)(2,1)S(1)}, bf16[32,7168]{1,0:T(8,128)(2,1)}, u32[]{:S(2)}, u32[]{:S(2)}) collective-permute-start(bf16[32,7168]{1,0:T(8,128)(2,1)S(1)} %get-tuple-element.63.refs_0_), channel_id=1, source_target_pairs={{0,8},{2,10},{8,16},{10,18},{16,24},{18,26},{24,28},{26,30},{28,20... | collective-permute-start | bytes 1376264 | tf_op jit(solution)/shard_map/ppermute | solution.py:201
  13.1 23.6 %collective-permute-start.2 = (bf16[32,7168]{1,0:T(8,128)(2,1)S(1)}, bf16[32,7168]{1,0:T(8,128)(2,1)}, u32[]{:S(2)}, u32[]{:S(2)}) collective-permute-start(bf16[32,7168]{1,0:T(8,128)(2,1)S(1)} %get-tuple-element.63.refs_0_), channel_id=1, source_target_pairs={{0,4},{2,6},{8,0},{10,2},{16,8},{18,10},{24,16},{26,18},{28,24},{3... | collective-permute-start | bytes 1376264 | tf_op jit(solution)/shard_map/ppermute | solution.py:201
  14.5 23.3 %collective-permute-start.8 = (bf16[64,7168]{1,0:T(8,128)(2,1)}, bf16[64,7168]{1,0:T(8,128)(2,1)S(1)}, u32[]{:S(2)}, u32[]{:S(2)}) collective-permute-start(bf16[64,7168]{1,0:T(8,128)(2,1)} %get-tuple-element.62), channel_id=1, source_target_pairs={{0,2},{2,0},{8,10},{10,8},{16,18},{18,16},{24,26},{26,24},{28,30},... | collective-permute-start | bytes 2752520 | tf_op jit(solution)/shard_map/ppermute | solution.py:201
  14.6 6.2 %collective-permute-start.4 = (bf16[32,7168]{1,0:T(8,128)(2,1)}, bf16[32,7168]{1,0:T(8,128)(2,1)}, u32[]{:S(2)}, u32[]{:S(2)}) collective-permute-start(bf16[32,7168]{1,0:T(8,128)(2,1)} %get-tuple-element.64), channel_id=1, source_target_pairs={{0,2},{2,0},{8,10},{10,8},{16,18},{18,16},{24,26},{26,24},{28,30},... | collective-permute-start | bytes 1376264 | tf_op jit(solution)/shard_map/ppermute | solution.py:201
  20.8 14.8 %collective-permute-start.6 = (bf16[32,7168]{1,0:T(8,128)(2,1)}, bf16[32,7168]{1,0:T(8,128)(2,1)}, u32[]{:S(2)}, u32[]{:S(2)}) collective-permute-start(bf16[32,7168]{1,0:T(8,128)(2,1)} %collective-permute-done.4.refs_1_), channel_id=1, source_target_pairs={{0,4},{2,6},{8,0},{10,2},{16,8},{18,10},{24,16},{26,18},{28,24},{3... | collective-permute-start | bytes 1376264 | tf_op jit(solution)/shard_map/ppermute | solution.py:201
  24.7 14.2 %collective-permute-start.5 = (bf16[32,7168]{1,0:T(8,128)(2,1)}, bf16[32,7168]{1,0:T(8,128)(2,1)}, u32[]{:S(2)}, u32[]{:S(2)}) collective-permute-start(bf16[32,7168]{1,0:T(8,128)(2,1)} %collective-permute-done.4.refs_1_), channel_id=1, source_target_pairs={{0,8},{2,10},{8,16},{10,18},{16,24},{18,26},{24,28},{26,30},{28,20... | collective-permute-start | bytes 1376264 | tf_op jit(solution)/shard_map/ppermute | solution.py:201
  35.6 13.8 %collective-permute-start.12 = (bf16[32,7168]{1,0:T(8,128)(2,1)}, bf16[32,7168]{1,0:T(8,128)(2,1)}, u32[]{:S(2)}, u32[]{:S(2)}) collective-permute-start(bf16[32,7168]{1,0:T(8,128)(2,1)} %collective-permute-done.6.refs_5_), channel_id=1, source_target_pairs={{0,4},{2,6},{8,0},{10,2},{16,8},{18,10},{24,16},{26,18},{28,24},{3... | collective-permute-start | bytes 1376264 | tf_op jit(solution)/shard_map/ppermute | solution.py:201
  36.7 23.5 %collective-permute-start.1 = (bf16[32,7168]{1,0:T(8,128)(2,1)}, bf16[32,7168]{1,0:T(8,128)(2,1)}, u32[]{:S(2)}, u32[]{:S(2)}) collective-permute-start(bf16[32,7168]{1,0:T(8,128)(2,1)} %collective-permute-done.refs_2_), channel_id=1, source_target_pairs={{0,8},{2,10},{8,16},{10,18},{16,24},{18,26},{24,28},{26,30},{28,20... | collective-permute-start | bytes 1376264 | tf_op jit(solution)/shard_map/ppermute | solution.py:201
  37.8 22.4 %collective-permute-start.3 = (bf16[32,7168]{1,0:T(8,128)(2,1)}, bf16[32,7168]{1,0:T(8,128)(2,1)}, u32[]{:S(2)}, u32[]{:S(2)}) collective-permute-start(bf16[32,7168]{1,0:T(8,128)(2,1)} %collective-permute-done.2.refs_4_), channel_id=1, source_target_pairs={{0,4},{2,6},{8,0},{10,2},{16,8},{18,10},{24,16},{26,18},{28,24},{3... | collective-permute-start | bytes 1376264 | tf_op jit(solution)/shard_map/ppermute | solution.py:201
  38.9 39.6 %collective-permute-start.11 = (bf16[32,7168]{1,0:T(8,128)(2,1)}, bf16[32,7168]{1,0:T(8,128)(2,1)}, u32[]{:S(2)}, u32[]{:S(2)}) collective-permute-start(bf16[32,7168]{1,0:T(8,128)(2,1)} %collective-permute-done.5.refs_3_), channel_id=1, source_target_pairs={{0,8},{2,10},{8,16},{10,18},{16,24},{18,26},{24,28},{26,30},{28,20... | collective-permute-start | bytes 1376264 | tf_op jit(solution)/shard_map/ppermute | solution.py:201
  49.3 37.0 %collective-permute-start.14 = (bf16[32,7168]{1,0:T(8,128)(2,1)}, bf16[32,7168]{1,0:T(8,128)(2,1)}, u32[]{:S(2)}, u32[]{:S(2)}) collective-permute-start(bf16[32,7168]{1,0:T(8,128)(2,1)} %collective-permute-done.12.refs_3_), channel_id=1, source_target_pairs={{0,4},{2,6},{8,0},{10,2},{16,8},{18,10},{24,16},{26,18},{28,24},{3... | collective-permute-start | bytes 1376264 | tf_op jit(solution)/shard_map/ppermute | solution.py:201
  58.7 0.8 copy-start.1
  59.5 0.8 copy-start.3
  60.3 27.6 %collective-permute-start.10 = (bf16[32,7168]{1,0:T(8,128)(2,1)}, bf16[32,7168]{1,0:T(8,128)(2,1)}, u32[]{:S(2)}, u32[]{:S(2)}) collective-permute-start(bf16[32,7168]{1,0:T(8,128)(2,1)} %collective-permute-done.3.refs_2_), channel_id=1, source_target_pairs={{0,4},{2,6},{8,0},{10,2},{16,8},{18,10},{24,16},{26,18},{28,24},{3... | collective-permute-start | bytes 1376264 | tf_op jit(solution)/shard_map/ppermute | solution.py:201
  61.8 27.9 %collective-permute-start.9 = (bf16[32,7168]{1,0:T(8,128)(2,1)}, bf16[32,7168]{1,0:T(8,128)(2,1)}, u32[]{:S(2)}, u32[]{:S(2)}) collective-permute-start(bf16[32,7168]{1,0:T(8,128)(2,1)} %collective-permute-done.1.refs_0_), channel_id=1, source_target_pairs={{0,8},{2,10},{8,16},{10,18},{16,24},{18,26},{24,28},{26,30},{28,20... | collective-permute-start | bytes 1376264 | tf_op jit(solution)/shard_map/ppermute | solution.py:201
  74.4 12.0 %copy-start.9 = (bf16[16,32,512]{2,1,0:T(8,128)(2,1)S(1)}, bf16[16,32,512]{2,1,0:T(8,128)(2,1)}, u32[]{:S(2)}) copy-start(bf16[16,32,512]{2,1,0:T(8,128)(2,1)} %param.12) | copy-start | bytes 1572868
  74.4 15.5 %copy-start.8 = (bf16[64,7168]{1,0:T(8,128)(2,1)S(1)}, bf16[64,7168]{1,0:T(8,128)(2,1)}, u32[]{:S(2)}) copy-start(bf16[64,7168]{1,0:T(8,128)(2,1)} %get-tuple-element.61) | copy-start | bytes 2752516
  74.4 15.5 %collective-permute-start.17 = (bf16[8,7168]{1,0:T(8,128)(2,1)S(1)}, bf16[8,7168]{1,0:T(8,128)(2,1)S(1)}, u32[]{:S(2)}, u32[]{:S(2)}) collective-permute-start(bf16[8,7168]{1,0:T(8,128)(2,1)S(1)} %convolution_convert_fusion), channel_id=1, source_target_pairs={{0,28},{2,30},{8,20},{10,22},{16,12},{18,14},{24,4},{26,6},{28,0},... | collective-permute-start | bytes 344072 | tf_op jit(solution)/shard_map/ppermute | solution.py:201
  78.5 12.2 %collective-permute-start.16 = (bf16[32,7168]{1,0:T(8,128)(2,1)}, bf16[32,7168]{1,0:T(8,128)(2,1)S(1)}, u32[]{:S(2)}, u32[]{:S(2)}) collective-permute-start(bf16[32,7168]{1,0:T(8,128)(2,1)} %collective-permute-done.11.refs_1_), channel_id=1, source_target_pairs={{0,8},{2,10},{8,16},{10,18},{16,24},{18,26},{24,28},{26,30},{28,20... | collective-permute-start | bytes 1376264 | tf_op jit(solution)/shard_map/ppermute | solution.py:201
  86.3 4.3 %copy-start.4 = (f32[3,2,32,512]{3,2,1,0:T(8,128)S(1)}, f32[3,2,32,512]{3,2,1,0:T(8,128)}, u32[]{:S(2)}) copy-start(f32[3,2,32,512]{3,2,1,0:T(8,128)} %copy-done.3) | copy-start | bytes 1179652
  86.4 13.5 %collective-permute-start.24 = (bf16[16,32,512]{2,1,0:T(8,128)(2,1)S(1)}, bf16[16,32,512]{2,1,0:T(8,128)(2,1)S(1)}, u32[]{:S(2)}, u32[]{:S(2)}) collective-permute-start(bf16[16,32,512]{2,1,0:T(8,128)(2,1)S(1)} %copy-done.9), channel_id=1, source_target_pairs={{0,1},{1,0},{2,3},{3,2},{4,5},{5,4},{6,7},{7,6},{8,9},{9,8},{10,11... | collective-permute-start | bytes 1572872 | tf_op jit(solution)/shard_map/ppermute | solution.py:314
  87.9 11.4 %collective-permute-start.15 = (bf16[32,7168]{1,0:T(8,128)(2,1)}, bf16[32,7168]{1,0:T(8,128)(2,1)S(1)}, u32[]{:S(2)}, u32[]{:S(2)}) collective-permute-start(bf16[32,7168]{1,0:T(8,128)(2,1)} %collective-permute-done.14.refs_3_), channel_id=1, source_target_pairs={{0,4},{2,6},{8,0},{10,2},{16,8},{18,10},{24,16},{26,18},{28,24},{3... | collective-permute-start | bytes 1376264 | tf_op jit(solution)/shard_map/ppermute | solution.py:201
  89.7 9.6 %collective-permute-start.13 = (bf16[32,7168]{1,0:T(8,128)(2,1)}, bf16[32,7168]{1,0:T(8,128)(2,1)S(1)}, u32[]{:S(2)}, u32[]{:S(2)}) collective-permute-start(bf16[32,7168]{1,0:T(8,128)(2,1)} %collective-permute-done.9.refs_0_), channel_id=1, source_target_pairs={{0,8},{2,10},{8,16},{10,18},{16,24},{18,26},{24,28},{26,30},{28,20... | collective-permute-start | bytes 1376264 | tf_op jit(solution)/shard_map/ppermute | solution.py:201
  90.6 10.8 %collective-permute-start.25 = (f32[3,2,32,512]{3,2,1,0:T(8,128)S(1)}, f32[3,2,32,512]{3,2,1,0:T(8,128)S(1)}, u32[]{:S(2)}, u32[]{:S(2)}) collective-permute-start(f32[3,2,32,512]{3,2,1,0:T(8,128)S(1)} %copy-done.4), channel_id=1, source_target_pairs={{0,2},{2,0},{8,10},{10,8},{16,18},{18,16},{24,26},{26,24},{28,30},... | collective-permute-start | bytes 1179656 | tf_op jit(solution)/shard_map/ppermute | solution.py:201
  90.6 11.6 %collective-permute-start.28 = (f32[2,2,32,512]{3,2,1,0:T(8,128)S(1)}, f32[2,2,32,512]{3,2,1,0:T(8,128)S(1)}, u32[]{:S(2)}, u32[]{:S(2)}) collective-permute-start(f32[2,2,32,512]{3,2,1,0:T(8,128)S(1)} %get-tuple-element.52), channel_id=1, source_target_pairs={{0,2},{2,0},{8,10},{10,8},{16,18},{18,16},{24,26},{26,24},{28,30},... | collective-permute-start | bytes 786440 | tf_op jit(solution)/shard_map/ppermute | solution.py:201
  99.3 2.1 %copy-start.2 = (f32[3,2,32,512]{3,2,1,0:T(8,128)S(1)}, f32[3,2,32,512]{3,2,1,0:T(8,128)}, u32[]{:S(2)}) copy-start(f32[3,2,32,512]{3,2,1,0:T(8,128)} %copy-done.1) | copy-start | bytes 1179652
  99.7 2.6 %collective-permute-start.18 = (f32[32,64]{1,0:T(8,128)S(1)}, f32[32,64]{1,0:T(8,128)S(1)}, u32[]{:S(2)}, u32[]{:S(2)}) collective-permute-start(f32[32,64]{1,0:T(8,128)S(1)} %fusion.20), channel_id=1, source_target_pairs={{0,2},{2,0},{8,10},{10,8},{16,18},{18,16},{24,26},{26,24},{28,30},... | collective-permute-start | bytes 24584 | tf_op jit(solution)/shard_map/ppermute | solution.py:201
  102.5 3.7 %collective-permute-start.19 = (f32[16,64]{1,0:T(8,128)S(1)}, f32[16,64]{1,0:T(8,128)S(1)}, u32[]{:S(2)}, u32[]{:S(2)}) collective-permute-start(f32[16,64]{1,0:T(8,128)S(1)} %slice_select_fusion.12), channel_id=1, source_target_pairs={{0,1},{1,0},{2,3},{3,2},{4,5},{5,4},{6,7},{7,6},{8,9},{9,8},{10,11... | collective-permute-start | bytes 12296 | tf_op jit(solution)/shard_map/ppermute | solution.py:302
  103.7 32.6 %collective-permute-start.29 = (f32[2,2,32,512]{3,2,1,0:T(8,128)}, f32[2,2,32,512]{3,2,1,0:T(8,128)}, u32[]{:S(2)}, u32[]{:S(2)}) collective-permute-start(f32[2,2,32,512]{3,2,1,0:T(8,128)} %get-tuple-element.54), channel_id=1, source_target_pairs={{0,2},{2,0},{8,10},{10,8},{16,18},{18,16},{24,26},{26,24},{28,30},... | collective-permute-start | bytes 786440 | tf_op jit(solution)/shard_map/ppermute | solution.py:201
  106.3 22.3 %copy-start.10 = (pred[8,32,16]{2,1,0:T(8,128)(4,1)S(1)}, pred[8,32,16]{2,1,0:T(8,128)(4,1)}, u32[]{:S(2)}) copy-start(pred[8,32,16]{2,1,0:T(8,128)(4,1)} %get-tuple-element.101) | copy-start | bytes 12292
  106.3 22.3 %copy-start.11 = (pred[8,32,16]{2,1,0:T(8,128)(4,1)S(1)}, pred[8,32,16]{2,1,0:T(8,128)(4,1)}, u32[]{:S(2)}) copy-start(pred[8,32,16]{2,1,0:T(8,128)(4,1)} %get-tuple-element.102) | copy-start | bytes 12292
  106.3 8.6 %collective-permute-start.20 = (bf16[1,16,64]{2,1,0:T(8,128)(2,1)S(1)}, bf16[1,16,64]{2,1,0:T(8,128)(2,1)S(1)}, u32[]{:S(2)}, u32[]{:S(2)}) collective-permute-start(bf16[1,16,64]{2,1,0:T(8,128)(2,1)S(1)} %bitcast.118), channel_id=1, source_target_pairs={{0,2},{2,0},{4,6},{6,4},{8,10},{10,8},{12,14},{14,12},{16,18},{18,... | collective-permute-start | bytes 6152 | tf_op jit(solution)/shard_map/ppermute | solution.py:305
  114.4 19.4 %copy-start.5 = (bf16[16,64,512]{2,1,0:T(8,128)(2,1)S(1)}, bf16[16,64,512]{2,1,0:T(8,128)(2,1)}, u32[]{:S(2)}) copy-start(bf16[16,64,512]{2,1,0:T(8,128)(2,1)} %maximum_select_fusion) | copy-start | bytes 3145732
  114.4 16.3 %collective-permute-start.26 = (f32[1,2,32,512]{3,2,1,0:T(8,128)S(1)}, f32[1,2,32,512]{3,2,1,0:T(8,128)S(1)}, u32[]{:S(2)}, u32[]{:S(2)}) collective-permute-start(f32[1,2,32,512]{3,2,1,0:T(8,128)S(1)} %get-tuple-element.50), channel_id=1, source_target_pairs={{0,2},{2,0},{8,10},{10,8},{16,18},{18,16},{24,26},{26,24},{28,30},... | collective-permute-start | bytes 393224 | tf_op jit(solution)/shard_map/ppermute | solution.py:201
  114.9 3.7 %collective-permute-start.21 = (bf16[2,16,64]{2,1,0:T(8,128)(2,1)S(1)}, bf16[2,16,64]{2,1,0:T(8,128)(2,1)S(1)}, u32[]{:S(2)}, u32[]{:S(2)}) collective-permute-start(bf16[2,16,64]{2,1,0:T(8,128)(2,1)S(1)} %maximum_select_fusion.7), channel_id=1, source_target_pairs={{0,4},{2,6},{4,0},{6,2},{8,12},{10,14},{12,8},{14,10},{16,20},{18,... | collective-permute-start | bytes 12296 | tf_op jit(solution)/shard_map/ppermute | solution.py:305
  118.6 4.0 %collective-permute-start.22 = (bf16[4,16,64]{2,1,0:T(8,128)(2,1)S(1)}, bf16[4,16,64]{2,1,0:T(8,128)(2,1)S(1)}, u32[]{:S(2)}, u32[]{:S(2)}) collective-permute-start(bf16[4,16,64]{2,1,0:T(8,128)(2,1)S(1)} %maximum_select_fusion.5), channel_id=1, source_target_pairs={{0,8},{2,10},{4,12},{6,14},{8,0},{10,2},{12,4},{14,6},{16,24},{18,... | collective-permute-start | bytes 24584 | tf_op jit(solution)/shard_map/ppermute | solution.py:305
  122.6 5.8 %collective-permute-start.23 = (bf16[8,16,64]{2,1,0:T(8,128)(2,1)S(1)}, bf16[8,16,64]{2,1,0:T(8,128)(2,1)S(1)}, u32[]{:S(2)}, u32[]{:S(2)}) collective-permute-start(bf16[8,16,64]{2,1,0:T(8,128)(2,1)S(1)} %maximum_select_fusion.3), channel_id=1, source_target_pairs={{0,16},{2,18},{4,20},{6,22},{8,24},{10,26},{12,28},{14,30},{16,0},... | collective-permute-start | bytes 49160 | tf_op jit(solution)/shard_map/ppermute | solution.py:305
  130.7 5.5 %copy-start.6 = (f32[3,2,32,512]{3,2,1,0:T(8,128)S(1)}, f32[3,2,32,512]{3,2,1,0:T(8,128)}, u32[]{:S(2)}) copy-start(f32[3,2,32,512]{3,2,1,0:T(8,128)} %add.162) | copy-start | bytes 1179652
  131.7 4.5 %collective-permute-start.27 = (bf16[1,2,32,512]{3,2,1,0:T(8,128)(2,1)S(1)}, bf16[1,2,32,512]{3,2,1,0:T(8,128)(2,1)S(1)}, u32[]{:S(2)}, u32[]{:S(2)}) collective-permute-start(bf16[1,2,32,512]{3,2,1,0:T(8,128)(2,1)S(1)} %select_convert_fusion.1), channel_id=1, source_target_pairs={{0,1},{1,0},{2,3},{3,2},{4,5},{5,4},{6,7},{7,6},{8,9},{9,8},{10,11... | collective-permute-start | bytes 196616 | tf_op jit(solution)/shard_map/ppermute | solution.py:349
  137.4 6.0 %collective-permute-start.30 = (bf16[3,2,32,512]{3,2,1,0:T(8,128)(2,1)S(1)}, bf16[3,2,32,512]{3,2,1,0:T(8,128)(2,1)S(1)}, u32[]{:S(2)}, u32[]{:S(2)}) collective-permute-start(bf16[3,2,32,512]{3,2,1,0:T(8,128)(2,1)S(1)} %select_convert_fusion), channel_id=1, source_target_pairs={{0,1},{1,0},{2,3},{3,2},{4,5},{5,4},{6,7},{7,6},{8,9},{9,8},{10,11... | collective-permute-start | bytes 589832 | tf_op jit(solution)/shard_map/ppermute | solution.py:349

commit v3 on v2

v3 whole, which is shorter than its diff:
```python
import functools

import jax
import jax.numpy as jnp
import numpy as np
from jax import lax
from jax.experimental import pallas as pl
from jax.experimental.pallas import tpu as pltpu
from jax.sharding import PartitionSpec as P

MOST = 2
INNER = ("mp", "sub")
SWAP = [(0, 1), (1, 0)]


def tile_of(depth, most=512):
    parts = 1
    while depth % parts or (depth // parts) % 128 or depth // parts > most:
        parts += 1
    return depth // parts


def rows_kernel(count, extra, with_base, with_low, lane_ref, *refs):
    pieces, refs = refs[:count], refs[count:]
    more, refs = refs[:extra], refs[extra:]
    weights, refs = refs[: 2 * with_base], refs[2 * with_base :]
    factors, refs = refs[: 2 * with_low], refs[2 * with_low :]
    outs = refs[: 2 * with_base + with_low + extra]
    sums = refs[2 * with_base + with_low + extra :]
    step = pl.program_id(0)

    @pl.when(step == 0)
    def _():
        for total in sums:
            total[...] = jnp.zeros_like(total)

    rows = jnp.concatenate([piece[...] for piece in pieces], axis=0)
    for weight, total in zip(weights, sums):
        total[...] += jnp.dot(rows, weight[...], preferred_element_type=jnp.float32)
    if with_low:
        table = jnp.concatenate([factor[...] for factor in factors], axis=0)
        for values, total in zip([rows] + [m[...] for m in more], sums[2 * with_base :]):
            total[...] += lax.dot_general(
                values, table, (((1,), (1,)), ((), ())), preferred_element_type=jnp.float32
            )

    @pl.when(step == pl.num_programs(0) - 1)
    def _():
        height = pieces[0].shape[0]
        for out, total in zip(outs[: 2 * with_base + with_low], sums):
            for index in range(count):
                lane = jnp.bitwise_xor(lane_ref[0], index % 2)
                out[index // 2, lane] = total[index * height : (index + 1) * height, :]
        for out, total in zip(outs[2 * with_base + with_low :], sums[2 * with_base + with_low :]):
            out[...] = total[...]


def rows_product(lane, pieces, weights=(), factors=(), more=()):
    count = len(pieces)
    row_count, depth = pieces[0].shape
    tile = tile_of(depth)
    tiles = depth // tile
    total = count * row_count
    in_specs = [pl.BlockSpec((row_count, tile), lambda i, lane: (0, i))] * count
    in_specs += [pl.BlockSpec((m.shape[0], tile), lambda i, lane: (0, i)) for m in more]
    in_specs += [pl.BlockSpec((tile, w.shape[1]), lambda i, lane: (lane[0] * tiles + i, 0)) for w in weights]
    in_specs += [pl.BlockSpec((f.shape[0], tile), lambda i, lane: (0, lane[0] * tiles + i)) for f in factors]
    sizes = [w.shape[1] for w in weights]
    if factors:
        sizes.append(sum(f.shape[0] for f in factors))
    out_specs = [
        pl.BlockSpec((count // 2, 2, row_count, size), lambda i, lane: (0, 0, 0, 0)) for size in sizes
    ]
    out_shape = [
        jax.ShapeDtypeStruct((count // 2, 2, row_count, size), jnp.float32) for size in sizes
    ]
    scratch = [pltpu.VMEM((total, size), jnp.float32) for size in sizes]
    for m in more:
        out_specs.append(pl.BlockSpec((m.shape[0], sizes[-1]), lambda i, lane: (0, 0)))
        out_shape.append(jax.ShapeDtypeStruct((m.shape[0], sizes[-1]), jnp.float32))
        scratch.append(pltpu.VMEM((m.shape[0], sizes[-1]), jnp.float32))
    return pl.pallas_call(
        functools.partial(rows_kernel, count, len(more), int(bool(weights)), int(bool(factors))),
        grid_spec=pltpu.PrefetchScalarGridSpec(
            num_scalar_prefetch=1,
            grid=(tiles,),
            in_specs=in_specs,
            out_specs=out_specs,
            scratch_shapes=scratch,
        ),
        out_shape=out_shape,
        compiler_params=pltpu.CompilerParams(vmem_limit_bytes=40 * 2**20),
        cost_estimate=pl.CostEstimate(
            flops=total * depth * sum(sizes) // 8,
            bytes_accessed=depth * sum(sizes) // 4,
            transcendentals=0,
        ),
    )(lane, *pieces, *more, *weights, *factors)


def hidden_of(gate, up):
    return (jax.nn.silu(gate.astype(jnp.float32)) * up.astype(jnp.float32)).astype(jnp.bfloat16)


def slots_of(row_adapter_index, adapter_storage_slot):
    names = jnp.arange(adapter_storage_slot.shape[0], dtype=jnp.int32)
    same = row_adapter_index == names[None, :]
    return jnp.sum(jnp.where(same, adapter_storage_slot[None, :], 0), axis=1)


def gathered(
    gate_activation,
    up_activation,
    down_base_weight,
    first_factor_table,
    second_factor_table,
    row_adapter_index,
    adapter_storage_slot,
):
    hidden = hidden_of(gate_activation, up_activation)
    row_count = hidden.shape[0]
    owners = lax.axis_size("wide")
    local_adapter = first_factor_table.shape[0]
    slots = local_adapter * owners
    rank_portion = second_factor_table.shape[1]
    home = lax.axis_index("wide")
    slot_all = slots_of(row_adapter_index, adapter_storage_slot)
    blocks = slot_all.reshape(owners, row_count)
    order = jnp.arange(row_count, dtype=jnp.int32)
    earlier = (blocks[:, :, None] == blocks[:, None, :]) & (order[None, :] < order[:, None])
    position = jnp.sum(earlier.astype(jnp.int32), axis=2)
    rows = lax.all_gather(hidden, "wide", axis=0, tiled=True)
    base = jnp.dot(rows, down_base_weight, preferred_element_type=jnp.float32)
    low = jnp.einsum("re,nqe->nrq", rows, first_factor_table, preferred_element_type=jnp.float32)
    low = low.reshape(local_adapter, owners, row_count, low.shape[2])
    own = home * local_adapter + jnp.arange(local_adapter, dtype=jnp.int32)
    kept = []
    for item in range(MOST):
        mask = (blocks[None] == own[:, None, None]) & (position == item)[None]
        kept.append(jnp.sum(jnp.where(mask[..., None], low, 0), axis=2))
    low = lax.psum_scatter(jnp.stack(kept, axis=2), INNER, scatter_dimension=3, tiled=True)
    low = lax.all_gather(low.astype(jnp.bfloat16), "wide", axis=0, tiled=True)
    spread = 0
    for item in range(MOST):
        mask = (blocks[None] == jnp.arange(slots, dtype=jnp.int32)[:, None, None]) & (position == item)
        spread += jnp.where(mask[..., None], low[:, :, item][:, :, None], 0)
    spread = spread.reshape(slots, owners * row_count, rank_portion)
    delta = jnp.einsum("srq,sqw->rw", spread, second_factor_table, preferred_element_type=jnp.float32)
    total = base + delta
    return lax.psum_scatter(total, INNER, scatter_dimension=0, tiled=True).astype(jnp.bfloat16)


def ring_order(nodes):
    return list(range(0, nodes, 2)) + list(range(nodes - 1, 0, -2))


def combine_kernel(first_pair, pairs, flags, near, near_sib, away, away_sib, kept, sent):
    for pair in range(pairs):
        here = near[pair] + near_sib[pair]
        there = away[pair] + away_sib[pair]
        mine = flags[first_pair + pair] == 1
        kept[pair] = jnp.where(mine, here, there)
        sent[pair] = jnp.where(mine, there, here).astype(jnp.bfloat16)


def combine(first_pair, flags, near, near_sib, away, away_sib):
    pairs = near.shape[0]
    return pl.pallas_call(
        functools.partial(combine_kernel, first_pair, pairs),
        in_specs=[pl.BlockSpec(memory_space=pltpu.SMEM)]
        + [pl.BlockSpec(memory_space=pltpu.VMEM)] * 4,
        out_specs=[pl.BlockSpec(memory_space=pltpu.VMEM)] * 2,
        out_shape=[
            jax.ShapeDtypeStruct(near.shape, jnp.float32),
            jax.ShapeDtypeStruct(near.shape, jnp.bfloat16),
        ],
    )(flags, near, near_sib, away, away_sib)


def delta_kernel(low, choose, mask, second, out):
    own = jnp.dot(choose[...], low[...], preferred_element_type=jnp.float32).astype(jnp.bfloat16)
    copies = mask.shape[1] // own.shape[1]
    spread = jnp.concatenate([own] * copies, axis=1) * mask[...]
    out[...] = jnp.dot(spread, second[...], preferred_element_type=jnp.float32)


def assemble_kernel(target, kept, got, kept_more, got_more, delta, out):
    pairs = out.shape[0]
    for pair in range(pairs):
        place = target[pair]
        if pair == 0:
            value = kept[0] + got[0].astype(jnp.float32)
        else:
            value = kept_more[pair - 1] + got_more[pair - 1].astype(jnp.float32)
        out[place] = (value + delta[place]).astype(jnp.bfloat16)


def whole_call(kernel, out_shape, scalars, *arrays):
    return pl.pallas_call(
        kernel,
        in_specs=[pl.BlockSpec(memory_space=pltpu.SMEM)] * len(scalars)
        + [pl.BlockSpec(memory_space=pltpu.VMEM)] * len(arrays),
        out_specs=pl.BlockSpec(memory_space=pltpu.VMEM),
        out_shape=out_shape,
    )(*scalars, *arrays)


def ringed(
    gate_activation,
    up_activation,
    down_base_weight,
    first_factor_table,
    second_factor_table,
    row_adapter_index,
    adapter_storage_slot,
):
    f32, bf16 = jnp.float32, jnp.bfloat16
    row_count, width_part = gate_activation.shape
    owners = lax.axis_size("wide")
    nodes = owners // 2
    far = nodes // 2
    steps = far - 1
    own_nodes = nodes // 2
    own_blocks = owners // 2
    group_rows = 2 * row_count
    order = ring_order(nodes)
    depth = width_part // 2
    width = down_base_weight.shape[1]
    rank = first_factor_table.shape[1]

    table = []
    for w in range(owners):
        p, lane = order.index(w // 2), w % 2
        at = lambda shift: order[(p + shift) % nodes]
        arrivals = [at(0)] + [at(s * k) for k in range(1, far) for s in (-1, 1)]
        row = [2 * node + side for node in arrivals for side in (0, 1)]
        row += [2 * at(far) + (lane ^ side) for side in (0, 1)]
        for half in (0, 1):
            here = [(at(s) < own_nodes) == (half == 0) for s in range(far)]
            row += [int(h) for h in here]
            row += [at(s if h else s + far) % own_nodes for s, h in enumerate(here)]
        table.append(row)
    home = lax.axis_index("wide")
    part = lax.axis_index(INNER)
    side = jnp.bitwise_and(home, 1)
    lane = side[None]

    def moved(shift, cross=0):
        return [
            (order[p] * 2 + c, order[(p + shift) % nodes] * 2 + (c ^ cross))
            for p in range(nodes)
            for c in (0, 1)
        ]

    def send(value, shift, cross=0):
        return lax.ppermute(value, "wide", moved(shift, cross))

    def half_of(value, which, axis):
        return lax.dynamic_slice_in_dim(value, which * depth, depth, axis)

    keep = hidden_of(half_of(gate_activation, side, 1), half_of(up_activation, side, 1))
    right, left = [send(keep, 1)], [send(keep, -1)]
    other_side, keep = lax.optimization_barrier((1 - side, keep))
    give = hidden_of(half_of(gate_activation, other_side, 1), half_of(up_activation, other_side, 1))
    twin = send(give, 0, 1)
    right.append(send(twin, 1))
    left.append(send(twin, -1))

    first = first_factor_table[0]
    first, twin = lax.optimization_barrier((first, twin))
    weight, first_sib = lax.optimization_barrier((down_base_weight, send(first, 0, 1)))
    weights = (weight, send(weight, 0, 1))
    factors = (first, first_sib)

    facts = lax.dynamic_index_in_dim(
        jnp.asarray(np.array(table, np.int32)), home, 0, keepdims=False
    )
    edges = np.cumsum([0, 2 * (nodes - 1), 2, far, far, far, far])
    arrived, far_wide, *rest = [facts[a:b] for a, b in zip(edges[:-1], edges[1:])]
    flags = jnp.where(part == 0, rest[0], rest[2])
    target = jnp.where(part == 0, rest[1], rest[3])
    slot_all = slots_of(row_adapter_index, adapter_storage_slot).reshape(owners, row_count)
    ranks = jnp.arange(row_count, dtype=jnp.int32)
    earlier = (slot_all[:, :, None] == slot_all[:, None, :]) & (ranks[None, :] < ranks[:, None])
    position = jnp.sum(earlier.astype(jnp.int32), axis=2)
    items = jnp.arange(MOST, dtype=jnp.int32)

    sides = jnp.arange(2, dtype=jnp.int32)
    own_wide = jnp.bitwise_xor(home, sides)
    blocks = jnp.arange(owners, dtype=jnp.int32)
    own_is = own_wide[:, None, None] == blocks[None, :, None]
    own_slot = jnp.sum(jnp.where(own_is, slot_all[None], 0), axis=1)
    own_position = jnp.sum(jnp.where(own_is, position[None], 0), axis=1)
    pick = (own_slot[None, :, None, :] == far_wide[:, None, None, None]) & (
        own_position[None, :, None, :] == items[None, None, :, None]
    )
    pick = jnp.where(
        (sides[:, None] == sides[None, :])[None, :, None, :, None], pick[:, :, :, None, :], False
    ).reshape(4 * MOST, group_rows)
    both = jnp.concatenate([keep, twin], axis=0)
    picked = jnp.dot(pick.astype(bf16), both, preferred_element_type=f32).astype(bf16)
    far_rows = send(picked, far)

    slot_here = lax.dynamic_slice_in_dim(slot_all, part * own_blocks, own_blocks)
    position_here = lax.dynamic_slice_in_dim(position, part * own_blocks, own_blocks)
    came = jnp.bitwise_xor(home, blocks)
    choose = (
        (slot_here[:, :, None, None, None] == came[:, None, None])
        & (position_here[:, :, None, None, None] == items)
        & (jnp.arange(own_blocks)[:, None] == jnp.arange(own_blocks)[None, :])[:, None, None, :, None]
    )
    choose = choose.astype(bf16).reshape(own_blocks * row_count, owners * own_blocks * MOST)
    mask = jnp.repeat(
        (slot_here.reshape(-1)[:, None] == blocks[None, :]).astype(bf16), rank, axis=1
    )

    other = lax.ppermute(second_factor_table, INNER, SWAP)
    second = jnp.where(
        part == 0,
        jnp.concatenate([second_factor_table, other], axis=1),
        jnp.concatenate([other, second_factor_table], axis=1),
    ).reshape(owners * rank, width)

    def chosen(slot):
        near = (
            (arrived[None, None, :, None] == blocks[:, None, None, None])
            & (slot_all == slot)[:, None, None, :]
            & (position[:, None, None, :] == items[None, :, None, None])
        ).reshape(owners * MOST, -1)
        there = (
            (far_wide[None, None, :, None] == blocks[:, None, None, None])
            & (items[:, None] == items[None, :])[None, :, None, :]
        ).reshape(owners * MOST, -1)
        return jnp.concatenate([near, there], axis=1).astype(f32)

    chosen_mine, chosen_sib = chosen(home), chosen(jnp.bitwise_xor(home, 1))

    results, sibs, lows = [], [], []

    def add(result):
        results.append(result)
        sibs.append(send(result[1], 0, 1))

    ready = (far_rows, second, choose, mask, chosen_mine, chosen_sib)
    pieces = [keep, twin]
    for step in range(1, steps + 1):
        if step > 1:
            right, left, ready, result = lax.optimization_barrier((right, left, ready, result))
            add(result[:2])
            lows.append(result[2])
        pieces += right + left
        if step < steps:
            right = [send(block, 1) for block in right]
            left = [send(block, -1) for block in left]
            result = rows_product(lane, pieces, weights, factors)
        else:
            last = [send(right[0], 1), send(left[1], -1)]
            far_rows, second, choose, mask, chosen_mine, chosen_sib = ready
            low, far_low = rows_product(lane, pieces, (), factors, (far_rows,))
            lows.append(low)
            result = rows_product(lane, pieces, weights)
        pieces = []
    result, last = lax.optimization_barrier((result, last))
    add(result)

    low = jnp.concatenate([values.reshape(-1, 2 * rank) for values in lows], axis=0)
    count = 2 * MOST

    def compact(choice, values, far_values):
        return jnp.dot(
            choice,
            jnp.concatenate([values, far_values], axis=0),
            precision=lax.Precision.HIGHEST,
        )

    low = jnp.stack(
        [
            compact(chosen_mine, low[:, :rank], far_low[:count, :rank]),
            compact(chosen_sib, low[:, rank:], far_low[count:, rank:]),
        ]
    )
    half = own_blocks * MOST
    kept = jnp.where(part == 0, low[:, :half], low[:, half:])
    sent = jnp.where(part == 0, low[:, half:], low[:, :half])
    low = kept + lax.ppermute(sent, INNER, SWAP)
    low = (low + send(low, 0, 1)[::-1]).astype(bf16)
    gap = 2
    while gap < owners:
        other = lax.ppermute(low, "wide", [(w, w ^ gap) for w in range(owners)])
        low = jnp.concatenate([low, other], axis=0)
        gap *= 2
    delta = whole_call(
        delta_kernel,
        jax.ShapeDtypeStruct((own_blocks * row_count, width), f32),
        (),
        low.reshape(owners * half, rank),
        choose,
        mask,
        second,
    ).reshape(own_nodes, group_rows, width)

    def node(values, shift):
        if shift == 0:
            return values[0][0]
        if shift == far:
            return values[-1][0]
        step = min(shift, nodes - shift)
        return values[step - 1][(1 if step == 1 else 0) + (0 if shift > far else 1)]

    def over_mp(shifts):
        stacks = []
        for offset in (0, far):
            for values in ([r[0] for r in results], sibs):
                group = jnp.stack([node(values, s + offset) for s in shifts])
                stacks.append(group.reshape(len(shifts), group_rows, width))
        kept, sent = combine(shifts[0], flags, *stacks)
        return kept, lax.ppermute(sent, INNER, SWAP)

    more = over_mp(list(range(1, far)))
    add(rows_product(lane, last, weights))
    out = whole_call(
        assemble_kernel,
        jax.ShapeDtypeStruct((own_nodes, group_rows, width), bf16),
        (target,),
        *over_mp([0]),
        *more,
        delta,
    )
    return out.reshape(-1, width)


def solution(mesh):
    shape = dict(mesh.shape)
    wide, inner = shape["wide"], shape["mp"] * shape["sub"]
    paired = shape["sub"] == 1 and inner == 2 and wide % 8 == 0 and wide & (wide - 1) == 0
    if paired:
        nodes = wide // 2
        order = ring_order(nodes)
        paired = all(
            (order[p] < nodes // 2) != (order[(p + nodes // 2) % nodes] < nodes // 2)
            for p in range(nodes)
        )
    return jax.shard_map(
        ringed if paired else gathered,
        mesh=mesh,
        in_specs=(
            P(("groups", "wide"), ("mp", "sub")),
            P(("groups", "wide"), ("mp", "sub")),
            P(("mp", "sub"), "wide"),
            P("wide", None, ("mp", "sub")),
            P(None, ("mp", "sub"), "wide"),
            P("groups", None),
            P(),
        ),
        out_specs=P(("groups", "mp", "sub"), "wide"),
        check_vma=False,
    )
```

time: 145 us -> 141 us (0.972)
  Pallas kernels: 32.3 us -> 61.5 us
  waiting for transfers between devices: 36.9 us -> 21.5 us
  between operations: 10.2 us -> 0.39 us
  starting transfers between devices: 37.7 us -> 33.1 us
  local copies, waits for them, and re-layouts: 12.8 us -> 9.76 us
  matrix products: 2.67 us -> 0.77 us
    pallas_call x4 -> x9, Pallas kernels: 32.3 us -> 61.5 us  [the longest x5 52.4 us: rows_product(): pl.pallas_call(functools.partial(rows_kernel, count, len(more), int(bool(...]
    ppermute x3, waiting for transfers between devices: 8.1 us -> 0.01 us  [the longest x2 0.01 us: over_mp(): return (kept, lax.ppermute(sent, INNER, SWAP))]
    dynamic_slice x3 -> x1, local copies, waits for them, and re-layouts: 8.01 us -> 0.01 us  [ringed(): lax.dynamic_slice_in_dim(position, part * own_blocks, own_blocks)]
    ppermute x4 -> x3, starting transfers between devices: 8.13 us -> 1.92 us  [ringed(): other = lax.ppermute(low, 'wide', [(w, w ^ gap) for w in range(owners)])]
    ppermute x4 -> x3, waiting for transfers between devices: 5.4 us -> 0.01 us  [ringed(): other = lax.ppermute(low, 'wide', [(w, w ^ gap) for w in range(owners)])]
    add x5 -> x1, other arithmetic: 3.4 us -> 0.01 us  [ringed(): low = kept + lax.ppermute(sent, INNER, SWAP)]
    ppermute x23, starting transfers between devices: 22.5 us -> 25.6 us  [send(): return lax.ppermute(value, 'wide', moved(shift, cross))]
    another operation x3 -> x4, other arithmetic: 1.01 us -> 3.12 us  [over_mp(): group = jnp.stack([node(values, s + offset) for s in shifts])]
  transfers between devices with their start and end apart: 31 -> 30, of which waited for: 9 -> 8; matrix products, arithmetic and copies ran while one was open for 11% -> 12% of each run, Pallas kernels for 22% -> 42%
where the time goes in v3:
time: 141 us; the launch traced here: 140 us
  Pallas kernels  61.5 us (44%)
  starting transfers between devices  33.1 us (23%)
  waiting for transfers between devices  21.5 us (15%)
  other arithmetic  12.8 us (9%)
  local copies, waits for them, and re-layouts  9.76 us (7%)
    pallas_call x5, Pallas kernels, rows_product(): pl.pallas_call(functools.partial(rows_kernel, count, len(more), int(bool(...  52.4 us
    ppermute x23, starting transfers between devices, send(): return lax.ppermute(value, 'wide', moved(shift, cross))  25.6 us
    ppermute x23, waiting for transfers between devices, send(): return lax.ppermute(value, 'wide', moved(shift, cross))  21.5 us
    pallas_call x2, Pallas kernels, whole_call(): pl.pallas_call(kernel, in_specs=[pl.BlockSpec(memory_space=pltpu.SMEM)] *...  5.07 us
    pallas_call x2, Pallas kernels, combine(): pl.pallas_call(functools.partial(combine_kernel, first_pair, pairs), in_s...  4.06 us
    unnamed x18, local copies, waits for them, and re-layouts  3.26 us
    another operation x4, other arithmetic, over_mp(): group = jnp.stack([node(values, s + offset) for s in shifts])  3.12 us
    convert_element_type x2, other arithmetic, hidden_of(): (jax.nn.silu(gate.astype(jnp.float32)) * up.astype(jnp.float32)).astype(j...  2.99 us
  transfers between devices with their start and end apart: 30, of which 8 were waited for; matrix products, arithmetic and copies ran while one was open for 12% of the time, Pallas kernels for 42%

profile of v3, /device:TPU:0, one launch (start us, length us, event | category | flops | bytes accessed | tf_op | source)
XLA Modules:
  0.0 139.8 jit_solution(17087950557561245861)
XLA Ops:
  0.0 1.6 %fusion.12.refs_0_ = bf16[32,7168]{1,0:T(8,128)(2,1)S(1)} fusion(bf16[32,14336]{1,0:T(8,128)(2,1)} %param.9, s32[]{:T(128)S(6)} %select_n.81, bf16[32,14336]{1,0:T(8,128)(2,1)} %param.8), kind=kLoop, calls=%fused_computation.21 | loop fusion | flops 1835008 | bytes 1376260 | tf_op jit(solution)/shard_map/convert_element_type | solution.py:102
  1.6 1.4 %fusion.11 = bf16[32,7168]{1,0:T(8,128)(2,1)S(1)} fusion(bf16[32,14336]{1,0:T(8,128)(2,1)} %param.9, s32[]{:T(128)S(6)} %select_n.82, bf16[32,14336]{1,0:T(8,128)(2,1)} %param.8), kind=kLoop, calls=%fused_computation.20 | loop fusion | flops 1835008 | bytes 1376260 | tf_op jit(solution)/shard_map/convert_element_type | solution.py:102
  3.5 1.4 %collective-permute-done.2.refs_1_ = bf16[32,7168]{1,0:T(8,128)(2,1)S(1)} collective-permute-done((bf16[32,7168]{1,0:T(8,128)(2,1)S(1)}, bf16[32,7168]{1,0:T(8,128)(2,1)S(1)}, u32[]{:S(2)}, u32[]{:S(2)}) %collective-permute-start.2) | collective-permute-done | bytes 458784 | tf_op jit(solution)/shard_map/ppermute | solution.py:256
  5.4 3.4 %collective-permute-done.11.refs_9_.refs_7_.refs_6_ = bf16[64,14336]{1,0:T(8,128)(2,1)S(1)} collective-permute-done((bf16[64,14336]{1,0:T(8,128)(2,1)S(1)}, bf16[64,14336]{1,0:T(8,128)(2,1)S(1)}, u32[]{:S(2)}, u32[]{:S(2)}) %collective-permute-start.11) | collective-permute-done | bytes 1835040 | tf_op jit(solution)/shard_map/ppermute | solution.py:256
  8.8 1.2 copy-done.1
  10.4 2.7 %collective-permute-start = (bf16[32,7168]{1,0:T(8,128)(2,1)S(1)}, bf16[32,7168]{1,0:T(8,128)(2,1)S(1)}, u32[]{:S(2)}, u32[]{:S(2)}) collective-permute-start(bf16[32,7168]{1,0:T(8,128)(2,1)S(1)} %fusion.12.refs_0_), channel_id=1, source_target_pairs={{0,8},{2,10},{8,16},{10,18},{16,24},{18,26},{24,28},{26,30},{28,20... | collective-permute-start | bytes 1376264 | tf_op jit(solution)/shard_map/ppermute | solution.py:256
  13.1 1.9 %collective-permute-start.10 = (bf16[16,32,512]{2,1,0:T(8,128)(2,1)}, bf16[16,32,512]{2,1,0:T(8,128)(2,1)}, u32[]{:S(2)}, u32[]{:S(2)}) collective-permute-start(bf16[16,32,512]{2,1,0:T(8,128)(2,1)} %param.12), channel_id=1, source_target_pairs={{0,1},{1,0},{2,3},{3,2},{4,5},{5,4},{6,7},{7,6},{8,9},{9,8},{10,11... | collective-permute-start | bytes 1572872 | tf_op jit(solution)/shard_map/ppermute | solution.py:317
  15.3 0.7 constant_dynamic-slice_fusion.2
  18.1 1.6 %collective-permute-start.3 = (bf16[32,7168]{1,0:T(8,128)(2,1)S(1)}, bf16[32,7168]{1,0:T(8,128)(2,1)}, u32[]{:S(2)}, u32[]{:S(2)}) collective-permute-start(bf16[32,7168]{1,0:T(8,128)(2,1)S(1)} %collective-permute-done.2.refs_1_), channel_id=1, source_target_pairs={{0,8},{2,10},{8,16},{10,18},{16,24},{18,26},{24,28},{26,30},{28,20... | collective-permute-start | bytes 1376264 | tf_op jit(solution)/shard_map/ppermute | solution.py:256
  19.8 4.6 %collective-permute-done.refs_2_ = bf16[32,7168]{1,0:T(8,128)(2,1)S(1)} collective-permute-done((bf16[32,7168]{1,0:T(8,128)(2,1)S(1)}, bf16[32,7168]{1,0:T(8,128)(2,1)S(1)}, u32[]{:S(2)}, u32[]{:S(2)}) %collective-permute-start) | collective-permute-done | bytes 458784 | tf_op jit(solution)/shard_map/ppermute | solution.py:256
  24.4 2.0 %collective-permute-start.7 = (bf16[32,7168]{1,0:T(8,128)(2,1)S(1)}, bf16[32,7168]{1,0:T(8,128)(2,1)}, u32[]{:S(2)}, u32[]{:S(2)}) collective-permute-start(bf16[32,7168]{1,0:T(8,128)(2,1)S(1)} %collective-permute-done.2.refs_1_), channel_id=1, source_target_pairs={{0,4},{2,6},{8,0},{10,2},{16,8},{18,10},{24,16},{26,18},{28,24},{3... | collective-permute-start | bytes 1376264 | tf_op jit(solution)/shard_map/ppermute | solution.py:256
  26.4 1.0 and_convert_fusion
  27.4 1.4 %reshape.288 = bf16[256,256]{0,1:T(8,128)(2,1)S(1)} reshape(bf16[8,32,16,8,2]{1,0,4,3,2:T(8,128)(2,1)} %and_convert_fusion) | data formatting | bytes 262144 | tf_op jit(solution)/shard_map/convert_element_type | solution.py:312
  29.0 2.0 %collective-permute-start.6 = (bf16[32,7168]{1,0:T(8,128)(2,1)}, bf16[32,7168]{1,0:T(8,128)(2,1)S(1)}, u32[]{:S(2)}, u32[]{:S(2)}) collective-permute-start(bf16[32,7168]{1,0:T(8,128)(2,1)} %collective-permute-done.5.refs_4_), channel_id=1, source_target_pairs={{0,4},{2,6},{8,0},{10,2},{16,8},{18,10},{24,16},{26,18},{28,24},{3... | collective-permute-start | bytes 1376264 | tf_op jit(solution)/shard_map/ppermute | solution.py:256
  30.9 3.4 %collective-permute-done.3.refs_3_ = bf16[32,7168]{1,0:T(8,128)(2,1)} collective-permute-done((bf16[32,7168]{1,0:T(8,128)(2,1)S(1)}, bf16[32,7168]{1,0:T(8,128)(2,1)}, u32[]{:S(2)}, u32[]{:S(2)}) %collective-permute-start.3) | collective-permute-done | bytes 458784 | tf_op jit(solution)/shard_map/ppermute | solution.py:256
  34.3 2.0 %collective-permute-start.4 = (bf16[32,7168]{1,0:T(8,128)(2,1)}, bf16[32,7168]{1,0:T(8,128)(2,1)S(1)}, u32[]{:S(2)}, u32[]{:S(2)}) collective-permute-start(bf16[32,7168]{1,0:T(8,128)(2,1)} %collective-permute-done.3.refs_3_), channel_id=1, source_target_pairs={{0,8},{2,10},{8,16},{10,18},{16,24},{18,26},{24,28},{26,30},{28,20... | collective-permute-start | bytes 1376264 | tf_op jit(solution)/shard_map/ppermute | solution.py:256
  36.4 1.6 %collective-permute-done.7.refs_5_ = bf16[32,7168]{1,0:T(8,128)(2,1)} collective-permute-done((bf16[32,7168]{1,0:T(8,128)(2,1)S(1)}, bf16[32,7168]{1,0:T(8,128)(2,1)}, u32[]{:S(2)}, u32[]{:S(2)}) %collective-permute-start.7) | collective-permute-done | bytes 458784 | tf_op jit(solution)/shard_map/ppermute | solution.py:256
  38.0 2.0 %collective-permute-start.8 = (bf16[32,7168]{1,0:T(8,128)(2,1)}, bf16[32,7168]{1,0:T(8,128)(2,1)S(1)}, u32[]{:S(2)}, u32[]{:S(2)}) collective-permute-start(bf16[32,7168]{1,0:T(8,128)(2,1)} %collective-permute-done.7.refs_5_), channel_id=1, source_target_pairs={{0,4},{2,6},{8,0},{10,2},{16,8},{18,10},{24,16},{26,18},{28,24},{3... | collective-permute-start | bytes 1376264 | tf_op jit(solution)/shard_map/ppermute | solution.py:256
  40.2 3.6 %collective-permute-start.9 = (bf16[8,7168]{1,0:T(8,128)(2,1)S(1)}, bf16[8,7168]{1,0:T(8,128)(2,1)S(1)}, u32[]{:S(2)}, u32[]{:S(2)}) collective-permute-start(bf16[8,7168]{1,0:T(8,128)(2,1)S(1)} %convolution_convert_fusion), channel_id=1, source_target_pairs={{0,28},{2,30},{8,20},{10,22},{16,12},{18,14},{24,4},{26,6},{28,0},... | collective-permute-start | bytes 344072 | tf_op jit(solution)/shard_map/ppermute | solution.py:256
  43.9 2.9 %maximum_select_fusion = bf16[16,64,512]{2,1,0:T(8,128)(2,1)} fusion(bf16[16,32,512]{2,1,0:T(8,128)(2,1)} %collective-permute-done.10, bf16[16,32,512]{2,1,0:T(8,128)(2,1)} %param.12, pred[]{:T(512)S(6)} %eq.297), kind=kLoop, calls=%fused_computation.7 | loop fusion | flops 4718592 | bytes 2097153 | tf_op jit(solution)/shard_map/jit(_where)/select_n | solution.py:318
  46.7 13.2 %shard_map.82 = (f32[3,2,32,512]{3,2,1,0:T(8,128)S(1)}, f32[3,2,32,512]{3,2,1,0:T(8,128)S(1)}, f32[3,2,32,128]{3,2,1,0:T(8,128)S(1)}) custom-call(s32[1]{0:T(128)} %bitcast.8.lane_ref, bf16[32,7168]{1,0:T(8,128)(2,1)S(1)} %fusion.12.refs_0_, bf16[32,7168]{1,0:T(8,128)(2,1)S(1)} %collective-permute-done.2.refs_1_, ...), custom_call_target="tpu_custom_call" | custom-call | flops 198180864 | bytes 2064384 | tf_op jit(solution)/shard_map/pallas_call | solution.py:82
  60.1 1.3 collective-permute-start.14
  61.4 3.8 %collective-permute-start.15 = (bf16[32,7168]{1,0:T(8,128)(2,1)S(1)}, bf16[32,7168]{1,0:T(8,128)(2,1)S(1)}, u32[]{:S(2)}, u32[]{:S(2)}) collective-permute-start(bf16[32,7168]{1,0:T(8,128)(2,1)S(1)} %collective-permute-done.4.refs_1_), channel_id=1, source_target_pairs={{0,8},{2,10},{8,16},{10,18},{16,24},{18,26},{24,28},{26,30},{28,20... | collective-permute-start | bytes 1376264 | tf_op jit(solution)/shard_map/ppermute | solution.py:256
  65.8 12.2 %shard_map.83 = (f32[2,2,32,512]{3,2,1,0:T(8,128)S(1)}, f32[2,2,32,512]{3,2,1,0:T(8,128)S(1)}, f32[2,2,32,128]{3,2,1,0:T(8,128)S(1)}) custom-call(s32[1]{0:T(128)} %bitcast.8.lane_ref, bf16[32,7168]{1,0:T(8,128)(2,1)S(1)} %collective-permute-done.1.refs_0_, bf16[32,7168]{1,0:T(8,128)(2,1)S(1)} %collective-permute-done.4.refs_1_, ...), custom_call_target="tpu_custom_call" | custom-call | flops 132120576 | bytes 2064384 | tf_op jit(solution)/shard_map/pallas_call | solution.py:82
  78.0 0.7 fusion.29
  78.7 2.5 %collective-permute-done.15.refs_1_ = bf16[32,7168]{1,0:T(8,128)(2,1)S(1)} collective-permute-done((bf16[32,7168]{1,0:T(8,128)(2,1)S(1)}, bf16[32,7168]{1,0:T(8,128)(2,1)S(1)}, u32[]{:S(2)}, u32[]{:S(2)}) %collective-permute-start.15) | collective-permute-done | bytes 458784 | tf_op jit(solution)/shard_map/ppermute | solution.py:256
  81.2 3.6 %collective-permute-done.17.refs_3_ = bf16[32,7168]{1,0:T(8,128)(2,1)S(1)} collective-permute-done((bf16[32,7168]{1,0:T(8,128)(2,1)S(1)}, bf16[32,7168]{1,0:T(8,128)(2,1)S(1)}, u32[]{:S(2)}, u32[]{:S(2)}) %collective-permute-start.17) | collective-permute-done | bytes 458784 | tf_op jit(solution)/shard_map/ppermute | solution.py:256
  84.8 3.6 %shard_map.88 = (f32[2,2,32,128]{3,2,1,0:T(8,128)S(1)}, f32[8,128]{1,0:T(8,128)S(1)}) custom-call(s32[1]{0:T(128)} %bitcast.8.lane_ref, bf16[32,7168]{1,0:T(8,128)(2,1)S(1)} %collective-permute-done.14.refs_0_, bf16[32,7168]{1,0:T(8,128)(2,1)S(1)} %collective-permute-done.15.refs_1_, bf16[32,7168]{1,0:T(8,128)(2,1)S(1)} %collective-permute-done.16.refs_2_, ...), custom_call_target="tpu_custom_call" | custom-call | flops 14680064 | bytes 229376 | tf_op jit(solution)/shard_map/pallas_call | solution.py:82
  89.2 1.6 %collective-permute-start.25 = (f32[2,16,64]{2,1,0:T(8,128)S(1)}, f32[2,16,64]{2,1,0:T(8,128)S(1)}, u32[]{:S(2)}, u32[]{:S(2)}) collective-permute-start(f32[2,16,64]{2,1,0:T(8,128)S(1)} %broadcast_select_fusion), channel_id=1, source_target_pairs={{0,1},{1,0},{2,3},{3,2},{4,5},{5,4},{6,7},{7,6},{8,9},{9,8},{10,11... | collective-permute-start | bytes 24584 | tf_op jit(solution)/shard_map/ppermute | solution.py:385
  90.7 0.7 fusion.28
  91.8 1.7 %collective-permute-start.19 = (bf16[32,7168]{1,0:T(8,128)(2,1)S(1)}, bf16[32,7168]{1,0:T(8,128)(2,1)S(1)}, u32[]{:S(2)}, u32[]{:S(2)}) collective-permute-start(bf16[32,7168]{1,0:T(8,128)(2,1)S(1)} %collective-permute-done.17.refs_3_), channel_id=1, source_target_pairs={{0,4},{2,6},{8,0},{10,2},{16,8},{18,10},{24,16},{26,18},{28,24},{3... | collective-permute-start | bytes 1376264 | tf_op jit(solution)/shard_map/ppermute | solution.py:256
  94.1 0.9 collective-permute-done.26
  95.4 11.8 %shard_map.84 = (f32[2,2,32,512]{3,2,1,0:T(8,128)S(1)}, f32[2,2,32,512]{3,2,1,0:T(8,128)S(1)}) custom-call(s32[1]{0:T(128)} %bitcast.8.lane_ref, bf16[32,7168]{1,0:T(8,128)(2,1)S(1)} %collective-permute-done.14.refs_0_, bf16[32,7168]{1,0:T(8,128)(2,1)S(1)} %collective-permute-done.15.refs_1_, bf16[32,7168]{1,0:T(8,128)(2,1)S(1)} %collective-permute-done.16.refs_2_, ...), custom_call_target="tpu_custom_call" | custom-call | flops 117440512 | bytes 1835008 | tf_op jit(solution)/shard_map/pallas_call | solution.py:82
  107.5 11.6 %shard_map.85 = (f32[1,2,32,512]{3,2,1,0:T(8,128)S(1)}, f32[1,2,32,512]{3,2,1,0:T(8,128)S(1)}) custom-call(s32[1]{0:T(128)} %bitcast.8.lane_ref, bf16[32,7168]{1,0:T(8,128)(2,1)S(1)} %collective-permute-done.18.refs_0_, bf16[32,7168]{1,0:T(8,128)(2,1)S(1)} %collective-permute-done.19.refs_1_, bf16[14336,512]{1,0:T(8,128)(2,1)} %refs_2_, ...), custom_call_target="tpu_custom_call" | custom-call | flops 58720256 | bytes 1835008 | tf_op jit(solution)/shard_map/pallas_call | solution.py:82
  120.3 0.8 pad_maximum_fusion.2
  121.1 0.8 pad_maximum_fusion
  121.8 0.8 pad_maximum_fusion.3
  122.6 0.8 pad_maximum_fusion.1
  123.4 2.2 %shard_map.87 = (f32[3,64,512]{2,1,0:T(8,128)}, bf16[3,64,512]{2,1,0:T(8,128)(2,1)}) custom-call(s32[4]{0:T(128)} %get-tuple-element.137.flags, f32[3,64,512]{2,1,0:T(8,128)} %bitcast.54, f32[3,64,512]{2,1,0:T(8,128)} %bitcast.56, f32[3,64,512]{2,1,0:T(8,128)} %bitcast.53, f32[3,64,512]{2,1,0:T(8,128)} %bitcast.55), custom_call_target="tpu_custom_call" | custom-call | tf_op jit(solution)/shard_map/pallas_call | solution.py:168
  125.7 0.7 collective-permute-start.24
  126.4 1.4 collective-permute-start.29
  127.8 1.0 copy.21.mask
  128.8 0.7 copy.20.choose
  130.2 1.8 %shard_map.86 = (f32[1,64,512]{2,1,0:T(8,128)}, bf16[1,64,512]{2,1,0:T(8,128)(2,1)}) custom-call(s32[4]{0:T(128)} %get-tuple-element.137.flags, f32[1,64,512]{2,1,0:T(8,128)} %bitcast.57, f32[1,64,512]{2,1,0:T(8,128)} %bitcast.58, f32[1,64,512]{2,1,0:T(8,128)} %bitcast.46, f32[1,64,512]{2,1,0:T(8,128)} %bitcast.60), custom_call_target="tpu_custom_call" | custom-call | tf_op jit(solution)/shard_map/pallas_call | solution.py:168
  132.0 1.3 collective-permute-start.21
  133.3 0.7 pad_maximum_fusion.5
  134.0 2.9 %shard_map.89 = f32[256,512]{1,0:T(8,128)} custom-call(bf16[256,64]{1,0:T(8,128)(2,1)} %bitcast.59, bf16[256,256]{1,0:T(8,128)(2,1)} %copy.20.choose, bf16[256,1024]{1,0:T(8,128)(2,1)} %copy.21.mask, bf16[1024,512]{1,0:T(8,128)(2,1)} %bitcast.50), custom_call_target="tpu_custom_call" | custom-call | tf_op jit(solution)/shard_map/pallas_call | solution.py:199
  137.7 2.1 %shard_map.90 = bf16[4,64,512]{2,1,0:T(8,128)(2,1)} custom-call(s32[4]{0:T(128)} %get-tuple-element.138.target, f32[1,64,512]{2,1,0:T(8,128)} %get-tuple-element.91.kept, bf16[1,64,512]{2,1,0:T(8,128)(2,1)} %copy-done.6, f32[3,64,512]{2,1,0:T(8,128)} %get-tuple-element.97.kept_more, bf16[3,64,512]{2,1,0:T(8,128)(2,1)} %copy-done.4, f32[4,64,512]{2,1,0:T(8,128)} %bitcast.52), custom_call_target="tpu_custom_call" | custom-call | tf_op jit(solution)/shard_map/pallas_call | solution.py:199
  (106 shorter events, 9.7 us)
Async XLA Ops:
  0.0 5.0 %copy-start = (bf16[1,64,14336]{2,1,0:T(8,128)(2,1)S(1)}, bf16[1,64,14336]{2,1,0:T(8,128)(2,1)}, u32[]{:S(2)}) copy-start(bf16[1,64,14336]{2,1,0:T(8,128)(2,1)} %param.11) | copy-start | bytes 5505028
  0.0 15.0 %copy-start.7 = (s32[512,1]{0,1:T(1,128)S(1)}, s32[512,1]{0,1:T(1,128)}, u32[]{:S(2)}) copy-start(s32[512,1]{0,1:T(1,128)} %param.13) | copy-start | bytes 6148
  0.0 15.0 %copy-start.8 = (s32[16]{0:T(128)S(1)}, s32[16]{0:T(128)}, u32[]{:S(2)}) copy-start(s32[16]{0:T(128)} %param.14) | copy-start | bytes 196
  3.0 2.0 %collective-permute-start.2 = (bf16[32,7168]{1,0:T(8,128)(2,1)S(1)}, bf16[32,7168]{1,0:T(8,128)(2,1)S(1)}, u32[]{:S(2)}, u32[]{:S(2)}) collective-permute-start(bf16[32,7168]{1,0:T(8,128)(2,1)S(1)} %fusion.11), channel_id=1, source_target_pairs={{0,2},{2,0},{8,10},{10,8},{16,18},{18,16},{24,26},{26,24},{28,30},... | collective-permute-start | bytes 1376264 | tf_op jit(solution)/shard_map/ppermute | solution.py:256
  5.0 3.8 %collective-permute-start.11 = (bf16[64,14336]{1,0:T(8,128)(2,1)S(1)}, bf16[64,14336]{1,0:T(8,128)(2,1)S(1)}, u32[]{:S(2)}, u32[]{:S(2)}) collective-permute-start(bf16[64,14336]{1,0:T(8,128)(2,1)S(1)} %bitcast.42), channel_id=1, source_target_pairs={{0,2},{2,0},{8,10},{10,8},{16,18},{18,16},{24,26},{26,24},{28,30},... | collective-permute-start | bytes 5505032 | tf_op jit(solution)/shard_map/ppermute | solution.py:256
  8.8 1.2 copy-start.1
  10.0 30.2 %collective-permute-start.12 = (bf16[14336,512]{1,0:T(8,128)(2,1)}, bf16[14336,512]{1,0:T(8,128)(2,1)}, u32[]{:S(2)}, u32[]{:S(2)}) collective-permute-start(bf16[14336,512]{1,0:T(8,128)(2,1)} %refs_2_), channel_id=1, source_target_pairs={{0,2},{2,0},{8,10},{10,8},{16,18},{18,16},{24,26},{26,24},{28,30},... | collective-permute-start | bytes 44040200 | tf_op jit(solution)/shard_map/ppermute | solution.py:256
  10.4 14.0 %collective-permute-start = (bf16[32,7168]{1,0:T(8,128)(2,1)S(1)}, bf16[32,7168]{1,0:T(8,128)(2,1)S(1)}, u32[]{:S(2)}, u32[]{:S(2)}) collective-permute-start(bf16[32,7168]{1,0:T(8,128)(2,1)S(1)} %fusion.12.refs_0_), channel_id=1, source_target_pairs={{0,8},{2,10},{8,16},{10,18},{16,24},{18,26},{24,28},{26,30},{28,20... | collective-permute-start | bytes 1376264 | tf_op jit(solution)/shard_map/ppermute | solution.py:256
  13.1 15.7 %collective-permute-start.5 = (bf16[32,7168]{1,0:T(8,128)(2,1)S(1)}, bf16[32,7168]{1,0:T(8,128)(2,1)}, u32[]{:S(2)}, u32[]{:S(2)}) collective-permute-start(bf16[32,7168]{1,0:T(8,128)(2,1)S(1)} %fusion.12.refs_0_), channel_id=1, source_target_pairs={{0,4},{2,6},{8,0},{10,2},{16,8},{18,10},{24,16},{26,18},{28,24},{3... | collective-permute-start | bytes 1376264 | tf_op jit(solution)/shard_map/ppermute | solution.py:256
  13.1 15.9 %collective-permute-start.10 = (bf16[16,32,512]{2,1,0:T(8,128)(2,1)}, bf16[16,32,512]{2,1,0:T(8,128)(2,1)}, u32[]{:S(2)}, u32[]{:S(2)}) collective-permute-start(bf16[16,32,512]{2,1,0:T(8,128)(2,1)} %param.12), channel_id=1, source_target_pairs={{0,1},{1,0},{2,3},{3,2},{4,5},{5,4},{6,7},{7,6},{8,9},{9,8},{10,11... | collective-permute-start | bytes 1572872 | tf_op jit(solution)/shard_map/ppermute | solution.py:317
  18.1 16.2 %collective-permute-start.3 = (bf16[32,7168]{1,0:T(8,128)(2,1)S(1)}, bf16[32,7168]{1,0:T(8,128)(2,1)}, u32[]{:S(2)}, u32[]{:S(2)}) collective-permute-start(bf16[32,7168]{1,0:T(8,128)(2,1)S(1)} %collective-permute-done.2.refs_1_), channel_id=1, source_target_pairs={{0,8},{2,10},{8,16},{10,18},{16,24},{18,26},{24,28},{26,30},{28,20... | collective-permute-start | bytes 1376264 | tf_op jit(solution)/shard_map/ppermute | solution.py:256
  24.4 13.6 %collective-permute-start.7 = (bf16[32,7168]{1,0:T(8,128)(2,1)S(1)}, bf16[32,7168]{1,0:T(8,128)(2,1)}, u32[]{:S(2)}, u32[]{:S(2)}) collective-permute-start(bf16[32,7168]{1,0:T(8,128)(2,1)S(1)} %collective-permute-done.2.refs_1_), channel_id=1, source_target_pairs={{0,4},{2,6},{8,0},{10,2},{16,8},{18,10},{24,16},{26,18},{28,24},{3... | collective-permute-start | bytes 1376264 | tf_op jit(solution)/shard_map/ppermute | solution.py:256
  28.8 17.9 %copy-start.2 = (bf16[64,14336]{1,0:T(8,128)(2,1)S(1)}, bf16[64,14336]{1,0:T(8,128)(2,1)}, u32[]{:S(2)}) copy-start(bf16[64,14336]{1,0:T(8,128)(2,1)} %copy-done.1) | copy-start | bytes 5505028
  28.8 31.1 %collective-permute-start.1 = (bf16[32,7168]{1,0:T(8,128)(2,1)S(1)}, bf16[32,7168]{1,0:T(8,128)(2,1)S(1)}, u32[]{:S(2)}, u32[]{:S(2)}) collective-permute-start(bf16[32,7168]{1,0:T(8,128)(2,1)S(1)} %collective-permute-done.refs_2_), channel_id=1, source_target_pairs={{0,8},{2,10},{8,16},{10,18},{16,24},{18,26},{24,28},{26,30},{28,20... | collective-permute-start | bytes 1376264 | tf_op jit(solution)/shard_map/ppermute | solution.py:256
  29.0 31.0 %collective-permute-start.6 = (bf16[32,7168]{1,0:T(8,128)(2,1)}, bf16[32,7168]{1,0:T(8,128)(2,1)S(1)}, u32[]{:S(2)}, u32[]{:S(2)}) collective-permute-start(bf16[32,7168]{1,0:T(8,128)(2,1)} %collective-permute-done.5.refs_4_), channel_id=1, source_target_pairs={{0,4},{2,6},{8,0},{10,2},{16,8},{18,10},{24,16},{26,18},{28,24},{3... | collective-permute-start | bytes 1376264 | tf_op jit(solution)/shard_map/ppermute | solution.py:256
  34.3 25.7 %collective-permute-start.4 = (bf16[32,7168]{1,0:T(8,128)(2,1)}, bf16[32,7168]{1,0:T(8,128)(2,1)S(1)}, u32[]{:S(2)}, u32[]{:S(2)}) collective-permute-start(bf16[32,7168]{1,0:T(8,128)(2,1)} %collective-permute-done.3.refs_3_), channel_id=1, source_target_pairs={{0,8},{2,10},{8,16},{10,18},{16,24},{18,26},{24,28},{26,30},{28,20... | collective-permute-start | bytes 1376264 | tf_op jit(solution)/shard_map/ppermute | solution.py:256
  38.0 22.1 %collective-permute-start.8 = (bf16[32,7168]{1,0:T(8,128)(2,1)}, bf16[32,7168]{1,0:T(8,128)(2,1)S(1)}, u32[]{:S(2)}, u32[]{:S(2)}) collective-permute-start(bf16[32,7168]{1,0:T(8,128)(2,1)} %collective-permute-done.7.refs_5_), channel_id=1, source_target_pairs={{0,4},{2,6},{8,0},{10,2},{16,8},{18,10},{24,16},{26,18},{28,24},{3... | collective-permute-start | bytes 1376264 | tf_op jit(solution)/shard_map/ppermute | solution.py:256
  40.2 19.7 %collective-permute-start.9 = (bf16[8,7168]{1,0:T(8,128)(2,1)S(1)}, bf16[8,7168]{1,0:T(8,128)(2,1)S(1)}, u32[]{:S(2)}, u32[]{:S(2)}) collective-permute-start(bf16[8,7168]{1,0:T(8,128)(2,1)S(1)} %convolution_convert_fusion), channel_id=1, source_target_pairs={{0,28},{2,30},{8,20},{10,22},{16,12},{18,14},{24,4},{26,6},{28,0},... | collective-permute-start | bytes 344072 | tf_op jit(solution)/shard_map/ppermute | solution.py:256
  60.1 18.6 %collective-permute-start.14 = (bf16[32,7168]{1,0:T(8,128)(2,1)S(1)}, bf16[32,7168]{1,0:T(8,128)(2,1)S(1)}, u32[]{:S(2)}, u32[]{:S(2)}) collective-permute-start(bf16[32,7168]{1,0:T(8,128)(2,1)S(1)} %collective-permute-done.1.refs_0_), channel_id=1, source_target_pairs={{0,8},{2,10},{8,16},{10,18},{16,24},{18,26},{24,28},{26,30},{28,20... | collective-permute-start | bytes 1376264 | tf_op jit(solution)/shard_map/ppermute | solution.py:256
  61.4 19.8 %collective-permute-start.15 = (bf16[32,7168]{1,0:T(8,128)(2,1)S(1)}, bf16[32,7168]{1,0:T(8,128)(2,1)S(1)}, u32[]{:S(2)}, u32[]{:S(2)}) collective-permute-start(bf16[32,7168]{1,0:T(8,128)(2,1)S(1)} %collective-permute-done.4.refs_1_), channel_id=1, source_target_pairs={{0,8},{2,10},{8,16},{10,18},{16,24},{18,26},{24,28},{26,30},{28,20... | collective-permute-start | bytes 1376264 | tf_op jit(solution)/shard_map/ppermute | solution.py:256
  65.2 16.0 %collective-permute-start.16 = (bf16[32,7168]{1,0:T(8,128)(2,1)S(1)}, bf16[32,7168]{1,0:T(8,128)(2,1)S(1)}, u32[]{:S(2)}, u32[]{:S(2)}) collective-permute-start(bf16[32,7168]{1,0:T(8,128)(2,1)S(1)} %collective-permute-done.6.refs_2_), channel_id=1, source_target_pairs={{0,4},{2,6},{8,0},{10,2},{16,8},{18,10},{24,16},{26,18},{28,24},{3... | collective-permute-start | bytes 1376264 | tf_op jit(solution)/shard_map/ppermute | solution.py:256
  65.2 19.6 %collective-permute-start.17 = (bf16[32,7168]{1,0:T(8,128)(2,1)S(1)}, bf16[32,7168]{1,0:T(8,128)(2,1)S(1)}, u32[]{:S(2)}, u32[]{:S(2)}) collective-permute-start(bf16[32,7168]{1,0:T(8,128)(2,1)S(1)} %collective-permute-done.8.refs_3_), channel_id=1, source_target_pairs={{0,4},{2,6},{8,0},{10,2},{16,8},{18,10},{24,16},{26,18},{28,24},{3... | collective-permute-start | bytes 1376264 | tf_op jit(solution)/shard_map/ppermute | solution.py:256
  65.8 24.9 %collective-permute-start.13 = (f32[3,2,32,512]{3,2,1,0:T(8,128)S(1)}, f32[3,2,32,512]{3,2,1,0:T(8,128)S(1)}, u32[]{:S(2)}, u32[]{:S(2)}) collective-permute-start(f32[3,2,32,512]{3,2,1,0:T(8,128)S(1)} %get-tuple-element.67), channel_id=1, source_target_pairs={{0,2},{2,0},{8,10},{10,8},{16,18},{18,16},{24,26},{26,24},{28,30},... | collective-permute-start | bytes 1179656 | tf_op jit(solution)/shard_map/ppermute | solution.py:256
  89.2 4.3 %collective-permute-start.25 = (f32[2,16,64]{2,1,0:T(8,128)S(1)}, f32[2,16,64]{2,1,0:T(8,128)S(1)}, u32[]{:S(2)}, u32[]{:S(2)}) collective-permute-start(f32[2,16,64]{2,1,0:T(8,128)S(1)} %broadcast_select_fusion), channel_id=1, source_target_pairs={{0,1},{1,0},{2,3},{3,2},{4,5},{5,4},{6,7},{7,6},{8,9},{9,8},{10,11... | collective-permute-start | bytes 24584 | tf_op jit(solution)/shard_map/ppermute | solution.py:385
  91.4 16.0 %collective-permute-start.18 = (bf16[32,7168]{1,0:T(8,128)(2,1)S(1)}, bf16[32,7168]{1,0:T(8,128)(2,1)S(1)}, u32[]{:S(2)}, u32[]{:S(2)}) collective-permute-start(bf16[32,7168]{1,0:T(8,128)(2,1)S(1)} %collective-permute-done.14.refs_0_), channel_id=1, source_target_pairs={{0,8},{2,10},{8,16},{10,18},{16,24},{18,26},{24,28},{26,30},{28,20... | collective-permute-start | bytes 1376264 | tf_op jit(solution)/shard_map/ppermute | solution.py:256
  91.8 15.7 %collective-permute-start.19 = (bf16[32,7168]{1,0:T(8,128)(2,1)S(1)}, bf16[32,7168]{1,0:T(8,128)(2,1)S(1)}, u32[]{:S(2)}, u32[]{:S(2)}) collective-permute-start(bf16[32,7168]{1,0:T(8,128)(2,1)S(1)} %collective-permute-done.17.refs_3_), channel_id=1, source_target_pairs={{0,4},{2,6},{8,0},{10,2},{16,8},{18,10},{24,16},{26,18},{28,24},{3... | collective-permute-start | bytes 1376264 | tf_op jit(solution)/shard_map/ppermute | solution.py:256
  93.4 13.9 %collective-permute-start.22 = (f32[2,2,32,512]{3,2,1,0:T(8,128)S(1)}, f32[2,2,32,512]{3,2,1,0:T(8,128)S(1)}, u32[]{:S(2)}, u32[]{:S(2)}) collective-permute-start(f32[2,2,32,512]{3,2,1,0:T(8,128)S(1)} %get-tuple-element.95), channel_id=1, source_target_pairs={{0,2},{2,0},{8,10},{10,8},{16,18},{18,16},{24,26},{26,24},{28,30},... | collective-permute-start | bytes 786440 | tf_op jit(solution)/shard_map/ppermute | solution.py:256
  93.5 1.5 %collective-permute-start.26 = (f32[2,16,64]{2,1,0:T(8,128)S(1)}, f32[2,16,64]{2,1,0:T(8,128)S(1)}, u32[]{:S(2)}, u32[]{:S(2)}) collective-permute-start(f32[2,16,64]{2,1,0:T(8,128)S(1)} %select_add_fusion), channel_id=1, source_target_pairs={{0,2},{2,0},{8,10},{10,8},{16,18},{18,16},{24,26},{26,24},{28,30},... | collective-permute-start | bytes 24584 | tf_op jit(solution)/shard_map/ppermute | solution.py:256
  95.0 12.1 %collective-permute-start.27 = (bf16[2,16,64]{2,1,0:T(8,128)(2,1)S(1)}, bf16[2,16,64]{2,1,0:T(8,128)(2,1)S(1)}, u32[]{:S(2)}, u32[]{:S(2)}) collective-permute-start(bf16[2,16,64]{2,1,0:T(8,128)(2,1)S(1)} %add_convert_fusion), channel_id=1, source_target_pairs={{0,4},{2,6},{4,0},{6,2},{8,12},{10,14},{12,8},{14,10},{16,20},{18,... | collective-permute-start | bytes 12296 | tf_op jit(solution)/shard_map/ppermute | solution.py:389
  107.2 19.2 %collective-permute-start.28 = (bf16[4,16,64]{2,1,0:T(8,128)(2,1)S(1)}, bf16[4,16,64]{2,1,0:T(8,128)(2,1)S(1)}, u32[]{:S(2)}, u32[]{:S(2)}) collective-permute-start(bf16[4,16,64]{2,1,0:T(8,128)(2,1)S(1)} %pad_maximum_fusion.8), channel_id=1, source_target_pairs={{0,8},{2,10},{4,12},{6,14},{8,0},{10,2},{12,4},{14,6},{16,24},{18,... | collective-permute-start | bytes 24584 | tf_op jit(solution)/shard_map/ppermute | solution.py:389
  107.4 14.4 %collective-permute-start.23 = (f32[2,2,32,512]{3,2,1,0:T(8,128)S(1)}, f32[2,2,32,512]{3,2,1,0:T(8,128)S(1)}, u32[]{:S(2)}, u32[]{:S(2)}) collective-permute-start(f32[2,2,32,512]{3,2,1,0:T(8,128)S(1)} %get-tuple-element.96), channel_id=1, source_target_pairs={{0,2},{2,0},{8,10},{10,8},{16,18},{18,16},{24,26},{26,24},{28,30},... | collective-permute-start | bytes 786440 | tf_op jit(solution)/shard_map/ppermute | solution.py:256
  119.1 0.7 copy-start.3
  119.8 9.8 %collective-permute-start.20 = (f32[1,2,32,512]{3,2,1,0:T(8,128)S(1)}, f32[1,2,32,512]{3,2,1,0:T(8,128)S(1)}, u32[]{:S(2)}, u32[]{:S(2)}) collective-permute-start(f32[1,2,32,512]{3,2,1,0:T(8,128)S(1)} %get-tuple-element.90), channel_id=1, source_target_pairs={{0,2},{2,0},{8,10},{10,8},{16,18},{18,16},{24,26},{26,24},{28,30},... | collective-permute-start | bytes 393224 | tf_op jit(solution)/shard_map/ppermute | solution.py:256
  125.7 11.3 %collective-permute-start.24 = (bf16[3,64,512]{2,1,0:T(8,128)(2,1)}, bf16[3,64,512]{2,1,0:T(8,128)(2,1)S(1)}, u32[]{:S(2)}, u32[]{:S(2)}) collective-permute-start(bf16[3,64,512]{2,1,0:T(8,128)(2,1)} %get-tuple-element.98), channel_id=1, source_target_pairs={{0,1},{1,0},{2,3},{3,2},{4,5},{5,4},{6,7},{7,6},{8,9},{9,8},{10,11... | collective-permute-start | bytes 589832 | tf_op jit(solution)/shard_map/ppermute | solution.py:417
  126.4 6.9 %collective-permute-start.29 = (bf16[8,16,64]{2,1,0:T(8,128)(2,1)S(1)}, bf16[8,16,64]{2,1,0:T(8,128)(2,1)S(1)}, u32[]{:S(2)}, u32[]{:S(2)}) collective-permute-start(bf16[8,16,64]{2,1,0:T(8,128)(2,1)S(1)} %pad_maximum_fusion.6), channel_id=1, source_target_pairs={{0,16},{2,18},{4,20},{6,22},{8,24},{10,26},{12,28},{14,30},{16,0},... | collective-permute-start | bytes 49160 | tf_op jit(solution)/shard_map/ppermute | solution.py:389
  129.6 0.7 copy-start.5
  132.0 4.9 %collective-permute-start.21 = (bf16[1,64,512]{2,1,0:T(8,128)(2,1)}, bf16[1,64,512]{2,1,0:T(8,128)(2,1)S(1)}, u32[]{:S(2)}, u32[]{:S(2)}) collective-permute-start(bf16[1,64,512]{2,1,0:T(8,128)(2,1)} %get-tuple-element.92), channel_id=1, source_target_pairs={{0,1},{1,0},{2,3},{3,2},{4,5},{5,4},{6,7},{7,6},{8,9},{9,8},{10,11... | collective-permute-start | bytes 196616 | tf_op jit(solution)/shard_map/ppermute | solution.py:417
  136.9 0.6 copy-start.6
  137.0 0.7 copy-start.4

commit v4 on v3

v4 whole, which is shorter than its diff:
```python
import functools

import jax
import jax.numpy as jnp
import numpy as np
from jax import lax
from jax.experimental import pallas as pl
from jax.experimental.pallas import tpu as pltpu
from jax.sharding import PartitionSpec as P

MOST = 2
INNER = ("mp", "sub")
SWAP = [(0, 1), (1, 0)]


def tile_of(depth, most=1024):
    parts = 1
    while depth % parts or (depth // parts) % 128 or depth // parts > most:
        parts += 1
    return depth // parts


def rows_kernel(count, extra, with_base, with_low, tile, lane_ref, *refs):
    pieces, refs = refs[:count], refs[count:]
    more, refs = refs[:extra], refs[extra:]
    weights, refs = refs[: 2 * with_base], refs[2 * with_base :]
    factors, refs = refs[: 2 * with_low], refs[2 * with_low :]
    made = 2 * with_base + with_low + extra
    outs, sums, refs = refs[:made], refs[made : 2 * made], refs[2 * made :]
    depth = pieces[0].shape[1]
    first_row = pl.multiple_of(lane_ref[0] * depth, 128)
    tiles = depth // tile

    weight_copies, factor_copies = [], []
    if with_base:
        held, arrived = refs[:2]
        for index in range(tiles):
            for which, weight in enumerate(weights):
                copy = pltpu.make_async_copy(
                    weight.at[pl.ds(first_row + index * tile, tile)],
                    held.at[which, index],
                    arrived.at[which, index],
                )
                copy.start()
                weight_copies.append(copy)
    if with_low:
        table, ready = refs[-2:]
        rank = factors[0].shape[0]
        for which, factor in enumerate(factors):
            copy = pltpu.make_async_copy(
                factor.at[:, pl.ds(first_row, depth)],
                table.at[pl.ds(which * rank, rank)],
                ready.at[which],
            )
            copy.start()
            factor_copies.append(copy)

    for total in sums:
        total[...] = jnp.zeros_like(total)
    for index in range(tiles if with_base else 0):
        rows = jnp.concatenate([p[:, index * tile : (index + 1) * tile] for p in pieces], axis=0)
        for which in range(2):
            weight_copies[2 * index + which].wait()
            sums[which][...] += jnp.dot(
                rows, held[which, index], preferred_element_type=jnp.float32
            )
    for copy in factor_copies:
        copy.wait()
    if with_low:

        def step(index, carry):
            columns = pl.ds(pl.multiple_of(index * tile, 128), tile)
            rows = jnp.concatenate([p[:, columns] for p in pieces], axis=0)
            for values, total in zip([rows] + [m[:, columns] for m in more], sums[2 * with_base :]):
                total[...] += lax.dot_general(
                    values,
                    table[:, columns],
                    (((1,), (1,)), ((), ())),
                    preferred_element_type=jnp.float32,
                )
            return carry

        lax.fori_loop(0, tiles, step, 0)
    for out, total in zip(outs[: made - extra], sums):
        height = out.shape[2]
        for index in range(2 * out.shape[0]):
            lane = jnp.bitwise_xor(lane_ref[0], index % 2)
            out[index // 2, lane] = total[index * height : (index + 1) * height, :]
    for out, total in zip(outs[made - extra :], sums[made - extra :]):
        out[...] = total[...]


def rows_product(lane, row_count, pieces, weights=(), factors=(), more=()):
    count = len(pieces)
    depth = pieces[0].shape[1]
    total = sum(piece.shape[0] for piece in pieces)
    nodes = total // (2 * row_count)
    tile = tile_of(depth)
    sizes = [w.shape[1] for w in weights]
    if factors:
        sizes.append(sum(f.shape[0] for f in factors))
    out_shape = [
        jax.ShapeDtypeStruct((nodes, 2, row_count, size), jnp.float32) for size in sizes
    ]
    scratch = [pltpu.VMEM((total, size), jnp.float32) for size in sizes]
    for m in more:
        out_shape.append(jax.ShapeDtypeStruct((m.shape[0], sizes[-1]), jnp.float32))
        scratch.append(pltpu.VMEM((m.shape[0], sizes[-1]), jnp.float32))
    if weights:
        scratch.append(pltpu.VMEM((2, depth // tile, tile, sizes[0]), jnp.bfloat16))
        scratch.append(pltpu.SemaphoreType.DMA((2, depth // tile)))
    if factors:
        scratch.append(pltpu.VMEM((sizes[-1], depth), jnp.bfloat16))
        scratch.append(pltpu.SemaphoreType.DMA((2,)))
    return pl.pallas_call(
        functools.partial(
            rows_kernel, count, len(more), int(bool(weights)), int(bool(factors)), tile
        ),
        in_specs=[pl.BlockSpec(memory_space=pltpu.SMEM)]
        + [pl.BlockSpec(memory_space=pltpu.VMEM)] * (count + len(more))
        + [pl.BlockSpec(memory_space=pl.ANY)] * (len(weights) + len(factors)),
        out_specs=[pl.BlockSpec(memory_space=pltpu.VMEM)] * len(out_shape),
        out_shape=out_shape,
        scratch_shapes=scratch,
        compiler_params=pltpu.CompilerParams(vmem_limit_bytes=40 * 2**20),
        cost_estimate=pl.CostEstimate(
            flops=total * depth * sum(sizes) // 64,
            bytes_accessed=depth * sum(sizes) // 32,
            transcendentals=0,
        ),
    )(lane, *pieces, *more, *weights, *factors)


def hidden_of(gate, up):
    return (jax.nn.silu(gate.astype(jnp.float32)) * up.astype(jnp.float32)).astype(jnp.bfloat16)


def slots_of(row_adapter_index, adapter_storage_slot):
    names = jnp.arange(adapter_storage_slot.shape[0], dtype=jnp.int32)
    same = row_adapter_index == names[None, :]
    return jnp.sum(jnp.where(same, adapter_storage_slot[None, :], 0), axis=1)


def gathered(
    gate_activation,
    up_activation,
    down_base_weight,
    first_factor_table,
    second_factor_table,
    row_adapter_index,
    adapter_storage_slot,
):
    hidden = hidden_of(gate_activation, up_activation)
    row_count = hidden.shape[0]
    owners = lax.axis_size("wide")
    local_adapter = first_factor_table.shape[0]
    slots = local_adapter * owners
    rank_portion = second_factor_table.shape[1]
    home = lax.axis_index("wide")
    slot_all = slots_of(row_adapter_index, adapter_storage_slot)
    blocks = slot_all.reshape(owners, row_count)
    order = jnp.arange(row_count, dtype=jnp.int32)
    earlier = (blocks[:, :, None] == blocks[:, None, :]) & (order[None, :] < order[:, None])
    position = jnp.sum(earlier.astype(jnp.int32), axis=2)
    rows = lax.all_gather(hidden, "wide", axis=0, tiled=True)
    base = jnp.dot(rows, down_base_weight, preferred_element_type=jnp.float32)
    low = jnp.einsum("re,nqe->nrq", rows, first_factor_table, preferred_element_type=jnp.float32)
    low = low.reshape(local_adapter, owners, row_count, low.shape[2])
    own = home * local_adapter + jnp.arange(local_adapter, dtype=jnp.int32)
    kept = []
    for item in range(MOST):
        mask = (blocks[None] == own[:, None, None]) & (position == item)[None]
        kept.append(jnp.sum(jnp.where(mask[..., None], low, 0), axis=2))
    low = lax.psum_scatter(jnp.stack(kept, axis=2), INNER, scatter_dimension=3, tiled=True)
    low = lax.all_gather(low.astype(jnp.bfloat16), "wide", axis=0, tiled=True)
    spread = 0
    for item in range(MOST):
        mask = (blocks[None] == jnp.arange(slots, dtype=jnp.int32)[:, None, None]) & (position == item)
        spread += jnp.where(mask[..., None], low[:, :, item][:, :, None], 0)
    spread = spread.reshape(slots, owners * row_count, rank_portion)
    delta = jnp.einsum("srq,sqw->rw", spread, second_factor_table, preferred_element_type=jnp.float32)
    total = base + delta
    return lax.psum_scatter(total, INNER, scatter_dimension=0, tiled=True).astype(jnp.bfloat16)


def ring_order(nodes):
    return list(range(0, nodes, 2)) + list(range(nodes - 1, 0, -2))


def ringed(
    gate_activation,
    up_activation,
    down_base_weight,
    first_factor_table,
    second_factor_table,
    row_adapter_index,
    adapter_storage_slot,
):
    f32, bf16 = jnp.float32, jnp.bfloat16
    row_count, width_part = gate_activation.shape
    owners = lax.axis_size("wide")
    nodes = owners // 2
    far = nodes // 2
    steps = far - 1
    own_nodes = nodes // 2
    own_blocks = owners // 2
    group_rows = 2 * row_count
    order = ring_order(nodes)
    depth = width_part // 2
    width = down_base_weight.shape[1]
    rank = first_factor_table.shape[1]

    table = []
    for w in range(owners):
        p, lane = order.index(w // 2), w % 2
        at = lambda shift: order[(p + shift) % nodes]
        arrivals = [at(0)] + [at(s * k) for k in range(1, far) for s in (-1, 1)]
        row = [2 * node + side for node in arrivals for side in (0, 1)]
        row += [2 * at(far) + (lane ^ side) for side in (0, 1)]
        for half in (0, 1):
            here = [(at(s) < own_nodes) == (half == 0) for s in range(far)]
            row += [int(h) for h in here]
            row += [at(s if h else s + far) % own_nodes for s, h in enumerate(here)]
        table.append(row)
    home = lax.axis_index("wide")
    part = lax.axis_index(INNER)
    side = jnp.bitwise_and(home, 1)
    lane = side[None]

    def moved(shift, cross=0):
        return [
            (order[p] * 2 + c, order[(p + shift) % nodes] * 2 + (c ^ cross))
            for p in range(nodes)
            for c in (0, 1)
        ]

    def send(value, shift, cross=0):
        return lax.ppermute(value, "wide", moved(shift, cross))

    def half_of(value, which, axis):
        return lax.dynamic_slice_in_dim(value, which * depth, depth, axis)

    facts = lax.dynamic_index_in_dim(
        jnp.asarray(np.array(table, np.int32)), home, 0, keepdims=False
    )
    edges = np.cumsum([0, 2 * (nodes - 1), 2, far, far, far, far])
    arrived, far_wide, *rest = [facts[a:b] for a, b in zip(edges[:-1], edges[1:])]
    flags = jnp.where(part == 0, rest[0], rest[2])
    target = jnp.where(part == 0, rest[1], rest[3])
    slot_all = slots_of(row_adapter_index, adapter_storage_slot).reshape(owners, row_count)
    ranks = jnp.arange(row_count, dtype=jnp.int32)
    earlier = (slot_all[:, :, None] == slot_all[:, None, :]) & (ranks[None, :] < ranks[:, None])
    position = jnp.sum(earlier.astype(jnp.int32), axis=2)
    items = jnp.arange(MOST, dtype=jnp.int32)

    sides = jnp.arange(2, dtype=jnp.int32)
    own_wide = jnp.bitwise_xor(home, sides)
    blocks = jnp.arange(owners, dtype=jnp.int32)
    own_is = own_wide[:, None, None] == blocks[None, :, None]
    own_slot = jnp.sum(jnp.where(own_is, slot_all[None], 0), axis=1)
    own_position = jnp.sum(jnp.where(own_is, position[None], 0), axis=1)
    pick = (own_slot[None, :, None, :] == far_wide[:, None, None, None]) & (
        own_position[None, :, None, :] == items[None, None, :, None]
    )
    pick = jnp.where(
        (sides[:, None] == sides[None, :])[None, :, None, :, None], pick[:, :, :, None, :], False
    ).reshape(4 * MOST, group_rows).astype(bf16)

    keep = hidden_of(half_of(gate_activation, side, 1), half_of(up_activation, side, 1))
    give = hidden_of(half_of(gate_activation, 1 - side, 1), half_of(up_activation, 1 - side, 1))
    twin, slot_all, position, pick = lax.optimization_barrier(
        (send(give, 0, 1), slot_all, position, pick)
    )
    block = jnp.concatenate([keep, twin], axis=0)
    right, left = send(block, 1), send(block, -1)

    weight, first, block = lax.optimization_barrier(
        (down_base_weight, first_factor_table[0], block)
    )
    weights = (weight, send(weight, 0, 1))
    factors = (first, send(first, 0, 1))
    slot_all, position, weights = lax.optimization_barrier((slot_all, position, weights))

    picked = jnp.dot(pick, block, preferred_element_type=f32).astype(bf16)
    far_rows = send(picked, far)

    slot_here = lax.dynamic_slice_in_dim(slot_all, part * own_blocks, own_blocks)
    position_here = lax.dynamic_slice_in_dim(position, part * own_blocks, own_blocks)
    came = jnp.bitwise_xor(home, blocks)
    spots = (
        (slot_here[:, :, None, None, None] == came[:, None, None])
        & (position_here[:, :, None, None, None] == items)
        & (jnp.arange(own_blocks)[:, None] == jnp.arange(own_blocks)[None, :])[:, None, None, :, None]
    )
    spots = spots.astype(bf16).reshape(own_blocks * row_count, owners * own_blocks * MOST)
    mask = jnp.repeat(
        (slot_here.reshape(-1)[:, None] == blocks[None, :]).astype(bf16), rank, axis=1
    )

    other = lax.ppermute(second_factor_table, INNER, SWAP)
    second = jnp.where(
        part == 0,
        jnp.concatenate([second_factor_table, other], axis=1),
        jnp.concatenate([other, second_factor_table], axis=1),
    ).reshape(owners * rank, width)

    def chosen(slot):
        near = (
            (arrived[None, None, :, None] == blocks[:, None, None, None])
            & (slot_all == slot)[:, None, None, :]
            & (position[:, None, None, :] == items[None, :, None, None])
        ).reshape(owners * MOST, -1)
        there = (
            (far_wide[None, None, :, None] == blocks[:, None, None, None])
            & (items[:, None] == items[None, :])[None, :, None, :]
        ).reshape(owners * MOST, -1)
        return jnp.concatenate([near, there], axis=1).astype(f32)

    chosen_mine, chosen_sib = chosen(home), chosen(jnp.bitwise_xor(home, 1))

    results, sibs, lows = [], [], []

    def add(result):
        results.append(result)
        sibs.append(send(result[1], 0, 1))

    ready = (second, spots, mask, chosen_mine, chosen_sib)
    pieces = [block]
    for step in range(1, steps + 1):
        if step > 1:
            right, left, result = lax.optimization_barrier((right, left, result))
            add(result[:2])
            lows.append(result[2])
        pieces += [right, left]
        if step < steps:
            right, left = send(right, 1), send(left, -1)
            result = rows_product(lane, row_count, pieces, weights, factors)
        else:
            right, left, far_rows, ready, sibs[0] = lax.optimization_barrier(
                (right, left, far_rows, ready, sibs[0])
            )
            last = [send(right[:row_count], 1), send(left[row_count:], -1)]
            second, spots, mask, chosen_mine, chosen_sib = ready
            low, far_low = rows_product(lane, row_count, pieces, (), factors, (far_rows,))
            lows.append(low)
            result = rows_product(lane, row_count, pieces, weights)
        pieces = []
    result, last, sibs = lax.optimization_barrier((result, last, sibs))
    add(result)

    def node(values, shift):
        if shift == 0:
            return values[0][0]
        if shift == far:
            return values[-1][0]
        step = min(shift, nodes - shift)
        return values[step - 1][(1 if step == 1 else 0) + (0 if shift > far else 1)]

    def total(shift):
        both = node([r[0] for r in results], shift) + node(sibs, shift)
        return both.reshape(1, group_rows, width)

    def over_mp(shifts):
        pairs = [(flags[s : s + 1, None, None] == 1, total(s), total(s + far)) for s in shifts]
        sent = jnp.concatenate([jnp.where(f, b, a).astype(bf16) for f, a, b in pairs], axis=0)
        got = lax.ppermute(sent, INNER, SWAP)
        return [jnp.where(f, a, b) for f, a, b in pairs], got


    low = jnp.concatenate([values.reshape(-1, 2 * rank) for values in lows], axis=0)
    count = 2 * MOST

    def compact(choice, values, far_values):
        return jnp.dot(
            choice,
            jnp.concatenate([values, far_values], axis=0),
            precision=lax.Precision.HIGHEST,
        )

    low = jnp.stack(
        [
            compact(chosen_mine, low[:, :rank], far_low[:count, :rank]),
            compact(chosen_sib, low[:, rank:], far_low[count:, rank:]),
        ]
    )
    half = own_blocks * MOST
    kept = jnp.where(part == 0, low[:, :half], low[:, half:])
    sent = jnp.where(part == 0, low[:, half:], low[:, :half])
    low = kept + lax.ppermute(sent, INNER, SWAP)
    low, last = lax.optimization_barrier((low, last))
    low = (low + send(low, 0, 1)[::-1]).astype(bf16)
    kept, got = over_mp(list(range(1, far)))
    add(rows_product(lane, row_count, last, weights))
    gap = 2
    while gap < owners:
        if gap * 2 == owners:
            low, results[-1], got = lax.optimization_barrier((low, results[-1], got))
        other = lax.ppermute(low, "wide", [(w, w ^ gap) for w in range(owners)])
        low = jnp.concatenate([low, other], axis=0)
        gap *= 2
    own_low = jnp.dot(spots, low.reshape(owners * half, rank), preferred_element_type=f32)
    copies = jnp.tile(jnp.eye(rank, dtype=bf16), (1, owners))
    spread = jnp.dot(own_low.astype(bf16), copies, preferred_element_type=f32).astype(bf16) * mask
    delta = jnp.dot(spread, second, preferred_element_type=f32)
    delta = delta.reshape(own_nodes, group_rows, width)

    places = jnp.arange(own_nodes, dtype=jnp.int32)[:, None, None]
    out = delta
    for pair, value in enumerate(kept, 1):
        value = value + got[pair - 1 : pair].astype(f32)
        out = out + jnp.where(places == target[pair : pair + 1, None, None], value, 0)
    kept, got = over_mp([0])
    out = out + jnp.where(places == target[:1, None, None], kept[0] + got.astype(f32), 0)
    return out.astype(bf16).reshape(-1, width)


def solution(mesh):
    shape = dict(mesh.shape)
    wide, inner = shape["wide"], shape["mp"] * shape["sub"]
    paired = shape["sub"] == 1 and inner == 2 and wide % 8 == 0 and wide & (wide - 1) == 0
    if paired:
        nodes = wide // 2
        order = ring_order(nodes)
        paired = all(
            (order[p] < nodes // 2) != (order[(p + nodes // 2) % nodes] < nodes // 2)
            for p in range(nodes)
        )
    return jax.shard_map(
        ringed if paired else gathered,
        mesh=mesh,
        in_specs=(
            P(("groups", "wide"), ("mp", "sub")),
            P(("groups", "wide"), ("mp", "sub")),
            P(("mp", "sub"), "wide"),
            P("wide", None, ("mp", "sub")),
            P(None, ("mp", "sub"), "wide"),
            P("groups", None),
            P(),
        ),
        out_specs=P(("groups", "mp", "sub"), "wide"),
        check_vma=False,
    )
```

time: 141 us -> 132 us (0.936)
  Pallas kernels: 61.5 us -> 35.6 us
  waiting for transfers between devices: 21.5 us -> 33.9 us
  starting transfers between devices: 33.1 us -> 28.2 us
  matrix products: 0.77 us -> 4.31 us
  other arithmetic: 12.8 us -> 16 us
  between operations: 0.39 us -> 3.11 us
    pallas_call x5, Pallas kernels: 52.4 us -> 35.6 us  [rows_product(): pl.pallas_call(functools.partial(rows_kernel, count, len(more), int(bool(...]
    pallas_call x4 -> x0, Pallas kernels: 9.13 us -> none  [the longest x2 5.07 us: whole_call(): pl.pallas_call(kernel, in_specs=[pl.BlockSpec(memory_space=pltpu.SMEM)] *...]
    ppermute x3, waiting for transfers between devices: 0.01 us -> 7.84 us  [ringed(): other = lax.ppermute(low, 'wide', [(w, w ^ gap) for w in range(owners)])]
    ppermute x23 -> x17, starting transfers between devices: 25.6 us -> 19.3 us  [send(): return lax.ppermute(value, 'wide', moved(shift, cross))]
    ppermute x23 -> x17, waiting for transfers between devices: 21.5 us -> 25.7 us  [send(): return lax.ppermute(value, 'wide', moved(shift, cross))]
    dot_general x1 -> x3, matrix products: 0.22 us -> 3.76 us  [the longest x1 1.71 us: ringed(): jnp.dot(own_low.astype(bf16), copies, preferred_element_type=f32)]
    another operation x4 -> x0, other arithmetic: 3.12 us -> none  [over_mp(): group = jnp.stack([node(values, s + offset) for s in shifts])]
    unnamed x18 -> x14, local copies, waits for them, and re-layouts: 3.26 us -> 0.82 us
  transfers between devices with their start and end apart: 30 -> 24, of which waited for: 8 -> 8; matrix products, arithmetic and copies ran while one was open for 12% -> 16% of each run, Pallas kernels for 42% -> 24%
where the time goes in v4:
time: 132 us; the launch traced here: 131 us
  Pallas kernels  35.6 us (27%)
  waiting for transfers between devices  33.9 us (26%)
  starting transfers between devices  28.2 us (21%)
  other arithmetic  16 us (12%)
  local copies, waits for them, and re-layouts  9.89 us (7%)
  matrix products  4.31 us (3%)
  between operations  3.11 us (2%)
    pallas_call x5, Pallas kernels, rows_product(): pl.pallas_call(functools.partial(rows_kernel, count, len(more), int(bool(...  35.6 us
    ppermute x17, waiting for transfers between devices, send(): return lax.ppermute(value, 'wide', moved(shift, cross))  25.7 us
    ppermute x17, starting transfers between devices, send(): return lax.ppermute(value, 'wide', moved(shift, cross))  19.3 us
    ppermute x3, waiting for transfers between devices, ringed(): other = lax.ppermute(low, 'wide', [(w, w ^ gap) for w in range(owners)])  7.84 us
    ppermute x2, starting transfers between devices, over_mp(): got = lax.ppermute(sent, INNER, SWAP)  3.03 us
    ppermute x1, starting transfers between devices, ringed(): other = lax.ppermute(second_factor_table, INNER, SWAP)  2.95 us
    convert_element_type x1, other arithmetic, hidden_of(): (jax.nn.silu(gate.astype(jnp.float32)) * up.astype(jnp.float32)).astype(j...  2.87 us
    select_n x1, other arithmetic, ringed(): jnp.where(part == 0, jnp.concatenate([second_factor_table, other], axis=1...  2.84 us
  transfers between devices with their start and end apart: 24, of which 8 were waited for; matrix products, arithmetic and copies ran while one was open for 16% of the time, Pallas kernels for 24%

profile of v4, /device:TPU:0, one launch (start us, length us, event | category | flops | bytes accessed | tf_op | source)
XLA Modules:
  0.0 131.0 jit_solution(8103841977247770064)
XLA Ops:
  0.0 2.9 %fusion.14 = (bf16[32,7168]{1,0:T(8,128)(2,1)}, bf16[32,7168]{1,0:T(8,128)(2,1)S(1)}) fusion(bf16[32,14336]{1,0:T(8,128)(2,1)} %param.9, s32[]{:T(128)S(6)} %select_n.193, bf16[32,14336]{1,0:T(8,128)(2,1)} %param.8, s32[]{:T(128)S(6)} %select_n.194), kind=kLoop, calls=%fused_computation.27 | loop fusion | flops 3670016 | bytes 2752520 | tf_op jit(solution)/shard_map/convert_element_type | solution.py:135
  2.9 0.5 collective-permute-start
  3.6 0.7 constant_dynamic-slice_fusion
  4.4 0.5 convert_reduce_fusion
  5.3 0.8 copy-done.4
  6.1 1.2 pad_maximum_fusion.refs_0_
  7.4 2.9 %collective-permute-start.10 = (bf16[16,32,512]{2,1,0:T(8,128)(2,1)}, bf16[16,32,512]{2,1,0:T(8,128)(2,1)}, u32[]{:S(2)}, u32[]{:S(2)}) collective-permute-start(bf16[16,32,512]{2,1,0:T(8,128)(2,1)} %param.12), channel_id=1, source_target_pairs={{0,1},{1,0},{2,3},{3,2},{4,5},{5,4},{6,7},{7,6},{8,9},{9,8},{10,11... | collective-permute-start | bytes 1572872 | tf_op jit(solution)/shard_map/ppermute | solution.py:300
  10.4 1.6 %collective-permute-start.1 = (bf16[64,7168]{1,0:T(8,128)(2,1)S(1)}, bf16[64,7168]{1,0:T(8,128)(2,1)}, u32[]{:S(2)}, u32[]{:S(2)}) collective-permute-start(bf16[64,7168]{1,0:T(8,128)(2,1)S(1)} %pad_maximum_fusion.refs_0_), channel_id=1, source_target_pairs={{0,8},{2,10},{8,16},{10,18},{16,24},{18,26},{24,28},{26,30},{28,20... | collective-permute-start | bytes 2752520 | tf_op jit(solution)/shard_map/ppermute | solution.py:238
  12.6 0.7 fusion.30
  13.4 19.2 %collective-permute-done.1.refs_1_ = bf16[64,7168]{1,0:T(8,128)(2,1)} collective-permute-done((bf16[64,7168]{1,0:T(8,128)(2,1)S(1)}, bf16[64,7168]{1,0:T(8,128)(2,1)}, u32[]{:S(2)}, u32[]{:S(2)}) %collective-permute-start.1) | collective-permute-done | bytes 917536 | tf_op jit(solution)/shard_map/ppermute | solution.py:238
  32.6 1.6 %collective-permute-start.2 = (bf16[64,7168]{1,0:T(8,128)(2,1)}, bf16[64,7168]{1,0:T(8,128)(2,1)}, u32[]{:S(2)}, u32[]{:S(2)}) collective-permute-start(bf16[64,7168]{1,0:T(8,128)(2,1)} %collective-permute-done.1.refs_1_), channel_id=1, source_target_pairs={{0,8},{2,10},{8,16},{10,18},{16,24},{18,26},{24,28},{26,30},{28,20... | collective-permute-start | bytes 2752520 | tf_op jit(solution)/shard_map/ppermute | solution.py:238
  34.6 0.6 iota_compare_fusion.12
  35.5 0.9 convolution_convert_fusion
  36.4 4.6 %collective-permute-start.9 = (bf16[8,7168]{1,0:T(8,128)(2,1)}, bf16[8,7168]{1,0:T(8,128)(2,1)S(1)}, u32[]{:S(2)}, u32[]{:S(2)}) collective-permute-start(bf16[8,7168]{1,0:T(8,128)(2,1)} %convolution_convert_fusion), channel_id=1, source_target_pairs={{0,28},{2,30},{8,20},{10,22},{16,12},{18,14},{24,4},{26,6},{28,0},... | collective-permute-start | bytes 344072 | tf_op jit(solution)/shard_map/ppermute | solution.py:238
  41.0 2.8 %maximum_select_fusion = bf16[16,64,512]{2,1,0:T(8,128)(2,1)} fusion(bf16[16,32,512]{2,1,0:T(8,128)(2,1)} %collective-permute-done.10, bf16[16,32,512]{2,1,0:T(8,128)(2,1)} %param.12, pred[]{:T(512)S(6)} %eq.396), kind=kLoop, calls=%fused_computation.15 | loop fusion | flops 4718592 | bytes 2097153 | tf_op jit(solution)/shard_map/jit(_where)/select_n | solution.py:301
  43.8 9.9 %shard_map.82 = (f32[3,2,32,512]{3,2,1,0:T(8,128)S(1)}, f32[3,2,32,512]{3,2,1,0:T(8,128)}, f32[3,2,32,128]{3,2,1,0:T(8,128)S(1)}) custom-call(s32[1]{0:T(128)} %bitcast.2.lane_ref, bf16[64,7168]{1,0:T(8,128)(2,1)S(1)} %pad_maximum_fusion.refs_0_, bf16[64,7168]{1,0:T(8,128)(2,1)} %collective-permute-done.1.refs_1_, ...), custom_call_target="tpu_custom_call" | custom-call | flops 24772608 | bytes 258048 | tf_op jit(solution)/shard_map/pallas_call | solution.py:115
  53.7 0.7 collective-permute-done.2.refs_0_
  54.4 1.3 %collective-permute-done.4.refs_1_ = bf16[64,7168]{1,0:T(8,128)(2,1)} collective-permute-done((bf16[64,7168]{1,0:T(8,128)(2,1)}, bf16[64,7168]{1,0:T(8,128)(2,1)}, u32[]{:S(2)}, u32[]{:S(2)}) %collective-permute-start.4) | collective-permute-done | bytes 917536 | tf_op jit(solution)/shard_map/ppermute | solution.py:238
  55.8 5.3 %collective-permute-start.7 = (bf16[64,7168]{1,0:T(8,128)(2,1)}, bf16[64,7168]{1,0:T(8,128)(2,1)S(1)}, u32[]{:S(2)}, u32[]{:S(2)}) collective-permute-start(bf16[64,7168]{1,0:T(8,128)(2,1)} %collective-permute-done.2.refs_0_), channel_id=1, source_target_pairs={{0,8},{2,10},{8,16},{10,18},{16,24},{18,26},{24,28},{26,30},{28,20... | collective-permute-start | bytes 2752520 | tf_op jit(solution)/shard_map/ppermute | solution.py:238
  61.4 1.0 and_convert_fusion
  62.6 2.1 %reshape.691 = bf16[256,256]{0,1:T(8,128)(2,1)} reshape(bf16[8,32,16,8,2]{1,0,4,3,2:T(8,128)(2,1)} %and_convert_fusion) | data formatting | bytes 262144 | tf_op jit(solution)/shard_map/convert_element_type | solution.py:295
  65.0 8.8 %shard_map.83 = (f32[2,2,32,512]{3,2,1,0:T(8,128)S(1)}, f32[2,2,32,512]{3,2,1,0:T(8,128)S(1)}, f32[2,2,32,128]{3,2,1,0:T(8,128)S(1)}) custom-call(s32[1]{0:T(128)} %bitcast.2.lane_ref, bf16[64,7168]{1,0:T(8,128)(2,1)} %collective-permute-done.2.refs_0_, bf16[64,7168]{1,0:T(8,128)(2,1)} %collective-permute-done.4.refs_1_, bf16[14336,512]{1,0:T(8,128)(2,1)} %refs_2_.2, ...), custom_call_target="tpu_custom_call" | custom-call | flops 16515072 | bytes 258048 | tf_op jit(solution)/shard_map/pallas_call | solution.py:115
  73.9 3.7 %collective-permute-done.7.refs_0_ = bf16[64,7168]{1,0:T(8,128)(2,1)S(1)} collective-permute-done((bf16[64,7168]{1,0:T(8,128)(2,1)}, bf16[64,7168]{1,0:T(8,128)(2,1)S(1)}, u32[]{:S(2)}, u32[]{:S(2)}) %collective-permute-start.7) | collective-permute-done | bytes 917536 | tf_op jit(solution)/shard_map/ppermute | solution.py:238
  77.5 0.8 collective-permute-done.8.refs_1_
  78.3 0.8 broadcast_in_dim.257
  79.2 4.4 %shard_map.84 = (f32[2,2,32,128]{3,2,1,0:T(8,128)S(1)}, f32[8,128]{1,0:T(8,128)S(1)}) custom-call(s32[1]{0:T(128)} %bitcast.2.lane_ref, bf16[64,7168]{1,0:T(8,128)(2,1)S(1)} %collective-permute-done.7.refs_0_, bf16[64,7168]{1,0:T(8,128)(2,1)} %collective-permute-done.8.refs_1_, bf16[8,7168]{1,0:T(8,128)(2,1)S(1)} %collective-permute-done.9.refs_2_, ...), custom_call_target="tpu_custom_call" | custom-call | flops 1835008 | bytes 28672 | tf_op jit(solution)/shard_map/pallas_call | solution.py:115
  83.8 3.3 %collective-permute-start.13 = (bf16[32,7168]{1,0:T(8,128)(2,1)S(1)}, bf16[32,7168]{1,0:T(8,128)(2,1)S(1)}, u32[]{:S(2)}, u32[]{:S(2)}) collective-permute-start(bf16[32,7168]{1,0:T(8,128)(2,1)S(1)} %slice.141), channel_id=1, source_target_pairs={{0,8},{2,10},{8,16},{10,18},{16,24},{18,26},{24,28},{26,30},{28,20... | collective-permute-start | bytes 1376264 | tf_op jit(solution)/shard_map/ppermute | solution.py:238
  87.1 1.0 slice.142
  89.0 0.6 collective-permute-start.12
  89.6 0.6 iota_compare_fusion.13
  90.2 6.8 %shard_map.85 = (f32[2,2,32,512]{3,2,1,0:T(8,128)S(1)}, f32[2,2,32,512]{3,2,1,0:T(8,128)S(1)}) custom-call(s32[1]{0:T(128)} %bitcast.2.lane_ref, bf16[64,7168]{1,0:T(8,128)(2,1)S(1)} %collective-permute-done.7.refs_0_, bf16[64,7168]{1,0:T(8,128)(2,1)} %collective-permute-done.8.refs_1_, bf16[14336,512]{1,0:T(8,128)(2,1)} %refs_2_.2, ...), custom_call_target="tpu_custom_call" | custom-call | flops 14680064 | bytes 229376 | tf_op jit(solution)/shard_map/pallas_call | solution.py:115
  97.1 0.6 collective-permute-start.16
  97.7 0.6 iota_compare_fusion.14
  100.3 5.6 %shard_map.86 = (f32[1,2,32,512]{3,2,1,0:T(8,128)S(1)}, f32[1,2,32,512]{3,2,1,0:T(8,128)S(1)}) custom-call(s32[1]{0:T(128)} %bitcast.2.lane_ref, bf16[32,7168]{1,0:T(8,128)(2,1)S(1)} %collective-permute-done.13.refs_0_, bf16[32,7168]{1,0:T(8,128)(2,1)S(1)} %collective-permute-done.14.refs_1_, bf16[14336,512]{1,0:T(8,128)(2,1)} %refs_2_.2, ...), custom_call_target="tpu_custom_call" | custom-call | flops 7340032 | bytes 229376 | tf_op jit(solution)/shard_map/pallas_call | solution.py:115
  106.0 0.6 collective-permute-start.22
  106.8 3.5 %collective-permute-done.17 = bf16[2,16,64]{2,1,0:T(8,128)(2,1)S(1)} collective-permute-done((bf16[2,16,64]{2,1,0:T(8,128)(2,1)S(1)}, bf16[2,16,64]{2,1,0:T(8,128)(2,1)S(1)}, u32[]{:S(2)}, u32[]{:S(2)}) %collective-permute-start.17) | collective-permute-done | bytes 4128 | tf_op jit(solution)/shard_map/ppermute | solution.py:398
  110.3 2.1 %collective-permute-start.18 = (bf16[4,16,64]{2,1,0:T(8,128)(2,1)S(1)}, bf16[4,16,64]{2,1,0:T(8,128)(2,1)S(1)}, u32[]{:S(2)}, u32[]{:S(2)}) collective-permute-start(bf16[4,16,64]{2,1,0:T(8,128)(2,1)S(1)} %pad_maximum_fusion.6), channel_id=1, source_target_pairs={{0,8},{2,10},{4,12},{6,14},{8,0},{10,2},{12,4},{14,6},{16,24},{18,... | collective-permute-start | bytes 24584 | tf_op jit(solution)/shard_map/ppermute | solution.py:398
  112.4 1.1 broadcast_select_fusion.3
  113.5 1.5 %collective-permute-start.20 = (bf16[3,64,512]{2,1,0:T(8,128)(2,1)S(1)}, bf16[3,64,512]{2,1,0:T(8,128)(2,1)S(1)}, u32[]{:S(2)}, u32[]{:S(2)}) collective-permute-start(bf16[3,64,512]{2,1,0:T(8,128)(2,1)S(1)} %pad_maximum_fusion.2), channel_id=1, source_target_pairs={{0,1},{1,0},{2,3},{3,2},{4,5},{5,4},{6,7},{7,6},{8,9},{9,8},{10,11... | collective-permute-start | bytes 589832 | tf_op jit(solution)/shard_map/ppermute | solution.py:366
  115.0 0.6 iota_compare_fusion.15
  117.0 0.9 tile.10
  117.8 1.0 copy.18
  119.2 1.6 %select_convert_fusion = (bf16[1,2,32,512]{3,2,1,0:T(8,128)(2,1)}, f32[1,2,32,512]{3,2,1,0:T(8,128)}) fusion(pred[]{:T(512)} %bitcast.32, f32[1,2,32,512]{3,2,1,0:T(8,128)S(1)} %get-tuple-element.112, f32[1,2,32,512]{3,2,1,0:T(8,128)S(1)} %collective-permute-done.22, f32[3,2,32,512]{3,2,1,0:T(8,128)} %collective-permute-done.11, ...), kind=kLoop, calls=%fused_computation.47 | loop fusion | flops 163840 | bytes 720897 | tf_op jit(solution)/shard_map/convert_element_type | solution.py:365
  120.8 1.5 %collective-permute-start.23 = (bf16[1,64,512]{2,1,0:T(8,128)(2,1)}, bf16[1,64,512]{2,1,0:T(8,128)(2,1)}, u32[]{:S(2)}, u32[]{:S(2)}) collective-permute-start(bf16[1,64,512]{2,1,0:T(8,128)(2,1)} %bitcast.34), channel_id=1, source_target_pairs={{0,1},{1,0},{2,3},{3,2},{4,5},{5,4},{6,7},{7,6},{8,9},{9,8},{10,11... | collective-permute-start | bytes 196616 | tf_op jit(solution)/shard_map/ppermute | solution.py:366
  122.8 4.3 %collective-permute-done.21 = bf16[8,16,64]{2,1,0:T(8,128)(2,1)S(1)} collective-permute-done((bf16[8,16,64]{2,1,0:T(8,128)(2,1)S(1)}, bf16[8,16,64]{2,1,0:T(8,128)(2,1)S(1)}, u32[]{:S(2)}, u32[]{:S(2)}) %collective-permute-start.21) | collective-permute-done | bytes 16416 | tf_op jit(solution)/shard_map/ppermute | solution.py:398
  127.1 1.7 %fusion.4 = bf16[256,1024]{1,0:T(8,128)(2,1)S(1)} fusion(bf16[256,1024]{1,0:T(8,128)(2,1)} %copy.18, bf16[64,1024]{1,0:T(8,128)(2,1)} %tile.10, bf16[256,256]{0,1:T(8,128)(2,1)} %reshape.691, bf16[256,64]{1,0:T(8,128)(2,1)S(1)} %bitcast.82), kind=kOutput, calls=%fused_computation.12 | convolution fusion | flops 43270144 | bytes 1343488 | tf_op jit(solution)/shard_map/dot_general | solution.py:403
  128.9 0.9 bitcast_add_fusion
  129.8 1.2 fusion.3
  (106 shorter events, 6.1 us)
Async XLA Ops:
  0.0 3.4 %copy-start.6 = (s32[16]{0:T(128)S(1)}, s32[16]{0:T(128)}, u32[]{:S(2)}) copy-start(s32[16]{0:T(128)} %param.14) | copy-start | bytes 196
  0.0 3.4 %copy-start.5 = (s32[512,1]{0,1:T(1,128)S(1)}, s32[512,1]{0,1:T(1,128)}, u32[]{:S(2)}) copy-start(s32[512,1]{0,1:T(1,128)} %param.13) | copy-start | bytes 6148
  0.0 12.5 %copy-start = (bf16[1,64,14336]{2,1,0:T(8,128)(2,1)S(1)}, bf16[1,64,14336]{2,1,0:T(8,128)(2,1)}, u32[]{:S(2)}) copy-start(bf16[1,64,14336]{2,1,0:T(8,128)(2,1)} %param.11) | copy-start | bytes 5505028
  2.9 2.4 %collective-permute-start = (bf16[32,7168]{1,0:T(8,128)(2,1)S(1)}, bf16[32,7168]{1,0:T(8,128)(2,1)S(1)}, u32[]{:S(2)}, u32[]{:S(2)}) collective-permute-start(bf16[32,7168]{1,0:T(8,128)(2,1)S(1)} %get-tuple-element.116), channel_id=1, source_target_pairs={{0,2},{2,0},{8,10},{10,8},{16,18},{18,16},{24,26},{26,24},{28,30},... | collective-permute-start | bytes 1376264 | tf_op jit(solution)/shard_map/ppermute | solution.py:238
  5.3 0.8 copy-start.4
  7.3 36.5 %collective-permute-start.5 = (bf16[14336,512]{1,0:T(8,128)(2,1)}, bf16[14336,512]{1,0:T(8,128)(2,1)}, u32[]{:S(2)}, u32[]{:S(2)}) collective-permute-start(bf16[14336,512]{1,0:T(8,128)(2,1)} %refs_2_.2), channel_id=1, source_target_pairs={{0,2},{2,0},{8,10},{10,8},{16,18},{18,16},{24,26},{26,24},{28,30},... | collective-permute-start | bytes 44040200 | tf_op jit(solution)/shard_map/ppermute | solution.py:238
  7.4 29.0 %collective-permute-start.10 = (bf16[16,32,512]{2,1,0:T(8,128)(2,1)}, bf16[16,32,512]{2,1,0:T(8,128)(2,1)}, u32[]{:S(2)}, u32[]{:S(2)}) collective-permute-start(bf16[16,32,512]{2,1,0:T(8,128)(2,1)} %param.12), channel_id=1, source_target_pairs={{0,1},{1,0},{2,3},{3,2},{4,5},{5,4},{6,7},{7,6},{8,9},{9,8},{10,11... | collective-permute-start | bytes 1572872 | tf_op jit(solution)/shard_map/ppermute | solution.py:300
  10.4 22.2 %collective-permute-start.1 = (bf16[64,7168]{1,0:T(8,128)(2,1)S(1)}, bf16[64,7168]{1,0:T(8,128)(2,1)}, u32[]{:S(2)}, u32[]{:S(2)}) collective-permute-start(bf16[64,7168]{1,0:T(8,128)(2,1)S(1)} %pad_maximum_fusion.refs_0_), channel_id=1, source_target_pairs={{0,8},{2,10},{8,16},{10,18},{16,24},{18,26},{24,28},{26,30},{28,20... | collective-permute-start | bytes 2752520 | tf_op jit(solution)/shard_map/ppermute | solution.py:238
  12.0 22.2 %collective-permute-start.3 = (bf16[64,7168]{1,0:T(8,128)(2,1)S(1)}, bf16[64,7168]{1,0:T(8,128)(2,1)}, u32[]{:S(2)}, u32[]{:S(2)}) collective-permute-start(bf16[64,7168]{1,0:T(8,128)(2,1)S(1)} %pad_maximum_fusion.refs_0_), channel_id=1, source_target_pairs={{0,4},{2,6},{8,0},{10,2},{16,8},{18,10},{24,16},{26,18},{28,24},{3... | collective-permute-start | bytes 2752520 | tf_op jit(solution)/shard_map/ppermute | solution.py:238
  12.5 31.3 %collective-permute-start.6 = (bf16[64,14336]{1,0:T(8,128)(2,1)S(1)}, bf16[64,14336]{1,0:T(8,128)(2,1)}, u32[]{:S(2)}, u32[]{:S(2)}) collective-permute-start(bf16[64,14336]{1,0:T(8,128)(2,1)S(1)} %bitcast.66), channel_id=1, source_target_pairs={{0,2},{2,0},{8,10},{10,8},{16,18},{18,16},{24,26},{26,24},{28,30},... | collective-permute-start | bytes 5505032 | tf_op jit(solution)/shard_map/ppermute | solution.py:238
  32.6 21.8 %collective-permute-start.2 = (bf16[64,7168]{1,0:T(8,128)(2,1)}, bf16[64,7168]{1,0:T(8,128)(2,1)}, u32[]{:S(2)}, u32[]{:S(2)}) collective-permute-start(bf16[64,7168]{1,0:T(8,128)(2,1)} %collective-permute-done.1.refs_1_), channel_id=1, source_target_pairs={{0,8},{2,10},{8,16},{10,18},{16,24},{18,26},{24,28},{26,30},{28,20... | collective-permute-start | bytes 2752520 | tf_op jit(solution)/shard_map/ppermute | solution.py:238
  34.2 21.6 %collective-permute-start.4 = (bf16[64,7168]{1,0:T(8,128)(2,1)}, bf16[64,7168]{1,0:T(8,128)(2,1)}, u32[]{:S(2)}, u32[]{:S(2)}) collective-permute-start(bf16[64,7168]{1,0:T(8,128)(2,1)} %collective-permute-done.3.refs_2_), channel_id=1, source_target_pairs={{0,4},{2,6},{8,0},{10,2},{16,8},{18,10},{24,16},{26,18},{28,24},{3... | collective-permute-start | bytes 2752520 | tf_op jit(solution)/shard_map/ppermute | solution.py:238
  36.4 41.9 %collective-permute-start.9 = (bf16[8,7168]{1,0:T(8,128)(2,1)}, bf16[8,7168]{1,0:T(8,128)(2,1)S(1)}, u32[]{:S(2)}, u32[]{:S(2)}) collective-permute-start(bf16[8,7168]{1,0:T(8,128)(2,1)} %convolution_convert_fusion), channel_id=1, source_target_pairs={{0,28},{2,30},{8,20},{10,22},{16,12},{18,14},{24,4},{26,6},{28,0},... | collective-permute-start | bytes 344072 | tf_op jit(solution)/shard_map/ppermute | solution.py:238
  55.8 21.8 %collective-permute-start.7 = (bf16[64,7168]{1,0:T(8,128)(2,1)}, bf16[64,7168]{1,0:T(8,128)(2,1)S(1)}, u32[]{:S(2)}, u32[]{:S(2)}) collective-permute-start(bf16[64,7168]{1,0:T(8,128)(2,1)} %collective-permute-done.2.refs_0_), channel_id=1, source_target_pairs={{0,8},{2,10},{8,16},{10,18},{16,24},{18,26},{24,28},{26,30},{28,20... | collective-permute-start | bytes 2752520 | tf_op jit(solution)/shard_map/ppermute | solution.py:238
  61.0 17.3 %collective-permute-start.8 = (bf16[64,7168]{1,0:T(8,128)(2,1)}, bf16[64,7168]{1,0:T(8,128)(2,1)}, u32[]{:S(2)}, u32[]{:S(2)}) collective-permute-start(bf16[64,7168]{1,0:T(8,128)(2,1)} %collective-permute-done.4.refs_1_), channel_id=1, source_target_pairs={{0,4},{2,6},{8,0},{10,2},{16,8},{18,10},{24,16},{26,18},{28,24},{3... | collective-permute-start | bytes 2752520 | tf_op jit(solution)/shard_map/ppermute | solution.py:238
  61.1 17.2 %collective-permute-start.11 = (f32[3,2,32,512]{3,2,1,0:T(8,128)}, f32[3,2,32,512]{3,2,1,0:T(8,128)}, u32[]{:S(2)}, u32[]{:S(2)}) collective-permute-start(f32[3,2,32,512]{3,2,1,0:T(8,128)} %get-tuple-element.80), channel_id=1, source_target_pairs={{0,2},{2,0},{8,10},{10,8},{16,18},{18,16},{24,26},{26,24},{28,30},... | collective-permute-start | bytes 1179656 | tf_op jit(solution)/shard_map/ppermute | solution.py:238
  83.8 13.3 %collective-permute-start.13 = (bf16[32,7168]{1,0:T(8,128)(2,1)S(1)}, bf16[32,7168]{1,0:T(8,128)(2,1)S(1)}, u32[]{:S(2)}, u32[]{:S(2)}) collective-permute-start(bf16[32,7168]{1,0:T(8,128)(2,1)S(1)} %slice.141), channel_id=1, source_target_pairs={{0,8},{2,10},{8,16},{10,18},{16,24},{18,26},{24,28},{26,30},{28,20... | collective-permute-start | bytes 1376264 | tf_op jit(solution)/shard_map/ppermute | solution.py:238
  88.2 8.9 %collective-permute-start.14 = (bf16[32,7168]{1,0:T(8,128)(2,1)S(1)}, bf16[32,7168]{1,0:T(8,128)(2,1)S(1)}, u32[]{:S(2)}, u32[]{:S(2)}) collective-permute-start(bf16[32,7168]{1,0:T(8,128)(2,1)S(1)} %slice.142), channel_id=1, source_target_pairs={{0,4},{2,6},{8,0},{10,2},{16,8},{18,10},{24,16},{26,18},{28,24},{3... | collective-permute-start | bytes 1376264 | tf_op jit(solution)/shard_map/ppermute | solution.py:238
  89.0 8.1 %collective-permute-start.12 = (f32[2,16,64]{2,1,0:T(8,128)S(1)}, f32[2,16,64]{2,1,0:T(8,128)S(1)}, u32[]{:S(2)}, u32[]{:S(2)}) collective-permute-start(f32[2,16,64]{2,1,0:T(8,128)S(1)} %broadcast_select_fusion.4), channel_id=1, source_target_pairs={{0,1},{1,0},{2,3},{3,2},{4,5},{5,4},{6,7},{7,6},{8,9},{9,8},{10,11... | collective-permute-start | bytes 24584 | tf_op jit(solution)/shard_map/ppermute | solution.py:389
  89.6 7.5 %collective-permute-start.15 = (f32[2,2,32,512]{3,2,1,0:T(8,128)S(1)}, f32[2,2,32,512]{3,2,1,0:T(8,128)S(1)}, u32[]{:S(2)}, u32[]{:S(2)}) collective-permute-start(f32[2,2,32,512]{3,2,1,0:T(8,128)S(1)} %get-tuple-element.94), channel_id=1, source_target_pairs={{0,2},{2,0},{8,10},{10,8},{16,18},{18,16},{24,26},{26,24},{28,30},... | collective-permute-start | bytes 786440 | tf_op jit(solution)/shard_map/ppermute | solution.py:238
  97.1 9.4 %collective-permute-start.16 = (f32[2,16,64]{2,1,0:T(8,128)S(1)}, f32[2,16,64]{2,1,0:T(8,128)S(1)}, u32[]{:S(2)}, u32[]{:S(2)}) collective-permute-start(f32[2,16,64]{2,1,0:T(8,128)S(1)} %select_add_fusion), channel_id=1, source_target_pairs={{0,2},{2,0},{8,10},{10,8},{16,18},{18,16},{24,26},{26,24},{28,30},... | collective-permute-start | bytes 24584 | tf_op jit(solution)/shard_map/ppermute | solution.py:238
  100.3 12.1 %collective-permute-start.19 = (f32[2,2,32,512]{3,2,1,0:T(8,128)S(1)}, f32[2,2,32,512]{3,2,1,0:T(8,128)S(1)}, u32[]{:S(2)}, u32[]{:S(2)}) collective-permute-start(f32[2,2,32,512]{3,2,1,0:T(8,128)S(1)} %get-tuple-element.103), channel_id=1, source_target_pairs={{0,2},{2,0},{8,10},{10,8},{16,18},{18,16},{24,26},{26,24},{28,30},... | collective-permute-start | bytes 786440 | tf_op jit(solution)/shard_map/ppermute | solution.py:238
  106.0 11.8 %copy-start.2 = (bf16[256,16,64]{0,2,1:T(8,128)(2,1)S(1)}, bf16[256,16,64]{0,2,1:T(8,128)(2,1)}, u32[]{:S(2)}) copy-start(bf16[256,16,64]{0,2,1:T(8,128)(2,1)} %broadcast_in_dim.257) | copy-start | bytes 1572868
  106.0 13.2 %collective-permute-start.22 = (f32[1,2,32,512]{3,2,1,0:T(8,128)S(1)}, f32[1,2,32,512]{3,2,1,0:T(8,128)S(1)}, u32[]{:S(2)}, u32[]{:S(2)}) collective-permute-start(f32[1,2,32,512]{3,2,1,0:T(8,128)S(1)} %get-tuple-element.101), channel_id=1, source_target_pairs={{0,2},{2,0},{8,10},{10,8},{16,18},{18,16},{24,26},{26,24},{28,30},... | collective-permute-start | bytes 393224 | tf_op jit(solution)/shard_map/ppermute | solution.py:238
  106.5 3.7 %collective-permute-start.17 = (bf16[2,16,64]{2,1,0:T(8,128)(2,1)S(1)}, bf16[2,16,64]{2,1,0:T(8,128)(2,1)S(1)}, u32[]{:S(2)}, u32[]{:S(2)}) collective-permute-start(bf16[2,16,64]{2,1,0:T(8,128)(2,1)S(1)} %add_convert_fusion), channel_id=1, source_target_pairs={{0,4},{2,6},{4,0},{6,2},{8,12},{10,14},{12,8},{14,10},{16,20},{18,... | collective-permute-start | bytes 12296 | tf_op jit(solution)/shard_map/ppermute | solution.py:398
  110.3 8.5 %collective-permute-start.18 = (bf16[4,16,64]{2,1,0:T(8,128)(2,1)S(1)}, bf16[4,16,64]{2,1,0:T(8,128)(2,1)S(1)}, u32[]{:S(2)}, u32[]{:S(2)}) collective-permute-start(bf16[4,16,64]{2,1,0:T(8,128)(2,1)S(1)} %pad_maximum_fusion.6), channel_id=1, source_target_pairs={{0,8},{2,10},{4,12},{6,14},{8,0},{10,2},{12,4},{14,6},{16,24},{18,... | collective-permute-start | bytes 24584 | tf_op jit(solution)/shard_map/ppermute | solution.py:398
  113.5 5.7 %collective-permute-start.20 = (bf16[3,64,512]{2,1,0:T(8,128)(2,1)S(1)}, bf16[3,64,512]{2,1,0:T(8,128)(2,1)S(1)}, u32[]{:S(2)}, u32[]{:S(2)}) collective-permute-start(bf16[3,64,512]{2,1,0:T(8,128)(2,1)S(1)} %pad_maximum_fusion.2), channel_id=1, source_target_pairs={{0,1},{1,0},{2,3},{3,2},{4,5},{5,4},{6,7},{7,6},{8,9},{9,8},{10,11... | collective-permute-start | bytes 589832 | tf_op jit(solution)/shard_map/ppermute | solution.py:366
  120.8 8.0 %collective-permute-start.23 = (bf16[1,64,512]{2,1,0:T(8,128)(2,1)}, bf16[1,64,512]{2,1,0:T(8,128)(2,1)}, u32[]{:S(2)}, u32[]{:S(2)}) collective-permute-start(bf16[1,64,512]{2,1,0:T(8,128)(2,1)} %bitcast.34), channel_id=1, source_target_pairs={{0,1},{1,0},{2,3},{3,2},{4,5},{5,4},{6,7},{7,6},{8,9},{9,8},{10,11... | collective-permute-start | bytes 196616 | tf_op jit(solution)/shard_map/ppermute | solution.py:366
  122.3 4.8 %collective-permute-start.21 = (bf16[8,16,64]{2,1,0:T(8,128)(2,1)S(1)}, bf16[8,16,64]{2,1,0:T(8,128)(2,1)S(1)}, u32[]{:S(2)}, u32[]{:S(2)}) collective-permute-start(bf16[8,16,64]{2,1,0:T(8,128)(2,1)S(1)} %pad_maximum_fusion.4), channel_id=1, source_target_pairs={{0,16},{2,18},{4,20},{6,22},{8,24},{10,26},{12,28},{14,30},{16,0},... | collective-permute-start | bytes 49160 | tf_op jit(solution)/shard_map/ppermute | solution.py:398
  122.4 6.5 %copy-start.3 = (f32[1,2,32,512]{3,2,1,0:T(8,128)S(1)}, f32[1,2,32,512]{3,2,1,0:T(8,128)}, u32[]{:S(2)}) copy-start(f32[1,2,32,512]{3,2,1,0:T(8,128)} %get-tuple-element.122) | copy-start | bytes 393220
  122.4 7.4 %copy-start.1 = (bf16[16,64,512]{2,1,0:T(8,128)(2,1)S(1)}, bf16[16,64,512]{2,1,0:T(8,128)(2,1)}, u32[]{:S(2)}) copy-start(bf16[16,64,512]{2,1,0:T(8,128)(2,1)} %maximum_select_fusion) | copy-start | bytes 3145732

commit v5 on v4

--- a/solution.py
+++ b/solution.py
@@ -212,11 +212,10 @@
 
     table = []
     for w in range(owners):
-        p, lane = order.index(w // 2), w % 2
+        p = order.index(w // 2)
         at = lambda shift: order[(p + shift) % nodes]
-        arrivals = [at(0)] + [at(s * k) for k in range(1, far) for s in (-1, 1)]
+        arrivals = [at(0)] + [at(s * k) for k in range(1, far) for s in (-1, 1)] + [at(far)]
         row = [2 * node + side for node in arrivals for side in (0, 1)]
-        row += [2 * at(far) + (lane ^ side) for side in (0, 1)]
         for half in (0, 1):
             here = [(at(s) < own_nodes) == (half == 0) for s in range(far)]
             row += [int(h) for h in here]
@@ -240,177 +239,144 @@
     def half_of(value, which, axis):
         return lax.dynamic_slice_in_dim(value, which * depth, depth, axis)
 
+    keep = hidden_of(half_of(gate_activation, side, 1), half_of(up_activation, side, 1))
+    give = hidden_of(half_of(gate_activation, 1 - side, 1), half_of(up_activation, 1 - side, 1))
+    right = [send(keep, 1), send(give, 1, 1)]
+    left = [send(keep, -1), send(give, -1, 1)]
+
+    first, twin = lax.optimization_barrier((first_factor_table[0], send(give, 0, 1)))
+    factors = (first, send(first, 0, 1))
+    weight, factors, twin, right, left = lax.optimization_barrier(
+        (down_base_weight, factors, twin, right, left)
+    )
+    weights = (weight, send(weight, 0, 1))
+    home_late, row_adapter_index, second_factor_table, weights = lax.optimization_barrier(
+        (home, row_adapter_index, second_factor_table, weights)
+    )
+
+    pieces = [keep, twin] + right + left
+    for step in range(2, steps + 1):
+        right = [send(block, 1) for block in right]
+        left = [send(block, -1) for block in left]
+        if step < steps:
+            right, left = lax.optimization_barrier((right, left))
+            pieces += right + left
+
     facts = lax.dynamic_index_in_dim(
-        jnp.asarray(np.array(table, np.int32)), home, 0, keepdims=False
-    )
-    edges = np.cumsum([0, 2 * (nodes - 1), 2, far, far, far, far])
-    arrived, far_wide, *rest = [facts[a:b] for a, b in zip(edges[:-1], edges[1:])]
-    flags = jnp.where(part == 0, rest[0], rest[2])
+        jnp.asarray(np.array(table, np.int32)), home_late, 0, keepdims=False
+    )
+    edges = np.cumsum([0, 2 * nodes, far, far, far, far])
+    arrived, *rest = [facts[a:b] for a, b in zip(edges[:-1], edges[1:])]
+    flags = jnp.where(part == 0, rest[0], rest[2])[:, None, None] == 1
     target = jnp.where(part == 0, rest[1], rest[3])
+    places = target[:, None] == jnp.arange(own_nodes, dtype=jnp.int32)[None, :]
     slot_all = slots_of(row_adapter_index, adapter_storage_slot).reshape(owners, row_count)
     ranks = jnp.arange(row_count, dtype=jnp.int32)
     earlier = (slot_all[:, :, None] == slot_all[:, None, :]) & (ranks[None, :] < ranks[:, None])
     position = jnp.sum(earlier.astype(jnp.int32), axis=2)
     items = jnp.arange(MOST, dtype=jnp.int32)
-
-    sides = jnp.arange(2, dtype=jnp.int32)
-    own_wide = jnp.bitwise_xor(home, sides)
     blocks = jnp.arange(owners, dtype=jnp.int32)
-    own_is = own_wide[:, None, None] == blocks[None, :, None]
-    own_slot = jnp.sum(jnp.where(own_is, slot_all[None], 0), axis=1)
-    own_position = jnp.sum(jnp.where(own_is, position[None], 0), axis=1)
-    pick = (own_slot[None, :, None, :] == far_wide[:, None, None, None]) & (
-        own_position[None, :, None, :] == items[None, None, :, None]
-    )
-    pick = jnp.where(
-        (sides[:, None] == sides[None, :])[None, :, None, :, None], pick[:, :, :, None, :], False
-    ).reshape(4 * MOST, group_rows).astype(bf16)
-
-    keep = hidden_of(half_of(gate_activation, side, 1), half_of(up_activation, side, 1))
-    give = hidden_of(half_of(gate_activation, 1 - side, 1), half_of(up_activation, 1 - side, 1))
-    twin, slot_all, position, pick = lax.optimization_barrier(
-        (send(give, 0, 1), slot_all, position, pick)
-    )
-    block = jnp.concatenate([keep, twin], axis=0)
-    right, left = send(block, 1), send(block, -1)
-
-    weight, first, block = lax.optimization_barrier(
-        (down_base_weight, first_factor_table[0], block)
-    )
-    weights = (weight, send(weight, 0, 1))
-    factors = (first, send(first, 0, 1))
-    slot_all, position, weights = lax.optimization_barrier((slot_all, position, weights))
-
-    picked = jnp.dot(pick, block, preferred_element_type=f32).astype(bf16)
-    far_rows = send(picked, far)
-
-    slot_here = lax.dynamic_slice_in_dim(slot_all, part * own_blocks, own_blocks)
-    position_here = lax.dynamic_slice_in_dim(position, part * own_blocks, own_blocks)
-    came = jnp.bitwise_xor(home, blocks)
-    spots = (
-        (slot_here[:, :, None, None, None] == came[:, None, None])
-        & (position_here[:, :, None, None, None] == items)
-        & (jnp.arange(own_blocks)[:, None] == jnp.arange(own_blocks)[None, :])[:, None, None, :, None]
-    )
-    spots = spots.astype(bf16).reshape(own_blocks * row_count, owners * own_blocks * MOST)
-    mask = jnp.repeat(
-        (slot_here.reshape(-1)[:, None] == blocks[None, :]).astype(bf16), rank, axis=1
-    )
-
-    other = lax.ppermute(second_factor_table, INNER, SWAP)
-    second = jnp.where(
-        part == 0,
-        jnp.concatenate([second_factor_table, other], axis=1),
-        jnp.concatenate([other, second_factor_table], axis=1),
-    ).reshape(owners * rank, width)
 
     def chosen(slot):
-        near = (
+        picks = (
             (arrived[None, None, :, None] == blocks[:, None, None, None])
             & (slot_all == slot)[:, None, None, :]
             & (position[:, None, None, :] == items[None, :, None, None])
-        ).reshape(owners * MOST, -1)
-        there = (
-            (far_wide[None, None, :, None] == blocks[:, None, None, None])
-            & (items[:, None] == items[None, :])[None, :, None, :]
-        ).reshape(owners * MOST, -1)
-        return jnp.concatenate([near, there], axis=1).astype(f32)
-
-    chosen_mine, chosen_sib = chosen(home), chosen(jnp.bitwise_xor(home, 1))
-
-    results, sibs, lows = [], [], []
-
-    def add(result):
-        results.append(result)
-        sibs.append(send(result[1], 0, 1))
-
-    ready = (second, spots, mask, chosen_mine, chosen_sib)
-    pieces = [block]
-    for step in range(1, steps + 1):
-        if step > 1:
-            right, left, result = lax.optimization_barrier((right, left, result))
-            add(result[:2])
-            lows.append(result[2])
-        pieces += [right, left]
-        if step < steps:
-            right, left = send(right, 1), send(left, -1)
-            result = rows_product(lane, row_count, pieces, weights, factors)
-        else:
-            right, left, far_rows, ready, sibs[0] = lax.optimization_barrier(
-                (right, left, far_rows, ready, sibs[0])
-            )
-            last = [send(right[:row_count], 1), send(left[row_count:], -1)]
-            second, spots, mask, chosen_mine, chosen_sib = ready
-            low, far_low = rows_product(lane, row_count, pieces, (), factors, (far_rows,))
-            lows.append(low)
-            result = rows_product(lane, row_count, pieces, weights)
-        pieces = []
-    result, last, sibs = lax.optimization_barrier((result, last, sibs))
-    add(result)
-
-    def node(values, shift):
-        if shift == 0:
-            return values[0][0]
-        if shift == far:
-            return values[-1][0]
-        step = min(shift, nodes - shift)
-        return values[step - 1][(1 if step == 1 else 0) + (0 if shift > far else 1)]
+        )
+        return picks.reshape(owners * MOST, -1).astype(f32)
+
+    chosen_mine, chosen_sib = chosen(home_late), chosen(jnp.bitwise_xor(home_late, 1))
+
+    half = own_blocks * MOST
+    here = own_blocks * row_count
+    slot_here = lax.dynamic_slice_in_dim(slot_all, part * own_blocks, own_blocks).reshape(here, 1)
+    position_here = lax.dynamic_slice_in_dim(position, part * own_blocks, own_blocks)
+    block_here = jnp.arange(here, dtype=jnp.int32)[:, None] // row_count
+    spot = (
+        jnp.bitwise_xor(slot_here, home_late) * half + block_here * MOST + position_here.reshape(here, 1)
+    )
+    spots = (spot == jnp.arange(owners * half, dtype=jnp.int32)[None, :]).astype(bf16)
+    column = jnp.arange(owners * rank, dtype=jnp.int32)[None, :]
+    piece = rank // 2
+    own_rank = jnp.bitwise_xor(part, column // (owners * piece)) * piece + column % piece
+    mask = (slot_here == column // piece % owners).astype(bf16)
+    copies = (jnp.arange(rank, dtype=jnp.int32)[:, None] == own_rank).astype(bf16)
+    ready = (spots, mask, copies, chosen_mine, chosen_sib, flags, places)
+
+    other = lax.ppermute(second_factor_table, INNER, SWAP)
+    second = jnp.concatenate(
+        [table.reshape(owners * piece, width) for table in (second_factor_table, other)], axis=0
+    )
+
+    results = [rows_product(lane, row_count, pieces, weights, factors)]
+    sibs = []
+    right, left, results, ready = lax.optimization_barrier((right, left, results, ready))
+    spots, mask, copies, chosen_mine, chosen_sib, flags, places = ready
+    last = [send(right[0], 1), send(left[1], -1)]
+    sibs.append(send(results[0][1], 0, 1))
+    results.append(rows_product(lane, row_count, right + left, weights, factors))
+    results, sibs, last, second = lax.optimization_barrier((results, sibs, last, second))
+    sibs.append(send(results[1][1], 0, 1))
+
+    low_last = rows_product(lane, row_count, last, (), factors)[0]
+    lows = [values[2] for values in results] + [low_last]
+    low = jnp.concatenate([values.reshape(-1, 2 * rank) for values in lows], axis=0)
+    low = jnp.stack(
+        [
+            jnp.dot(chosen_mine, low[:, :rank], precision=lax.Precision.HIGHEST),
+            jnp.dot(chosen_sib, low[:, rank:], precision=lax.Precision.HIGHEST),
+        ]
+    )
+    kept = jnp.where(part == 0, low[:, :half], low[:, half:])
+    sent = jnp.where(part == 0, low[:, half:], low[:, :half])
+    crossed = [(2 * w + m, 2 * (w ^ 1) + (1 - m)) for w in range(owners) for m in (0, 1)]
+    low_mp = lax.ppermute(sent, INNER, SWAP)
+    low_sib = send(kept, 0, 1)
+    low_both = lax.ppermute(sent, ("wide",) + INNER, crossed)
+
+    low_mp, low_sib, low_both, last = lax.optimization_barrier((low_mp, low_sib, low_both, last))
+    results.append(rows_product(lane, row_count, last, weights))
+    sibs.append(send(results[2][1], 0, 1))
+
+    low = (kept + low_mp + (low_sib + low_both)[::-1]).astype(bf16)
+
+    def from_node(value, gap):
+        return lax.ppermute(value, "wide", [(w, w ^ (2 * gap)) for w in range(owners)])
+
+    gap = 1
+    while gap < nodes:
+        reach = min(4, nodes // gap)
+        low = jnp.concatenate([low] + [from_node(low, gap * k) for k in range(1, reach)], axis=0)
+        gap *= reach
+
+    order_of = [0] + [s * k for k in range(1, far) for s in (-1, 1)] + [far]
+    of_result = [nodes - 3, 2, 1]
 
     def total(shift):
-        both = node([r[0] for r in results], shift) + node(sibs, shift)
-        return both.reshape(1, group_rows, width)
+        index = [s % nodes for s in order_of].index(shift)
+        for values, sib, size in zip(results, sibs, of_result):
+            if index < size:
+                return (values[0][index] + sib[index]).reshape(1, group_rows, width)
+            index -= size
 
     def over_mp(shifts):
-        pairs = [(flags[s : s + 1, None, None] == 1, total(s), total(s + far)) for s in shifts]
+        pairs = [(flags[s : s + 1], total(s), total(s + far)) for s in shifts]
         sent = jnp.concatenate([jnp.where(f, b, a).astype(bf16) for f, a, b in pairs], axis=0)
         got = lax.ppermute(sent, INNER, SWAP)
         return [jnp.where(f, a, b) for f, a, b in pairs], got
 
-
-    low = jnp.concatenate([values.reshape(-1, 2 * rank) for values in lows], axis=0)
-    count = 2 * MOST
-
-    def compact(choice, values, far_values):
-        return jnp.dot(
-            choice,
-            jnp.concatenate([values, far_values], axis=0),
-            precision=lax.Precision.HIGHEST,
-        )
-
-    low = jnp.stack(
-        [
-            compact(chosen_mine, low[:, :rank], far_low[:count, :rank]),
-            compact(chosen_sib, low[:, rank:], far_low[count:, rank:]),
-        ]
-    )
-    half = own_blocks * MOST
-    kept = jnp.where(part == 0, low[:, :half], low[:, half:])
-    sent = jnp.where(part == 0, low[:, half:], low[:, :half])
-    low = kept + lax.ppermute(sent, INNER, SWAP)
-    low, last = lax.optimization_barrier((low, last))
-    low = (low + send(low, 0, 1)[::-1]).astype(bf16)
-    kept, got = over_mp(list(range(1, far)))
-    add(rows_product(lane, row_count, last, weights))
-    gap = 2
-    while gap < owners:
-        if gap * 2 == owners:
-            low, results[-1], got = lax.optimization_barrier((low, results[-1], got))
-        other = lax.ppermute(low, "wide", [(w, w ^ gap) for w in range(owners)])
-        low = jnp.concatenate([low, other], axis=0)
-        gap *= 2
+    kept_more, got_more = over_mp(list(range(1, far)))
+    low, got_more, results[2] = lax.optimization_barrier((low, got_more, results[2]))
+    kept_one, got_one = over_mp([0])
+
     own_low = jnp.dot(spots, low.reshape(owners * half, rank), preferred_element_type=f32)
-    copies = jnp.tile(jnp.eye(rank, dtype=bf16), (1, owners))
     spread = jnp.dot(own_low.astype(bf16), copies, preferred_element_type=f32).astype(bf16) * mask
-    delta = jnp.dot(spread, second, preferred_element_type=f32)
-    delta = delta.reshape(own_nodes, group_rows, width)
-
-    places = jnp.arange(own_nodes, dtype=jnp.int32)[:, None, None]
-    out = delta
-    for pair, value in enumerate(kept, 1):
-        value = value + got[pair - 1 : pair].astype(f32)
-        out = out + jnp.where(places == target[pair : pair + 1, None, None], value, 0)
-    kept, got = over_mp([0])
-    out = out + jnp.where(places == target[:1, None, None], kept[0] + got.astype(f32), 0)
+    out = jnp.dot(spread, second, preferred_element_type=f32).reshape(own_nodes, group_rows, width)
+    for pair, value in enumerate(kept_more, 1):
+        value = value + got_more[pair - 1 : pair].astype(f32)
+        out = out + jnp.where(places[pair][:, None, None], value, 0)
+    value = kept_one[0] + got_one.astype(f32)
+    out = out + jnp.where(places[0][:, None, None], value, 0)
     return out.astype(bf16).reshape(-1, width)
 
 

time: 132 us -> 133 us (level)
  waiting for transfers between devices: 33.9 us -> 52.4 us
  Pallas kernels: 35.6 us -> 27.9 us
  other arithmetic: 16 us -> 12.5 us
  between operations: 3.11 us -> 0.46 us
  starting transfers between devices: 28.2 us -> 26.5 us
    ppermute x17 -> x21, waiting for transfers between devices: 25.7 us -> 44.5 us  [send(): return lax.ppermute(value, 'wide', moved(shift, cross))]
    pallas_call x5 -> x4, Pallas kernels: 35.6 us -> 27.9 us  [rows_product(): pl.pallas_call(functools.partial(rows_kernel, count, len(more), int(bool(...]
    ppermute x4 -> x6, waiting for transfers between devices: 7.84 us -> 2.51 us  [the longest x4 2.09 us: from_node(): lax.ppermute(value, 'wide', [(w, w ^ 2 * gap) for w in range(owners)])]
    ppermute x2, waiting for transfers between devices: 0.37 us -> 5.38 us  [over_mp(): got = lax.ppermute(sent, INNER, SWAP)]
    unnamed x14 -> x43, local copies, waits for them, and re-layouts: 0.82 us -> 4.61 us
    eq x11 -> x2, other arithmetic: 2.75 us -> 0.15 us  [the longest x1 0.07 us: ringed(): flags = jnp.where(part == 0, rest[0], rest[2])[:, None, None] == 1]
    ppermute x17 -> x21, starting transfers between devices: 19.3 us -> 16.9 us  [send(): return lax.ppermute(value, 'wide', moved(shift, cross))]
    ppermute x4 -> x6, starting transfers between devices: 2.95 us -> 5.26 us  [the longest x4 3.95 us: from_node(): lax.ppermute(value, 'wide', [(w, w ^ 2 * gap) for w in range(owners)])]
  transfers between devices with their start and end apart: 24 -> 30, of which waited for: 8 -> 11; matrix products, arithmetic and copies ran while one was open for 16% -> 10% of each run, Pallas kernels for 24% -> 20%
where the time goes in v5:
time: 133 us
  waiting for transfers between devices  52.4 us (39%)
  Pallas kernels  27.9 us (21%)
  starting transfers between devices  26.5 us (20%)
  other arithmetic  12.5 us (9%)
  local copies, waits for them, and re-layouts  9.03 us (7%)
  matrix products  3.74 us (3%)
    ppermute x21, waiting for transfers between devices, send(): return lax.ppermute(value, 'wide', moved(shift, cross))  44.5 us
    pallas_call x4, Pallas kernels, rows_product(): pl.pallas_call(functools.partial(rows_kernel, count, len(more), int(bool(...  27.9 us
    ppermute x21, starting transfers between devices, send(): return lax.ppermute(value, 'wide', moved(shift, cross))  16.9 us
    ppermute x2, waiting for transfers between devices, over_mp(): got = lax.ppermute(sent, INNER, SWAP)  5.38 us
    unnamed x43, local copies, waits for them, and re-layouts  4.61 us
    ppermute x4, starting transfers between devices, from_node(): lax.ppermute(value, 'wide', [(w, w ^ 2 * gap) for w in range(owners)])  3.95 us
    convert_element_type x2, other arithmetic, over_mp(): jnp.where(f, b, a).astype(bf16)  2.9 us
    ppermute x2, starting transfers between devices, over_mp(): got = lax.ppermute(sent, INNER, SWAP)  2.74 us
  transfers between devices with their start and end apart: 30, of which 11 were waited for; matrix products, arithmetic and copies ran while one was open for 10% of the time, Pallas kernels for 20%

profile of v5, /device:TPU:0, one launch (start us, length us, event | category | flops | bytes accessed | tf_op | source)
XLA Modules:
  0.0 132.6 jit_solution(6856329161439662277)
XLA Ops:
  0.0 2.1 %fusion.13 = (bf16[32,7168]{1,0:T(8,128)(2,1)S(1)}, bf16[32,7168]{1,0:T(8,128)(2,1)S(1)}) fusion(bf16[32,14336]{1,0:T(8,128)(2,1)} %param.9, s32[]{:T(128)S(6)} %select_n.231, bf16[32,14336]{1,0:T(8,128)(2,1)} %param.8, s32[]{:T(128)S(6)} %select_n.230), kind=kLoop, calls=%fused_computation.24 | loop fusion | flops 3670016 | bytes 2752520 | tf_op jit(solution)/shard_map/convert_element_type | solution.py:135
  2.6 1.4 %collective-permute-done.refs_1_ = bf16[32,7168]{1,0:T(8,128)(2,1)S(1)} collective-permute-done((bf16[32,7168]{1,0:T(8,128)(2,1)S(1)}, bf16[32,7168]{1,0:T(8,128)(2,1)S(1)}, u32[]{:S(2)}, u32[]{:S(2)}) %collective-permute-start) | collective-permute-done | bytes 458784 | tf_op jit(solution)/shard_map/ppermute | solution.py:237
  4.5 2.7 %collective-permute-start.2 = (bf16[32,7168]{1,0:T(8,128)(2,1)S(1)}, bf16[32,7168]{1,0:T(8,128)(2,1)S(1)}, u32[]{:S(2)}, u32[]{:S(2)}) collective-permute-start(bf16[32,7168]{1,0:T(8,128)(2,1)S(1)} %get-tuple-element.127.refs_0_), channel_id=1, source_target_pairs={{0,8},{2,10},{8,16},{10,18},{16,24},{18,26},{24,28},{26,30},{28,20... | collective-permute-start | bytes 1376264 | tf_op jit(solution)/shard_map/ppermute | solution.py:237
  7.2 1.3 collective-permute-start.3
  9.0 9.5 %collective-permute-done.2.refs_2_ = bf16[32,7168]{1,0:T(8,128)(2,1)S(1)} collective-permute-done((bf16[32,7168]{1,0:T(8,128)(2,1)S(1)}, bf16[32,7168]{1,0:T(8,128)(2,1)S(1)}, u32[]{:S(2)}, u32[]{:S(2)}) %collective-permute-start.2) | collective-permute-done | bytes 458784 | tf_op jit(solution)/shard_map/ppermute | solution.py:237
  18.5 9.3 %collective-permute-done.3.refs_3_ = bf16[32,7168]{1,0:T(8,128)(2,1)} collective-permute-done((bf16[32,7168]{1,0:T(8,128)(2,1)S(1)}, bf16[32,7168]{1,0:T(8,128)(2,1)}, u32[]{:S(2)}, u32[]{:S(2)}) %collective-permute-start.3) | collective-permute-done | bytes 458784 | tf_op jit(solution)/shard_map/ppermute | solution.py:237
  27.8 3.0 %collective-permute-done.5.refs_5_ = bf16[32,7168]{1,0:T(8,128)(2,1)} collective-permute-done((bf16[32,7168]{1,0:T(8,128)(2,1)S(1)}, bf16[32,7168]{1,0:T(8,128)(2,1)}, u32[]{:S(2)}, u32[]{:S(2)}) %collective-permute-start.5) | collective-permute-done | bytes 458784 | tf_op jit(solution)/shard_map/ppermute | solution.py:237
  30.8 1.2 copy-done.1
  32.3 1.6 %collective-permute-start.6 = (bf16[32,7168]{1,0:T(8,128)(2,1)S(1)}, bf16[32,7168]{1,0:T(8,128)(2,1)}, u32[]{:S(2)}, u32[]{:S(2)}) collective-permute-start(bf16[32,7168]{1,0:T(8,128)(2,1)S(1)} %collective-permute-done.2.refs_2_), channel_id=1, source_target_pairs={{0,8},{2,10},{8,16},{10,18},{16,24},{18,26},{24,28},{26,30},{28,20... | collective-permute-start | bytes 1376264 | tf_op jit(solution)/shard_map/ppermute | solution.py:237
  33.9 0.8 copy-done.4
  34.7 1.5 %collective-permute-start.7 = (bf16[32,7168]{1,0:T(8,128)(2,1)}, bf16[32,7168]{1,0:T(8,128)(2,1)}, u32[]{:S(2)}, u32[]{:S(2)}) collective-permute-start(bf16[32,7168]{1,0:T(8,128)(2,1)} %collective-permute-done.3.refs_3_), channel_id=1, source_target_pairs={{0,8},{2,10},{8,16},{10,18},{16,24},{18,26},{24,28},{26,30},{28,20... | collective-permute-start | bytes 1376264 | tf_op jit(solution)/shard_map/ppermute | solution.py:237
  37.2 8.6 %collective-permute-done.6.refs_6_ = bf16[32,7168]{1,0:T(8,128)(2,1)} collective-permute-done((bf16[32,7168]{1,0:T(8,128)(2,1)S(1)}, bf16[32,7168]{1,0:T(8,128)(2,1)}, u32[]{:S(2)}, u32[]{:S(2)}) %collective-permute-start.6) | collective-permute-done | bytes 458784 | tf_op jit(solution)/shard_map/ppermute | solution.py:237
  45.8 9.1 %collective-permute-done.7.refs_7_ = bf16[32,7168]{1,0:T(8,128)(2,1)} collective-permute-done((bf16[32,7168]{1,0:T(8,128)(2,1)}, bf16[32,7168]{1,0:T(8,128)(2,1)}, u32[]{:S(2)}, u32[]{:S(2)}) %collective-permute-start.7) | collective-permute-done | bytes 458784 | tf_op jit(solution)/shard_map/ppermute | solution.py:237
  54.9 3.5 %collective-permute-done.9.refs_9_ = bf16[32,7168]{1,0:T(8,128)(2,1)} collective-permute-done((bf16[32,7168]{1,0:T(8,128)(2,1)}, bf16[32,7168]{1,0:T(8,128)(2,1)}, u32[]{:S(2)}, u32[]{:S(2)}) %collective-permute-start.9) | collective-permute-done | bytes 458784 | tf_op jit(solution)/shard_map/ppermute | solution.py:237
  59.3 1.6 %collective-permute-start.12 = (bf16[32,7168]{1,0:T(8,128)(2,1)}, bf16[32,7168]{1,0:T(8,128)(2,1)}, u32[]{:S(2)}, u32[]{:S(2)}) collective-permute-start(bf16[32,7168]{1,0:T(8,128)(2,1)} %collective-permute-done.8.refs_8_), channel_id=1, source_target_pairs={{0,4},{2,6},{8,0},{10,2},{16,8},{18,10},{24,16},{26,18},{28,24},{3... | collective-permute-start | bytes 1376264 | tf_op jit(solution)/shard_map/ppermute | solution.py:237
  60.9 1.6 %collective-permute-start.13 = (bf16[32,7168]{1,0:T(8,128)(2,1)}, bf16[32,7168]{1,0:T(8,128)(2,1)}, u32[]{:S(2)}, u32[]{:S(2)}) collective-permute-start(bf16[32,7168]{1,0:T(8,128)(2,1)} %collective-permute-done.9.refs_9_), channel_id=1, source_target_pairs={{0,4},{2,6},{8,0},{10,2},{16,8},{18,10},{24,16},{26,18},{28,24},{3... | collective-permute-start | bytes 1376264 | tf_op jit(solution)/shard_map/ppermute | solution.py:237
  62.5 0.7 constant_dynamic-slice_fusion.2
  64.2 1.6 %collective-permute-start.18 = (bf16[16,32,512]{2,1,0:T(8,128)(2,1)}, bf16[16,32,512]{2,1,0:T(8,128)(2,1)}, u32[]{:S(2)}, u32[]{:S(2)}) collective-permute-start(bf16[16,32,512]{2,1,0:T(8,128)(2,1)} %param.12), channel_id=1, source_target_pairs={{0,1},{1,0},{2,3},{3,2},{4,5},{5,4},{6,7},{7,6},{8,9},{9,8},{10,11... | collective-permute-start | bytes 1572872 | tf_op jit(solution)/shard_map/ppermute | solution.py:306
  65.7 0.9 compare_convert_fusion
  66.9 0.8 fusion.17
  67.7 0.8 reshape.675
  68.5 0.8 reshape.676
  69.2 1.5 %copy-done.2 = bf16[64,14336]{1,0:T(8,128)(2,1)S(1)} copy-done((bf16[64,14336]{1,0:T(8,128)(2,1)S(1)}, bf16[64,14336]{1,0:T(8,128)(2,1)}, u32[]{:S(2)}) %copy-start.2) | copy-done | bytes 1835032
  70.7 1.0 copy-done.5
  71.7 11.7 %shard_map.82 = (f32[5,2,32,512]{3,2,1,0:T(8,128)S(1)}, f32[5,2,32,512]{3,2,1,0:T(8,128)S(1)}, f32[5,2,32,128]{3,2,1,0:T(8,128)S(1)}) custom-call(s32[1]{0:T(128)} %bitcast.1.lane_ref, bf16[32,7168]{1,0:T(8,128)(2,1)S(1)} %get-tuple-element.127.refs_0_, bf16[32,7168]{1,0:T(8,128)(2,1)S(1)} %collective-permute-done.refs_1_, bf16[32,7168]{1,0:T(8,128)(2,1)S(1)} %copy-done.5, ...), custom_call_target="tpu_custom_call" | custom-call | flops 41287680 | bytes 258048 | tf_op jit(solution)/shard_map/pallas_call | solution.py:115
  84.1 1.6 %collective-permute-start.17 = (bf16[32,7168]{1,0:T(8,128)(2,1)}, bf16[32,7168]{1,0:T(8,128)(2,1)S(1)}, u32[]{:S(2)}, u32[]{:S(2)}) collective-permute-start(bf16[32,7168]{1,0:T(8,128)(2,1)} %collective-permute-done.13.refs_3_), channel_id=1, source_target_pairs={{0,4},{2,6},{8,0},{10,2},{16,8},{18,10},{24,16},{26,18},{28,24},{3... | collective-permute-start | bytes 1376264 | tf_op jit(solution)/shard_map/ppermute | solution.py:237
  85.7 8.8 %shard_map.83 = (f32[2,2,32,512]{3,2,1,0:T(8,128)S(1)}, f32[2,2,32,512]{3,2,1,0:T(8,128)S(1)}, f32[2,2,32,128]{3,2,1,0:T(8,128)S(1)}) custom-call(s32[1]{0:T(128)} %bitcast.1.lane_ref, bf16[32,7168]{1,0:T(8,128)(2,1)} %collective-permute-done.10.refs_0_, bf16[32,7168]{1,0:T(8,128)(2,1)} %collective-permute-done.11.refs_1_, ...), custom_call_target="tpu_custom_call" | custom-call | flops 16515072 | bytes 258048 | tf_op jit(solution)/shard_map/pallas_call | solution.py:115
  94.5 0.7 slice_bitcast_fusion.3
  95.1 2.1 %pad_maximum_fusion = bf16[1024,512]{1,0:T(8,128)(2,1)} fusion(bf16[512,512]{1,0:T(8,128)(2,1)} %bitcast.7, bf16[512,512]{1,0:T(8,128)(2,1)S(1)} %bitcast.77), kind=kLoop, calls=%fused_computation.14 | loop fusion | flops 2097152 | bytes 2097152 | tf_op jit(solution)/shard_map/concatenate | solution.py:307
  97.3 1.7 %shard_map.84 = f32[1,2,32,128]{3,2,1,0:T(8,128)S(1)} custom-call(s32[1]{0:T(128)} %bitcast.1.lane_ref, bf16[32,7168]{1,0:T(8,128)(2,1)S(1)} %collective-permute-done.16.refs_0_, bf16[32,7168]{1,0:T(8,128)(2,1)S(1)} %collective-permute-done.17.refs_1_, bf16[64,14336]{1,0:T(8,128)(2,1)S(1)} %bitcast.69, bf16[64,14336]{1,0:T(8,128)(2,1)S(1)} %copy-done.3), custom_call_target="tpu_custom_call" | custom-call | flops 917504 | bytes 28672 | tf_op jit(solution)/shard_map/pallas_call | solution.py:115
  99.7 0.6 collective-permute-start.19
  100.3 0.7 collective-permute-start.21
  101.0 0.9 collective-permute-start.20
  101.9 0.7 fusion.37
  103.7 1.2 collective-permute-start.22
  105.4 1.8 %collective-permute-start.24 = (bf16[2,16,64]{2,1,0:T(8,128)(2,1)S(1)}, bf16[2,16,64]{2,1,0:T(8,128)(2,1)S(1)}, u32[]{:S(2)}, u32[]{:S(2)}) collective-permute-start(bf16[2,16,64]{2,1,0:T(8,128)(2,1)S(1)} %get-tuple-element.122), channel_id=1, source_target_pairs={{0,12},{2,14},{4,8},{6,10},{8,4},{10,6},{12,0},{14,2},{16,28},{18,... | collective-permute-start | bytes 12296 | tf_op jit(solution)/shard_map/ppermute | solution.py:344
  107.3 1.6 %select_convert_fusion.2 = bf16[1,2,32,512]{3,2,1,0:T(8,128)(2,1)S(1)} fusion(pred[]{:T(512)} %bitcast.15, f32[5,2,32,512]{3,2,1,0:T(8,128)} %copy-done.11, f32[5,2,32,512]{3,2,1,0:T(8,128)S(1)} %get-tuple-element.108), kind=kLoop, calls=%fused_computation.51 | loop fusion | flops 131072 | bytes 589825 | tf_op jit(solution)/shard_map/convert_element_type | solution.py:364
  108.9 5.7 %shard_map.85 = (f32[1,2,32,512]{3,2,1,0:T(8,128)S(1)}, f32[1,2,32,512]{3,2,1,0:T(8,128)S(1)}) custom-call(s32[1]{0:T(128)} %bitcast.1.lane_ref, bf16[32,7168]{1,0:T(8,128)(2,1)S(1)} %collective-permute-done.16.refs_0_, bf16[32,7168]{1,0:T(8,128)(2,1)S(1)} %collective-permute-done.17.refs_1_, bf16[14336,512]{1,0:T(8,128)(2,1)} %refs_2_, ...), custom_call_target="tpu_custom_call" | custom-call | flops 7340032 | bytes 229376 | tf_op jit(solution)/shard_map/pallas_call | solution.py:115
  115.2 1.4 %broadcast_select_fusion.3 = (f32[1,2,32,512]{3,2,1,0:T(8,128)S(1)}, f32[1,2,32,512]{3,2,1,0:T(8,128)S(1)}, bf16[1,2,32,512]{3,2,1,0:T(8,128)(2,1)S(1)}, bf16[1,2,32,512]{3,2,1,0:T(8,128)(2,1)S(1)}) fusion(pred[]{:T(512)} %bitcast.13, f32[5,2,32,512]{3,2,1,0:T(8,128)S(1)} %copy-done.12, f32[5,2,32,512]{3,2,1,0:T(8,128)S(1)} %get-tuple-element.108, ...), kind=kLoop, calls=%fused_computation.59 | loop fusion | flops 327680 | bytes 1441794 | tf_op jit(solution)/shard_map/jit(_where)/select_n | solution.py:366
  116.6 1.4 %collective-permute-start.27 = (bf16[3,64,512]{2,1,0:T(8,128)(2,1)S(1)}, bf16[3,64,512]{2,1,0:T(8,128)(2,1)S(1)}, u32[]{:S(2)}, u32[]{:S(2)}) collective-permute-start(bf16[3,64,512]{2,1,0:T(8,128)(2,1)S(1)} %pad_maximum_fusion.2), channel_id=1, source_target_pairs={{0,1},{1,0},{2,3},{3,2},{4,5},{5,4},{6,7},{7,6},{8,9},{9,8},{10,11... | collective-permute-start | bytes 589832 | tf_op jit(solution)/shard_map/ppermute | solution.py:365
  118.0 2.1 %collective-permute-done.25 = bf16[8,16,64]{2,1,0:T(8,128)(2,1)S(1)} collective-permute-done((bf16[8,16,64]{2,1,0:T(8,128)(2,1)S(1)}, bf16[8,16,64]{2,1,0:T(8,128)(2,1)S(1)}, u32[]{:S(2)}, u32[]{:S(2)}) %collective-permute-start.25) | collective-permute-done | bytes 16416 | tf_op jit(solution)/shard_map/ppermute | solution.py:344
  120.1 3.6 %collective-permute-done.27 = bf16[3,64,512]{2,1,0:T(8,128)(2,1)S(1)} collective-permute-done((bf16[3,64,512]{2,1,0:T(8,128)(2,1)S(1)}, bf16[3,64,512]{2,1,0:T(8,128)(2,1)S(1)}, u32[]{:S(2)}, u32[]{:S(2)}) %collective-permute-start.27) | collective-permute-done | bytes 196640 | tf_op jit(solution)/shard_map/ppermute | solution.py:365
  123.7 1.3 select_convert_fusion
  124.9 1.4 %collective-permute-start.29 = (bf16[1,64,512]{2,1,0:T(8,128)(2,1)S(1)}, bf16[1,64,512]{2,1,0:T(8,128)(2,1)S(1)}, u32[]{:S(2)}, u32[]{:S(2)}) collective-permute-start(bf16[1,64,512]{2,1,0:T(8,128)(2,1)S(1)} %bitcast.82), channel_id=1, source_target_pairs={{0,1},{1,0},{2,3},{3,2},{4,5},{5,4},{6,7},{7,6},{8,9},{9,8},{10,11... | collective-permute-start | bytes 196616 | tf_op jit(solution)/shard_map/ppermute | solution.py:365
  126.4 0.8 convolution_convert_fusion.1
  127.5 1.8 %collective-permute-done.29 = bf16[1,64,512]{2,1,0:T(8,128)(2,1)S(1)} collective-permute-done((bf16[1,64,512]{2,1,0:T(8,128)(2,1)S(1)}, bf16[1,64,512]{2,1,0:T(8,128)(2,1)S(1)}, u32[]{:S(2)}, u32[]{:S(2)}) %collective-permute-start.29) | collective-permute-done | bytes 65568 | tf_op jit(solution)/shard_map/ppermute | solution.py:365
  129.3 0.9 bitcast_select_fusion
  130.2 2.4 %fusion.4 = bf16[256,512]{1,0:T(8,128)(2,1)} fusion(f32[256,512]{1,0:T(8,128)} %bitcast_select_fusion, f32[256,512]{1,0:T(8,128)S(1)} %bitcast_select_fusion.1, f32[256,512]{1,0:T(8,128)S(1)} %bitcast_select_fusion.2, f32[256,512]{1,0:T(8,128)S(1)} %bitcast_select_fusion.3, bf16[1024,512]{1,0:T(8,128)(2,1)S(1)} %copy-done.9, ...), kind=kOutput, calls=%fused_computation.6 | convolution fusion | flops 303169536 | bytes 4096000 | tf_op jit(solution)/shard_map/dot_general | solution.py:374
  (116 shorter events, 8.6 us)
Async XLA Ops:
  0.0 4.1 %copy-start = (bf16[1,64,14336]{2,1,0:T(8,128)(2,1)S(1)}, bf16[1,64,14336]{2,1,0:T(8,128)(2,1)}, u32[]{:S(2)}) copy-start(bf16[1,64,14336]{2,1,0:T(8,128)(2,1)} %param.11) | copy-start | bytes 5505028
  0.0 63.3 %copy-start.17 = (s32[512,1]{0,1:T(1,128)S(1)}, s32[512,1]{0,1:T(1,128)}, u32[]{:S(2)}) copy-start(s32[512,1]{0,1:T(1,128)} %param.13) | copy-start | bytes 6148
  0.0 63.3 %copy-start.18 = (s32[16]{0:T(128)S(1)}, s32[16]{0:T(128)}, u32[]{:S(2)}) copy-start(s32[16]{0:T(128)} %param.14) | copy-start | bytes 196
  2.1 2.0 %collective-permute-start = (bf16[32,7168]{1,0:T(8,128)(2,1)S(1)}, bf16[32,7168]{1,0:T(8,128)(2,1)S(1)}, u32[]{:S(2)}, u32[]{:S(2)}) collective-permute-start(bf16[32,7168]{1,0:T(8,128)(2,1)S(1)} %get-tuple-element.128), channel_id=1, source_target_pairs={{0,2},{2,0},{8,10},{10,8},{16,18},{18,16},{24,26},{26,24},{28,30},... | collective-permute-start | bytes 1376264 | tf_op jit(solution)/shard_map/ppermute | solution.py:237
  4.1 26.7 %collective-permute-start.1 = (bf16[64,14336]{1,0:T(8,128)(2,1)S(1)}, bf16[64,14336]{1,0:T(8,128)(2,1)S(1)}, u32[]{:S(2)}, u32[]{:S(2)}) collective-permute-start(bf16[64,14336]{1,0:T(8,128)(2,1)S(1)} %bitcast.66), channel_id=1, source_target_pairs={{0,2},{2,0},{8,10},{10,8},{16,18},{18,16},{24,26},{26,24},{28,30},... | collective-permute-start | bytes 5505032 | tf_op jit(solution)/shard_map/ppermute | solution.py:237
  4.5 14.0 %collective-permute-start.2 = (bf16[32,7168]{1,0:T(8,128)(2,1)S(1)}, bf16[32,7168]{1,0:T(8,128)(2,1)S(1)}, u32[]{:S(2)}, u32[]{:S(2)}) collective-permute-start(bf16[32,7168]{1,0:T(8,128)(2,1)S(1)} %get-tuple-element.127.refs_0_), channel_id=1, source_target_pairs={{0,8},{2,10},{8,16},{10,18},{16,24},{18,26},{24,28},{26,30},{28,20... | collective-permute-start | bytes 1376264 | tf_op jit(solution)/shard_map/ppermute | solution.py:237
  7.2 20.6 %collective-permute-start.3 = (bf16[32,7168]{1,0:T(8,128)(2,1)S(1)}, bf16[32,7168]{1,0:T(8,128)(2,1)}, u32[]{:S(2)}, u32[]{:S(2)}) collective-permute-start(bf16[32,7168]{1,0:T(8,128)(2,1)S(1)} %get-tuple-element.128), channel_id=1, source_target_pairs={{0,10},{2,8},{8,18},{10,16},{16,26},{18,24},{24,30},{26,28},{28,22... | collective-permute-start | bytes 1376264 | tf_op jit(solution)/shard_map/ppermute | solution.py:237
  8.4 19.3 %collective-permute-start.4 = (bf16[32,7168]{1,0:T(8,128)(2,1)S(1)}, bf16[32,7168]{1,0:T(8,128)(2,1)}, u32[]{:S(2)}, u32[]{:S(2)}) collective-permute-start(bf16[32,7168]{1,0:T(8,128)(2,1)S(1)} %get-tuple-element.127.refs_0_), channel_id=1, source_target_pairs={{0,4},{2,6},{8,0},{10,2},{16,8},{18,10},{24,16},{26,18},{28,24},{3... | collective-permute-start | bytes 1376264 | tf_op jit(solution)/shard_map/ppermute | solution.py:237
  8.9 21.9 %collective-permute-start.5 = (bf16[32,7168]{1,0:T(8,128)(2,1)S(1)}, bf16[32,7168]{1,0:T(8,128)(2,1)}, u32[]{:S(2)}, u32[]{:S(2)}) collective-permute-start(bf16[32,7168]{1,0:T(8,128)(2,1)S(1)} %get-tuple-element.128), channel_id=1, source_target_pairs={{0,6},{2,4},{8,2},{10,0},{16,10},{18,8},{24,18},{26,16},{28,26},{3... | collective-permute-start | bytes 1376264 | tf_op jit(solution)/shard_map/ppermute | solution.py:237
  30.8 1.2 copy-start.1
  32.0 30.5 %collective-permute-start.14 = (bf16[14336,512]{1,0:T(8,128)(2,1)}, bf16[14336,512]{1,0:T(8,128)(2,1)}, u32[]{:S(2)}, u32[]{:S(2)}) collective-permute-start(bf16[14336,512]{1,0:T(8,128)(2,1)} %refs_2_), channel_id=1, source_target_pairs={{0,2},{2,0},{8,10},{10,8},{16,18},{18,16},{24,26},{26,24},{28,30},... | collective-permute-start | bytes 44040200 | tf_op jit(solution)/shard_map/ppermute | solution.py:237
  32.3 13.5 %collective-permute-start.6 = (bf16[32,7168]{1,0:T(8,128)(2,1)S(1)}, bf16[32,7168]{1,0:T(8,128)(2,1)}, u32[]{:S(2)}, u32[]{:S(2)}) collective-permute-start(bf16[32,7168]{1,0:T(8,128)(2,1)S(1)} %collective-permute-done.2.refs_2_), channel_id=1, source_target_pairs={{0,8},{2,10},{8,16},{10,18},{16,24},{18,26},{24,28},{26,30},{28,20... | collective-permute-start | bytes 1376264 | tf_op jit(solution)/shard_map/ppermute | solution.py:237
  34.7 20.2 %collective-permute-start.7 = (bf16[32,7168]{1,0:T(8,128)(2,1)}, bf16[32,7168]{1,0:T(8,128)(2,1)}, u32[]{:S(2)}, u32[]{:S(2)}) collective-permute-start(bf16[32,7168]{1,0:T(8,128)(2,1)} %collective-permute-done.3.refs_3_), channel_id=1, source_target_pairs={{0,8},{2,10},{8,16},{10,18},{16,24},{18,26},{24,28},{26,30},{28,20... | collective-permute-start | bytes 1376264 | tf_op jit(solution)/shard_map/ppermute | solution.py:237
  36.2 18.7 %collective-permute-start.8 = (bf16[32,7168]{1,0:T(8,128)(2,1)}, bf16[32,7168]{1,0:T(8,128)(2,1)}, u32[]{:S(2)}, u32[]{:S(2)}) collective-permute-start(bf16[32,7168]{1,0:T(8,128)(2,1)} %collective-permute-done.4.refs_4_), channel_id=1, source_target_pairs={{0,4},{2,6},{8,0},{10,2},{16,8},{18,10},{24,16},{26,18},{28,24},{3... | collective-permute-start | bytes 1376264 | tf_op jit(solution)/shard_map/ppermute | solution.py:237
  36.7 21.7 %collective-permute-start.9 = (bf16[32,7168]{1,0:T(8,128)(2,1)}, bf16[32,7168]{1,0:T(8,128)(2,1)}, u32[]{:S(2)}, u32[]{:S(2)}) collective-permute-start(bf16[32,7168]{1,0:T(8,128)(2,1)} %collective-permute-done.5.refs_5_), channel_id=1, source_target_pairs={{0,4},{2,6},{8,0},{10,2},{16,8},{18,10},{24,16},{26,18},{28,24},{3... | collective-permute-start | bytes 1376264 | tf_op jit(solution)/shard_map/ppermute | solution.py:237
  58.4 25.1 %collective-permute-start.10 = (bf16[32,7168]{1,0:T(8,128)(2,1)}, bf16[32,7168]{1,0:T(8,128)(2,1)}, u32[]{:S(2)}, u32[]{:S(2)}) collective-permute-start(bf16[32,7168]{1,0:T(8,128)(2,1)} %collective-permute-done.6.refs_6_), channel_id=1, source_target_pairs={{0,8},{2,10},{8,16},{10,18},{16,24},{18,26},{24,28},{26,30},{28,20... | collective-permute-start | bytes 1376264 | tf_op jit(solution)/shard_map/ppermute | solution.py:237
  58.9 24.6 %collective-permute-start.11 = (bf16[32,7168]{1,0:T(8,128)(2,1)}, bf16[32,7168]{1,0:T(8,128)(2,1)}, u32[]{:S(2)}, u32[]{:S(2)}) collective-permute-start(bf16[32,7168]{1,0:T(8,128)(2,1)} %collective-permute-done.7.refs_7_), channel_id=1, source_target_pairs={{0,8},{2,10},{8,16},{10,18},{16,24},{18,26},{24,28},{26,30},{28,20... | collective-permute-start | bytes 1376264 | tf_op jit(solution)/shard_map/ppermute | solution.py:237
  59.3 24.2 %collective-permute-start.12 = (bf16[32,7168]{1,0:T(8,128)(2,1)}, bf16[32,7168]{1,0:T(8,128)(2,1)}, u32[]{:S(2)}, u32[]{:S(2)}) collective-permute-start(bf16[32,7168]{1,0:T(8,128)(2,1)} %collective-permute-done.8.refs_8_), channel_id=1, source_target_pairs={{0,4},{2,6},{8,0},{10,2},{16,8},{18,10},{24,16},{26,18},{28,24},{3... | collective-permute-start | bytes 1376264 | tf_op jit(solution)/shard_map/ppermute | solution.py:237
  60.9 22.6 %collective-permute-start.13 = (bf16[32,7168]{1,0:T(8,128)(2,1)}, bf16[32,7168]{1,0:T(8,128)(2,1)}, u32[]{:S(2)}, u32[]{:S(2)}) collective-permute-start(bf16[32,7168]{1,0:T(8,128)(2,1)} %collective-permute-done.9.refs_9_), channel_id=1, source_target_pairs={{0,4},{2,6},{8,0},{10,2},{16,8},{18,10},{24,16},{26,18},{28,24},{3... | collective-permute-start | bytes 1376264 | tf_op jit(solution)/shard_map/ppermute | solution.py:237
  64.2 30.9 %collective-permute-start.18 = (bf16[16,32,512]{2,1,0:T(8,128)(2,1)}, bf16[16,32,512]{2,1,0:T(8,128)(2,1)}, u32[]{:S(2)}, u32[]{:S(2)}) collective-permute-start(bf16[16,32,512]{2,1,0:T(8,128)(2,1)} %param.12), channel_id=1, source_target_pairs={{0,1},{1,0},{2,3},{3,2},{4,5},{5,4},{6,7},{7,6},{8,9},{9,8},{10,11... | collective-permute-start | bytes 1572872 | tf_op jit(solution)/shard_map/ppermute | solution.py:306
  69.2 1.5 %copy-start.2 = (bf16[64,14336]{1,0:T(8,128)(2,1)S(1)}, bf16[64,14336]{1,0:T(8,128)(2,1)}, u32[]{:S(2)}) copy-start(bf16[64,14336]{1,0:T(8,128)(2,1)} %copy-done.1) | copy-start | bytes 5505028
  71.7 14.0 %copy-start.3 = (bf16[64,14336]{1,0:T(8,128)(2,1)S(1)}, bf16[64,14336]{1,0:T(8,128)(2,1)}, u32[]{:S(2)}) copy-start(bf16[64,14336]{1,0:T(8,128)(2,1)} %copy-done.1) | copy-start | bytes 5505028
  83.5 11.6 %copy-start.14 = (bf16[16,32,512]{2,1,0:T(8,128)(2,1)S(1)}, bf16[16,32,512]{2,1,0:T(8,128)(2,1)}, u32[]{:S(2)}) copy-start(bf16[16,32,512]{2,1,0:T(8,128)(2,1)} %param.12) | copy-start | bytes 1572868
  83.5 13.7 %collective-permute-start.15 = (f32[5,2,32,512]{3,2,1,0:T(8,128)S(1)}, f32[5,2,32,512]{3,2,1,0:T(8,128)S(1)}, u32[]{:S(2)}, u32[]{:S(2)}) collective-permute-start(f32[5,2,32,512]{3,2,1,0:T(8,128)S(1)} %get-tuple-element.87), channel_id=1, source_target_pairs={{0,2},{2,0},{8,10},{10,8},{16,18},{18,16},{24,26},{26,24},{28,30},... | collective-permute-start | bytes 1966088 | tf_op jit(solution)/shard_map/ppermute | solution.py:237
  83.6 13.6 %collective-permute-start.16 = (bf16[32,7168]{1,0:T(8,128)(2,1)}, bf16[32,7168]{1,0:T(8,128)(2,1)S(1)}, u32[]{:S(2)}, u32[]{:S(2)}) collective-permute-start(bf16[32,7168]{1,0:T(8,128)(2,1)} %collective-permute-done.10.refs_0_), channel_id=1, source_target_pairs={{0,8},{2,10},{8,16},{10,18},{16,24},{18,26},{24,28},{26,30},{28,20... | collective-permute-start | bytes 1376264 | tf_op jit(solution)/shard_map/ppermute | solution.py:237
  84.1 13.1 %collective-permute-start.17 = (bf16[32,7168]{1,0:T(8,128)(2,1)}, bf16[32,7168]{1,0:T(8,128)(2,1)S(1)}, u32[]{:S(2)}, u32[]{:S(2)}) collective-permute-start(bf16[32,7168]{1,0:T(8,128)(2,1)} %collective-permute-done.13.refs_3_), channel_id=1, source_target_pairs={{0,4},{2,6},{8,0},{10,2},{16,8},{18,10},{24,16},{26,18},{28,24},{3... | collective-permute-start | bytes 1376264 | tf_op jit(solution)/shard_map/ppermute | solution.py:237
  94.5 4.6 %copy-start.6 = (f32[2,2,32,512]{3,2,1,0:T(8,128)}, f32[2,2,32,512]{3,2,1,0:T(8,128)S(1)}, u32[]{:S(2)}) copy-start(f32[2,2,32,512]{3,2,1,0:T(8,128)S(1)} %get-tuple-element.106) | copy-start | bytes 786436
  94.5 4.6 %copy-start.8 = (f32[2,2,32,512]{3,2,1,0:T(8,128)}, f32[2,2,32,512]{3,2,1,0:T(8,128)S(1)}, u32[]{:S(2)}) copy-start(f32[2,2,32,512]{3,2,1,0:T(8,128)S(1)} %get-tuple-element.107) | copy-start | bytes 786436
  97.3 1.8 %copy-start.11 = (f32[5,2,32,512]{3,2,1,0:T(8,128)}, f32[5,2,32,512]{3,2,1,0:T(8,128)S(1)}, u32[]{:S(2)}) copy-start(f32[5,2,32,512]{3,2,1,0:T(8,128)S(1)} %collective-permute-done.15) | copy-start | bytes 1966084
  97.3 1.8 %copy-start.16 = (f32[32,512]{1,0:T(8,128)S(1)}, f32[32,512]{1,0:T(8,128)}, u32[]{:S(2)}) copy-start(f32[32,512]{1,0:T(8,128)} %reshape.676) | copy-start | bytes 196612
  97.3 2.2 %copy-start.15 = (f32[32,512]{1,0:T(8,128)S(1)}, f32[32,512]{1,0:T(8,128)}, u32[]{:S(2)}) copy-start(f32[32,512]{1,0:T(8,128)} %reshape.675) | copy-start | bytes 196612
  97.3 5.5 %copy-start.19 = (pred[4]{0:T(512)(128)(4,1)S(1)}, pred[4]{0:T(512)(128)(4,1)}, u32[]{:S(2)}) copy-start(pred[4]{0:T(512)(128)(4,1)} %get-tuple-element.145) | copy-start | bytes 16
  99.7 3.9 %collective-permute-start.19 = (f32[2,16,64]{2,1,0:T(8,128)S(1)}, f32[2,16,64]{2,1,0:T(8,128)S(1)}, u32[]{:S(2)}, u32[]{:S(2)}) collective-permute-start(f32[2,16,64]{2,1,0:T(8,128)S(1)} %get-tuple-element.136), channel_id=1, source_target_pairs={{0,1},{1,0},{2,3},{3,2},{4,5},{5,4},{6,7},{7,6},{8,9},{9,8},{10,11... | collective-permute-start | bytes 24584 | tf_op jit(solution)/shard_map/ppermute | solution.py:333
  100.3 3.3 %collective-permute-start.21 = (f32[2,16,64]{2,1,0:T(8,128)S(1)}, f32[2,16,64]{2,1,0:T(8,128)S(1)}, u32[]{:S(2)}, u32[]{:S(2)}) collective-permute-start(f32[2,16,64]{2,1,0:T(8,128)S(1)} %get-tuple-element.136), channel_id=1, source_target_pairs={{0,3},{1,2},{2,1},{3,0},{4,7},{5,6},{6,5},{7,4},{8,11},{9,10},{10,... | collective-permute-start | bytes 24584 | tf_op jit(solution)/shard_map/ppermute | solution.py:335
  101.0 2.6 %collective-permute-start.20 = (f32[2,16,64]{2,1,0:T(8,128)S(1)}, f32[2,16,64]{2,1,0:T(8,128)S(1)}, u32[]{:S(2)}, u32[]{:S(2)}) collective-permute-start(f32[2,16,64]{2,1,0:T(8,128)S(1)} %get-tuple-element.135), channel_id=1, source_target_pairs={{0,2},{2,0},{8,10},{10,8},{16,18},{18,16},{24,26},{26,24},{28,30},... | collective-permute-start | bytes 24584 | tf_op jit(solution)/shard_map/ppermute | solution.py:237
  103.2 11.9 %collective-permute-start.26 = (f32[2,2,32,512]{3,2,1,0:T(8,128)}, f32[2,2,32,512]{3,2,1,0:T(8,128)S(1)}, u32[]{:S(2)}, u32[]{:S(2)}) collective-permute-start(f32[2,2,32,512]{3,2,1,0:T(8,128)} %copy-done.8), channel_id=1, source_target_pairs={{0,2},{2,0},{8,10},{10,8},{16,18},{18,16},{24,26},{26,24},{28,30},... | collective-permute-start | bytes 786440 | tf_op jit(solution)/shard_map/ppermute | solution.py:237
  103.7 11.0 %collective-permute-start.22 = (bf16[2,16,64]{2,1,0:T(8,128)(2,1)S(1)}, bf16[2,16,64]{2,1,0:T(8,128)(2,1)S(1)}, u32[]{:S(2)}, u32[]{:S(2)}) collective-permute-start(bf16[2,16,64]{2,1,0:T(8,128)(2,1)S(1)} %get-tuple-element.122), channel_id=1, source_target_pairs={{0,4},{2,6},{4,0},{6,2},{8,12},{10,14},{12,8},{14,10},{16,20},{18,... | collective-permute-start | bytes 12296 | tf_op jit(solution)/shard_map/ppermute | solution.py:344
  104.9 9.8 %collective-permute-start.23 = (bf16[2,16,64]{2,1,0:T(8,128)(2,1)S(1)}, bf16[2,16,64]{2,1,0:T(8,128)(2,1)S(1)}, u32[]{:S(2)}, u32[]{:S(2)}) collective-permute-start(bf16[2,16,64]{2,1,0:T(8,128)(2,1)S(1)} %get-tuple-element.122), channel_id=1, source_target_pairs={{0,8},{2,10},{4,12},{6,14},{8,0},{10,2},{12,4},{14,6},{16,24},{18,... | collective-permute-start | bytes 12296 | tf_op jit(solution)/shard_map/ppermute | solution.py:344
  105.4 9.3 %collective-permute-start.24 = (bf16[2,16,64]{2,1,0:T(8,128)(2,1)S(1)}, bf16[2,16,64]{2,1,0:T(8,128)(2,1)S(1)}, u32[]{:S(2)}, u32[]{:S(2)}) collective-permute-start(bf16[2,16,64]{2,1,0:T(8,128)(2,1)S(1)} %get-tuple-element.122), channel_id=1, source_target_pairs={{0,12},{2,14},{4,8},{6,10},{8,4},{10,6},{12,0},{14,2},{16,28},{18,... | collective-permute-start | bytes 12296 | tf_op jit(solution)/shard_map/ppermute | solution.py:344
  108.9 6.3 %copy-start.7 = (f32[2,2,32,512]{3,2,1,0:T(8,128)S(1)}, f32[2,2,32,512]{3,2,1,0:T(8,128)}, u32[]{:S(2)}) copy-start(f32[2,2,32,512]{3,2,1,0:T(8,128)} %copy-done.6) | copy-start | bytes 786436
  108.9 6.3 %copy-start.12 = (f32[5,2,32,512]{3,2,1,0:T(8,128)S(1)}, f32[5,2,32,512]{3,2,1,0:T(8,128)}, u32[]{:S(2)}) copy-start(f32[5,2,32,512]{3,2,1,0:T(8,128)} %copy-done.11) | copy-start | bytes 1966084
  114.6 9.1 %collective-permute-start.28 = (f32[1,2,32,512]{3,2,1,0:T(8,128)S(1)}, f32[1,2,32,512]{3,2,1,0:T(8,128)S(1)}, u32[]{:S(2)}, u32[]{:S(2)}) collective-permute-start(f32[1,2,32,512]{3,2,1,0:T(8,128)S(1)} %get-tuple-element.113), channel_id=1, source_target_pairs={{0,2},{2,0},{8,10},{10,8},{16,18},{18,16},{24,26},{26,24},{28,30},... | collective-permute-start | bytes 393224 | tf_op jit(solution)/shard_map/ppermute | solution.py:237
  114.7 5.3 %collective-permute-start.25 = (bf16[8,16,64]{2,1,0:T(8,128)(2,1)S(1)}, bf16[8,16,64]{2,1,0:T(8,128)(2,1)S(1)}, u32[]{:S(2)}, u32[]{:S(2)}) collective-permute-start(bf16[8,16,64]{2,1,0:T(8,128)(2,1)S(1)} %pad_maximum_fusion.3), channel_id=1, source_target_pairs={{0,16},{2,18},{4,20},{6,22},{8,24},{10,26},{12,28},{14,30},{16,0},... | collective-permute-start | bytes 49160 | tf_op jit(solution)/shard_map/ppermute | solution.py:344
  115.2 11.2 %copy-start.13 = (bf16[256,256]{1,0:T(8,128)(2,1)S(1)}, bf16[256,256]{1,0:T(8,128)(2,1)}, u32[]{:S(2)}) copy-start(bf16[256,256]{1,0:T(8,128)(2,1)} %fusion.17) | copy-start | bytes 393220
  116.6 7.1 %collective-permute-start.27 = (bf16[3,64,512]{2,1,0:T(8,128)(2,1)S(1)}, bf16[3,64,512]{2,1,0:T(8,128)(2,1)S(1)}, u32[]{:S(2)}, u32[]{:S(2)}) collective-permute-start(bf16[3,64,512]{2,1,0:T(8,128)(2,1)S(1)} %pad_maximum_fusion.2), channel_id=1, source_target_pairs={{0,1},{1,0},{2,3},{3,2},{4,5},{5,4},{6,7},{7,6},{8,9},{9,8},{10,11... | collective-permute-start | bytes 589832 | tf_op jit(solution)/shard_map/ppermute | solution.py:365
  124.9 4.3 %collective-permute-start.29 = (bf16[1,64,512]{2,1,0:T(8,128)(2,1)S(1)}, bf16[1,64,512]{2,1,0:T(8,128)(2,1)S(1)}, u32[]{:S(2)}, u32[]{:S(2)}) collective-permute-start(bf16[1,64,512]{2,1,0:T(8,128)(2,1)S(1)} %bitcast.82), channel_id=1, source_target_pairs={{0,1},{1,0},{2,3},{3,2},{4,5},{5,4},{6,7},{7,6},{8,9},{9,8},{10,11... | collective-permute-start | bytes 196616 | tf_op jit(solution)/shard_map/ppermute | solution.py:365
  126.3 3.9 %copy-start.9 = (bf16[1024,512]{1,0:T(8,128)(2,1)S(1)}, bf16[1024,512]{1,0:T(8,128)(2,1)}, u32[]{:S(2)}) copy-start(bf16[1024,512]{1,0:T(8,128)(2,1)} %pad_maximum_fusion) | copy-start | bytes 3145732
  126.3 3.9 %copy-start.10 = (bf16[256,1024]{1,0:T(8,128)(2,1)S(1)}, bf16[256,1024]{1,0:T(8,128)(2,1)}, u32[]{:S(2)}) copy-start(bf16[256,1024]{1,0:T(8,128)(2,1)} %compare_convert_fusion) | copy-start | bytes 1572868
  (2 other events, 1.8 us)

commit v6 on v5

v6 whole, which is shorter than its diff:
```python
import functools

import jax
import jax.numpy as jnp
import numpy as np
from jax import lax
from jax.experimental import pallas as pl
from jax.experimental.pallas import tpu as pltpu
from jax.sharding import PartitionSpec as P

MOST = 2
INNER = ("mp", "sub")
SWAP = [(0, 1), (1, 0)]


def accumulate(pieces, tables, sums=(), lows=()):
    depth, width = pieces[0].shape[1], tables[0].shape[1]
    rank = (tables[0].shape[0] - depth) * width // depth
    for total in (*sums, *lows):
        total[...] = jnp.zeros_like(total)
    for index in range(depth // width):
        here = slice(index * width, (index + 1) * width)
        rows = jnp.concatenate([piece[:, here] for piece in pieces], axis=0)
        for table, total in zip(tables, sums):
            total[...] += jnp.dot(rows, table[here, :], preferred_element_type=jnp.float32)
        for table, total in zip(tables, lows):
            block = table[depth + index * rank : depth + (index + 1) * rank, :]
            total[...] += lax.dot_general(
                rows, block, (((1,), (1,)), ((), ())), preferred_element_type=jnp.float32
            )


def in_lanes(lane, total, index, height):
    first = total[2 * index * height : (2 * index + 1) * height]
    other = total[(2 * index + 1) * height : (2 * index + 2) * height]
    whole = jnp.concatenate([first, other], axis=0)
    turned = jnp.concatenate([other, first], axis=0)
    return jnp.where(lane == 0, whole, turned)


def compacted(choice, low):
    return jnp.dot(choice, low, precision=lax.Precision.HIGHEST, preferred_element_type=jnp.float32)


def early_kernel(count, facts, *refs):
    pieces, tables, choices = refs[:count], refs[count : count + 2], refs[count + 2]
    base, base_sib, compact = refs[count + 3 : count + 6]
    sums, lows = refs[count + 6 : count + 8], refs[count + 8 :]
    accumulate(pieces, tables, sums, lows)
    height = pieces[0].shape[0]
    for which, (out, total) in enumerate(zip((base, base_sib), sums)):
        for index in range(count // 2):
            out[index] = in_lanes(facts[0], total, index, height)
        compact[which] = compacted(choices[which], lows[which][...])


def share(flag, near, away, outs, pair):
    (near_own, near_sib), (away_own, away_sib) = near, away
    kept, to_sib, to_mp, to_both = outs
    kept[pair] = jnp.where(flag == 1, near_own, away_own)
    to_sib[pair] = jnp.where(flag == 1, near_sib, away_sib)
    to_mp[pair] = jnp.where(flag == 1, away_own, near_own).astype(to_mp.dtype)
    to_both[pair] = jnp.where(flag == 1, away_sib, near_sib).astype(to_both.dtype)


def middle_kernel(count, facts, *refs):
    pieces, tables = refs[:count], refs[count : count + 2]
    choices, compact_in, base, base_sib = refs[count + 2 : count + 6]
    outs, compact = refs[count + 6 : count + 10], refs[count + 10]
    sums, lows = refs[count + 11 : count + 13], refs[count + 13 :]
    accumulate(pieces, tables, sums, lows)
    height = pieces[0].shape[0]
    fresh = [[in_lanes(facts[0], total, index, height) for total in sums] for index in (0, 1)]
    pairs = outs[0].shape[0]
    for pair in range(pairs):
        step = pair + 1
        near = fresh[1] if step == pairs else (base[2 * step], base_sib[2 * step])
        back = pairs + 1 - step
        away = fresh[0] if back == pairs else (base[2 * back - 1], base_sib[2 * back - 1])
        share(facts[2 + step], near, away, outs, pair)
    for which, total in enumerate(lows):
        compact[which] = compact_in[which] + compacted(choices[which], total[...])


def low_kernel(facts, piece, other, table, table_sib, choices, compact_in, kept, sent, *lows):
    accumulate((piece, other), (table, table_sib), (), lows)
    half = kept.shape[1]
    for which, total in enumerate(lows):
        compact = compact_in[which] + compacted(choices[which], total[...])
        kept[which] = jnp.where(facts[1] == 0, compact[:half], compact[half:])
        sent[which] = jnp.where(facts[1] == 0, compact[half:], compact[:half])


def last_kernel(facts, piece, other, table, table_sib, base, base_sib, *refs):
    outs, sums = refs[:4], refs[4:]
    accumulate((piece, other), (table, table_sib), sums)
    away = [in_lanes(facts[0], total, 0, piece.shape[0]) for total in sums]
    share(facts[2], (base[0], base_sib[0]), away, outs, 0)


def kernel_call(kernel, facts, arrays, shapes, scratch, flops):
    in_vmem = pl.BlockSpec(memory_space=pltpu.VMEM)
    return pl.pallas_call(
        kernel,
        in_specs=[pl.BlockSpec(memory_space=pltpu.SMEM)] + [in_vmem] * len(arrays),
        out_specs=[in_vmem] * len(shapes),
        out_shape=[jax.ShapeDtypeStruct(shape, kind) for shape, kind in shapes],
        scratch_shapes=[pltpu.VMEM(shape, jnp.float32) for shape in scratch for _ in (0, 1)],
        compiler_params=pltpu.CompilerParams(vmem_limit_bytes=16 * 2**20),
        cost_estimate=pl.CostEstimate(flops=flops, bytes_accessed=flops // 64, transcendentals=0),
    )(facts, *arrays)


def hidden_of(gate, up):
    return (jax.nn.silu(gate.astype(jnp.float32)) * up.astype(jnp.float32)).astype(jnp.bfloat16)


def slots_of(row_adapter_index, adapter_storage_slot):
    names = jnp.arange(adapter_storage_slot.shape[0], dtype=jnp.int32)
    same = row_adapter_index == names[None, :]
    return jnp.sum(jnp.where(same, adapter_storage_slot[None, :], 0), axis=1)


def gathered(
    gate_activation,
    up_activation,
    down_base_weight,
    first_factor_table,
    second_factor_table,
    row_adapter_index,
    adapter_storage_slot,
):
    hidden = hidden_of(gate_activation, up_activation)
    row_count = hidden.shape[0]
    owners = lax.axis_size("wide")
    local_adapter = first_factor_table.shape[0]
    slots = local_adapter * owners
    rank_portion = second_factor_table.shape[1]
    home = lax.axis_index("wide")
    slot_all = slots_of(row_adapter_index, adapter_storage_slot)
    blocks = slot_all.reshape(owners, row_count)
    order = jnp.arange(row_count, dtype=jnp.int32)
    earlier = (blocks[:, :, None] == blocks[:, None, :]) & (order[None, :] < order[:, None])
    position = jnp.sum(earlier.astype(jnp.int32), axis=2)
    rows = lax.all_gather(hidden, "wide", axis=0, tiled=True)
    base = jnp.dot(rows, down_base_weight, preferred_element_type=jnp.float32)
    low = jnp.einsum("re,nqe->nrq", rows, first_factor_table, preferred_element_type=jnp.float32)
    low = low.reshape(local_adapter, owners, row_count, low.shape[2])
    own = home * local_adapter + jnp.arange(local_adapter, dtype=jnp.int32)
    kept = []
    for item in range(MOST):
        mask = (blocks[None] == own[:, None, None]) & (position == item)[None]
        kept.append(jnp.sum(jnp.where(mask[..., None], low, 0), axis=2))
    low = lax.psum_scatter(jnp.stack(kept, axis=2), INNER, scatter_dimension=3, tiled=True)
    low = lax.all_gather(low.astype(jnp.bfloat16), "wide", axis=0, tiled=True)
    spread = 0
    for item in range(MOST):
        mask = (blocks[None] == jnp.arange(slots, dtype=jnp.int32)[:, None, None]) & (position == item)
        spread += jnp.where(mask[..., None], low[:, :, item][:, :, None], 0)
    spread = spread.reshape(slots, owners * row_count, rank_portion)
    delta = jnp.einsum("srq,sqw->rw", spread, second_factor_table, preferred_element_type=jnp.float32)
    total = base + delta
    return lax.psum_scatter(total, INNER, scatter_dimension=0, tiled=True).astype(jnp.bfloat16)


def ring_order(nodes):
    return list(range(0, nodes, 2)) + list(range(nodes - 1, 0, -2))


def ringed(
    gate_activation,
    up_activation,
    down_base_weight,
    first_factor_table,
    second_factor_table,
    row_adapter_index,
    adapter_storage_slot,
):
    f32, bf16 = jnp.float32, jnp.bfloat16
    row_count, width_part = gate_activation.shape
    owners = lax.axis_size("wide")
    nodes = owners // 2
    far = nodes // 2
    steps = far - 1
    own_nodes = nodes // 2
    own_blocks = owners // 2
    group_rows = 2 * row_count
    order = ring_order(nodes)
    depth = width_part // 2
    width = down_base_weight.shape[1]
    rank = first_factor_table.shape[1]

    table = []
    for w in range(owners):
        p = order.index(w // 2)
        at = lambda shift: order[(p + shift) % nodes]
        arrivals = [at(0)] + [at(s * k) for k in range(1, far) for s in (-1, 1)] + [at(far)]
        row = [2 * node + (w % 2 ^ side) for node in arrivals for side in (0, 1)]
        for half in (0, 1):
            here = [(at(s) < own_nodes) == (half == 0) for s in range(far)]
            row += [int(h) for h in here]
            row += [at(s if h else s + far) % own_nodes for s, h in enumerate(here)]
        table.append(row)
    home = lax.axis_index("wide")
    part = lax.axis_index(INNER)
    side = jnp.bitwise_and(home, 1)

    def moved(shift, cross=0):
        return [
            (order[p] * 2 + c, order[(p + shift) % nodes] * 2 + (c ^ cross))
            for p in range(nodes)
            for c in (0, 1)
        ]

    def send(value, shift, cross=0):
        return lax.ppermute(value, "wide", moved(shift, cross))

    def half_of(value, which, axis):
        return lax.dynamic_slice_in_dim(value, which * depth, depth, axis)

    crossed = [(2 * w + m, 2 * (w ^ 1) + (1 - m)) for w in range(owners) for m in (0, 1)]

    def to_three(to_sib, to_mp, to_both):
        return (
            send(to_sib, 0, 1),
            lax.ppermute(to_mp, INNER, SWAP),
            lax.ppermute(to_both, ("wide",) + INNER, crossed),
        )

    keep = hidden_of(half_of(gate_activation, side, 1), half_of(up_activation, side, 1))
    give = hidden_of(half_of(gate_activation, 1 - side, 1), half_of(up_activation, 1 - side, 1))
    right = [send(keep, 1), send(give, 1, 1)]
    left = [send(keep, -1), send(give, -1, 1)]
    twin = send(give, 0, 1)

    def joined(which):
        first = half_of(first_factor_table[0], which, 1).reshape(rank, depth // width, width)
        first = jnp.swapaxes(first, 0, 1).reshape(-1, width)
        return jnp.concatenate([half_of(down_base_weight, which, 0), first], axis=0)

    own_table, sib_table = joined(side), joined(1 - side)
    own_table, sib_table, twin, right, left = lax.optimization_barrier(
        (own_table, sib_table, twin, right, left)
    )
    sib_table = send(sib_table, 0, 1)
    home_late, row_adapter_index, second_factor_table, sib_table = lax.optimization_barrier(
        (home, row_adapter_index, second_factor_table, sib_table)
    )
    tables = [own_table, sib_table]

    pieces = [keep, twin] + right + left
    for step in range(2, steps + 1):
        right = [send(block, 1) for block in right]
        left = [send(block, -1) for block in left]
        if step < steps:
            right, left = lax.optimization_barrier((right, left))
            pieces += right + left

    row = lax.dynamic_index_in_dim(
        jnp.asarray(np.array(table, np.int32)), home_late, 0, keepdims=False
    )
    edges = np.cumsum([0, 2 * nodes, far, far, far, far])
    arrived, *rest = [row[a:b] for a, b in zip(edges[:-1], edges[1:])]
    flags = jnp.where(part == 0, rest[0], rest[2])
    facts = jnp.concatenate([side[None], part[None].astype(jnp.int32), flags])
    target = jnp.where(part == 0, rest[1], rest[3])
    places = target[:, None] == jnp.arange(own_nodes, dtype=jnp.int32)[None, :]
    slot_all = slots_of(row_adapter_index, adapter_storage_slot).reshape(owners, row_count)
    ranks = jnp.arange(row_count, dtype=jnp.int32)
    earlier = (slot_all[:, :, None] == slot_all[:, None, :]) & (ranks[None, :] < ranks[:, None])
    position = jnp.sum(earlier.astype(jnp.int32), axis=2)
    blocks = jnp.arange(owners, dtype=jnp.int32)

    items = jnp.arange(owners * MOST, dtype=jnp.int32)
    came = arrived[:, None] == blocks[None, :]
    slot_came = jnp.sum(jnp.where(came[:, :, None], slot_all[None], 0), axis=1).reshape(1, -1)
    place_came = jnp.sum(
        jnp.where(came[:, :, None], position[None] + MOST * blocks[None, :, None], 0), axis=1
    ).reshape(1, -1)
    chosen = jnp.stack(
        [
            ((place_came == items[:, None]) & (slot_came == slot)).astype(f32)
            for slot in (home_late, jnp.bitwise_xor(home_late, 1))
        ]
    )
    early_rows = len(pieces) * row_count
    middle_rows = early_rows + 4 * row_count
    choices = [
        chosen[:, :, :early_rows],
        chosen[:, :, early_rows:middle_rows],
        chosen[:, :, middle_rows:],
    ]

    half = own_blocks * MOST
    here = own_blocks * row_count
    slot_here = lax.dynamic_slice_in_dim(slot_all, part * own_blocks, own_blocks).reshape(here, 1)
    position_here = lax.dynamic_slice_in_dim(position, part * own_blocks, own_blocks)
    block_here = jnp.arange(here, dtype=jnp.int32)[:, None] // row_count
    spot = (
        jnp.bitwise_xor(slot_here, home_late) * half
        + block_here * MOST
        + position_here.reshape(here, 1)
    )
    spots = (spot == jnp.arange(owners * half, dtype=jnp.int32)[None, :]).astype(bf16)
    column = jnp.arange(owners * rank, dtype=jnp.int32)[None, :]
    piece = rank // 2
    own_rank = jnp.bitwise_xor(part, column // (owners * piece)) * piece + column % piece
    mask = (slot_here == column // piece % owners).astype(bf16)
    copies = (jnp.arange(rank, dtype=jnp.int32)[:, None] == own_rank).astype(bf16)

    other = lax.ppermute(second_factor_table, INNER, SWAP)
    second = jnp.concatenate(
        [values.reshape(owners * piece, width) for values in (second_factor_table, other)], axis=0
    )

    def flops(rows, columns):
        return rows * depth * columns // 16

    count = len(pieces)
    early = kernel_call(
        functools.partial(early_kernel, count),
        facts,
        (*pieces, *tables, choices[0]),
        [((count // 2, group_rows, width), f32)] * 2 + [((2, owners * MOST, rank), f32)],
        [(early_rows, width), (early_rows, rank)],
        flops(early_rows, width + rank),
    )
    ready = (facts, spots, mask, copies, choices, places)
    right, left, early, ready = lax.optimization_barrier((right, left, early, ready))
    facts, spots, mask, copies, choices, places = ready

    last = [send(right[0], 1), send(left[1], -1)]

    def shares(pairs):
        shape = (pairs, group_rows, width)
        return [(shape, f32)] * 2 + [(shape, bf16)] * 2

    *middle, compact = kernel_call(
        functools.partial(middle_kernel, 4),
        facts,
        (*right, *left, *tables, choices[1], early[2], early[0], early[1]),
        shares(far - 1) + [((2, owners * MOST, rank), f32)],
        [(4 * row_count, width), (4 * row_count, rank)],
        flops(4 * row_count, width + rank),
    )
    kept_more = middle[0]
    got_more = to_three(*middle[1:])
    last, compact, second = lax.optimization_barrier((last, compact, second))

    kept, sent = kernel_call(
        low_kernel,
        facts,
        (*last, *tables, choices[2], compact),
        [((2, half, rank), f32)] * 2,
        [(group_rows, rank)],
        flops(group_rows, rank),
    )
    got = to_three(kept, sent, sent)
    got, last = lax.optimization_barrier((got, last))

    kept_one, *one = kernel_call(
        last_kernel,
        facts,
        (*last, *tables, early[0], early[1]),
        shares(1),
        [(group_rows, width)],
        flops(group_rows, width),
    )
    got_one = to_three(*one)

    low = (kept + got[1] + (got[0] + got[2])[::-1]).astype(bf16)

    def from_node(value, gap):
        return lax.ppermute(value, "wide", [(w, w ^ (2 * gap)) for w in range(owners)])

    gap = 1
    while gap < nodes:
        reach = min(4, nodes // gap)
        low = jnp.concatenate([low] + [from_node(low, gap * k) for k in range(1, reach)], axis=0)
        gap *= reach

    more = kept_more + got_more[0] + got_more[1].astype(f32) + got_more[2].astype(f32)
    rows = 0
    for pair in range(1, far):
        rows = rows + jnp.where(places[pair][:, None, None], more[pair - 1 : pair], 0)
    own_low = jnp.dot(spots, low.reshape(owners * half, rank), preferred_element_type=f32)
    spread = jnp.dot(own_low.astype(bf16), copies, preferred_element_type=f32).astype(bf16) * mask
    delta = jnp.dot(spread, second, preferred_element_type=f32)
    one = kept_one + got_one[0] + got_one[1].astype(f32) + got_one[2].astype(f32)
    rows = rows + jnp.where(places[0][:, None, None], one, 0)
    return (delta + rows.reshape(-1, width)).astype(bf16)


def solution(mesh):
    shape = dict(mesh.shape)
    wide, inner = shape["wide"], shape["mp"] * shape["sub"]
    paired = shape["sub"] == 1 and inner == 2 and wide % 8 == 0 and wide & (wide - 1) == 0
    if paired:
        nodes = wide // 2
        order = ring_order(nodes)
        paired = all(
            (order[p] < nodes // 2) != (order[(p + nodes // 2) % nodes] < nodes // 2)
            for p in range(nodes)
        )
    return jax.shard_map(
        ringed if paired else gathered,
        mesh=mesh,
        in_specs=(
            P(("groups", "wide"), ("mp", "sub")),
            P(("groups", "wide"), ("mp", "sub")),
            P(("mp", "sub"), "wide"),
            P("wide", None, ("mp", "sub")),
            P(None, ("mp", "sub"), "wide"),
            P("groups", None),
            P(),
        ),
        out_specs=P(("groups", "mp", "sub"), "wide"),
        check_vma=False,
    )
```

time: 133 us -> 139 us (1.045)
  waiting for transfers between devices: 52.4 us -> 23.4 us
  local copies, waits for them, and re-layouts: 9.03 us -> 32 us
  other arithmetic: 12.5 us -> 20.8 us
  starting transfers between devices: 26.5 us -> 29.3 us
  Pallas kernels: 27.9 us -> 29.6 us
    ppermute x21 -> x19, waiting for transfers between devices: 44.5 us -> 20.7 us  [send(): return lax.ppermute(value, 'wide', moved(shift, cross))]
    dynamic_slice x0 -> x3, local copies, waits for them, and re-layouts: none -> 11.8 us  [the longest x2 11.7 us: half_of(): return lax.dynamic_slice_in_dim(value, which * depth, depth, axis)]
    concatenate x3, other arithmetic: 2.15 us -> 13.6 us  [the longest x1 11.3 us: joined(): return jnp.concatenate([half_of(down_base_weight, which, 0), first], axis=0)]
    ppermute x4 -> x6, waiting for transfers between devices: 5.79 us -> 0.42 us  [the longest x3 0.41 us: to_three(): lax.ppermute(to_mp, INNER, SWAP)]
    reshape x1 -> x2, local copies, waits for them, and re-layouts: 0.08 us -> 5.18 us  [joined(): half_of(first_factor_table[0], which, 1)]
    transpose x0 -> x2, local copies, waits for them, and re-layouts: none -> 4.41 us  [joined(): first = jnp.swapaxes(first, 0, 1).reshape(-1, width)]
    unnamed x43 -> x29, local copies, waits for them, and re-layouts: 4.61 us -> 8.79 us
    convert_element_type x3 -> x0, other arithmetic: 2.96 us -> none  [the longest x2 2.9 us: over_mp(): jnp.where(f, b, a).astype(bf16)]
  transfers between devices with their start and end apart: 30 -> 30, of which waited for: 11 -> 5; matrix products, arithmetic and copies ran while one was open for 10% -> 30% of each run, Pallas kernels for 20% -> 21%
where the time goes in v6:
time: 139 us; the launch traced here: 138 us
  local copies, waits for them, and re-layouts  32 us (23%)
  Pallas kernels  29.6 us (21%)
  starting transfers between devices  29.3 us (21%)
  waiting for transfers between devices  23.4 us (17%)
  other arithmetic  20.8 us (15%)
  matrix products  2.71 us (2%)
    pallas_call x4, Pallas kernels, kernel_call(): pl.pallas_call(kernel, in_specs=[pl.BlockSpec(memory_space=pltpu.SMEM)] +...  29.6 us
    ppermute x19, waiting for transfers between devices, send(): return lax.ppermute(value, 'wide', moved(shift, cross))  20.7 us
    ppermute x19, starting transfers between devices, send(): return lax.ppermute(value, 'wide', moved(shift, cross))  16.2 us
    dynamic_slice x2, local copies, waits for them, and re-layouts, half_of(): return lax.dynamic_slice_in_dim(value, which * depth, depth, axis)  11.7 us
    concatenate x1, other arithmetic, joined(): return jnp.concatenate([half_of(down_base_weight, which, 0), first], axis=0)  11.3 us
    unnamed x29, local copies, waits for them, and re-layouts  8.79 us
    ppermute x4, starting transfers between devices, from_node(): lax.ppermute(value, 'wide', [(w, w ^ 2 * gap) for w in range(owners)])  6.15 us
    reshape x2, local copies, waits for them, and re-layouts, joined(): half_of(first_factor_table[0], which, 1)  5.18 us
  transfers between devices with their start and end apart: 30, of which 5 were waited for; matrix products, arithmetic and copies ran while one was open for 30% of the time, Pallas kernels for 21%

profile of v6, /device:TPU:0, one launch (start us, length us, event | category | flops | bytes accessed | tf_op | source)
XLA Modules:
  0.0 138.1 jit_solution(14544809918908802167)
XLA Ops:
  0.0 2.0 %fusion.10 = (bf16[32,7168]{1,0:T(8,128)(2,1)S(1)}, bf16[32,7168]{1,0:T(8,128)(2,1)S(1)}) fusion(bf16[32,14336]{1,0:T(8,128)(2,1)} %param.9, s32[]{:T(128)S(6)} %select_n.119, bf16[32,14336]{1,0:T(8,128)(2,1)} %param.8, s32[]{:T(128)S(6)} %select_n.120), kind=kLoop, calls=%fused_computation.21 | loop fusion | flops 3670016 | bytes 2752520 | tf_op jit(solution)/shard_map/convert_element_type | solution.py:115
  2.0 0.5 collective-permute-start
  2.5 2.7 %collective-permute-start.2 = (bf16[32,7168]{1,0:T(8,128)(2,1)S(1)}, bf16[32,7168]{1,0:T(8,128)(2,1)S(1)}, u32[]{:S(2)}, u32[]{:S(2)}) collective-permute-start(bf16[32,7168]{1,0:T(8,128)(2,1)S(1)} %get-tuple-element.116), channel_id=1, source_target_pairs={{0,10},{2,8},{8,18},{10,16},{16,26},{18,24},{24,30},{26,28},{28,22... | collective-permute-start | bytes 1376264 | tf_op jit(solution)/shard_map/ppermute | solution.py:216
  5.2 1.6 %collective-permute-start.1 = (bf16[32,7168]{1,0:T(8,128)(2,1)S(1)}, bf16[32,7168]{1,0:T(8,128)(2,1)S(1)}, u32[]{:S(2)}, u32[]{:S(2)}) collective-permute-start(bf16[32,7168]{1,0:T(8,128)(2,1)S(1)} %get-tuple-element.115.refs_0_), channel_id=1, source_target_pairs={{0,8},{2,10},{8,16},{10,18},{16,24},{18,26},{24,28},{26,30},{28,20... | collective-permute-start | bytes 1376264 | tf_op jit(solution)/shard_map/ppermute | solution.py:216
  7.2 10.4 %constant_dynamic-slice_fusion.4 = (bf16[7168,512]{1,0:T(8,128)(2,1)}, bf16[7168,512]{1,0:T(8,128)(2,1)}) fusion(bf16[14336,512]{1,0:T(8,128)(2,1)} %param.10, s32[]{:T(128)S(6)} %select_n.120, s32[]{:T(128)S(6)} %select_n.119), kind=kLoop, calls=%fused_computation.89 | loop fusion | bytes 29360136 | tf_op jit(solution)/shard_map/dynamic_slice | solution.py:219
  17.6 1.4 constant_dynamic-slice_fusion.3
  19.0 2.6 %reshape.426 = bf16[64,14,512]{2,1,0:T(8,128)(2,1)} reshape(bf16[1,64,7168]{2,1,0:T(8,128)(2,1)} %get-tuple-element.118) | data formatting | bytes 1835008 | tf_op jit(solution)/shard_map/reshape | solution.py:237
  21.6 2.7 %copy.11 = bf16[14,64,512]{2,1,0:T(8,128)(2,1)} copy(bf16[14,64,512]{2,0,1:T(8,128)(2,1)} %bitcast.57) | data formatting | bytes 1835008 | tf_op jit(solution)/shard_map/transpose | solution.py:238
  24.2 2.6 %reshape.428 = bf16[64,14,512]{2,1,0:T(8,128)(2,1)} reshape(bf16[1,64,7168]{2,1,0:T(8,128)(2,1)} %get-tuple-element.117) | data formatting | bytes 1835008 | tf_op jit(solution)/shard_map/reshape | solution.py:237
  26.8 1.7 %copy.12 = bf16[14,64,512]{2,1,0:T(8,128)(2,1)S(1)} copy(bf16[14,64,512]{2,0,1:T(8,128)(2,1)} %bitcast.58) | data formatting | bytes 1835008 | tf_op jit(solution)/shard_map/transpose | solution.py:238
  28.6 11.3 %pad_maximum_fusion = (bf16[8064,512]{1,0:T(8,128)(2,1)}, bf16[8064,512]{1,0:T(8,128)(2,1)}) fusion(bf16[896,512]{1,0:T(8,128)(2,1)} %bitcast.59, bf16[7168,512]{1,0:T(8,128)(2,1)} %get-tuple-element.114, bf16[896,512]{1,0:T(8,128)(2,1)S(1)} %bitcast.60, bf16[7168,512]{1,0:T(8,128)(2,1)} %get-tuple-element.113), kind=kLoop, calls=%fused_computation | loop fusion | flops 33030144 | bytes 33030144 | tf_op jit(solution)/shard_map/concatenate | solution.py:239
  40.1 2.0 %collective-permute-start.5 = (bf16[32,7168]{1,0:T(8,128)(2,1)S(1)}, bf16[32,7168]{1,0:T(8,128)(2,1)}, u32[]{:S(2)}, u32[]{:S(2)}) collective-permute-start(bf16[32,7168]{1,0:T(8,128)(2,1)S(1)} %collective-permute-done.1.refs_2_), channel_id=1, source_target_pairs={{0,8},{2,10},{8,16},{10,18},{16,24},{18,26},{24,28},{26,30},{28,20... | collective-permute-start | bytes 1376264 | tf_op jit(solution)/shard_map/ppermute | solution.py:216
  42.1 1.6 %collective-permute-start.6 = (bf16[32,7168]{1,0:T(8,128)(2,1)S(1)}, bf16[32,7168]{1,0:T(8,128)(2,1)}, u32[]{:S(2)}, u32[]{:S(2)}) collective-permute-start(bf16[32,7168]{1,0:T(8,128)(2,1)S(1)} %collective-permute-done.2.refs_3_), channel_id=1, source_target_pairs={{0,8},{2,10},{8,16},{10,18},{16,24},{18,26},{24,28},{26,30},{28,20... | collective-permute-start | bytes 1376264 | tf_op jit(solution)/shard_map/ppermute | solution.py:216
  44.2 0.7 fusion.16
  44.9 8.7 %collective-permute-done.5.refs_6_ = bf16[32,7168]{1,0:T(8,128)(2,1)} collective-permute-done((bf16[32,7168]{1,0:T(8,128)(2,1)S(1)}, bf16[32,7168]{1,0:T(8,128)(2,1)}, u32[]{:S(2)}, u32[]{:S(2)}) %collective-permute-start.5) | collective-permute-done | bytes 458784 | tf_op jit(solution)/shard_map/ppermute | solution.py:216
  53.6 9.3 %collective-permute-done.6.refs_7_ = bf16[32,7168]{1,0:T(8,128)(2,1)} collective-permute-done((bf16[32,7168]{1,0:T(8,128)(2,1)S(1)}, bf16[32,7168]{1,0:T(8,128)(2,1)}, u32[]{:S(2)}, u32[]{:S(2)}) %collective-permute-start.6) | collective-permute-done | bytes 458784 | tf_op jit(solution)/shard_map/ppermute | solution.py:216
  62.8 2.7 %collective-permute-done.8.refs_9_ = bf16[32,7168]{1,0:T(8,128)(2,1)} collective-permute-done((bf16[32,7168]{1,0:T(8,128)(2,1)S(1)}, bf16[32,7168]{1,0:T(8,128)(2,1)}, u32[]{:S(2)}, u32[]{:S(2)}) %collective-permute-start.8) | collective-permute-done | bytes 458784 | tf_op jit(solution)/shard_map/ppermute | solution.py:216
  65.5 1.6 %collective-permute-start.10 = (bf16[32,7168]{1,0:T(8,128)(2,1)}, bf16[32,7168]{1,0:T(8,128)(2,1)}, u32[]{:S(2)}, u32[]{:S(2)}) collective-permute-start(bf16[32,7168]{1,0:T(8,128)(2,1)} %collective-permute-done.6.refs_7_), channel_id=1, source_target_pairs={{0,8},{2,10},{8,16},{10,18},{16,24},{18,26},{24,28},{26,30},{28,20... | collective-permute-start | bytes 1376264 | tf_op jit(solution)/shard_map/ppermute | solution.py:216
  68.0 1.6 %collective-permute-start.9 = (bf16[32,7168]{1,0:T(8,128)(2,1)}, bf16[32,7168]{1,0:T(8,128)(2,1)}, u32[]{:S(2)}, u32[]{:S(2)}) collective-permute-start(bf16[32,7168]{1,0:T(8,128)(2,1)} %collective-permute-done.5.refs_6_), channel_id=1, source_target_pairs={{0,8},{2,10},{8,16},{10,18},{16,24},{18,26},{24,28},{26,30},{28,20... | collective-permute-start | bytes 1376264 | tf_op jit(solution)/shard_map/ppermute | solution.py:216
  69.6 0.7 constant_dynamic-slice_fusion.2
  70.6 0.5 convert_reduce_fusion
  71.7 1.6 %collective-permute-start.16 = (bf16[16,32,512]{2,1,0:T(8,128)(2,1)}, bf16[16,32,512]{2,1,0:T(8,128)(2,1)}, u32[]{:S(2)}, u32[]{:S(2)}) collective-permute-start(bf16[16,32,512]{2,1,0:T(8,128)(2,1)} %param.12), channel_id=1, source_target_pairs={{0,1},{1,0},{2,3},{3,2},{4,5},{5,4},{6,7},{7,6},{8,9},{9,8},{10,11... | collective-permute-start | bytes 1572872 | tf_op jit(solution)/shard_map/ppermute | solution.py:311
  73.4 0.8 fusion.15
  74.4 3.3 %copy-done = bf16[8064,512]{1,0:T(8,128)(2,1)S(1)} copy-done((bf16[8064,512]{1,0:T(8,128)(2,1)S(1)}, bf16[8064,512]{1,0:T(8,128)(2,1)}, u32[]{:S(2)}) %copy-start) | copy-done | bytes 8257560
  77.7 1.0 copy-done.4
  78.7 1.0 copy-done.6
  79.8 11.6 %shard_map.82 = (f32[5,64,512]{2,1,0:T(8,128)S(1)}, f32[5,64,512]{2,1,0:T(8,128)S(1)}, f32[2,32,64]{2,1,0:T(8,128)S(1)}) custom-call(s32[6]{0:T(128)S(1)} %pad_add_fusion.facts, bf16[32,7168]{1,0:T(8,128)(2,1)S(1)} %get-tuple-element.115.refs_0_, bf16[32,7168]{1,0:T(8,128)(2,1)S(1)} %collective-permute-done.refs_1_, ...), custom_call_target="tpu_custom_call" | custom-call | flops 82575360 | bytes 1290240 | tf_op jit(solution)/shard_map/pallas_call | solution.py:103
  91.4 1.0 compare_convert_fusion
  92.4 1.6 %collective-permute-start.14 = (bf16[32,7168]{1,0:T(8,128)(2,1)}, bf16[32,7168]{1,0:T(8,128)(2,1)S(1)}, u32[]{:S(2)}, u32[]{:S(2)}) collective-permute-start(bf16[32,7168]{1,0:T(8,128)(2,1)} %collective-permute-done.9.refs_0_), channel_id=1, source_target_pairs={{0,8},{2,10},{8,16},{10,18},{16,24},{18,26},{24,28},{26,30},{28,20... | collective-permute-start | bytes 1376264 | tf_op jit(solution)/shard_map/ppermute | solution.py:216
  94.5 7.8 %shard_map.83 = (f32[3,64,512]{2,1,0:T(8,128)S(1)}, f32[3,64,512]{2,1,0:T(8,128)S(1)}, bf16[3,64,512]{2,1,0:T(8,128)(2,1)}, bf16[3,64,512]{2,1,0:T(8,128)(2,1)S(1)}, f32[2,32,64]{2,1,0:T(8,128)S(1)}) custom-call(s32[6]{0:T(128)S(1)} %pad_add_fusion.facts, bf16[32,7168]{1,0:T(8,128)(2,1)} %collective-permute-done.9.refs_0_, ...), custom_call_target="tpu_custom_call" | custom-call | flops 33030144 | bytes 516096 | tf_op jit(solution)/shard_map/pallas_call | solution.py:103
  102.3 0.5 collective-permute-start.25
  102.8 1.3 collective-permute-start.26
  104.8 2.2 %pad_maximum_fusion.2 = bf16[1024,512]{1,0:T(8,128)(2,1)} fusion(bf16[512,512]{1,0:T(8,128)(2,1)} %bitcast.11, bf16[512,512]{1,0:T(8,128)(2,1)} %bitcast.10), kind=kLoop, calls=%fused_computation.11 | loop fusion | flops 2097152 | bytes 2097152 | tf_op jit(solution)/shard_map/concatenate | solution.py:312
  107.1 3.3 %copy-done.2 = bf16[8064,512]{1,0:T(8,128)(2,1)S(1)} copy-done((bf16[8064,512]{1,0:T(8,128)(2,1)S(1)}, bf16[8064,512]{1,0:T(8,128)(2,1)}, u32[]{:S(2)}) %copy-start.2) | copy-done | bytes 8257560
  110.4 4.1 %shard_map.84 = (f32[2,16,64]{2,1,0:T(8,128)S(1)}, f32[2,16,64]{2,1,0:T(8,128)S(1)}) custom-call(s32[6]{0:T(128)S(1)} %pad_add_fusion.facts, bf16[32,7168]{1,0:T(8,128)(2,1)S(1)} %collective-permute-done.14.piece, bf16[32,7168]{1,0:T(8,128)(2,1)S(1)} %collective-permute-done.15.other, bf16[8064,512]{1,0:T(8,128)(2,1)S(1)} %copy-done.2, ...), custom_call_target="tpu_custom_call" | custom-call | flops 1835008 | bytes 28672 | tf_op jit(solution)/shard_map/pallas_call | solution.py:103
  114.6 0.6 collective-permute-start.18
  115.2 1.1 collective-permute-start.19
  116.3 0.5 collective-permute-start.17
  116.8 1.3 convert_add_fusion
  118.5 0.5 collective-permute-start.20
  119.1 1.2 collective-permute-start.21
  120.3 1.8 %collective-permute-start.22 = (bf16[2,16,64]{2,1,0:T(8,128)(2,1)S(1)}, bf16[2,16,64]{2,1,0:T(8,128)(2,1)S(1)}, u32[]{:S(2)}, u32[]{:S(2)}) collective-permute-start(bf16[2,16,64]{2,1,0:T(8,128)(2,1)S(1)} %get-tuple-element.112), channel_id=1, source_target_pairs={{0,12},{2,14},{4,8},{6,10},{8,4},{10,6},{12,0},{14,2},{16,28},{18,... | collective-permute-start | bytes 12296 | tf_op jit(solution)/shard_map/ppermute | solution.py:374
  122.2 6.1 %shard_map.85 = (f32[1,64,512]{2,1,0:T(8,128)S(1)}, f32[1,64,512]{2,1,0:T(8,128)S(1)}, bf16[1,64,512]{2,1,0:T(8,128)(2,1)S(1)}, bf16[1,64,512]{2,1,0:T(8,128)(2,1)S(1)}) custom-call(s32[6]{0:T(128)S(1)} %pad_add_fusion.facts, bf16[32,7168]{1,0:T(8,128)(2,1)S(1)} %collective-permute-done.14.piece, bf16[32,7168]{1,0:T(8,128)(2,1)S(1)} %collective-permute-done.15.other, ...), custom_call_target="tpu_custom_call" | custom-call | flops 14680064 | bytes 229376 | tf_op jit(solution)/shard_map/pallas_call | solution.py:103
  128.3 1.4 collective-permute-start.28
  129.7 0.5 collective-permute-start.29
  130.2 2.6 %collective-permute-start.23 = (bf16[8,16,64]{2,1,0:T(8,128)(2,1)S(1)}, bf16[8,16,64]{2,1,0:T(8,128)(2,1)S(1)}, u32[]{:S(2)}, u32[]{:S(2)}) collective-permute-start(bf16[8,16,64]{2,1,0:T(8,128)(2,1)S(1)} %pad_maximum_fusion.3), channel_id=1, source_target_pairs={{0,16},{2,18},{4,20},{6,22},{8,24},{10,26},{12,28},{14,30},{16,0},... | collective-permute-start | bytes 49160 | tf_op jit(solution)/shard_map/ppermute | solution.py:374
  132.8 2.3 %collective-permute-done.23 = bf16[8,16,64]{2,1,0:T(8,128)(2,1)S(1)} collective-permute-done((bf16[8,16,64]{2,1,0:T(8,128)(2,1)S(1)}, bf16[8,16,64]{2,1,0:T(8,128)(2,1)S(1)}, u32[]{:S(2)}, u32[]{:S(2)}) %collective-permute-start.23) | collective-permute-done | bytes 16416 | tf_op jit(solution)/shard_map/ppermute | solution.py:374
  135.6 2.5 %fusion.1 = bf16[256,512]{1,0:T(8,128)(2,1)} fusion(f32[256,512]{1,0:T(8,128)S(1)} %fusion.12, bf16[1024,512]{1,0:T(8,128)(2,1)} %pad_maximum_fusion.2, bf16[256,1024]{1,0:T(8,128)(2,1)S(1)} %copy-done.7, bf16[256,64]{0,1:T(8,128)(2,1)S(1)} %convolution_convert_fusion.1, bf16[64,1024]{1,0:T(8,128)(2,1)S(1)} %copy-done.9), kind=kOutput, calls=%fused_computation.5 | convolution fusion | flops 302776320 | bytes 2523136 | tf_op jit(solution)/shard_map/dot_general | solution.py:388
  (104 shorter events, 5.6 us)
Async XLA Ops:
  2.0 37.9 %collective-permute-start = (bf16[32,7168]{1,0:T(8,128)(2,1)S(1)}, bf16[32,7168]{1,0:T(8,128)(2,1)S(1)}, u32[]{:S(2)}, u32[]{:S(2)}) collective-permute-start(bf16[32,7168]{1,0:T(8,128)(2,1)S(1)} %get-tuple-element.116), channel_id=1, source_target_pairs={{0,2},{2,0},{8,10},{10,8},{16,18},{18,16},{24,26},{26,24},{28,30},... | collective-permute-start | bytes 1376264 | tf_op jit(solution)/shard_map/ppermute | solution.py:216
  2.5 37.4 %collective-permute-start.2 = (bf16[32,7168]{1,0:T(8,128)(2,1)S(1)}, bf16[32,7168]{1,0:T(8,128)(2,1)S(1)}, u32[]{:S(2)}, u32[]{:S(2)}) collective-permute-start(bf16[32,7168]{1,0:T(8,128)(2,1)S(1)} %get-tuple-element.116), channel_id=1, source_target_pairs={{0,10},{2,8},{8,18},{10,16},{16,26},{18,24},{24,30},{26,28},{28,22... | collective-permute-start | bytes 1376264 | tf_op jit(solution)/shard_map/ppermute | solution.py:216
  5.2 12.4 %copy-start.8 = (bf16[1,64,14336]{2,1,0:T(8,128)(2,1)S(1)}, bf16[1,64,14336]{2,1,0:T(8,128)(2,1)}, u32[]{:S(2)}) copy-start(bf16[1,64,14336]{2,1,0:T(8,128)(2,1)} %param.11) | copy-start | bytes 5505028
  5.2 34.7 %collective-permute-start.1 = (bf16[32,7168]{1,0:T(8,128)(2,1)S(1)}, bf16[32,7168]{1,0:T(8,128)(2,1)S(1)}, u32[]{:S(2)}, u32[]{:S(2)}) collective-permute-start(bf16[32,7168]{1,0:T(8,128)(2,1)S(1)} %get-tuple-element.115.refs_0_), channel_id=1, source_target_pairs={{0,8},{2,10},{8,16},{10,18},{16,24},{18,26},{24,28},{26,30},{28,20... | collective-permute-start | bytes 1376264 | tf_op jit(solution)/shard_map/ppermute | solution.py:216
  6.8 33.1 %collective-permute-start.3 = (bf16[32,7168]{1,0:T(8,128)(2,1)S(1)}, bf16[32,7168]{1,0:T(8,128)(2,1)S(1)}, u32[]{:S(2)}, u32[]{:S(2)}) collective-permute-start(bf16[32,7168]{1,0:T(8,128)(2,1)S(1)} %get-tuple-element.115.refs_0_), channel_id=1, source_target_pairs={{0,4},{2,6},{8,0},{10,2},{16,8},{18,10},{24,16},{26,18},{28,24},{3... | collective-permute-start | bytes 1376264 | tf_op jit(solution)/shard_map/ppermute | solution.py:216
  7.2 32.7 %collective-permute-start.4 = (bf16[32,7168]{1,0:T(8,128)(2,1)S(1)}, bf16[32,7168]{1,0:T(8,128)(2,1)S(1)}, u32[]{:S(2)}, u32[]{:S(2)}) collective-permute-start(bf16[32,7168]{1,0:T(8,128)(2,1)S(1)} %get-tuple-element.116), channel_id=1, source_target_pairs={{0,6},{2,4},{8,2},{10,0},{16,10},{18,8},{24,18},{26,16},{28,26},{3... | collective-permute-start | bytes 1376264 | tf_op jit(solution)/shard_map/ppermute | solution.py:216
  28.6 41.8 %copy-start.11 = (s32[512,1]{0,1:T(1,128)S(1)}, s32[512,1]{0,1:T(1,128)}, u32[]{:S(2)}) copy-start(s32[512,1]{0,1:T(1,128)} %param.13) | copy-start | bytes 6148
  28.6 41.8 %copy-start.12 = (s32[16]{0:T(128)S(1)}, s32[16]{0:T(128)}, u32[]{:S(2)}) copy-start(s32[16]{0:T(128)} %param.14) | copy-start | bytes 196
  39.9 34.4 %copy-start.3 = (bf16[32,7168]{1,0:T(8,128)(2,1)}, bf16[32,7168]{1,0:T(8,128)(2,1)S(1)}, u32[]{:S(2)}) copy-start(bf16[32,7168]{1,0:T(8,128)(2,1)S(1)} %collective-permute-done.3.refs_4_) | copy-start | bytes 1376260
  39.9 34.4 %copy-start.5 = (bf16[32,7168]{1,0:T(8,128)(2,1)}, bf16[32,7168]{1,0:T(8,128)(2,1)S(1)}, u32[]{:S(2)}) copy-start(bf16[32,7168]{1,0:T(8,128)(2,1)S(1)} %collective-permute-done.4.refs_5_) | copy-start | bytes 1376260
  39.9 29.7 %collective-permute-start.13 = (bf16[8064,512]{1,0:T(8,128)(2,1)}, bf16[8064,512]{1,0:T(8,128)(2,1)}, u32[]{:S(2)}, u32[]{:S(2)}) collective-permute-start(bf16[8064,512]{1,0:T(8,128)(2,1)} %get-tuple-element.65), channel_id=1, source_target_pairs={{0,2},{2,0},{8,10},{10,8},{16,18},{18,16},{24,26},{26,24},{28,30},... | collective-permute-start | bytes 24772616 | tf_op jit(solution)/shard_map/ppermute | solution.py:216
  40.1 13.5 %collective-permute-start.5 = (bf16[32,7168]{1,0:T(8,128)(2,1)S(1)}, bf16[32,7168]{1,0:T(8,128)(2,1)}, u32[]{:S(2)}, u32[]{:S(2)}) collective-permute-start(bf16[32,7168]{1,0:T(8,128)(2,1)S(1)} %collective-permute-done.1.refs_2_), channel_id=1, source_target_pairs={{0,8},{2,10},{8,16},{10,18},{16,24},{18,26},{24,28},{26,30},{28,20... | collective-permute-start | bytes 1376264 | tf_op jit(solution)/shard_map/ppermute | solution.py:216
  42.1 20.7 %collective-permute-start.6 = (bf16[32,7168]{1,0:T(8,128)(2,1)S(1)}, bf16[32,7168]{1,0:T(8,128)(2,1)}, u32[]{:S(2)}, u32[]{:S(2)}) collective-permute-start(bf16[32,7168]{1,0:T(8,128)(2,1)S(1)} %collective-permute-done.2.refs_3_), channel_id=1, source_target_pairs={{0,8},{2,10},{8,16},{10,18},{16,24},{18,26},{24,28},{26,30},{28,20... | collective-permute-start | bytes 1376264 | tf_op jit(solution)/shard_map/ppermute | solution.py:216
  43.7 19.2 %collective-permute-start.7 = (bf16[32,7168]{1,0:T(8,128)(2,1)S(1)}, bf16[32,7168]{1,0:T(8,128)(2,1)}, u32[]{:S(2)}, u32[]{:S(2)}) collective-permute-start(bf16[32,7168]{1,0:T(8,128)(2,1)S(1)} %collective-permute-done.3.refs_4_), channel_id=1, source_target_pairs={{0,4},{2,6},{8,0},{10,2},{16,8},{18,10},{24,16},{26,18},{28,24},{3... | collective-permute-start | bytes 1376264 | tf_op jit(solution)/shard_map/ppermute | solution.py:216
  44.1 21.4 %collective-permute-start.8 = (bf16[32,7168]{1,0:T(8,128)(2,1)S(1)}, bf16[32,7168]{1,0:T(8,128)(2,1)}, u32[]{:S(2)}, u32[]{:S(2)}) collective-permute-start(bf16[32,7168]{1,0:T(8,128)(2,1)S(1)} %collective-permute-done.4.refs_5_), channel_id=1, source_target_pairs={{0,4},{2,6},{8,0},{10,2},{16,8},{18,10},{24,16},{26,18},{28,24},{3... | collective-permute-start | bytes 1376264 | tf_op jit(solution)/shard_map/ppermute | solution.py:216
  65.5 26.9 %collective-permute-start.10 = (bf16[32,7168]{1,0:T(8,128)(2,1)}, bf16[32,7168]{1,0:T(8,128)(2,1)}, u32[]{:S(2)}, u32[]{:S(2)}) collective-permute-start(bf16[32,7168]{1,0:T(8,128)(2,1)} %collective-permute-done.6.refs_7_), channel_id=1, source_target_pairs={{0,8},{2,10},{8,16},{10,18},{16,24},{18,26},{24,28},{26,30},{28,20... | collective-permute-start | bytes 1376264 | tf_op jit(solution)/shard_map/ppermute | solution.py:216
  67.1 25.3 %collective-permute-start.11 = (bf16[32,7168]{1,0:T(8,128)(2,1)}, bf16[32,7168]{1,0:T(8,128)(2,1)}, u32[]{:S(2)}, u32[]{:S(2)}) collective-permute-start(bf16[32,7168]{1,0:T(8,128)(2,1)} %collective-permute-done.7.refs_8_), channel_id=1, source_target_pairs={{0,4},{2,6},{8,0},{10,2},{16,8},{18,10},{24,16},{26,18},{28,24},{3... | collective-permute-start | bytes 1376264 | tf_op jit(solution)/shard_map/ppermute | solution.py:216
  67.6 24.9 %collective-permute-start.12 = (bf16[32,7168]{1,0:T(8,128)(2,1)}, bf16[32,7168]{1,0:T(8,128)(2,1)}, u32[]{:S(2)}, u32[]{:S(2)}) collective-permute-start(bf16[32,7168]{1,0:T(8,128)(2,1)} %collective-permute-done.8.refs_9_), channel_id=1, source_target_pairs={{0,4},{2,6},{8,0},{10,2},{16,8},{18,10},{24,16},{26,18},{28,24},{3... | collective-permute-start | bytes 1376264 | tf_op jit(solution)/shard_map/ppermute | solution.py:216
  68.0 24.4 %collective-permute-start.9 = (bf16[32,7168]{1,0:T(8,128)(2,1)}, bf16[32,7168]{1,0:T(8,128)(2,1)}, u32[]{:S(2)}, u32[]{:S(2)}) collective-permute-start(bf16[32,7168]{1,0:T(8,128)(2,1)} %collective-permute-done.5.refs_6_), channel_id=1, source_target_pairs={{0,8},{2,10},{8,16},{10,18},{16,24},{18,26},{24,28},{26,30},{28,20... | collective-permute-start | bytes 1376264 | tf_op jit(solution)/shard_map/ppermute | solution.py:216
  71.7 31.1 %collective-permute-start.16 = (bf16[16,32,512]{2,1,0:T(8,128)(2,1)}, bf16[16,32,512]{2,1,0:T(8,128)(2,1)}, u32[]{:S(2)}, u32[]{:S(2)}) collective-permute-start(bf16[16,32,512]{2,1,0:T(8,128)(2,1)} %param.12), channel_id=1, source_target_pairs={{0,1},{1,0},{2,3},{3,2},{4,5},{5,4},{6,7},{7,6},{8,9},{9,8},{10,11... | collective-permute-start | bytes 1572872 | tf_op jit(solution)/shard_map/ppermute | solution.py:311
  74.4 3.4 %copy-start = (bf16[8064,512]{1,0:T(8,128)(2,1)S(1)}, bf16[8064,512]{1,0:T(8,128)(2,1)}, u32[]{:S(2)}) copy-start(bf16[8064,512]{1,0:T(8,128)(2,1)} %get-tuple-element.68.refs_10_.refs_4_.table) | copy-start | bytes 24772612
  77.7 1.0 copy-start.4
  78.7 1.0 copy-start.6
  79.8 14.8 %copy-start.1 = (bf16[8064,512]{1,0:T(8,128)(2,1)S(1)}, bf16[8064,512]{1,0:T(8,128)(2,1)}, u32[]{:S(2)}) copy-start(bf16[8064,512]{1,0:T(8,128)(2,1)} %get-tuple-element.68.refs_10_.refs_4_.table) | copy-start | bytes 24772612
  92.4 14.6 %collective-permute-start.14 = (bf16[32,7168]{1,0:T(8,128)(2,1)}, bf16[32,7168]{1,0:T(8,128)(2,1)S(1)}, u32[]{:S(2)}, u32[]{:S(2)}) collective-permute-start(bf16[32,7168]{1,0:T(8,128)(2,1)} %collective-permute-done.9.refs_0_), channel_id=1, source_target_pairs={{0,8},{2,10},{8,16},{10,18},{16,24},{18,26},{24,28},{26,30},{28,20... | collective-permute-start | bytes 1376264 | tf_op jit(solution)/shard_map/ppermute | solution.py:216
  94.1 13.0 %collective-permute-start.15 = (bf16[32,7168]{1,0:T(8,128)(2,1)}, bf16[32,7168]{1,0:T(8,128)(2,1)S(1)}, u32[]{:S(2)}, u32[]{:S(2)}) collective-permute-start(bf16[32,7168]{1,0:T(8,128)(2,1)} %collective-permute-done.12.refs_3_), channel_id=1, source_target_pairs={{0,4},{2,6},{8,0},{10,2},{16,8},{18,10},{24,16},{26,18},{28,24},{3... | collective-permute-start | bytes 1376264 | tf_op jit(solution)/shard_map/ppermute | solution.py:216
  102.3 14.5 %collective-permute-start.24 = (f32[3,64,512]{2,1,0:T(8,128)S(1)}, f32[3,64,512]{2,1,0:T(8,128)}, u32[]{:S(2)}, u32[]{:S(2)}) collective-permute-start(f32[3,64,512]{2,1,0:T(8,128)S(1)} %get-tuple-element.100), channel_id=1, source_target_pairs={{0,2},{2,0},{8,10},{10,8},{16,18},{18,16},{24,26},{26,24},{28,30},... | collective-permute-start | bytes 1179656 | tf_op jit(solution)/shard_map/ppermute | solution.py:216
  102.3 14.0 %collective-permute-start.25 = (bf16[3,64,512]{2,1,0:T(8,128)(2,1)}, bf16[3,64,512]{2,1,0:T(8,128)(2,1)}, u32[]{:S(2)}, u32[]{:S(2)}) collective-permute-start(bf16[3,64,512]{2,1,0:T(8,128)(2,1)} %get-tuple-element.101), channel_id=1, source_target_pairs={{0,1},{1,0},{2,3},{3,2},{4,5},{5,4},{6,7},{7,6},{8,9},{9,8},{10,11... | collective-permute-start | bytes 589832 | tf_op jit(solution)/shard_map/ppermute | solution.py:226
  102.8 13.9 %collective-permute-start.26 = (bf16[3,64,512]{2,1,0:T(8,128)(2,1)S(1)}, bf16[3,64,512]{2,1,0:T(8,128)(2,1)}, u32[]{:S(2)}, u32[]{:S(2)}) collective-permute-start(bf16[3,64,512]{2,1,0:T(8,128)(2,1)S(1)} %get-tuple-element.102), channel_id=1, source_target_pairs={{0,3},{1,2},{2,1},{3,0},{4,7},{5,6},{6,5},{7,4},{8,11},{9,10},{10,... | collective-permute-start | bytes 589832 | tf_op jit(solution)/shard_map/ppermute | solution.py:227
  107.1 3.3 %copy-start.2 = (bf16[8064,512]{1,0:T(8,128)(2,1)S(1)}, bf16[8064,512]{1,0:T(8,128)(2,1)}, u32[]{:S(2)}) copy-start(bf16[8064,512]{1,0:T(8,128)(2,1)} %get-tuple-element.68.refs_10_.refs_4_.table) | copy-start | bytes 24772612
  114.6 3.9 %collective-permute-start.18 = (f32[2,16,64]{2,1,0:T(8,128)S(1)}, f32[2,16,64]{2,1,0:T(8,128)S(1)}, u32[]{:S(2)}, u32[]{:S(2)}) collective-permute-start(f32[2,16,64]{2,1,0:T(8,128)S(1)} %get-tuple-element.91), channel_id=1, source_target_pairs={{0,1},{1,0},{2,3},{3,2},{4,5},{5,4},{6,7},{7,6},{8,9},{9,8},{10,11... | collective-permute-start | bytes 24584 | tf_op jit(solution)/shard_map/ppermute | solution.py:226
  115.2 3.3 %collective-permute-start.19 = (f32[2,16,64]{2,1,0:T(8,128)S(1)}, f32[2,16,64]{2,1,0:T(8,128)S(1)}, u32[]{:S(2)}, u32[]{:S(2)}) collective-permute-start(f32[2,16,64]{2,1,0:T(8,128)S(1)} %get-tuple-element.91), channel_id=1, source_target_pairs={{0,3},{1,2},{2,1},{3,0},{4,7},{5,6},{6,5},{7,4},{8,11},{9,10},{10,... | collective-permute-start | bytes 24584 | tf_op jit(solution)/shard_map/ppermute | solution.py:227
  116.3 1.8 %collective-permute-start.17 = (f32[2,16,64]{2,1,0:T(8,128)S(1)}, f32[2,16,64]{2,1,0:T(8,128)S(1)}, u32[]{:S(2)}, u32[]{:S(2)}) collective-permute-start(f32[2,16,64]{2,1,0:T(8,128)S(1)} %get-tuple-element.90), channel_id=1, source_target_pairs={{0,2},{2,0},{8,10},{10,8},{16,18},{18,16},{24,26},{26,24},{28,30},... | collective-permute-start | bytes 24584 | tf_op jit(solution)/shard_map/ppermute | solution.py:216
  118.5 11.1 %collective-permute-start.20 = (bf16[2,16,64]{2,1,0:T(8,128)(2,1)S(1)}, bf16[2,16,64]{2,1,0:T(8,128)(2,1)S(1)}, u32[]{:S(2)}, u32[]{:S(2)}) collective-permute-start(bf16[2,16,64]{2,1,0:T(8,128)(2,1)S(1)} %get-tuple-element.112), channel_id=1, source_target_pairs={{0,4},{2,6},{4,0},{6,2},{8,12},{10,14},{12,8},{14,10},{16,20},{18,... | collective-permute-start | bytes 12296 | tf_op jit(solution)/shard_map/ppermute | solution.py:374
  119.1 11.1 %collective-permute-start.21 = (bf16[2,16,64]{2,1,0:T(8,128)(2,1)S(1)}, bf16[2,16,64]{2,1,0:T(8,128)(2,1)S(1)}, u32[]{:S(2)}, u32[]{:S(2)}) collective-permute-start(bf16[2,16,64]{2,1,0:T(8,128)(2,1)S(1)} %get-tuple-element.112), channel_id=1, source_target_pairs={{0,8},{2,10},{4,12},{6,14},{8,0},{10,2},{12,4},{14,6},{16,24},{18,... | collective-permute-start | bytes 12296 | tf_op jit(solution)/shard_map/ppermute | solution.py:374
  120.3 9.9 %collective-permute-start.22 = (bf16[2,16,64]{2,1,0:T(8,128)(2,1)S(1)}, bf16[2,16,64]{2,1,0:T(8,128)(2,1)S(1)}, u32[]{:S(2)}, u32[]{:S(2)}) collective-permute-start(bf16[2,16,64]{2,1,0:T(8,128)(2,1)S(1)} %get-tuple-element.112), channel_id=1, source_target_pairs={{0,12},{2,14},{4,8},{6,10},{8,4},{10,6},{12,0},{14,2},{16,28},{18,... | collective-permute-start | bytes 12296 | tf_op jit(solution)/shard_map/ppermute | solution.py:374
  122.1 13.0 %copy-start.10 = (bf16[256,256]{1,0:T(8,128)(2,1)S(1)}, bf16[256,256]{1,0:T(8,128)(2,1)}, u32[]{:S(2)}) copy-start(bf16[256,256]{1,0:T(8,128)(2,1)} %fusion.15) | copy-start | bytes 393220
  122.1 13.5 %copy-start.7 = (bf16[256,1024]{1,0:T(8,128)(2,1)S(1)}, bf16[256,1024]{1,0:T(8,128)(2,1)}, u32[]{:S(2)}) copy-start(bf16[256,1024]{1,0:T(8,128)(2,1)} %compare_convert_fusion) | copy-start | bytes 1572868
  122.1 13.5 %copy-start.9 = (bf16[64,1024]{1,0:T(8,128)(2,1)S(1)}, bf16[64,1024]{1,0:T(8,128)(2,1)}, u32[]{:S(2)}) copy-start(bf16[64,1024]{1,0:T(8,128)(2,1)} %fusion.16) | copy-start | bytes 393220
  128.2 7.1 %collective-permute-start.27 = (f32[1,64,512]{2,1,0:T(8,128)S(1)}, f32[1,64,512]{2,1,0:T(8,128)S(1)}, u32[]{:S(2)}, u32[]{:S(2)}) collective-permute-start(f32[1,64,512]{2,1,0:T(8,128)S(1)} %get-tuple-element.106), channel_id=1, source_target_pairs={{0,2},{2,0},{8,10},{10,8},{16,18},{18,16},{24,26},{26,24},{28,30},... | collective-permute-start | bytes 393224 | tf_op jit(solution)/shard_map/ppermute | solution.py:216
  128.3 7.0 %collective-permute-start.28 = (bf16[1,64,512]{2,1,0:T(8,128)(2,1)S(1)}, bf16[1,64,512]{2,1,0:T(8,128)(2,1)S(1)}, u32[]{:S(2)}, u32[]{:S(2)}) collective-permute-start(bf16[1,64,512]{2,1,0:T(8,128)(2,1)S(1)} %get-tuple-element.107), channel_id=1, source_target_pairs={{0,1},{1,0},{2,3},{3,2},{4,5},{5,4},{6,7},{7,6},{8,9},{9,8},{10,11... | collective-permute-start | bytes 196616 | tf_op jit(solution)/shard_map/ppermute | solution.py:226
  129.7 5.6 %collective-permute-start.29 = (bf16[1,64,512]{2,1,0:T(8,128)(2,1)S(1)}, bf16[1,64,512]{2,1,0:T(8,128)(2,1)S(1)}, u32[]{:S(2)}, u32[]{:S(2)}) collective-permute-start(bf16[1,64,512]{2,1,0:T(8,128)(2,1)S(1)} %get-tuple-element.108), channel_id=1, source_target_pairs={{0,3},{1,2},{2,1},{3,0},{4,7},{5,6},{6,5},{7,4},{8,11},{9,10},{10,... | collective-permute-start | bytes 196616 | tf_op jit(solution)/shard_map/ppermute | solution.py:227
  130.2 4.9 %collective-permute-start.23 = (bf16[8,16,64]{2,1,0:T(8,128)(2,1)S(1)}, bf16[8,16,64]{2,1,0:T(8,128)(2,1)S(1)}, u32[]{:S(2)}, u32[]{:S(2)}) collective-permute-start(bf16[8,16,64]{2,1,0:T(8,128)(2,1)S(1)} %pad_maximum_fusion.3), channel_id=1, source_target_pairs={{0,16},{2,18},{4,20},{6,22},{8,24},{10,26},{12,28},{14,30},{16,0},... | collective-permute-start | bytes 49160 | tf_op jit(solution)/shard_map/ppermute | solution.py:374

commit v7 on v6

--- a/solution.py
+++ b/solution.py
@@ -13,21 +13,65 @@
 SWAP = [(0, 1), (1, 0)]
 
 
-def accumulate(pieces, tables, sums=(), lows=()):
-    depth, width = pieces[0].shape[1], tables[0].shape[1]
-    rank = (tables[0].shape[0] - depth) * width // depth
-    for total in (*sums, *lows):
+def tile_of(depth, most=1024):
+    parts = 1
+    while depth % parts or (depth // parts) % 128 or depth // parts > most:
+        parts += 1
+    return depth // parts
+
+
+def started(sources, places, ready):
+    copies = []
+    for index, (source, place) in enumerate(zip(sources, places)):
+        copies.append(pltpu.make_async_copy(source, place, ready.at[index]))
+        copies[-1].start()
+    return copies
+
+
+def weight_copies(lane, weights, held, ready):
+    tiles, tile = held.shape[1:3]
+    first = pl.multiple_of(lane * tiles * tile, 128)
+    sources = [w.at[pl.ds(first + i * tile, tile)] for i in range(tiles) for w in weights]
+    places = [held.at[which, i] for i in range(tiles) for which in (0, 1)]
+    return started(sources, places, ready)
+
+
+def factor_copies(lane, factors, held, ready):
+    rank, depth = held.shape[1:]
+    first = pl.multiple_of(lane * depth, 128)
+    sources = [f.at[:, pl.ds(first, depth)] for f in factors]
+    return started(sources, [held.at[which] for which in (0, 1)], ready)
+
+
+def weight_products(pieces, copies, held, sums):
+    tiles, tile = held.shape[1:3]
+    for total in sums:
         total[...] = jnp.zeros_like(total)
-    for index in range(depth // width):
-        here = slice(index * width, (index + 1) * width)
+    for index in range(tiles):
+        here = slice(index * tile, (index + 1) * tile)
         rows = jnp.concatenate([piece[:, here] for piece in pieces], axis=0)
-        for table, total in zip(tables, sums):
-            total[...] += jnp.dot(rows, table[here, :], preferred_element_type=jnp.float32)
-        for table, total in zip(tables, lows):
-            block = table[depth + index * rank : depth + (index + 1) * rank, :]
-            total[...] += lax.dot_general(
-                rows, block, (((1,), (1,)), ((), ())), preferred_element_type=jnp.float32
-            )
+        for which, total in enumerate(sums):
+            copies[2 * index + which].wait()
+            total[...] += jnp.dot(rows, held[which, index], preferred_element_type=jnp.float32)
+
+
+def factor_products(pieces, copies, held, low):
+    rank, depth = held.shape[1:]
+    tile = tile_of(depth)
+    low[...] = jnp.zeros_like(low)
+    for copy in copies:
+        copy.wait()
+
+    def step(index, carry):
+        here = pl.ds(pl.multiple_of(index * tile, 128), tile)
+        rows = jnp.concatenate([piece[:, here] for piece in pieces], axis=0)
+        both = jnp.concatenate([held[which, :, here] for which in (0, 1)], axis=0)
+        low[...] += lax.dot_general(
+            rows, both, (((1,), (1,)), ((), ())), preferred_element_type=jnp.float32
+        )
+        return carry
+
+    lax.fori_loop(0, depth // tile, step, 0)
 
 
 def in_lanes(lane, total, index, height):
@@ -43,15 +87,20 @@
 
 
 def early_kernel(count, facts, *refs):
-    pieces, tables, choices = refs[:count], refs[count : count + 2], refs[count + 2]
-    base, base_sib, compact = refs[count + 3 : count + 6]
-    sums, lows = refs[count + 6 : count + 8], refs[count + 8 :]
-    accumulate(pieces, tables, sums, lows)
-    height = pieces[0].shape[0]
+    pieces, refs = refs[:count], refs[count:]
+    weights, factors, choices = refs[:2], refs[2:4], refs[4]
+    (base, base_sib, compact), refs = refs[5:8], refs[8:]
+    sums, low, held, ready, held_low, ready_low = refs[:2], *refs[2:]
+    rank = held_low.shape[1]
+    in_flight = weight_copies(facts[0], weights, held, ready)
+    in_flight_low = factor_copies(facts[0], factors, held_low, ready_low)
+    weight_products(pieces, in_flight, held, sums)
+    factor_products(pieces, in_flight_low, held_low, low)
+    height = base.shape[1] // 2
     for which, (out, total) in enumerate(zip((base, base_sib), sums)):
-        for index in range(count // 2):
+        for index in range(out.shape[0]):
             out[index] = in_lanes(facts[0], total, index, height)
-        compact[which] = compacted(choices[which], lows[which][...])
+        compact[which] = compacted(choices[which], low[:, which * rank : (which + 1) * rank])
 
 
 def share(flag, near, away, outs, pair):
@@ -63,52 +112,83 @@
     to_both[pair] = jnp.where(flag == 1, away_sib, near_sib).astype(to_both.dtype)
 
 
-def middle_kernel(count, facts, *refs):
-    pieces, tables = refs[:count], refs[count : count + 2]
-    choices, compact_in, base, base_sib = refs[count + 2 : count + 6]
-    outs, compact = refs[count + 6 : count + 10], refs[count + 10]
-    sums, lows = refs[count + 11 : count + 13], refs[count + 13 :]
-    accumulate(pieces, tables, sums, lows)
-    height = pieces[0].shape[0]
-    fresh = [[in_lanes(facts[0], total, index, height) for total in sums] for index in (0, 1)]
-    pairs = outs[0].shape[0]
+def middle_kernel(facts, piece, other, *refs):
+    weights, factors = refs[:2], refs[2:4]
+    (choices, compact_in, base, base_sib), refs = refs[4:8], refs[8:]
+    outs, compact, refs = refs[:4], refs[4], refs[5:]
+    sums, low, held, ready, held_low, ready_low = refs[:2], *refs[2:]
+    rank = held_low.shape[1]
+    in_flight = weight_copies(facts[0], weights, held, ready)
+    in_flight_low = factor_copies(facts[0], factors, held_low, ready_low)
+    weight_products((piece, other), in_flight, held, sums)
+    factor_products((piece, other), in_flight_low, held_low, low)
+    pairs, group = outs[0].shape[:2]
+    fresh = [[in_lanes(facts[0], total, index, group // 2) for total in sums] for index in (0, 1)]
     for pair in range(pairs):
-        step = pair + 1
+        step, back = pair + 1, pairs - pair
         near = fresh[1] if step == pairs else (base[2 * step], base_sib[2 * step])
-        back = pairs + 1 - step
         away = fresh[0] if back == pairs else (base[2 * back - 1], base_sib[2 * back - 1])
         share(facts[2 + step], near, away, outs, pair)
-    for which, total in enumerate(lows):
-        compact[which] = compact_in[which] + compacted(choices[which], total[...])
-
-
-def low_kernel(facts, piece, other, table, table_sib, choices, compact_in, kept, sent, *lows):
-    accumulate((piece, other), (table, table_sib), (), lows)
-    half = kept.shape[1]
-    for which, total in enumerate(lows):
-        compact = compact_in[which] + compacted(choices[which], total[...])
+    for which in (0, 1):
+        compact[which] = compact_in[which] + compacted(
+            choices[which], low[:, which * rank : (which + 1) * rank]
+        )
+
+
+def low_kernel(facts, piece, other, *refs):
+    factors, (choices, compact_in, kept, sent, low, held, ready) = refs[:2], refs[2:]
+    rank, half = held.shape[1], kept.shape[1]
+    factor_products((piece, other), factor_copies(facts[0], factors, held, ready), held, low)
+    for which in (0, 1):
+        compact = compact_in[which] + compacted(
+            choices[which], low[:, which * rank : (which + 1) * rank]
+        )
         kept[which] = jnp.where(facts[1] == 0, compact[:half], compact[half:])
         sent[which] = jnp.where(facts[1] == 0, compact[half:], compact[:half])
 
 
-def last_kernel(facts, piece, other, table, table_sib, base, base_sib, *refs):
-    outs, sums = refs[:4], refs[4:]
-    accumulate((piece, other), (table, table_sib), sums)
+def last_kernel(facts, piece, other, *refs):
+    weights, (base, base_sib), refs = refs[:2], refs[2:4], refs[4:]
+    outs, sums, (held, ready) = refs[:4], refs[4:6], refs[6:]
+    weight_products((piece, other), weight_copies(facts[0], weights, held, ready), held, sums)
     away = [in_lanes(facts[0], total, 0, piece.shape[0]) for total in sums]
     share(facts[2], (base[0], base_sib[0]), away, outs, 0)
 
 
-def kernel_call(kernel, facts, arrays, shapes, scratch, flops):
-    in_vmem = pl.BlockSpec(memory_space=pltpu.VMEM)
+def kernel_call(kernel, facts, rows, weights, factors, others, shapes):
+    in_vmem, anywhere = pl.BlockSpec(memory_space=pltpu.VMEM), pl.BlockSpec(memory_space=pl.ANY)
+    depth, total = rows[0].shape[1], sum(values.shape[0] for values in rows)
+    tile = tile_of(depth)
+    scratch, columns = [], 0
+    if weights:
+        width = weights[0].shape[1]
+        columns += 2 * width
+        scratch += [pltpu.VMEM((total, width), jnp.float32)] * 2
+    if factors:
+        rank = factors[0].shape[0]
+        columns += 2 * rank
+        scratch += [pltpu.VMEM((total, 2 * rank), jnp.float32)]
+    if weights:
+        scratch += [pltpu.VMEM((2, depth // tile, tile, width), jnp.bfloat16)]
+        scratch += [pltpu.SemaphoreType.DMA((2 * depth // tile,))]
+    if factors:
+        scratch += [pltpu.VMEM((2, rank, depth), jnp.bfloat16), pltpu.SemaphoreType.DMA((2,))]
     return pl.pallas_call(
         kernel,
-        in_specs=[pl.BlockSpec(memory_space=pltpu.SMEM)] + [in_vmem] * len(arrays),
+        in_specs=[pl.BlockSpec(memory_space=pltpu.SMEM)]
+        + [in_vmem] * len(rows)
+        + [anywhere] * (len(weights) + len(factors))
+        + [in_vmem] * len(others),
         out_specs=[in_vmem] * len(shapes),
         out_shape=[jax.ShapeDtypeStruct(shape, kind) for shape, kind in shapes],
-        scratch_shapes=[pltpu.VMEM(shape, jnp.float32) for shape in scratch for _ in (0, 1)],
-        compiler_params=pltpu.CompilerParams(vmem_limit_bytes=16 * 2**20),
-        cost_estimate=pl.CostEstimate(flops=flops, bytes_accessed=flops // 64, transcendentals=0),
-    )(facts, *arrays)
+        scratch_shapes=scratch,
+        compiler_params=pltpu.CompilerParams(vmem_limit_bytes=40 * 2**20),
+        cost_estimate=pl.CostEstimate(
+            flops=total * depth * columns // 32,
+            bytes_accessed=depth * columns // 16,
+            transcendentals=0,
+        ),
+    )(facts, *rows, *weights, *factors, *others)
 
 
 def hidden_of(gate, up):
@@ -229,32 +309,24 @@
 
     keep = hidden_of(half_of(gate_activation, side, 1), half_of(up_activation, side, 1))
     give = hidden_of(half_of(gate_activation, 1 - side, 1), half_of(up_activation, 1 - side, 1))
-    right = [send(keep, 1), send(give, 1, 1)]
-    left = [send(keep, -1), send(give, -1, 1)]
-    twin = send(give, 0, 1)
-
-    def joined(which):
-        first = half_of(first_factor_table[0], which, 1).reshape(rank, depth // width, width)
-        first = jnp.swapaxes(first, 0, 1).reshape(-1, width)
-        return jnp.concatenate([half_of(down_base_weight, which, 0), first], axis=0)
-
-    own_table, sib_table = joined(side), joined(1 - side)
-    own_table, sib_table, twin, right, left = lax.optimization_barrier(
-        (own_table, sib_table, twin, right, left)
-    )
-    sib_table = send(sib_table, 0, 1)
-    home_late, row_adapter_index, second_factor_table, sib_table = lax.optimization_barrier(
-        (home, row_adapter_index, second_factor_table, sib_table)
-    )
-    tables = [own_table, sib_table]
-
-    pieces = [keep, twin] + right + left
+    block = jnp.concatenate([keep, send(give, 0, 1)], axis=0)
+    right, left = send(block, 1), send(block, -1)
+
+    weight, first, block = lax.optimization_barrier(
+        (down_base_weight, first_factor_table[0], block)
+    )
+    weights = (weight, send(weight, 0, 1))
+    factors = (first, send(first, 0, 1))
+    home_late, row_adapter_index, second_factor_table, weights = lax.optimization_barrier(
+        (home, row_adapter_index, second_factor_table, weights)
+    )
+
+    pieces = [block, right, left]
     for step in range(2, steps + 1):
-        right = [send(block, 1) for block in right]
-        left = [send(block, -1) for block in left]
+        right, left = send(right, 1), send(left, -1)
         if step < steps:
             right, left = lax.optimization_barrier((right, left))
-            pieces += right + left
+            pieces += [right, left]
 
     row = lax.dynamic_index_in_dim(
         jnp.asarray(np.array(table, np.int32)), home_late, 0, keepdims=False
@@ -283,7 +355,7 @@
             for slot in (home_late, jnp.bitwise_xor(home_late, 1))
         ]
     )
-    early_rows = len(pieces) * row_count
+    early_rows = len(pieces) * group_rows
     middle_rows = early_rows + 4 * row_count
     choices = [
         chosen[:, :, :early_rows],
@@ -313,58 +385,46 @@
         [values.reshape(owners * piece, width) for values in (second_factor_table, other)], axis=0
     )
 
-    def flops(rows, columns):
-        return rows * depth * columns // 16
-
-    count = len(pieces)
+    compact_shape = ((2, owners * MOST, rank), f32)
     early = kernel_call(
-        functools.partial(early_kernel, count),
+        functools.partial(early_kernel, len(pieces)),
         facts,
-        (*pieces, *tables, choices[0]),
-        [((count // 2, group_rows, width), f32)] * 2 + [((2, owners * MOST, rank), f32)],
-        [(early_rows, width), (early_rows, rank)],
-        flops(early_rows, width + rank),
+        pieces,
+        weights,
+        factors,
+        (choices[0],),
+        [((len(pieces), group_rows, width), f32)] * 2 + [compact_shape],
     )
     ready = (facts, spots, mask, copies, choices, places)
     right, left, early, ready = lax.optimization_barrier((right, left, early, ready))
     facts, spots, mask, copies, choices, places = ready
 
-    last = [send(right[0], 1), send(left[1], -1)]
+    last = [send(right[:row_count], 1), send(left[row_count:], -1)]
 
     def shares(pairs):
         shape = (pairs, group_rows, width)
         return [(shape, f32)] * 2 + [(shape, bf16)] * 2
 
-    *middle, compact = kernel_call(
-        functools.partial(middle_kernel, 4),
+    kept_more, *more, compact = kernel_call(
+        middle_kernel,
         facts,
-        (*right, *left, *tables, choices[1], early[2], early[0], early[1]),
-        shares(far - 1) + [((2, owners * MOST, rank), f32)],
-        [(4 * row_count, width), (4 * row_count, rank)],
-        flops(4 * row_count, width + rank),
-    )
-    kept_more = middle[0]
-    got_more = to_three(*middle[1:])
+        (right, left),
+        weights,
+        factors,
+        (choices[1], early[2], early[0], early[1]),
+        shares(far - 1) + [compact_shape],
+    )
+    got_more = to_three(*more)
     last, compact, second = lax.optimization_barrier((last, compact, second))
 
     kept, sent = kernel_call(
-        low_kernel,
-        facts,
-        (*last, *tables, choices[2], compact),
-        [((2, half, rank), f32)] * 2,
-        [(group_rows, rank)],
-        flops(group_rows, rank),
+        low_kernel, facts, last, (), factors, (choices[2], compact), [((2, half, rank), f32)] * 2
     )
     got = to_three(kept, sent, sent)
     got, last = lax.optimization_barrier((got, last))
 
     kept_one, *one = kernel_call(
-        last_kernel,
-        facts,
-        (*last, *tables, early[0], early[1]),
-        shares(1),
-        [(group_rows, width)],
-        flops(group_rows, width),
+        last_kernel, facts, last, weights, (), (early[0], early[1]), shares(1)
     )
     got_one = to_three(*one)
 

time: 139 us -> 122 us (0.88)
  local copies, waits for them, and re-layouts: 32 us -> 6.35 us
  waiting for transfers between devices: 23.4 us -> 49 us
  other arithmetic: 20.8 us -> 9.78 us
  starting transfers between devices: 29.3 us -> 23.4 us
  Pallas kernels: 29.6 us -> 31.7 us
    ppermute x19 -> x14, waiting for transfers between devices: 20.7 us -> 45.5 us  [send(): return lax.ppermute(value, 'wide', moved(shift, cross))]
    dynamic_slice x3 -> x0, local copies, waits for them, and re-layouts: 11.8 us -> none  [the longest x2 11.7 us: half_of(): return lax.dynamic_slice_in_dim(value, which * depth, depth, axis)]
    concatenate x1, other arithmetic: 11.3 us -> 0.06 us  [ringed(): block = jnp.concatenate([keep, send(give, 0, 1)], axis=0)]
    unnamed x29 -> x25, local copies, waits for them, and re-layouts: 8.79 us -> 0.82 us
    ppermute x19 -> x14, starting transfers between devices: 16.2 us -> 10.4 us  [send(): return lax.ppermute(value, 'wide', moved(shift, cross))]
    reshape x2 -> x0, local copies, waits for them, and re-layouts: 5.18 us -> none  [joined(): half_of(first_factor_table[0], which, 1)]
    transpose x2 -> x0, local copies, waits for them, and re-layouts: 4.41 us -> none  [joined(): first = jnp.swapaxes(first, 0, 1).reshape(-1, width)]
    slice x0 -> x2, local copies, waits for them, and re-layouts: none -> 3.65 us  [ringed(): last = [send(right[:row_count], 1), send(left[row_count:], -1)]]
  transfers between devices with their start and end apart: 30 -> 25, of which waited for: 5 -> 9; matrix products, arithmetic and copies ran while one was open for 30% -> 11% of each run, Pallas kernels for 21% -> 26%
where the time goes in v7:
time: 122 us
  waiting for transfers between devices  49 us (40%)
  Pallas kernels  31.7 us (26%)
  starting transfers between devices  23.4 us (19%)
  other arithmetic  9.78 us (8%)
  local copies, waits for them, and re-layouts  6.35 us (5%)
  matrix products  1.42 us (1%)
    ppermute x14, waiting for transfers between devices, send(): return lax.ppermute(value, 'wide', moved(shift, cross))  45.5 us
    pallas_call x4, Pallas kernels, kernel_call(): pl.pallas_call(kernel, in_specs=[pl.BlockSpec(memory_space=pltpu.SMEM)] +...  31.7 us
    ppermute x14, starting transfers between devices, send(): return lax.ppermute(value, 'wide', moved(shift, cross))  10.4 us
    ppermute x4, starting transfers between devices, from_node(): lax.ppermute(value, 'wide', [(w, w ^ 2 * gap) for w in range(owners)])  6.15 us
    ppermute x3, starting transfers between devices, to_three(): lax.ppermute(to_mp, INNER, SWAP)  4.4 us
    slice x2, local copies, waits for them, and re-layouts, ringed(): last = [send(right[:row_count], 1), send(left[row_count:], -1)]  3.65 us
  transfers between devices with their start and end apart: 25, of which 9 were waited for; matrix products, arithmetic and copies ran while one was open for 11% of the time, Pallas kernels for 26%

profile of v7, /device:TPU:0, one launch (start us, length us, event | category | flops | bytes accessed | tf_op | source)
XLA Modules:
  0.0 122.0 jit_solution(17055649063754591579)
XLA Ops:
  0.0 2.1 %fusion.11 = (bf16[32,7168]{1,0:T(8,128)(2,1)S(1)}, bf16[32,7168]{1,0:T(8,128)(2,1)S(1)}) fusion(bf16[32,14336]{1,0:T(8,128)(2,1)} %param.9, s32[]{:T(128)S(6)} %select_n.115, bf16[32,14336]{1,0:T(8,128)(2,1)} %param.8, s32[]{:T(128)S(6)} %select_n.116), kind=kLoop, calls=%fused_computation.21 | loop fusion | flops 3670016 | bytes 2752520 | tf_op jit(solution)/shard_map/convert_element_type | solution.py:195
  2.1 0.5 collective-permute-start
  2.6 1.4 %collective-permute-done = bf16[32,7168]{1,0:T(8,128)(2,1)S(1)} collective-permute-done((bf16[32,7168]{1,0:T(8,128)(2,1)S(1)}, bf16[32,7168]{1,0:T(8,128)(2,1)S(1)}, u32[]{:S(2)}, u32[]{:S(2)}) %collective-permute-start) | collective-permute-done | bytes 458784 | tf_op jit(solution)/shard_map/ppermute | solution.py:296
  4.1 0.4 collective-permute-start.7
  4.6 2.7 %collective-permute-start.1 = (bf16[64,7168]{1,0:T(8,128)(2,1)S(1)}, bf16[64,7168]{1,0:T(8,128)(2,1)}, u32[]{:S(2)}, u32[]{:S(2)}) collective-permute-start(bf16[64,7168]{1,0:T(8,128)(2,1)S(1)} %pad_maximum_fusion.1.refs_0_), channel_id=1, source_target_pairs={{0,8},{2,10},{8,16},{10,18},{16,24},{18,26},{24,28},{26,30},{28,20... | collective-permute-start | bytes 2752520 | tf_op jit(solution)/shard_map/ppermute | solution.py:296
  7.3 20.9 %collective-permute-done.1.refs_1_ = bf16[64,7168]{1,0:T(8,128)(2,1)} collective-permute-done((bf16[64,7168]{1,0:T(8,128)(2,1)S(1)}, bf16[64,7168]{1,0:T(8,128)(2,1)}, u32[]{:S(2)}, u32[]{:S(2)}) %collective-permute-start.1) | collective-permute-done | bytes 917536 | tf_op jit(solution)/shard_map/ppermute | solution.py:296
  28.2 1.8 %collective-permute-start.2 = (bf16[64,7168]{1,0:T(8,128)(2,1)}, bf16[64,7168]{1,0:T(8,128)(2,1)}, u32[]{:S(2)}, u32[]{:S(2)}) collective-permute-start(bf16[64,7168]{1,0:T(8,128)(2,1)} %collective-permute-done.1.refs_1_), channel_id=1, source_target_pairs={{0,8},{2,10},{8,16},{10,18},{16,24},{18,26},{24,28},{26,30},{28,20... | collective-permute-start | bytes 2752520 | tf_op jit(solution)/shard_map/ppermute | solution.py:296
  30.0 0.2 collective-permute-start.4
  30.3 0.7 fusion.16
  31.0 19.6 %collective-permute-done.2.refs_3_ = bf16[64,7168]{1,0:T(8,128)(2,1)} collective-permute-done((bf16[64,7168]{1,0:T(8,128)(2,1)}, bf16[64,7168]{1,0:T(8,128)(2,1)}, u32[]{:S(2)}, u32[]{:S(2)}) %collective-permute-start.2) | collective-permute-done | bytes 917536 | tf_op jit(solution)/shard_map/ppermute | solution.py:296
  50.6 1.3 %collective-permute-done.4.refs_4_ = bf16[64,7168]{1,0:T(8,128)(2,1)} collective-permute-done((bf16[64,7168]{1,0:T(8,128)(2,1)}, bf16[64,7168]{1,0:T(8,128)(2,1)}, u32[]{:S(2)}, u32[]{:S(2)}) %collective-permute-start.4) | collective-permute-done | bytes 917536 | tf_op jit(solution)/shard_map/ppermute | solution.py:296
  51.9 1.6 %collective-permute-start.5 = (bf16[64,7168]{1,0:T(8,128)(2,1)}, bf16[64,7168]{1,0:T(8,128)(2,1)}, u32[]{:S(2)}, u32[]{:S(2)}) collective-permute-start(bf16[64,7168]{1,0:T(8,128)(2,1)} %collective-permute-done.2.refs_3_), channel_id=1, source_target_pairs={{0,8},{2,10},{8,16},{10,18},{16,24},{18,26},{24,28},{26,30},{28,20... | collective-permute-start | bytes 2752520 | tf_op jit(solution)/shard_map/ppermute | solution.py:296
  53.5 0.4 collective-permute-start.6
  53.9 1.5 %collective-permute-start.11 = (bf16[16,32,512]{2,1,0:T(8,128)(2,1)}, bf16[16,32,512]{2,1,0:T(8,128)(2,1)}, u32[]{:S(2)}, u32[]{:S(2)}) collective-permute-start(bf16[16,32,512]{2,1,0:T(8,128)(2,1)} %param.12), channel_id=1, source_target_pairs={{0,1},{1,0},{2,3},{3,2},{4,5},{5,4},{6,7},{7,6},{8,9},{9,8},{10,11... | collective-permute-start | bytes 1572872 | tf_op jit(solution)/shard_map/ppermute | solution.py:383
  55.4 0.7 constant_dynamic-slice_fusion.2
  56.3 0.5 convert_reduce_fusion
  56.9 0.1 select_reduce_fusion
  57.8 12.1 %shard_map.82 = (f32[5,64,512]{2,1,0:T(8,128)S(1)}, f32[5,64,512]{2,1,0:T(8,128)S(1)}, f32[2,32,64]{2,1,0:T(8,128)S(1)}) custom-call(s32[6]{0:T(128)S(1)} %pad_add_fusion.facts, bf16[64,7168]{1,0:T(8,128)(2,1)S(1)} %pad_maximum_fusion.1.refs_0_, bf16[64,7168]{1,0:T(8,128)(2,1)} %collective-permute-done.1.refs_1_, ...), custom_call_target="tpu_custom_call" | custom-call | flops 82575360 | bytes 516096 | tf_op jit(solution)/shard_map/pallas_call | solution.py:176
  69.9 0.9 fusion.15
  70.9 1.0 compare_convert_fusion
  71.8 1.0 collective-permute-done.5.piece
  72.8 1.3 %collective-permute-done.6.other = bf16[64,7168]{1,0:T(8,128)(2,1)} collective-permute-done((bf16[64,7168]{1,0:T(8,128)(2,1)}, bf16[64,7168]{1,0:T(8,128)(2,1)}, u32[]{:S(2)}, u32[]{:S(2)}) %collective-permute-start.6) | collective-permute-done | bytes 917536 | tf_op jit(solution)/shard_map/ppermute | solution.py:296
  74.1 1.8 %slice.65 = bf16[32,7168]{1,0:T(8,128)(2,1)} slice(bf16[64,7168]{1,0:T(8,128)(2,1)} %collective-permute-done.6.other), slice={[32:64], [0:7168]} | slice | bytes 917504 | tf_op jit(solution)/shard_map/slice | solution.py:402
  75.9 0.4 collective-permute-start.10
  76.4 1.8 %slice.64 = bf16[32,7168]{1,0:T(8,128)(2,1)} slice(bf16[64,7168]{1,0:T(8,128)(2,1)} %collective-permute-done.5.piece), slice={[0:32], [0:7168]} | slice | bytes 917504 | tf_op jit(solution)/shard_map/slice | solution.py:402
  78.2 1.6 %collective-permute-start.9 = (bf16[32,7168]{1,0:T(8,128)(2,1)}, bf16[32,7168]{1,0:T(8,128)(2,1)S(1)}, u32[]{:S(2)}, u32[]{:S(2)}) collective-permute-start(bf16[32,7168]{1,0:T(8,128)(2,1)} %slice.64), channel_id=1, source_target_pairs={{0,8},{2,10},{8,16},{10,18},{16,24},{18,26},{24,28},{26,30},{28,20... | collective-permute-start | bytes 1376264 | tf_op jit(solution)/shard_map/ppermute | solution.py:296
  79.8 9.9 %shard_map.83 = (f32[3,64,512]{2,1,0:T(8,128)S(1)}, f32[3,64,512]{2,1,0:T(8,128)}, bf16[3,64,512]{2,1,0:T(8,128)(2,1)}, bf16[3,64,512]{2,1,0:T(8,128)(2,1)}, f32[2,32,64]{2,1,0:T(8,128)S(1)}) custom-call(s32[6]{0:T(128)S(1)} %pad_add_fusion.facts, bf16[64,7168]{1,0:T(8,128)(2,1)} %collective-permute-done.5.piece, ...), custom_call_target="tpu_custom_call" | custom-call | flops 33030144 | bytes 516096 | tf_op jit(solution)/shard_map/pallas_call | solution.py:176
  89.7 0.8 copy-done.3
  90.5 1.5 %collective-permute-start.20 = (bf16[3,64,512]{2,1,0:T(8,128)(2,1)}, bf16[3,64,512]{2,1,0:T(8,128)(2,1)}, u32[]{:S(2)}, u32[]{:S(2)}) collective-permute-start(bf16[3,64,512]{2,1,0:T(8,128)(2,1)} %get-tuple-element.87), channel_id=1, source_target_pairs={{0,1},{1,0},{2,3},{3,2},{4,5},{5,4},{6,7},{7,6},{8,9},{9,8},{10,11... | collective-permute-start | bytes 589832 | tf_op jit(solution)/shard_map/ppermute | solution.py:306
  92.0 0.4 collective-permute-start.21
  93.0 2.3 %pad_maximum_fusion = bf16[1024,512]{1,0:T(8,128)(2,1)} fusion(bf16[512,512]{1,0:T(8,128)(2,1)} %bitcast.8, bf16[512,512]{1,0:T(8,128)(2,1)} %bitcast.7), kind=kLoop, calls=%fused_computation.9 | loop fusion | flops 2097152 | bytes 2097152 | tf_op jit(solution)/shard_map/concatenate | solution.py:384
  95.3 3.5 %shard_map.84 = (f32[2,16,64]{2,1,0:T(8,128)S(1)}, f32[2,16,64]{2,1,0:T(8,128)S(1)}) custom-call(s32[6]{0:T(128)S(1)} %pad_add_fusion.facts, bf16[32,7168]{1,0:T(8,128)(2,1)S(1)} %collective-permute-done.9.piece, bf16[32,7168]{1,0:T(8,128)(2,1)S(1)} %collective-permute-done.10.other, bf16[64,14336]{1,0:T(8,128)(2,1)S(1)} %bitcast.57, ...), custom_call_target="tpu_custom_call" | custom-call | flops 1835008 | bytes 57344 | tf_op jit(solution)/shard_map/pallas_call | solution.py:176
  98.8 1.6 %collective-permute-start.13 = (f32[2,16,64]{2,1,0:T(8,128)S(1)}, f32[2,16,64]{2,1,0:T(8,128)S(1)}, u32[]{:S(2)}, u32[]{:S(2)}) collective-permute-start(f32[2,16,64]{2,1,0:T(8,128)S(1)} %get-tuple-element.77), channel_id=1, source_target_pairs={{0,1},{1,0},{2,3},{3,2},{4,5},{5,4},{6,7},{7,6},{8,9},{9,8},{10,11... | collective-permute-start | bytes 24584 | tf_op jit(solution)/shard_map/ppermute | solution.py:306
  100.5 0.5 collective-permute-start.12
  101.0 0.9 collective-permute-done.21
  102.0 1.3 %convert_add_fusion = f32[3,64,512]{2,1,0:T(8,128)S(1)} fusion(bf16[3,64,512]{2,1,0:T(8,128)(2,1)} %collective-permute-done.21, bf16[3,64,512]{2,1,0:T(8,128)(2,1)} %collective-permute-done.20, f32[3,64,512]{2,1,0:T(8,128)S(1)} %copy-done.4, f32[3,64,512]{2,1,0:T(8,128)} %collective-permute-done.19), kind=kLoop, calls=%fused_computation.29 | loop fusion | flops 491520 | bytes 1572864 | tf_op jit(solution)/shard_map/add | solution.py:442
  103.3 0.3 collective-permute-done.14
  103.6 0.5 collective-permute-start.15
  104.1 1.2 collective-permute-start.16
  105.3 1.8 %collective-permute-start.17 = (bf16[2,16,64]{2,1,0:T(8,128)(2,1)S(1)}, bf16[2,16,64]{2,1,0:T(8,128)(2,1)S(1)}, u32[]{:S(2)}, u32[]{:S(2)}) collective-permute-start(bf16[2,16,64]{2,1,0:T(8,128)(2,1)S(1)} %get-tuple-element.98), channel_id=1, source_target_pairs={{0,12},{2,14},{4,8},{6,10},{8,4},{10,6},{12,0},{14,2},{16,28},{18,... | collective-permute-start | bytes 12296 | tf_op jit(solution)/shard_map/ppermute | solution.py:434
  107.2 6.2 %shard_map.85 = (f32[1,64,512]{2,1,0:T(8,128)S(1)}, f32[1,64,512]{2,1,0:T(8,128)S(1)}, bf16[1,64,512]{2,1,0:T(8,128)(2,1)S(1)}, bf16[1,64,512]{2,1,0:T(8,128)(2,1)S(1)}) custom-call(s32[6]{0:T(128)S(1)} %pad_add_fusion.facts, bf16[32,7168]{1,0:T(8,128)(2,1)S(1)} %collective-permute-done.9.piece, bf16[32,7168]{1,0:T(8,128)(2,1)S(1)} %collective-permute-done.10.other, ...), custom_call_target="tpu_custom_call" | custom-call | flops 14680064 | bytes 458752 | tf_op jit(solution)/shard_map/pallas_call | solution.py:176
  113.5 1.3 %collective-permute-start.23 = (bf16[1,64,512]{2,1,0:T(8,128)(2,1)S(1)}, bf16[1,64,512]{2,1,0:T(8,128)(2,1)S(1)}, u32[]{:S(2)}, u32[]{:S(2)}) collective-permute-start(bf16[1,64,512]{2,1,0:T(8,128)(2,1)S(1)} %get-tuple-element.93), channel_id=1, source_target_pairs={{0,1},{1,0},{2,3},{3,2},{4,5},{5,4},{6,7},{7,6},{8,9},{9,8},{10,11... | collective-permute-start | bytes 196616 | tf_op jit(solution)/shard_map/ppermute | solution.py:306
  114.8 0.5 collective-permute-start.24
  115.4 2.6 %collective-permute-start.18 = (bf16[8,16,64]{2,1,0:T(8,128)(2,1)S(1)}, bf16[8,16,64]{2,1,0:T(8,128)(2,1)S(1)}, u32[]{:S(2)}, u32[]{:S(2)}) collective-permute-start(bf16[8,16,64]{2,1,0:T(8,128)(2,1)S(1)} %pad_maximum_fusion.2), channel_id=1, source_target_pairs={{0,16},{2,18},{4,20},{6,22},{8,24},{10,26},{12,28},{14,30},{16,0},... | collective-permute-start | bytes 49160 | tf_op jit(solution)/shard_map/ppermute | solution.py:434
  118.0 2.3 %collective-permute-done.18 = bf16[8,16,64]{2,1,0:T(8,128)(2,1)S(1)} collective-permute-done((bf16[8,16,64]{2,1,0:T(8,128)(2,1)S(1)}, bf16[8,16,64]{2,1,0:T(8,128)(2,1)S(1)}, u32[]{:S(2)}, u32[]{:S(2)}) %collective-permute-start.18) | collective-permute-done | bytes 16416 | tf_op jit(solution)/shard_map/ppermute | solution.py:434
  120.3 0.2 convolution_convert_fusion.1
  120.5 0.2 fusion.12
  120.8 1.3 %fusion.1 = bf16[256,512]{1,0:T(8,128)(2,1)} fusion(f32[256,512]{1,0:T(8,128)S(1)} %fusion.12, bf16[1024,512]{1,0:T(8,128)(2,1)S(1)} %copy-done.5, bf16[256,1024]{1,0:T(8,128)(2,1)S(1)} %copy-done.6, bf16[256,64]{1,0:T(8,128)(2,1)S(1)} %convolution_convert_fusion.1, bf16[64,1024]{1,0:T(8,128)(2,1)S(1)} %copy-done.7), kind=kOutput, calls=%fused_computation.3 | convolution fusion | flops 302776320 | bytes 2523136 | tf_op jit(solution)/shard_map/dot_general | solution.py:448
  (86 shorter events, 2.3 us)
Async XLA Ops:
  0.0 31.0 %copy-start = (bf16[1,64,14336]{2,1,0:T(8,128)(2,1)S(1)}, bf16[1,64,14336]{2,1,0:T(8,128)(2,1)}, u32[]{:S(2)}) copy-start(bf16[1,64,14336]{2,1,0:T(8,128)(2,1)} %param.11) | copy-start | bytes 5505028
  0.0 56.1 %copy-start.9 = (s32[512,1]{0,1:T(1,128)S(1)}, s32[512,1]{0,1:T(1,128)}, u32[]{:S(2)}) copy-start(s32[512,1]{0,1:T(1,128)} %param.13) | copy-start | bytes 6148
  0.0 56.1 %copy-start.10 = (s32[16]{0:T(128)S(1)}, s32[16]{0:T(128)}, u32[]{:S(2)}) copy-start(s32[16]{0:T(128)} %param.14) | copy-start | bytes 196
  2.1 2.0 %collective-permute-start = (bf16[32,7168]{1,0:T(8,128)(2,1)S(1)}, bf16[32,7168]{1,0:T(8,128)(2,1)S(1)}, u32[]{:S(2)}, u32[]{:S(2)}) collective-permute-start(bf16[32,7168]{1,0:T(8,128)(2,1)S(1)} %get-tuple-element.100), channel_id=1, source_target_pairs={{0,2},{2,0},{8,10},{10,8},{16,18},{18,16},{24,26},{26,24},{28,30},... | collective-permute-start | bytes 1376264 | tf_op jit(solution)/shard_map/ppermute | solution.py:296
  4.1 49.8 %collective-permute-start.7 = (bf16[14336,512]{1,0:T(8,128)(2,1)}, bf16[14336,512]{1,0:T(8,128)(2,1)}, u32[]{:S(2)}, u32[]{:S(2)}) collective-permute-start(bf16[14336,512]{1,0:T(8,128)(2,1)} %refs_0_.1), channel_id=1, source_target_pairs={{0,2},{2,0},{8,10},{10,8},{16,18},{18,16},{24,26},{26,24},{28,30},... | collective-permute-start | bytes 44040200 | tf_op jit(solution)/shard_map/ppermute | solution.py:296
  4.6 23.6 %collective-permute-start.1 = (bf16[64,7168]{1,0:T(8,128)(2,1)S(1)}, bf16[64,7168]{1,0:T(8,128)(2,1)}, u32[]{:S(2)}, u32[]{:S(2)}) collective-permute-start(bf16[64,7168]{1,0:T(8,128)(2,1)S(1)} %pad_maximum_fusion.1.refs_0_), channel_id=1, source_target_pairs={{0,8},{2,10},{8,16},{10,18},{16,24},{18,26},{24,28},{26,30},{28,20... | collective-permute-start | bytes 2752520 | tf_op jit(solution)/shard_map/ppermute | solution.py:296
  7.3 22.7 %collective-permute-start.3 = (bf16[64,7168]{1,0:T(8,128)(2,1)S(1)}, bf16[64,7168]{1,0:T(8,128)(2,1)}, u32[]{:S(2)}, u32[]{:S(2)}) collective-permute-start(bf16[64,7168]{1,0:T(8,128)(2,1)S(1)} %pad_maximum_fusion.1.refs_0_), channel_id=1, source_target_pairs={{0,4},{2,6},{8,0},{10,2},{16,8},{18,10},{24,16},{26,18},{28,24},{3... | collective-permute-start | bytes 2752520 | tf_op jit(solution)/shard_map/ppermute | solution.py:296
  28.2 22.4 %collective-permute-start.2 = (bf16[64,7168]{1,0:T(8,128)(2,1)}, bf16[64,7168]{1,0:T(8,128)(2,1)}, u32[]{:S(2)}, u32[]{:S(2)}) collective-permute-start(bf16[64,7168]{1,0:T(8,128)(2,1)} %collective-permute-done.1.refs_1_), channel_id=1, source_target_pairs={{0,8},{2,10},{8,16},{10,18},{16,24},{18,26},{24,28},{26,30},{28,20... | collective-permute-start | bytes 2752520 | tf_op jit(solution)/shard_map/ppermute | solution.py:296
  30.0 21.8 %collective-permute-start.4 = (bf16[64,7168]{1,0:T(8,128)(2,1)}, bf16[64,7168]{1,0:T(8,128)(2,1)}, u32[]{:S(2)}, u32[]{:S(2)}) collective-permute-start(bf16[64,7168]{1,0:T(8,128)(2,1)} %collective-permute-done.3.refs_2_), channel_id=1, source_target_pairs={{0,4},{2,6},{8,0},{10,2},{16,8},{18,10},{24,16},{26,18},{28,24},{3... | collective-permute-start | bytes 2752520 | tf_op jit(solution)/shard_map/ppermute | solution.py:296
  31.0 26.9 %collective-permute-start.8 = (bf16[64,14336]{1,0:T(8,128)(2,1)S(1)}, bf16[64,14336]{1,0:T(8,128)(2,1)}, u32[]{:S(2)}, u32[]{:S(2)}) collective-permute-start(bf16[64,14336]{1,0:T(8,128)(2,1)S(1)} %bitcast.54), channel_id=1, source_target_pairs={{0,2},{2,0},{8,10},{10,8},{16,18},{18,16},{24,26},{26,24},{28,30},... | collective-permute-start | bytes 5505032 | tf_op jit(solution)/shard_map/ppermute | solution.py:296
  51.9 20.9 %collective-permute-start.5 = (bf16[64,7168]{1,0:T(8,128)(2,1)}, bf16[64,7168]{1,0:T(8,128)(2,1)}, u32[]{:S(2)}, u32[]{:S(2)}) collective-permute-start(bf16[64,7168]{1,0:T(8,128)(2,1)} %collective-permute-done.2.refs_3_), channel_id=1, source_target_pairs={{0,8},{2,10},{8,16},{10,18},{16,24},{18,26},{24,28},{26,30},{28,20... | collective-permute-start | bytes 2752520 | tf_op jit(solution)/shard_map/ppermute | solution.py:296
  53.5 20.6 %collective-permute-start.6 = (bf16[64,7168]{1,0:T(8,128)(2,1)}, bf16[64,7168]{1,0:T(8,128)(2,1)}, u32[]{:S(2)}, u32[]{:S(2)}) collective-permute-start(bf16[64,7168]{1,0:T(8,128)(2,1)} %collective-permute-done.4.refs_4_), channel_id=1, source_target_pairs={{0,4},{2,6},{8,0},{10,2},{16,8},{18,10},{24,16},{26,18},{28,24},{3... | collective-permute-start | bytes 2752520 | tf_op jit(solution)/shard_map/ppermute | solution.py:296
  53.9 38.1 %collective-permute-start.11 = (bf16[16,32,512]{2,1,0:T(8,128)(2,1)}, bf16[16,32,512]{2,1,0:T(8,128)(2,1)}, u32[]{:S(2)}, u32[]{:S(2)}) collective-permute-start(bf16[16,32,512]{2,1,0:T(8,128)(2,1)} %param.12), channel_id=1, source_target_pairs={{0,1},{1,0},{2,3},{3,2},{4,5},{5,4},{6,7},{7,6},{8,9},{9,8},{10,11... | collective-permute-start | bytes 1572872 | tf_op jit(solution)/shard_map/ppermute | solution.py:383
  69.9 19.8 %copy-start.1 = (f32[5,64,512]{2,1,0:T(8,128)}, f32[5,64,512]{2,1,0:T(8,128)S(1)}, u32[]{:S(2)}) copy-start(f32[5,64,512]{2,1,0:T(8,128)S(1)} %get-tuple-element.69.refs_7_.refs_3_) | copy-start | bytes 1966084
  75.9 19.3 %collective-permute-start.10 = (bf16[32,7168]{1,0:T(8,128)(2,1)}, bf16[32,7168]{1,0:T(8,128)(2,1)S(1)}, u32[]{:S(2)}, u32[]{:S(2)}) collective-permute-start(bf16[32,7168]{1,0:T(8,128)(2,1)} %slice.65), channel_id=1, source_target_pairs={{0,4},{2,6},{8,0},{10,2},{16,8},{18,10},{24,16},{26,18},{28,24},{3... | collective-permute-start | bytes 1376264 | tf_op jit(solution)/shard_map/ppermute | solution.py:296
  78.2 17.1 %collective-permute-start.9 = (bf16[32,7168]{1,0:T(8,128)(2,1)}, bf16[32,7168]{1,0:T(8,128)(2,1)S(1)}, u32[]{:S(2)}, u32[]{:S(2)}) collective-permute-start(bf16[32,7168]{1,0:T(8,128)(2,1)} %slice.64), channel_id=1, source_target_pairs={{0,8},{2,10},{8,16},{10,18},{16,24},{18,26},{24,28},{26,30},{28,20... | collective-permute-start | bytes 1376264 | tf_op jit(solution)/shard_map/ppermute | solution.py:296
  89.7 0.8 copy-start.3
  90.5 11.5 %collective-permute-start.19 = (f32[3,64,512]{2,1,0:T(8,128)}, f32[3,64,512]{2,1,0:T(8,128)}, u32[]{:S(2)}, u32[]{:S(2)}) collective-permute-start(f32[3,64,512]{2,1,0:T(8,128)} %get-tuple-element.86), channel_id=1, source_target_pairs={{0,2},{2,0},{8,10},{10,8},{16,18},{18,16},{24,26},{26,24},{28,30},... | collective-permute-start | bytes 1179656 | tf_op jit(solution)/shard_map/ppermute | solution.py:296
  90.5 10.0 %collective-permute-start.20 = (bf16[3,64,512]{2,1,0:T(8,128)(2,1)}, bf16[3,64,512]{2,1,0:T(8,128)(2,1)}, u32[]{:S(2)}, u32[]{:S(2)}) collective-permute-start(bf16[3,64,512]{2,1,0:T(8,128)(2,1)} %get-tuple-element.87), channel_id=1, source_target_pairs={{0,1},{1,0},{2,3},{3,2},{4,5},{5,4},{6,7},{7,6},{8,9},{9,8},{10,11... | collective-permute-start | bytes 589832 | tf_op jit(solution)/shard_map/ppermute | solution.py:306
  92.0 10.0 %collective-permute-start.21 = (bf16[3,64,512]{2,1,0:T(8,128)(2,1)}, bf16[3,64,512]{2,1,0:T(8,128)(2,1)}, u32[]{:S(2)}, u32[]{:S(2)}) collective-permute-start(bf16[3,64,512]{2,1,0:T(8,128)(2,1)} %get-tuple-element.88), channel_id=1, source_target_pairs={{0,3},{1,2},{2,1},{3,0},{4,7},{5,6},{6,5},{7,4},{8,11},{9,10},{10,... | collective-permute-start | bytes 589832 | tf_op jit(solution)/shard_map/ppermute | solution.py:307
  95.3 6.7 %copy-start.4 = (f32[3,64,512]{2,1,0:T(8,128)S(1)}, f32[3,64,512]{2,1,0:T(8,128)}, u32[]{:S(2)}) copy-start(f32[3,64,512]{2,1,0:T(8,128)} %copy-done.3) | copy-start | bytes 1179652
  98.8 8.3 %copy-start.2 = (f32[5,64,512]{2,1,0:T(8,128)S(1)}, f32[5,64,512]{2,1,0:T(8,128)}, u32[]{:S(2)}) copy-start(f32[5,64,512]{2,1,0:T(8,128)} %copy-done.1) | copy-start | bytes 1966084
  98.8 4.4 %collective-permute-start.13 = (f32[2,16,64]{2,1,0:T(8,128)S(1)}, f32[2,16,64]{2,1,0:T(8,128)S(1)}, u32[]{:S(2)}, u32[]{:S(2)}) collective-permute-start(f32[2,16,64]{2,1,0:T(8,128)S(1)} %get-tuple-element.77), channel_id=1, source_target_pairs={{0,1},{1,0},{2,3},{3,2},{4,5},{5,4},{6,7},{7,6},{8,9},{9,8},{10,11... | collective-permute-start | bytes 24584 | tf_op jit(solution)/shard_map/ppermute | solution.py:306
  100.4 3.2 %collective-permute-start.14 = (f32[2,16,64]{2,1,0:T(8,128)S(1)}, f32[2,16,64]{2,1,0:T(8,128)S(1)}, u32[]{:S(2)}, u32[]{:S(2)}) collective-permute-start(f32[2,16,64]{2,1,0:T(8,128)S(1)} %get-tuple-element.77), channel_id=1, source_target_pairs={{0,3},{1,2},{2,1},{3,0},{4,7},{5,6},{6,5},{7,4},{8,11},{9,10},{10,... | collective-permute-start | bytes 24584 | tf_op jit(solution)/shard_map/ppermute | solution.py:307
  100.5 2.7 %collective-permute-start.12 = (f32[2,16,64]{2,1,0:T(8,128)S(1)}, f32[2,16,64]{2,1,0:T(8,128)S(1)}, u32[]{:S(2)}, u32[]{:S(2)}) collective-permute-start(f32[2,16,64]{2,1,0:T(8,128)S(1)} %get-tuple-element.76), channel_id=1, source_target_pairs={{0,2},{2,0},{8,10},{10,8},{16,18},{18,16},{24,26},{26,24},{28,30},... | collective-permute-start | bytes 24584 | tf_op jit(solution)/shard_map/ppermute | solution.py:296
  103.6 11.2 %collective-permute-start.15 = (bf16[2,16,64]{2,1,0:T(8,128)(2,1)S(1)}, bf16[2,16,64]{2,1,0:T(8,128)(2,1)S(1)}, u32[]{:S(2)}, u32[]{:S(2)}) collective-permute-start(bf16[2,16,64]{2,1,0:T(8,128)(2,1)S(1)} %get-tuple-element.98), channel_id=1, source_target_pairs={{0,4},{2,6},{4,0},{6,2},{8,12},{10,14},{12,8},{14,10},{16,20},{18,... | collective-permute-start | bytes 12296 | tf_op jit(solution)/shard_map/ppermute | solution.py:434
  104.1 11.3 %collective-permute-start.16 = (bf16[2,16,64]{2,1,0:T(8,128)(2,1)S(1)}, bf16[2,16,64]{2,1,0:T(8,128)(2,1)S(1)}, u32[]{:S(2)}, u32[]{:S(2)}) collective-permute-start(bf16[2,16,64]{2,1,0:T(8,128)(2,1)S(1)} %get-tuple-element.98), channel_id=1, source_target_pairs={{0,8},{2,10},{4,12},{6,14},{8,0},{10,2},{12,4},{14,6},{16,24},{18,... | collective-permute-start | bytes 12296 | tf_op jit(solution)/shard_map/ppermute | solution.py:434
  105.3 10.1 %collective-permute-start.17 = (bf16[2,16,64]{2,1,0:T(8,128)(2,1)S(1)}, bf16[2,16,64]{2,1,0:T(8,128)(2,1)S(1)}, u32[]{:S(2)}, u32[]{:S(2)}) collective-permute-start(bf16[2,16,64]{2,1,0:T(8,128)(2,1)S(1)} %get-tuple-element.98), channel_id=1, source_target_pairs={{0,12},{2,14},{4,8},{6,10},{8,4},{10,6},{12,0},{14,2},{16,28},{18,... | collective-permute-start | bytes 12296 | tf_op jit(solution)/shard_map/ppermute | solution.py:434
  107.2 13.1 %copy-start.8 = (bf16[256,256]{1,0:T(8,128)(2,1)S(1)}, bf16[256,256]{1,0:T(8,128)(2,1)}, u32[]{:S(2)}) copy-start(bf16[256,256]{1,0:T(8,128)(2,1)} %fusion.15) | copy-start | bytes 393220
  113.4 7.4 %copy-start.5 = (bf16[1024,512]{1,0:T(8,128)(2,1)S(1)}, bf16[1024,512]{1,0:T(8,128)(2,1)}, u32[]{:S(2)}) copy-start(bf16[1024,512]{1,0:T(8,128)(2,1)} %pad_maximum_fusion) | copy-start | bytes 3145732
  113.4 7.4 %copy-start.6 = (bf16[256,1024]{1,0:T(8,128)(2,1)S(1)}, bf16[256,1024]{1,0:T(8,128)(2,1)}, u32[]{:S(2)}) copy-start(bf16[256,1024]{1,0:T(8,128)(2,1)} %compare_convert_fusion) | copy-start | bytes 1572868
  113.4 7.4 %copy-start.7 = (bf16[64,1024]{1,0:T(8,128)(2,1)S(1)}, bf16[64,1024]{1,0:T(8,128)(2,1)}, u32[]{:S(2)}) copy-start(bf16[64,1024]{1,0:T(8,128)(2,1)} %fusion.16) | copy-start | bytes 393220
  113.4 7.1 %collective-permute-start.22 = (f32[1,64,512]{2,1,0:T(8,128)S(1)}, f32[1,64,512]{2,1,0:T(8,128)S(1)}, u32[]{:S(2)}, u32[]{:S(2)}) collective-permute-start(f32[1,64,512]{2,1,0:T(8,128)S(1)} %get-tuple-element.92), channel_id=1, source_target_pairs={{0,2},{2,0},{8,10},{10,8},{16,18},{18,16},{24,26},{26,24},{28,30},... | collective-permute-start | bytes 393224 | tf_op jit(solution)/shard_map/ppermute | solution.py:296
  113.5 7.0 %collective-permute-start.23 = (bf16[1,64,512]{2,1,0:T(8,128)(2,1)S(1)}, bf16[1,64,512]{2,1,0:T(8,128)(2,1)S(1)}, u32[]{:S(2)}, u32[]{:S(2)}) collective-permute-start(bf16[1,64,512]{2,1,0:T(8,128)(2,1)S(1)} %get-tuple-element.93), channel_id=1, source_target_pairs={{0,1},{1,0},{2,3},{3,2},{4,5},{5,4},{6,7},{7,6},{8,9},{9,8},{10,11... | collective-permute-start | bytes 196616 | tf_op jit(solution)/shard_map/ppermute | solution.py:306
  114.8 5.6 %collective-permute-start.24 = (bf16[1,64,512]{2,1,0:T(8,128)(2,1)S(1)}, bf16[1,64,512]{2,1,0:T(8,128)(2,1)S(1)}, u32[]{:S(2)}, u32[]{:S(2)}) collective-permute-start(bf16[1,64,512]{2,1,0:T(8,128)(2,1)S(1)} %get-tuple-element.94), channel_id=1, source_target_pairs={{0,3},{1,2},{2,1},{3,0},{4,7},{5,6},{6,5},{7,4},{8,11},{9,10},{10,... | collective-permute-start | bytes 196616 | tf_op jit(solution)/shard_map/ppermute | solution.py:307
  115.4 4.9 %collective-permute-start.18 = (bf16[8,16,64]{2,1,0:T(8,128)(2,1)S(1)}, bf16[8,16,64]{2,1,0:T(8,128)(2,1)S(1)}, u32[]{:S(2)}, u32[]{:S(2)}) collective-permute-start(bf16[8,16,64]{2,1,0:T(8,128)(2,1)S(1)} %pad_maximum_fusion.2), channel_id=1, source_target_pairs={{0,16},{2,18},{4,20},{6,22},{8,24},{10,26},{12,28},{14,30},{16,0},... | collective-permute-start | bytes 49160 | tf_op jit(solution)/shard_map/ppermute | solution.py:434

commit v8 on v7

--- a/solution.py
+++ b/solution.py
@@ -43,19 +43,18 @@
     return started(sources, [held.at[which] for which in (0, 1)], ready)
 
 
-def weight_products(pieces, copies, held, sums):
+def weight_products(rows_of, copies, held, sums):
     tiles, tile = held.shape[1:3]
     for total in sums:
         total[...] = jnp.zeros_like(total)
     for index in range(tiles):
-        here = slice(index * tile, (index + 1) * tile)
-        rows = jnp.concatenate([piece[:, here] for piece in pieces], axis=0)
+        rows = rows_of(slice(index * tile, (index + 1) * tile))
         for which, total in enumerate(sums):
             copies[2 * index + which].wait()
             total[...] += jnp.dot(rows, held[which, index], preferred_element_type=jnp.float32)
 
 
-def factor_products(pieces, copies, held, low):
+def factor_products(rows_of, copies, held, low):
     rank, depth = held.shape[1:]
     tile = tile_of(depth)
     low[...] = jnp.zeros_like(low)
@@ -64,10 +63,9 @@
 
     def step(index, carry):
         here = pl.ds(pl.multiple_of(index * tile, 128), tile)
-        rows = jnp.concatenate([piece[:, here] for piece in pieces], axis=0)
         both = jnp.concatenate([held[which, :, here] for which in (0, 1)], axis=0)
         low[...] += lax.dot_general(
-            rows, both, (((1,), (1,)), ((), ())), preferred_element_type=jnp.float32
+            rows_of(here), both, (((1,), (1,)), ((), ())), preferred_element_type=jnp.float32
         )
         return carry
 
@@ -83,7 +81,23 @@
 
 
 def compacted(choice, low):
-    return jnp.dot(choice, low, precision=lax.Precision.HIGHEST, preferred_element_type=jnp.float32)
+    high = low.astype(jnp.bfloat16)
+    rest = low - high.astype(jnp.float32)
+    middle = rest.astype(jnp.bfloat16)
+    tail = (rest - middle.astype(jnp.float32)).astype(jnp.bfloat16)
+    picked = jnp.dot(
+        choice,
+        jnp.concatenate([high, middle, tail], axis=1),
+        preferred_element_type=jnp.float32,
+    )
+    size = low.shape[1]
+    total = picked[:, :size] + (picked[:, size : 2 * size] + picked[:, 2 * size :])
+    count, rank = choice.shape[0] // 2, size // 2
+    return total[:count, :rank], total[count:, rank:]
+
+
+def last_rows(lane, piece, other, here):
+    return jnp.where(lane == 0, piece[:, here], other[:, here])
 
 
 def early_kernel(count, facts, *refs):
@@ -91,16 +105,16 @@
     weights, factors, choices = refs[:2], refs[2:4], refs[4]
     (base, base_sib, compact), refs = refs[5:8], refs[8:]
     sums, low, held, ready, held_low, ready_low = refs[:2], *refs[2:]
-    rank = held_low.shape[1]
+    rows_of = lambda here: jnp.concatenate([piece[:, here] for piece in pieces], axis=0)
     in_flight = weight_copies(facts[0], weights, held, ready)
     in_flight_low = factor_copies(facts[0], factors, held_low, ready_low)
-    weight_products(pieces, in_flight, held, sums)
-    factor_products(pieces, in_flight_low, held_low, low)
+    weight_products(rows_of, in_flight, held, sums)
+    factor_products(rows_of, in_flight_low, held_low, low)
     height = base.shape[1] // 2
-    for which, (out, total) in enumerate(zip((base, base_sib), sums)):
+    for out, total in zip((base, base_sib), sums):
         for index in range(out.shape[0]):
             out[index] = in_lanes(facts[0], total, index, height)
-        compact[which] = compacted(choices[which], low[:, which * rank : (which + 1) * rank])
+    compact[0], compact[1] = compacted(choices[...], low[...])
 
 
 def share(flag, near, away, outs, pair):
@@ -117,11 +131,11 @@
     (choices, compact_in, base, base_sib), refs = refs[4:8], refs[8:]
     outs, compact, refs = refs[:4], refs[4], refs[5:]
     sums, low, held, ready, held_low, ready_low = refs[:2], *refs[2:]
-    rank = held_low.shape[1]
+    rows_of = lambda here: jnp.concatenate([piece[:, here], other[:, here]], axis=0)
     in_flight = weight_copies(facts[0], weights, held, ready)
     in_flight_low = factor_copies(facts[0], factors, held_low, ready_low)
-    weight_products((piece, other), in_flight, held, sums)
-    factor_products((piece, other), in_flight_low, held_low, low)
+    weight_products(rows_of, in_flight, held, sums)
+    factor_products(rows_of, in_flight_low, held_low, low)
     pairs, group = outs[0].shape[:2]
     fresh = [[in_lanes(facts[0], total, index, group // 2) for total in sums] for index in (0, 1)]
     for pair in range(pairs):
@@ -129,35 +143,33 @@
         near = fresh[1] if step == pairs else (base[2 * step], base_sib[2 * step])
         away = fresh[0] if back == pairs else (base[2 * back - 1], base_sib[2 * back - 1])
         share(facts[2 + step], near, away, outs, pair)
-    for which in (0, 1):
-        compact[which] = compact_in[which] + compacted(
-            choices[which], low[:, which * rank : (which + 1) * rank]
-        )
+    for which, fresh_low in enumerate(compacted(choices[...], low[...])):
+        compact[which] = compact_in[which] + fresh_low
 
 
 def low_kernel(facts, piece, other, *refs):
     factors, (choices, compact_in, kept, sent, low, held, ready) = refs[:2], refs[2:]
-    rank, half = held.shape[1], kept.shape[1]
-    factor_products((piece, other), factor_copies(facts[0], factors, held, ready), held, low)
-    for which in (0, 1):
-        compact = compact_in[which] + compacted(
-            choices[which], low[:, which * rank : (which + 1) * rank]
-        )
-        kept[which] = jnp.where(facts[1] == 0, compact[:half], compact[half:])
-        sent[which] = jnp.where(facts[1] == 0, compact[half:], compact[:half])
+    half = kept.shape[1]
+    rows_of = functools.partial(last_rows, facts[0], piece, other)
+    factor_products(rows_of, factor_copies(facts[0], factors, held, ready), held, low)
+    for which, fresh_low in enumerate(compacted(choices[...], low[...])):
+        total = compact_in[which] + fresh_low
+        kept[which] = jnp.where(facts[1] == 0, total[:half], total[half:])
+        sent[which] = jnp.where(facts[1] == 0, total[half:], total[:half])
 
 
 def last_kernel(facts, piece, other, *refs):
     weights, (base, base_sib), refs = refs[:2], refs[2:4], refs[4:]
     outs, sums, (held, ready) = refs[:4], refs[4:6], refs[6:]
-    weight_products((piece, other), weight_copies(facts[0], weights, held, ready), held, sums)
-    away = [in_lanes(facts[0], total, 0, piece.shape[0]) for total in sums]
+    rows_of = functools.partial(last_rows, facts[0], piece, other)
+    weight_products(rows_of, weight_copies(facts[0], weights, held, ready), held, sums)
+    away = [in_lanes(facts[0], total, 0, piece.shape[0] // 2) for total in sums]
     share(facts[2], (base[0], base_sib[0]), away, outs, 0)
 
 
-def kernel_call(kernel, facts, rows, weights, factors, others, shapes):
+def kernel_call(kernel, facts, rows, total, weights, factors, others, shapes):
     in_vmem, anywhere = pl.BlockSpec(memory_space=pltpu.VMEM), pl.BlockSpec(memory_space=pl.ANY)
-    depth, total = rows[0].shape[1], sum(values.shape[0] for values in rows)
+    depth = rows[0].shape[1]
     tile = tile_of(depth)
     scratch, columns = [], 0
     if weights:
@@ -349,18 +361,19 @@
     place_came = jnp.sum(
         jnp.where(came[:, :, None], position[None] + MOST * blocks[None, :, None], 0), axis=1
     ).reshape(1, -1)
-    chosen = jnp.stack(
+    chosen = jnp.concatenate(
         [
-            ((place_came == items[:, None]) & (slot_came == slot)).astype(f32)
+            ((place_came == items[:, None]) & (slot_came == slot)).astype(bf16)
             for slot in (home_late, jnp.bitwise_xor(home_late, 1))
-        ]
+        ],
+        axis=0,
     )
     early_rows = len(pieces) * group_rows
-    middle_rows = early_rows + 4 * row_count
+    middle_rows = early_rows + 2 * group_rows
     choices = [
-        chosen[:, :, :early_rows],
-        chosen[:, :, early_rows:middle_rows],
-        chosen[:, :, middle_rows:],
+        chosen[:, :early_rows],
+        chosen[:, early_rows:middle_rows],
+        chosen[:, middle_rows:],
     ]
 
     half = own_blocks * MOST
@@ -374,32 +387,38 @@
         + position_here.reshape(here, 1)
     )
     spots = (spot == jnp.arange(owners * half, dtype=jnp.int32)[None, :]).astype(bf16)
-    column = jnp.arange(owners * rank, dtype=jnp.int32)[None, :]
     piece = rank // 2
-    own_rank = jnp.bitwise_xor(part, column // (owners * piece)) * piece + column % piece
-    mask = (slot_here == column // piece % owners).astype(bf16)
-    copies = (jnp.arange(rank, dtype=jnp.int32)[:, None] == own_rank).astype(bf16)
-
-    other = lax.ppermute(second_factor_table, INNER, SWAP)
-    second = jnp.concatenate(
-        [values.reshape(owners * piece, width) for values in (second_factor_table, other)], axis=0
-    )
+    column = jnp.arange(owners * piece, dtype=jnp.int32)[None, :]
+    mask = (slot_here == column // piece).astype(bf16)
+    copies = [
+        (jnp.arange(rank, dtype=jnp.int32)[:, None] == which * piece + column % piece).astype(bf16)
+        for which in (part, 1 - part)
+    ]
+
+    seconds = [
+        values.reshape(owners * piece, width)
+        for values in (second_factor_table, lax.ppermute(second_factor_table, INNER, SWAP))
+    ]
 
     compact_shape = ((2, owners * MOST, rank), f32)
     early = kernel_call(
         functools.partial(early_kernel, len(pieces)),
         facts,
         pieces,
+        early_rows,
         weights,
         factors,
         (choices[0],),
         [((len(pieces), group_rows, width), f32)] * 2 + [compact_shape],
     )
-    ready = (facts, spots, mask, copies, choices, places)
+    ready = (facts, spots, mask, copies, choices, places, seconds)
     right, left, early, ready = lax.optimization_barrier((right, left, early, ready))
-    facts, spots, mask, copies, choices, places = ready
-
-    last = [send(right[:row_count], 1), send(left[row_count:], -1)]
+    facts, spots, mask, copies, choices, places, seconds = ready
+
+    last = [
+        lax.ppermute(right, "wide", [(a, b) for a, b in moved(1) if a % 2 == 0]),
+        lax.ppermute(left, "wide", [(a, b) for a, b in moved(-1) if a % 2 == 1]),
+    ]
 
     def shares(pairs):
         shape = (pairs, group_rows, width)
@@ -409,23 +428,31 @@
         middle_kernel,
         facts,
         (right, left),
+        2 * group_rows,
         weights,
         factors,
         (choices[1], early[2], early[0], early[1]),
         shares(far - 1) + [compact_shape],
     )
     got_more = to_three(*more)
-    last, compact, second = lax.optimization_barrier((last, compact, second))
+    last, compact = lax.optimization_barrier((last, compact))
 
     kept, sent = kernel_call(
-        low_kernel, facts, last, (), factors, (choices[2], compact), [((2, half, rank), f32)] * 2
+        low_kernel,
+        facts,
+        last,
+        group_rows,
+        (),
+        factors,
+        (choices[2], compact),
+        [((2, half, rank), f32)] * 2,
     )
     got = to_three(kept, sent, sent)
-    got, last = lax.optimization_barrier((got, last))
 
     kept_one, *one = kernel_call(
-        last_kernel, facts, last, weights, (), (early[0], early[1]), shares(1)
-    )
+        last_kernel, facts, last, group_rows, weights, (), (early[0], early[1]), shares(1)
+    )
+    got, got_more, one = lax.optimization_barrier((got, got_more, one))
     got_one = to_three(*one)
 
     low = (kept + got[1] + (got[0] + got[2])[::-1]).astype(bf16)
@@ -444,8 +471,11 @@
     for pair in range(1, far):
         rows = rows + jnp.where(places[pair][:, None, None], more[pair - 1 : pair], 0)
     own_low = jnp.dot(spots, low.reshape(owners * half, rank), preferred_element_type=f32)
-    spread = jnp.dot(own_low.astype(bf16), copies, preferred_element_type=f32).astype(bf16) * mask
-    delta = jnp.dot(spread, second, preferred_element_type=f32)
+    own_low = own_low.astype(bf16)
+    delta = 0
+    for copy, second in zip(copies, seconds):
+        spread = jnp.dot(own_low, copy, preferred_element_type=f32).astype(bf16) * mask
+        delta = delta + jnp.dot(spread, second, preferred_element_type=f32)
     one = kept_one + got_one[0] + got_one[1].astype(f32) + got_one[2].astype(f32)
     rows = rows + jnp.where(places[0][:, None, None], one, 0)
     return (delta + rows.reshape(-1, width)).astype(bf16)

time: 122 us -> 122 us (level)
  other arithmetic: 9.78 us -> 7.15 us
  starting transfers between devices: 23.4 us -> 25.2 us
  matrix products: 1.42 us -> 2.85 us
    ppermute x1 -> x3, starting transfers between devices: 1.49 us -> 5.93 us  [the longest x1 3.47 us: ringed(): lax.ppermute(right, 'wide', [(a, b) for a, b in moved(1) if a % 2 == 0])]
    slice x3 -> x1, local copies, waits for them, and re-layouts: 3.66 us -> 0.01 us  [ringed(): chosen[:, :early_rows]]
    unnamed x25 -> x35, local copies, waits for them, and re-layouts: 0.82 us -> 3.82 us
    concatenate x1, other arithmetic: 2.25 us -> 0.01 us  [ringed(): jnp.concatenate([((place_came == items[:, None]) & (slot_came == slot)).a...]
    ppermute x14 -> x12, starting transfers between devices: 10.4 us -> 8.54 us  [send(): return lax.ppermute(value, 'wide', moved(shift, cross))]
    dot_general x1 -> x2, matrix products: 1.26 us -> 2.65 us  [ringed(): delta = delta + jnp.dot(spread, second, preferred_element_type=f32)]
    ppermute x14 -> x12, waiting for transfers between devices: 45.5 us -> 45.7 us  [send(): return lax.ppermute(value, 'wide', moved(shift, cross))]
  transfers between devices with their start and end apart: 25 -> 25, of which waited for: 9 -> 7; matrix products, arithmetic and copies ran while one was open for 11% -> 6% of each run, Pallas kernels for 26% -> 26%
where the time goes in v8:
time: 122 us
  waiting for transfers between devices  49.1 us (40%)
  Pallas kernels  31.7 us (26%)
  starting transfers between devices  25.2 us (21%)
  other arithmetic  7.15 us (6%)
  local copies, waits for them, and re-layouts  5.69 us (5%)
  matrix products  2.85 us (2%)
    ppermute x12, waiting for transfers between devices, send(): return lax.ppermute(value, 'wide', moved(shift, cross))  45.7 us
    pallas_call x4, Pallas kernels, kernel_call(): pl.pallas_call(kernel, in_specs=[pl.BlockSpec(memory_space=pltpu.SMEM)] +...  31.7 us
    ppermute x12, starting transfers between devices, send(): return lax.ppermute(value, 'wide', moved(shift, cross))  8.54 us
    ppermute x4, starting transfers between devices, from_node(): lax.ppermute(value, 'wide', [(w, w ^ 2 * gap) for w in range(owners)])  5.13 us
    ppermute x3, starting transfers between devices, to_three(): lax.ppermute(to_mp, INNER, SWAP)  4.66 us
    unnamed x35, local copies, waits for them, and re-layouts  3.82 us
    ppermute x1, starting transfers between devices, ringed(): lax.ppermute(right, 'wide', [(a, b) for a, b in moved(1) if a % 2 == 0])  3.47 us
    ppermute x4, waiting for transfers between devices, from_node(): lax.ppermute(value, 'wide', [(w, w ^ 2 * gap) for w in range(owners)])  3.29 us
  transfers between devices with their start and end apart: 25, of which 7 were waited for; matrix products, arithmetic and copies ran while one was open for 6% of the time, Pallas kernels for 26%

profile of v8, /device:TPU:0, one launch (start us, length us, event | category | flops | bytes accessed | tf_op | source)
XLA Modules:
  0.0 122.0 jit_solution(10070359914936536018)
XLA Ops:
  0.0 2.1 %fusion.14 = (bf16[32,7168]{1,0:T(8,128)(2,1)S(1)}, bf16[32,7168]{1,0:T(8,128)(2,1)S(1)}) fusion(bf16[32,14336]{1,0:T(8,128)(2,1)} %param.9, s32[]{:T(128)S(6)} %select_n.105, bf16[32,14336]{1,0:T(8,128)(2,1)} %param.8, s32[]{:T(128)S(6)} %select_n.106), kind=kLoop, calls=%fused_computation.23 | loop fusion | flops 3670016 | bytes 2752520 | tf_op jit(solution)/shard_map/convert_element_type | solution.py:207
  2.1 0.5 collective-permute-start
  2.6 1.4 %collective-permute-done = bf16[32,7168]{1,0:T(8,128)(2,1)S(1)} collective-permute-done((bf16[32,7168]{1,0:T(8,128)(2,1)S(1)}, bf16[32,7168]{1,0:T(8,128)(2,1)S(1)}, u32[]{:S(2)}, u32[]{:S(2)}) %collective-permute-start) | collective-permute-done | bytes 458784 | tf_op jit(solution)/shard_map/ppermute | solution.py:308
  4.1 0.4 collective-permute-start.7
  4.6 2.7 %collective-permute-start.1 = (bf16[64,7168]{1,0:T(8,128)(2,1)S(1)}, bf16[64,7168]{1,0:T(8,128)(2,1)}, u32[]{:S(2)}, u32[]{:S(2)}) collective-permute-start(bf16[64,7168]{1,0:T(8,128)(2,1)S(1)} %pad_maximum_fusion.refs_0_), channel_id=1, source_target_pairs={{0,8},{2,10},{8,16},{10,18},{16,24},{18,26},{24,28},{26,30},{28,20... | collective-permute-start | bytes 2752520 | tf_op jit(solution)/shard_map/ppermute | solution.py:308
  7.3 20.9 %collective-permute-done.1.refs_1_ = bf16[64,7168]{1,0:T(8,128)(2,1)} collective-permute-done((bf16[64,7168]{1,0:T(8,128)(2,1)S(1)}, bf16[64,7168]{1,0:T(8,128)(2,1)}, u32[]{:S(2)}, u32[]{:S(2)}) %collective-permute-start.1) | collective-permute-done | bytes 917536 | tf_op jit(solution)/shard_map/ppermute | solution.py:308
  28.2 1.8 %collective-permute-start.2 = (bf16[64,7168]{1,0:T(8,128)(2,1)}, bf16[64,7168]{1,0:T(8,128)(2,1)}, u32[]{:S(2)}, u32[]{:S(2)}) collective-permute-start(bf16[64,7168]{1,0:T(8,128)(2,1)} %collective-permute-done.1.refs_1_), channel_id=1, source_target_pairs={{0,8},{2,10},{8,16},{10,18},{16,24},{18,26},{24,28},{26,30},{28,20... | collective-permute-start | bytes 2752520 | tf_op jit(solution)/shard_map/ppermute | solution.py:308
  30.0 0.2 collective-permute-start.4
  30.3 0.6 fusion.20
  31.0 19.6 %collective-permute-done.2.refs_3_ = bf16[64,7168]{1,0:T(8,128)(2,1)} collective-permute-done((bf16[64,7168]{1,0:T(8,128)(2,1)}, bf16[64,7168]{1,0:T(8,128)(2,1)}, u32[]{:S(2)}, u32[]{:S(2)}) %collective-permute-start.2) | collective-permute-done | bytes 917536 | tf_op jit(solution)/shard_map/ppermute | solution.py:308
  50.6 1.3 %collective-permute-done.4.refs_4_ = bf16[64,7168]{1,0:T(8,128)(2,1)} collective-permute-done((bf16[64,7168]{1,0:T(8,128)(2,1)}, bf16[64,7168]{1,0:T(8,128)(2,1)}, u32[]{:S(2)}, u32[]{:S(2)}) %collective-permute-start.4) | collective-permute-done | bytes 917536 | tf_op jit(solution)/shard_map/ppermute | solution.py:308
  51.9 1.6 %collective-permute-start.5 = (bf16[64,7168]{1,0:T(8,128)(2,1)}, bf16[64,7168]{1,0:T(8,128)(2,1)}, u32[]{:S(2)}, u32[]{:S(2)}) collective-permute-start(bf16[64,7168]{1,0:T(8,128)(2,1)} %collective-permute-done.2.refs_3_), channel_id=1, source_target_pairs={{0,8},{2,10},{8,16},{10,18},{16,24},{18,26},{24,28},{26,30},{28,20... | collective-permute-start | bytes 2752520 | tf_op jit(solution)/shard_map/ppermute | solution.py:308
  53.5 0.4 collective-permute-start.6
  53.9 0.7 constant_dynamic-slice_fusion.2
  54.8 0.5 convert_reduce_fusion
  55.4 0.1 select_reduce_fusion
  56.0 1.6 %collective-permute-start.9 = (bf16[16,32,512]{2,1,0:T(8,128)(2,1)}, bf16[16,32,512]{2,1,0:T(8,128)(2,1)S(1)}, u32[]{:S(2)}, u32[]{:S(2)}) collective-permute-start(bf16[16,32,512]{2,1,0:T(8,128)(2,1)} %param.12), channel_id=1, source_target_pairs={{0,1},{1,0},{2,3},{3,2},{4,5},{5,4},{6,7},{7,6},{8,9},{9,8},{10,11... | collective-permute-start | bytes 1572872 | tf_op jit(solution)/shard_map/ppermute | solution.py:400
  57.8 12.0 %shard_map.82 = (f32[5,64,512]{2,1,0:T(8,128)S(1)}, f32[5,64,512]{2,1,0:T(8,128)S(1)}, f32[2,32,64]{2,1,0:T(8,128)S(1)}) custom-call(s32[6]{0:T(128)S(1)} %pad_add_fusion.facts, bf16[64,7168]{1,0:T(8,128)(2,1)S(1)} %pad_maximum_fusion.refs_0_, bf16[64,7168]{1,0:T(8,128)(2,1)} %collective-permute-done.1.refs_1_, ...), custom_call_target="tpu_custom_call" | custom-call | flops 82575360 | bytes 516096 | tf_op jit(solution)/shard_map/pallas_call | solution.py:188
  70.0 0.8 fusion.18
  70.8 0.8 compare_convert_fusion
  71.6 1.2 collective-permute-done.5.piece
  72.8 1.3 %collective-permute-done.6.other = bf16[64,7168]{1,0:T(8,128)(2,1)} collective-permute-done((bf16[64,7168]{1,0:T(8,128)(2,1)}, bf16[64,7168]{1,0:T(8,128)(2,1)}, u32[]{:S(2)}, u32[]{:S(2)}) %collective-permute-start.6) | collective-permute-done | bytes 917536 | tf_op jit(solution)/shard_map/ppermute | solution.py:308
  74.1 0.8 copy-done.9
  74.9 3.5 %collective-permute-start.10 = (bf16[64,7168]{1,0:T(8,128)(2,1)}, bf16[64,7168]{1,0:T(8,128)(2,1)S(1)}, u32[]{:S(2)}, u32[]{:S(2)}) collective-permute-start(bf16[64,7168]{1,0:T(8,128)(2,1)} %collective-permute-done.5.piece), channel_id=1, source_target_pairs={{0,8},{8,16},{16,24},{24,28},{28,20},{20,12},{12,4},{4,0},{1,9},{9... | collective-permute-start | bytes 2752520 | tf_op jit(solution)/shard_map/ppermute | solution.py:419
  78.4 0.9 collective-permute-start.11
  79.3 9.9 %shard_map.83 = (f32[3,64,512]{2,1,0:T(8,128)S(1)}, f32[3,64,512]{2,1,0:T(8,128)}, bf16[3,64,512]{2,1,0:T(8,128)(2,1)S(1)}, bf16[3,64,512]{2,1,0:T(8,128)(2,1)}, f32[2,32,64]{2,1,0:T(8,128)S(1)}) custom-call(s32[6]{0:T(128)S(1)} %pad_add_fusion.facts, bf16[64,7168]{1,0:T(8,128)(2,1)} %collective-permute-done.5.piece, ...), custom_call_target="tpu_custom_call" | custom-call | flops 33030144 | bytes 516096 | tf_op jit(solution)/shard_map/pallas_call | solution.py:188
  89.2 1.6 %collective-permute-start.16 = (bf16[3,64,512]{2,1,0:T(8,128)(2,1)S(1)}, bf16[3,64,512]{2,1,0:T(8,128)(2,1)S(1)}, u32[]{:S(2)}, u32[]{:S(2)}) collective-permute-start(bf16[3,64,512]{2,1,0:T(8,128)(2,1)S(1)} %get-tuple-element.85), channel_id=1, source_target_pairs={{0,1},{1,0},{2,3},{3,2},{4,5},{5,4},{6,7},{7,6},{8,9},{9,8},{10,11... | collective-permute-start | bytes 589832 | tf_op jit(solution)/shard_map/ppermute | solution.py:318
  90.8 0.6 collective-permute-start.17
  91.4 3.5 %shard_map.84 = (f32[2,16,64]{2,1,0:T(8,128)S(1)}, f32[2,16,64]{2,1,0:T(8,128)S(1)}) custom-call(s32[6]{0:T(128)S(1)} %pad_add_fusion.facts, bf16[64,7168]{1,0:T(8,128)(2,1)S(1)} %collective-permute-done.10.piece, bf16[64,7168]{1,0:T(8,128)(2,1)S(1)} %collective-permute-done.11.other, bf16[64,14336]{1,0:T(8,128)(2,1)S(1)} %bitcast.60, ...), custom_call_target="tpu_custom_call" | custom-call | flops 1835008 | bytes 57344 | tf_op jit(solution)/shard_map/pallas_call | solution.py:188
  95.0 1.6 %collective-permute-start.13 = (f32[2,16,64]{2,1,0:T(8,128)S(1)}, f32[2,16,64]{2,1,0:T(8,128)S(1)}, u32[]{:S(2)}, u32[]{:S(2)}) collective-permute-start(f32[2,16,64]{2,1,0:T(8,128)S(1)} %get-tuple-element.83), channel_id=1, source_target_pairs={{0,1},{1,0},{2,3},{3,2},{4,5},{5,4},{6,7},{7,6},{8,9},{9,8},{10,11... | collective-permute-start | bytes 24584 | tf_op jit(solution)/shard_map/ppermute | solution.py:318
  96.6 0.7 copy-done.12
  97.3 0.6 collective-permute-start.12
  98.0 0.1 broadcast_in_dim.170
  98.6 1.2 copy-done.2
  99.8 1.1 copy-done.4
  100.8 6.2 %shard_map.85 = (f32[1,64,512]{2,1,0:T(8,128)S(1)}, f32[1,64,512]{2,1,0:T(8,128)S(1)}, bf16[1,64,512]{2,1,0:T(8,128)(2,1)S(1)}, bf16[1,64,512]{2,1,0:T(8,128)(2,1)S(1)}) custom-call(s32[6]{0:T(128)S(1)} %pad_add_fusion.facts, bf16[64,7168]{1,0:T(8,128)(2,1)S(1)} %collective-permute-done.10.piece, bf16[64,7168]{1,0:T(8,128)(2,1)S(1)} %copy-done.2, ...), custom_call_target="tpu_custom_call" | custom-call | flops 14680064 | bytes 458752 | tf_op jit(solution)/shard_map/pallas_call | solution.py:188
  107.2 0.5 collective-permute-start.18
  107.7 1.1 collective-permute-start.19
  108.8 1.9 %collective-permute-start.20 = (bf16[2,16,64]{2,1,0:T(8,128)(2,1)S(1)}, bf16[2,16,64]{2,1,0:T(8,128)(2,1)S(1)}, u32[]{:S(2)}, u32[]{:S(2)}) collective-permute-start(bf16[2,16,64]{2,1,0:T(8,128)(2,1)S(1)} %get-tuple-element.110), channel_id=1, source_target_pairs={{0,12},{2,14},{4,8},{6,10},{8,4},{10,6},{12,0},{14,2},{16,28},{18,... | collective-permute-start | bytes 12296 | tf_op jit(solution)/shard_map/ppermute | solution.py:461
  110.7 1.2 convert_add_fusion
  112.1 1.6 %collective-permute-start.23 = (bf16[1,64,512]{2,1,0:T(8,128)(2,1)S(1)}, bf16[1,64,512]{2,1,0:T(8,128)(2,1)S(1)}, u32[]{:S(2)}, u32[]{:S(2)}) collective-permute-start(bf16[1,64,512]{2,1,0:T(8,128)(2,1)S(1)} %get-tuple-element.105), channel_id=1, source_target_pairs={{0,1},{1,0},{2,3},{3,2},{4,5},{5,4},{6,7},{7,6},{8,9},{9,8},{10,11... | collective-permute-start | bytes 196616 | tf_op jit(solution)/shard_map/ppermute | solution.py:318
  113.6 0.3 collective-permute-start.24
  113.9 1.6 %collective-permute-start.21 = (bf16[8,16,64]{2,1,0:T(8,128)(2,1)S(1)}, bf16[8,16,64]{2,1,0:T(8,128)(2,1)S(1)}, u32[]{:S(2)}, u32[]{:S(2)}) collective-permute-start(bf16[8,16,64]{2,1,0:T(8,128)(2,1)S(1)} %pad_maximum_fusion.1), channel_id=1, source_target_pairs={{0,16},{2,18},{4,20},{6,22},{8,24},{10,26},{12,28},{14,30},{16,0},... | collective-permute-start | bytes 49160 | tf_op jit(solution)/shard_map/ppermute | solution.py:461
  115.5 3.3 %collective-permute-done.21 = bf16[8,16,64]{2,1,0:T(8,128)(2,1)S(1)} collective-permute-done((bf16[8,16,64]{2,1,0:T(8,128)(2,1)S(1)}, bf16[8,16,64]{2,1,0:T(8,128)(2,1)S(1)}, u32[]{:S(2)}, u32[]{:S(2)}) %collective-permute-start.21) | collective-permute-done | bytes 16416 | tf_op jit(solution)/shard_map/ppermute | solution.py:461
  118.8 0.2 convolution_convert_fusion.2
  119.1 0.4 fusion.4
  119.6 0.2 fusion.15
  119.8 2.2 %fusion.1 = bf16[256,512]{1,0:T(8,128)(2,1)} fusion(f32[256,512]{1,0:T(8,128)S(1)} %fusion.15, f32[256,512]{1,0:T(8,128)S(1)} %fusion.4, bf16[512,512]{1,0:T(8,128)(2,1)} %bitcast.7, bf16[256,512]{1,0:T(8,128)(2,1)S(1)} %copy-done.7, bf16[256,64]{0,1:T(8,128)(2,1)S(1)} %convolution_convert_fusion.2, bf16[64,512]{1,0:T(8,128)(2,1)S(1)} %fusion.19), kind=kOutput, calls=%fused_computation.2 | convolution fusion | flops 151650304 | bytes 2195456 | tf_op jit(solution)/shard_map/dot_general | solution.py:478
  (95 shorter events, 2.2 us)
Async XLA Ops:
  0.0 30.9 %copy-start = (bf16[1,64,14336]{2,1,0:T(8,128)(2,1)S(1)}, bf16[1,64,14336]{2,1,0:T(8,128)(2,1)}, u32[]{:S(2)}) copy-start(bf16[1,64,14336]{2,1,0:T(8,128)(2,1)} %param.11) | copy-start | bytes 5505028
  0.0 54.6 %copy-start.14 = (s32[512,1]{0,1:T(1,128)S(1)}, s32[512,1]{0,1:T(1,128)}, u32[]{:S(2)}) copy-start(s32[512,1]{0,1:T(1,128)} %param.13) | copy-start | bytes 6148
  0.0 54.6 %copy-start.15 = (s32[16]{0:T(128)S(1)}, s32[16]{0:T(128)}, u32[]{:S(2)}) copy-start(s32[16]{0:T(128)} %param.14) | copy-start | bytes 196
  2.1 2.0 %collective-permute-start = (bf16[32,7168]{1,0:T(8,128)(2,1)S(1)}, bf16[32,7168]{1,0:T(8,128)(2,1)S(1)}, u32[]{:S(2)}, u32[]{:S(2)}) collective-permute-start(bf16[32,7168]{1,0:T(8,128)(2,1)S(1)} %get-tuple-element.112), channel_id=1, source_target_pairs={{0,2},{2,0},{8,10},{10,8},{16,18},{18,16},{24,26},{26,24},{28,30},... | collective-permute-start | bytes 1376264 | tf_op jit(solution)/shard_map/ppermute | solution.py:308
  4.1 49.8 %collective-permute-start.7 = (bf16[14336,512]{1,0:T(8,128)(2,1)}, bf16[14336,512]{1,0:T(8,128)(2,1)}, u32[]{:S(2)}, u32[]{:S(2)}) collective-permute-start(bf16[14336,512]{1,0:T(8,128)(2,1)} %refs_0_.1), channel_id=1, source_target_pairs={{0,2},{2,0},{8,10},{10,8},{16,18},{18,16},{24,26},{26,24},{28,30},... | collective-permute-start | bytes 44040200 | tf_op jit(solution)/shard_map/ppermute | solution.py:308
  4.6 23.6 %collective-permute-start.1 = (bf16[64,7168]{1,0:T(8,128)(2,1)S(1)}, bf16[64,7168]{1,0:T(8,128)(2,1)}, u32[]{:S(2)}, u32[]{:S(2)}) collective-permute-start(bf16[64,7168]{1,0:T(8,128)(2,1)S(1)} %pad_maximum_fusion.refs_0_), channel_id=1, source_target_pairs={{0,8},{2,10},{8,16},{10,18},{16,24},{18,26},{24,28},{26,30},{28,20... | collective-permute-start | bytes 2752520 | tf_op jit(solution)/shard_map/ppermute | solution.py:308
  7.3 22.7 %collective-permute-start.3 = (bf16[64,7168]{1,0:T(8,128)(2,1)S(1)}, bf16[64,7168]{1,0:T(8,128)(2,1)}, u32[]{:S(2)}, u32[]{:S(2)}) collective-permute-start(bf16[64,7168]{1,0:T(8,128)(2,1)S(1)} %pad_maximum_fusion.refs_0_), channel_id=1, source_target_pairs={{0,4},{2,6},{8,0},{10,2},{16,8},{18,10},{24,16},{26,18},{28,24},{3... | collective-permute-start | bytes 2752520 | tf_op jit(solution)/shard_map/ppermute | solution.py:308
  28.2 22.4 %collective-permute-start.2 = (bf16[64,7168]{1,0:T(8,128)(2,1)}, bf16[64,7168]{1,0:T(8,128)(2,1)}, u32[]{:S(2)}, u32[]{:S(2)}) collective-permute-start(bf16[64,7168]{1,0:T(8,128)(2,1)} %collective-permute-done.1.refs_1_), channel_id=1, source_target_pairs={{0,8},{2,10},{8,16},{10,18},{16,24},{18,26},{24,28},{26,30},{28,20... | collective-permute-start | bytes 2752520 | tf_op jit(solution)/shard_map/ppermute | solution.py:308
  30.0 21.8 %collective-permute-start.4 = (bf16[64,7168]{1,0:T(8,128)(2,1)}, bf16[64,7168]{1,0:T(8,128)(2,1)}, u32[]{:S(2)}, u32[]{:S(2)}) collective-permute-start(bf16[64,7168]{1,0:T(8,128)(2,1)} %collective-permute-done.3.refs_2_), channel_id=1, source_target_pairs={{0,4},{2,6},{8,0},{10,2},{16,8},{18,10},{24,16},{26,18},{28,24},{3... | collective-permute-start | bytes 2752520 | tf_op jit(solution)/shard_map/ppermute | solution.py:308
  30.9 26.9 %collective-permute-start.8 = (bf16[64,14336]{1,0:T(8,128)(2,1)S(1)}, bf16[64,14336]{1,0:T(8,128)(2,1)}, u32[]{:S(2)}, u32[]{:S(2)}) collective-permute-start(bf16[64,14336]{1,0:T(8,128)(2,1)S(1)} %bitcast.57), channel_id=1, source_target_pairs={{0,2},{2,0},{8,10},{10,8},{16,18},{18,16},{24,26},{26,24},{28,30},... | collective-permute-start | bytes 5505032 | tf_op jit(solution)/shard_map/ppermute | solution.py:308
  51.9 20.9 %collective-permute-start.5 = (bf16[64,7168]{1,0:T(8,128)(2,1)}, bf16[64,7168]{1,0:T(8,128)(2,1)}, u32[]{:S(2)}, u32[]{:S(2)}) collective-permute-start(bf16[64,7168]{1,0:T(8,128)(2,1)} %collective-permute-done.2.refs_3_), channel_id=1, source_target_pairs={{0,8},{2,10},{8,16},{10,18},{16,24},{18,26},{24,28},{26,30},{28,20... | collective-permute-start | bytes 2752520 | tf_op jit(solution)/shard_map/ppermute | solution.py:308
  53.5 20.6 %collective-permute-start.6 = (bf16[64,7168]{1,0:T(8,128)(2,1)}, bf16[64,7168]{1,0:T(8,128)(2,1)}, u32[]{:S(2)}, u32[]{:S(2)}) collective-permute-start(bf16[64,7168]{1,0:T(8,128)(2,1)} %collective-permute-done.4.refs_4_), channel_id=1, source_target_pairs={{0,4},{2,6},{8,0},{10,2},{16,8},{18,10},{24,16},{26,18},{28,24},{3... | collective-permute-start | bytes 2752520 | tf_op jit(solution)/shard_map/ppermute | solution.py:308
  56.0 18.1 %collective-permute-start.9 = (bf16[16,32,512]{2,1,0:T(8,128)(2,1)}, bf16[16,32,512]{2,1,0:T(8,128)(2,1)S(1)}, u32[]{:S(2)}, u32[]{:S(2)}) collective-permute-start(bf16[16,32,512]{2,1,0:T(8,128)(2,1)} %param.12), channel_id=1, source_target_pairs={{0,1},{1,0},{2,3},{3,2},{4,5},{5,4},{6,7},{7,6},{8,9},{9,8},{10,11... | collective-permute-start | bytes 1572872 | tf_op jit(solution)/shard_map/ppermute | solution.py:400
  69.8 19.4 %copy-start.3 = (f32[5,64,512]{2,1,0:T(8,128)}, f32[5,64,512]{2,1,0:T(8,128)S(1)}, u32[]{:S(2)}) copy-start(f32[5,64,512]{2,1,0:T(8,128)S(1)} %get-tuple-element.76.refs_7_.refs_3_) | copy-start | bytes 1966084
  74.1 0.8 copy-start.9
  74.9 16.5 %collective-permute-start.10 = (bf16[64,7168]{1,0:T(8,128)(2,1)}, bf16[64,7168]{1,0:T(8,128)(2,1)S(1)}, u32[]{:S(2)}, u32[]{:S(2)}) collective-permute-start(bf16[64,7168]{1,0:T(8,128)(2,1)} %collective-permute-done.5.piece), channel_id=1, source_target_pairs={{0,8},{8,16},{16,24},{24,28},{28,20},{20,12},{12,4},{4,0},{1,9},{9... | collective-permute-start | bytes 2752520 | tf_op jit(solution)/shard_map/ppermute | solution.py:419
  78.4 13.1 %collective-permute-start.11 = (bf16[64,7168]{1,0:T(8,128)(2,1)}, bf16[64,7168]{1,0:T(8,128)(2,1)S(1)}, u32[]{:S(2)}, u32[]{:S(2)}) collective-permute-start(bf16[64,7168]{1,0:T(8,128)(2,1)} %collective-permute-done.6.other), channel_id=1, source_target_pairs={{2,6},{10,2},{18,10},{26,18},{30,26},{22,30},{14,22},{6,14},{3,7},... | collective-permute-start | bytes 2752520 | tf_op jit(solution)/shard_map/ppermute | solution.py:420
  89.2 5.8 %copy-start.5 = (f32[3,64,512]{2,1,0:T(8,128)}, f32[3,64,512]{2,1,0:T(8,128)S(1)}, u32[]{:S(2)}) copy-start(f32[3,64,512]{2,1,0:T(8,128)S(1)} %get-tuple-element.99) | copy-start | bytes 1179652
  89.2 7.4 %collective-permute-start.16 = (bf16[3,64,512]{2,1,0:T(8,128)(2,1)S(1)}, bf16[3,64,512]{2,1,0:T(8,128)(2,1)S(1)}, u32[]{:S(2)}, u32[]{:S(2)}) collective-permute-start(bf16[3,64,512]{2,1,0:T(8,128)(2,1)S(1)} %get-tuple-element.85), channel_id=1, source_target_pairs={{0,1},{1,0},{2,3},{3,2},{4,5},{5,4},{6,7},{7,6},{8,9},{9,8},{10,11... | collective-permute-start | bytes 589832 | tf_op jit(solution)/shard_map/ppermute | solution.py:318
  90.8 16.3 %collective-permute-start.15 = (f32[3,64,512]{2,1,0:T(8,128)}, f32[3,64,512]{2,1,0:T(8,128)}, u32[]{:S(2)}, u32[]{:S(2)}) collective-permute-start(f32[3,64,512]{2,1,0:T(8,128)} %get-tuple-element.84), channel_id=1, source_target_pairs={{0,2},{2,0},{8,10},{10,8},{16,18},{18,16},{24,26},{26,24},{28,30},... | collective-permute-start | bytes 1179656 | tf_op jit(solution)/shard_map/ppermute | solution.py:308
  90.8 16.3 %collective-permute-start.17 = (bf16[3,64,512]{2,1,0:T(8,128)(2,1)}, bf16[3,64,512]{2,1,0:T(8,128)(2,1)}, u32[]{:S(2)}, u32[]{:S(2)}) collective-permute-start(bf16[3,64,512]{2,1,0:T(8,128)(2,1)} %get-tuple-element.86), channel_id=1, source_target_pairs={{0,3},{1,2},{2,1},{3,0},{4,7},{5,6},{6,5},{7,4},{8,11},{9,10},{10,... | collective-permute-start | bytes 589832 | tf_op jit(solution)/shard_map/ppermute | solution.py:319
  91.4 3.6 %copy-start.1 = (bf16[64,7168]{1,0:T(8,128)(2,1)}, bf16[64,7168]{1,0:T(8,128)(2,1)S(1)}, u32[]{:S(2)}) copy-start(bf16[64,7168]{1,0:T(8,128)(2,1)S(1)} %collective-permute-done.11.other) | copy-start | bytes 2752516
  95.0 12.1 %collective-permute-start.13 = (f32[2,16,64]{2,1,0:T(8,128)S(1)}, f32[2,16,64]{2,1,0:T(8,128)S(1)}, u32[]{:S(2)}, u32[]{:S(2)}) collective-permute-start(f32[2,16,64]{2,1,0:T(8,128)S(1)} %get-tuple-element.83), channel_id=1, source_target_pairs={{0,1},{1,0},{2,3},{3,2},{4,5},{5,4},{6,7},{7,6},{8,9},{9,8},{10,11... | collective-permute-start | bytes 24584 | tf_op jit(solution)/shard_map/ppermute | solution.py:318
  96.6 10.5 %collective-permute-start.14 = (f32[2,16,64]{2,1,0:T(8,128)S(1)}, f32[2,16,64]{2,1,0:T(8,128)S(1)}, u32[]{:S(2)}, u32[]{:S(2)}) collective-permute-start(f32[2,16,64]{2,1,0:T(8,128)S(1)} %get-tuple-element.83), channel_id=1, source_target_pairs={{0,3},{1,2},{2,1},{3,0},{4,7},{5,6},{6,5},{7,4},{8,11},{9,10},{10,... | collective-permute-start | bytes 24584 | tf_op jit(solution)/shard_map/ppermute | solution.py:319
  96.6 0.7 copy-start.12
  97.3 9.8 %collective-permute-start.12 = (f32[2,16,64]{2,1,0:T(8,128)S(1)}, f32[2,16,64]{2,1,0:T(8,128)S(1)}, u32[]{:S(2)}, u32[]{:S(2)}) collective-permute-start(f32[2,16,64]{2,1,0:T(8,128)S(1)} %get-tuple-element.82), channel_id=1, source_target_pairs={{0,2},{2,0},{8,10},{10,8},{16,18},{18,16},{24,26},{26,24},{28,30},... | collective-permute-start | bytes 24584 | tf_op jit(solution)/shard_map/ppermute | solution.py:308
  98.6 1.2 copy-start.2
  99.8 1.1 copy-start.4
  100.8 9.9 %copy-start.6 = (f32[3,64,512]{2,1,0:T(8,128)S(1)}, f32[3,64,512]{2,1,0:T(8,128)}, u32[]{:S(2)}) copy-start(f32[3,64,512]{2,1,0:T(8,128)} %copy-done.5) | copy-start | bytes 1179652
  100.8 9.9 %copy-start.13 = (bf16[3,64,512]{2,1,0:T(8,128)(2,1)S(1)}, bf16[3,64,512]{2,1,0:T(8,128)(2,1)}, u32[]{:S(2)}) copy-start(bf16[3,64,512]{2,1,0:T(8,128)(2,1)} %copy-done.12) | copy-start | bytes 589828
  107.0 11.8 %copy-start.8 = (bf16[256,256]{1,0:T(8,128)(2,1)S(1)}, bf16[256,256]{1,0:T(8,128)(2,1)}, u32[]{:S(2)}) copy-start(bf16[256,256]{1,0:T(8,128)(2,1)} %fusion.18) | copy-start | bytes 393220
  107.0 12.0 %copy-start.7 = (bf16[256,512]{1,0:T(8,128)(2,1)S(1)}, bf16[256,512]{1,0:T(8,128)(2,1)}, u32[]{:S(2)}) copy-start(bf16[256,512]{1,0:T(8,128)(2,1)} %compare_convert_fusion) | copy-start | bytes 786436
  107.1 12.0 %copy-start.10 = (bf16[16,32,512]{2,1,0:T(8,128)(2,1)S(1)}, bf16[16,32,512]{2,1,0:T(8,128)(2,1)}, u32[]{:S(2)}) copy-start(bf16[16,32,512]{2,1,0:T(8,128)(2,1)} %copy-done.9) | copy-start | bytes 1572868
  107.1 12.0 %copy-start.11 = (bf16[64,512]{1,0:T(8,128)(2,1)S(1)}, bf16[64,512]{1,0:T(8,128)(2,1)}, u32[]{:S(2)}) copy-start(bf16[64,512]{1,0:T(8,128)(2,1)} %fusion.20) | copy-start | bytes 196612
  107.2 6.4 %collective-permute-start.18 = (bf16[2,16,64]{2,1,0:T(8,128)(2,1)S(1)}, bf16[2,16,64]{2,1,0:T(8,128)(2,1)S(1)}, u32[]{:S(2)}, u32[]{:S(2)}) collective-permute-start(bf16[2,16,64]{2,1,0:T(8,128)(2,1)S(1)} %get-tuple-element.110), channel_id=1, source_target_pairs={{0,4},{2,6},{4,0},{6,2},{8,12},{10,14},{12,8},{14,10},{16,20},{18,... | collective-permute-start | bytes 12296 | tf_op jit(solution)/shard_map/ppermute | solution.py:461
  107.7 6.2 %collective-permute-start.19 = (bf16[2,16,64]{2,1,0:T(8,128)(2,1)S(1)}, bf16[2,16,64]{2,1,0:T(8,128)(2,1)S(1)}, u32[]{:S(2)}, u32[]{:S(2)}) collective-permute-start(bf16[2,16,64]{2,1,0:T(8,128)(2,1)S(1)} %get-tuple-element.110), channel_id=1, source_target_pairs={{0,8},{2,10},{4,12},{6,14},{8,0},{10,2},{12,4},{14,6},{16,24},{18,... | collective-permute-start | bytes 12296 | tf_op jit(solution)/shard_map/ppermute | solution.py:461
  108.8 5.1 %collective-permute-start.20 = (bf16[2,16,64]{2,1,0:T(8,128)(2,1)S(1)}, bf16[2,16,64]{2,1,0:T(8,128)(2,1)S(1)}, u32[]{:S(2)}, u32[]{:S(2)}) collective-permute-start(bf16[2,16,64]{2,1,0:T(8,128)(2,1)S(1)} %get-tuple-element.110), channel_id=1, source_target_pairs={{0,12},{2,14},{4,8},{6,10},{8,4},{10,6},{12,0},{14,2},{16,28},{18,... | collective-permute-start | bytes 12296 | tf_op jit(solution)/shard_map/ppermute | solution.py:461
  112.0 7.6 %collective-permute-start.22 = (f32[1,64,512]{2,1,0:T(8,128)S(1)}, f32[1,64,512]{2,1,0:T(8,128)S(1)}, u32[]{:S(2)}, u32[]{:S(2)}) collective-permute-start(f32[1,64,512]{2,1,0:T(8,128)S(1)} %get-tuple-element.104), channel_id=1, source_target_pairs={{0,2},{2,0},{8,10},{10,8},{16,18},{18,16},{24,26},{26,24},{28,30},... | collective-permute-start | bytes 393224 | tf_op jit(solution)/shard_map/ppermute | solution.py:308
  112.1 7.5 %collective-permute-start.23 = (bf16[1,64,512]{2,1,0:T(8,128)(2,1)S(1)}, bf16[1,64,512]{2,1,0:T(8,128)(2,1)S(1)}, u32[]{:S(2)}, u32[]{:S(2)}) collective-permute-start(bf16[1,64,512]{2,1,0:T(8,128)(2,1)S(1)} %get-tuple-element.105), channel_id=1, source_target_pairs={{0,1},{1,0},{2,3},{3,2},{4,5},{5,4},{6,7},{7,6},{8,9},{9,8},{10,11... | collective-permute-start | bytes 196616 | tf_op jit(solution)/shard_map/ppermute | solution.py:318
  113.6 5.9 %collective-permute-start.24 = (bf16[1,64,512]{2,1,0:T(8,128)(2,1)S(1)}, bf16[1,64,512]{2,1,0:T(8,128)(2,1)S(1)}, u32[]{:S(2)}, u32[]{:S(2)}) collective-permute-start(bf16[1,64,512]{2,1,0:T(8,128)(2,1)S(1)} %get-tuple-element.106), channel_id=1, source_target_pairs={{0,3},{1,2},{2,1},{3,0},{4,7},{5,6},{6,5},{7,4},{8,11},{9,10},{10,... | collective-permute-start | bytes 196616 | tf_op jit(solution)/shard_map/ppermute | solution.py:319
  113.9 4.9 %collective-permute-start.21 = (bf16[8,16,64]{2,1,0:T(8,128)(2,1)S(1)}, bf16[8,16,64]{2,1,0:T(8,128)(2,1)S(1)}, u32[]{:S(2)}, u32[]{:S(2)}) collective-permute-start(bf16[8,16,64]{2,1,0:T(8,128)(2,1)S(1)} %pad_maximum_fusion.1), channel_id=1, source_target_pairs={{0,16},{2,18},{4,20},{6,22},{8,24},{10,26},{12,28},{14,30},{16,0},... | collective-permute-start | bytes 49160 | tf_op jit(solution)/shard_map/ppermute | solution.py:461

commit v9 on v8

--- a/solution.py
+++ b/solution.py
@@ -129,14 +129,15 @@
 def middle_kernel(facts, piece, other, *refs):
     weights, factors = refs[:2], refs[2:4]
     (choices, compact_in, base, base_sib), refs = refs[4:8], refs[8:]
-    outs, compact, refs = refs[:4], refs[4], refs[5:]
+    (own, sib, compact), refs = refs[:3], refs[3:]
     sums, low, held, ready, held_low, ready_low = refs[:2], *refs[2:]
+    outs = own.at[0], sib.at[0], own.at[1], sib.at[1]
     rows_of = lambda here: jnp.concatenate([piece[:, here], other[:, here]], axis=0)
     in_flight = weight_copies(facts[0], weights, held, ready)
     in_flight_low = factor_copies(facts[0], factors, held_low, ready_low)
     weight_products(rows_of, in_flight, held, sums)
     factor_products(rows_of, in_flight_low, held_low, low)
-    pairs, group = outs[0].shape[:2]
+    pairs, group = own.shape[1:3]
     fresh = [[in_lanes(facts[0], total, index, group // 2) for total in sums] for index in (0, 1)]
     for pair in range(pairs):
         step, back = pair + 1, pairs - pair
@@ -194,7 +195,7 @@
         out_specs=[in_vmem] * len(shapes),
         out_shape=[jax.ShapeDtypeStruct(shape, kind) for shape, kind in shapes],
         scratch_shapes=scratch,
-        compiler_params=pltpu.CompilerParams(vmem_limit_bytes=40 * 2**20),
+        compiler_params=pltpu.CompilerParams(vmem_limit_bytes=(28 if weights else 8) * 2**20),
         cost_estimate=pl.CostEstimate(
             flops=total * depth * columns // 32,
             bytes_accessed=depth * columns // 16,
@@ -324,13 +325,14 @@
     block = jnp.concatenate([keep, send(give, 0, 1)], axis=0)
     right, left = send(block, 1), send(block, -1)
 
-    weight, first, block = lax.optimization_barrier(
-        (down_base_weight, first_factor_table[0], block)
-    )
+    weight, first, second_factor_table, block = lax.optimization_barrier(
+        (down_base_weight, first_factor_table[0], second_factor_table, block)
+    )
+    other_second = lax.ppermute(second_factor_table, INNER, SWAP)
     weights = (weight, send(weight, 0, 1))
     factors = (first, send(first, 0, 1))
-    home_late, row_adapter_index, second_factor_table, weights = lax.optimization_barrier(
-        (home, row_adapter_index, second_factor_table, weights)
+    home_late, row_adapter_index, weights = lax.optimization_barrier(
+        (home, row_adapter_index, weights)
     )
 
     pieces = [block, right, left]
@@ -388,17 +390,15 @@
     )
     spots = (spot == jnp.arange(owners * half, dtype=jnp.int32)[None, :]).astype(bf16)
     piece = rank // 2
-    column = jnp.arange(owners * piece, dtype=jnp.int32)[None, :]
-    mask = (slot_here == column // piece).astype(bf16)
-    copies = [
-        (jnp.arange(rank, dtype=jnp.int32)[:, None] == which * piece + column % piece).astype(bf16)
-        for which in (part, 1 - part)
-    ]
-
-    seconds = [
-        values.reshape(owners * piece, width)
-        for values in (second_factor_table, lax.ppermute(second_factor_table, INNER, SWAP))
-    ]
+    column = jnp.arange(owners * rank, dtype=jnp.int32)[None, :]
+    own_rank = jnp.bitwise_xor(part, column // (owners * piece)) * piece + column % piece
+    mask = (slot_here == column // piece % owners).astype(bf16)
+    copies = (jnp.arange(rank, dtype=jnp.int32)[:, None] == own_rank).astype(bf16)
+
+    second = jnp.concatenate(
+        [values.reshape(owners * piece, width) for values in (second_factor_table, other_second)],
+        axis=0,
+    )
 
     compact_shape = ((2, owners * MOST, rank), f32)
     early = kernel_call(
@@ -411,9 +411,9 @@
         (choices[0],),
         [((len(pieces), group_rows, width), f32)] * 2 + [compact_shape],
     )
-    ready = (facts, spots, mask, copies, choices, places, seconds)
+    ready = (facts, spots, mask, copies, choices, places, second)
     right, left, early, ready = lax.optimization_barrier((right, left, early, ready))
-    facts, spots, mask, copies, choices, places, seconds = ready
+    facts, spots, mask, copies, choices, places, second = ready
 
     last = [
         lax.ppermute(right, "wide", [(a, b) for a, b in moved(1) if a % 2 == 0]),
@@ -424,7 +424,7 @@
         shape = (pairs, group_rows, width)
         return [(shape, f32)] * 2 + [(shape, bf16)] * 2
 
-    kept_more, *more, compact = kernel_call(
+    own_more, sib_more, compact = kernel_call(
         middle_kernel,
         facts,
         (right, left),
@@ -432,9 +432,8 @@
         weights,
         factors,
         (choices[1], early[2], early[0], early[1]),
-        shares(far - 1) + [compact_shape],
-    )
-    got_more = to_three(*more)
+        [((2, far - 1, group_rows, width), f32)] * 2 + [compact_shape],
+    )
     last, compact = lax.optimization_barrier((last, compact))
 
     kept, sent = kernel_call(
@@ -447,35 +446,44 @@
         (choices[2], compact),
         [((2, half, rank), f32)] * 2,
     )
+    kept, sent, sib_more = lax.optimization_barrier((kept, sent, sib_more))
     got = to_three(kept, sent, sent)
+    low = (kept + got[1] + (got[0] + got[2])[::-1]).astype(bf16)
+
+    kept_more, out_more = [
+        a + b for a, b in zip(own_more, send(sib_more, 0, 1))
+    ]
+    out_more = out_more.astype(bf16)
+
+    def from_node(value, gap):
+        return lax.ppermute(value, "wide", [(w, w ^ (2 * gap)) for w in range(owners)])
+
+    def gather(value, gap, reach):
+        parts = [from_node(value, gap * k) for k in range(1, reach)]
+        return jnp.concatenate([value] + parts, axis=0)
+
+    low, out_more, last = lax.optimization_barrier((low, out_more, last))
+    got_more = lax.ppermute(out_more, INNER, SWAP)
+    reach = min(4, nodes)
+    low = gather(low, 1, reach)
 
     kept_one, *one = kernel_call(
         last_kernel, facts, last, group_rows, weights, (), (early[0], early[1]), shares(1)
     )
-    got, got_more, one = lax.optimization_barrier((got, got_more, one))
+    low, one, got_more = lax.optimization_barrier((low, one, got_more))
+    gap = reach
+    while gap < nodes:
+        low = gather(low, gap, 2)
+        gap *= 2
     got_one = to_three(*one)
 
-    low = (kept + got[1] + (got[0] + got[2])[::-1]).astype(bf16)
-
-    def from_node(value, gap):
-        return lax.ppermute(value, "wide", [(w, w ^ (2 * gap)) for w in range(owners)])
-
-    gap = 1
-    while gap < nodes:
-        reach = min(4, nodes // gap)
-        low = jnp.concatenate([low] + [from_node(low, gap * k) for k in range(1, reach)], axis=0)
-        gap *= reach
-
-    more = kept_more + got_more[0] + got_more[1].astype(f32) + got_more[2].astype(f32)
+    more = kept_more + got_more.astype(f32)
     rows = 0
     for pair in range(1, far):
         rows = rows + jnp.where(places[pair][:, None, None], more[pair - 1 : pair], 0)
     own_low = jnp.dot(spots, low.reshape(owners * half, rank), preferred_element_type=f32)
-    own_low = own_low.astype(bf16)
-    delta = 0
-    for copy, second in zip(copies, seconds):
-        spread = jnp.dot(own_low, copy, preferred_element_type=f32).astype(bf16) * mask
-        delta = delta + jnp.dot(spread, second, preferred_element_type=f32)
+    spread = jnp.dot(own_low.astype(bf16), copies, preferred_element_type=f32).astype(bf16) * mask
+    delta = jnp.dot(spread, second, preferred_element_type=f32)
     one = kept_one + got_one[0] + got_one[1].astype(f32) + got_one[2].astype(f32)
     rows = rows + jnp.where(places[0][:, None, None], one, 0)
     return (delta + rows.reshape(-1, width)).astype(bf16)

time: 122 us -> 131 us (1.074)
  local copies, waits for them, and re-layouts: 5.69 us -> 21.1 us
  Pallas kernels: 31.7 us -> 27.9 us
  matrix products: 2.85 us -> 1.43 us
  waiting for transfers between devices: 49.1 us -> 47.7 us
    ppermute x12, waiting for transfers between devices: 45.7 us -> 29.9 us  [send(): return lax.ppermute(value, 'wide', moved(shift, cross))]
    unnamed x35 -> x38, local copies, waits for them, and re-layouts: 3.82 us -> 18.7 us
    ppermute x1 -> x2, waiting for transfers between devices: 0.01 us -> 11.2 us  [the longest x1 11.2 us: ringed(): other_second = lax.ppermute(second_factor_table, INNER, SWAP)]
    ppermute x3 -> x2, waiting for transfers between devices: 0.01 us -> 4.18 us  [to_three(): lax.ppermute(to_mp, INNER, SWAP)]
    pallas_call x4, Pallas kernels: 31.7 us -> 27.9 us  [kernel_call(): pl.pallas_call(kernel, in_specs=[pl.BlockSpec(memory_space=pltpu.SMEM)] +...]
    ppermute x4, waiting for transfers between devices: 3.29 us -> 0.01 us  [from_node(): lax.ppermute(value, 'wide', [(w, w ^ 2 * gap) for w in range(owners)])]
    ppermute x3 -> x2, starting transfers between devices: 4.66 us -> 2.09 us  [to_three(): lax.ppermute(to_mp, INNER, SWAP)]
    ppermute x3 -> x2, waiting for transfers between devices: 0.01 us -> 2.46 us  [to_three(): lax.ppermute(to_both, ('wide',) + INNER, crossed)]
  transfers between devices with their start and end apart: 25 -> 24, of which waited for: 7 -> 10; matrix products, arithmetic and copies ran while one was open for 6% -> 6% of each run, Pallas kernels for 26% -> 19%
where the time goes in v9:
time: 131 us
  waiting for transfers between devices  47.7 us (36%)
  Pallas kernels  27.9 us (21%)
  starting transfers between devices  24.8 us (19%)
  local copies, waits for them, and re-layouts  21.1 us (16%)
  other arithmetic  7.65 us (6%)
  matrix products  1.43 us (1%)
    ppermute x12, waiting for transfers between devices, send(): return lax.ppermute(value, 'wide', moved(shift, cross))  29.9 us
    pallas_call x4, Pallas kernels, kernel_call(): pl.pallas_call(kernel, in_specs=[pl.BlockSpec(memory_space=pltpu.SMEM)] +...  27.9 us
    unnamed x38, local copies, waits for them, and re-layouts  18.7 us
    ppermute x1, waiting for transfers between devices, ringed(): other_second = lax.ppermute(second_factor_table, INNER, SWAP)  11.2 us
    ppermute x12, starting transfers between devices, send(): return lax.ppermute(value, 'wide', moved(shift, cross))  8.44 us
    ppermute x4, starting transfers between devices, from_node(): lax.ppermute(value, 'wide', [(w, w ^ 2 * gap) for w in range(owners)])  6.09 us
    ppermute x2, waiting for transfers between devices, to_three(): lax.ppermute(to_mp, INNER, SWAP)  4.18 us
    ppermute x1, starting transfers between devices, ringed(): lax.ppermute(right, 'wide', [(a, b) for a, b in moved(1) if a % 2 == 0])  3.48 us
  transfers between devices with their start and end apart: 24, of which 10 were waited for; matrix products, arithmetic and copies ran while one was open for 6% of the time, Pallas kernels for 19%

profile of v9, /device:TPU:0, one launch (start us, length us, event | category | flops | bytes accessed | tf_op | source)
XLA Modules:
  0.0 131.0 jit_solution(9777820344072811974)
XLA Ops:
  0.0 2.1 %fusion.11 = (bf16[32,7168]{1,0:T(8,128)(2,1)S(1)}, bf16[32,7168]{1,0:T(8,128)(2,1)S(1)}) fusion(bf16[32,14336]{1,0:T(8,128)(2,1)} %param.9, s32[]{:T(128)S(6)} %select_n.115, bf16[32,14336]{1,0:T(8,128)(2,1)} %param.8, s32[]{:T(128)S(6)} %select_n.116), kind=kLoop, calls=%fused_computation.21 | loop fusion | flops 3670016 | bytes 2752520 | tf_op jit(solution)/shard_map/convert_element_type | solution.py:208
  2.2 0.5 collective-permute-start
  2.7 1.4 %collective-permute-done = bf16[32,7168]{1,0:T(8,128)(2,1)S(1)} collective-permute-done((bf16[32,7168]{1,0:T(8,128)(2,1)S(1)}, bf16[32,7168]{1,0:T(8,128)(2,1)S(1)}, u32[]{:S(2)}, u32[]{:S(2)}) %collective-permute-start) | collective-permute-done | bytes 458784 | tf_op jit(solution)/shard_map/ppermute | solution.py:309
  4.2 0.4 collective-permute-start.7
  4.6 2.7 %collective-permute-start.1 = (bf16[64,7168]{1,0:T(8,128)(2,1)S(1)}, bf16[64,7168]{1,0:T(8,128)(2,1)}, u32[]{:S(2)}, u32[]{:S(2)}) collective-permute-start(bf16[64,7168]{1,0:T(8,128)(2,1)S(1)} %pad_maximum_fusion.1.refs_0_), channel_id=1, source_target_pairs={{0,8},{2,10},{8,16},{10,18},{16,24},{18,26},{24,28},{26,30},{28,20... | collective-permute-start | bytes 2752520 | tf_op jit(solution)/shard_map/ppermute | solution.py:309
  7.3 20.9 %collective-permute-done.1.refs_1_ = bf16[64,7168]{1,0:T(8,128)(2,1)} collective-permute-done((bf16[64,7168]{1,0:T(8,128)(2,1)S(1)}, bf16[64,7168]{1,0:T(8,128)(2,1)}, u32[]{:S(2)}, u32[]{:S(2)}) %collective-permute-start.1) | collective-permute-done | bytes 917536 | tf_op jit(solution)/shard_map/ppermute | solution.py:309
  28.3 1.8 %collective-permute-start.2 = (bf16[64,7168]{1,0:T(8,128)(2,1)}, bf16[64,7168]{1,0:T(8,128)(2,1)}, u32[]{:S(2)}, u32[]{:S(2)}) collective-permute-start(bf16[64,7168]{1,0:T(8,128)(2,1)} %collective-permute-done.1.refs_1_), channel_id=1, source_target_pairs={{0,8},{2,10},{8,16},{10,18},{16,24},{18,26},{24,28},{26,30},{28,20... | collective-permute-start | bytes 2752520 | tf_op jit(solution)/shard_map/ppermute | solution.py:309
  30.1 0.2 collective-permute-start.4
  30.3 1.8 %collective-permute-start.9 = (bf16[16,32,512]{2,1,0:T(8,128)(2,1)S(1)}, bf16[16,32,512]{2,1,0:T(8,128)(2,1)S(1)}, u32[]{:S(2)}, u32[]{:S(2)}) collective-permute-start(bf16[16,32,512]{2,1,0:T(8,128)(2,1)S(1)} %copy-done.15), channel_id=1, source_target_pairs={{0,1},{1,0},{2,3},{3,2},{4,5},{5,4},{6,7},{7,6},{8,9},{9,8},{10,11... | collective-permute-start | bytes 1572872 | tf_op jit(solution)/shard_map/ppermute | solution.py:331
  32.2 11.2 %collective-permute-done.9 = bf16[16,32,512]{2,1,0:T(8,128)(2,1)S(1)} collective-permute-done((bf16[16,32,512]{2,1,0:T(8,128)(2,1)S(1)}, bf16[16,32,512]{2,1,0:T(8,128)(2,1)S(1)}, u32[]{:S(2)}, u32[]{:S(2)}) %collective-permute-start.9) | collective-permute-done | bytes 524320 | tf_op jit(solution)/shard_map/ppermute | solution.py:331
  43.4 1.1 pad_maximum_fusion
  44.5 6.1 %collective-permute-done.2.refs_3_ = bf16[64,7168]{1,0:T(8,128)(2,1)} collective-permute-done((bf16[64,7168]{1,0:T(8,128)(2,1)}, bf16[64,7168]{1,0:T(8,128)(2,1)}, u32[]{:S(2)}, u32[]{:S(2)}) %collective-permute-start.2) | collective-permute-done | bytes 917536 | tf_op jit(solution)/shard_map/ppermute | solution.py:309
  50.6 1.3 collective-permute-done.4.refs_4_
  51.9 1.6 %collective-permute-start.5 = (bf16[64,7168]{1,0:T(8,128)(2,1)}, bf16[64,7168]{1,0:T(8,128)(2,1)}, u32[]{:S(2)}, u32[]{:S(2)}) collective-permute-start(bf16[64,7168]{1,0:T(8,128)(2,1)} %collective-permute-done.2.refs_3_), channel_id=1, source_target_pairs={{0,8},{2,10},{8,16},{10,18},{16,24},{18,26},{24,28},{26,30},{28,20... | collective-permute-start | bytes 2752520 | tf_op jit(solution)/shard_map/ppermute | solution.py:309
  53.5 0.4 collective-permute-start.6
  53.9 0.7 constant_dynamic-slice_fusion.2
  54.8 0.5 convert_reduce_fusion
  56.4 5.2 %copy-done = bf16[14336,512]{1,0:T(8,128)(2,1)S(1)} copy-done((bf16[14336,512]{1,0:T(8,128)(2,1)S(1)}, bf16[14336,512]{1,0:T(8,128)(2,1)}, u32[]{:S(2)}) %copy-start) | copy-done | bytes 14680088
  61.6 11.7 %shard_map.82 = (f32[5,64,512]{2,1,0:T(8,128)S(1)}, f32[5,64,512]{2,1,0:T(8,128)S(1)}, f32[2,32,64]{2,1,0:T(8,128)S(1)}) custom-call(s32[6]{0:T(128)S(1)} %pad_add_fusion.facts, bf16[64,7168]{1,0:T(8,128)(2,1)S(1)} %pad_maximum_fusion.1.refs_0_, bf16[64,7168]{1,0:T(8,128)(2,1)} %collective-permute-done.1.refs_1_, ...), custom_call_target="tpu_custom_call" | custom-call | flops 82575360 | bytes 516096 | tf_op jit(solution)/shard_map/pallas_call | solution.py:189
  73.3 0.8 fusion.18
  74.1 0.9 compare_convert_fusion
  75.1 3.5 %collective-permute-start.10 = (bf16[64,7168]{1,0:T(8,128)(2,1)}, bf16[64,7168]{1,0:T(8,128)(2,1)S(1)}, u32[]{:S(2)}, u32[]{:S(2)}) collective-permute-start(bf16[64,7168]{1,0:T(8,128)(2,1)} %collective-permute-done.5.piece), channel_id=1, source_target_pairs={{0,8},{8,16},{16,24},{24,28},{28,20},{20,12},{12,4},{4,0},{1,9},{9... | collective-permute-start | bytes 2752520 | tf_op jit(solution)/shard_map/ppermute | solution.py:419
  78.6 0.9 collective-permute-start.11
  79.5 5.2 %copy-done.1 = bf16[14336,512]{1,0:T(8,128)(2,1)S(1)} copy-done((bf16[14336,512]{1,0:T(8,128)(2,1)S(1)}, bf16[14336,512]{1,0:T(8,128)(2,1)}, u32[]{:S(2)}) %copy-start.1) | copy-done | bytes 14680088
  84.6 7.8 %shard_map.83 = (f32[2,3,64,512]{3,2,1,0:T(8,128)S(1)}, f32[2,3,64,512]{3,2,1,0:T(8,128)S(1)}, f32[2,32,64]{2,1,0:T(8,128)S(1)}) custom-call(s32[6]{0:T(128)S(1)} %pad_add_fusion.facts, bf16[64,7168]{1,0:T(8,128)(2,1)} %collective-permute-done.5.piece, bf16[64,7168]{1,0:T(8,128)(2,1)} %collective-permute-done.6.other, bf16[14336,512]{1,0:T(8,128)(2,1)S(1)} %copy-done.1, ...), custom_call_target="tpu_custom_call" | custom-call | flops 33030144 | bytes 516096 | tf_op jit(solution)/shard_map/pallas_call | solution.py:189
  92.5 3.5 %shard_map.84 = (f32[2,16,64]{2,1,0:T(8,128)S(1)}, f32[2,16,64]{2,1,0:T(8,128)S(1)}) custom-call(s32[6]{0:T(128)S(1)} %pad_add_fusion.facts, bf16[64,7168]{1,0:T(8,128)(2,1)S(1)} %collective-permute-done.10.piece, bf16[64,7168]{1,0:T(8,128)(2,1)S(1)} %collective-permute-done.11.other, bf16[64,14336]{1,0:T(8,128)(2,1)S(1)} %bitcast.63, ...), custom_call_target="tpu_custom_call" | custom-call | flops 1835008 | bytes 57344 | tf_op jit(solution)/shard_map/pallas_call | solution.py:189
  96.2 0.5 collective-permute-start.13
  96.7 1.2 collective-permute-start.14
  97.8 0.5 collective-permute-start.12
  98.4 1.4 %collective-permute-done.14 = f32[2,16,64]{2,1,0:T(8,128)S(1)} collective-permute-done((f32[2,16,64]{2,1,0:T(8,128)S(1)}, f32[2,16,64]{2,1,0:T(8,128)S(1)}, u32[]{:S(2)}, u32[]{:S(2)}) %collective-permute-start.14) | collective-permute-done | bytes 8224 | tf_op jit(solution)/shard_map/ppermute | solution.py:320
  99.8 1.7 %collective-permute-done.12 = f32[2,16,64]{2,1,0:T(8,128)S(1)} collective-permute-done((f32[2,16,64]{2,1,0:T(8,128)S(1)}, f32[2,16,64]{2,1,0:T(8,128)S(1)}, u32[]{:S(2)}, u32[]{:S(2)}) %collective-permute-start.12) | collective-permute-done | bytes 8224 | tf_op jit(solution)/shard_map/ppermute | solution.py:319
  101.7 0.8 copy-done.12
  102.5 0.4 collective-permute-start.16
  102.9 1.1 collective-permute-start.17
  104.1 1.9 %collective-permute-start.18 = (bf16[2,16,64]{2,1,0:T(8,128)(2,1)S(1)}, bf16[2,16,64]{2,1,0:T(8,128)(2,1)S(1)}, u32[]{:S(2)}, u32[]{:S(2)}) collective-permute-start(bf16[2,16,64]{2,1,0:T(8,128)(2,1)S(1)} %add_convert_fusion.3), channel_id=1, source_target_pairs={{0,12},{2,14},{4,8},{6,10},{8,4},{10,6},{12,0},{14,2},{16,28},{18,... | collective-permute-start | bytes 12296 | tf_op jit(solution)/shard_map/ppermute | solution.py:459
  106.0 0.5 collective-permute-start.19
  107.1 0.7 broadcast_in_dim.191
  107.7 5.2 %copy-done.2 = bf16[14336,512]{1,0:T(8,128)(2,1)S(1)} copy-done((bf16[14336,512]{1,0:T(8,128)(2,1)S(1)}, bf16[14336,512]{1,0:T(8,128)(2,1)}, u32[]{:S(2)}) %copy-start.2) | copy-done | bytes 14680088
  112.9 1.2 copy-done.5
  114.1 1.1 copy-done.7
  115.2 4.8 %shard_map.85 = (f32[1,64,512]{2,1,0:T(8,128)S(1)}, f32[1,64,512]{2,1,0:T(8,128)S(1)}, bf16[1,64,512]{2,1,0:T(8,128)(2,1)S(1)}, bf16[1,64,512]{2,1,0:T(8,128)(2,1)S(1)}) custom-call(s32[6]{0:T(128)S(1)} %pad_add_fusion.facts, bf16[64,7168]{1,0:T(8,128)(2,1)S(1)} %collective-permute-done.10.piece, bf16[64,7168]{1,0:T(8,128)(2,1)S(1)} %copy-done.5, ...), custom_call_target="tpu_custom_call" | custom-call | flops 14680064 | bytes 458752 | tf_op jit(solution)/shard_map/pallas_call | solution.py:189
  120.1 2.6 %collective-permute-start.20 = (bf16[8,16,64]{2,1,0:T(8,128)(2,1)S(1)}, bf16[8,16,64]{2,1,0:T(8,128)(2,1)S(1)}, u32[]{:S(2)}, u32[]{:S(2)}) collective-permute-start(bf16[8,16,64]{2,1,0:T(8,128)(2,1)S(1)} %pad_maximum_fusion.3), channel_id=1, source_target_pairs={{0,16},{2,18},{4,20},{6,22},{8,24},{10,26},{12,28},{14,30},{16,0},... | collective-permute-start | bytes 49160 | tf_op jit(solution)/shard_map/ppermute | solution.py:459
  122.7 1.0 fusion.16
  123.9 1.6 %collective-permute-start.22 = (bf16[1,64,512]{2,1,0:T(8,128)(2,1)S(1)}, bf16[1,64,512]{2,1,0:T(8,128)(2,1)S(1)}, u32[]{:S(2)}, u32[]{:S(2)}) collective-permute-start(bf16[1,64,512]{2,1,0:T(8,128)(2,1)S(1)} %get-tuple-element.103), channel_id=1, source_target_pairs={{0,1},{1,0},{2,3},{3,2},{4,5},{5,4},{6,7},{7,6},{8,9},{9,8},{10,11... | collective-permute-start | bytes 196616 | tf_op jit(solution)/shard_map/ppermute | solution.py:319
  125.4 0.3 collective-permute-start.23
  125.9 2.4 %collective-permute-done.22 = bf16[1,64,512]{2,1,0:T(8,128)(2,1)S(1)} collective-permute-done((bf16[1,64,512]{2,1,0:T(8,128)(2,1)S(1)}, bf16[1,64,512]{2,1,0:T(8,128)(2,1)S(1)}, u32[]{:S(2)}, u32[]{:S(2)}) %collective-permute-start.22) | collective-permute-done | bytes 65568 | tf_op jit(solution)/shard_map/ppermute | solution.py:319
  128.4 1.1 collective-permute-done.23
  129.8 1.3 fusion.1
  (96 shorter events, 2.9 us)
Async XLA Ops:
  0.0 30.3 %copy-start.15 = (bf16[16,32,512]{2,1,0:T(8,128)(2,1)S(1)}, bf16[16,32,512]{2,1,0:T(8,128)(2,1)}, u32[]{:S(2)}) copy-start(bf16[16,32,512]{2,1,0:T(8,128)(2,1)} %param.12) | copy-start | bytes 1572868
  0.0 32.1 %copy-start.3 = (bf16[1,64,14336]{2,1,0:T(8,128)(2,1)S(1)}, bf16[1,64,14336]{2,1,0:T(8,128)(2,1)}, u32[]{:S(2)}) copy-start(bf16[1,64,14336]{2,1,0:T(8,128)(2,1)} %param.11) | copy-start | bytes 5505028
  2.1 52.5 %copy-start.16 = (s32[512,1]{0,1:T(1,128)S(1)}, s32[512,1]{0,1:T(1,128)}, u32[]{:S(2)}) copy-start(s32[512,1]{0,1:T(1,128)} %param.13) | copy-start | bytes 6148
  2.1 52.5 %copy-start.18 = (s32[16]{0:T(128)S(1)}, s32[16]{0:T(128)}, u32[]{:S(2)}) copy-start(s32[16]{0:T(128)} %param.14) | copy-start | bytes 196
  2.2 2.0 %collective-permute-start = (bf16[32,7168]{1,0:T(8,128)(2,1)S(1)}, bf16[32,7168]{1,0:T(8,128)(2,1)S(1)}, u32[]{:S(2)}, u32[]{:S(2)}) collective-permute-start(bf16[32,7168]{1,0:T(8,128)(2,1)S(1)} %get-tuple-element.108), channel_id=1, source_target_pairs={{0,2},{2,0},{8,10},{10,8},{16,18},{18,16},{24,26},{26,24},{28,30},... | collective-permute-start | bytes 1376264 | tf_op jit(solution)/shard_map/ppermute | solution.py:309
  4.2 49.8 %collective-permute-start.7 = (bf16[14336,512]{1,0:T(8,128)(2,1)}, bf16[14336,512]{1,0:T(8,128)(2,1)}, u32[]{:S(2)}, u32[]{:S(2)}) collective-permute-start(bf16[14336,512]{1,0:T(8,128)(2,1)} %refs_0_.1), channel_id=1, source_target_pairs={{0,2},{2,0},{8,10},{10,8},{16,18},{18,16},{24,26},{26,24},{28,30},... | collective-permute-start | bytes 44040200 | tf_op jit(solution)/shard_map/ppermute | solution.py:309
  4.6 23.6 %collective-permute-start.1 = (bf16[64,7168]{1,0:T(8,128)(2,1)S(1)}, bf16[64,7168]{1,0:T(8,128)(2,1)}, u32[]{:S(2)}, u32[]{:S(2)}) collective-permute-start(bf16[64,7168]{1,0:T(8,128)(2,1)S(1)} %pad_maximum_fusion.1.refs_0_), channel_id=1, source_target_pairs={{0,8},{2,10},{8,16},{10,18},{16,24},{18,26},{24,28},{26,30},{28,20... | collective-permute-start | bytes 2752520 | tf_op jit(solution)/shard_map/ppermute | solution.py:309
  7.3 22.7 %collective-permute-start.3 = (bf16[64,7168]{1,0:T(8,128)(2,1)S(1)}, bf16[64,7168]{1,0:T(8,128)(2,1)}, u32[]{:S(2)}, u32[]{:S(2)}) collective-permute-start(bf16[64,7168]{1,0:T(8,128)(2,1)S(1)} %pad_maximum_fusion.1.refs_0_), channel_id=1, source_target_pairs={{0,4},{2,6},{8,0},{10,2},{16,8},{18,10},{24,16},{26,18},{28,24},{3... | collective-permute-start | bytes 2752520 | tf_op jit(solution)/shard_map/ppermute | solution.py:309
  28.3 22.4 %collective-permute-start.2 = (bf16[64,7168]{1,0:T(8,128)(2,1)}, bf16[64,7168]{1,0:T(8,128)(2,1)}, u32[]{:S(2)}, u32[]{:S(2)}) collective-permute-start(bf16[64,7168]{1,0:T(8,128)(2,1)} %collective-permute-done.1.refs_1_), channel_id=1, source_target_pairs={{0,8},{2,10},{8,16},{10,18},{16,24},{18,26},{24,28},{26,30},{28,20... | collective-permute-start | bytes 2752520 | tf_op jit(solution)/shard_map/ppermute | solution.py:309
  30.1 21.8 %collective-permute-start.4 = (bf16[64,7168]{1,0:T(8,128)(2,1)}, bf16[64,7168]{1,0:T(8,128)(2,1)}, u32[]{:S(2)}, u32[]{:S(2)}) collective-permute-start(bf16[64,7168]{1,0:T(8,128)(2,1)} %collective-permute-done.3.refs_2_), channel_id=1, source_target_pairs={{0,4},{2,6},{8,0},{10,2},{16,8},{18,10},{24,16},{26,18},{28,24},{3... | collective-permute-start | bytes 2752520 | tf_op jit(solution)/shard_map/ppermute | solution.py:309
  30.3 13.1 %collective-permute-start.9 = (bf16[16,32,512]{2,1,0:T(8,128)(2,1)S(1)}, bf16[16,32,512]{2,1,0:T(8,128)(2,1)S(1)}, u32[]{:S(2)}, u32[]{:S(2)}) collective-permute-start(bf16[16,32,512]{2,1,0:T(8,128)(2,1)S(1)} %copy-done.15), channel_id=1, source_target_pairs={{0,1},{1,0},{2,3},{3,2},{4,5},{5,4},{6,7},{7,6},{8,9},{9,8},{10,11... | collective-permute-start | bytes 1572872 | tf_op jit(solution)/shard_map/ppermute | solution.py:331
  32.1 24.2 %collective-permute-start.8 = (bf16[64,14336]{1,0:T(8,128)(2,1)S(1)}, bf16[64,14336]{1,0:T(8,128)(2,1)}, u32[]{:S(2)}, u32[]{:S(2)}) collective-permute-start(bf16[64,14336]{1,0:T(8,128)(2,1)S(1)} %bitcast.60), channel_id=1, source_target_pairs={{0,2},{2,0},{8,10},{10,8},{16,18},{18,16},{24,26},{26,24},{28,30},... | collective-permute-start | bytes 5505032 | tf_op jit(solution)/shard_map/ppermute | solution.py:309
  51.9 23.2 %collective-permute-start.5 = (bf16[64,7168]{1,0:T(8,128)(2,1)}, bf16[64,7168]{1,0:T(8,128)(2,1)}, u32[]{:S(2)}, u32[]{:S(2)}) collective-permute-start(bf16[64,7168]{1,0:T(8,128)(2,1)} %collective-permute-done.2.refs_3_), channel_id=1, source_target_pairs={{0,8},{2,10},{8,16},{10,18},{16,24},{18,26},{24,28},{26,30},{28,20... | collective-permute-start | bytes 2752520 | tf_op jit(solution)/shard_map/ppermute | solution.py:309
  53.5 21.6 %collective-permute-start.6 = (bf16[64,7168]{1,0:T(8,128)(2,1)}, bf16[64,7168]{1,0:T(8,128)(2,1)}, u32[]{:S(2)}, u32[]{:S(2)}) collective-permute-start(bf16[64,7168]{1,0:T(8,128)(2,1)} %collective-permute-done.4.refs_4_), channel_id=1, source_target_pairs={{0,4},{2,6},{8,0},{10,2},{16,8},{18,10},{24,16},{26,18},{28,24},{3... | collective-permute-start | bytes 2752520 | tf_op jit(solution)/shard_map/ppermute | solution.py:309
  56.4 5.2 %copy-start = (bf16[14336,512]{1,0:T(8,128)(2,1)S(1)}, bf16[14336,512]{1,0:T(8,128)(2,1)}, u32[]{:S(2)}) copy-start(bf16[14336,512]{1,0:T(8,128)(2,1)} %refs_0_.1) | copy-start | bytes 44040196
  73.3 19.2 %copy-start.6 = (f32[5,64,512]{2,1,0:T(8,128)}, f32[5,64,512]{2,1,0:T(8,128)S(1)}, u32[]{:S(2)}) copy-start(f32[5,64,512]{2,1,0:T(8,128)S(1)} %get-tuple-element.75.refs_7_.refs_3_) | copy-start | bytes 1966084
  75.1 17.4 %collective-permute-start.10 = (bf16[64,7168]{1,0:T(8,128)(2,1)}, bf16[64,7168]{1,0:T(8,128)(2,1)S(1)}, u32[]{:S(2)}, u32[]{:S(2)}) collective-permute-start(bf16[64,7168]{1,0:T(8,128)(2,1)} %collective-permute-done.5.piece), channel_id=1, source_target_pairs={{0,8},{8,16},{16,24},{24,28},{28,20},{20,12},{12,4},{4,0},{1,9},{9... | collective-permute-start | bytes 2752520 | tf_op jit(solution)/shard_map/ppermute | solution.py:419
  78.6 13.9 %collective-permute-start.11 = (bf16[64,7168]{1,0:T(8,128)(2,1)}, bf16[64,7168]{1,0:T(8,128)(2,1)S(1)}, u32[]{:S(2)}, u32[]{:S(2)}) collective-permute-start(bf16[64,7168]{1,0:T(8,128)(2,1)} %collective-permute-done.6.other), channel_id=1, source_target_pairs={{2,6},{10,2},{18,10},{26,18},{30,26},{22,30},{14,22},{6,14},{3,7},... | collective-permute-start | bytes 2752520 | tf_op jit(solution)/shard_map/ppermute | solution.py:420
  79.5 5.2 %copy-start.1 = (bf16[14336,512]{1,0:T(8,128)(2,1)S(1)}, bf16[14336,512]{1,0:T(8,128)(2,1)}, u32[]{:S(2)}) copy-start(bf16[14336,512]{1,0:T(8,128)(2,1)} %refs_0_.1) | copy-start | bytes 44040196
  92.5 9.1 %copy-start.8 = (f32[2,3,64,512]{3,2,1,0:T(8,128)}, f32[2,3,64,512]{3,2,1,0:T(8,128)S(1)}, u32[]{:S(2)}) copy-start(f32[2,3,64,512]{3,2,1,0:T(8,128)S(1)} %get-tuple-element.86) | copy-start | bytes 2359300
  92.5 3.6 %copy-start.4 = (bf16[64,7168]{1,0:T(8,128)(2,1)}, bf16[64,7168]{1,0:T(8,128)(2,1)S(1)}, u32[]{:S(2)}) copy-start(bf16[64,7168]{1,0:T(8,128)(2,1)S(1)} %collective-permute-done.11.other) | copy-start | bytes 2752516
  96.1 5.5 %collective-permute-start.15 = (f32[2,3,64,512]{3,2,1,0:T(8,128)S(1)}, f32[2,3,64,512]{3,2,1,0:T(8,128)S(1)}, u32[]{:S(2)}, u32[]{:S(2)}) collective-permute-start(f32[2,3,64,512]{3,2,1,0:T(8,128)S(1)} %get-tuple-element.87), channel_id=1, source_target_pairs={{0,2},{2,0},{8,10},{10,8},{16,18},{18,16},{24,26},{26,24},{28,30},... | collective-permute-start | bytes 2359304 | tf_op jit(solution)/shard_map/ppermute | solution.py:309
  96.2 2.3 %collective-permute-start.13 = (f32[2,16,64]{2,1,0:T(8,128)S(1)}, f32[2,16,64]{2,1,0:T(8,128)S(1)}, u32[]{:S(2)}, u32[]{:S(2)}) collective-permute-start(f32[2,16,64]{2,1,0:T(8,128)S(1)} %get-tuple-element.84), channel_id=1, source_target_pairs={{0,2},{2,0},{8,10},{10,8},{16,18},{18,16},{24,26},{26,24},{28,30},... | collective-permute-start | bytes 24584 | tf_op jit(solution)/shard_map/ppermute | solution.py:309
  96.7 3.2 %collective-permute-start.14 = (f32[2,16,64]{2,1,0:T(8,128)S(1)}, f32[2,16,64]{2,1,0:T(8,128)S(1)}, u32[]{:S(2)}, u32[]{:S(2)}) collective-permute-start(f32[2,16,64]{2,1,0:T(8,128)S(1)} %get-tuple-element.85), channel_id=1, source_target_pairs={{0,3},{1,2},{2,1},{3,0},{4,7},{5,6},{6,5},{7,4},{8,11},{9,10},{10,... | collective-permute-start | bytes 24584 | tf_op jit(solution)/shard_map/ppermute | solution.py:320
  97.8 3.7 %collective-permute-start.12 = (f32[2,16,64]{2,1,0:T(8,128)S(1)}, f32[2,16,64]{2,1,0:T(8,128)S(1)}, u32[]{:S(2)}, u32[]{:S(2)}) collective-permute-start(f32[2,16,64]{2,1,0:T(8,128)S(1)} %get-tuple-element.85), channel_id=1, source_target_pairs={{0,1},{1,0},{2,3},{3,2},{4,5},{5,4},{6,7},{7,6},{8,9},{9,8},{10,11... | collective-permute-start | bytes 24584 | tf_op jit(solution)/shard_map/ppermute | solution.py:319
  101.6 0.9 copy-start.12
  102.5 17.6 %collective-permute-start.16 = (bf16[2,16,64]{2,1,0:T(8,128)(2,1)S(1)}, bf16[2,16,64]{2,1,0:T(8,128)(2,1)S(1)}, u32[]{:S(2)}, u32[]{:S(2)}) collective-permute-start(bf16[2,16,64]{2,1,0:T(8,128)(2,1)S(1)} %add_convert_fusion.3), channel_id=1, source_target_pairs={{0,4},{2,6},{4,0},{6,2},{8,12},{10,14},{12,8},{14,10},{16,20},{18,... | collective-permute-start | bytes 12296 | tf_op jit(solution)/shard_map/ppermute | solution.py:459
  102.9 17.1 %collective-permute-start.17 = (bf16[2,16,64]{2,1,0:T(8,128)(2,1)S(1)}, bf16[2,16,64]{2,1,0:T(8,128)(2,1)S(1)}, u32[]{:S(2)}, u32[]{:S(2)}) collective-permute-start(bf16[2,16,64]{2,1,0:T(8,128)(2,1)S(1)} %add_convert_fusion.3), channel_id=1, source_target_pairs={{0,8},{2,10},{4,12},{6,14},{8,0},{10,2},{12,4},{14,6},{16,24},{18,... | collective-permute-start | bytes 12296 | tf_op jit(solution)/shard_map/ppermute | solution.py:459
  104.1 16.0 %collective-permute-start.18 = (bf16[2,16,64]{2,1,0:T(8,128)(2,1)S(1)}, bf16[2,16,64]{2,1,0:T(8,128)(2,1)S(1)}, u32[]{:S(2)}, u32[]{:S(2)}) collective-permute-start(bf16[2,16,64]{2,1,0:T(8,128)(2,1)S(1)} %add_convert_fusion.3), channel_id=1, source_target_pairs={{0,12},{2,14},{4,8},{6,10},{8,4},{10,6},{12,0},{14,2},{16,28},{18,... | collective-permute-start | bytes 12296 | tf_op jit(solution)/shard_map/ppermute | solution.py:459
  106.0 14.1 %collective-permute-start.19 = (bf16[3,64,512]{2,1,0:T(8,128)(2,1)S(1)}, bf16[3,64,512]{2,1,0:T(8,128)(2,1)}, u32[]{:S(2)}, u32[]{:S(2)}) collective-permute-start(bf16[3,64,512]{2,1,0:T(8,128)(2,1)S(1)} %fusion.20), channel_id=1, source_target_pairs={{0,1},{1,0},{2,3},{3,2},{4,5},{5,4},{6,7},{7,6},{8,9},{9,8},{10,11... | collective-permute-start | bytes 589832 | tf_op jit(solution)/shard_map/ppermute | solution.py:466
  107.7 5.2 %copy-start.2 = (bf16[14336,512]{1,0:T(8,128)(2,1)S(1)}, bf16[14336,512]{1,0:T(8,128)(2,1)}, u32[]{:S(2)}) copy-start(bf16[14336,512]{1,0:T(8,128)(2,1)} %refs_0_.1) | copy-start | bytes 44040196
  112.9 1.2 copy-start.5
  114.1 1.1 copy-start.7
  115.2 7.5 %copy-start.9 = (f32[2,3,64,512]{3,2,1,0:T(8,128)S(1)}, f32[2,3,64,512]{3,2,1,0:T(8,128)}, u32[]{:S(2)}) copy-start(f32[2,3,64,512]{3,2,1,0:T(8,128)} %copy-done.8) | copy-start | bytes 2359300
  115.2 7.5 %copy-start.13 = (f32[2,3,64,512]{3,2,1,0:T(8,128)S(1)}, f32[2,3,64,512]{3,2,1,0:T(8,128)}, u32[]{:S(2)}) copy-start(f32[2,3,64,512]{3,2,1,0:T(8,128)} %copy-done.12) | copy-start | bytes 2359300
  120.0 5.7 %copy-start.14 = (bf16[256,256]{1,0:T(8,128)(2,1)S(1)}, bf16[256,256]{1,0:T(8,128)(2,1)}, u32[]{:S(2)}) copy-start(bf16[256,256]{1,0:T(8,128)(2,1)} %fusion.18) | copy-start | bytes 393220
  120.0 9.5 %copy-start.17 = (pred[256]{0:T(512)(128)(4,1)S(1)}, pred[256]{0:T(512)(128)(4,1)}, u32[]{:S(2)}) copy-start(pred[256]{0:T(512)(128)(4,1)} %broadcast_in_dim.191) | copy-start | bytes 772
  120.0 9.7 %copy-start.10 = (bf16[1024,512]{1,0:T(8,128)(2,1)S(1)}, bf16[1024,512]{1,0:T(8,128)(2,1)}, u32[]{:S(2)}) copy-start(bf16[1024,512]{1,0:T(8,128)(2,1)} %pad_maximum_fusion) | copy-start | bytes 3145732
  120.0 9.7 %copy-start.11 = (bf16[256,1024]{1,0:T(8,128)(2,1)S(1)}, bf16[256,1024]{1,0:T(8,128)(2,1)}, u32[]{:S(2)}) copy-start(bf16[256,1024]{1,0:T(8,128)(2,1)} %compare_convert_fusion) | copy-start | bytes 1572868
  120.1 5.6 %collective-permute-start.20 = (bf16[8,16,64]{2,1,0:T(8,128)(2,1)S(1)}, bf16[8,16,64]{2,1,0:T(8,128)(2,1)S(1)}, u32[]{:S(2)}, u32[]{:S(2)}) collective-permute-start(bf16[8,16,64]{2,1,0:T(8,128)(2,1)S(1)} %pad_maximum_fusion.3), channel_id=1, source_target_pairs={{0,16},{2,18},{4,20},{6,22},{8,24},{10,26},{12,28},{14,30},{16,0},... | collective-permute-start | bytes 49160 | tf_op jit(solution)/shard_map/ppermute | solution.py:459
  123.8 5.7 %collective-permute-start.21 = (f32[1,64,512]{2,1,0:T(8,128)S(1)}, f32[1,64,512]{2,1,0:T(8,128)S(1)}, u32[]{:S(2)}, u32[]{:S(2)}) collective-permute-start(f32[1,64,512]{2,1,0:T(8,128)S(1)} %get-tuple-element.102), channel_id=1, source_target_pairs={{0,2},{2,0},{8,10},{10,8},{16,18},{18,16},{24,26},{26,24},{28,30},... | collective-permute-start | bytes 393224 | tf_op jit(solution)/shard_map/ppermute | solution.py:309
  123.9 4.5 %collective-permute-start.22 = (bf16[1,64,512]{2,1,0:T(8,128)(2,1)S(1)}, bf16[1,64,512]{2,1,0:T(8,128)(2,1)S(1)}, u32[]{:S(2)}, u32[]{:S(2)}) collective-permute-start(bf16[1,64,512]{2,1,0:T(8,128)(2,1)S(1)} %get-tuple-element.103), channel_id=1, source_target_pairs={{0,1},{1,0},{2,3},{3,2},{4,5},{5,4},{6,7},{7,6},{8,9},{9,8},{10,11... | collective-permute-start | bytes 196616 | tf_op jit(solution)/shard_map/ppermute | solution.py:319
  125.4 4.0 %collective-permute-start.23 = (bf16[1,64,512]{2,1,0:T(8,128)(2,1)S(1)}, bf16[1,64,512]{2,1,0:T(8,128)(2,1)S(1)}, u32[]{:S(2)}, u32[]{:S(2)}) collective-permute-start(bf16[1,64,512]{2,1,0:T(8,128)(2,1)S(1)} %get-tuple-element.104), channel_id=1, source_target_pairs={{0,3},{1,2},{2,1},{3,0},{4,7},{5,6},{6,5},{7,4},{8,11},{9,10},{10,... | collective-permute-start | bytes 196616 | tf_op jit(solution)/shard_map/ppermute | solution.py:320

commit v10 on v9

--- a/solution.py
+++ b/solution.py
@@ -37,10 +37,10 @@
 
 
 def factor_copies(lane, factors, held, ready):
-    rank, depth = held.shape[1:]
+    rank, depth = held.shape[0] // 2, held.shape[1]
     first = pl.multiple_of(lane * depth, 128)
     sources = [f.at[:, pl.ds(first, depth)] for f in factors]
-    return started(sources, [held.at[which] for which in (0, 1)], ready)
+    return started(sources, [held.at[pl.ds(which * rank, rank)] for which in (0, 1)], ready)
 
 
 def weight_products(rows_of, copies, held, sums):
@@ -55,7 +55,7 @@
 
 
 def factor_products(rows_of, copies, held, low):
-    rank, depth = held.shape[1:]
+    depth = held.shape[1]
     tile = tile_of(depth)
     low[...] = jnp.zeros_like(low)
     for copy in copies:
@@ -63,9 +63,8 @@
 
     def step(index, carry):
         here = pl.ds(pl.multiple_of(index * tile, 128), tile)
-        both = jnp.concatenate([held[which, :, here] for which in (0, 1)], axis=0)
         low[...] += lax.dot_general(
-            rows_of(here), both, (((1,), (1,)), ((), ())), preferred_element_type=jnp.float32
+            rows_of(here), held[:, here], (((1,), (1,)), ((), ())), preferred_element_type=jnp.float32
         )
         return carry
 
@@ -94,10 +93,6 @@
     total = picked[:, :size] + (picked[:, size : 2 * size] + picked[:, 2 * size :])
     count, rank = choice.shape[0] // 2, size // 2
     return total[:count, :rank], total[count:, rank:]
-
-
-def last_rows(lane, piece, other, here):
-    return jnp.where(lane == 0, piece[:, here], other[:, here])
 
 
 def early_kernel(count, facts, *refs):
@@ -139,19 +134,23 @@
     factor_products(rows_of, in_flight_low, held_low, low)
     pairs, group = own.shape[1:3]
     fresh = [[in_lanes(facts[0], total, index, group // 2) for total in sums] for index in (0, 1)]
+    lane = facts[0]
+    ahead = [jnp.where(lane == 0, b, a) for a, b in zip(*fresh)]
+    behind = [jnp.where(lane == 0, a, b) for a, b in zip(*fresh)]
     for pair in range(pairs):
         step, back = pair + 1, pairs - pair
-        near = fresh[1] if step == pairs else (base[2 * step], base_sib[2 * step])
-        away = fresh[0] if back == pairs else (base[2 * back - 1], base_sib[2 * back - 1])
+        near, away = 2 * step - lane, 2 * back - 1 + lane
+        near = ahead if step == pairs else (base[near], base_sib[near])
+        away = behind if back == pairs else (base[away], base_sib[away])
         share(facts[2 + step], near, away, outs, pair)
     for which, fresh_low in enumerate(compacted(choices[...], low[...])):
         compact[which] = compact_in[which] + fresh_low
 
 
-def low_kernel(facts, piece, other, *refs):
+def low_kernel(facts, piece, *refs):
     factors, (choices, compact_in, kept, sent, low, held, ready) = refs[:2], refs[2:]
     half = kept.shape[1]
-    rows_of = functools.partial(last_rows, facts[0], piece, other)
+    rows_of = lambda here: piece[:, here]
     factor_products(rows_of, factor_copies(facts[0], factors, held, ready), held, low)
     for which, fresh_low in enumerate(compacted(choices[...], low[...])):
         total = compact_in[which] + fresh_low
@@ -159,10 +158,10 @@
         sent[which] = jnp.where(facts[1] == 0, total[half:], total[:half])
 
 
-def last_kernel(facts, piece, other, *refs):
+def last_kernel(facts, piece, *refs):
     weights, (base, base_sib), refs = refs[:2], refs[2:4], refs[4:]
     outs, sums, (held, ready) = refs[:4], refs[4:6], refs[6:]
-    rows_of = functools.partial(last_rows, facts[0], piece, other)
+    rows_of = lambda here: piece[:, here]
     weight_products(rows_of, weight_copies(facts[0], weights, held, ready), held, sums)
     away = [in_lanes(facts[0], total, 0, piece.shape[0] // 2) for total in sums]
     share(facts[2], (base[0], base_sib[0]), away, outs, 0)
@@ -185,7 +184,7 @@
         scratch += [pltpu.VMEM((2, depth // tile, tile, width), jnp.bfloat16)]
         scratch += [pltpu.SemaphoreType.DMA((2 * depth // tile,))]
     if factors:
-        scratch += [pltpu.VMEM((2, rank, depth), jnp.bfloat16), pltpu.SemaphoreType.DMA((2,))]
+        scratch += [pltpu.VMEM((2 * rank, depth), jnp.bfloat16), pltpu.SemaphoreType.DMA((2,))]
     return pl.pallas_call(
         kernel,
         in_specs=[pl.BlockSpec(memory_space=pltpu.SMEM)]
@@ -195,7 +194,7 @@
         out_specs=[in_vmem] * len(shapes),
         out_shape=[jax.ShapeDtypeStruct(shape, kind) for shape, kind in shapes],
         scratch_shapes=scratch,
-        compiler_params=pltpu.CompilerParams(vmem_limit_bytes=(28 if weights else 8) * 2**20),
+        compiler_params=pltpu.CompilerParams(vmem_limit_bytes=(40 if weights else 8) * 2**20),
         cost_estimate=pl.CostEstimate(
             flops=total * depth * columns // 32,
             bytes_accessed=depth * columns // 16,
@@ -287,7 +286,8 @@
     for w in range(owners):
         p = order.index(w // 2)
         at = lambda shift: order[(p + shift) % nodes]
-        arrivals = [at(0)] + [at(s * k) for k in range(1, far) for s in (-1, 1)] + [at(far)]
+        ways = (-1, 1) if w % 2 == 0 else (1, -1)
+        arrivals = [at(0)] + [at(s * k) for k in range(1, far) for s in ways] + [at(far)]
         row = [2 * node + (w % 2 ^ side) for node in arrivals for side in (0, 1)]
         for half in (0, 1):
             here = [(at(s) < own_nodes) == (half == 0) for s in range(far)]
@@ -308,6 +308,12 @@
     def send(value, shift, cross=0):
         return lax.ppermute(value, "wide", moved(shift, cross))
 
+    def turn(value, way):
+        to_right, to_left = moved(way), moved(-way)
+        pairs = [pair for pair in to_right if pair[0] % 2 == 0]
+        pairs += [pair for pair in to_left if pair[0] % 2 == 1]
+        return lax.ppermute(value, "wide", pairs)
+
     def half_of(value, which, axis):
         return lax.dynamic_slice_in_dim(value, which * depth, depth, axis)
 
@@ -323,7 +329,7 @@
     keep = hidden_of(half_of(gate_activation, side, 1), half_of(up_activation, side, 1))
     give = hidden_of(half_of(gate_activation, 1 - side, 1), half_of(up_activation, 1 - side, 1))
     block = jnp.concatenate([keep, send(give, 0, 1)], axis=0)
-    right, left = send(block, 1), send(block, -1)
+    one_way, other_way = turn(block, 1), turn(block, -1)
 
     weight, first, second_factor_table, block = lax.optimization_barrier(
         (down_base_weight, first_factor_table[0], second_factor_table, block)
@@ -335,12 +341,12 @@
         (home, row_adapter_index, weights)
     )
 
-    pieces = [block, right, left]
+    pieces = [block, one_way, other_way]
     for step in range(2, steps + 1):
-        right, left = send(right, 1), send(left, -1)
+        one_way, other_way = turn(one_way, 1), turn(other_way, -1)
         if step < steps:
-            right, left = lax.optimization_barrier((right, left))
-            pieces += [right, left]
+            one_way, other_way = lax.optimization_barrier((one_way, other_way))
+            pieces += [one_way, other_way]
 
     row = lax.dynamic_index_in_dim(
         jnp.asarray(np.array(table, np.int32)), home_late, 0, keepdims=False
@@ -412,13 +418,12 @@
         [((len(pieces), group_rows, width), f32)] * 2 + [compact_shape],
     )
     ready = (facts, spots, mask, copies, choices, places, second)
-    right, left, early, ready = lax.optimization_barrier((right, left, early, ready))
+    one_way, other_way, early, ready = lax.optimization_barrier(
+        (one_way, other_way, early, ready)
+    )
     facts, spots, mask, copies, choices, places, second = ready
 
-    last = [
-        lax.ppermute(right, "wide", [(a, b) for a, b in moved(1) if a % 2 == 0]),
-        lax.ppermute(left, "wide", [(a, b) for a, b in moved(-1) if a % 2 == 1]),
-    ]
+    last = turn(one_way, 1)
 
     def shares(pairs):
         shape = (pairs, group_rows, width)
@@ -427,7 +432,7 @@
     own_more, sib_more, compact = kernel_call(
         middle_kernel,
         facts,
-        (right, left),
+        (one_way, other_way),
         2 * group_rows,
         weights,
         factors,
@@ -439,7 +444,7 @@
     kept, sent = kernel_call(
         low_kernel,
         facts,
-        last,
+        (last,),
         group_rows,
         (),
         factors,
@@ -468,7 +473,7 @@
     low = gather(low, 1, reach)
 
     kept_one, *one = kernel_call(
-        last_kernel, facts, last, group_rows, weights, (), (early[0], early[1]), shares(1)
+        last_kernel, facts, (last,), group_rows, weights, (), (early[0], early[1]), shares(1)
     )
     low, one, got_more = lax.optimization_barrier((low, one, got_more))
     gap = reach

time: 131 us -> 121 us (0.924)
  local copies, waits for them, and re-layouts: 21.1 us -> 3.67 us
  waiting for transfers between devices: 47.7 us -> 54.5 us
  starting transfers between devices: 24.8 us -> 21.3 us
  Pallas kernels: 27.9 us -> 30.9 us
    ppermute x2 -> x7, waiting for transfers between devices: 0.01 us -> 35 us  [turn(): return lax.ppermute(value, 'wide', pairs)]
    ppermute x12 -> x6, waiting for transfers between devices: 29.9 us -> 1.46 us  [send(): return lax.ppermute(value, 'wide', moved(shift, cross))]
    unnamed x38 -> x28, local copies, waits for them, and re-layouts: 18.7 us -> 1.26 us
    ppermute x12 -> x6, starting transfers between devices: 8.44 us -> 1.67 us  [send(): return lax.ppermute(value, 'wide', moved(shift, cross))]
    ppermute x2 -> x7, starting transfers between devices: 4.38 us -> 8.57 us  [turn(): return lax.ppermute(value, 'wide', pairs)]
    pallas_call x4, Pallas kernels: 27.9 us -> 30.9 us  [kernel_call(): pl.pallas_call(kernel, in_specs=[pl.BlockSpec(memory_space=pltpu.SMEM)] +...]
  transfers between devices with their start and end apart: 24 -> 23, of which waited for: 10 -> 11; matrix products, arithmetic and copies ran while one was open for 6% -> 6% of each run, Pallas kernels for 19% -> 23%
where the time goes in v10:
time: 121 us
  waiting for transfers between devices  54.5 us (45%)
  Pallas kernels  30.9 us (26%)
  starting transfers between devices  21.3 us (18%)
  other arithmetic  8.44 us (7%)
  local copies, waits for them, and re-layouts  3.67 us (3%)
  matrix products  1.42 us (1%)
    ppermute x7, waiting for transfers between devices, turn(): return lax.ppermute(value, 'wide', pairs)  35 us
    pallas_call x4, Pallas kernels, kernel_call(): pl.pallas_call(kernel, in_specs=[pl.BlockSpec(memory_space=pltpu.SMEM)] +...  30.9 us
    ppermute x1, waiting for transfers between devices, ringed(): other_second = lax.ppermute(second_factor_table, INNER, SWAP)  11.2 us
    ppermute x7, starting transfers between devices, turn(): return lax.ppermute(value, 'wide', pairs)  8.57 us
    ppermute x4, starting transfers between devices, from_node(): lax.ppermute(value, 'wide', [(w, w ^ 2 * gap) for w in range(owners)])  4.85 us
    ppermute x2, waiting for transfers between devices, to_three(): lax.ppermute(to_mp, INNER, SWAP)  4.19 us
  transfers between devices with their start and end apart: 23, of which 11 were waited for; matrix products, arithmetic and copies ran while one was open for 6% of the time, Pallas kernels for 23%

profile of v10, /device:TPU:0, one launch (start us, length us, event | category | flops | bytes accessed | tf_op | source)
XLA Modules:
  0.0 120.6 jit_solution(331101293094379728)
XLA Ops:
  0.0 2.1 %fusion.11 = (bf16[32,7168]{1,0:T(8,128)(2,1)S(1)}, bf16[32,7168]{1,0:T(8,128)(2,1)S(1)}) fusion(bf16[32,14336]{1,0:T(8,128)(2,1)} %param.9, s32[]{:T(128)S(6)} %select_n.115, bf16[32,14336]{1,0:T(8,128)(2,1)} %param.8, s32[]{:T(128)S(6)} %select_n.116), kind=kLoop, calls=%fused_computation.21 | loop fusion | flops 3670016 | bytes 2752520 | tf_op jit(solution)/shard_map/convert_element_type | solution.py:207
  2.2 0.5 collective-permute-start
  2.7 1.4 %collective-permute-done = bf16[32,7168]{1,0:T(8,128)(2,1)S(1)} collective-permute-done((bf16[32,7168]{1,0:T(8,128)(2,1)S(1)}, bf16[32,7168]{1,0:T(8,128)(2,1)S(1)}, u32[]{:S(2)}, u32[]{:S(2)}) %collective-permute-start) | collective-permute-done | bytes 458784 | tf_op jit(solution)/shard_map/ppermute | solution.py:309
  4.2 0.4 collective-permute-start.7
  4.6 2.7 %collective-permute-start.1 = (bf16[64,7168]{1,0:T(8,128)(2,1)S(1)}, bf16[64,7168]{1,0:T(8,128)(2,1)}, u32[]{:S(2)}, u32[]{:S(2)}) collective-permute-start(bf16[64,7168]{1,0:T(8,128)(2,1)S(1)} %pad_maximum_fusion.1.refs_0_), channel_id=1, source_target_pairs={{0,8},{8,16},{16,24},{24,28},{28,20},{20,12},{12,4},{4,0},{2,6},{1... | collective-permute-start | bytes 2752520 | tf_op jit(solution)/shard_map/ppermute | solution.py:315
  7.3 20.1 %collective-permute-done.1.refs_1_ = bf16[64,7168]{1,0:T(8,128)(2,1)} collective-permute-done((bf16[64,7168]{1,0:T(8,128)(2,1)S(1)}, bf16[64,7168]{1,0:T(8,128)(2,1)}, u32[]{:S(2)}, u32[]{:S(2)}) %collective-permute-start.1) | collective-permute-done | bytes 917536 | tf_op jit(solution)/shard_map/ppermute | solution.py:315
  27.5 2.6 %collective-permute-start.2 = (bf16[64,7168]{1,0:T(8,128)(2,1)}, bf16[64,7168]{1,0:T(8,128)(2,1)}, u32[]{:S(2)}, u32[]{:S(2)}) collective-permute-start(bf16[64,7168]{1,0:T(8,128)(2,1)} %collective-permute-done.1.refs_1_), channel_id=1, source_target_pairs={{0,8},{8,16},{16,24},{24,28},{28,20},{20,12},{12,4},{4,0},{2,6},{1... | collective-permute-start | bytes 2752520 | tf_op jit(solution)/shard_map/ppermute | solution.py:315
  30.1 2.0 %collective-permute-start.9 = (bf16[16,32,512]{2,1,0:T(8,128)(2,1)S(1)}, bf16[16,32,512]{2,1,0:T(8,128)(2,1)S(1)}, u32[]{:S(2)}, u32[]{:S(2)}) collective-permute-start(bf16[16,32,512]{2,1,0:T(8,128)(2,1)S(1)} %copy-done.10), channel_id=1, source_target_pairs={{0,1},{1,0},{2,3},{3,2},{4,5},{5,4},{6,7},{7,6},{8,9},{9,8},{10,11... | collective-permute-start | bytes 1572872 | tf_op jit(solution)/shard_map/ppermute | solution.py:337
  32.2 11.2 %collective-permute-done.9 = bf16[16,32,512]{2,1,0:T(8,128)(2,1)S(1)} collective-permute-done((bf16[16,32,512]{2,1,0:T(8,128)(2,1)S(1)}, bf16[16,32,512]{2,1,0:T(8,128)(2,1)S(1)}, u32[]{:S(2)}, u32[]{:S(2)}) %collective-permute-start.9) | collective-permute-done | bytes 524320 | tf_op jit(solution)/shard_map/ppermute | solution.py:337
  43.4 1.1 pad_maximum_fusion
  44.4 6.7 %collective-permute-done.2.refs_3_ = bf16[64,7168]{1,0:T(8,128)(2,1)} collective-permute-done((bf16[64,7168]{1,0:T(8,128)(2,1)}, bf16[64,7168]{1,0:T(8,128)(2,1)}, u32[]{:S(2)}, u32[]{:S(2)}) %collective-permute-start.2) | collective-permute-done | bytes 917536 | tf_op jit(solution)/shard_map/ppermute | solution.py:315
  51.1 1.1 collective-permute-start.5
  52.2 1.0 collective-permute-start.6
  53.2 0.7 constant_dynamic-slice_fusion.2
  54.0 0.5 convert_reduce_fusion
  54.6 0.1 select_reduce_fusion
  55.6 12.0 %shard_map.82 = (f32[5,64,512]{2,1,0:T(8,128)S(1)}, f32[5,64,512]{2,1,0:T(8,128)S(1)}, f32[2,32,64]{2,1,0:T(8,128)S(1)}) custom-call(s32[6]{0:T(128)S(1)} %pad_add_fusion.facts, bf16[64,7168]{1,0:T(8,128)(2,1)S(1)} %pad_maximum_fusion.1.refs_0_, bf16[64,7168]{1,0:T(8,128)(2,1)} %collective-permute-done.1.refs_1_, ...), custom_call_target="tpu_custom_call" | custom-call | flops 82575360 | bytes 516096 | tf_op jit(solution)/shard_map/pallas_call | solution.py:188
  67.7 0.8 fusion.18
  68.5 1.0 compare_convert_fusion
  69.5 4.9 %collective-permute-done.5.piece = bf16[64,7168]{1,0:T(8,128)(2,1)} collective-permute-done((bf16[64,7168]{1,0:T(8,128)(2,1)}, bf16[64,7168]{1,0:T(8,128)(2,1)}, u32[]{:S(2)}, u32[]{:S(2)}) %collective-permute-start.5) | collective-permute-done | bytes 917536 | tf_op jit(solution)/shard_map/ppermute | solution.py:315
  74.4 1.2 %collective-permute-start.10 = (bf16[64,7168]{1,0:T(8,128)(2,1)}, bf16[64,7168]{1,0:T(8,128)(2,1)S(1)}, u32[]{:S(2)}, u32[]{:S(2)}) collective-permute-start(bf16[64,7168]{1,0:T(8,128)(2,1)} %collective-permute-done.5.piece), channel_id=1, source_target_pairs={{0,8},{8,16},{16,24},{24,28},{28,20},{20,12},{12,4},{4,0},{2,6},{1... | collective-permute-start | bytes 2752520 | tf_op jit(solution)/shard_map/ppermute | solution.py:315
  75.6 9.2 %shard_map.83 = (f32[2,3,64,512]{3,2,1,0:T(8,128)S(1)}, f32[2,3,64,512]{3,2,1,0:T(8,128)S(1)}, f32[2,32,64]{2,1,0:T(8,128)S(1)}) custom-call(s32[6]{0:T(128)S(1)} %pad_add_fusion.facts, bf16[64,7168]{1,0:T(8,128)(2,1)} %collective-permute-done.5.piece, bf16[64,7168]{1,0:T(8,128)(2,1)} %collective-permute-done.6.other, bf16[14336,512]{1,0:T(8,128)(2,1)} %refs_0_.1, ...), custom_call_target="tpu_custom_call" | custom-call | flops 33030144 | bytes 516096 | tf_op jit(solution)/shard_map/pallas_call | solution.py:188
  84.8 3.3 %collective-permute-done.10.piece = bf16[64,7168]{1,0:T(8,128)(2,1)S(1)} collective-permute-done((bf16[64,7168]{1,0:T(8,128)(2,1)}, bf16[64,7168]{1,0:T(8,128)(2,1)S(1)}, u32[]{:S(2)}, u32[]{:S(2)}) %collective-permute-start.10) | collective-permute-done | bytes 917536 | tf_op jit(solution)/shard_map/ppermute | solution.py:315
  88.1 3.5 %shard_map.84 = (f32[2,16,64]{2,1,0:T(8,128)S(1)}, f32[2,16,64]{2,1,0:T(8,128)S(1)}) custom-call(s32[6]{0:T(128)S(1)} %pad_add_fusion.facts, bf16[64,7168]{1,0:T(8,128)(2,1)S(1)} %collective-permute-done.10.piece, bf16[64,14336]{1,0:T(8,128)(2,1)S(1)} %bitcast.63, bf16[64,14336]{1,0:T(8,128)(2,1)} %collective-permute-done.8.refs_8_.refs_3_.refs_1_, ...), custom_call_target="tpu_custom_call" | custom-call | flops 1835008 | bytes 57344 | tf_op jit(solution)/shard_map/pallas_call | solution.py:188
  91.7 0.5 collective-permute-start.12
  92.2 1.7 %collective-permute-start.13 = (f32[2,16,64]{2,1,0:T(8,128)S(1)}, f32[2,16,64]{2,1,0:T(8,128)S(1)}, u32[]{:S(2)}, u32[]{:S(2)}) collective-permute-start(f32[2,16,64]{2,1,0:T(8,128)S(1)} %get-tuple-element.82), channel_id=1, source_target_pairs={{0,3},{1,2},{2,1},{3,0},{4,7},{5,6},{6,5},{7,4},{8,11},{9,10},{10,... | collective-permute-start | bytes 24584 | tf_op jit(solution)/shard_map/ppermute | solution.py:326
  93.9 0.3 collective-permute-start.11
  94.2 1.2 collective-permute-done.13
  95.4 2.2 %collective-permute-done.11 = f32[2,16,64]{2,1,0:T(8,128)S(1)} collective-permute-done((f32[2,16,64]{2,1,0:T(8,128)S(1)}, f32[2,16,64]{2,1,0:T(8,128)S(1)}, u32[]{:S(2)}, u32[]{:S(2)}) %collective-permute-start.11) | collective-permute-done | bytes 8224 | tf_op jit(solution)/shard_map/ppermute | solution.py:325
  97.6 0.8 fusion.20
  98.5 0.1 copy-done.7
  98.6 1.5 %collective-permute-start.15 = (bf16[2,16,64]{2,1,0:T(8,128)(2,1)S(1)}, bf16[2,16,64]{2,1,0:T(8,128)(2,1)S(1)}, u32[]{:S(2)}, u32[]{:S(2)}) collective-permute-start(bf16[2,16,64]{2,1,0:T(8,128)(2,1)S(1)} %add_convert_fusion.3), channel_id=1, source_target_pairs={{0,4},{2,6},{4,0},{6,2},{8,12},{10,14},{12,8},{14,10},{16,20},{18,... | collective-permute-start | bytes 12296 | tf_op jit(solution)/shard_map/ppermute | solution.py:464
  100.1 1.6 %collective-permute-start.16 = (bf16[2,16,64]{2,1,0:T(8,128)(2,1)S(1)}, bf16[2,16,64]{2,1,0:T(8,128)(2,1)S(1)}, u32[]{:S(2)}, u32[]{:S(2)}) collective-permute-start(bf16[2,16,64]{2,1,0:T(8,128)(2,1)S(1)} %add_convert_fusion.3), channel_id=1, source_target_pairs={{0,8},{2,10},{4,12},{6,14},{8,0},{10,2},{12,4},{14,6},{16,24},{18,... | collective-permute-start | bytes 12296 | tf_op jit(solution)/shard_map/ppermute | solution.py:464
  101.7 0.4 collective-permute-start.17
  102.1 0.3 collective-permute-start.18
  103.0 0.6 broadcast_in_dim.191
  103.6 1.1 copy-done.2
  104.7 6.2 %shard_map.85 = (f32[1,64,512]{2,1,0:T(8,128)S(1)}, f32[1,64,512]{2,1,0:T(8,128)S(1)}, bf16[1,64,512]{2,1,0:T(8,128)(2,1)S(1)}, bf16[1,64,512]{2,1,0:T(8,128)(2,1)S(1)}) custom-call(s32[6]{0:T(128)S(1)} %pad_add_fusion.facts, bf16[64,7168]{1,0:T(8,128)(2,1)S(1)} %collective-permute-done.10.piece, bf16[14336,512]{1,0:T(8,128)(2,1)} %refs_0_.1, ...), custom_call_target="tpu_custom_call" | custom-call | flops 14680064 | bytes 458752 | tf_op jit(solution)/shard_map/pallas_call | solution.py:188
  111.0 1.4 %collective-permute-start.19 = (bf16[8,16,64]{2,1,0:T(8,128)(2,1)S(1)}, bf16[8,16,64]{2,1,0:T(8,128)(2,1)S(1)}, u32[]{:S(2)}, u32[]{:S(2)}) collective-permute-start(bf16[8,16,64]{2,1,0:T(8,128)(2,1)S(1)} %pad_maximum_fusion.3), channel_id=1, source_target_pairs={{0,16},{2,18},{4,20},{6,22},{8,24},{10,26},{12,28},{14,30},{16,0},... | collective-permute-start | bytes 49160 | tf_op jit(solution)/shard_map/ppermute | solution.py:464
  112.4 1.0 fusion.16
  113.5 1.5 %collective-permute-start.21 = (bf16[1,64,512]{2,1,0:T(8,128)(2,1)S(1)}, bf16[1,64,512]{2,1,0:T(8,128)(2,1)S(1)}, u32[]{:S(2)}, u32[]{:S(2)}) collective-permute-start(bf16[1,64,512]{2,1,0:T(8,128)(2,1)S(1)} %get-tuple-element.99), channel_id=1, source_target_pairs={{0,1},{1,0},{2,3},{3,2},{4,5},{5,4},{6,7},{7,6},{8,9},{9,8},{10,11... | collective-permute-start | bytes 196616 | tf_op jit(solution)/shard_map/ppermute | solution.py:325
  115.0 0.4 collective-permute-start.22
  115.4 0.5 collective-permute-done.19
  115.9 0.2 convolution_convert_fusion.1
  116.1 2.0 %collective-permute-done.21 = bf16[1,64,512]{2,1,0:T(8,128)(2,1)S(1)} collective-permute-done((bf16[1,64,512]{2,1,0:T(8,128)(2,1)S(1)}, bf16[1,64,512]{2,1,0:T(8,128)(2,1)S(1)}, u32[]{:S(2)}, u32[]{:S(2)}) %collective-permute-start.21) | collective-permute-done | bytes 65568 | tf_op jit(solution)/shard_map/ppermute | solution.py:325
  118.0 1.0 collective-permute-done.22
  119.1 0.2 fusion.12
  119.4 1.3 %fusion.1 = bf16[256,512]{1,0:T(8,128)(2,1)} fusion(f32[256,512]{1,0:T(8,128)S(1)} %fusion.12, bf16[1024,512]{1,0:T(8,128)(2,1)S(1)} %copy-done.5, bf16[256,1024]{1,0:T(8,128)(2,1)S(1)} %copy-done.6, bf16[256,64]{1,0:T(8,128)(2,1)S(1)} %convolution_convert_fusion.1, bf16[64,1024]{1,0:T(8,128)(2,1)S(1)} %fusion.19), kind=kOutput, calls=%fused_computation.3 | convolution fusion | flops 302776320 | bytes 2523136 | tf_op jit(solution)/shard_map/dot_general | solution.py:491
  (84 shorter events, 2.2 us)
Async XLA Ops:
  0.0 30.1 %copy-start.10 = (bf16[16,32,512]{2,1,0:T(8,128)(2,1)S(1)}, bf16[16,32,512]{2,1,0:T(8,128)(2,1)}, u32[]{:S(2)}) copy-start(bf16[16,32,512]{2,1,0:T(8,128)(2,1)} %param.12) | copy-start | bytes 1572868
  0.0 32.1 %copy-start = (bf16[1,64,14336]{2,1,0:T(8,128)(2,1)S(1)}, bf16[1,64,14336]{2,1,0:T(8,128)(2,1)}, u32[]{:S(2)}) copy-start(bf16[1,64,14336]{2,1,0:T(8,128)(2,1)} %param.11) | copy-start | bytes 5505028
  2.1 51.7 %copy-start.11 = (s32[512,1]{0,1:T(1,128)S(1)}, s32[512,1]{0,1:T(1,128)}, u32[]{:S(2)}) copy-start(s32[512,1]{0,1:T(1,128)} %param.13) | copy-start | bytes 6148
  2.1 51.7 %copy-start.13 = (s32[16]{0:T(128)S(1)}, s32[16]{0:T(128)}, u32[]{:S(2)}) copy-start(s32[16]{0:T(128)} %param.14) | copy-start | bytes 196
  2.2 2.0 %collective-permute-start = (bf16[32,7168]{1,0:T(8,128)(2,1)S(1)}, bf16[32,7168]{1,0:T(8,128)(2,1)S(1)}, u32[]{:S(2)}, u32[]{:S(2)}) collective-permute-start(bf16[32,7168]{1,0:T(8,128)(2,1)S(1)} %get-tuple-element.104), channel_id=1, source_target_pairs={{0,2},{2,0},{8,10},{10,8},{16,18},{18,16},{24,26},{26,24},{28,30},... | collective-permute-start | bytes 1376264 | tf_op jit(solution)/shard_map/ppermute | solution.py:309
  4.2 49.0 %collective-permute-start.7 = (bf16[14336,512]{1,0:T(8,128)(2,1)}, bf16[14336,512]{1,0:T(8,128)(2,1)}, u32[]{:S(2)}, u32[]{:S(2)}) collective-permute-start(bf16[14336,512]{1,0:T(8,128)(2,1)} %refs_0_.1), channel_id=1, source_target_pairs={{0,2},{2,0},{8,10},{10,8},{16,18},{18,16},{24,26},{26,24},{28,30},... | collective-permute-start | bytes 44040200 | tf_op jit(solution)/shard_map/ppermute | solution.py:309
  4.6 22.9 %collective-permute-start.1 = (bf16[64,7168]{1,0:T(8,128)(2,1)S(1)}, bf16[64,7168]{1,0:T(8,128)(2,1)}, u32[]{:S(2)}, u32[]{:S(2)}) collective-permute-start(bf16[64,7168]{1,0:T(8,128)(2,1)S(1)} %pad_maximum_fusion.1.refs_0_), channel_id=1, source_target_pairs={{0,8},{8,16},{16,24},{24,28},{28,20},{20,12},{12,4},{4,0},{2,6},{1... | collective-permute-start | bytes 2752520 | tf_op jit(solution)/shard_map/ppermute | solution.py:315
  7.3 22.7 %collective-permute-start.3 = (bf16[64,7168]{1,0:T(8,128)(2,1)S(1)}, bf16[64,7168]{1,0:T(8,128)(2,1)}, u32[]{:S(2)}, u32[]{:S(2)}) collective-permute-start(bf16[64,7168]{1,0:T(8,128)(2,1)S(1)} %pad_maximum_fusion.1.refs_0_), channel_id=1, source_target_pairs={{0,4},{8,0},{16,8},{24,16},{28,24},{20,28},{12,20},{4,12},{2,10},{... | collective-permute-start | bytes 2752520 | tf_op jit(solution)/shard_map/ppermute | solution.py:315
  27.5 23.7 %collective-permute-start.2 = (bf16[64,7168]{1,0:T(8,128)(2,1)}, bf16[64,7168]{1,0:T(8,128)(2,1)}, u32[]{:S(2)}, u32[]{:S(2)}) collective-permute-start(bf16[64,7168]{1,0:T(8,128)(2,1)} %collective-permute-done.1.refs_1_), channel_id=1, source_target_pairs={{0,8},{8,16},{16,24},{24,28},{28,20},{20,12},{12,4},{4,0},{2,6},{1... | collective-permute-start | bytes 2752520 | tf_op jit(solution)/shard_map/ppermute | solution.py:315
  30.1 21.1 %collective-permute-start.4 = (bf16[64,7168]{1,0:T(8,128)(2,1)}, bf16[64,7168]{1,0:T(8,128)(2,1)}, u32[]{:S(2)}, u32[]{:S(2)}) collective-permute-start(bf16[64,7168]{1,0:T(8,128)(2,1)} %collective-permute-done.3.refs_2_), channel_id=1, source_target_pairs={{0,4},{8,0},{16,8},{24,16},{28,24},{20,28},{12,20},{4,12},{2,10},{... | collective-permute-start | bytes 2752520 | tf_op jit(solution)/shard_map/ppermute | solution.py:315
  30.1 13.3 %collective-permute-start.9 = (bf16[16,32,512]{2,1,0:T(8,128)(2,1)S(1)}, bf16[16,32,512]{2,1,0:T(8,128)(2,1)S(1)}, u32[]{:S(2)}, u32[]{:S(2)}) collective-permute-start(bf16[16,32,512]{2,1,0:T(8,128)(2,1)S(1)} %copy-done.10), channel_id=1, source_target_pairs={{0,1},{1,0},{2,3},{3,2},{4,5},{5,4},{6,7},{7,6},{8,9},{9,8},{10,11... | collective-permute-start | bytes 1572872 | tf_op jit(solution)/shard_map/ppermute | solution.py:337
  32.1 23.4 %collective-permute-start.8 = (bf16[64,14336]{1,0:T(8,128)(2,1)S(1)}, bf16[64,14336]{1,0:T(8,128)(2,1)}, u32[]{:S(2)}, u32[]{:S(2)}) collective-permute-start(bf16[64,14336]{1,0:T(8,128)(2,1)S(1)} %bitcast.60), channel_id=1, source_target_pairs={{0,2},{2,0},{8,10},{10,8},{16,18},{18,16},{24,26},{26,24},{28,30},... | collective-permute-start | bytes 5505032 | tf_op jit(solution)/shard_map/ppermute | solution.py:309
  51.1 23.2 %collective-permute-start.5 = (bf16[64,7168]{1,0:T(8,128)(2,1)}, bf16[64,7168]{1,0:T(8,128)(2,1)}, u32[]{:S(2)}, u32[]{:S(2)}) collective-permute-start(bf16[64,7168]{1,0:T(8,128)(2,1)} %collective-permute-done.2.refs_3_), channel_id=1, source_target_pairs={{0,8},{8,16},{16,24},{24,28},{28,20},{20,12},{12,4},{4,0},{2,6},{1... | collective-permute-start | bytes 2752520 | tf_op jit(solution)/shard_map/ppermute | solution.py:315
  52.2 22.2 %collective-permute-start.6 = (bf16[64,7168]{1,0:T(8,128)(2,1)}, bf16[64,7168]{1,0:T(8,128)(2,1)}, u32[]{:S(2)}, u32[]{:S(2)}) collective-permute-start(bf16[64,7168]{1,0:T(8,128)(2,1)} %collective-permute-done.4.refs_4_), channel_id=1, source_target_pairs={{0,4},{8,0},{16,8},{24,16},{28,24},{20,28},{12,20},{4,12},{2,10},{... | collective-permute-start | bytes 2752520 | tf_op jit(solution)/shard_map/ppermute | solution.py:315
  67.6 17.2 %copy-start.1 = (f32[5,64,512]{2,1,0:T(8,128)}, f32[5,64,512]{2,1,0:T(8,128)S(1)}, u32[]{:S(2)}) copy-start(f32[5,64,512]{2,1,0:T(8,128)S(1)} %get-tuple-element.73.refs_7_.refs_3_) | copy-start | bytes 1966084
  74.4 13.7 %collective-permute-start.10 = (bf16[64,7168]{1,0:T(8,128)(2,1)}, bf16[64,7168]{1,0:T(8,128)(2,1)S(1)}, u32[]{:S(2)}, u32[]{:S(2)}) collective-permute-start(bf16[64,7168]{1,0:T(8,128)(2,1)} %collective-permute-done.5.piece), channel_id=1, source_target_pairs={{0,8},{8,16},{16,24},{24,28},{28,20},{20,12},{12,4},{4,0},{2,6},{1... | collective-permute-start | bytes 2752520 | tf_op jit(solution)/shard_map/ppermute | solution.py:315
  84.8 12.8 %copy-start.3 = (f32[2,3,64,512]{3,2,1,0:T(8,128)}, f32[2,3,64,512]{3,2,1,0:T(8,128)S(1)}, u32[]{:S(2)}) copy-start(f32[2,3,64,512]{3,2,1,0:T(8,128)S(1)} %get-tuple-element.83) | copy-start | bytes 2359300
  91.6 6.0 %collective-permute-start.14 = (f32[2,3,64,512]{3,2,1,0:T(8,128)S(1)}, f32[2,3,64,512]{3,2,1,0:T(8,128)S(1)}, u32[]{:S(2)}, u32[]{:S(2)}) collective-permute-start(f32[2,3,64,512]{3,2,1,0:T(8,128)S(1)} %get-tuple-element.84), channel_id=1, source_target_pairs={{0,2},{2,0},{8,10},{10,8},{16,18},{18,16},{24,26},{26,24},{28,30},... | collective-permute-start | bytes 2359304 | tf_op jit(solution)/shard_map/ppermute | solution.py:309
  91.7 2.5 %collective-permute-start.12 = (f32[2,16,64]{2,1,0:T(8,128)S(1)}, f32[2,16,64]{2,1,0:T(8,128)S(1)}, u32[]{:S(2)}, u32[]{:S(2)}) collective-permute-start(f32[2,16,64]{2,1,0:T(8,128)S(1)} %get-tuple-element.81), channel_id=1, source_target_pairs={{0,2},{2,0},{8,10},{10,8},{16,18},{18,16},{24,26},{26,24},{28,30},... | collective-permute-start | bytes 24584 | tf_op jit(solution)/shard_map/ppermute | solution.py:309
  92.2 3.2 %collective-permute-start.13 = (f32[2,16,64]{2,1,0:T(8,128)S(1)}, f32[2,16,64]{2,1,0:T(8,128)S(1)}, u32[]{:S(2)}, u32[]{:S(2)}) collective-permute-start(f32[2,16,64]{2,1,0:T(8,128)S(1)} %get-tuple-element.82), channel_id=1, source_target_pairs={{0,3},{1,2},{2,1},{3,0},{4,7},{5,6},{6,5},{7,4},{8,11},{9,10},{10,... | collective-permute-start | bytes 24584 | tf_op jit(solution)/shard_map/ppermute | solution.py:326
  93.9 3.7 %collective-permute-start.11 = (f32[2,16,64]{2,1,0:T(8,128)S(1)}, f32[2,16,64]{2,1,0:T(8,128)S(1)}, u32[]{:S(2)}, u32[]{:S(2)}) collective-permute-start(f32[2,16,64]{2,1,0:T(8,128)S(1)} %get-tuple-element.82), channel_id=1, source_target_pairs={{0,1},{1,0},{2,3},{3,2},{4,5},{5,4},{6,7},{7,6},{8,9},{9,8},{10,11... | collective-permute-start | bytes 24584 | tf_op jit(solution)/shard_map/ppermute | solution.py:325
  97.6 1.0 copy-start.7
  98.6 12.4 %collective-permute-start.15 = (bf16[2,16,64]{2,1,0:T(8,128)(2,1)S(1)}, bf16[2,16,64]{2,1,0:T(8,128)(2,1)S(1)}, u32[]{:S(2)}, u32[]{:S(2)}) collective-permute-start(bf16[2,16,64]{2,1,0:T(8,128)(2,1)S(1)} %add_convert_fusion.3), channel_id=1, source_target_pairs={{0,4},{2,6},{4,0},{6,2},{8,12},{10,14},{12,8},{14,10},{16,20},{18,... | collective-permute-start | bytes 12296 | tf_op jit(solution)/shard_map/ppermute | solution.py:464
  100.1 10.8 %collective-permute-start.16 = (bf16[2,16,64]{2,1,0:T(8,128)(2,1)S(1)}, bf16[2,16,64]{2,1,0:T(8,128)(2,1)S(1)}, u32[]{:S(2)}, u32[]{:S(2)}) collective-permute-start(bf16[2,16,64]{2,1,0:T(8,128)(2,1)S(1)} %add_convert_fusion.3), channel_id=1, source_target_pairs={{0,8},{2,10},{4,12},{6,14},{8,0},{10,2},{12,4},{14,6},{16,24},{18,... | collective-permute-start | bytes 12296 | tf_op jit(solution)/shard_map/ppermute | solution.py:464
  101.7 9.3 %collective-permute-start.17 = (bf16[2,16,64]{2,1,0:T(8,128)(2,1)S(1)}, bf16[2,16,64]{2,1,0:T(8,128)(2,1)S(1)}, u32[]{:S(2)}, u32[]{:S(2)}) collective-permute-start(bf16[2,16,64]{2,1,0:T(8,128)(2,1)S(1)} %add_convert_fusion.3), channel_id=1, source_target_pairs={{0,12},{2,14},{4,8},{6,10},{8,4},{10,6},{12,0},{14,2},{16,28},{18,... | collective-permute-start | bytes 12296 | tf_op jit(solution)/shard_map/ppermute | solution.py:464
  102.1 8.9 %collective-permute-start.18 = (bf16[3,64,512]{2,1,0:T(8,128)(2,1)}, bf16[3,64,512]{2,1,0:T(8,128)(2,1)}, u32[]{:S(2)}, u32[]{:S(2)}) collective-permute-start(bf16[3,64,512]{2,1,0:T(8,128)(2,1)} %fusion.20), channel_id=1, source_target_pairs={{0,1},{1,0},{2,3},{3,2},{4,5},{5,4},{6,7},{7,6},{8,9},{9,8},{10,11... | collective-permute-start | bytes 589832 | tf_op jit(solution)/shard_map/ppermute | solution.py:471
  103.6 1.1 copy-start.2
  104.7 7.7 %copy-start.4 = (f32[2,3,64,512]{3,2,1,0:T(8,128)S(1)}, f32[2,3,64,512]{3,2,1,0:T(8,128)}, u32[]{:S(2)}) copy-start(f32[2,3,64,512]{3,2,1,0:T(8,128)} %copy-done.3) | copy-start | bytes 2359300
  104.7 7.7 %copy-start.8 = (f32[2,3,64,512]{3,2,1,0:T(8,128)S(1)}, f32[2,3,64,512]{3,2,1,0:T(8,128)}, u32[]{:S(2)}) copy-start(f32[2,3,64,512]{3,2,1,0:T(8,128)} %copy-done.7) | copy-start | bytes 2359300
  110.9 5.0 %copy-start.9 = (bf16[256,256]{1,0:T(8,128)(2,1)S(1)}, bf16[256,256]{1,0:T(8,128)(2,1)}, u32[]{:S(2)}) copy-start(bf16[256,256]{1,0:T(8,128)(2,1)} %fusion.18) | copy-start | bytes 393220
  110.9 8.2 %copy-start.12 = (pred[256]{0:T(512)(128)(4,1)S(1)}, pred[256]{0:T(512)(128)(4,1)}, u32[]{:S(2)}) copy-start(pred[256]{0:T(512)(128)(4,1)} %broadcast_in_dim.191) | copy-start | bytes 772
  110.9 8.5 %copy-start.5 = (bf16[1024,512]{1,0:T(8,128)(2,1)S(1)}, bf16[1024,512]{1,0:T(8,128)(2,1)}, u32[]{:S(2)}) copy-start(bf16[1024,512]{1,0:T(8,128)(2,1)} %pad_maximum_fusion) | copy-start | bytes 3145732
  110.9 8.5 %copy-start.6 = (bf16[256,1024]{1,0:T(8,128)(2,1)S(1)}, bf16[256,1024]{1,0:T(8,128)(2,1)}, u32[]{:S(2)}) copy-start(bf16[256,1024]{1,0:T(8,128)(2,1)} %compare_convert_fusion) | copy-start | bytes 1572868
  111.0 4.9 %collective-permute-start.19 = (bf16[8,16,64]{2,1,0:T(8,128)(2,1)S(1)}, bf16[8,16,64]{2,1,0:T(8,128)(2,1)S(1)}, u32[]{:S(2)}, u32[]{:S(2)}) collective-permute-start(bf16[8,16,64]{2,1,0:T(8,128)(2,1)S(1)} %pad_maximum_fusion.3), channel_id=1, source_target_pairs={{0,16},{2,18},{4,20},{6,22},{8,24},{10,26},{12,28},{14,30},{16,0},... | collective-permute-start | bytes 49160 | tf_op jit(solution)/shard_map/ppermute | solution.py:464
  113.4 5.7 %collective-permute-start.20 = (f32[1,64,512]{2,1,0:T(8,128)S(1)}, f32[1,64,512]{2,1,0:T(8,128)S(1)}, u32[]{:S(2)}, u32[]{:S(2)}) collective-permute-start(f32[1,64,512]{2,1,0:T(8,128)S(1)} %get-tuple-element.98), channel_id=1, source_target_pairs={{0,2},{2,0},{8,10},{10,8},{16,18},{18,16},{24,26},{26,24},{28,30},... | collective-permute-start | bytes 393224 | tf_op jit(solution)/shard_map/ppermute | solution.py:309
  113.5 4.5 %collective-permute-start.21 = (bf16[1,64,512]{2,1,0:T(8,128)(2,1)S(1)}, bf16[1,64,512]{2,1,0:T(8,128)(2,1)S(1)}, u32[]{:S(2)}, u32[]{:S(2)}) collective-permute-start(bf16[1,64,512]{2,1,0:T(8,128)(2,1)S(1)} %get-tuple-element.99), channel_id=1, source_target_pairs={{0,1},{1,0},{2,3},{3,2},{4,5},{5,4},{6,7},{7,6},{8,9},{9,8},{10,11... | collective-permute-start | bytes 196616 | tf_op jit(solution)/shard_map/ppermute | solution.py:325
  115.0 4.1 %collective-permute-start.22 = (bf16[1,64,512]{2,1,0:T(8,128)(2,1)S(1)}, bf16[1,64,512]{2,1,0:T(8,128)(2,1)S(1)}, u32[]{:S(2)}, u32[]{:S(2)}) collective-permute-start(bf16[1,64,512]{2,1,0:T(8,128)(2,1)S(1)} %get-tuple-element.100), channel_id=1, source_target_pairs={{0,3},{1,2},{2,1},{3,0},{4,7},{5,6},{6,5},{7,4},{8,11},{9,10},{10,... | collective-permute-start | bytes 196616 | tf_op jit(solution)/shard_map/ppermute | solution.py:326

commit v11 on v10

--- a/solution.py
+++ b/solution.py
@@ -34,13 +34,6 @@
     sources = [w.at[pl.ds(first + i * tile, tile)] for i in range(tiles) for w in weights]
     places = [held.at[which, i] for i in range(tiles) for which in (0, 1)]
     return started(sources, places, ready)
-
-
-def factor_copies(lane, factors, held, ready):
-    rank, depth = held.shape[0] // 2, held.shape[1]
-    first = pl.multiple_of(lane * depth, 128)
-    sources = [f.at[:, pl.ds(first, depth)] for f in factors]
-    return started(sources, [held.at[pl.ds(which * rank, rank)] for which in (0, 1)], ready)
 
 
 def weight_products(rows_of, copies, held, sums):
@@ -54,17 +47,15 @@
             total[...] += jnp.dot(rows, held[which, index], preferred_element_type=jnp.float32)
 
 
-def factor_products(rows_of, copies, held, low):
-    depth = held.shape[1]
+def factor_products(rows_of, table, low):
+    depth = table.shape[1]
     tile = tile_of(depth)
     low[...] = jnp.zeros_like(low)
-    for copy in copies:
-        copy.wait()
 
     def step(index, carry):
         here = pl.ds(pl.multiple_of(index * tile, 128), tile)
         low[...] += lax.dot_general(
-            rows_of(here), held[:, here], (((1,), (1,)), ((), ())), preferred_element_type=jnp.float32
+            rows_of(here), table[:, here], (((1,), (1,)), ((), ())), preferred_element_type=jnp.float32
         )
         return carry
 
@@ -97,18 +88,18 @@
 
 def early_kernel(count, facts, *refs):
     pieces, refs = refs[:count], refs[count:]
-    weights, factors, choices = refs[:2], refs[2:4], refs[4]
-    (base, base_sib, compact), refs = refs[5:8], refs[8:]
-    sums, low, held, ready, held_low, ready_low = refs[:2], *refs[2:]
+    weights, (factors, choices), refs = refs[:2], refs[2:4], refs[4:]
+    owns, rests, compact, refs = refs[:2], refs[2:4], refs[4], refs[5:]
+    sums, (held, ready, low) = refs[:2], refs[2:]
     rows_of = lambda here: jnp.concatenate([piece[:, here] for piece in pieces], axis=0)
     in_flight = weight_copies(facts[0], weights, held, ready)
-    in_flight_low = factor_copies(facts[0], factors, held_low, ready_low)
+    factor_products(rows_of, factors, low)
     weight_products(rows_of, in_flight, held, sums)
-    factor_products(rows_of, in_flight_low, held_low, low)
-    height = base.shape[1] // 2
-    for out, total in zip((base, base_sib), sums):
-        for index in range(out.shape[0]):
-            out[index] = in_lanes(facts[0], total, index, height)
+    height = owns[0].shape[1] // 2
+    for own, rest, total in zip(owns, rests, sums):
+        own[0] = in_lanes(facts[0], total, 0, height)
+        for index in range(1, count):
+            rest[index - 1] = in_lanes(facts[0], total, index, height)
     compact[0], compact[1] = compacted(choices[...], low[...])
 
 
@@ -122,16 +113,13 @@
 
 
 def middle_kernel(facts, piece, other, *refs):
-    weights, factors = refs[:2], refs[2:4]
-    (choices, compact_in, base, base_sib), refs = refs[4:8], refs[8:]
-    (own, sib, compact), refs = refs[:3], refs[3:]
-    sums, low, held, ready, held_low, ready_low = refs[:2], *refs[2:]
+    weights, (factors, choices, compact_in, base, base_sib), refs = refs[:2], refs[2:7], refs[7:]
+    (own, sib, compact), sums, (held, ready, low) = refs[:3], refs[3:5], refs[5:]
     outs = own.at[0], sib.at[0], own.at[1], sib.at[1]
     rows_of = lambda here: jnp.concatenate([piece[:, here], other[:, here]], axis=0)
     in_flight = weight_copies(facts[0], weights, held, ready)
-    in_flight_low = factor_copies(facts[0], factors, held_low, ready_low)
+    factor_products(rows_of, factors, low)
     weight_products(rows_of, in_flight, held, sums)
-    factor_products(rows_of, in_flight_low, held_low, low)
     pairs, group = own.shape[1:3]
     fresh = [[in_lanes(facts[0], total, index, group // 2) for total in sums] for index in (0, 1)]
     lane = facts[0]
@@ -139,7 +127,7 @@
     behind = [jnp.where(lane == 0, a, b) for a, b in zip(*fresh)]
     for pair in range(pairs):
         step, back = pair + 1, pairs - pair
-        near, away = 2 * step - lane, 2 * back - 1 + lane
+        near, away = 2 * step - 1 - lane, 2 * back - 2 + lane
         near = ahead if step == pairs else (base[near], base_sib[near])
         away = behind if back == pairs else (base[away], base_sib[away])
         share(facts[2 + step], near, away, outs, pair)
@@ -147,11 +135,9 @@
         compact[which] = compact_in[which] + fresh_low
 
 
-def low_kernel(facts, piece, *refs):
-    factors, (choices, compact_in, kept, sent, low, held, ready) = refs[:2], refs[2:]
+def low_kernel(facts, piece, factors, choices, compact_in, kept, sent, low):
     half = kept.shape[1]
-    rows_of = lambda here: piece[:, here]
-    factor_products(rows_of, factor_copies(facts[0], factors, held, ready), held, low)
+    factor_products(lambda here: piece[:, here], factors, low)
     for which, fresh_low in enumerate(compacted(choices[...], low[...])):
         total = compact_in[which] + fresh_low
         kept[which] = jnp.where(facts[1] == 0, total[:half], total[half:])
@@ -161,14 +147,14 @@
 def last_kernel(facts, piece, *refs):
     weights, (base, base_sib), refs = refs[:2], refs[2:4], refs[4:]
     outs, sums, (held, ready) = refs[:4], refs[4:6], refs[6:]
-    rows_of = lambda here: piece[:, here]
-    weight_products(rows_of, weight_copies(facts[0], weights, held, ready), held, sums)
+    in_flight = weight_copies(facts[0], weights, held, ready)
+    weight_products(lambda here: piece[:, here], in_flight, held, sums)
     away = [in_lanes(facts[0], total, 0, piece.shape[0] // 2) for total in sums]
     share(facts[2], (base[0], base_sib[0]), away, outs, 0)
 
 
 def kernel_call(kernel, facts, rows, total, weights, factors, others, shapes):
-    in_vmem, anywhere = pl.BlockSpec(memory_space=pltpu.VMEM), pl.BlockSpec(memory_space=pl.ANY)
+    in_vmem, in_hbm = pl.BlockSpec(memory_space=pltpu.VMEM), pl.BlockSpec(memory_space=pl.ANY)
     depth = rows[0].shape[1]
     tile = tile_of(depth)
     scratch, columns = [], 0
@@ -176,21 +162,17 @@
         width = weights[0].shape[1]
         columns += 2 * width
         scratch += [pltpu.VMEM((total, width), jnp.float32)] * 2
-    if factors:
-        rank = factors[0].shape[0]
-        columns += 2 * rank
-        scratch += [pltpu.VMEM((total, 2 * rank), jnp.float32)]
-    if weights:
         scratch += [pltpu.VMEM((2, depth // tile, tile, width), jnp.bfloat16)]
         scratch += [pltpu.SemaphoreType.DMA((2 * depth // tile,))]
     if factors:
-        scratch += [pltpu.VMEM((2 * rank, depth), jnp.bfloat16), pltpu.SemaphoreType.DMA((2,))]
+        columns += factors[0].shape[0]
+        scratch += [pltpu.VMEM((total, factors[0].shape[0]), jnp.float32)]
     return pl.pallas_call(
         kernel,
         in_specs=[pl.BlockSpec(memory_space=pltpu.SMEM)]
         + [in_vmem] * len(rows)
-        + [anywhere] * (len(weights) + len(factors))
-        + [in_vmem] * len(others),
+        + [in_hbm] * len(weights)
+        + [in_vmem] * (len(factors) + len(others)),
         out_specs=[in_vmem] * len(shapes),
         out_shape=[jax.ShapeDtypeStruct(shape, kind) for shape, kind in shapes],
         scratch_shapes=scratch,
@@ -336,7 +318,9 @@
     )
     other_second = lax.ppermute(second_factor_table, INNER, SWAP)
     weights = (weight, send(weight, 0, 1))
-    factors = (first, send(first, 0, 1))
+    factors = (
+        jnp.concatenate([half_of(first, side, 1), half_of(send(first, 0, 1), side, 1)], axis=0),
+    )
     home_late, row_adapter_index, weights = lax.optimization_barrier(
         (home, row_adapter_index, weights)
     )
@@ -415,7 +399,9 @@
         weights,
         factors,
         (choices[0],),
-        [((len(pieces), group_rows, width), f32)] * 2 + [compact_shape],
+        [((1, group_rows, width), f32)] * 2
+        + [((len(pieces) - 1, group_rows, width), f32)] * 2
+        + [compact_shape],
     )
     ready = (facts, spots, mask, copies, choices, places, second)
     one_way, other_way, early, ready = lax.optimization_barrier(
@@ -436,7 +422,7 @@
         2 * group_rows,
         weights,
         factors,
-        (choices[1], early[2], early[0], early[1]),
+        (choices[1], early[4], early[2], early[3]),
         [((2, far - 1, group_rows, width), f32)] * 2 + [compact_shape],
     )
     last, compact = lax.optimization_barrier((last, compact))
@@ -451,7 +437,6 @@
         (choices[2], compact),
         [((2, half, rank), f32)] * 2,
     )
-    kept, sent, sib_more = lax.optimization_barrier((kept, sent, sib_more))
     got = to_three(kept, sent, sent)
     low = (kept + got[1] + (got[0] + got[2])[::-1]).astype(bf16)
 
@@ -481,6 +466,7 @@
         low = gather(low, gap, 2)
         gap *= 2
     got_one = to_three(*one)
+    low, got_more = lax.optimization_barrier((low, got_more))
 
     more = kept_more + got_more.astype(f32)
     rows = 0

time: 121 us -> 115 us (0.950)
  Pallas kernels: 30.9 us -> 25.8 us
  waiting for transfers between devices: 54.5 us -> 50.5 us
  local copies, waits for them, and re-layouts: 3.67 us -> 7.1 us
  other arithmetic: 8.44 us -> 7.06 us
    ppermute x1, waiting for transfers between devices: 11.2 us -> 0.01 us  [ringed(): other_second = lax.ppermute(second_factor_table, INNER, SWAP)]
    ppermute x7, waiting for transfers between devices: 35 us -> 44.6 us  [turn(): return lax.ppermute(value, 'wide', pairs)]
    pallas_call x4, Pallas kernels: 30.9 us -> 25.8 us  [kernel_call(): pl.pallas_call(kernel, in_specs=[pl.BlockSpec(memory_space=pltpu.SMEM)] +...]
    dynamic_slice x0 -> x2, local copies, waits for them, and re-layouts: none -> 2.82 us  [half_of(): return lax.dynamic_slice_in_dim(value, which * depth, depth, axis)]
    ppermute x2, waiting for transfers between devices: 4.19 us -> 1.67 us  [to_three(): lax.ppermute(to_mp, INNER, SWAP)]
    ppermute x2, waiting for transfers between devices: 2.19 us -> 0.51 us  [to_three(): lax.ppermute(to_both, ('wide',) + INNER, crossed)]
  transfers between devices with their start and end apart: 23 -> 23, of which waited for: 11 -> 10; matrix products, arithmetic and copies ran while one was open for 6% -> 8% of each run, Pallas kernels for 23% -> 23%
where the time goes in v11:
time: 115 us; the launch traced here: 114 us
  waiting for transfers between devices  50.5 us (44%)
  Pallas kernels  25.8 us (22%)
  starting transfers between devices  22.1 us (19%)
  local copies, waits for them, and re-layouts  7.1 us (6%)
  other arithmetic  7.06 us (6%)
  matrix products  1.42 us (1%)
    ppermute x7, waiting for transfers between devices, turn(): return lax.ppermute(value, 'wide', pairs)  44.6 us
    pallas_call x4, Pallas kernels, kernel_call(): pl.pallas_call(kernel, in_specs=[pl.BlockSpec(memory_space=pltpu.SMEM)] +...  25.8 us
    ppermute x7, starting transfers between devices, turn(): return lax.ppermute(value, 'wide', pairs)  8.47 us
    ppermute x4, starting transfers between devices, from_node(): lax.ppermute(value, 'wide', [(w, w ^ 2 * gap) for w in range(owners)])  4.63 us
    dynamic_slice x2, local copies, waits for them, and re-layouts, half_of(): return lax.dynamic_slice_in_dim(value, which * depth, depth, axis)  2.82 us
    ppermute x6, waiting for transfers between devices, send(): return lax.ppermute(value, 'wide', moved(shift, cross))  2.52 us
    unnamed x20, local copies, waits for them, and re-layouts  2.4 us
  transfers between devices with their start and end apart: 23, of which 10 were waited for; matrix products, arithmetic and copies ran while one was open for 8% of the time, Pallas kernels for 23%

profile of v11, /device:TPU:0, one launch (start us, length us, event | category | flops | bytes accessed | tf_op | source)
XLA Modules:
  0.0 114.4 jit_solution(13644716517874762777)
XLA Ops:
  0.0 2.0 %fusion.11 = (bf16[32,7168]{1,0:T(8,128)(2,1)S(1)}, bf16[32,7168]{1,0:T(8,128)(2,1)S(1)}) fusion(bf16[32,14336]{1,0:T(8,128)(2,1)} %param.9, s32[]{:T(128)S(6)} %select_n.117, bf16[32,14336]{1,0:T(8,128)(2,1)} %param.8, s32[]{:T(128)S(6)} %select_n.118), kind=kLoop, calls=%fused_computation.22 | loop fusion | flops 3670016 | bytes 2752520 | tf_op jit(solution)/shard_map/convert_element_type | solution.py:189
  2.0 0.5 collective-permute-start
  2.6 1.4 %collective-permute-done = bf16[32,7168]{1,0:T(8,128)(2,1)S(1)} collective-permute-done((bf16[32,7168]{1,0:T(8,128)(2,1)S(1)}, bf16[32,7168]{1,0:T(8,128)(2,1)S(1)}, u32[]{:S(2)}, u32[]{:S(2)}) %collective-permute-start) | collective-permute-done | bytes 458784 | tf_op jit(solution)/shard_map/ppermute | solution.py:291
  4.1 0.4 collective-permute-start.7
  4.5 2.7 %collective-permute-start.1 = (bf16[64,7168]{1,0:T(8,128)(2,1)S(1)}, bf16[64,7168]{1,0:T(8,128)(2,1)S(1)}, u32[]{:S(2)}, u32[]{:S(2)}) collective-permute-start(bf16[64,7168]{1,0:T(8,128)(2,1)S(1)} %pad_maximum_fusion.2.refs_0_), channel_id=1, source_target_pairs={{0,8},{8,16},{16,24},{24,28},{28,20},{20,12},{12,4},{4,0},{2,6},{1... | collective-permute-start | bytes 2752520 | tf_op jit(solution)/shard_map/ppermute | solution.py:297
  7.4 1.9 %collective-permute-start.9 = (bf16[16,32,512]{2,1,0:T(8,128)(2,1)S(1)}, bf16[16,32,512]{2,1,0:T(8,128)(2,1)S(1)}, u32[]{:S(2)}, u32[]{:S(2)}) collective-permute-start(bf16[16,32,512]{2,1,0:T(8,128)(2,1)S(1)} %copy-done.7), channel_id=1, source_target_pairs={{0,1},{1,0},{2,3},{3,2},{4,5},{5,4},{6,7},{7,6},{8,9},{9,8},{10,11... | collective-permute-start | bytes 1572872 | tf_op jit(solution)/shard_map/ppermute | solution.py:319
  9.3 18.1 %collective-permute-done.1.refs_1_ = bf16[64,7168]{1,0:T(8,128)(2,1)S(1)} collective-permute-done((bf16[64,7168]{1,0:T(8,128)(2,1)S(1)}, bf16[64,7168]{1,0:T(8,128)(2,1)S(1)}, u32[]{:S(2)}, u32[]{:S(2)}) %collective-permute-start.1) | collective-permute-done | bytes 917536 | tf_op jit(solution)/shard_map/ppermute | solution.py:297
  27.4 2.5 %collective-permute-start.2 = (bf16[64,7168]{1,0:T(8,128)(2,1)S(1)}, bf16[64,7168]{1,0:T(8,128)(2,1)}, u32[]{:S(2)}, u32[]{:S(2)}) collective-permute-start(bf16[64,7168]{1,0:T(8,128)(2,1)S(1)} %collective-permute-done.1.refs_1_), channel_id=1, source_target_pairs={{0,8},{8,16},{16,24},{24,28},{28,20},{20,12},{12,4},{4,0},{2,6},{1... | collective-permute-start | bytes 2752520 | tf_op jit(solution)/shard_map/ppermute | solution.py:297
  29.9 1.6 %constant_dynamic-slice_fusion.3 = bf16[64,7168]{1,0:T(8,128)(2,1)S(1)} fusion(bf16[64,14336]{1,0:T(8,128)(2,1)} %bitcast.2, s32[]{:T(128)S(6)} %select_n.117), kind=kLoop, calls=%fused_computation.89 | loop fusion | bytes 1835012 | tf_op jit(solution)/shard_map/dynamic_slice | solution.py:300
  31.4 1.1 pad_maximum_fusion.1
  32.5 18.2 %collective-permute-done.2.refs_3_ = bf16[64,7168]{1,0:T(8,128)(2,1)} collective-permute-done((bf16[64,7168]{1,0:T(8,128)(2,1)S(1)}, bf16[64,7168]{1,0:T(8,128)(2,1)}, u32[]{:S(2)}, u32[]{:S(2)}) %collective-permute-start.2) | collective-permute-done | bytes 917536 | tf_op jit(solution)/shard_map/ppermute | solution.py:297
  50.7 1.1 collective-permute-start.5
  51.8 1.0 collective-permute-start.6
  52.7 1.2 %constant_dynamic-slice_fusion.2 = bf16[64,7168]{1,0:T(8,128)(2,1)S(1)} fusion(bf16[64,14336]{1,0:T(8,128)(2,1)} %collective-permute-done.8, s32[]{:T(128)S(6)} %select_n.117), kind=kLoop, calls=%fused_computation.88 | loop fusion | bytes 1835012 | tf_op jit(solution)/shard_map/dynamic_slice | solution.py:300
  54.0 0.1 pad_maximum_fusion.refs_7_.refs_2_.factors
  54.1 0.7 constant_dynamic-slice_fusion.4
  55.1 0.5 convert_reduce_fusion
  55.6 0.1 select_reduce_fusion
  56.6 1.2 %copy-done.1 = bf16[64,7168]{1,0:T(8,128)(2,1)S(1)} copy-done((bf16[64,7168]{1,0:T(8,128)(2,1)S(1)}, bf16[64,7168]{1,0:T(8,128)(2,1)}, u32[]{:S(2)}) %copy-start.1) | copy-done | bytes 917528
  57.8 1.2 %copy-done.3 = bf16[64,7168]{1,0:T(8,128)(2,1)S(1)} copy-done((bf16[64,7168]{1,0:T(8,128)(2,1)S(1)}, bf16[64,7168]{1,0:T(8,128)(2,1)}, u32[]{:S(2)}) %copy-start.3) | copy-done | bytes 917528
  58.9 10.1 %shard_map.82 = (f32[1,64,512]{2,1,0:T(8,128)S(1)}, f32[1,64,512]{2,1,0:T(8,128)S(1)}, f32[4,64,512]{2,1,0:T(8,128)S(1)}, f32[4,64,512]{2,1,0:T(8,128)S(1)}, f32[2,32,64]{2,1,0:T(8,128)S(1)}) custom-call(s32[6]{0:T(128)S(1)} %pad_add_fusion.facts, bf16[64,7168]{1,0:T(8,128)(2,1)S(1)} %pad_maximum_fusion.2.refs_0_, bf16[64,7168]{1,0:T(8,128)(2,1)S(1)} %copy-done.1, ...), custom_call_target="tpu_custom_call" | custom-call | flops 82575360 | bytes 516096 | tf_op jit(solution)/shard_map/pallas_call | solution.py:170
  69.1 0.8 fusion.18
  69.9 0.1 compare_convert_fusion
  70.0 3.9 %collective-permute-done.5.piece = bf16[64,7168]{1,0:T(8,128)(2,1)} collective-permute-done((bf16[64,7168]{1,0:T(8,128)(2,1)}, bf16[64,7168]{1,0:T(8,128)(2,1)}, u32[]{:S(2)}, u32[]{:S(2)}) %collective-permute-start.5) | collective-permute-done | bytes 917536 | tf_op jit(solution)/shard_map/ppermute | solution.py:297
  73.9 1.2 %collective-permute-start.10 = (bf16[64,7168]{1,0:T(8,128)(2,1)}, bf16[64,7168]{1,0:T(8,128)(2,1)S(1)}, u32[]{:S(2)}, u32[]{:S(2)}) collective-permute-start(bf16[64,7168]{1,0:T(8,128)(2,1)} %collective-permute-done.5.piece), channel_id=1, source_target_pairs={{0,8},{8,16},{16,24},{24,28},{28,20},{20,12},{12,4},{4,0},{2,6},{1... | collective-permute-start | bytes 2752520 | tf_op jit(solution)/shard_map/ppermute | solution.py:297
  75.2 7.3 %shard_map.83 = (f32[2,3,64,512]{3,2,1,0:T(8,128)S(1)}, f32[2,3,64,512]{3,2,1,0:T(8,128)S(1)}, f32[2,32,64]{2,1,0:T(8,128)S(1)}) custom-call(s32[6]{0:T(128)S(1)} %pad_add_fusion.facts, bf16[64,7168]{1,0:T(8,128)(2,1)} %collective-permute-done.5.piece, bf16[64,7168]{1,0:T(8,128)(2,1)} %collective-permute-done.6.other, bf16[14336,512]{1,0:T(8,128)(2,1)} %refs_0_.1, ...), custom_call_target="tpu_custom_call" | custom-call | flops 33030144 | bytes 516096 | tf_op jit(solution)/shard_map/pallas_call | solution.py:170
  82.4 0.8 collective-permute-start.14
  83.2 4.4 %collective-permute-done.10.piece = bf16[64,7168]{1,0:T(8,128)(2,1)S(1)} collective-permute-done((bf16[64,7168]{1,0:T(8,128)(2,1)}, bf16[64,7168]{1,0:T(8,128)(2,1)S(1)}, u32[]{:S(2)}, u32[]{:S(2)}) %collective-permute-start.10) | collective-permute-done | bytes 917536 | tf_op jit(solution)/shard_map/ppermute | solution.py:297
  87.7 2.3 %shard_map.84 = (f32[2,16,64]{2,1,0:T(8,128)S(1)}, f32[2,16,64]{2,1,0:T(8,128)S(1)}) custom-call(s32[6]{0:T(128)S(1)} %pad_add_fusion.facts, bf16[64,7168]{1,0:T(8,128)(2,1)S(1)} %collective-permute-done.10.piece, bf16[128,7168]{1,0:T(8,128)(2,1)S(1)} %pad_maximum_fusion.refs_7_.refs_2_.factors, bf16[64,64]{1,0:T(8,128)(2,1)S(1)} %add_convert_fusion.1.choices, ...), custom_call_target="tpu_custom_call" | custom-call | flops 1835008 | bytes 57344 | tf_op jit(solution)/shard_map/pallas_call | solution.py:170
  90.0 0.8 collective-permute-start.13
  90.7 1.3 %collective-permute-start.11 = (f32[2,16,64]{2,1,0:T(8,128)S(1)}, f32[2,16,64]{2,1,0:T(8,128)S(1)}, u32[]{:S(2)}, u32[]{:S(2)}) collective-permute-start(f32[2,16,64]{2,1,0:T(8,128)S(1)} %get-tuple-element.84), channel_id=1, source_target_pairs={{0,1},{1,0},{2,3},{3,2},{4,5},{5,4},{6,7},{7,6},{8,9},{9,8},{10,11... | collective-permute-start | bytes 24584 | tf_op jit(solution)/shard_map/ppermute | solution.py:307
  92.1 1.1 collective-permute-done.12
  93.2 1.3 %collective-permute-done.11 = f32[2,16,64]{2,1,0:T(8,128)S(1)} collective-permute-done((f32[2,16,64]{2,1,0:T(8,128)S(1)}, f32[2,16,64]{2,1,0:T(8,128)S(1)}, u32[]{:S(2)}, u32[]{:S(2)}) %collective-permute-start.11) | collective-permute-done | bytes 8224 | tf_op jit(solution)/shard_map/ppermute | solution.py:307
  94.5 1.3 %collective-permute-start.18 = (bf16[3,64,512]{2,1,0:T(8,128)(2,1)S(1)}, bf16[3,64,512]{2,1,0:T(8,128)(2,1)}, u32[]{:S(2)}, u32[]{:S(2)}) collective-permute-start(bf16[3,64,512]{2,1,0:T(8,128)(2,1)S(1)} %fusion.20), channel_id=1, source_target_pairs={{0,1},{1,0},{2,3},{3,2},{4,5},{5,4},{6,7},{7,6},{8,9},{9,8},{10,11... | collective-permute-start | bytes 589832 | tf_op jit(solution)/shard_map/ppermute | solution.py:456
  95.8 1.5 %collective-permute-start.15 = (bf16[2,16,64]{2,1,0:T(8,128)(2,1)S(1)}, bf16[2,16,64]{2,1,0:T(8,128)(2,1)S(1)}, u32[]{:S(2)}, u32[]{:S(2)}) collective-permute-start(bf16[2,16,64]{2,1,0:T(8,128)(2,1)S(1)} %add_convert_fusion.3), channel_id=1, source_target_pairs={{0,4},{2,6},{4,0},{6,2},{8,12},{10,14},{12,8},{14,10},{16,20},{18,... | collective-permute-start | bytes 12296 | tf_op jit(solution)/shard_map/ppermute | solution.py:449
  97.3 1.6 %collective-permute-start.16 = (bf16[2,16,64]{2,1,0:T(8,128)(2,1)S(1)}, bf16[2,16,64]{2,1,0:T(8,128)(2,1)S(1)}, u32[]{:S(2)}, u32[]{:S(2)}) collective-permute-start(bf16[2,16,64]{2,1,0:T(8,128)(2,1)S(1)} %add_convert_fusion.3), channel_id=1, source_target_pairs={{0,8},{2,10},{4,12},{6,14},{8,0},{10,2},{12,4},{14,6},{16,24},{18,... | collective-permute-start | bytes 12296 | tf_op jit(solution)/shard_map/ppermute | solution.py:449
  98.9 0.3 collective-permute-start.17
  99.3 6.2 %shard_map.85 = (f32[1,64,512]{2,1,0:T(8,128)S(1)}, f32[1,64,512]{2,1,0:T(8,128)S(1)}, bf16[1,64,512]{2,1,0:T(8,128)(2,1)S(1)}, bf16[1,64,512]{2,1,0:T(8,128)(2,1)S(1)}) custom-call(s32[6]{0:T(128)S(1)} %pad_add_fusion.facts, bf16[64,7168]{1,0:T(8,128)(2,1)S(1)} %collective-permute-done.10.piece, bf16[14336,512]{1,0:T(8,128)(2,1)} %refs_0_.1, ...), custom_call_target="tpu_custom_call" | custom-call | flops 14680064 | bytes 458752 | tf_op jit(solution)/shard_map/pallas_call | solution.py:170
  105.6 1.1 collective-permute-start.19
  107.4 0.6 collective-permute-start.21
  108.0 1.2 %collective-permute-start.22 = (bf16[1,64,512]{2,1,0:T(8,128)(2,1)S(1)}, bf16[1,64,512]{2,1,0:T(8,128)(2,1)S(1)}, u32[]{:S(2)}, u32[]{:S(2)}) collective-permute-start(bf16[1,64,512]{2,1,0:T(8,128)(2,1)S(1)} %get-tuple-element.106), channel_id=1, source_target_pairs={{0,3},{1,2},{2,1},{3,0},{4,7},{5,6},{6,5},{7,4},{8,11},{9,10},{10,... | collective-permute-start | bytes 196616 | tf_op jit(solution)/shard_map/ppermute | solution.py:308
  109.2 1.2 %collective-permute-done.19 = bf16[8,16,64]{2,1,0:T(8,128)(2,1)S(1)} collective-permute-done((bf16[8,16,64]{2,1,0:T(8,128)(2,1)S(1)}, bf16[8,16,64]{2,1,0:T(8,128)(2,1)S(1)}, u32[]{:S(2)}, u32[]{:S(2)}) %collective-permute-start.19) | collective-permute-done | bytes 16416 | tf_op jit(solution)/shard_map/ppermute | solution.py:449
  110.5 1.2 %fusion.16 = f32[3,64,512]{2,1,0:T(8,128)S(1)} fusion(f32[2,3,64,512]{3,2,1,0:T(8,128)} %copy-done.5, bf16[3,64,512]{2,1,0:T(8,128)(2,1)} %collective-permute-done.18, f32[2,3,64,512]{3,2,1,0:T(8,128)S(1)} %get-tuple-element.85), kind=kLoop, calls=%fused_computation.32 | loop fusion | flops 294912 | bytes 1376256 | tf_op jit(solution)/shard_map/add | solution.py:471
  111.8 0.2 convolution_convert_fusion.1
  111.9 0.4 collective-permute-done.21
  112.3 0.5 collective-permute-done.22
  112.9 0.2 fusion.12
  113.1 1.3 %fusion.1 = bf16[256,512]{1,0:T(8,128)(2,1)} fusion(f32[256,512]{1,0:T(8,128)S(1)} %fusion.12, bf16[1024,512]{1,0:T(8,128)(2,1)S(1)} %copy-done.4, bf16[256,1024]{1,0:T(8,128)(2,1)S(1)} %compare_convert_fusion, bf16[256,64]{1,0:T(8,128)(2,1)S(1)} %convolution_convert_fusion.1, bf16[64,1024]{1,0:T(8,128)(2,1)S(1)} %fusion.19), kind=kOutput, calls=%fused_computation.4 | convolution fusion | flops 302776320 | bytes 2523136 | tf_op jit(solution)/shard_map/dot_general | solution.py:477
  (78 shorter events, 2.3 us)
Async XLA Ops:
  0.0 7.4 %copy-start.7 = (bf16[16,32,512]{2,1,0:T(8,128)(2,1)S(1)}, bf16[16,32,512]{2,1,0:T(8,128)(2,1)}, u32[]{:S(2)}) copy-start(bf16[16,32,512]{2,1,0:T(8,128)(2,1)} %param.12) | copy-start | bytes 1572868
  2.0 2.0 %collective-permute-start = (bf16[32,7168]{1,0:T(8,128)(2,1)S(1)}, bf16[32,7168]{1,0:T(8,128)(2,1)S(1)}, u32[]{:S(2)}, u32[]{:S(2)}) collective-permute-start(bf16[32,7168]{1,0:T(8,128)(2,1)S(1)} %get-tuple-element.110), channel_id=1, source_target_pairs={{0,2},{2,0},{8,10},{10,8},{16,18},{18,16},{24,26},{26,24},{28,30},... | collective-permute-start | bytes 1376264 | tf_op jit(solution)/shard_map/ppermute | solution.py:291
  4.1 50.1 %collective-permute-start.7 = (bf16[14336,512]{1,0:T(8,128)(2,1)}, bf16[14336,512]{1,0:T(8,128)(2,1)}, u32[]{:S(2)}, u32[]{:S(2)}) collective-permute-start(bf16[14336,512]{1,0:T(8,128)(2,1)} %refs_0_.1), channel_id=1, source_target_pairs={{0,2},{2,0},{8,10},{10,8},{16,18},{18,16},{24,26},{26,24},{28,30},... | collective-permute-start | bytes 44040200 | tf_op jit(solution)/shard_map/ppermute | solution.py:291
  4.5 22.9 %collective-permute-start.1 = (bf16[64,7168]{1,0:T(8,128)(2,1)S(1)}, bf16[64,7168]{1,0:T(8,128)(2,1)S(1)}, u32[]{:S(2)}, u32[]{:S(2)}) collective-permute-start(bf16[64,7168]{1,0:T(8,128)(2,1)S(1)} %pad_maximum_fusion.2.refs_0_), channel_id=1, source_target_pairs={{0,8},{8,16},{16,24},{24,28},{28,20},{20,12},{12,4},{4,0},{2,6},{1... | collective-permute-start | bytes 2752520 | tf_op jit(solution)/shard_map/ppermute | solution.py:297
  7.2 22.6 %collective-permute-start.3 = (bf16[64,7168]{1,0:T(8,128)(2,1)S(1)}, bf16[64,7168]{1,0:T(8,128)(2,1)S(1)}, u32[]{:S(2)}, u32[]{:S(2)}) collective-permute-start(bf16[64,7168]{1,0:T(8,128)(2,1)S(1)} %pad_maximum_fusion.2.refs_0_), channel_id=1, source_target_pairs={{0,4},{8,0},{16,8},{24,16},{28,24},{20,28},{12,20},{4,12},{2,10},{... | collective-permute-start | bytes 2752520 | tf_op jit(solution)/shard_map/ppermute | solution.py:297
  7.2 45.5 %collective-permute-start.8 = (bf16[64,14336]{1,0:T(8,128)(2,1)}, bf16[64,14336]{1,0:T(8,128)(2,1)}, u32[]{:S(2)}, u32[]{:S(2)}) collective-permute-start(bf16[64,14336]{1,0:T(8,128)(2,1)} %bitcast.2), channel_id=1, source_target_pairs={{0,2},{2,0},{8,10},{10,8},{16,18},{18,16},{24,26},{26,24},{28,30},... | collective-permute-start | bytes 5505032 | tf_op jit(solution)/shard_map/ppermute | solution.py:291
  7.4 24.1 %collective-permute-start.9 = (bf16[16,32,512]{2,1,0:T(8,128)(2,1)S(1)}, bf16[16,32,512]{2,1,0:T(8,128)(2,1)S(1)}, u32[]{:S(2)}, u32[]{:S(2)}) collective-permute-start(bf16[16,32,512]{2,1,0:T(8,128)(2,1)S(1)} %copy-done.7), channel_id=1, source_target_pairs={{0,1},{1,0},{2,3},{3,2},{4,5},{5,4},{6,7},{7,6},{8,9},{9,8},{10,11... | collective-permute-start | bytes 1572872 | tf_op jit(solution)/shard_map/ppermute | solution.py:319
  27.4 5.1 %copy-start = (bf16[64,7168]{1,0:T(8,128)(2,1)}, bf16[64,7168]{1,0:T(8,128)(2,1)S(1)}, u32[]{:S(2)}) copy-start(bf16[64,7168]{1,0:T(8,128)(2,1)S(1)} %collective-permute-done.1.refs_1_) | copy-start | bytes 2752516
  27.4 23.3 %collective-permute-start.2 = (bf16[64,7168]{1,0:T(8,128)(2,1)S(1)}, bf16[64,7168]{1,0:T(8,128)(2,1)}, u32[]{:S(2)}, u32[]{:S(2)}) collective-permute-start(bf16[64,7168]{1,0:T(8,128)(2,1)S(1)} %collective-permute-done.1.refs_1_), channel_id=1, source_target_pairs={{0,8},{8,16},{16,24},{24,28},{28,20},{20,12},{12,4},{4,0},{2,6},{1... | collective-permute-start | bytes 2752520 | tf_op jit(solution)/shard_map/ppermute | solution.py:297
  29.8 2.7 %copy-start.2 = (bf16[64,7168]{1,0:T(8,128)(2,1)}, bf16[64,7168]{1,0:T(8,128)(2,1)S(1)}, u32[]{:S(2)}) copy-start(bf16[64,7168]{1,0:T(8,128)(2,1)S(1)} %collective-permute-done.3.refs_2_) | copy-start | bytes 2752516
  29.8 20.8 %collective-permute-start.4 = (bf16[64,7168]{1,0:T(8,128)(2,1)S(1)}, bf16[64,7168]{1,0:T(8,128)(2,1)}, u32[]{:S(2)}, u32[]{:S(2)}) collective-permute-start(bf16[64,7168]{1,0:T(8,128)(2,1)S(1)} %collective-permute-done.3.refs_2_), channel_id=1, source_target_pairs={{0,4},{8,0},{16,8},{24,16},{28,24},{20,28},{12,20},{4,12},{2,10},{... | collective-permute-start | bytes 2752520 | tf_op jit(solution)/shard_map/ppermute | solution.py:297
  50.7 23.2 %collective-permute-start.5 = (bf16[64,7168]{1,0:T(8,128)(2,1)}, bf16[64,7168]{1,0:T(8,128)(2,1)}, u32[]{:S(2)}, u32[]{:S(2)}) collective-permute-start(bf16[64,7168]{1,0:T(8,128)(2,1)} %collective-permute-done.2.refs_3_), channel_id=1, source_target_pairs={{0,8},{8,16},{16,24},{24,28},{28,20},{20,12},{12,4},{4,0},{2,6},{1... | collective-permute-start | bytes 2752520 | tf_op jit(solution)/shard_map/ppermute | solution.py:297
  51.8 22.2 %collective-permute-start.6 = (bf16[64,7168]{1,0:T(8,128)(2,1)}, bf16[64,7168]{1,0:T(8,128)(2,1)}, u32[]{:S(2)}, u32[]{:S(2)}) collective-permute-start(bf16[64,7168]{1,0:T(8,128)(2,1)} %collective-permute-done.4.refs_4_), channel_id=1, source_target_pairs={{0,4},{8,0},{16,8},{24,16},{28,24},{20,28},{12,20},{4,12},{2,10},{... | collective-permute-start | bytes 2752520 | tf_op jit(solution)/shard_map/ppermute | solution.py:297
  54.0 0.9 copy-start.8
  54.0 0.9 copy-start.9
  56.6 1.2 %copy-start.1 = (bf16[64,7168]{1,0:T(8,128)(2,1)S(1)}, bf16[64,7168]{1,0:T(8,128)(2,1)}, u32[]{:S(2)}) copy-start(bf16[64,7168]{1,0:T(8,128)(2,1)} %copy-done) | copy-start | bytes 2752516
  57.8 1.2 %copy-start.3 = (bf16[64,7168]{1,0:T(8,128)(2,1)S(1)}, bf16[64,7168]{1,0:T(8,128)(2,1)}, u32[]{:S(2)}) copy-start(bf16[64,7168]{1,0:T(8,128)(2,1)} %copy-done.2) | copy-start | bytes 2752516
  73.9 13.7 %collective-permute-start.10 = (bf16[64,7168]{1,0:T(8,128)(2,1)}, bf16[64,7168]{1,0:T(8,128)(2,1)S(1)}, u32[]{:S(2)}, u32[]{:S(2)}) collective-permute-start(bf16[64,7168]{1,0:T(8,128)(2,1)} %collective-permute-done.5.piece), channel_id=1, source_target_pairs={{0,8},{8,16},{16,24},{24,28},{28,20},{20,12},{12,4},{4,0},{2,6},{1... | collective-permute-start | bytes 2752520 | tf_op jit(solution)/shard_map/ppermute | solution.py:297
  82.4 9.6 %collective-permute-start.14 = (f32[2,3,64,512]{3,2,1,0:T(8,128)S(1)}, f32[2,3,64,512]{3,2,1,0:T(8,128)S(1)}, u32[]{:S(2)}, u32[]{:S(2)}) collective-permute-start(f32[2,3,64,512]{3,2,1,0:T(8,128)S(1)} %get-tuple-element.86), channel_id=1, source_target_pairs={{0,2},{2,0},{8,10},{10,8},{16,18},{18,16},{24,26},{26,24},{28,30},... | collective-permute-start | bytes 2359304 | tf_op jit(solution)/shard_map/ppermute | solution.py:291
  90.0 3.2 %collective-permute-start.13 = (f32[2,16,64]{2,1,0:T(8,128)S(1)}, f32[2,16,64]{2,1,0:T(8,128)S(1)}, u32[]{:S(2)}, u32[]{:S(2)}) collective-permute-start(f32[2,16,64]{2,1,0:T(8,128)S(1)} %get-tuple-element.84), channel_id=1, source_target_pairs={{0,3},{1,2},{2,1},{3,0},{4,7},{5,6},{6,5},{7,4},{8,11},{9,10},{10,... | collective-permute-start | bytes 24584 | tf_op jit(solution)/shard_map/ppermute | solution.py:308
  90.7 3.7 %collective-permute-start.11 = (f32[2,16,64]{2,1,0:T(8,128)S(1)}, f32[2,16,64]{2,1,0:T(8,128)S(1)}, u32[]{:S(2)}, u32[]{:S(2)}) collective-permute-start(f32[2,16,64]{2,1,0:T(8,128)S(1)} %get-tuple-element.84), channel_id=1, source_target_pairs={{0,1},{1,0},{2,3},{3,2},{4,5},{5,4},{6,7},{7,6},{8,9},{9,8},{10,11... | collective-permute-start | bytes 24584 | tf_op jit(solution)/shard_map/ppermute | solution.py:307
  92.0 1.2 %collective-permute-start.12 = (f32[2,16,64]{2,1,0:T(8,128)S(1)}, f32[2,16,64]{2,1,0:T(8,128)S(1)}, u32[]{:S(2)}, u32[]{:S(2)}) collective-permute-start(f32[2,16,64]{2,1,0:T(8,128)S(1)} %get-tuple-element.83), channel_id=1, source_target_pairs={{0,2},{2,0},{8,10},{10,8},{16,18},{18,16},{24,26},{26,24},{28,30},... | collective-permute-start | bytes 24584 | tf_op jit(solution)/shard_map/ppermute | solution.py:291
  92.0 13.5 %copy-start.5 = (f32[2,3,64,512]{3,2,1,0:T(8,128)}, f32[2,3,64,512]{3,2,1,0:T(8,128)S(1)}, u32[]{:S(2)}) copy-start(f32[2,3,64,512]{3,2,1,0:T(8,128)S(1)} %collective-permute-done.14) | copy-start | bytes 2359300
  94.5 11.1 %collective-permute-start.18 = (bf16[3,64,512]{2,1,0:T(8,128)(2,1)S(1)}, bf16[3,64,512]{2,1,0:T(8,128)(2,1)}, u32[]{:S(2)}, u32[]{:S(2)}) collective-permute-start(bf16[3,64,512]{2,1,0:T(8,128)(2,1)S(1)} %fusion.20), channel_id=1, source_target_pairs={{0,1},{1,0},{2,3},{3,2},{4,5},{5,4},{6,7},{7,6},{8,9},{9,8},{10,11... | collective-permute-start | bytes 589832 | tf_op jit(solution)/shard_map/ppermute | solution.py:456
  95.8 9.7 %collective-permute-start.15 = (bf16[2,16,64]{2,1,0:T(8,128)(2,1)S(1)}, bf16[2,16,64]{2,1,0:T(8,128)(2,1)S(1)}, u32[]{:S(2)}, u32[]{:S(2)}) collective-permute-start(bf16[2,16,64]{2,1,0:T(8,128)(2,1)S(1)} %add_convert_fusion.3), channel_id=1, source_target_pairs={{0,4},{2,6},{4,0},{6,2},{8,12},{10,14},{12,8},{14,10},{16,20},{18,... | collective-permute-start | bytes 12296 | tf_op jit(solution)/shard_map/ppermute | solution.py:449
  97.3 8.2 %collective-permute-start.16 = (bf16[2,16,64]{2,1,0:T(8,128)(2,1)S(1)}, bf16[2,16,64]{2,1,0:T(8,128)(2,1)S(1)}, u32[]{:S(2)}, u32[]{:S(2)}) collective-permute-start(bf16[2,16,64]{2,1,0:T(8,128)(2,1)S(1)} %add_convert_fusion.3), channel_id=1, source_target_pairs={{0,8},{2,10},{4,12},{6,14},{8,0},{10,2},{12,4},{14,6},{16,24},{18,... | collective-permute-start | bytes 12296 | tf_op jit(solution)/shard_map/ppermute | solution.py:449
  98.9 6.6 %collective-permute-start.17 = (bf16[2,16,64]{2,1,0:T(8,128)(2,1)S(1)}, bf16[2,16,64]{2,1,0:T(8,128)(2,1)S(1)}, u32[]{:S(2)}, u32[]{:S(2)}) collective-permute-start(bf16[2,16,64]{2,1,0:T(8,128)(2,1)S(1)} %add_convert_fusion.3), channel_id=1, source_target_pairs={{0,12},{2,14},{4,8},{6,10},{8,4},{10,6},{12,0},{14,2},{16,28},{18,... | collective-permute-start | bytes 12296 | tf_op jit(solution)/shard_map/ppermute | solution.py:449
  105.5 6.2 %copy-start.6 = (bf16[256,256]{1,0:T(8,128)(2,1)S(1)}, bf16[256,256]{1,0:T(8,128)(2,1)}, u32[]{:S(2)}) copy-start(bf16[256,256]{1,0:T(8,128)(2,1)} %fusion.18) | copy-start | bytes 393220
  105.6 4.9 %collective-permute-start.19 = (bf16[8,16,64]{2,1,0:T(8,128)(2,1)S(1)}, bf16[8,16,64]{2,1,0:T(8,128)(2,1)S(1)}, u32[]{:S(2)}, u32[]{:S(2)}) collective-permute-start(bf16[8,16,64]{2,1,0:T(8,128)(2,1)S(1)} %pad_maximum_fusion.4), channel_id=1, source_target_pairs={{0,16},{2,18},{4,20},{6,22},{8,24},{10,26},{12,28},{14,30},{16,0},... | collective-permute-start | bytes 49160 | tf_op jit(solution)/shard_map/ppermute | solution.py:449
  107.4 5.5 %collective-permute-start.20 = (f32[1,64,512]{2,1,0:T(8,128)S(1)}, f32[1,64,512]{2,1,0:T(8,128)S(1)}, u32[]{:S(2)}, u32[]{:S(2)}) collective-permute-start(f32[1,64,512]{2,1,0:T(8,128)S(1)} %get-tuple-element.104), channel_id=1, source_target_pairs={{0,2},{2,0},{8,10},{10,8},{16,18},{18,16},{24,26},{26,24},{28,30},... | collective-permute-start | bytes 393224 | tf_op jit(solution)/shard_map/ppermute | solution.py:291
  107.4 4.9 %collective-permute-start.21 = (bf16[1,64,512]{2,1,0:T(8,128)(2,1)S(1)}, bf16[1,64,512]{2,1,0:T(8,128)(2,1)S(1)}, u32[]{:S(2)}, u32[]{:S(2)}) collective-permute-start(bf16[1,64,512]{2,1,0:T(8,128)(2,1)S(1)} %get-tuple-element.105), channel_id=1, source_target_pairs={{0,1},{1,0},{2,3},{3,2},{4,5},{5,4},{6,7},{7,6},{8,9},{9,8},{10,11... | collective-permute-start | bytes 196616 | tf_op jit(solution)/shard_map/ppermute | solution.py:307
  108.0 4.8 %collective-permute-start.22 = (bf16[1,64,512]{2,1,0:T(8,128)(2,1)S(1)}, bf16[1,64,512]{2,1,0:T(8,128)(2,1)S(1)}, u32[]{:S(2)}, u32[]{:S(2)}) collective-permute-start(bf16[1,64,512]{2,1,0:T(8,128)(2,1)S(1)} %get-tuple-element.106), channel_id=1, source_target_pairs={{0,3},{1,2},{2,1},{3,0},{4,7},{5,6},{6,5},{7,4},{8,11},{9,10},{10,... | collective-permute-start | bytes 196616 | tf_op jit(solution)/shard_map/ppermute | solution.py:308
  110.5 2.6 %copy-start.4 = (bf16[1024,512]{1,0:T(8,128)(2,1)S(1)}, bf16[1024,512]{1,0:T(8,128)(2,1)}, u32[]{:S(2)}) copy-start(bf16[1024,512]{1,0:T(8,128)(2,1)} %pad_maximum_fusion.1) | copy-start | bytes 3145732

commit v12 on v11

--- a/solution.py
+++ b/solution.py
@@ -36,14 +36,15 @@
     return started(sources, places, ready)
 
 
-def weight_products(rows_of, copies, held, sums):
+def weight_products(rows_of, held, sums, copies=None):
     tiles, tile = held.shape[1:3]
     for total in sums:
         total[...] = jnp.zeros_like(total)
     for index in range(tiles):
         rows = rows_of(slice(index * tile, (index + 1) * tile))
         for which, total in enumerate(sums):
-            copies[2 * index + which].wait()
+            if copies:
+                copies[2 * index + which].wait()
             total[...] += jnp.dot(rows, held[which, index], preferred_element_type=jnp.float32)
 
 
@@ -88,13 +89,13 @@
 
 def early_kernel(count, facts, *refs):
     pieces, refs = refs[:count], refs[count:]
-    weights, (factors, choices), refs = refs[:2], refs[2:4], refs[4:]
-    owns, rests, compact, refs = refs[:2], refs[2:4], refs[4], refs[5:]
-    sums, (held, ready, low) = refs[:2], refs[2:]
+    (factors, choices), weights, refs = refs[:2], refs[2:4], refs[4:]
+    owns, rests, (compact, held), refs = refs[:2], refs[2:4], refs[4:6], refs[6:]
+    sums, (low, ready) = refs[:2], refs[2:]
     rows_of = lambda here: jnp.concatenate([piece[:, here] for piece in pieces], axis=0)
     in_flight = weight_copies(facts[0], weights, held, ready)
     factor_products(rows_of, factors, low)
-    weight_products(rows_of, in_flight, held, sums)
+    weight_products(rows_of, held, sums, in_flight)
     height = owns[0].shape[1] // 2
     for own, rest, total in zip(owns, rests, sums):
         own[0] = in_lanes(facts[0], total, 0, height)
@@ -113,13 +114,12 @@
 
 
 def middle_kernel(facts, piece, other, *refs):
-    weights, (factors, choices, compact_in, base, base_sib), refs = refs[:2], refs[2:7], refs[7:]
-    (own, sib, compact), sums, (held, ready, low) = refs[:3], refs[3:5], refs[5:]
+    (held, factors, choices, compact_in, base, base_sib), refs = refs[:6], refs[6:]
+    (own, sib, compact), sums, low = refs[:3], refs[3:5], refs[5]
     outs = own.at[0], sib.at[0], own.at[1], sib.at[1]
     rows_of = lambda here: jnp.concatenate([piece[:, here], other[:, here]], axis=0)
-    in_flight = weight_copies(facts[0], weights, held, ready)
     factor_products(rows_of, factors, low)
-    weight_products(rows_of, in_flight, held, sums)
+    weight_products(rows_of, held, sums)
     pairs, group = own.shape[1:3]
     fresh = [[in_lanes(facts[0], total, index, group // 2) for total in sums] for index in (0, 1)]
     lane = facts[0]
@@ -144,45 +144,30 @@
         sent[which] = jnp.where(facts[1] == 0, total[half:], total[:half])
 
 
-def last_kernel(facts, piece, *refs):
-    weights, (base, base_sib), refs = refs[:2], refs[2:4], refs[4:]
-    outs, sums, (held, ready) = refs[:4], refs[4:6], refs[6:]
-    in_flight = weight_copies(facts[0], weights, held, ready)
-    weight_products(lambda here: piece[:, here], in_flight, held, sums)
+def last_kernel(facts, piece, held, base, base_sib, *refs):
+    outs, sums = refs[:4], refs[4:]
+    weight_products(lambda here: piece[:, here], held, sums)
     away = [in_lanes(facts[0], total, 0, piece.shape[0] // 2) for total in sums]
     share(facts[2], (base[0], base_sib[0]), away, outs, 0)
 
 
-def kernel_call(kernel, facts, rows, total, weights, factors, others, shapes):
-    in_vmem, in_hbm = pl.BlockSpec(memory_space=pltpu.VMEM), pl.BlockSpec(memory_space=pl.ANY)
-    depth = rows[0].shape[1]
-    tile = tile_of(depth)
-    scratch, columns = [], 0
+def kernel_call(kernel, facts, arrays, shapes, scratch, flops, weights=(), grant=12):
+    in_vmem = pl.BlockSpec(memory_space=pltpu.VMEM)
     if weights:
-        width = weights[0].shape[1]
-        columns += 2 * width
-        scratch += [pltpu.VMEM((total, width), jnp.float32)] * 2
-        scratch += [pltpu.VMEM((2, depth // tile, tile, width), jnp.bfloat16)]
-        scratch += [pltpu.SemaphoreType.DMA((2 * depth // tile,))]
-    if factors:
-        columns += factors[0].shape[0]
-        scratch += [pltpu.VMEM((total, factors[0].shape[0]), jnp.float32)]
+        scratch = scratch + [pltpu.SemaphoreType.DMA((len(weights) * shapes[-1][0][1],))]
     return pl.pallas_call(
         kernel,
         in_specs=[pl.BlockSpec(memory_space=pltpu.SMEM)]
-        + [in_vmem] * len(rows)
-        + [in_hbm] * len(weights)
-        + [in_vmem] * (len(factors) + len(others)),
+        + [in_vmem] * len(arrays)
+        + [pl.BlockSpec(memory_space=pl.ANY)] * len(weights),
         out_specs=[in_vmem] * len(shapes),
         out_shape=[jax.ShapeDtypeStruct(shape, kind) for shape, kind in shapes],
         scratch_shapes=scratch,
-        compiler_params=pltpu.CompilerParams(vmem_limit_bytes=(40 if weights else 8) * 2**20),
+        compiler_params=pltpu.CompilerParams(vmem_limit_bytes=grant * 2**20),
         cost_estimate=pl.CostEstimate(
-            flops=total * depth * columns // 32,
-            bytes_accessed=depth * columns // 16,
-            transcendentals=0,
+            flops=flops // 32, bytes_accessed=flops // 1024, transcendentals=0
         ),
-    )(facts, *rows, *weights, *factors, *others)
+    )(facts, *arrays, *weights)
 
 
 def hidden_of(gate, up):
@@ -308,8 +293,9 @@
             lax.ppermute(to_both, ("wide",) + INNER, crossed),
         )
 
-    keep = hidden_of(half_of(gate_activation, side, 1), half_of(up_activation, side, 1))
     give = hidden_of(half_of(gate_activation, 1 - side, 1), half_of(up_activation, 1 - side, 1))
+    keep_side, give = lax.optimization_barrier((side, give))
+    keep = hidden_of(half_of(gate_activation, keep_side, 1), half_of(up_activation, keep_side, 1))
     block = jnp.concatenate([keep, send(give, 0, 1)], axis=0)
     one_way, other_way = turn(block, 1), turn(block, -1)
 
@@ -318,8 +304,8 @@
     )
     other_second = lax.ppermute(second_factor_table, INNER, SWAP)
     weights = (weight, send(weight, 0, 1))
-    factors = (
-        jnp.concatenate([half_of(first, side, 1), half_of(send(first, 0, 1), side, 1)], axis=0),
+    factors = jnp.concatenate(
+        [half_of(first, side, 1), half_of(send(first, 0, 1), side, 1)], axis=0
     )
     home_late, row_adapter_index, weights = lax.optimization_barrier(
         (home, row_adapter_index, weights)
@@ -391,21 +377,30 @@
     )
 
     compact_shape = ((2, owners * MOST, rank), f32)
-    early = kernel_call(
+    tile = tile_of(depth)
+
+    def sums(rows, with_low=True):
+        columns = [width, width] + [2 * rank] * with_low
+        return [pltpu.VMEM((rows, size), f32) for size in columns]
+
+    def flops(rows, columns):
+        return 2 * rows * depth * columns
+
+    *early, held = kernel_call(
         functools.partial(early_kernel, len(pieces)),
         facts,
-        pieces,
-        early_rows,
-        weights,
-        factors,
-        (choices[0],),
+        (*pieces, factors, choices[0]),
         [((1, group_rows, width), f32)] * 2
         + [((len(pieces) - 1, group_rows, width), f32)] * 2
-        + [compact_shape],
+        + [compact_shape, ((2, depth // tile, tile, width), bf16)],
+        sums(early_rows),
+        flops(early_rows, 2 * (width + rank)),
+        weights,
+        32,
     )
     ready = (facts, spots, mask, copies, choices, places, second)
-    one_way, other_way, early, ready = lax.optimization_barrier(
-        (one_way, other_way, early, ready)
+    one_way, other_way, early, held, ready = lax.optimization_barrier(
+        (one_way, other_way, early, held, ready)
     )
     facts, spots, mask, copies, choices, places, second = ready
 
@@ -418,32 +413,26 @@
     own_more, sib_more, compact = kernel_call(
         middle_kernel,
         facts,
-        (one_way, other_way),
-        2 * group_rows,
-        weights,
-        factors,
-        (choices[1], early[4], early[2], early[3]),
+        (one_way, other_way, held, factors, choices[1], early[4], early[2], early[3]),
         [((2, far - 1, group_rows, width), f32)] * 2 + [compact_shape],
-    )
+        sums(2 * group_rows),
+        flops(2 * group_rows, 2 * (width + rank)),
+    )
+
+    kept_more, out_more = [a + b for a, b in zip(own_more, send(sib_more, 0, 1))]
+    out_more = out_more.astype(bf16)
     last, compact = lax.optimization_barrier((last, compact))
 
     kept, sent = kernel_call(
         low_kernel,
         facts,
-        (last,),
-        group_rows,
-        (),
-        factors,
-        (choices[2], compact),
+        (last, factors, choices[2], compact),
         [((2, half, rank), f32)] * 2,
+        [pltpu.VMEM((group_rows, 2 * rank), f32)],
+        flops(group_rows, 2 * rank),
     )
     got = to_three(kept, sent, sent)
     low = (kept + got[1] + (got[0] + got[2])[::-1]).astype(bf16)
-
-    kept_more, out_more = [
-        a + b for a, b in zip(own_more, send(sib_more, 0, 1))
-    ]
-    out_more = out_more.astype(bf16)
 
     def from_node(value, gap):
         return lax.ppermute(value, "wide", [(w, w ^ (2 * gap)) for w in range(owners)])
@@ -458,7 +447,12 @@
     low = gather(low, 1, reach)
 
     kept_one, *one = kernel_call(
-        last_kernel, facts, (last,), group_rows, weights, (), (early[0], early[1]), shares(1)
+        last_kernel,
+        facts,
+        (last, held, early[0], early[1]),
+        shares(1),
+        sums(group_rows, False),
+        flops(group_rows, 2 * width),
     )
     low, one, got_more = lax.optimization_barrier((low, one, got_more))
     gap = reach

time: 115 us -> 123 us (1.070)
  local copies, waits for them, and re-layouts: 7.1 us -> 24 us
  waiting for transfers between devices: 50.5 us -> 41.6 us
  other arithmetic: 7.06 us -> 12.5 us
  Pallas kernels: 25.8 us -> 21.1 us
    unnamed x20 -> x46, local copies, waits for them, and re-layouts: 2.4 us -> 17.4 us
    ppermute x7, waiting for transfers between devices: 44.6 us -> 35.1 us  [turn(): return lax.ppermute(value, 'wide', pairs)]
    pallas_call x4, Pallas kernels: 25.8 us -> 21.1 us  [kernel_call(): pl.pallas_call(kernel, in_specs=[pl.BlockSpec(memory_space=pltpu.SMEM)] +...]
    ppermute x2, waiting for transfers between devices: 1.67 us -> 3.45 us  [to_three(): lax.ppermute(to_mp, INNER, SWAP)]
    ppermute x4, starting transfers between devices: 4.63 us -> 6.14 us  [from_node(): lax.ppermute(value, 'wide', [(w, w ^ 2 * gap) for w in range(owners)])]
    convert_element_type x1, other arithmetic: 0.15 us -> 1.63 us  [ringed(): mask = (slot_here == column // piece % owners).astype(bf16)]
    ppermute x6, waiting for transfers between devices: 2.52 us -> 1.11 us  [send(): return lax.ppermute(value, 'wide', moved(shift, cross))]
    convert_element_type x1 -> x2, other arithmetic: 2.03 us -> 2.85 us  [hidden_of(): (jax.nn.silu(gate.astype(jnp.float32)) * up.astype(jnp.float32)).astype(j...]
  transfers between devices with their start and end apart: 23 -> 23, of which waited for: 10 -> 8; matrix products, arithmetic and copies ran while one was open for 8% -> 14% of each run, Pallas kernels for 23% -> 17%
where the time goes in v12:
time: 123 us; the launch traced here: 122 us
  waiting for transfers between devices  41.6 us (34%)
  local copies, waits for them, and re-layouts  24 us (20%)
  starting transfers between devices  21.6 us (18%)
  Pallas kernels  21.1 us (17%)
  other arithmetic  12.5 us (10%)
  matrix products  1.42 us (1%)
    ppermute x7, waiting for transfers between devices, turn(): return lax.ppermute(value, 'wide', pairs)  35.1 us
    pallas_call x4, Pallas kernels, kernel_call(): pl.pallas_call(kernel, in_specs=[pl.BlockSpec(memory_space=pltpu.SMEM)] +...  21.1 us
    unnamed x46, local copies, waits for them, and re-layouts  17.4 us
    ppermute x7, starting transfers between devices, turn(): return lax.ppermute(value, 'wide', pairs)  8.31 us
    ppermute x4, starting transfers between devices, from_node(): lax.ppermute(value, 'wide', [(w, w ^ 2 * gap) for w in range(owners)])  6.14 us
    ppermute x2, waiting for transfers between devices, to_three(): lax.ppermute(to_mp, INNER, SWAP)  3.45 us
    convert_element_type x2, other arithmetic, hidden_of(): (jax.nn.silu(gate.astype(jnp.float32)) * up.astype(jnp.float32)).astype(j...  2.85 us
    dynamic_slice x2, local copies, waits for them, and re-layouts, half_of(): return lax.dynamic_slice_in_dim(value, which * depth, depth, axis)  2.82 us
  transfers between devices with their start and end apart: 23, of which 8 were waited for; matrix products, arithmetic and copies ran while one was open for 14% of the time, Pallas kernels for 17%

profile of v12, /device:TPU:0, one launch (start us, length us, event | category | flops | bytes accessed | tf_op | source)
XLA Modules:
  0.0 122.5 jit_solution(13628318609378064579)
XLA Ops:
  0.0 1.4 %fusion.11 = bf16[32,7168]{1,0:T(8,128)(2,1)S(1)} fusion(bf16[32,14336]{1,0:T(8,128)(2,1)} %param.9, s32[]{:T(128)S(6)} %select_n.119, bf16[32,14336]{1,0:T(8,128)(2,1)} %param.8), kind=kLoop, calls=%fused_computation.22 | loop fusion | flops 1835008 | bytes 1376260 | tf_op jit(solution)/shard_map/convert_element_type | solution.py:174
  2.0 1.4 %fusion.10 = bf16[32,7168]{1,0:T(8,128)(2,1)S(1)} fusion(bf16[32,14336]{1,0:T(8,128)(2,1)} %param.9, s32[]{:T(128)S(6)} %select_n.120, bf16[32,14336]{1,0:T(8,128)(2,1)} %param.8), kind=kLoop, calls=%fused_computation.21 | loop fusion | flops 1835008 | bytes 1376260 | tf_op jit(solution)/shard_map/convert_element_type | solution.py:174
  3.9 2.7 %collective-permute-start.1 = (bf16[64,7168]{1,0:T(8,128)(2,1)S(1)}, bf16[64,7168]{1,0:T(8,128)(2,1)S(1)}, u32[]{:S(2)}, u32[]{:S(2)}) collective-permute-start(bf16[64,7168]{1,0:T(8,128)(2,1)S(1)} %pad_maximum_fusion.2.refs_0_), channel_id=1, source_target_pairs={{0,8},{8,16},{16,24},{24,28},{28,20},{20,12},{12,4},{4,0},{2,6},{1... | collective-permute-start | bytes 2752520 | tf_op jit(solution)/shard_map/ppermute | solution.py:282
  7.3 0.7 fusion.19
  8.0 1.8 %collective-permute-start.9 = (bf16[16,32,512]{2,1,0:T(8,128)(2,1)S(1)}, bf16[16,32,512]{2,1,0:T(8,128)(2,1)S(1)}, u32[]{:S(2)}, u32[]{:S(2)}) collective-permute-start(bf16[16,32,512]{2,1,0:T(8,128)(2,1)S(1)} %copy-done.20), channel_id=1, source_target_pairs={{0,1},{1,0},{2,3},{3,2},{4,5},{5,4},{6,7},{7,6},{8,9},{9,8},{10,11... | collective-permute-start | bytes 1572872 | tf_op jit(solution)/shard_map/ppermute | solution.py:305
  9.8 16.9 %collective-permute-done.1.refs_1_ = bf16[64,7168]{1,0:T(8,128)(2,1)S(1)} collective-permute-done((bf16[64,7168]{1,0:T(8,128)(2,1)S(1)}, bf16[64,7168]{1,0:T(8,128)(2,1)S(1)}, u32[]{:S(2)}, u32[]{:S(2)}) %collective-permute-start.1) | collective-permute-done | bytes 917536 | tf_op jit(solution)/shard_map/ppermute | solution.py:282
  26.8 2.5 %collective-permute-start.2 = (bf16[64,7168]{1,0:T(8,128)(2,1)S(1)}, bf16[64,7168]{1,0:T(8,128)(2,1)}, u32[]{:S(2)}, u32[]{:S(2)}) collective-permute-start(bf16[64,7168]{1,0:T(8,128)(2,1)S(1)} %collective-permute-done.1.refs_1_), channel_id=1, source_target_pairs={{0,8},{8,16},{16,24},{24,28},{28,20},{20,12},{12,4},{4,0},{2,6},{1... | collective-permute-start | bytes 2752520 | tf_op jit(solution)/shard_map/ppermute | solution.py:282
  29.3 1.6 %constant_dynamic-slice_fusion.3 = bf16[64,7168]{1,0:T(8,128)(2,1)S(1)} fusion(bf16[64,14336]{1,0:T(8,128)(2,1)} %bitcast.63, s32[]{:T(128)S(6)} %select_n.125), kind=kLoop, calls=%fused_computation.89 | loop fusion | bytes 1835012 | tf_op jit(solution)/shard_map/dynamic_slice | solution.py:285
  30.9 1.1 pad_maximum_fusion.1
  31.9 18.2 %collective-permute-done.2.refs_3_ = bf16[64,7168]{1,0:T(8,128)(2,1)} collective-permute-done((bf16[64,7168]{1,0:T(8,128)(2,1)S(1)}, bf16[64,7168]{1,0:T(8,128)(2,1)}, u32[]{:S(2)}, u32[]{:S(2)}) %collective-permute-start.2) | collective-permute-done | bytes 917536 | tf_op jit(solution)/shard_map/ppermute | solution.py:282
  50.1 1.1 collective-permute-start.5
  51.2 1.0 collective-permute-start.6
  52.1 1.2 %constant_dynamic-slice_fusion.2 = bf16[64,7168]{1,0:T(8,128)(2,1)S(1)} fusion(bf16[64,14336]{1,0:T(8,128)(2,1)} %collective-permute-done.8, s32[]{:T(128)S(6)} %select_n.125), kind=kLoop, calls=%fused_computation.88 | loop fusion | bytes 1835012 | tf_op jit(solution)/shard_map/dynamic_slice | solution.py:285
  53.5 0.7 constant_dynamic-slice_fusion.4
  55.6 0.7 add_convert_fusion.2.refs_2_
  56.9 0.7 fusion.40
  57.6 1.2 copy-done.4
  58.8 1.2 copy-done.6
  59.9 10.2 %shard_map.82 = (f32[1,64,512]{2,1,0:T(8,128)S(1)}, f32[1,64,512]{2,1,0:T(8,128)S(1)}, f32[4,64,512]{2,1,0:T(8,128)S(1)}, f32[4,64,512]{2,1,0:T(8,128)S(1)}, f32...) custom-call(s32[6]{0:T(128)S(1)} %pad_add_fusion.facts, bf16[64,7168]{1,0:T(8,128)(2,1)S(1)} %pad_maximum_fusion.2.refs_0_, ...), custom_call_target="tpu_custom_call" | custom-call | flops 165150720 | bytes 5160960 | tf_op jit(solution)/shard_map/pallas_call | solution.py:158
  70.2 5.2 %copy-done = bf16[2,7,1024,512]{3,2,1,0:T(8,128)(2,1)} copy-done((bf16[2,7,1024,512]{3,2,1,0:T(8,128)(2,1)}, bf16[2,7,1024,512]{3,2,1,0:T(8,128)(2,1)S(1)}, u32[]{:S(2)}) %copy-start) | copy-done | bytes 14680088
  75.3 0.8 copy-done.7
  76.7 0.8 reshape.299
  77.5 0.8 reshape.300
  78.3 0.7 iota_compare_fusion.6
  79.0 0.8 fusion.18
  79.8 1.6 %compare_convert_fusion = bf16[256,1024]{1,0:T(8,128)(2,1)} fusion(s32[1024]{0:T(1024)} %get-tuple-element.130, s32[256]{0:T(256)S(1)} %reshape.299), kind=kLoop, calls=%fused_computation.11 | loop fusion | flops 524288 | bytes 529408 | tf_op jit(solution)/shard_map/convert_element_type | solution.py:371
  81.4 1.1 collective-permute-start.10
  82.5 5.2 %copy-done.1 = bf16[2,7,1024,512]{3,2,1,0:T(8,128)(2,1)S(1)} copy-done((bf16[2,7,1024,512]{3,2,1,0:T(8,128)(2,1)S(1)}, bf16[2,7,1024,512]{3,2,1,0:T(8,128)(2,1)}, u32[]{:S(2)}) %copy-start.1) | copy-done | bytes 14680088
  87.7 1.0 copy-done.8
  88.7 0.7 copy-done.9
  89.4 0.8 copy-done.11
  90.2 0.7 copy-done.13
  90.8 5.4 %shard_map.83 = (f32[2,3,64,512]{3,2,1,0:T(8,128)S(1)}, f32[2,3,64,512]{3,2,1,0:T(8,128)S(1)}, f32[2,32,64]{2,1,0:T(8,128)S(1)}) custom-call(s32[6]{0:T(128)S(1)} %copy-done.13, bf16[64,7168]{1,0:T(8,128)(2,1)} %collective-permute-done.5.piece, bf16[64,7168]{1,0:T(8,128)(2,1)} %collective-permute-done.6.other, bf16[2,7,1024,512]{3,2,1,0:T(8,128)(2,1)S(1)} %copy-done.1, ...), custom_call_target="tpu_custom_call" | custom-call | flops 66060288 | bytes 2064384 | tf_op jit(solution)/shard_map/pallas_call | solution.py:158
  96.3 2.3 %shard_map.84 = (f32[2,16,64]{2,1,0:T(8,128)S(1)}, f32[2,16,64]{2,1,0:T(8,128)S(1)}) custom-call(s32[6]{0:T(128)S(1)} %copy-done.13, bf16[64,7168]{1,0:T(8,128)(2,1)S(1)} %collective-permute-done.10.piece, bf16[128,7168]{1,0:T(8,128)(2,1)S(1)} %pad_maximum_fusion.refs_5_.refs_1_.factors, bf16[64,64]{1,0:T(8,128)(2,1)S(1)} %add_convert_fusion.1.choices, ...), custom_call_target="tpu_custom_call" | custom-call | flops 3670016 | bytes 114688 | tf_op jit(solution)/shard_map/pallas_call | solution.py:158
  98.6 2.0 %collective-permute-start.13 = (f32[2,16,64]{2,1,0:T(8,128)S(1)}, f32[2,16,64]{2,1,0:T(8,128)S(1)}, u32[]{:S(2)}, u32[]{:S(2)}) collective-permute-start(f32[2,16,64]{2,1,0:T(8,128)S(1)} %get-tuple-element.92), channel_id=1, source_target_pairs={{0,3},{1,2},{2,1},{3,0},{4,7},{5,6},{6,5},{7,4},{8,11},{9,10},{10,... | collective-permute-start | bytes 24584 | tf_op jit(solution)/shard_map/ppermute | solution.py:293
  100.8 1.1 collective-permute-done.12
  102.0 2.3 %collective-permute-done.11 = f32[2,16,64]{2,1,0:T(8,128)S(1)} collective-permute-done((f32[2,16,64]{2,1,0:T(8,128)S(1)}, f32[2,16,64]{2,1,0:T(8,128)S(1)}, u32[]{:S(2)}, u32[]{:S(2)}) %collective-permute-start.11) | collective-permute-done | bytes 8224 | tf_op jit(solution)/shard_map/ppermute | solution.py:292
  104.5 0.9 collective-permute-start.15
  105.5 1.9 %collective-permute-start.16 = (bf16[2,16,64]{2,1,0:T(8,128)(2,1)S(1)}, bf16[2,16,64]{2,1,0:T(8,128)(2,1)S(1)}, u32[]{:S(2)}, u32[]{:S(2)}) collective-permute-start(bf16[2,16,64]{2,1,0:T(8,128)(2,1)S(1)} %add_convert_fusion.3), channel_id=1, source_target_pairs={{0,8},{2,10},{4,12},{6,14},{8,0},{10,2},{12,4},{14,6},{16,24},{18,... | collective-permute-start | bytes 12296 | tf_op jit(solution)/shard_map/ppermute | solution.py:438
  107.3 0.7 collective-permute-start.17
  108.0 3.2 %shard_map.85 = (f32[1,64,512]{2,1,0:T(8,128)S(1)}, f32[1,64,512]{2,1,0:T(8,128)S(1)}, bf16[1,64,512]{2,1,0:T(8,128)(2,1)S(1)}, bf16[1,64,512]{2,1,0:T(8,128)(2,1)S(1)}) custom-call(s32[6]{0:T(128)S(1)} %copy-done.14, bf16[64,7168]{1,0:T(8,128)(2,1)S(1)} %collective-permute-done.10.piece, bf16[2,7,1024,512]{3,2,1,0:T(8,128)(2,1)S(1)} %copy-done.2, ...), custom_call_target="tpu_custom_call" | custom-call | flops 29360128 | bytes 917504 | tf_op jit(solution)/shard_map/pallas_call | solution.py:158
  111.3 0.6 collective-permute-done.17
  111.9 2.7 %collective-permute-start.19 = (bf16[8,16,64]{2,1,0:T(8,128)(2,1)S(1)}, bf16[8,16,64]{2,1,0:T(8,128)(2,1)S(1)}, u32[]{:S(2)}, u32[]{:S(2)}) collective-permute-start(bf16[8,16,64]{2,1,0:T(8,128)(2,1)S(1)} %pad_maximum_fusion.4), channel_id=1, source_target_pairs={{0,16},{2,18},{4,20},{6,22},{8,24},{10,26},{12,28},{14,30},{16,0},... | collective-permute-start | bytes 49160 | tf_op jit(solution)/shard_map/ppermute | solution.py:438
  115.2 1.5 %collective-permute-start.21 = (bf16[1,64,512]{2,1,0:T(8,128)(2,1)S(1)}, bf16[1,64,512]{2,1,0:T(8,128)(2,1)S(1)}, u32[]{:S(2)}, u32[]{:S(2)}) collective-permute-start(bf16[1,64,512]{2,1,0:T(8,128)(2,1)S(1)} %get-tuple-element.113), channel_id=1, source_target_pairs={{0,1},{1,0},{2,3},{3,2},{4,5},{5,4},{6,7},{7,6},{8,9},{9,8},{10,11... | collective-permute-start | bytes 196616 | tf_op jit(solution)/shard_map/ppermute | solution.py:292
  117.2 1.2 fusion.16
  118.6 1.2 collective-permute-done.21
  119.7 1.2 collective-permute-done.22
  121.2 1.3 %fusion.1 = bf16[256,512]{1,0:T(8,128)(2,1)} fusion(f32[256,512]{1,0:T(8,128)S(1)} %fusion.12, bf16[1024,512]{1,0:T(8,128)(2,1)S(1)} %copy-done.15, bf16[256,1024]{1,0:T(8,128)(2,1)S(1)} %copy-done.16, bf16[256,64]{1,0:T(8,128)(2,1)S(1)} %convolution_convert_fusion.1, bf16[64,1024]{1,0:T(8,128)(2,1)S(1)} %copy-done.18), kind=kOutput, calls=%fused_computation.4 | convolution fusion | flops 302776320 | bytes 2523136 | tf_op jit(solution)/shard_map/dot_general | solution.py:471
  (105 shorter events, 6.6 us)
Async XLA Ops:
  1.4 6.6 %copy-start.20 = (bf16[16,32,512]{2,1,0:T(8,128)(2,1)S(1)}, bf16[16,32,512]{2,1,0:T(8,128)(2,1)}, u32[]{:S(2)}) copy-start(bf16[16,32,512]{2,1,0:T(8,128)(2,1)} %param.12) | copy-start | bytes 1572868
  1.4 2.0 %collective-permute-start = (bf16[32,7168]{1,0:T(8,128)(2,1)S(1)}, bf16[32,7168]{1,0:T(8,128)(2,1)S(1)}, u32[]{:S(2)}, u32[]{:S(2)}) collective-permute-start(bf16[32,7168]{1,0:T(8,128)(2,1)S(1)} %fusion.11), channel_id=1, source_target_pairs={{0,2},{2,0},{8,10},{10,8},{16,18},{18,16},{24,26},{26,24},{28,30},... | collective-permute-start | bytes 1376264 | tf_op jit(solution)/shard_map/ppermute | solution.py:276
  3.5 50.1 %collective-permute-start.7 = (bf16[14336,512]{1,0:T(8,128)(2,1)}, bf16[14336,512]{1,0:T(8,128)(2,1)}, u32[]{:S(2)}, u32[]{:S(2)}) collective-permute-start(bf16[14336,512]{1,0:T(8,128)(2,1)} %refs_7_), channel_id=1, source_target_pairs={{0,2},{2,0},{8,10},{10,8},{16,18},{18,16},{24,26},{26,24},{28,30},... | collective-permute-start | bytes 44040200 | tf_op jit(solution)/shard_map/ppermute | solution.py:276
  3.9 22.9 %collective-permute-start.1 = (bf16[64,7168]{1,0:T(8,128)(2,1)S(1)}, bf16[64,7168]{1,0:T(8,128)(2,1)S(1)}, u32[]{:S(2)}, u32[]{:S(2)}) collective-permute-start(bf16[64,7168]{1,0:T(8,128)(2,1)S(1)} %pad_maximum_fusion.2.refs_0_), channel_id=1, source_target_pairs={{0,8},{8,16},{16,24},{24,28},{28,20},{20,12},{12,4},{4,0},{2,6},{1... | collective-permute-start | bytes 2752520 | tf_op jit(solution)/shard_map/ppermute | solution.py:282
  6.6 22.6 %collective-permute-start.3 = (bf16[64,7168]{1,0:T(8,128)(2,1)S(1)}, bf16[64,7168]{1,0:T(8,128)(2,1)S(1)}, u32[]{:S(2)}, u32[]{:S(2)}) collective-permute-start(bf16[64,7168]{1,0:T(8,128)(2,1)S(1)} %pad_maximum_fusion.2.refs_0_), channel_id=1, source_target_pairs={{0,4},{8,0},{16,8},{24,16},{28,24},{20,28},{12,20},{4,12},{2,10},{... | collective-permute-start | bytes 2752520 | tf_op jit(solution)/shard_map/ppermute | solution.py:282
  6.6 45.5 %collective-permute-start.8 = (bf16[64,14336]{1,0:T(8,128)(2,1)}, bf16[64,14336]{1,0:T(8,128)(2,1)}, u32[]{:S(2)}, u32[]{:S(2)}) collective-permute-start(bf16[64,14336]{1,0:T(8,128)(2,1)} %bitcast.62), channel_id=1, source_target_pairs={{0,2},{2,0},{8,10},{10,8},{16,18},{18,16},{24,26},{26,24},{28,30},... | collective-permute-start | bytes 5505032 | tf_op jit(solution)/shard_map/ppermute | solution.py:276
  8.0 22.9 %collective-permute-start.9 = (bf16[16,32,512]{2,1,0:T(8,128)(2,1)S(1)}, bf16[16,32,512]{2,1,0:T(8,128)(2,1)S(1)}, u32[]{:S(2)}, u32[]{:S(2)}) collective-permute-start(bf16[16,32,512]{2,1,0:T(8,128)(2,1)S(1)} %copy-done.20), channel_id=1, source_target_pairs={{0,1},{1,0},{2,3},{3,2},{4,5},{5,4},{6,7},{7,6},{8,9},{9,8},{10,11... | collective-permute-start | bytes 1572872 | tf_op jit(solution)/shard_map/ppermute | solution.py:305
  26.8 5.2 %copy-start.3 = (bf16[64,7168]{1,0:T(8,128)(2,1)}, bf16[64,7168]{1,0:T(8,128)(2,1)S(1)}, u32[]{:S(2)}) copy-start(bf16[64,7168]{1,0:T(8,128)(2,1)S(1)} %collective-permute-done.1.refs_1_) | copy-start | bytes 2752516
  26.8 23.3 %collective-permute-start.2 = (bf16[64,7168]{1,0:T(8,128)(2,1)S(1)}, bf16[64,7168]{1,0:T(8,128)(2,1)}, u32[]{:S(2)}, u32[]{:S(2)}) collective-permute-start(bf16[64,7168]{1,0:T(8,128)(2,1)S(1)} %collective-permute-done.1.refs_1_), channel_id=1, source_target_pairs={{0,8},{8,16},{16,24},{24,28},{28,20},{20,12},{12,4},{4,0},{2,6},{1... | collective-permute-start | bytes 2752520 | tf_op jit(solution)/shard_map/ppermute | solution.py:282
  29.3 2.7 %copy-start.5 = (bf16[64,7168]{1,0:T(8,128)(2,1)}, bf16[64,7168]{1,0:T(8,128)(2,1)S(1)}, u32[]{:S(2)}) copy-start(bf16[64,7168]{1,0:T(8,128)(2,1)S(1)} %collective-permute-done.3.refs_2_) | copy-start | bytes 2752516
  29.3 20.8 %collective-permute-start.4 = (bf16[64,7168]{1,0:T(8,128)(2,1)S(1)}, bf16[64,7168]{1,0:T(8,128)(2,1)}, u32[]{:S(2)}, u32[]{:S(2)}) collective-permute-start(bf16[64,7168]{1,0:T(8,128)(2,1)S(1)} %collective-permute-done.3.refs_2_), channel_id=1, source_target_pairs={{0,4},{8,0},{16,8},{24,16},{28,24},{20,28},{12,20},{4,12},{2,10},{... | collective-permute-start | bytes 2752520 | tf_op jit(solution)/shard_map/ppermute | solution.py:282
  50.1 31.3 %collective-permute-start.5 = (bf16[64,7168]{1,0:T(8,128)(2,1)}, bf16[64,7168]{1,0:T(8,128)(2,1)}, u32[]{:S(2)}, u32[]{:S(2)}) collective-permute-start(bf16[64,7168]{1,0:T(8,128)(2,1)} %collective-permute-done.2.refs_3_), channel_id=1, source_target_pairs={{0,8},{8,16},{16,24},{24,28},{28,20},{20,12},{12,4},{4,0},{2,6},{1... | collective-permute-start | bytes 2752520 | tf_op jit(solution)/shard_map/ppermute | solution.py:282
  51.2 30.2 %collective-permute-start.6 = (bf16[64,7168]{1,0:T(8,128)(2,1)}, bf16[64,7168]{1,0:T(8,128)(2,1)}, u32[]{:S(2)}, u32[]{:S(2)}) collective-permute-start(bf16[64,7168]{1,0:T(8,128)(2,1)} %collective-permute-done.4.refs_4_), channel_id=1, source_target_pairs={{0,4},{8,0},{16,8},{24,16},{28,24},{20,28},{12,20},{4,12},{2,10},{... | collective-permute-start | bytes 2752520 | tf_op jit(solution)/shard_map/ppermute | solution.py:282
  53.4 0.9 copy-start.21
  53.4 0.9 copy-start.22
  57.6 1.2 copy-start.4
  58.8 1.2 copy-start.6
  59.9 10.2 %copy-start.12 = (s32[6]{0:T(128)}, s32[6]{0:T(128)S(1)}, u32[]{:S(2)}) copy-start(s32[6]{0:T(128)S(1)} %pad_add_fusion.facts) | copy-start | bytes 76
  70.1 5.2 %copy-start = (bf16[2,7,1024,512]{3,2,1,0:T(8,128)(2,1)}, bf16[2,7,1024,512]{3,2,1,0:T(8,128)(2,1)S(1)}, u32[]{:S(2)}) copy-start(bf16[2,7,1024,512]{3,2,1,0:T(8,128)(2,1)S(1)} %get-tuple-element.82.refs_0_.held) | copy-start | bytes 44040196
  75.3 0.8 copy-start.7
  76.1 0.6 copy-start.10
  81.4 14.9 %collective-permute-start.10 = (bf16[64,7168]{1,0:T(8,128)(2,1)}, bf16[64,7168]{1,0:T(8,128)(2,1)S(1)}, u32[]{:S(2)}, u32[]{:S(2)}) collective-permute-start(bf16[64,7168]{1,0:T(8,128)(2,1)} %collective-permute-done.5.piece), channel_id=1, source_target_pairs={{0,8},{8,16},{16,24},{24,28},{28,20},{20,12},{12,4},{4,0},{2,6},{1... | collective-permute-start | bytes 2752520 | tf_op jit(solution)/shard_map/ppermute | solution.py:282
  82.5 5.2 %copy-start.1 = (bf16[2,7,1024,512]{3,2,1,0:T(8,128)(2,1)S(1)}, bf16[2,7,1024,512]{3,2,1,0:T(8,128)(2,1)}, u32[]{:S(2)}) copy-start(bf16[2,7,1024,512]{3,2,1,0:T(8,128)(2,1)} %copy-done) | copy-start | bytes 44040196
  87.7 1.0 copy-start.8
  88.7 0.7 copy-start.9
  89.4 0.8 copy-start.11
  90.2 0.7 copy-start.13
  90.8 17.2 %copy-start.2 = (bf16[2,7,1024,512]{3,2,1,0:T(8,128)(2,1)S(1)}, bf16[2,7,1024,512]{3,2,1,0:T(8,128)(2,1)}, u32[]{:S(2)}) copy-start(bf16[2,7,1024,512]{3,2,1,0:T(8,128)(2,1)} %copy-done) | copy-start | bytes 44040196
  96.3 4.5 %collective-permute-start.14 = (f32[2,3,64,512]{3,2,1,0:T(8,128)S(1)}, f32[2,3,64,512]{3,2,1,0:T(8,128)S(1)}, u32[]{:S(2)}, u32[]{:S(2)}) collective-permute-start(f32[2,3,64,512]{3,2,1,0:T(8,128)S(1)} %get-tuple-element.94), channel_id=1, source_target_pairs={{0,2},{2,0},{8,10},{10,8},{16,18},{18,16},{24,26},{26,24},{28,30},... | collective-permute-start | bytes 2359304 | tf_op jit(solution)/shard_map/ppermute | solution.py:276
  96.3 11.7 %copy-start.14 = (s32[6]{0:T(128)S(1)}, s32[6]{0:T(128)}, u32[]{:S(2)}) copy-start(s32[6]{0:T(128)} %copy-done.12) | copy-start | bytes 76
  98.6 3.4 %collective-permute-start.13 = (f32[2,16,64]{2,1,0:T(8,128)S(1)}, f32[2,16,64]{2,1,0:T(8,128)S(1)}, u32[]{:S(2)}, u32[]{:S(2)}) collective-permute-start(f32[2,16,64]{2,1,0:T(8,128)S(1)} %get-tuple-element.92), channel_id=1, source_target_pairs={{0,3},{1,2},{2,1},{3,0},{4,7},{5,6},{6,5},{7,4},{8,11},{9,10},{10,... | collective-permute-start | bytes 24584 | tf_op jit(solution)/shard_map/ppermute | solution.py:293
  100.6 3.7 %collective-permute-start.11 = (f32[2,16,64]{2,1,0:T(8,128)S(1)}, f32[2,16,64]{2,1,0:T(8,128)S(1)}, u32[]{:S(2)}, u32[]{:S(2)}) collective-permute-start(f32[2,16,64]{2,1,0:T(8,128)S(1)} %get-tuple-element.92), channel_id=1, source_target_pairs={{0,1},{1,0},{2,3},{3,2},{4,5},{5,4},{6,7},{7,6},{8,9},{9,8},{10,11... | collective-permute-start | bytes 24584 | tf_op jit(solution)/shard_map/ppermute | solution.py:292
  100.7 1.2 collective-permute-start.12
  100.8 10.5 %copy-start.17 = (f32[2,3,64,512]{3,2,1,0:T(8,128)}, f32[2,3,64,512]{3,2,1,0:T(8,128)S(1)}, u32[]{:S(2)}) copy-start(f32[2,3,64,512]{3,2,1,0:T(8,128)S(1)} %collective-permute-done.14) | copy-start | bytes 2359300
  104.3 7.6 %collective-permute-start.18 = (bf16[3,64,512]{2,1,0:T(8,128)(2,1)S(1)}, bf16[3,64,512]{2,1,0:T(8,128)(2,1)S(1)}, u32[]{:S(2)}, u32[]{:S(2)}) collective-permute-start(bf16[3,64,512]{2,1,0:T(8,128)(2,1)S(1)} %fusion.20), channel_id=1, source_target_pairs={{0,1},{1,0},{2,3},{3,2},{4,5},{5,4},{6,7},{7,6},{8,9},{9,8},{10,11... | collective-permute-start | bytes 589832 | tf_op jit(solution)/shard_map/ppermute | solution.py:445
  104.5 6.7 %collective-permute-start.15 = (bf16[2,16,64]{2,1,0:T(8,128)(2,1)S(1)}, bf16[2,16,64]{2,1,0:T(8,128)(2,1)S(1)}, u32[]{:S(2)}, u32[]{:S(2)}) collective-permute-start(bf16[2,16,64]{2,1,0:T(8,128)(2,1)S(1)} %add_convert_fusion.3), channel_id=1, source_target_pairs={{0,4},{2,6},{4,0},{6,2},{8,12},{10,14},{12,8},{14,10},{16,20},{18,... | collective-permute-start | bytes 12296 | tf_op jit(solution)/shard_map/ppermute | solution.py:438
  105.5 5.8 %collective-permute-start.16 = (bf16[2,16,64]{2,1,0:T(8,128)(2,1)S(1)}, bf16[2,16,64]{2,1,0:T(8,128)(2,1)S(1)}, u32[]{:S(2)}, u32[]{:S(2)}) collective-permute-start(bf16[2,16,64]{2,1,0:T(8,128)(2,1)S(1)} %add_convert_fusion.3), channel_id=1, source_target_pairs={{0,8},{2,10},{4,12},{6,14},{8,0},{10,2},{12,4},{14,6},{16,24},{18,... | collective-permute-start | bytes 12296 | tf_op jit(solution)/shard_map/ppermute | solution.py:438
  107.3 4.5 %collective-permute-start.17 = (bf16[2,16,64]{2,1,0:T(8,128)(2,1)S(1)}, bf16[2,16,64]{2,1,0:T(8,128)(2,1)S(1)}, u32[]{:S(2)}, u32[]{:S(2)}) collective-permute-start(bf16[2,16,64]{2,1,0:T(8,128)(2,1)S(1)} %add_convert_fusion.3), channel_id=1, source_target_pairs={{0,12},{2,14},{4,8},{6,10},{8,4},{10,6},{12,0},{14,2},{16,28},{18,... | collective-permute-start | bytes 12296 | tf_op jit(solution)/shard_map/ppermute | solution.py:438
  111.2 7.2 %copy-start.19 = (bf16[256,256]{1,0:T(8,128)(2,1)S(1)}, bf16[256,256]{1,0:T(8,128)(2,1)}, u32[]{:S(2)}) copy-start(bf16[256,256]{1,0:T(8,128)(2,1)} %fusion.18) | copy-start | bytes 393220
  111.9 5.2 %collective-permute-start.19 = (bf16[8,16,64]{2,1,0:T(8,128)(2,1)S(1)}, bf16[8,16,64]{2,1,0:T(8,128)(2,1)S(1)}, u32[]{:S(2)}, u32[]{:S(2)}) collective-permute-start(bf16[8,16,64]{2,1,0:T(8,128)(2,1)S(1)} %pad_maximum_fusion.4), channel_id=1, source_target_pairs={{0,16},{2,18},{4,20},{6,22},{8,24},{10,26},{12,28},{14,30},{16,0},... | collective-permute-start | bytes 49160 | tf_op jit(solution)/shard_map/ppermute | solution.py:438
  115.2 5.7 %collective-permute-start.20 = (f32[1,64,512]{2,1,0:T(8,128)S(1)}, f32[1,64,512]{2,1,0:T(8,128)S(1)}, u32[]{:S(2)}, u32[]{:S(2)}) collective-permute-start(f32[1,64,512]{2,1,0:T(8,128)S(1)} %get-tuple-element.112), channel_id=1, source_target_pairs={{0,2},{2,0},{8,10},{10,8},{16,18},{18,16},{24,26},{26,24},{28,30},... | collective-permute-start | bytes 393224 | tf_op jit(solution)/shard_map/ppermute | solution.py:276
  115.2 4.5 %collective-permute-start.21 = (bf16[1,64,512]{2,1,0:T(8,128)(2,1)S(1)}, bf16[1,64,512]{2,1,0:T(8,128)(2,1)S(1)}, u32[]{:S(2)}, u32[]{:S(2)}) collective-permute-start(bf16[1,64,512]{2,1,0:T(8,128)(2,1)S(1)} %get-tuple-element.113), channel_id=1, source_target_pairs={{0,1},{1,0},{2,3},{3,2},{4,5},{5,4},{6,7},{7,6},{8,9},{9,8},{10,11... | collective-permute-start | bytes 196616 | tf_op jit(solution)/shard_map/ppermute | solution.py:292
  116.8 4.1 %collective-permute-start.22 = (bf16[1,64,512]{2,1,0:T(8,128)(2,1)S(1)}, bf16[1,64,512]{2,1,0:T(8,128)(2,1)S(1)}, u32[]{:S(2)}, u32[]{:S(2)}) collective-permute-start(bf16[1,64,512]{2,1,0:T(8,128)(2,1)S(1)} %get-tuple-element.114), channel_id=1, source_target_pairs={{0,3},{1,2},{2,1},{3,0},{4,7},{5,6},{6,5},{7,4},{8,11},{9,10},{10,... | collective-permute-start | bytes 196616 | tf_op jit(solution)/shard_map/ppermute | solution.py:293
  117.1 4.1 %copy-start.15 = (bf16[1024,512]{1,0:T(8,128)(2,1)S(1)}, bf16[1024,512]{1,0:T(8,128)(2,1)}, u32[]{:S(2)}) copy-start(bf16[1024,512]{1,0:T(8,128)(2,1)} %pad_maximum_fusion.1) | copy-start | bytes 3145732
  117.1 4.1 %copy-start.16 = (bf16[256,1024]{1,0:T(8,128)(2,1)S(1)}, bf16[256,1024]{1,0:T(8,128)(2,1)}, u32[]{:S(2)}) copy-start(bf16[256,1024]{1,0:T(8,128)(2,1)} %compare_convert_fusion) | copy-start | bytes 1572868
  117.1 4.1 %copy-start.18 = (bf16[64,1024]{1,0:T(8,128)(2,1)S(1)}, bf16[64,1024]{1,0:T(8,128)(2,1)}, u32[]{:S(2)}) copy-start(bf16[64,1024]{1,0:T(8,128)(2,1)} %fusion.19) | copy-start | bytes 393220

commit v13 on v12

--- a/solution.py
+++ b/solution.py
@@ -149,6 +149,21 @@
     weight_products(lambda here: piece[:, here], held, sums)
     away = [in_lanes(facts[0], total, 0, piece.shape[0] // 2) for total in sums]
     share(facts[2], (base[0], base_sib[0]), away, outs, 0)
+
+
+def final_kernel(pairs, facts, low, spots, mask, copies, second, *refs):
+    kept_more, got_more, kept_one, got_sib, got_mp, got_both, out, delta = refs
+    f32 = jnp.float32
+    own = jnp.dot(spots[...], low[...], preferred_element_type=f32).astype(jnp.bfloat16)
+    spread = jnp.dot(own, copies[...], preferred_element_type=f32).astype(jnp.bfloat16) * mask[...]
+    delta[...] = jnp.dot(spread, second[...], preferred_element_type=f32).reshape(delta.shape)
+    for pair in range(pairs):
+        place = facts[2 + pairs + pair]
+        if pair:
+            value = kept_more[pair - 1] + got_more[pair - 1].astype(f32)
+        else:
+            value = kept_one[0] + got_sib[0] + (got_mp[0].astype(f32) + got_both[0].astype(f32))
+        out[place] = (value + delta[place]).astype(out.dtype)
 
 
 def kernel_call(kernel, facts, arrays, shapes, scratch, flops, weights=(), grant=12):
@@ -323,10 +338,10 @@
     )
     edges = np.cumsum([0, 2 * nodes, far, far, far, far])
     arrived, *rest = [row[a:b] for a, b in zip(edges[:-1], edges[1:])]
-    flags = jnp.where(part == 0, rest[0], rest[2])
-    facts = jnp.concatenate([side[None], part[None].astype(jnp.int32), flags])
-    target = jnp.where(part == 0, rest[1], rest[3])
-    places = target[:, None] == jnp.arange(own_nodes, dtype=jnp.int32)[None, :]
+    facts = jnp.concatenate(
+        [side[None], part[None].astype(jnp.int32)]
+        + [jnp.where(part == 0, a, b) for a, b in zip(rest[:2], rest[2:])]
+    )
     slot_all = slots_of(row_adapter_index, adapter_storage_slot).reshape(owners, row_count)
     ranks = jnp.arange(row_count, dtype=jnp.int32)
     earlier = (slot_all[:, :, None] == slot_all[:, None, :]) & (ranks[None, :] < ranks[:, None])
@@ -386,6 +401,9 @@
     def flops(rows, columns):
         return 2 * rows * depth * columns
 
+    facts, spots, mask, copies, choices, second = lax.optimization_barrier(
+        (facts, spots, mask, copies, choices, second)
+    )
     *early, held = kernel_call(
         functools.partial(early_kernel, len(pieces)),
         facts,
@@ -398,11 +416,7 @@
         weights,
         32,
     )
-    ready = (facts, spots, mask, copies, choices, places, second)
-    one_way, other_way, early, held, ready = lax.optimization_barrier(
-        (one_way, other_way, early, held, ready)
-    )
-    facts, spots, mask, copies, choices, places, second = ready
+    one_way, other_way, early, held = lax.optimization_barrier((one_way, other_way, early, held))
 
     last = turn(one_way, 1)
 
@@ -460,18 +474,26 @@
         low = gather(low, gap, 2)
         gap *= 2
     got_one = to_three(*one)
-    low, got_more = lax.optimization_barrier((low, got_more))
-
-    more = kept_more + got_more.astype(f32)
-    rows = 0
-    for pair in range(1, far):
-        rows = rows + jnp.where(places[pair][:, None, None], more[pair - 1 : pair], 0)
-    own_low = jnp.dot(spots, low.reshape(owners * half, rank), preferred_element_type=f32)
-    spread = jnp.dot(own_low.astype(bf16), copies, preferred_element_type=f32).astype(bf16) * mask
-    delta = jnp.dot(spread, second, preferred_element_type=f32)
-    one = kept_one + got_one[0] + got_one[1].astype(f32) + got_one[2].astype(f32)
-    rows = rows + jnp.where(places[0][:, None, None], one, 0)
-    return (delta + rows.reshape(-1, width)).astype(bf16)
+
+    out = kernel_call(
+        functools.partial(final_kernel, far),
+        facts,
+        (
+            low.reshape(owners * half, rank),
+            spots,
+            mask,
+            copies,
+            second,
+            kept_more,
+            got_more,
+            kept_one,
+            *got_one,
+        ),
+        [((own_nodes, group_rows, width), bf16)],
+        [pltpu.VMEM((own_nodes, group_rows, width), f32)],
+        2 * here * owners * rank * width,
+    )[0]
+    return out.reshape(-1, width)
 
 
 def solution(mesh):

time: 123 us -> 112 us (0.911)
  local copies, waits for them, and re-layouts: 24 us -> 6.57 us
  waiting for transfers between devices: 41.6 us -> 53.7 us
  other arithmetic: 12.5 us -> 4.78 us
  Pallas kernels: 21.1 us -> 23.3 us
  matrix products: 1.42 us -> 0 us
    unnamed x46 -> x14, local copies, waits for them, and re-layouts: 17.4 us -> 2.9 us
    ppermute x7, waiting for transfers between devices: 35.1 us -> 47 us  [turn(): return lax.ppermute(value, 'wide', pairs)]
    ppermute x4, waiting for transfers between devices: 0.63 us -> 3.75 us  [from_node(): lax.ppermute(value, 'wide', [(w, w ^ 2 * gap) for w in range(owners)])]
    pallas_call x4 -> x5, Pallas kernels: 21.1 us -> 23.3 us  [kernel_call(): pl.pallas_call(kernel, in_specs=[pl.BlockSpec(memory_space=pltpu.SMEM)] +...]
    ppermute x4, starting transfers between devices: 6.14 us -> 4.4 us  [from_node(): lax.ppermute(value, 'wide', [(w, w ^ 2 * gap) for w in range(owners)])]
    ppermute x2, waiting for transfers between devices: 3.45 us -> 1.9 us  [to_three(): lax.ppermute(to_mp, INNER, SWAP)]
    convert_element_type x1, other arithmetic: 1.63 us -> 0.15 us  [ringed(): mask = (slot_here == column // piece % owners).astype(bf16)]
    dot_general x2 -> x0, matrix products: 1.42 us -> none  [the longest x1 1.25 us: ringed(): delta = jnp.dot(spread, second, preferred_element_type=f32)]
  transfers between devices with their start and end apart: 23 -> 23, of which waited for: 8 -> 9; matrix products, arithmetic and copies ran while one was open for 14% -> 6% of each run, Pallas kernels for 17% -> 19%
where the time goes in v13:
time: 112 us; the launch traced here: 111 us
  waiting for transfers between devices  53.7 us (48%)
  Pallas kernels  23.3 us (21%)
  starting transfers between devices  22.4 us (20%)
  local copies, waits for them, and re-layouts  6.57 us (6%)
  other arithmetic  4.78 us (4%)
    ppermute x7, waiting for transfers between devices, turn(): return lax.ppermute(value, 'wide', pairs)  47 us
    pallas_call x5, Pallas kernels, kernel_call(): pl.pallas_call(kernel, in_specs=[pl.BlockSpec(memory_space=pltpu.SMEM)] +...  23.3 us
    ppermute x7, starting transfers between devices, turn(): return lax.ppermute(value, 'wide', pairs)  9.34 us
    ppermute x4, starting transfers between devices, from_node(): lax.ppermute(value, 'wide', [(w, w ^ 2 * gap) for w in range(owners)])  4.4 us
    ppermute x4, waiting for transfers between devices, from_node(): lax.ppermute(value, 'wide', [(w, w ^ 2 * gap) for w in range(owners)])  3.75 us
    unnamed x14, local copies, waits for them, and re-layouts  2.9 us
    convert_element_type x2, other arithmetic, hidden_of(): (jax.nn.silu(gate.astype(jnp.float32)) * up.astype(jnp.float32)).astype(j...  2.85 us
    dynamic_slice x2, local copies, waits for them, and re-layouts, half_of(): return lax.dynamic_slice_in_dim(value, which * depth, depth, axis)  2.48 us
  transfers between devices with their start and end apart: 23, of which 9 were waited for; matrix products, arithmetic and copies ran while one was open for 6% of the time, Pallas kernels for 19%

profile of v13, /device:TPU:0, one launch (start us, length us, event | category | flops | bytes accessed | tf_op | source)
XLA Modules:
  0.0 111.0 jit_solution(13631763133087504772)
XLA Ops:
  0.0 1.4 %fusion.9 = bf16[32,7168]{1,0:T(8,128)(2,1)S(1)} fusion(bf16[32,14336]{1,0:T(8,128)(2,1)} %param.9, s32[]{:T(128)S(6)} %select_n.99, bf16[32,14336]{1,0:T(8,128)(2,1)} %param.8), kind=kLoop, calls=%fused_computation.17 | loop fusion | flops 1835008 | bytes 1376260 | tf_op jit(solution)/shard_map/convert_element_type | solution.py:189
  1.4 0.5 collective-permute-start
  2.0 1.4 %fusion.8 = bf16[32,7168]{1,0:T(8,128)(2,1)S(1)} fusion(bf16[32,14336]{1,0:T(8,128)(2,1)} %param.9, s32[]{:T(128)S(6)} %select_n.100, bf16[32,14336]{1,0:T(8,128)(2,1)} %param.8), kind=kLoop, calls=%fused_computation.16 | loop fusion | flops 1835008 | bytes 1376260 | tf_op jit(solution)/shard_map/convert_element_type | solution.py:189
  3.5 0.4 collective-permute-start.1
  3.9 2.7 %collective-permute-start.3 = (bf16[64,7168]{1,0:T(8,128)(2,1)S(1)}, bf16[64,7168]{1,0:T(8,128)(2,1)S(1)}, u32[]{:S(2)}, u32[]{:S(2)}) collective-permute-start(bf16[64,7168]{1,0:T(8,128)(2,1)S(1)} %pad_maximum_fusion.2.refs_0_), channel_id=1, source_target_pairs={{0,8},{8,16},{16,24},{24,28},{28,20},{20,12},{12,4},{4,0},{2,6},{1... | collective-permute-start | bytes 2752520 | tf_op jit(solution)/shard_map/ppermute | solution.py:297
  6.8 1.9 %collective-permute-start.2 = (bf16[16,32,512]{2,1,0:T(8,128)(2,1)S(1)}, bf16[16,32,512]{2,1,0:T(8,128)(2,1)S(1)}, u32[]{:S(2)}, u32[]{:S(2)}) collective-permute-start(bf16[16,32,512]{2,1,0:T(8,128)(2,1)S(1)} %copy-done.4), channel_id=1, source_target_pairs={{0,1},{1,0},{2,3},{3,2},{4,5},{5,4},{6,7},{7,6},{8,9},{9,8},{10,11... | collective-permute-start | bytes 1572872 | tf_op jit(solution)/shard_map/ppermute | solution.py:320
  8.7 18.1 %collective-permute-done.3.refs_1_ = bf16[64,7168]{1,0:T(8,128)(2,1)S(1)} collective-permute-done((bf16[64,7168]{1,0:T(8,128)(2,1)S(1)}, bf16[64,7168]{1,0:T(8,128)(2,1)S(1)}, u32[]{:S(2)}, u32[]{:S(2)}) %collective-permute-start.3) | collective-permute-done | bytes 917536 | tf_op jit(solution)/shard_map/ppermute | solution.py:297
  26.8 2.5 %collective-permute-start.4 = (bf16[64,7168]{1,0:T(8,128)(2,1)S(1)}, bf16[64,7168]{1,0:T(8,128)(2,1)}, u32[]{:S(2)}, u32[]{:S(2)}) collective-permute-start(bf16[64,7168]{1,0:T(8,128)(2,1)S(1)} %collective-permute-done.3.refs_1_), channel_id=1, source_target_pairs={{0,8},{8,16},{16,24},{24,28},{28,20},{20,12},{12,4},{4,0},{2,6},{1... | collective-permute-start | bytes 2752520 | tf_op jit(solution)/shard_map/ppermute | solution.py:297
  29.3 1.2 %constant_dynamic-slice_fusion.1 = bf16[64,7168]{1,0:T(8,128)(2,1)S(1)} fusion(bf16[64,14336]{1,0:T(8,128)(2,1)} %bitcast.22, s32[]{:T(128)S(6)} %select_n.115), kind=kLoop, calls=%fused_computation.70 | loop fusion | bytes 1835012 | tf_op jit(solution)/shard_map/dynamic_slice | solution.py:300
  30.6 19.2 %collective-permute-done.4.refs_3_ = bf16[64,7168]{1,0:T(8,128)(2,1)} collective-permute-done((bf16[64,7168]{1,0:T(8,128)(2,1)S(1)}, bf16[64,7168]{1,0:T(8,128)(2,1)}, u32[]{:S(2)}, u32[]{:S(2)}) %collective-permute-start.4) | collective-permute-done | bytes 917536 | tf_op jit(solution)/shard_map/ppermute | solution.py:297
  49.8 1.6 %collective-permute-start.7 = (bf16[64,7168]{1,0:T(8,128)(2,1)}, bf16[64,7168]{1,0:T(8,128)(2,1)}, u32[]{:S(2)}, u32[]{:S(2)}) collective-permute-start(bf16[64,7168]{1,0:T(8,128)(2,1)} %collective-permute-done.4.refs_3_), channel_id=1, source_target_pairs={{0,8},{8,16},{16,24},{24,28},{28,20},{20,12},{12,4},{4,0},{2,6},{1... | collective-permute-start | bytes 2752520 | tf_op jit(solution)/shard_map/ppermute | solution.py:297
  51.5 0.8 collective-permute-start.8
  52.3 1.2 %constant_dynamic-slice_fusion = bf16[64,7168]{1,0:T(8,128)(2,1)S(1)} fusion(bf16[64,14336]{1,0:T(8,128)(2,1)} %collective-permute-done.9, s32[]{:T(128)S(6)} %select_n.115), kind=kLoop, calls=%fused_computation.69 | loop fusion | bytes 1835012 | tf_op jit(solution)/shard_map/dynamic_slice | solution.py:300
  53.6 0.1 pad_maximum_fusion.refs_5_.refs_1_.factors
  53.7 0.5 copy-done.5
  54.2 0.1 select_reduce_fusion.2
  54.4 0.7 constant_dynamic-slice_fusion.4
  55.2 0.5 convert_reduce_fusion
  55.7 0.1 select_reduce_fusion
  55.9 0.1 eq.170
  56.7 0.1 fusion.12.spots
  56.8 0.2 compare_convert_fusion.mask
  57.0 1.2 %copy-done.1 = bf16[64,7168]{1,0:T(8,128)(2,1)S(1)} copy-done((bf16[64,7168]{1,0:T(8,128)(2,1)S(1)}, bf16[64,7168]{1,0:T(8,128)(2,1)}, u32[]{:S(2)}) %copy-start.1) | copy-done | bytes 917528
  58.1 1.2 %copy-done.3 = bf16[64,7168]{1,0:T(8,128)(2,1)S(1)} copy-done((bf16[64,7168]{1,0:T(8,128)(2,1)S(1)}, bf16[64,7168]{1,0:T(8,128)(2,1)}, u32[]{:S(2)}) %copy-start.3) | copy-done | bytes 917528
  59.3 10.5 %shard_map.82 = (f32[1,64,512]{2,1,0:T(8,128)S(1)}, f32[1,64,512]{2,1,0:T(8,128)S(1)}, f32[4,64,512]{2,1,0:T(8,128)S(1)}, f32[4,64,512]{2,1,0:T(8,128)S(1)}, f32...) custom-call(s32[10]{0:T(128)S(1)} %pad_add_fusion.facts, bf16[64,7168]{1,0:T(8,128)(2,1)S(1)} %copy-done.1, ...), custom_call_target="tpu_custom_call" | custom-call | flops 165150720 | bytes 5160960 | tf_op jit(solution)/shard_map/pallas_call | solution.py:173
  69.8 3.4 %collective-permute-done.7.piece = bf16[64,7168]{1,0:T(8,128)(2,1)} collective-permute-done((bf16[64,7168]{1,0:T(8,128)(2,1)}, bf16[64,7168]{1,0:T(8,128)(2,1)}, u32[]{:S(2)}, u32[]{:S(2)}) %collective-permute-start.7) | collective-permute-done | bytes 917536 | tf_op jit(solution)/shard_map/ppermute | solution.py:297
  73.1 1.7 %collective-permute-start.10 = (bf16[64,7168]{1,0:T(8,128)(2,1)}, bf16[64,7168]{1,0:T(8,128)(2,1)S(1)}, u32[]{:S(2)}, u32[]{:S(2)}) collective-permute-start(bf16[64,7168]{1,0:T(8,128)(2,1)} %collective-permute-done.7.piece), channel_id=1, source_target_pairs={{0,8},{8,16},{16,24},{24,28},{28,20},{20,12},{12,4},{4,0},{2,6},{1... | collective-permute-start | bytes 2752520 | tf_op jit(solution)/shard_map/ppermute | solution.py:297
  74.8 5.3 %shard_map.83 = (f32[2,3,64,512]{3,2,1,0:T(8,128)S(1)}, f32[2,3,64,512]{3,2,1,0:T(8,128)S(1)}, f32[2,32,64]{2,1,0:T(8,128)S(1)}) custom-call(s32[10]{0:T(128)S(1)} %pad_add_fusion.facts, bf16[64,7168]{1,0:T(8,128)(2,1)} %collective-permute-done.7.piece, bf16[64,7168]{1,0:T(8,128)(2,1)} %collective-permute-done.8.other, ...), custom_call_target="tpu_custom_call" | custom-call | flops 66060288 | bytes 2064384 | tf_op jit(solution)/shard_map/pallas_call | solution.py:173
  80.1 0.6 collective-permute-start.14
  80.8 6.4 %collective-permute-done.10.piece = bf16[64,7168]{1,0:T(8,128)(2,1)S(1)} collective-permute-done((bf16[64,7168]{1,0:T(8,128)(2,1)}, bf16[64,7168]{1,0:T(8,128)(2,1)S(1)}, u32[]{:S(2)}, u32[]{:S(2)}) %collective-permute-start.10) | collective-permute-done | bytes 917536 | tf_op jit(solution)/shard_map/ppermute | solution.py:297
  87.2 2.3 %shard_map.84 = (f32[2,16,64]{2,1,0:T(8,128)S(1)}, f32[2,16,64]{2,1,0:T(8,128)S(1)}) custom-call(s32[10]{0:T(128)S(1)} %pad_add_fusion.facts, bf16[64,7168]{1,0:T(8,128)(2,1)S(1)} %collective-permute-done.10.piece, bf16[128,7168]{1,0:T(8,128)(2,1)S(1)} %pad_maximum_fusion.refs_5_.refs_1_.factors, bf16[64,64]{1,0:T(8,128)(2,1)S(1)} %add_convert_fusion.1.choices, ...), custom_call_target="tpu_custom_call" | custom-call | flops 3670016 | bytes 114688 | tf_op jit(solution)/shard_map/pallas_call | solution.py:173
  89.4 0.9 collective-permute-start.13
  90.4 1.2 %collective-permute-start.11 = (f32[2,16,64]{2,1,0:T(8,128)S(1)}, f32[2,16,64]{2,1,0:T(8,128)S(1)}, u32[]{:S(2)}, u32[]{:S(2)}) collective-permute-start(f32[2,16,64]{2,1,0:T(8,128)S(1)} %get-tuple-element.90), channel_id=1, source_target_pairs={{0,1},{1,0},{2,3},{3,2},{4,5},{5,4},{6,7},{7,6},{8,9},{9,8},{10,11... | collective-permute-start | bytes 24584 | tf_op jit(solution)/shard_map/ppermute | solution.py:307
  91.6 0.2 fusion.10
  91.8 1.0 collective-permute-done.12
  92.8 1.3 %collective-permute-done.11 = f32[2,16,64]{2,1,0:T(8,128)S(1)} collective-permute-done((f32[2,16,64]{2,1,0:T(8,128)S(1)}, f32[2,16,64]{2,1,0:T(8,128)S(1)}, u32[]{:S(2)}, u32[]{:S(2)}) %collective-permute-start.11) | collective-permute-done | bytes 8224 | tf_op jit(solution)/shard_map/ppermute | solution.py:307
  94.1 1.3 %collective-permute-start.18 = (bf16[3,64,512]{2,1,0:T(8,128)(2,1)S(1)}, bf16[3,64,512]{2,1,0:T(8,128)(2,1)S(1)}, u32[]{:S(2)}, u32[]{:S(2)}) collective-permute-start(bf16[3,64,512]{2,1,0:T(8,128)(2,1)S(1)} %get-tuple-element.100), channel_id=1, source_target_pairs={{0,1},{1,0},{2,3},{3,2},{4,5},{5,4},{6,7},{7,6},{8,9},{9,8},{10,11... | collective-permute-start | bytes 589832 | tf_op jit(solution)/shard_map/ppermute | solution.py:459
  95.4 1.5 %collective-permute-start.15 = (bf16[2,16,64]{2,1,0:T(8,128)(2,1)S(1)}, bf16[2,16,64]{2,1,0:T(8,128)(2,1)S(1)}, u32[]{:S(2)}, u32[]{:S(2)}) collective-permute-start(bf16[2,16,64]{2,1,0:T(8,128)(2,1)S(1)} %add_convert_fusion.3), channel_id=1, source_target_pairs={{0,4},{2,6},{4,0},{6,2},{8,12},{10,14},{12,8},{14,10},{16,20},{18,... | collective-permute-start | bytes 12296 | tf_op jit(solution)/shard_map/ppermute | solution.py:452
  96.8 1.6 %collective-permute-start.16 = (bf16[2,16,64]{2,1,0:T(8,128)(2,1)S(1)}, bf16[2,16,64]{2,1,0:T(8,128)(2,1)S(1)}, u32[]{:S(2)}, u32[]{:S(2)}) collective-permute-start(bf16[2,16,64]{2,1,0:T(8,128)(2,1)S(1)} %add_convert_fusion.3), channel_id=1, source_target_pairs={{0,8},{2,10},{4,12},{6,14},{8,0},{10,2},{12,4},{14,6},{16,24},{18,... | collective-permute-start | bytes 12296 | tf_op jit(solution)/shard_map/ppermute | solution.py:452
  98.4 0.4 collective-permute-start.17
  98.9 3.2 %shard_map.85 = (f32[1,64,512]{2,1,0:T(8,128)S(1)}, f32[1,64,512]{2,1,0:T(8,128)S(1)}, bf16[1,64,512]{2,1,0:T(8,128)(2,1)S(1)}, bf16[1,64,512]{2,1,0:T(8,128)(2,1)S(1)}) custom-call(s32[10]{0:T(128)S(1)} %pad_add_fusion.facts, bf16[64,7168]{1,0:T(8,128)(2,1)S(1)} %collective-permute-done.10.piece, ...), custom_call_target="tpu_custom_call" | custom-call | flops 29360128 | bytes 917504 | tf_op jit(solution)/shard_map/pallas_call | solution.py:173
  102.1 0.9 collective-permute-done.17
  103.1 0.9 collective-permute-start.19
  104.0 0.6 collective-permute-start.21
  104.6 0.9 collective-permute-start.22
  105.5 2.8 %collective-permute-done.19 = bf16[8,16,64]{2,1,0:T(8,128)(2,1)S(1)} collective-permute-done((bf16[8,16,64]{2,1,0:T(8,128)(2,1)S(1)}, bf16[8,16,64]{2,1,0:T(8,128)(2,1)S(1)}, u32[]{:S(2)}, u32[]{:S(2)}) %collective-permute-start.19) | collective-permute-done | bytes 16416 | tf_op jit(solution)/shard_map/ppermute | solution.py:452
  108.4 0.6 collective-permute-done.21.refs_4_
  109.0 2.1 %shard_map.86 = bf16[4,64,512]{2,1,0:T(8,128)(2,1)} custom-call(s32[10]{0:T(128)S(1)} %pad_add_fusion.facts, bf16[256,64]{1,0:T(8,128)(2,1)S(1)} %bitcast.18, bf16[256,256]{1,0:T(8,128)(2,1)S(1)} %fusion.12.spots, bf16[256,1024]{1,0:T(8,128)(2,1)S(1)} %compare_convert_fusion.mask, bf16[64,1024]{1,0:T(8,128)(2,1)S(1)} %fusion.13.copies, ...), custom_call_target="tpu_custom_call" | custom-call | flops 8388608 | bytes 262144 | tf_op jit(solution)/shard_map/pallas_call | solution.py:173
  (58 shorter events, 1.5 us)
Async XLA Ops:
  1.4 5.4 %copy-start.4 = (bf16[16,32,512]{2,1,0:T(8,128)(2,1)S(1)}, bf16[16,32,512]{2,1,0:T(8,128)(2,1)}, u32[]{:S(2)}) copy-start(bf16[16,32,512]{2,1,0:T(8,128)(2,1)} %param.12) | copy-start | bytes 1572868
  1.4 2.0 %collective-permute-start = (bf16[32,7168]{1,0:T(8,128)(2,1)S(1)}, bf16[32,7168]{1,0:T(8,128)(2,1)S(1)}, u32[]{:S(2)}, u32[]{:S(2)}) collective-permute-start(bf16[32,7168]{1,0:T(8,128)(2,1)S(1)} %fusion.9), channel_id=1, source_target_pairs={{0,2},{2,0},{8,10},{10,8},{16,18},{18,16},{24,26},{26,24},{28,30},... | collective-permute-start | bytes 1376264 | tf_op jit(solution)/shard_map/ppermute | solution.py:291
  3.5 27.2 %copy-start = (bf16[64,7168]{1,0:T(8,128)(2,1)}, bf16[64,7168]{1,0:T(8,128)(2,1)S(1)}, u32[]{:S(2)}) copy-start(bf16[64,7168]{1,0:T(8,128)(2,1)S(1)} %pad_maximum_fusion.2.refs_0_) | copy-start | bytes 2752516
  3.5 50.2 %collective-permute-start.1 = (bf16[14336,512]{1,0:T(8,128)(2,1)}, bf16[14336,512]{1,0:T(8,128)(2,1)}, u32[]{:S(2)}, u32[]{:S(2)}) collective-permute-start(bf16[14336,512]{1,0:T(8,128)(2,1)} %refs_7_), channel_id=1, source_target_pairs={{0,2},{2,0},{8,10},{10,8},{16,18},{18,16},{24,26},{26,24},{28,30},... | collective-permute-start | bytes 44040200 | tf_op jit(solution)/shard_map/ppermute | solution.py:291
  3.9 22.9 %collective-permute-start.3 = (bf16[64,7168]{1,0:T(8,128)(2,1)S(1)}, bf16[64,7168]{1,0:T(8,128)(2,1)S(1)}, u32[]{:S(2)}, u32[]{:S(2)}) collective-permute-start(bf16[64,7168]{1,0:T(8,128)(2,1)S(1)} %pad_maximum_fusion.2.refs_0_), channel_id=1, source_target_pairs={{0,8},{8,16},{16,24},{24,28},{28,20},{20,12},{12,4},{4,0},{2,6},{1... | collective-permute-start | bytes 2752520 | tf_op jit(solution)/shard_map/ppermute | solution.py:297
  6.6 22.6 %collective-permute-start.5 = (bf16[64,7168]{1,0:T(8,128)(2,1)S(1)}, bf16[64,7168]{1,0:T(8,128)(2,1)}, u32[]{:S(2)}, u32[]{:S(2)}) collective-permute-start(bf16[64,7168]{1,0:T(8,128)(2,1)S(1)} %pad_maximum_fusion.2.refs_0_), channel_id=1, source_target_pairs={{0,4},{8,0},{16,8},{24,16},{28,24},{20,28},{12,20},{4,12},{2,10},{... | collective-permute-start | bytes 2752520 | tf_op jit(solution)/shard_map/ppermute | solution.py:297
  6.6 45.7 %collective-permute-start.9 = (bf16[64,14336]{1,0:T(8,128)(2,1)}, bf16[64,14336]{1,0:T(8,128)(2,1)}, u32[]{:S(2)}, u32[]{:S(2)}) collective-permute-start(bf16[64,14336]{1,0:T(8,128)(2,1)} %bitcast.21), channel_id=1, source_target_pairs={{0,2},{2,0},{8,10},{10,8},{16,18},{18,16},{24,26},{26,24},{28,30},... | collective-permute-start | bytes 5505032 | tf_op jit(solution)/shard_map/ppermute | solution.py:291
  6.8 23.8 %collective-permute-start.2 = (bf16[16,32,512]{2,1,0:T(8,128)(2,1)S(1)}, bf16[16,32,512]{2,1,0:T(8,128)(2,1)S(1)}, u32[]{:S(2)}, u32[]{:S(2)}) collective-permute-start(bf16[16,32,512]{2,1,0:T(8,128)(2,1)S(1)} %copy-done.4), channel_id=1, source_target_pairs={{0,1},{1,0},{2,3},{3,2},{4,5},{5,4},{6,7},{7,6},{8,9},{9,8},{10,11... | collective-permute-start | bytes 1572872 | tf_op jit(solution)/shard_map/ppermute | solution.py:320
  26.8 3.9 %copy-start.2 = (bf16[64,7168]{1,0:T(8,128)(2,1)}, bf16[64,7168]{1,0:T(8,128)(2,1)S(1)}, u32[]{:S(2)}) copy-start(bf16[64,7168]{1,0:T(8,128)(2,1)S(1)} %collective-permute-done.3.refs_1_) | copy-start | bytes 2752516
  26.8 23.1 %collective-permute-start.4 = (bf16[64,7168]{1,0:T(8,128)(2,1)S(1)}, bf16[64,7168]{1,0:T(8,128)(2,1)}, u32[]{:S(2)}, u32[]{:S(2)}) collective-permute-start(bf16[64,7168]{1,0:T(8,128)(2,1)S(1)} %collective-permute-done.3.refs_1_), channel_id=1, source_target_pairs={{0,8},{8,16},{16,24},{24,28},{28,20},{20,12},{12,4},{4,0},{2,6},{1... | collective-permute-start | bytes 2752520 | tf_op jit(solution)/shard_map/ppermute | solution.py:297
  29.3 20.6 %collective-permute-start.6 = (bf16[64,7168]{1,0:T(8,128)(2,1)}, bf16[64,7168]{1,0:T(8,128)(2,1)}, u32[]{:S(2)}, u32[]{:S(2)}) collective-permute-start(bf16[64,7168]{1,0:T(8,128)(2,1)} %collective-permute-done.5.refs_2_), channel_id=1, source_target_pairs={{0,4},{8,0},{16,8},{24,16},{28,24},{20,28},{12,20},{4,12},{2,10},{... | collective-permute-start | bytes 2752520 | tf_op jit(solution)/shard_map/ppermute | solution.py:297
  49.8 23.3 %collective-permute-start.7 = (bf16[64,7168]{1,0:T(8,128)(2,1)}, bf16[64,7168]{1,0:T(8,128)(2,1)}, u32[]{:S(2)}, u32[]{:S(2)}) collective-permute-start(bf16[64,7168]{1,0:T(8,128)(2,1)} %collective-permute-done.4.refs_3_), channel_id=1, source_target_pairs={{0,8},{8,16},{16,24},{24,28},{28,20},{20,12},{12,4},{4,0},{2,6},{1... | collective-permute-start | bytes 2752520 | tf_op jit(solution)/shard_map/ppermute | solution.py:297
  51.5 21.7 %collective-permute-start.8 = (bf16[64,7168]{1,0:T(8,128)(2,1)}, bf16[64,7168]{1,0:T(8,128)(2,1)}, u32[]{:S(2)}, u32[]{:S(2)}) collective-permute-start(bf16[64,7168]{1,0:T(8,128)(2,1)} %collective-permute-done.6.refs_4_), channel_id=1, source_target_pairs={{0,4},{8,0},{16,8},{24,16},{28,24},{20,28},{12,20},{4,12},{2,10},{... | collective-permute-start | bytes 2752520 | tf_op jit(solution)/shard_map/ppermute | solution.py:297
  53.5 0.7 copy-start.5
  53.6 0.7 copy-start.6
  56.9 1.2 %copy-start.1 = (bf16[64,7168]{1,0:T(8,128)(2,1)S(1)}, bf16[64,7168]{1,0:T(8,128)(2,1)}, u32[]{:S(2)}) copy-start(bf16[64,7168]{1,0:T(8,128)(2,1)} %copy-done) | copy-start | bytes 2752516
  58.1 1.2 %copy-start.3 = (bf16[64,7168]{1,0:T(8,128)(2,1)S(1)}, bf16[64,7168]{1,0:T(8,128)(2,1)}, u32[]{:S(2)}) copy-start(bf16[64,7168]{1,0:T(8,128)(2,1)} %copy-done.2) | copy-start | bytes 2752516
  73.1 14.0 %collective-permute-start.10 = (bf16[64,7168]{1,0:T(8,128)(2,1)}, bf16[64,7168]{1,0:T(8,128)(2,1)S(1)}, u32[]{:S(2)}, u32[]{:S(2)}) collective-permute-start(bf16[64,7168]{1,0:T(8,128)(2,1)} %collective-permute-done.7.piece), channel_id=1, source_target_pairs={{0,8},{8,16},{16,24},{24,28},{28,20},{20,12},{12,4},{4,0},{2,6},{1... | collective-permute-start | bytes 2752520 | tf_op jit(solution)/shard_map/ppermute | solution.py:297
  80.1 11.5 %collective-permute-start.14 = (f32[2,3,64,512]{3,2,1,0:T(8,128)S(1)}, f32[2,3,64,512]{3,2,1,0:T(8,128)S(1)}, u32[]{:S(2)}, u32[]{:S(2)}) collective-permute-start(f32[2,3,64,512]{3,2,1,0:T(8,128)S(1)} %get-tuple-element.92), channel_id=1, source_target_pairs={{0,2},{2,0},{8,10},{10,8},{16,18},{18,16},{24,26},{26,24},{28,30},... | collective-permute-start | bytes 2359304 | tf_op jit(solution)/shard_map/ppermute | solution.py:291
  89.4 3.3 %collective-permute-start.13 = (f32[2,16,64]{2,1,0:T(8,128)S(1)}, f32[2,16,64]{2,1,0:T(8,128)S(1)}, u32[]{:S(2)}, u32[]{:S(2)}) collective-permute-start(f32[2,16,64]{2,1,0:T(8,128)S(1)} %get-tuple-element.90), channel_id=1, source_target_pairs={{0,3},{1,2},{2,1},{3,0},{4,7},{5,6},{6,5},{7,4},{8,11},{9,10},{10,... | collective-permute-start | bytes 24584 | tf_op jit(solution)/shard_map/ppermute | solution.py:308
  90.4 3.7 %collective-permute-start.11 = (f32[2,16,64]{2,1,0:T(8,128)S(1)}, f32[2,16,64]{2,1,0:T(8,128)S(1)}, u32[]{:S(2)}, u32[]{:S(2)}) collective-permute-start(f32[2,16,64]{2,1,0:T(8,128)S(1)} %get-tuple-element.90), channel_id=1, source_target_pairs={{0,1},{1,0},{2,3},{3,2},{4,5},{5,4},{6,7},{7,6},{8,9},{9,8},{10,11... | collective-permute-start | bytes 24584 | tf_op jit(solution)/shard_map/ppermute | solution.py:307
  91.6 1.2 %collective-permute-start.12 = (f32[2,16,64]{2,1,0:T(8,128)S(1)}, f32[2,16,64]{2,1,0:T(8,128)S(1)}, u32[]{:S(2)}, u32[]{:S(2)}) collective-permute-start(f32[2,16,64]{2,1,0:T(8,128)S(1)} %get-tuple-element.89), channel_id=1, source_target_pairs={{0,2},{2,0},{8,10},{10,8},{16,18},{18,16},{24,26},{26,24},{28,30},... | collective-permute-start | bytes 24584 | tf_op jit(solution)/shard_map/ppermute | solution.py:291
  94.1 8.9 %collective-permute-start.18 = (bf16[3,64,512]{2,1,0:T(8,128)(2,1)S(1)}, bf16[3,64,512]{2,1,0:T(8,128)(2,1)S(1)}, u32[]{:S(2)}, u32[]{:S(2)}) collective-permute-start(bf16[3,64,512]{2,1,0:T(8,128)(2,1)S(1)} %get-tuple-element.100), channel_id=1, source_target_pairs={{0,1},{1,0},{2,3},{3,2},{4,5},{5,4},{6,7},{7,6},{8,9},{9,8},{10,11... | collective-permute-start | bytes 589832 | tf_op jit(solution)/shard_map/ppermute | solution.py:459
  95.4 6.7 %collective-permute-start.15 = (bf16[2,16,64]{2,1,0:T(8,128)(2,1)S(1)}, bf16[2,16,64]{2,1,0:T(8,128)(2,1)S(1)}, u32[]{:S(2)}, u32[]{:S(2)}) collective-permute-start(bf16[2,16,64]{2,1,0:T(8,128)(2,1)S(1)} %add_convert_fusion.3), channel_id=1, source_target_pairs={{0,4},{2,6},{4,0},{6,2},{8,12},{10,14},{12,8},{14,10},{16,20},{18,... | collective-permute-start | bytes 12296 | tf_op jit(solution)/shard_map/ppermute | solution.py:452
  96.8 5.2 %collective-permute-start.16 = (bf16[2,16,64]{2,1,0:T(8,128)(2,1)S(1)}, bf16[2,16,64]{2,1,0:T(8,128)(2,1)S(1)}, u32[]{:S(2)}, u32[]{:S(2)}) collective-permute-start(bf16[2,16,64]{2,1,0:T(8,128)(2,1)S(1)} %add_convert_fusion.3), channel_id=1, source_target_pairs={{0,8},{2,10},{4,12},{6,14},{8,0},{10,2},{12,4},{14,6},{16,24},{18,... | collective-permute-start | bytes 12296 | tf_op jit(solution)/shard_map/ppermute | solution.py:452
  98.4 4.5 %collective-permute-start.17 = (bf16[2,16,64]{2,1,0:T(8,128)(2,1)S(1)}, bf16[2,16,64]{2,1,0:T(8,128)(2,1)S(1)}, u32[]{:S(2)}, u32[]{:S(2)}) collective-permute-start(bf16[2,16,64]{2,1,0:T(8,128)(2,1)S(1)} %add_convert_fusion.3), channel_id=1, source_target_pairs={{0,12},{2,14},{4,8},{6,10},{8,4},{10,6},{12,0},{14,2},{16,28},{18,... | collective-permute-start | bytes 12296 | tf_op jit(solution)/shard_map/ppermute | solution.py:452
  103.0 6.0 %collective-permute-start.20 = (f32[1,64,512]{2,1,0:T(8,128)S(1)}, f32[1,64,512]{2,1,0:T(8,128)S(1)}, u32[]{:S(2)}, u32[]{:S(2)}) collective-permute-start(f32[1,64,512]{2,1,0:T(8,128)S(1)} %get-tuple-element.108), channel_id=1, source_target_pairs={{0,2},{2,0},{8,10},{10,8},{16,18},{18,16},{24,26},{26,24},{28,30},... | collective-permute-start | bytes 393224 | tf_op jit(solution)/shard_map/ppermute | solution.py:291
  103.1 5.3 %collective-permute-start.19 = (bf16[8,16,64]{2,1,0:T(8,128)(2,1)S(1)}, bf16[8,16,64]{2,1,0:T(8,128)(2,1)S(1)}, u32[]{:S(2)}, u32[]{:S(2)}) collective-permute-start(bf16[8,16,64]{2,1,0:T(8,128)(2,1)S(1)} %pad_maximum_fusion.4), channel_id=1, source_target_pairs={{0,16},{2,18},{4,20},{6,22},{8,24},{10,26},{12,28},{14,30},{16,0},... | collective-permute-start | bytes 49160 | tf_op jit(solution)/shard_map/ppermute | solution.py:452
  104.0 5.0 %collective-permute-start.21 = (bf16[1,64,512]{2,1,0:T(8,128)(2,1)S(1)}, bf16[1,64,512]{2,1,0:T(8,128)(2,1)S(1)}, u32[]{:S(2)}, u32[]{:S(2)}) collective-permute-start(bf16[1,64,512]{2,1,0:T(8,128)(2,1)S(1)} %get-tuple-element.109), channel_id=1, source_target_pairs={{0,1},{1,0},{2,3},{3,2},{4,5},{5,4},{6,7},{7,6},{8,9},{9,8},{10,11... | collective-permute-start | bytes 196616 | tf_op jit(solution)/shard_map/ppermute | solution.py:307
  104.6 4.4 %collective-permute-start.22 = (bf16[1,64,512]{2,1,0:T(8,128)(2,1)S(1)}, bf16[1,64,512]{2,1,0:T(8,128)(2,1)S(1)}, u32[]{:S(2)}, u32[]{:S(2)}) collective-permute-start(bf16[1,64,512]{2,1,0:T(8,128)(2,1)S(1)} %get-tuple-element.110), channel_id=1, source_target_pairs={{0,3},{1,2},{2,1},{3,0},{4,7},{5,6},{6,5},{7,4},{8,11},{9,10},{10,... | collective-permute-start | bytes 196616 | tf_op jit(solution)/shard_map/ppermute | solution.py:308

commit v14 on v13

--- a/solution.py
+++ b/solution.py
@@ -51,16 +51,13 @@
 def factor_products(rows_of, table, low):
     depth = table.shape[1]
     tile = tile_of(depth)
-    low[...] = jnp.zeros_like(low)
-
-    def step(index, carry):
-        here = pl.ds(pl.multiple_of(index * tile, 128), tile)
-        low[...] += lax.dot_general(
+    total = jnp.zeros(low.shape, jnp.float32)
+    for index in range(depth // tile):
+        here = slice(index * tile, (index + 1) * tile)
+        total += lax.dot_general(
             rows_of(here), table[:, here], (((1,), (1,)), ((), ())), preferred_element_type=jnp.float32
         )
-        return carry
-
-    lax.fori_loop(0, depth // tile, step, 0)
+    low[...] = total
 
 
 def in_lanes(lane, total, index, height):
@@ -151,19 +148,22 @@
     share(facts[2], (base[0], base_sib[0]), away, outs, 0)
 
 
-def final_kernel(pairs, facts, low, spots, mask, copies, second, *refs):
-    kept_more, got_more, kept_one, got_sib, got_mp, got_both, out, delta = refs
+def delta_kernel(pairs, facts, low, spots, mask, copies, second, kept, got, out):
     f32 = jnp.float32
     own = jnp.dot(spots[...], low[...], preferred_element_type=f32).astype(jnp.bfloat16)
     spread = jnp.dot(own, copies[...], preferred_element_type=f32).astype(jnp.bfloat16) * mask[...]
-    delta[...] = jnp.dot(spread, second[...], preferred_element_type=f32).reshape(delta.shape)
-    for pair in range(pairs):
+    out[...] = jnp.dot(spread, second[...], preferred_element_type=f32).reshape(out.shape)
+    for pair in range(1, pairs):
         place = facts[2 + pairs + pair]
-        if pair:
-            value = kept_more[pair - 1] + got_more[pair - 1].astype(f32)
-        else:
-            value = kept_one[0] + got_sib[0] + (got_mp[0].astype(f32) + got_both[0].astype(f32))
-        out[place] = (value + delta[place]).astype(out.dtype)
+        out[place] = out[place] + (kept[pair - 1] + got[pair - 1].astype(f32))
+
+
+def final_kernel(pairs, facts, rest, kept, got_sib, got_mp, got_both, out):
+    f32 = jnp.float32
+    value = kept[0] + got_sib[0] + (got_mp[0].astype(f32) + got_both[0].astype(f32))
+    for place in range(out.shape[0]):
+        there = jnp.where(facts[2 + pairs] == place, value, 0)
+        out[place] = (rest[place] + there).astype(out.dtype)
 
 
 def kernel_call(kernel, facts, arrays, shapes, scratch, flops, weights=(), grant=12):
@@ -475,23 +475,22 @@
         gap *= 2
     got_one = to_three(*one)
 
+    shape = (own_nodes, group_rows, width)
+    rest = kernel_call(
+        functools.partial(delta_kernel, far),
+        facts,
+        (low.reshape(owners * half, rank), spots, mask, copies, second, kept_more, got_more),
+        [(shape, f32)],
+        [],
+        2 * here * owners * rank * width,
+    )[0]
     out = kernel_call(
         functools.partial(final_kernel, far),
         facts,
-        (
-            low.reshape(owners * half, rank),
-            spots,
-            mask,
-            copies,
-            second,
-            kept_more,
-            got_more,
-            kept_one,
-            *got_one,
-        ),
-        [((own_nodes, group_rows, width), bf16)],
-        [pltpu.VMEM((own_nodes, group_rows, width), f32)],
-        2 * here * owners * rank * width,
+        (rest, kept_one, *got_one),
+        [(shape, bf16)],
+        [],
+        here * width,
     )[0]
     return out.reshape(-1, width)
 

time: 112 us -> 113 us (level)
  Pallas kernels: 23.3 us -> 27.3 us
  waiting for transfers between devices: 53.7 us -> 50.1 us
  starting transfers between devices: 22.4 us -> 23.9 us
    pallas_call x5 -> x6, Pallas kernels: 23.3 us -> 27.3 us  [kernel_call(): pl.pallas_call(kernel, in_specs=[pl.BlockSpec(memory_space=pltpu.SMEM)] +...]
    ppermute x4, waiting for transfers between devices: 3.75 us -> 1.9 us  [from_node(): lax.ppermute(value, 'wide', [(w, w ^ 2 * gap) for w in range(owners)])]
    ppermute x7, waiting for transfers between devices: 47 us -> 45.3 us  [turn(): return lax.ppermute(value, 'wide', pairs)]
    ppermute x4, starting transfers between devices: 4.4 us -> 5.79 us  [from_node(): lax.ppermute(value, 'wide', [(w, w ^ 2 * gap) for w in range(owners)])]
  transfers between devices with their start and end apart: 23 -> 23, of which waited for: 9 -> 9; matrix products, arithmetic and copies ran while one was open for 6% -> 6% of each run, Pallas kernels for 19% -> 23%
where the time goes in v14:
time: 113 us
  waiting for transfers between devices  50.1 us (44%)
  Pallas kernels  27.3 us (24%)
  starting transfers between devices  23.9 us (21%)
  local copies, waits for them, and re-layouts  6.57 us (6%)
  other arithmetic  4.78 us (4%)
    ppermute x7, waiting for transfers between devices, turn(): return lax.ppermute(value, 'wide', pairs)  45.3 us
    pallas_call x6, Pallas kernels, kernel_call(): pl.pallas_call(kernel, in_specs=[pl.BlockSpec(memory_space=pltpu.SMEM)] +...  27.3 us
    ppermute x7, starting transfers between devices, turn(): return lax.ppermute(value, 'wide', pairs)  9.15 us
    ppermute x4, starting transfers between devices, from_node(): lax.ppermute(value, 'wide', [(w, w ^ 2 * gap) for w in range(owners)])  5.79 us
    unnamed x14, local copies, waits for them, and re-layouts  2.9 us
    convert_element_type x2, other arithmetic, hidden_of(): (jax.nn.silu(gate.astype(jnp.float32)) * up.astype(jnp.float32)).astype(j...  2.85 us
    ppermute x2, starting transfers between devices, to_three(): lax.ppermute(to_mp, INNER, SWAP)  2.59 us
    dynamic_slice x2, local copies, waits for them, and re-layouts, half_of(): return lax.dynamic_slice_in_dim(value, which * depth, depth, axis)  2.48 us
  transfers between devices with their start and end apart: 23, of which 9 were waited for; matrix products, arithmetic and copies ran while one was open for 6% of the time, Pallas kernels for 23%

profile of v14, /device:TPU:0, one launch (start us, length us, event | category | flops | bytes accessed | tf_op | source)
XLA Modules:
  0.0 113.0 jit_solution(1262842336719159104)
XLA Ops:
  0.0 1.4 %fusion.9 = bf16[32,7168]{1,0:T(8,128)(2,1)S(1)} fusion(bf16[32,14336]{1,0:T(8,128)(2,1)} %param.9, s32[]{:T(128)S(6)} %select_n.99, bf16[32,14336]{1,0:T(8,128)(2,1)} %param.8), kind=kLoop, calls=%fused_computation.17 | loop fusion | flops 1835008 | bytes 1376260 | tf_op jit(solution)/shard_map/convert_element_type | solution.py:189
  1.4 0.5 collective-permute-start
  2.0 1.4 %fusion.8 = bf16[32,7168]{1,0:T(8,128)(2,1)S(1)} fusion(bf16[32,14336]{1,0:T(8,128)(2,1)} %param.9, s32[]{:T(128)S(6)} %select_n.100, bf16[32,14336]{1,0:T(8,128)(2,1)} %param.8), kind=kLoop, calls=%fused_computation.16 | loop fusion | flops 1835008 | bytes 1376260 | tf_op jit(solution)/shard_map/convert_element_type | solution.py:189
  3.5 0.4 collective-permute-start.1
  3.9 2.7 %collective-permute-start.3 = (bf16[64,7168]{1,0:T(8,128)(2,1)S(1)}, bf16[64,7168]{1,0:T(8,128)(2,1)S(1)}, u32[]{:S(2)}, u32[]{:S(2)}) collective-permute-start(bf16[64,7168]{1,0:T(8,128)(2,1)S(1)} %pad_maximum_fusion.2.refs_0_), channel_id=1, source_target_pairs={{0,8},{8,16},{16,24},{24,28},{28,20},{20,12},{12,4},{4,0},{2,6},{1... | collective-permute-start | bytes 2752520 | tf_op jit(solution)/shard_map/ppermute | solution.py:297
  6.8 1.9 %collective-permute-start.2 = (bf16[16,32,512]{2,1,0:T(8,128)(2,1)S(1)}, bf16[16,32,512]{2,1,0:T(8,128)(2,1)S(1)}, u32[]{:S(2)}, u32[]{:S(2)}) collective-permute-start(bf16[16,32,512]{2,1,0:T(8,128)(2,1)S(1)} %copy-done.4), channel_id=1, source_target_pairs={{0,1},{1,0},{2,3},{3,2},{4,5},{5,4},{6,7},{7,6},{8,9},{9,8},{10,11... | collective-permute-start | bytes 1572872 | tf_op jit(solution)/shard_map/ppermute | solution.py:320
  8.7 18.1 %collective-permute-done.3.refs_1_ = bf16[64,7168]{1,0:T(8,128)(2,1)S(1)} collective-permute-done((bf16[64,7168]{1,0:T(8,128)(2,1)S(1)}, bf16[64,7168]{1,0:T(8,128)(2,1)S(1)}, u32[]{:S(2)}, u32[]{:S(2)}) %collective-permute-start.3) | collective-permute-done | bytes 917536 | tf_op jit(solution)/shard_map/ppermute | solution.py:297
  26.8 2.5 %collective-permute-start.4 = (bf16[64,7168]{1,0:T(8,128)(2,1)S(1)}, bf16[64,7168]{1,0:T(8,128)(2,1)}, u32[]{:S(2)}, u32[]{:S(2)}) collective-permute-start(bf16[64,7168]{1,0:T(8,128)(2,1)S(1)} %collective-permute-done.3.refs_1_), channel_id=1, source_target_pairs={{0,8},{8,16},{16,24},{24,28},{28,20},{20,12},{12,4},{4,0},{2,6},{1... | collective-permute-start | bytes 2752520 | tf_op jit(solution)/shard_map/ppermute | solution.py:297
  29.3 1.2 %constant_dynamic-slice_fusion.1 = bf16[64,7168]{1,0:T(8,128)(2,1)S(1)} fusion(bf16[64,14336]{1,0:T(8,128)(2,1)} %bitcast.22, s32[]{:T(128)S(6)} %select_n.115), kind=kLoop, calls=%fused_computation.70 | loop fusion | bytes 1835012 | tf_op jit(solution)/shard_map/dynamic_slice | solution.py:300
  30.6 19.2 %collective-permute-done.4.refs_3_ = bf16[64,7168]{1,0:T(8,128)(2,1)} collective-permute-done((bf16[64,7168]{1,0:T(8,128)(2,1)S(1)}, bf16[64,7168]{1,0:T(8,128)(2,1)}, u32[]{:S(2)}, u32[]{:S(2)}) %collective-permute-start.4) | collective-permute-done | bytes 917536 | tf_op jit(solution)/shard_map/ppermute | solution.py:297
  49.8 1.6 %collective-permute-start.7 = (bf16[64,7168]{1,0:T(8,128)(2,1)}, bf16[64,7168]{1,0:T(8,128)(2,1)}, u32[]{:S(2)}, u32[]{:S(2)}) collective-permute-start(bf16[64,7168]{1,0:T(8,128)(2,1)} %collective-permute-done.4.refs_3_), channel_id=1, source_target_pairs={{0,8},{8,16},{16,24},{24,28},{28,20},{20,12},{12,4},{4,0},{2,6},{1... | collective-permute-start | bytes 2752520 | tf_op jit(solution)/shard_map/ppermute | solution.py:297
  51.5 0.8 collective-permute-start.8
  52.3 1.2 %constant_dynamic-slice_fusion = bf16[64,7168]{1,0:T(8,128)(2,1)S(1)} fusion(bf16[64,14336]{1,0:T(8,128)(2,1)} %collective-permute-done.9, s32[]{:T(128)S(6)} %select_n.115), kind=kLoop, calls=%fused_computation.69 | loop fusion | bytes 1835012 | tf_op jit(solution)/shard_map/dynamic_slice | solution.py:300
  53.6 0.1 pad_maximum_fusion.refs_5_.refs_1_.factors
  53.7 0.5 copy-done.5
  54.2 0.1 select_reduce_fusion.2
  54.4 0.7 constant_dynamic-slice_fusion.4
  55.2 0.5 convert_reduce_fusion
  55.7 0.1 select_reduce_fusion
  55.9 0.1 eq.170
  56.0 0.1 eq.173
  56.7 0.1 fusion.12.spots
  56.8 0.2 compare_convert_fusion.mask
  57.0 1.2 %copy-done.1 = bf16[64,7168]{1,0:T(8,128)(2,1)S(1)} copy-done((bf16[64,7168]{1,0:T(8,128)(2,1)S(1)}, bf16[64,7168]{1,0:T(8,128)(2,1)}, u32[]{:S(2)}) %copy-start.1) | copy-done | bytes 917528
  58.1 1.2 %copy-done.3 = bf16[64,7168]{1,0:T(8,128)(2,1)S(1)} copy-done((bf16[64,7168]{1,0:T(8,128)(2,1)S(1)}, bf16[64,7168]{1,0:T(8,128)(2,1)}, u32[]{:S(2)}) %copy-start.3) | copy-done | bytes 917528
  59.3 15.6 %shard_map.82 = (f32[1,64,512]{2,1,0:T(8,128)S(1)}, f32[1,64,512]{2,1,0:T(8,128)S(1)}, f32[4,64,512]{2,1,0:T(8,128)S(1)}, f32[4,64,512]{2,1,0:T(8,128)S(1)}, f32...) custom-call(s32[10]{0:T(128)S(1)} %pad_add_fusion.facts, bf16[64,7168]{1,0:T(8,128)(2,1)S(1)} %copy-done.1, ...), custom_call_target="tpu_custom_call" | custom-call | flops 165150720 | bytes 5160960 | tf_op jit(solution)/shard_map/pallas_call | solution.py:173
  74.9 1.5 %collective-permute-start.10 = (bf16[64,7168]{1,0:T(8,128)(2,1)}, bf16[64,7168]{1,0:T(8,128)(2,1)S(1)}, u32[]{:S(2)}, u32[]{:S(2)}) collective-permute-start(bf16[64,7168]{1,0:T(8,128)(2,1)} %collective-permute-done.7.piece), channel_id=1, source_target_pairs={{0,8},{8,16},{16,24},{24,28},{28,20},{20,12},{12,4},{4,0},{2,6},{1... | collective-permute-start | bytes 2752520 | tf_op jit(solution)/shard_map/ppermute | solution.py:297
  76.4 4.4 %shard_map.83 = (f32[2,3,64,512]{3,2,1,0:T(8,128)S(1)}, f32[2,3,64,512]{3,2,1,0:T(8,128)S(1)}, f32[2,32,64]{2,1,0:T(8,128)S(1)}) custom-call(s32[10]{0:T(128)S(1)} %pad_add_fusion.facts, bf16[64,7168]{1,0:T(8,128)(2,1)} %collective-permute-done.7.piece, bf16[64,7168]{1,0:T(8,128)(2,1)} %collective-permute-done.8.other, ...), custom_call_target="tpu_custom_call" | custom-call | flops 66060288 | bytes 2064384 | tf_op jit(solution)/shard_map/pallas_call | solution.py:173
  80.8 8.0 %collective-permute-done.10.piece = bf16[64,7168]{1,0:T(8,128)(2,1)S(1)} collective-permute-done((bf16[64,7168]{1,0:T(8,128)(2,1)}, bf16[64,7168]{1,0:T(8,128)(2,1)S(1)}, u32[]{:S(2)}, u32[]{:S(2)}) %collective-permute-start.10) | collective-permute-done | bytes 917536 | tf_op jit(solution)/shard_map/ppermute | solution.py:297
  88.8 1.5 %shard_map.84 = (f32[2,16,64]{2,1,0:T(8,128)S(1)}, f32[2,16,64]{2,1,0:T(8,128)S(1)}) custom-call(s32[10]{0:T(128)S(1)} %pad_add_fusion.facts, bf16[64,7168]{1,0:T(8,128)(2,1)S(1)} %collective-permute-done.10.piece, bf16[128,7168]{1,0:T(8,128)(2,1)S(1)} %pad_maximum_fusion.refs_5_.refs_1_.factors, bf16[64,64]{1,0:T(8,128)(2,1)S(1)} %add_convert_fusion.1.choices, ...), custom_call_target="tpu_custom_call" | custom-call | flops 3670016 | bytes 114688 | tf_op jit(solution)/shard_map/pallas_call | solution.py:173
  90.4 2.0 %collective-permute-start.11 = (f32[2,16,64]{2,1,0:T(8,128)S(1)}, f32[2,16,64]{2,1,0:T(8,128)S(1)}, u32[]{:S(2)}, u32[]{:S(2)}) collective-permute-start(f32[2,16,64]{2,1,0:T(8,128)S(1)} %get-tuple-element.90), channel_id=1, source_target_pairs={{0,1},{1,0},{2,3},{3,2},{4,5},{5,4},{6,7},{7,6},{8,9},{9,8},{10,11... | collective-permute-start | bytes 24584 | tf_op jit(solution)/shard_map/ppermute | solution.py:307
  92.4 0.2 fusion.10
  92.6 1.0 collective-permute-done.12
  93.6 0.6 collective-permute-done.11
  94.2 2.0 %collective-permute-start.18 = (bf16[3,64,512]{2,1,0:T(8,128)(2,1)S(1)}, bf16[3,64,512]{2,1,0:T(8,128)(2,1)S(1)}, u32[]{:S(2)}, u32[]{:S(2)}) collective-permute-start(bf16[3,64,512]{2,1,0:T(8,128)(2,1)S(1)} %get-tuple-element.100), channel_id=1, source_target_pairs={{0,1},{1,0},{2,3},{3,2},{4,5},{5,4},{6,7},{7,6},{8,9},{9,8},{10,11... | collective-permute-start | bytes 589832 | tf_op jit(solution)/shard_map/ppermute | solution.py:459
  96.2 1.5 %collective-permute-start.15 = (bf16[2,16,64]{2,1,0:T(8,128)(2,1)S(1)}, bf16[2,16,64]{2,1,0:T(8,128)(2,1)S(1)}, u32[]{:S(2)}, u32[]{:S(2)}) collective-permute-start(bf16[2,16,64]{2,1,0:T(8,128)(2,1)S(1)} %add_convert_fusion.3), channel_id=1, source_target_pairs={{0,4},{2,6},{4,0},{6,2},{8,12},{10,14},{12,8},{14,10},{16,20},{18,... | collective-permute-start | bytes 12296 | tf_op jit(solution)/shard_map/ppermute | solution.py:452
  97.7 1.6 %collective-permute-start.16 = (bf16[2,16,64]{2,1,0:T(8,128)(2,1)S(1)}, bf16[2,16,64]{2,1,0:T(8,128)(2,1)S(1)}, u32[]{:S(2)}, u32[]{:S(2)}) collective-permute-start(bf16[2,16,64]{2,1,0:T(8,128)(2,1)S(1)} %add_convert_fusion.3), channel_id=1, source_target_pairs={{0,8},{2,10},{4,12},{6,14},{8,0},{10,2},{12,4},{14,6},{16,24},{18,... | collective-permute-start | bytes 12296 | tf_op jit(solution)/shard_map/ppermute | solution.py:452
  99.3 0.4 collective-permute-start.17
  99.7 3.2 %shard_map.85 = (f32[1,64,512]{2,1,0:T(8,128)S(1)}, f32[1,64,512]{2,1,0:T(8,128)S(1)}, bf16[1,64,512]{2,1,0:T(8,128)(2,1)S(1)}, bf16[1,64,512]{2,1,0:T(8,128)(2,1)S(1)}) custom-call(s32[10]{0:T(128)S(1)} %pad_add_fusion.facts, bf16[64,7168]{1,0:T(8,128)(2,1)S(1)} %collective-permute-done.10.piece, ...), custom_call_target="tpu_custom_call" | custom-call | flops 29360128 | bytes 917504 | tf_op jit(solution)/shard_map/pallas_call | solution.py:173
  102.9 0.9 collective-permute-done.17
  103.9 2.3 %collective-permute-start.19 = (bf16[8,16,64]{2,1,0:T(8,128)(2,1)S(1)}, bf16[8,16,64]{2,1,0:T(8,128)(2,1)S(1)}, u32[]{:S(2)}, u32[]{:S(2)}) collective-permute-start(bf16[8,16,64]{2,1,0:T(8,128)(2,1)S(1)} %pad_maximum_fusion.4), channel_id=1, source_target_pairs={{0,16},{2,18},{4,20},{6,22},{8,24},{10,26},{12,28},{14,30},{16,0},... | collective-permute-start | bytes 49160 | tf_op jit(solution)/shard_map/ppermute | solution.py:452
  106.2 0.6 collective-permute-start.21
  106.7 1.3 %collective-permute-start.22 = (bf16[1,64,512]{2,1,0:T(8,128)(2,1)S(1)}, bf16[1,64,512]{2,1,0:T(8,128)(2,1)S(1)}, u32[]{:S(2)}, u32[]{:S(2)}) collective-permute-start(bf16[1,64,512]{2,1,0:T(8,128)(2,1)S(1)} %get-tuple-element.110), channel_id=1, source_target_pairs={{0,3},{1,2},{2,1},{3,0},{4,7},{5,6},{6,5},{7,4},{8,11},{9,10},{10,... | collective-permute-start | bytes 196616 | tf_op jit(solution)/shard_map/ppermute | solution.py:308
  108.0 1.0 collective-permute-done.19
  109.0 1.3 %shard_map.86.rest = f32[4,64,512]{2,1,0:T(8,128)S(1)} custom-call(s32[10]{0:T(128)S(1)} %pad_add_fusion.facts, bf16[256,64]{1,0:T(8,128)(2,1)S(1)} %bitcast.18, bf16[256,256]{1,0:T(8,128)(2,1)S(1)} %fusion.12.spots, bf16[256,1024]{1,0:T(8,128)(2,1)S(1)} %compare_convert_fusion.mask, bf16[64,1024]{1,0:T(8,128)(2,1)S(1)} %fusion.13.copies, ...), custom_call_target="tpu_custom_call" | custom-call | flops 8388608 | bytes 262144 | tf_op jit(solution)/shard_map/pallas_call | solution.py:173
  110.4 0.7 collective-permute-done.21.got_mp
  111.1 0.6 collective-permute-done.22.got_both
  111.7 1.3 %shard_map.87 = bf16[4,64,512]{2,1,0:T(8,128)(2,1)} custom-call(s32[10]{0:T(128)S(1)} %pad_add_fusion.facts, f32[4,64,512]{2,1,0:T(8,128)S(1)} %shard_map.86.rest, f32[1,64,512]{2,1,0:T(8,128)S(1)} %get-tuple-element.107.kept, f32[1,64,512]{2,1,0:T(8,128)S(1)} %collective-permute-done.20.got_sib, bf16[1,64,512]{2,1,0:T(8,128)(2,1)S(1)} %collective-permute-done.21.got_mp, ...), custom_call_target="tpu_custom_call" | custom-call | flops 4096 | bytes 128 | tf_op jit(solution)/shard_map/pallas_call | solution.py:173
  (59 shorter events, 1.4 us)
Async XLA Ops:
  1.4 5.4 %copy-start.4 = (bf16[16,32,512]{2,1,0:T(8,128)(2,1)S(1)}, bf16[16,32,512]{2,1,0:T(8,128)(2,1)}, u32[]{:S(2)}) copy-start(bf16[16,32,512]{2,1,0:T(8,128)(2,1)} %param.12) | copy-start | bytes 1572868
  1.4 2.0 %collective-permute-start = (bf16[32,7168]{1,0:T(8,128)(2,1)S(1)}, bf16[32,7168]{1,0:T(8,128)(2,1)S(1)}, u32[]{:S(2)}, u32[]{:S(2)}) collective-permute-start(bf16[32,7168]{1,0:T(8,128)(2,1)S(1)} %fusion.9), channel_id=1, source_target_pairs={{0,2},{2,0},{8,10},{10,8},{16,18},{18,16},{24,26},{26,24},{28,30},... | collective-permute-start | bytes 1376264 | tf_op jit(solution)/shard_map/ppermute | solution.py:291
  3.5 27.2 %copy-start = (bf16[64,7168]{1,0:T(8,128)(2,1)}, bf16[64,7168]{1,0:T(8,128)(2,1)S(1)}, u32[]{:S(2)}) copy-start(bf16[64,7168]{1,0:T(8,128)(2,1)S(1)} %pad_maximum_fusion.2.refs_0_) | copy-start | bytes 2752516
  3.5 50.2 %collective-permute-start.1 = (bf16[14336,512]{1,0:T(8,128)(2,1)}, bf16[14336,512]{1,0:T(8,128)(2,1)}, u32[]{:S(2)}, u32[]{:S(2)}) collective-permute-start(bf16[14336,512]{1,0:T(8,128)(2,1)} %refs_7_), channel_id=1, source_target_pairs={{0,2},{2,0},{8,10},{10,8},{16,18},{18,16},{24,26},{26,24},{28,30},... | collective-permute-start | bytes 44040200 | tf_op jit(solution)/shard_map/ppermute | solution.py:291
  3.9 22.9 %collective-permute-start.3 = (bf16[64,7168]{1,0:T(8,128)(2,1)S(1)}, bf16[64,7168]{1,0:T(8,128)(2,1)S(1)}, u32[]{:S(2)}, u32[]{:S(2)}) collective-permute-start(bf16[64,7168]{1,0:T(8,128)(2,1)S(1)} %pad_maximum_fusion.2.refs_0_), channel_id=1, source_target_pairs={{0,8},{8,16},{16,24},{24,28},{28,20},{20,12},{12,4},{4,0},{2,6},{1... | collective-permute-start | bytes 2752520 | tf_op jit(solution)/shard_map/ppermute | solution.py:297
  6.6 22.6 %collective-permute-start.5 = (bf16[64,7168]{1,0:T(8,128)(2,1)S(1)}, bf16[64,7168]{1,0:T(8,128)(2,1)}, u32[]{:S(2)}, u32[]{:S(2)}) collective-permute-start(bf16[64,7168]{1,0:T(8,128)(2,1)S(1)} %pad_maximum_fusion.2.refs_0_), channel_id=1, source_target_pairs={{0,4},{8,0},{16,8},{24,16},{28,24},{20,28},{12,20},{4,12},{2,10},{... | collective-permute-start | bytes 2752520 | tf_op jit(solution)/shard_map/ppermute | solution.py:297
  6.6 45.7 %collective-permute-start.9 = (bf16[64,14336]{1,0:T(8,128)(2,1)}, bf16[64,14336]{1,0:T(8,128)(2,1)}, u32[]{:S(2)}, u32[]{:S(2)}) collective-permute-start(bf16[64,14336]{1,0:T(8,128)(2,1)} %bitcast.21), channel_id=1, source_target_pairs={{0,2},{2,0},{8,10},{10,8},{16,18},{18,16},{24,26},{26,24},{28,30},... | collective-permute-start | bytes 5505032 | tf_op jit(solution)/shard_map/ppermute | solution.py:291
  6.8 23.8 %collective-permute-start.2 = (bf16[16,32,512]{2,1,0:T(8,128)(2,1)S(1)}, bf16[16,32,512]{2,1,0:T(8,128)(2,1)S(1)}, u32[]{:S(2)}, u32[]{:S(2)}) collective-permute-start(bf16[16,32,512]{2,1,0:T(8,128)(2,1)S(1)} %copy-done.4), channel_id=1, source_target_pairs={{0,1},{1,0},{2,3},{3,2},{4,5},{5,4},{6,7},{7,6},{8,9},{9,8},{10,11... | collective-permute-start | bytes 1572872 | tf_op jit(solution)/shard_map/ppermute | solution.py:320
  26.8 3.9 %copy-start.2 = (bf16[64,7168]{1,0:T(8,128)(2,1)}, bf16[64,7168]{1,0:T(8,128)(2,1)S(1)}, u32[]{:S(2)}) copy-start(bf16[64,7168]{1,0:T(8,128)(2,1)S(1)} %collective-permute-done.3.refs_1_) | copy-start | bytes 2752516
  26.8 23.1 %collective-permute-start.4 = (bf16[64,7168]{1,0:T(8,128)(2,1)S(1)}, bf16[64,7168]{1,0:T(8,128)(2,1)}, u32[]{:S(2)}, u32[]{:S(2)}) collective-permute-start(bf16[64,7168]{1,0:T(8,128)(2,1)S(1)} %collective-permute-done.3.refs_1_), channel_id=1, source_target_pairs={{0,8},{8,16},{16,24},{24,28},{28,20},{20,12},{12,4},{4,0},{2,6},{1... | collective-permute-start | bytes 2752520 | tf_op jit(solution)/shard_map/ppermute | solution.py:297
  29.3 20.6 %collective-permute-start.6 = (bf16[64,7168]{1,0:T(8,128)(2,1)}, bf16[64,7168]{1,0:T(8,128)(2,1)}, u32[]{:S(2)}, u32[]{:S(2)}) collective-permute-start(bf16[64,7168]{1,0:T(8,128)(2,1)} %collective-permute-done.5.refs_2_), channel_id=1, source_target_pairs={{0,4},{8,0},{16,8},{24,16},{28,24},{20,28},{12,20},{4,12},{2,10},{... | collective-permute-start | bytes 2752520 | tf_op jit(solution)/shard_map/ppermute | solution.py:297
  49.8 25.1 %collective-permute-start.7 = (bf16[64,7168]{1,0:T(8,128)(2,1)}, bf16[64,7168]{1,0:T(8,128)(2,1)}, u32[]{:S(2)}, u32[]{:S(2)}) collective-permute-start(bf16[64,7168]{1,0:T(8,128)(2,1)} %collective-permute-done.4.refs_3_), channel_id=1, source_target_pairs={{0,8},{8,16},{16,24},{24,28},{28,20},{20,12},{12,4},{4,0},{2,6},{1... | collective-permute-start | bytes 2752520 | tf_op jit(solution)/shard_map/ppermute | solution.py:297
  51.5 23.4 %collective-permute-start.8 = (bf16[64,7168]{1,0:T(8,128)(2,1)}, bf16[64,7168]{1,0:T(8,128)(2,1)}, u32[]{:S(2)}, u32[]{:S(2)}) collective-permute-start(bf16[64,7168]{1,0:T(8,128)(2,1)} %collective-permute-done.6.refs_4_), channel_id=1, source_target_pairs={{0,4},{8,0},{16,8},{24,16},{28,24},{20,28},{12,20},{4,12},{2,10},{... | collective-permute-start | bytes 2752520 | tf_op jit(solution)/shard_map/ppermute | solution.py:297
  53.5 0.7 copy-start.5
  53.6 0.7 copy-start.6
  56.9 1.2 %copy-start.1 = (bf16[64,7168]{1,0:T(8,128)(2,1)S(1)}, bf16[64,7168]{1,0:T(8,128)(2,1)}, u32[]{:S(2)}) copy-start(bf16[64,7168]{1,0:T(8,128)(2,1)} %copy-done) | copy-start | bytes 2752516
  58.1 1.2 %copy-start.3 = (bf16[64,7168]{1,0:T(8,128)(2,1)S(1)}, bf16[64,7168]{1,0:T(8,128)(2,1)}, u32[]{:S(2)}) copy-start(bf16[64,7168]{1,0:T(8,128)(2,1)} %copy-done.2) | copy-start | bytes 2752516
  74.9 13.8 %collective-permute-start.10 = (bf16[64,7168]{1,0:T(8,128)(2,1)}, bf16[64,7168]{1,0:T(8,128)(2,1)S(1)}, u32[]{:S(2)}, u32[]{:S(2)}) collective-permute-start(bf16[64,7168]{1,0:T(8,128)(2,1)} %collective-permute-done.7.piece), channel_id=1, source_target_pairs={{0,8},{8,16},{16,24},{24,28},{28,20},{20,12},{12,4},{4,0},{2,6},{1... | collective-permute-start | bytes 2752520 | tf_op jit(solution)/shard_map/ppermute | solution.py:297
  80.8 11.7 %collective-permute-start.14 = (f32[2,3,64,512]{3,2,1,0:T(8,128)S(1)}, f32[2,3,64,512]{3,2,1,0:T(8,128)S(1)}, u32[]{:S(2)}, u32[]{:S(2)}) collective-permute-start(f32[2,3,64,512]{3,2,1,0:T(8,128)S(1)} %get-tuple-element.92), channel_id=1, source_target_pairs={{0,2},{2,0},{8,10},{10,8},{16,18},{18,16},{24,26},{26,24},{28,30},... | collective-permute-start | bytes 2359304 | tf_op jit(solution)/shard_map/ppermute | solution.py:291
  90.3 3.3 %collective-permute-start.13 = (f32[2,16,64]{2,1,0:T(8,128)S(1)}, f32[2,16,64]{2,1,0:T(8,128)S(1)}, u32[]{:S(2)}, u32[]{:S(2)}) collective-permute-start(f32[2,16,64]{2,1,0:T(8,128)S(1)} %get-tuple-element.90), channel_id=1, source_target_pairs={{0,3},{1,2},{2,1},{3,0},{4,7},{5,6},{6,5},{7,4},{8,11},{9,10},{10,... | collective-permute-start | bytes 24584 | tf_op jit(solution)/shard_map/ppermute | solution.py:308
  90.4 3.9 %collective-permute-start.11 = (f32[2,16,64]{2,1,0:T(8,128)S(1)}, f32[2,16,64]{2,1,0:T(8,128)S(1)}, u32[]{:S(2)}, u32[]{:S(2)}) collective-permute-start(f32[2,16,64]{2,1,0:T(8,128)S(1)} %get-tuple-element.90), channel_id=1, source_target_pairs={{0,1},{1,0},{2,3},{3,2},{4,5},{5,4},{6,7},{7,6},{8,9},{9,8},{10,11... | collective-permute-start | bytes 24584 | tf_op jit(solution)/shard_map/ppermute | solution.py:307
  92.4 1.2 %collective-permute-start.12 = (f32[2,16,64]{2,1,0:T(8,128)S(1)}, f32[2,16,64]{2,1,0:T(8,128)S(1)}, u32[]{:S(2)}, u32[]{:S(2)}) collective-permute-start(f32[2,16,64]{2,1,0:T(8,128)S(1)} %get-tuple-element.89), channel_id=1, source_target_pairs={{0,2},{2,0},{8,10},{10,8},{16,18},{18,16},{24,26},{26,24},{28,30},... | collective-permute-start | bytes 24584 | tf_op jit(solution)/shard_map/ppermute | solution.py:291
  94.2 9.6 %collective-permute-start.18 = (bf16[3,64,512]{2,1,0:T(8,128)(2,1)S(1)}, bf16[3,64,512]{2,1,0:T(8,128)(2,1)S(1)}, u32[]{:S(2)}, u32[]{:S(2)}) collective-permute-start(bf16[3,64,512]{2,1,0:T(8,128)(2,1)S(1)} %get-tuple-element.100), channel_id=1, source_target_pairs={{0,1},{1,0},{2,3},{3,2},{4,5},{5,4},{6,7},{7,6},{8,9},{9,8},{10,11... | collective-permute-start | bytes 589832 | tf_op jit(solution)/shard_map/ppermute | solution.py:459
  96.2 6.7 %collective-permute-start.15 = (bf16[2,16,64]{2,1,0:T(8,128)(2,1)S(1)}, bf16[2,16,64]{2,1,0:T(8,128)(2,1)S(1)}, u32[]{:S(2)}, u32[]{:S(2)}) collective-permute-start(bf16[2,16,64]{2,1,0:T(8,128)(2,1)S(1)} %add_convert_fusion.3), channel_id=1, source_target_pairs={{0,4},{2,6},{4,0},{6,2},{8,12},{10,14},{12,8},{14,10},{16,20},{18,... | collective-permute-start | bytes 12296 | tf_op jit(solution)/shard_map/ppermute | solution.py:452
  97.7 5.2 %collective-permute-start.16 = (bf16[2,16,64]{2,1,0:T(8,128)(2,1)S(1)}, bf16[2,16,64]{2,1,0:T(8,128)(2,1)S(1)}, u32[]{:S(2)}, u32[]{:S(2)}) collective-permute-start(bf16[2,16,64]{2,1,0:T(8,128)(2,1)S(1)} %add_convert_fusion.3), channel_id=1, source_target_pairs={{0,8},{2,10},{4,12},{6,14},{8,0},{10,2},{12,4},{14,6},{16,24},{18,... | collective-permute-start | bytes 12296 | tf_op jit(solution)/shard_map/ppermute | solution.py:452
  99.3 4.5 %collective-permute-start.17 = (bf16[2,16,64]{2,1,0:T(8,128)(2,1)S(1)}, bf16[2,16,64]{2,1,0:T(8,128)(2,1)S(1)}, u32[]{:S(2)}, u32[]{:S(2)}) collective-permute-start(bf16[2,16,64]{2,1,0:T(8,128)(2,1)S(1)} %add_convert_fusion.3), channel_id=1, source_target_pairs={{0,12},{2,14},{4,8},{6,10},{8,4},{10,6},{12,0},{14,2},{16,28},{18,... | collective-permute-start | bytes 12296 | tf_op jit(solution)/shard_map/ppermute | solution.py:452
  103.9 5.1 %collective-permute-start.19 = (bf16[8,16,64]{2,1,0:T(8,128)(2,1)S(1)}, bf16[8,16,64]{2,1,0:T(8,128)(2,1)S(1)}, u32[]{:S(2)}, u32[]{:S(2)}) collective-permute-start(bf16[8,16,64]{2,1,0:T(8,128)(2,1)S(1)} %pad_maximum_fusion.4), channel_id=1, source_target_pairs={{0,16},{2,18},{4,20},{6,22},{8,24},{10,26},{12,28},{14,30},{16,0},... | collective-permute-start | bytes 49160 | tf_op jit(solution)/shard_map/ppermute | solution.py:452
  106.2 5.5 %collective-permute-start.20 = (f32[1,64,512]{2,1,0:T(8,128)S(1)}, f32[1,64,512]{2,1,0:T(8,128)S(1)}, u32[]{:S(2)}, u32[]{:S(2)}) collective-permute-start(f32[1,64,512]{2,1,0:T(8,128)S(1)} %get-tuple-element.108), channel_id=1, source_target_pairs={{0,2},{2,0},{8,10},{10,8},{16,18},{18,16},{24,26},{26,24},{28,30},... | collective-permute-start | bytes 393224 | tf_op jit(solution)/shard_map/ppermute | solution.py:291
  106.2 4.9 %collective-permute-start.21 = (bf16[1,64,512]{2,1,0:T(8,128)(2,1)S(1)}, bf16[1,64,512]{2,1,0:T(8,128)(2,1)S(1)}, u32[]{:S(2)}, u32[]{:S(2)}) collective-permute-start(bf16[1,64,512]{2,1,0:T(8,128)(2,1)S(1)} %get-tuple-element.109), channel_id=1, source_target_pairs={{0,1},{1,0},{2,3},{3,2},{4,5},{5,4},{6,7},{7,6},{8,9},{9,8},{10,11... | collective-permute-start | bytes 196616 | tf_op jit(solution)/shard_map/ppermute | solution.py:307
  106.7 5.0 %collective-permute-start.22 = (bf16[1,64,512]{2,1,0:T(8,128)(2,1)S(1)}, bf16[1,64,512]{2,1,0:T(8,128)(2,1)S(1)}, u32[]{:S(2)}, u32[]{:S(2)}) collective-permute-start(bf16[1,64,512]{2,1,0:T(8,128)(2,1)S(1)} %get-tuple-element.110), channel_id=1, source_target_pairs={{0,3},{1,2},{2,1},{3,0},{4,7},{5,6},{6,5},{7,4},{8,11},{9,10},{10,... | collective-permute-start | bytes 196616 | tf_op jit(solution)/shard_map/ppermute | solution.py:308

commit v15 on v14

--- a/solution.py
+++ b/solution.py
@@ -51,13 +51,25 @@
 def factor_products(rows_of, table, low):
     depth = table.shape[1]
     tile = tile_of(depth)
-    total = jnp.zeros(low.shape, jnp.float32)
-    for index in range(depth // tile):
-        here = slice(index * tile, (index + 1) * tile)
-        total += lax.dot_general(
+
+    def product(here):
+        return lax.dot_general(
             rows_of(here), table[:, here], (((1,), (1,)), ((), ())), preferred_element_type=jnp.float32
         )
-    low[...] = total
+
+    if low.shape[0] <= 128:
+        total = jnp.zeros(low.shape, jnp.float32)
+        for index in range(depth // tile):
+            total += product(slice(index * tile, (index + 1) * tile))
+        low[...] = total
+        return
+    low[...] = jnp.zeros_like(low)
+
+    def step(index, carry):
+        low[...] += product(pl.ds(pl.multiple_of(index * tile, 128), tile))
+        return carry
+
+    lax.fori_loop(0, depth // tile, step, 0)
 
 
 def in_lanes(lane, total, index, height):
@@ -110,12 +122,9 @@
     to_both[pair] = jnp.where(flag == 1, away_sib, near_sib).astype(to_both.dtype)
 
 
-def middle_kernel(facts, piece, other, *refs):
-    (held, factors, choices, compact_in, base, base_sib), refs = refs[:6], refs[6:]
-    (own, sib, compact), sums, low = refs[:3], refs[3:5], refs[5]
+def middle_kernel(facts, piece, other, held, base, base_sib, own, sib, *sums):
     outs = own.at[0], sib.at[0], own.at[1], sib.at[1]
     rows_of = lambda here: jnp.concatenate([piece[:, here], other[:, here]], axis=0)
-    factor_products(rows_of, factors, low)
     weight_products(rows_of, held, sums)
     pairs, group = own.shape[1:3]
     fresh = [[in_lanes(facts[0], total, index, group // 2) for total in sums] for index in (0, 1)]
@@ -128,14 +137,15 @@
         near = ahead if step == pairs else (base[near], base_sib[near])
         away = behind if back == pairs else (base[away], base_sib[away])
         share(facts[2 + step], near, away, outs, pair)
-    for which, fresh_low in enumerate(compacted(choices[...], low[...])):
-        compact[which] = compact_in[which] + fresh_low
-
-
-def low_kernel(facts, piece, factors, choices, compact_in, kept, sent, low):
+
+
+def low_kernel(facts, piece, other, far_rows, factors, choices, compact_in, kept, sent, low, low_far):
     half = kept.shape[1]
-    factor_products(lambda here: piece[:, here], factors, low)
-    for which, fresh_low in enumerate(compacted(choices[...], low[...])):
+    rows_of = lambda here: jnp.concatenate([piece[:, here], other[:, here]], axis=0)
+    factor_products(rows_of, factors, low)
+    factor_products(lambda here: far_rows[:, here], factors, low_far)
+    both = jnp.concatenate([low[...], low_far[...]], axis=0)
+    for which, fresh_low in enumerate(compacted(choices[...], both)):
         total = compact_in[which] + fresh_low
         kept[which] = jnp.where(facts[1] == 0, total[:half], total[half:])
         sent[which] = jnp.where(facts[1] == 0, total[half:], total[:half])
@@ -322,8 +332,8 @@
     factors = jnp.concatenate(
         [half_of(first, side, 1), half_of(send(first, 0, 1), side, 1)], axis=0
     )
-    home_late, row_adapter_index, weights = lax.optimization_barrier(
-        (home, row_adapter_index, weights)
+    home_late, part_late, row_adapter_index, other_second = lax.optimization_barrier(
+        (home, part, row_adapter_index, other_second)
     )
 
     pieces = [block, one_way, other_way]
@@ -339,8 +349,8 @@
     edges = np.cumsum([0, 2 * nodes, far, far, far, far])
     arrived, *rest = [row[a:b] for a, b in zip(edges[:-1], edges[1:])]
     facts = jnp.concatenate(
-        [side[None], part[None].astype(jnp.int32)]
-        + [jnp.where(part == 0, a, b) for a, b in zip(rest[:2], rest[2:])]
+        [side[None], part_late[None].astype(jnp.int32)]
+        + [jnp.where(part_late == 0, a, b) for a, b in zip(rest[:2], rest[2:])]
     )
     slot_all = slots_of(row_adapter_index, adapter_storage_slot).reshape(owners, row_count)
     ranks = jnp.arange(row_count, dtype=jnp.int32)
@@ -362,17 +372,35 @@
         axis=0,
     )
     early_rows = len(pieces) * group_rows
-    middle_rows = early_rows + 2 * group_rows
+    sides, places = jnp.arange(2, dtype=jnp.int32), jnp.arange(MOST, dtype=jnp.int32)
+    far_wide = arrived[-2:]
+    far_choice = (
+        (sides[:, None, None, None, None, None] == sides[:, None, None])
+        & (blocks[:, None, None, None, None] == far_wide[:, None])
+        & (places[:, None, None, None] == places)
+    )
+    far_choice = far_choice.reshape(2 * owners * MOST, 4 * MOST).astype(bf16)
     choices = [
         chosen[:, :early_rows],
-        chosen[:, early_rows:middle_rows],
-        chosen[:, middle_rows:],
+        jnp.concatenate([chosen[:, early_rows : early_rows + 2 * group_rows], far_choice], axis=1),
     ]
+
+    own_is = jnp.bitwise_xor(home_late, sides)[:, None, None] == blocks[None, :, None]
+    own_slot = jnp.sum(jnp.where(own_is, slot_all[None], 0), axis=1)
+    own_position = jnp.sum(jnp.where(own_is, position[None], 0), axis=1)
+    pick = (
+        (sides[:, None, None, None] == sides[:, None])
+        & (own_slot[:, None, None, :] == far_wide[:, None, None, None, None])
+        & (own_position[:, None, None, :] == places[:, None, None])
+    )
+    pick = pick.reshape(4 * MOST, group_rows).astype(bf16)
+    picked = jnp.dot(pick, block, preferred_element_type=f32).astype(bf16)
+    far_rows = send(picked, far)
 
     half = own_blocks * MOST
     here = own_blocks * row_count
-    slot_here = lax.dynamic_slice_in_dim(slot_all, part * own_blocks, own_blocks).reshape(here, 1)
-    position_here = lax.dynamic_slice_in_dim(position, part * own_blocks, own_blocks)
+    slot_here = lax.dynamic_slice_in_dim(slot_all, part_late * own_blocks, own_blocks).reshape(here, 1)
+    position_here = lax.dynamic_slice_in_dim(position, part_late * own_blocks, own_blocks)
     block_here = jnp.arange(here, dtype=jnp.int32)[:, None] // row_count
     spot = (
         jnp.bitwise_xor(slot_here, home_late) * half
@@ -382,10 +410,11 @@
     spots = (spot == jnp.arange(owners * half, dtype=jnp.int32)[None, :]).astype(bf16)
     piece = rank // 2
     column = jnp.arange(owners * rank, dtype=jnp.int32)[None, :]
-    own_rank = jnp.bitwise_xor(part, column // (owners * piece)) * piece + column % piece
+    own_rank = jnp.bitwise_xor(part_late, column // (owners * piece)) * piece + column % piece
     mask = (slot_here == column // piece % owners).astype(bf16)
     copies = (jnp.arange(rank, dtype=jnp.int32)[:, None] == own_rank).astype(bf16)
 
+    other_second, far_rows = lax.optimization_barrier((other_second, far_rows))
     second = jnp.concatenate(
         [values.reshape(owners * piece, width) for values in (second_factor_table, other_second)],
         axis=0,
@@ -424,41 +453,28 @@
         shape = (pairs, group_rows, width)
         return [(shape, f32)] * 2 + [(shape, bf16)] * 2
 
-    own_more, sib_more, compact = kernel_call(
-        middle_kernel,
-        facts,
-        (one_way, other_way, held, factors, choices[1], early[4], early[2], early[3]),
-        [((2, far - 1, group_rows, width), f32)] * 2 + [compact_shape],
-        sums(2 * group_rows),
-        flops(2 * group_rows, 2 * (width + rank)),
-    )
-
-    kept_more, out_more = [a + b for a, b in zip(own_more, send(sib_more, 0, 1))]
-    out_more = out_more.astype(bf16)
-    last, compact = lax.optimization_barrier((last, compact))
-
     kept, sent = kernel_call(
         low_kernel,
         facts,
-        (last, factors, choices[2], compact),
+        (one_way, other_way, far_rows, factors, choices[1], early[4]),
         [((2, half, rank), f32)] * 2,
-        [pltpu.VMEM((group_rows, 2 * rank), f32)],
-        flops(group_rows, 2 * rank),
-    )
+        [pltpu.VMEM((rows, 2 * rank), f32) for rows in (2 * group_rows, 4 * MOST)],
+        flops(2 * group_rows, 2 * rank),
+    )
+    kept, sent, one_way, other_way = lax.optimization_barrier((kept, sent, one_way, other_way))
+
     got = to_three(kept, sent, sent)
-    low = (kept + got[1] + (got[0] + got[2])[::-1]).astype(bf16)
-
-    def from_node(value, gap):
-        return lax.ppermute(value, "wide", [(w, w ^ (2 * gap)) for w in range(owners)])
-
-    def gather(value, gap, reach):
-        parts = [from_node(value, gap * k) for k in range(1, reach)]
-        return jnp.concatenate([value] + parts, axis=0)
-
-    low, out_more, last = lax.optimization_barrier((low, out_more, last))
-    got_more = lax.ppermute(out_more, INNER, SWAP)
-    reach = min(4, nodes)
-    low = gather(low, 1, reach)
+
+    own_more, sib_more = kernel_call(
+        middle_kernel,
+        facts,
+        (one_way, other_way, held, early[2], early[3]),
+        [((2, far - 1, group_rows, width), f32)] * 2,
+        sums(2 * group_rows, False),
+        flops(2 * group_rows, 2 * width),
+    )
+    kept_more, out_more = [a + b for a, b in zip(own_more, send(sib_more, 0, 1))]
+    out_more = out_more.astype(bf16)
 
     kept_one, *one = kernel_call(
         last_kernel,
@@ -466,13 +482,24 @@
         (last, held, early[0], early[1]),
         shares(1),
         sums(group_rows, False),
-        flops(group_rows, 2 * width),
-    )
-    low, one, got_more = lax.optimization_barrier((low, one, got_more))
-    gap = reach
+        1024 * flops(group_rows, 2 * width),
+    )
+
+    def from_node(value, gap):
+        return lax.ppermute(value, "wide", [(w, w ^ (2 * gap)) for w in range(owners)])
+
+    def gather(value, gap, reach):
+        parts = [from_node(value, gap * k) for k in range(1, reach)]
+        return jnp.concatenate([value] + parts, axis=0)
+
+    got, one = lax.optimization_barrier((got, one))
+    low = (kept + got[1] + (got[0] + got[2])[::-1]).astype(bf16)
+    gap = 1
     while gap < nodes:
-        low = gather(low, gap, 2)
-        gap *= 2
+        reach = min(4, nodes // gap)
+        low = gather(low, gap, reach)
+        gap *= reach
+    got_more = lax.ppermute(out_more, INNER, SWAP)
     got_one = to_three(*one)
 
     shape = (own_nodes, group_rows, width)

time: 113 us -> 109 us (0.965)
  waiting for transfers between devices: 50.1 us -> 43.1 us
  Pallas kernels: 27.3 us -> 20.8 us
  other arithmetic: 4.78 us -> 9.12 us
  starting transfers between devices: 23.9 us -> 26.7 us
    ppermute x7, waiting for transfers between devices: 45.3 us -> 28.9 us  [turn(): return lax.ppermute(value, 'wide', pairs)]
    ppermute x1, waiting for transfers between devices: 0.01 us -> 10.5 us  [ringed(): other_second = lax.ppermute(second_factor_table, INNER, SWAP)]
    pallas_call x6, Pallas kernels: 27.3 us -> 20.8 us  [kernel_call(): pl.pallas_call(kernel, in_specs=[pl.BlockSpec(memory_space=pltpu.SMEM)] +...]
    ppermute x6 -> x7, starting transfers between devices: 1.09 us -> 6.69 us  [send(): return lax.ppermute(value, 'wide', moved(shift, cross))]
    unnamed x14 -> x11, local copies, waits for them, and re-layouts: 2.9 us -> 0.05 us
    ppermute x4, waiting for transfers between devices: 1.9 us -> 3.62 us  [from_node(): lax.ppermute(value, 'wide', [(w, w ^ 2 * gap) for w in range(owners)])]
    convert_element_type x0 -> x2, local copies, waits for them, and re-layouts: none -> 1.66 us  [ringed(): far_choice = far_choice.reshape(2 * owners * MOST, 4 * MOST).astype(bf16)]
    ppermute x2, waiting for transfers between devices: 1.33 us -> 0.01 us  [to_three(): lax.ppermute(to_mp, INNER, SWAP)]
  transfers between devices with their start and end apart: 23 -> 24, of which waited for: 9 -> 5; matrix products, arithmetic and copies ran while one was open for 6% -> 15% of each run, Pallas kernels for 23% -> 18%
where the time goes in v15:
time: 109 us; the launch traced here: 108 us
  waiting for transfers between devices  43.1 us (40%)
  starting transfers between devices  26.7 us (24%)
  Pallas kernels  20.8 us (19%)
  other arithmetic  9.12 us (8%)
  local copies, waits for them, and re-layouts  7.39 us (7%)
    ppermute x7, waiting for transfers between devices, turn(): return lax.ppermute(value, 'wide', pairs)  28.9 us
    pallas_call x6, Pallas kernels, kernel_call(): pl.pallas_call(kernel, in_specs=[pl.BlockSpec(memory_space=pltpu.SMEM)] +...  20.8 us
    ppermute x1, waiting for transfers between devices, ringed(): other_second = lax.ppermute(second_factor_table, INNER, SWAP)  10.5 us
    ppermute x7, starting transfers between devices, turn(): return lax.ppermute(value, 'wide', pairs)  8.19 us
    ppermute x7, starting transfers between devices, send(): return lax.ppermute(value, 'wide', moved(shift, cross))  6.69 us
    ppermute x4, starting transfers between devices, from_node(): lax.ppermute(value, 'wide', [(w, w ^ 2 * gap) for w in range(owners)])  5.15 us
    ppermute x4, waiting for transfers between devices, from_node(): lax.ppermute(value, 'wide', [(w, w ^ 2 * gap) for w in range(owners)])  3.62 us
    dynamic_slice x2, local copies, waits for them, and re-layouts, half_of(): return lax.dynamic_slice_in_dim(value, which * depth, depth, axis)  3.42 us
  transfers between devices with their start and end apart: 24, of which 5 were waited for; matrix products, arithmetic and copies ran while one was open for 15% of the time, Pallas kernels for 18%

profile of v15, /device:TPU:0, one launch (start us, length us, event | category | flops | bytes accessed | tf_op | source)
XLA Modules:
  0.0 108.3 jit_solution(6382631315525343640)
XLA Ops:
  0.0 1.4 %fusion.9 = bf16[32,7168]{1,0:T(8,128)(2,1)S(1)} fusion(bf16[32,14336]{1,0:T(8,128)(2,1)} %param.9, s32[]{:T(128)S(6)} %select_n.105, bf16[32,14336]{1,0:T(8,128)(2,1)} %param.8), kind=kLoop, calls=%fused_computation.18 | loop fusion | flops 1835008 | bytes 1376260 | tf_op jit(solution)/shard_map/convert_element_type | solution.py:199
  1.4 0.5 collective-permute-start
  2.0 1.4 %fusion.8 = bf16[32,7168]{1,0:T(8,128)(2,1)S(1)} fusion(bf16[32,14336]{1,0:T(8,128)(2,1)} %param.9, s32[]{:T(128)S(6)} %select_n.106, bf16[32,14336]{1,0:T(8,128)(2,1)} %param.8), kind=kLoop, calls=%fused_computation.17 | loop fusion | flops 1835008 | bytes 1376260 | tf_op jit(solution)/shard_map/convert_element_type | solution.py:199
  3.5 0.4 collective-permute-start.10
  4.0 2.8 %collective-permute-start.3 = (bf16[64,7168]{1,0:T(8,128)(2,1)S(1)}, bf16[64,7168]{1,0:T(8,128)(2,1)S(1)}, u32[]{:S(2)}, u32[]{:S(2)}) collective-permute-start(bf16[64,7168]{1,0:T(8,128)(2,1)S(1)} %pad_maximum_fusion.2.refs_0_), channel_id=1, source_target_pairs={{0,8},{8,16},{16,24},{24,28},{28,20},{20,12},{12,4},{4,0},{2,6},{1... | collective-permute-start | bytes 2752520 | tf_op jit(solution)/shard_map/ppermute | solution.py:307
  6.8 0.1 collective-permute-start.9
  7.0 1.8 %collective-permute-start.1 = (bf16[16,32,512]{2,1,0:T(8,128)(2,1)S(1)}, bf16[16,32,512]{2,1,0:T(8,128)(2,1)}, u32[]{:S(2)}, u32[]{:S(2)}) collective-permute-start(bf16[16,32,512]{2,1,0:T(8,128)(2,1)S(1)} %copy-done.1), channel_id=1, source_target_pairs={{0,1},{1,0},{2,3},{3,2},{4,5},{5,4},{6,7},{7,6},{8,9},{9,8},{10,11... | collective-permute-start | bytes 1572872 | tf_op jit(solution)/shard_map/ppermute | solution.py:330
  8.8 2.2 %constant_dynamic-slice_fusion = bf16[64,7168]{1,0:T(8,128)(2,1)} fusion(bf16[64,14336]{1,0:T(8,128)(2,1)} %bitcast.29, s32[]{:T(128)S(6)} %select_n.124), kind=kLoop, calls=%fused_computation.80 | loop fusion | bytes 1835012 | tf_op jit(solution)/shard_map/dynamic_slice | solution.py:310
  10.9 10.5 %collective-permute-done.1 = bf16[16,32,512]{2,1,0:T(8,128)(2,1)} collective-permute-done((bf16[16,32,512]{2,1,0:T(8,128)(2,1)S(1)}, bf16[16,32,512]{2,1,0:T(8,128)(2,1)}, u32[]{:S(2)}, u32[]{:S(2)}) %collective-permute-start.1) | collective-permute-done | bytes 524320 | tf_op jit(solution)/shard_map/ppermute | solution.py:330
  21.6 0.7 constant_dynamic-slice_fusion.4
  22.3 0.5 convert_reduce_fusion
  23.3 0.9 convolution_convert_fusion
  24.2 4.8 %collective-permute-start.2 = (bf16[8,7168]{1,0:T(8,128)(2,1)}, bf16[8,7168]{1,0:T(8,128)(2,1)}, u32[]{:S(2)}, u32[]{:S(2)}) collective-permute-start(bf16[8,7168]{1,0:T(8,128)(2,1)} %convolution_convert_fusion), channel_id=1, source_target_pairs={{0,28},{2,30},{8,20},{10,22},{16,12},{18,14},{24,4},{26,6},{28,0},... | collective-permute-start | bytes 344072 | tf_op jit(solution)/shard_map/ppermute | solution.py:301
  29.1 0.1 select_reduce_fusion
  29.6 0.7 add_convert_fusion.1
  30.3 0.6 add_convert_fusion
  31.3 0.7 and_convert_fusion
  32.2 2.0 %collective-permute-start.6 = (bf16[64,7168]{1,0:T(8,128)(2,1)S(1)}, bf16[64,7168]{1,0:T(8,128)(2,1)}, u32[]{:S(2)}, u32[]{:S(2)}) collective-permute-start(bf16[64,7168]{1,0:T(8,128)(2,1)S(1)} %collective-permute-done.5.refs_2_), channel_id=1, source_target_pairs={{0,4},{8,0},{16,8},{24,16},{28,24},{20,28},{12,20},{4,12},{2,10},{... | collective-permute-start | bytes 2752520 | tf_op jit(solution)/shard_map/ppermute | solution.py:307
  34.2 0.2 compare_convert_fusion.mask
  34.5 1.0 reshape.433
  35.4 0.7 copy.11
  36.1 0.8 slice.39.refs_6_
  36.9 0.7 pad_maximum_fusion.3.choices
  37.7 1.3 %pad_maximum_fusion.1.second = bf16[1024,512]{1,0:T(8,128)(2,1)S(1)} fusion(bf16[512,512]{1,0:T(8,128)(2,1)} %bitcast.9, bf16[512,512]{1,0:T(8,128)(2,1)} %bitcast.27), kind=kLoop, calls=%fused_computation.6 | loop fusion | flops 2097152 | bytes 2097152 | tf_op jit(solution)/shard_map/concatenate | solution.py:418
  39.0 15.2 %collective-permute-done.4.refs_3_ = bf16[64,7168]{1,0:T(8,128)(2,1)} collective-permute-done((bf16[64,7168]{1,0:T(8,128)(2,1)S(1)}, bf16[64,7168]{1,0:T(8,128)(2,1)}, u32[]{:S(2)}, u32[]{:S(2)}) %collective-permute-start.4) | collective-permute-done | bytes 917536 | tf_op jit(solution)/shard_map/ppermute | solution.py:307
  54.2 1.1 collective-permute-start.7
  55.3 0.9 collective-permute-start.8
  56.2 1.2 %constant_dynamic-slice_fusion.1 = bf16[64,7168]{1,0:T(8,128)(2,1)S(1)} fusion(bf16[64,14336]{1,0:T(8,128)(2,1)} %collective-permute-done.9, s32[]{:T(128)S(6)} %select_n.124), kind=kLoop, calls=%fused_computation.81 | loop fusion | bytes 1835012 | tf_op jit(solution)/shard_map/dynamic_slice | solution.py:310
  57.6 10.1 %shard_map.82 = (f32[1,64,512]{2,1,0:T(8,128)S(1)}, f32[1,64,512]{2,1,0:T(8,128)S(1)}, f32[4,64,512]{2,1,0:T(8,128)S(1)}, f32[4,64,512]{2,1,0:T(8,128)S(1)}, f32...) custom-call(s32[10]{0:T(128)S(1)} %pad_add_fusion.facts, bf16[64,7168]{1,0:T(8,128)(2,1)S(1)} %pad_maximum_fusion.2.refs_0_, ...), custom_call_target="tpu_custom_call" | custom-call | flops 165150720 | bytes 5160960 | tf_op jit(solution)/shard_map/pallas_call | solution.py:183
  67.7 8.9 %collective-permute-done.7.piece = bf16[64,7168]{1,0:T(8,128)(2,1)S(1)} collective-permute-done((bf16[64,7168]{1,0:T(8,128)(2,1)}, bf16[64,7168]{1,0:T(8,128)(2,1)S(1)}, u32[]{:S(2)}, u32[]{:S(2)}) %collective-permute-start.7) | collective-permute-done | bytes 917536 | tf_op jit(solution)/shard_map/ppermute | solution.py:307
  76.5 1.3 %collective-permute-start.14 = (bf16[64,7168]{1,0:T(8,128)(2,1)S(1)}, bf16[64,7168]{1,0:T(8,128)(2,1)S(1)}, u32[]{:S(2)}, u32[]{:S(2)}) collective-permute-start(bf16[64,7168]{1,0:T(8,128)(2,1)S(1)} %collective-permute-done.7.piece), channel_id=1, source_target_pairs={{0,8},{8,16},{16,24},{24,28},{28,20},{20,12},{12,4},{4,0},{2,6},{1... | collective-permute-start | bytes 2752520 | tf_op jit(solution)/shard_map/ppermute | solution.py:307
  77.9 2.2 %shard_map.83 = (f32[2,16,64]{2,1,0:T(8,128)S(1)}, f32[2,16,64]{2,1,0:T(8,128)S(1)}) custom-call(s32[10]{0:T(128)S(1)} %pad_add_fusion.facts, bf16[64,7168]{1,0:T(8,128)(2,1)S(1)} %collective-permute-done.7.piece, bf16[64,7168]{1,0:T(8,128)(2,1)S(1)} %collective-permute-done.8.other, bf16[8,7168]{1,0:T(8,128)(2,1)} %collective-permute-done.2.far_rows, ...), custom_call_target="tpu_custom_call" | custom-call | flops 7340032 | bytes 229376 | tf_op jit(solution)/shard_map/pallas_call | solution.py:183
  80.1 1.5 %collective-permute-start.12 = (f32[2,16,64]{2,1,0:T(8,128)S(1)}, f32[2,16,64]{2,1,0:T(8,128)S(1)}, u32[]{:S(2)}, u32[]{:S(2)}) collective-permute-start(f32[2,16,64]{2,1,0:T(8,128)S(1)} %get-tuple-element.87), channel_id=1, source_target_pairs={{0,1},{1,0},{2,3},{3,2},{4,5},{5,4},{6,7},{7,6},{8,9},{9,8},{10,11... | collective-permute-start | bytes 24584 | tf_op jit(solution)/shard_map/ppermute | solution.py:317
  81.6 2.6 %shard_map.85 = (f32[2,3,64,512]{3,2,1,0:T(8,128)S(1)}, f32[2,3,64,512]{3,2,1,0:T(8,128)S(1)}) custom-call(s32[10]{0:T(128)S(1)} %pad_add_fusion.facts, bf16[64,7168]{1,0:T(8,128)(2,1)S(1)} %collective-permute-done.7.piece, bf16[64,7168]{1,0:T(8,128)(2,1)S(1)} %collective-permute-done.8.other, bf16[2,7,1024,512]{3,2,1,0:T(8,128)(2,1)S(1)} %get-tuple-element.88.held, ...), custom_call_target="tpu_custom_call" | custom-call | flops 58720256 | bytes 1835008 | tf_op jit(solution)/shard_map/pallas_call | solution.py:183
  84.2 0.7 collective-permute-start.19
  85.0 4.9 %collective-permute-done.14.piece = bf16[64,7168]{1,0:T(8,128)(2,1)S(1)} collective-permute-done((bf16[64,7168]{1,0:T(8,128)(2,1)S(1)}, bf16[64,7168]{1,0:T(8,128)(2,1)S(1)}, u32[]{:S(2)}, u32[]{:S(2)}) %collective-permute-start.14) | collective-permute-done | bytes 917536 | tf_op jit(solution)/shard_map/ppermute | solution.py:307
  89.9 3.2 %shard_map.84 = (f32[1,64,512]{2,1,0:T(8,128)S(1)}, f32[1,64,512]{2,1,0:T(8,128)S(1)}, bf16[1,64,512]{2,1,0:T(8,128)(2,1)S(1)}, bf16[1,64,512]{2,1,0:T(8,128)(2,1)S(1)}) custom-call(s32[10]{0:T(128)S(1)} %pad_add_fusion.facts, bf16[64,7168]{1,0:T(8,128)(2,1)S(1)} %collective-permute-done.14.piece, bf16[2,7,1024,512]{3,2,1,0:T(8,128)(2,1)S(1)} %get-tuple-element.88.held, ...), custom_call_target="tpu_custom_call" | custom-call | flops 30064771072 | bytes 939524096 | tf_op jit(solution)/shard_map/pallas_call | solution.py:183
  93.2 1.2 %collective-permute-start.15 = (bf16[2,16,64]{2,1,0:T(8,128)(2,1)S(1)}, bf16[2,16,64]{2,1,0:T(8,128)(2,1)S(1)}, u32[]{:S(2)}, u32[]{:S(2)}) collective-permute-start(bf16[2,16,64]{2,1,0:T(8,128)(2,1)S(1)} %get-tuple-element.116), channel_id=1, source_target_pairs={{0,4},{2,6},{4,0},{6,2},{8,12},{10,14},{12,8},{14,10},{16,20},{18,... | collective-permute-start | bytes 12296 | tf_op jit(solution)/shard_map/ppermute | solution.py:489
  94.4 1.1 collective-permute-start.16
  95.4 1.3 %collective-permute-start.17 = (bf16[2,16,64]{2,1,0:T(8,128)(2,1)S(1)}, bf16[2,16,64]{2,1,0:T(8,128)(2,1)S(1)}, u32[]{:S(2)}, u32[]{:S(2)}) collective-permute-start(bf16[2,16,64]{2,1,0:T(8,128)(2,1)S(1)} %get-tuple-element.116), channel_id=1, source_target_pairs={{0,12},{2,14},{4,8},{6,10},{8,4},{10,6},{12,0},{14,2},{16,28},{18,... | collective-permute-start | bytes 12296 | tf_op jit(solution)/shard_map/ppermute | solution.py:489
  96.8 0.2 fusion.14
  96.9 1.6 %collective-permute-start.20 = (bf16[3,64,512]{2,1,0:T(8,128)(2,1)S(1)}, bf16[3,64,512]{2,1,0:T(8,128)(2,1)S(1)}, u32[]{:S(2)}, u32[]{:S(2)}) collective-permute-start(bf16[3,64,512]{2,1,0:T(8,128)(2,1)S(1)} %get-tuple-element.117), channel_id=1, source_target_pairs={{0,1},{1,0},{2,3},{3,2},{4,5},{5,4},{6,7},{7,6},{8,9},{9,8},{10,11... | collective-permute-start | bytes 589832 | tf_op jit(solution)/shard_map/ppermute | solution.py:502
  98.5 0.5 collective-permute-start.22
  99.0 1.3 %collective-permute-start.23 = (bf16[1,64,512]{2,1,0:T(8,128)(2,1)S(1)}, bf16[1,64,512]{2,1,0:T(8,128)(2,1)S(1)}, u32[]{:S(2)}, u32[]{:S(2)}) collective-permute-start(bf16[1,64,512]{2,1,0:T(8,128)(2,1)S(1)} %get-tuple-element.110), channel_id=1, source_target_pairs={{0,3},{1,2},{2,1},{3,0},{4,7},{5,6},{6,5},{7,4},{8,11},{9,10},{10,... | collective-permute-start | bytes 196616 | tf_op jit(solution)/shard_map/ppermute | solution.py:318
  100.4 1.6 %collective-permute-start.18 = (bf16[8,16,64]{2,1,0:T(8,128)(2,1)S(1)}, bf16[8,16,64]{2,1,0:T(8,128)(2,1)S(1)}, u32[]{:S(2)}, u32[]{:S(2)}) collective-permute-start(bf16[8,16,64]{2,1,0:T(8,128)(2,1)S(1)} %pad_maximum_fusion.4), channel_id=1, source_target_pairs={{0,16},{2,18},{4,20},{6,22},{8,24},{10,26},{12,28},{14,30},{16,0},... | collective-permute-start | bytes 49160 | tf_op jit(solution)/shard_map/ppermute | solution.py:489
  102.0 3.6 %collective-permute-done.18 = bf16[8,16,64]{2,1,0:T(8,128)(2,1)S(1)} collective-permute-done((bf16[8,16,64]{2,1,0:T(8,128)(2,1)S(1)}, bf16[8,16,64]{2,1,0:T(8,128)(2,1)S(1)}, u32[]{:S(2)}, u32[]{:S(2)}) %collective-permute-start.18) | collective-permute-done | bytes 16416 | tf_op jit(solution)/shard_map/ppermute | solution.py:489
  105.6 1.3 %shard_map.86.rest = f32[4,64,512]{2,1,0:T(8,128)S(1)} custom-call(s32[10]{0:T(128)S(1)} %pad_add_fusion.facts, bf16[256,64]{1,0:T(8,128)(2,1)S(1)} %bitcast.26, bf16[256,256]{1,0:T(8,128)(2,1)S(1)} %fusion.12.spots, bf16[256,1024]{1,0:T(8,128)(2,1)S(1)} %compare_convert_fusion.mask, bf16[64,1024]{1,0:T(8,128)(2,1)S(1)} %fusion.13.copies, ...), custom_call_target="tpu_custom_call" | custom-call | flops 8388608 | bytes 262144 | tf_op jit(solution)/shard_map/pallas_call | solution.py:183
  107.0 1.3 %shard_map.87 = bf16[4,64,512]{2,1,0:T(8,128)(2,1)} custom-call(s32[10]{0:T(128)S(1)} %pad_add_fusion.facts, f32[4,64,512]{2,1,0:T(8,128)S(1)} %shard_map.86.rest, f32[1,64,512]{2,1,0:T(8,128)S(1)} %get-tuple-element.107.kept, f32[1,64,512]{2,1,0:T(8,128)S(1)} %collective-permute-done.21.got_sib, bf16[1,64,512]{2,1,0:T(8,128)(2,1)S(1)} %collective-permute-done.22.got_mp, ...), custom_call_target="tpu_custom_call" | custom-call | flops 4096 | bytes 128 | tf_op jit(solution)/shard_map/pallas_call | solution.py:183
  (74 shorter events, 2.3 us)
Async XLA Ops:
  1.4 5.5 %copy-start.1 = (bf16[16,32,512]{2,1,0:T(8,128)(2,1)S(1)}, bf16[16,32,512]{2,1,0:T(8,128)(2,1)}, u32[]{:S(2)}) copy-start(bf16[16,32,512]{2,1,0:T(8,128)(2,1)} %param.12) | copy-start | bytes 1572868
  1.4 2.0 %collective-permute-start = (bf16[32,7168]{1,0:T(8,128)(2,1)S(1)}, bf16[32,7168]{1,0:T(8,128)(2,1)S(1)}, u32[]{:S(2)}, u32[]{:S(2)}) collective-permute-start(bf16[32,7168]{1,0:T(8,128)(2,1)S(1)} %fusion.9), channel_id=1, source_target_pairs={{0,2},{2,0},{8,10},{10,8},{16,18},{18,16},{24,26},{26,24},{28,30},... | collective-permute-start | bytes 1376264 | tf_op jit(solution)/shard_map/ppermute | solution.py:301
  3.4 18.1 %copy-start.2 = (s32[512,1]{0,1:T(1,128)S(1)}, s32[512,1]{0,1:T(1,128)}, u32[]{:S(2)}) copy-start(s32[512,1]{0,1:T(1,128)} %param.13) | copy-start | bytes 6148
  3.4 18.1 %copy-start.3 = (s32[16]{0:T(128)S(1)}, s32[16]{0:T(128)}, u32[]{:S(2)}) copy-start(s32[16]{0:T(128)} %param.14) | copy-start | bytes 196
  3.5 54.1 %collective-permute-start.10 = (bf16[14336,512]{1,0:T(8,128)(2,1)}, bf16[14336,512]{1,0:T(8,128)(2,1)}, u32[]{:S(2)}, u32[]{:S(2)}) collective-permute-start(bf16[14336,512]{1,0:T(8,128)(2,1)} %refs_7_), channel_id=1, source_target_pairs={{0,2},{2,0},{8,10},{10,8},{16,18},{18,16},{24,26},{26,24},{28,30},... | collective-permute-start | bytes 44040200 | tf_op jit(solution)/shard_map/ppermute | solution.py:301
  4.0 28.1 %collective-permute-start.3 = (bf16[64,7168]{1,0:T(8,128)(2,1)S(1)}, bf16[64,7168]{1,0:T(8,128)(2,1)S(1)}, u32[]{:S(2)}, u32[]{:S(2)}) collective-permute-start(bf16[64,7168]{1,0:T(8,128)(2,1)S(1)} %pad_maximum_fusion.2.refs_0_), channel_id=1, source_target_pairs={{0,8},{8,16},{16,24},{24,28},{28,20},{20,12},{12,4},{4,0},{2,6},{1... | collective-permute-start | bytes 2752520 | tf_op jit(solution)/shard_map/ppermute | solution.py:307
  6.8 25.4 %collective-permute-start.5 = (bf16[64,7168]{1,0:T(8,128)(2,1)S(1)}, bf16[64,7168]{1,0:T(8,128)(2,1)S(1)}, u32[]{:S(2)}, u32[]{:S(2)}) collective-permute-start(bf16[64,7168]{1,0:T(8,128)(2,1)S(1)} %pad_maximum_fusion.2.refs_0_), channel_id=1, source_target_pairs={{0,4},{8,0},{16,8},{24,16},{28,24},{20,28},{12,20},{4,12},{2,10},{... | collective-permute-start | bytes 2752520 | tf_op jit(solution)/shard_map/ppermute | solution.py:307
  6.8 49.4 %collective-permute-start.9 = (bf16[64,14336]{1,0:T(8,128)(2,1)}, bf16[64,14336]{1,0:T(8,128)(2,1)}, u32[]{:S(2)}, u32[]{:S(2)}) collective-permute-start(bf16[64,14336]{1,0:T(8,128)(2,1)} %bitcast.28), channel_id=1, source_target_pairs={{0,2},{2,0},{8,10},{10,8},{16,18},{18,16},{24,26},{26,24},{28,30},... | collective-permute-start | bytes 5505032 | tf_op jit(solution)/shard_map/ppermute | solution.py:301
  7.0 14.5 %collective-permute-start.1 = (bf16[16,32,512]{2,1,0:T(8,128)(2,1)S(1)}, bf16[16,32,512]{2,1,0:T(8,128)(2,1)}, u32[]{:S(2)}, u32[]{:S(2)}) collective-permute-start(bf16[16,32,512]{2,1,0:T(8,128)(2,1)S(1)} %copy-done.1), channel_id=1, source_target_pairs={{0,1},{1,0},{2,3},{3,2},{4,5},{5,4},{6,7},{7,6},{8,9},{9,8},{10,11... | collective-permute-start | bytes 1572872 | tf_op jit(solution)/shard_map/ppermute | solution.py:330
  24.2 13.5 %collective-permute-start.2 = (bf16[8,7168]{1,0:T(8,128)(2,1)}, bf16[8,7168]{1,0:T(8,128)(2,1)}, u32[]{:S(2)}, u32[]{:S(2)}) collective-permute-start(bf16[8,7168]{1,0:T(8,128)(2,1)} %convolution_convert_fusion), channel_id=1, source_target_pairs={{0,28},{2,30},{8,20},{10,22},{16,12},{18,14},{24,4},{26,6},{28,0},... | collective-permute-start | bytes 344072 | tf_op jit(solution)/shard_map/ppermute | solution.py:301
  32.1 22.1 %collective-permute-start.4 = (bf16[64,7168]{1,0:T(8,128)(2,1)S(1)}, bf16[64,7168]{1,0:T(8,128)(2,1)}, u32[]{:S(2)}, u32[]{:S(2)}) collective-permute-start(bf16[64,7168]{1,0:T(8,128)(2,1)S(1)} %collective-permute-done.3.refs_1_), channel_id=1, source_target_pairs={{0,8},{8,16},{16,24},{24,28},{28,20},{20,12},{12,4},{4,0},{2,6},{1... | collective-permute-start | bytes 2752520 | tf_op jit(solution)/shard_map/ppermute | solution.py:307
  32.2 22.0 %collective-permute-start.6 = (bf16[64,7168]{1,0:T(8,128)(2,1)S(1)}, bf16[64,7168]{1,0:T(8,128)(2,1)}, u32[]{:S(2)}, u32[]{:S(2)}) collective-permute-start(bf16[64,7168]{1,0:T(8,128)(2,1)S(1)} %collective-permute-done.5.refs_2_), channel_id=1, source_target_pairs={{0,4},{8,0},{16,8},{24,16},{28,24},{20,28},{12,20},{4,12},{2,10},{... | collective-permute-start | bytes 2752520 | tf_op jit(solution)/shard_map/ppermute | solution.py:307
  37.7 19.8 %copy-start = (bf16[64,7168]{1,0:T(8,128)(2,1)S(1)}, bf16[64,7168]{1,0:T(8,128)(2,1)}, u32[]{:S(2)}) copy-start(bf16[64,7168]{1,0:T(8,128)(2,1)} %constant_dynamic-slice_fusion) | copy-start | bytes 2752516
  54.2 22.4 %collective-permute-start.7 = (bf16[64,7168]{1,0:T(8,128)(2,1)}, bf16[64,7168]{1,0:T(8,128)(2,1)S(1)}, u32[]{:S(2)}, u32[]{:S(2)}) collective-permute-start(bf16[64,7168]{1,0:T(8,128)(2,1)} %collective-permute-done.4.refs_3_), channel_id=1, source_target_pairs={{0,8},{8,16},{16,24},{24,28},{28,20},{20,12},{12,4},{4,0},{2,6},{1... | collective-permute-start | bytes 2752520 | tf_op jit(solution)/shard_map/ppermute | solution.py:307
  55.3 21.3 %collective-permute-start.8 = (bf16[64,7168]{1,0:T(8,128)(2,1)}, bf16[64,7168]{1,0:T(8,128)(2,1)S(1)}, u32[]{:S(2)}, u32[]{:S(2)}) collective-permute-start(bf16[64,7168]{1,0:T(8,128)(2,1)} %collective-permute-done.6.refs_4_), channel_id=1, source_target_pairs={{0,4},{8,0},{16,8},{24,16},{28,24},{20,28},{12,20},{4,12},{2,10},{... | collective-permute-start | bytes 2752520 | tf_op jit(solution)/shard_map/ppermute | solution.py:307
  76.5 13.4 %collective-permute-start.14 = (bf16[64,7168]{1,0:T(8,128)(2,1)S(1)}, bf16[64,7168]{1,0:T(8,128)(2,1)S(1)}, u32[]{:S(2)}, u32[]{:S(2)}) collective-permute-start(bf16[64,7168]{1,0:T(8,128)(2,1)S(1)} %collective-permute-done.7.piece), channel_id=1, source_target_pairs={{0,8},{8,16},{16,24},{24,28},{28,20},{20,12},{12,4},{4,0},{2,6},{1... | collective-permute-start | bytes 2752520 | tf_op jit(solution)/shard_map/ppermute | solution.py:307
  80.1 13.1 %collective-permute-start.12 = (f32[2,16,64]{2,1,0:T(8,128)S(1)}, f32[2,16,64]{2,1,0:T(8,128)S(1)}, u32[]{:S(2)}, u32[]{:S(2)}) collective-permute-start(f32[2,16,64]{2,1,0:T(8,128)S(1)} %get-tuple-element.87), channel_id=1, source_target_pairs={{0,1},{1,0},{2,3},{3,2},{4,5},{5,4},{6,7},{7,6},{8,9},{9,8},{10,11... | collective-permute-start | bytes 24584 | tf_op jit(solution)/shard_map/ppermute | solution.py:317
  81.6 11.6 %collective-permute-start.13 = (f32[2,16,64]{2,1,0:T(8,128)S(1)}, f32[2,16,64]{2,1,0:T(8,128)S(1)}, u32[]{:S(2)}, u32[]{:S(2)}) collective-permute-start(f32[2,16,64]{2,1,0:T(8,128)S(1)} %get-tuple-element.87), channel_id=1, source_target_pairs={{0,3},{1,2},{2,1},{3,0},{4,7},{5,6},{6,5},{7,4},{8,11},{9,10},{10,... | collective-permute-start | bytes 24584 | tf_op jit(solution)/shard_map/ppermute | solution.py:318
  84.2 12.5 %collective-permute-start.19 = (f32[2,3,64,512]{3,2,1,0:T(8,128)S(1)}, f32[2,3,64,512]{3,2,1,0:T(8,128)S(1)}, u32[]{:S(2)}, u32[]{:S(2)}) collective-permute-start(f32[2,3,64,512]{3,2,1,0:T(8,128)S(1)} %get-tuple-element.106), channel_id=1, source_target_pairs={{0,2},{2,0},{8,10},{10,8},{16,18},{18,16},{24,26},{26,24},{28,30},... | collective-permute-start | bytes 2359304 | tf_op jit(solution)/shard_map/ppermute | solution.py:301
  85.0 8.2 %collective-permute-start.11 = (f32[2,16,64]{2,1,0:T(8,128)S(1)}, f32[2,16,64]{2,1,0:T(8,128)S(1)}, u32[]{:S(2)}, u32[]{:S(2)}) collective-permute-start(f32[2,16,64]{2,1,0:T(8,128)S(1)} %get-tuple-element.86), channel_id=1, source_target_pairs={{0,2},{2,0},{8,10},{10,8},{16,18},{18,16},{24,26},{26,24},{28,30},... | collective-permute-start | bytes 24584 | tf_op jit(solution)/shard_map/ppermute | solution.py:301
  93.2 5.3 %collective-permute-start.15 = (bf16[2,16,64]{2,1,0:T(8,128)(2,1)S(1)}, bf16[2,16,64]{2,1,0:T(8,128)(2,1)S(1)}, u32[]{:S(2)}, u32[]{:S(2)}) collective-permute-start(bf16[2,16,64]{2,1,0:T(8,128)(2,1)S(1)} %get-tuple-element.116), channel_id=1, source_target_pairs={{0,4},{2,6},{4,0},{6,2},{8,12},{10,14},{12,8},{14,10},{16,20},{18,... | collective-permute-start | bytes 12296 | tf_op jit(solution)/shard_map/ppermute | solution.py:489
  94.4 4.6 %collective-permute-start.16 = (bf16[2,16,64]{2,1,0:T(8,128)(2,1)S(1)}, bf16[2,16,64]{2,1,0:T(8,128)(2,1)S(1)}, u32[]{:S(2)}, u32[]{:S(2)}) collective-permute-start(bf16[2,16,64]{2,1,0:T(8,128)(2,1)S(1)} %get-tuple-element.116), channel_id=1, source_target_pairs={{0,8},{2,10},{4,12},{6,14},{8,0},{10,2},{12,4},{14,6},{16,24},{18,... | collective-permute-start | bytes 12296 | tf_op jit(solution)/shard_map/ppermute | solution.py:489
  95.4 4.9 %collective-permute-start.17 = (bf16[2,16,64]{2,1,0:T(8,128)(2,1)S(1)}, bf16[2,16,64]{2,1,0:T(8,128)(2,1)S(1)}, u32[]{:S(2)}, u32[]{:S(2)}) collective-permute-start(bf16[2,16,64]{2,1,0:T(8,128)(2,1)S(1)} %get-tuple-element.116), channel_id=1, source_target_pairs={{0,12},{2,14},{4,8},{6,10},{8,4},{10,6},{12,0},{14,2},{16,28},{18,... | collective-permute-start | bytes 12296 | tf_op jit(solution)/shard_map/ppermute | solution.py:489
  96.9 8.7 %collective-permute-start.20 = (bf16[3,64,512]{2,1,0:T(8,128)(2,1)S(1)}, bf16[3,64,512]{2,1,0:T(8,128)(2,1)S(1)}, u32[]{:S(2)}, u32[]{:S(2)}) collective-permute-start(bf16[3,64,512]{2,1,0:T(8,128)(2,1)S(1)} %get-tuple-element.117), channel_id=1, source_target_pairs={{0,1},{1,0},{2,3},{3,2},{4,5},{5,4},{6,7},{7,6},{8,9},{9,8},{10,11... | collective-permute-start | bytes 589832 | tf_op jit(solution)/shard_map/ppermute | solution.py:502
  98.5 8.5 %collective-permute-start.21 = (f32[1,64,512]{2,1,0:T(8,128)S(1)}, f32[1,64,512]{2,1,0:T(8,128)S(1)}, u32[]{:S(2)}, u32[]{:S(2)}) collective-permute-start(f32[1,64,512]{2,1,0:T(8,128)S(1)} %get-tuple-element.108), channel_id=1, source_target_pairs={{0,2},{2,0},{8,10},{10,8},{16,18},{18,16},{24,26},{26,24},{28,30},... | collective-permute-start | bytes 393224 | tf_op jit(solution)/shard_map/ppermute | solution.py:301
  98.5 8.5 %collective-permute-start.22 = (bf16[1,64,512]{2,1,0:T(8,128)(2,1)S(1)}, bf16[1,64,512]{2,1,0:T(8,128)(2,1)S(1)}, u32[]{:S(2)}, u32[]{:S(2)}) collective-permute-start(bf16[1,64,512]{2,1,0:T(8,128)(2,1)S(1)} %get-tuple-element.109), channel_id=1, source_target_pairs={{0,1},{1,0},{2,3},{3,2},{4,5},{5,4},{6,7},{7,6},{8,9},{9,8},{10,11... | collective-permute-start | bytes 196616 | tf_op jit(solution)/shard_map/ppermute | solution.py:317
  99.0 7.9 %collective-permute-start.23 = (bf16[1,64,512]{2,1,0:T(8,128)(2,1)S(1)}, bf16[1,64,512]{2,1,0:T(8,128)(2,1)S(1)}, u32[]{:S(2)}, u32[]{:S(2)}) collective-permute-start(bf16[1,64,512]{2,1,0:T(8,128)(2,1)S(1)} %get-tuple-element.110), channel_id=1, source_target_pairs={{0,3},{1,2},{2,1},{3,0},{4,7},{5,6},{6,5},{7,4},{8,11},{9,10},{10,... | collective-permute-start | bytes 196616 | tf_op jit(solution)/shard_map/ppermute | solution.py:318
  100.4 5.2 %collective-permute-start.18 = (bf16[8,16,64]{2,1,0:T(8,128)(2,1)S(1)}, bf16[8,16,64]{2,1,0:T(8,128)(2,1)S(1)}, u32[]{:S(2)}, u32[]{:S(2)}) collective-permute-start(bf16[8,16,64]{2,1,0:T(8,128)(2,1)S(1)} %pad_maximum_fusion.4), channel_id=1, source_target_pairs={{0,16},{2,18},{4,20},{6,22},{8,24},{10,26},{12,28},{14,30},{16,0},... | collective-permute-start | bytes 49160 | tf_op jit(solution)/shard_map/ppermute | solution.py:489

commit v16 on v15

--- a/solution.py
+++ b/solution.py
@@ -494,11 +494,12 @@
 
     got, one = lax.optimization_barrier((got, one))
     low = (kept + got[1] + (got[0] + got[2])[::-1]).astype(bf16)
-    gap = 1
-    while gap < nodes:
-        reach = min(4, nodes // gap)
-        low = gather(low, gap, reach)
-        gap *= reach
+    reach = min(4, nodes)
+    low = gather(low, 1, reach)
+    low, one[0] = lax.optimization_barrier((low, one[0]))
+    while reach < nodes:
+        low = gather(low, reach, 2)
+        reach *= 2
     got_more = lax.ppermute(out_more, INNER, SWAP)
     got_one = to_three(*one)
 

time: 109 us -> 109 us (level)
  transfers between devices with their start and end apart: 24 -> 24, of which waited for: 5 -> 8; matrix products, arithmetic and copies ran while one was open for 15% -> 15% of each run, Pallas kernels for 18% -> 18%
where the time goes in v16:
time: 109 us
  waiting for transfers between devices  43.4 us (40%)
  starting transfers between devices  26.9 us (25%)
  Pallas kernels  20.8 us (19%)
  other arithmetic  9.15 us (8%)
  local copies, waits for them, and re-layouts  7.36 us (7%)
    ppermute x7, waiting for transfers between devices, turn(): return lax.ppermute(value, 'wide', pairs)  28.9 us
    pallas_call x6, Pallas kernels, kernel_call(): pl.pallas_call(kernel, in_specs=[pl.BlockSpec(memory_space=pltpu.SMEM)] +...  20.8 us
    ppermute x1, waiting for transfers between devices, ringed(): other_second = lax.ppermute(second_factor_table, INNER, SWAP)  10.5 us
    ppermute x7, starting transfers between devices, turn(): return lax.ppermute(value, 'wide', pairs)  8.2 us
    ppermute x7, starting transfers between devices, send(): return lax.ppermute(value, 'wide', moved(shift, cross))  6.68 us
    ppermute x4, starting transfers between devices, from_node(): lax.ppermute(value, 'wide', [(w, w ^ 2 * gap) for w in range(owners)])  5.32 us
    dynamic_slice x2, local copies, waits for them, and re-layouts, half_of(): return lax.dynamic_slice_in_dim(value, which * depth, depth, axis)  3.42 us
    ppermute x2, starting transfers between devices, to_three(): lax.ppermute(to_mp, INNER, SWAP)  2.99 us
  transfers between devices with their start and end apart: 24, of which 8 were waited for; matrix products, arithmetic and copies ran while one was open for 15% of the time, Pallas kernels for 18%

profile of v16, /device:TPU:0, one launch (start us, length us, event | category | flops | bytes accessed | tf_op | source)
XLA Modules:
  0.0 108.7 jit_solution(14767506862025971328)
XLA Ops:
  0.0 1.4 %fusion.9 = bf16[32,7168]{1,0:T(8,128)(2,1)S(1)} fusion(bf16[32,14336]{1,0:T(8,128)(2,1)} %param.9, s32[]{:T(128)S(6)} %select_n.105, bf16[32,14336]{1,0:T(8,128)(2,1)} %param.8), kind=kLoop, calls=%fused_computation.18 | loop fusion | flops 1835008 | bytes 1376260 | tf_op jit(solution)/shard_map/convert_element_type | solution.py:199
  1.4 0.5 collective-permute-start
  2.0 1.4 %fusion.8 = bf16[32,7168]{1,0:T(8,128)(2,1)S(1)} fusion(bf16[32,14336]{1,0:T(8,128)(2,1)} %param.9, s32[]{:T(128)S(6)} %select_n.106, bf16[32,14336]{1,0:T(8,128)(2,1)} %param.8), kind=kLoop, calls=%fused_computation.17 | loop fusion | flops 1835008 | bytes 1376260 | tf_op jit(solution)/shard_map/convert_element_type | solution.py:199
  3.5 0.4 collective-permute-start.10
  4.0 2.8 %collective-permute-start.3 = (bf16[64,7168]{1,0:T(8,128)(2,1)S(1)}, bf16[64,7168]{1,0:T(8,128)(2,1)S(1)}, u32[]{:S(2)}, u32[]{:S(2)}) collective-permute-start(bf16[64,7168]{1,0:T(8,128)(2,1)S(1)} %pad_maximum_fusion.2.refs_0_), channel_id=1, source_target_pairs={{0,8},{8,16},{16,24},{24,28},{28,20},{20,12},{12,4},{4,0},{2,6},{1... | collective-permute-start | bytes 2752520 | tf_op jit(solution)/shard_map/ppermute | solution.py:307
  7.0 1.8 %collective-permute-start.1 = (bf16[16,32,512]{2,1,0:T(8,128)(2,1)S(1)}, bf16[16,32,512]{2,1,0:T(8,128)(2,1)}, u32[]{:S(2)}, u32[]{:S(2)}) collective-permute-start(bf16[16,32,512]{2,1,0:T(8,128)(2,1)S(1)} %copy-done.1), channel_id=1, source_target_pairs={{0,1},{1,0},{2,3},{3,2},{4,5},{5,4},{6,7},{7,6},{8,9},{9,8},{10,11... | collective-permute-start | bytes 1572872 | tf_op jit(solution)/shard_map/ppermute | solution.py:330
  8.8 2.2 %constant_dynamic-slice_fusion = bf16[64,7168]{1,0:T(8,128)(2,1)} fusion(bf16[64,14336]{1,0:T(8,128)(2,1)} %bitcast.29, s32[]{:T(128)S(6)} %select_n.124), kind=kLoop, calls=%fused_computation.76 | loop fusion | bytes 1835012 | tf_op jit(solution)/shard_map/dynamic_slice | solution.py:310
  10.9 10.5 %collective-permute-done.1 = bf16[16,32,512]{2,1,0:T(8,128)(2,1)} collective-permute-done((bf16[16,32,512]{2,1,0:T(8,128)(2,1)S(1)}, bf16[16,32,512]{2,1,0:T(8,128)(2,1)}, u32[]{:S(2)}, u32[]{:S(2)}) %collective-permute-start.1) | collective-permute-done | bytes 524320 | tf_op jit(solution)/shard_map/ppermute | solution.py:330
  21.6 0.7 constant_dynamic-slice_fusion.4
  22.3 0.5 convert_reduce_fusion
  23.3 0.9 convolution_convert_fusion
  24.2 4.8 %collective-permute-start.2 = (bf16[8,7168]{1,0:T(8,128)(2,1)}, bf16[8,7168]{1,0:T(8,128)(2,1)}, u32[]{:S(2)}, u32[]{:S(2)}) collective-permute-start(bf16[8,7168]{1,0:T(8,128)(2,1)} %convolution_convert_fusion), channel_id=1, source_target_pairs={{0,28},{2,30},{8,20},{10,22},{16,12},{18,14},{24,4},{26,6},{28,0},... | collective-permute-start | bytes 344072 | tf_op jit(solution)/shard_map/ppermute | solution.py:301
  29.6 0.7 add_convert_fusion.1
  30.3 0.6 add_convert_fusion
  31.3 0.7 and_convert_fusion
  32.2 2.0 %collective-permute-start.6 = (bf16[64,7168]{1,0:T(8,128)(2,1)S(1)}, bf16[64,7168]{1,0:T(8,128)(2,1)}, u32[]{:S(2)}, u32[]{:S(2)}) collective-permute-start(bf16[64,7168]{1,0:T(8,128)(2,1)S(1)} %collective-permute-done.5.refs_2_), channel_id=1, source_target_pairs={{0,4},{8,0},{16,8},{24,16},{28,24},{20,28},{12,20},{4,12},{2,10},{... | collective-permute-start | bytes 2752520 | tf_op jit(solution)/shard_map/ppermute | solution.py:307
  34.2 0.2 compare_convert_fusion.mask
  34.5 1.0 reshape.433
  35.4 0.7 copy.11
  36.1 0.8 slice.39.refs_6_
  36.9 0.7 pad_maximum_fusion.4.choices
  37.7 1.3 %pad_maximum_fusion.1.second = bf16[1024,512]{1,0:T(8,128)(2,1)S(1)} fusion(bf16[512,512]{1,0:T(8,128)(2,1)} %bitcast.9, bf16[512,512]{1,0:T(8,128)(2,1)} %bitcast.27), kind=kLoop, calls=%fused_computation.6 | loop fusion | flops 2097152 | bytes 2097152 | tf_op jit(solution)/shard_map/concatenate | solution.py:418
  39.0 15.1 %collective-permute-done.4.refs_3_ = bf16[64,7168]{1,0:T(8,128)(2,1)} collective-permute-done((bf16[64,7168]{1,0:T(8,128)(2,1)S(1)}, bf16[64,7168]{1,0:T(8,128)(2,1)}, u32[]{:S(2)}, u32[]{:S(2)}) %collective-permute-start.4) | collective-permute-done | bytes 917536 | tf_op jit(solution)/shard_map/ppermute | solution.py:307
  54.2 1.1 collective-permute-start.7
  55.3 0.9 collective-permute-start.8
  56.2 1.2 %constant_dynamic-slice_fusion.1 = bf16[64,7168]{1,0:T(8,128)(2,1)S(1)} fusion(bf16[64,14336]{1,0:T(8,128)(2,1)} %collective-permute-done.9, s32[]{:T(128)S(6)} %select_n.124), kind=kLoop, calls=%fused_computation.77 | loop fusion | bytes 1835012 | tf_op jit(solution)/shard_map/dynamic_slice | solution.py:310
  57.6 10.1 %shard_map.82 = (f32[1,64,512]{2,1,0:T(8,128)S(1)}, f32[1,64,512]{2,1,0:T(8,128)S(1)}, f32[4,64,512]{2,1,0:T(8,128)S(1)}, f32[4,64,512]{2,1,0:T(8,128)S(1)}, f32...) custom-call(s32[10]{0:T(128)S(1)} %pad_add_fusion.facts, bf16[64,7168]{1,0:T(8,128)(2,1)S(1)} %pad_maximum_fusion.2.refs_0_, ...), custom_call_target="tpu_custom_call" | custom-call | flops 165150720 | bytes 5160960 | tf_op jit(solution)/shard_map/pallas_call | solution.py:183
  67.7 8.8 %collective-permute-done.7.piece = bf16[64,7168]{1,0:T(8,128)(2,1)S(1)} collective-permute-done((bf16[64,7168]{1,0:T(8,128)(2,1)}, bf16[64,7168]{1,0:T(8,128)(2,1)S(1)}, u32[]{:S(2)}, u32[]{:S(2)}) %collective-permute-start.7) | collective-permute-done | bytes 917536 | tf_op jit(solution)/shard_map/ppermute | solution.py:307
  76.5 1.3 %collective-permute-start.14 = (bf16[64,7168]{1,0:T(8,128)(2,1)S(1)}, bf16[64,7168]{1,0:T(8,128)(2,1)S(1)}, u32[]{:S(2)}, u32[]{:S(2)}) collective-permute-start(bf16[64,7168]{1,0:T(8,128)(2,1)S(1)} %collective-permute-done.7.piece), channel_id=1, source_target_pairs={{0,8},{8,16},{16,24},{24,28},{28,20},{20,12},{12,4},{4,0},{2,6},{1... | collective-permute-start | bytes 2752520 | tf_op jit(solution)/shard_map/ppermute | solution.py:307
  77.9 2.2 %shard_map.83 = (f32[2,16,64]{2,1,0:T(8,128)S(1)}, f32[2,16,64]{2,1,0:T(8,128)S(1)}) custom-call(s32[10]{0:T(128)S(1)} %pad_add_fusion.facts, bf16[64,7168]{1,0:T(8,128)(2,1)S(1)} %collective-permute-done.7.piece, bf16[64,7168]{1,0:T(8,128)(2,1)S(1)} %collective-permute-done.8.other, bf16[8,7168]{1,0:T(8,128)(2,1)} %collective-permute-done.2.far_rows, ...), custom_call_target="tpu_custom_call" | custom-call | flops 7340032 | bytes 229376 | tf_op jit(solution)/shard_map/pallas_call | solution.py:183
  80.1 1.5 %collective-permute-start.12 = (f32[2,16,64]{2,1,0:T(8,128)S(1)}, f32[2,16,64]{2,1,0:T(8,128)S(1)}, u32[]{:S(2)}, u32[]{:S(2)}) collective-permute-start(f32[2,16,64]{2,1,0:T(8,128)S(1)} %get-tuple-element.89), channel_id=1, source_target_pairs={{0,1},{1,0},{2,3},{3,2},{4,5},{5,4},{6,7},{7,6},{8,9},{9,8},{10,11... | collective-permute-start | bytes 24584 | tf_op jit(solution)/shard_map/ppermute | solution.py:317
  81.6 2.6 %shard_map.85 = (f32[2,3,64,512]{3,2,1,0:T(8,128)S(1)}, f32[2,3,64,512]{3,2,1,0:T(8,128)S(1)}) custom-call(s32[10]{0:T(128)S(1)} %pad_add_fusion.facts, bf16[64,7168]{1,0:T(8,128)(2,1)S(1)} %collective-permute-done.7.piece, bf16[64,7168]{1,0:T(8,128)(2,1)S(1)} %collective-permute-done.8.other, bf16[2,7,1024,512]{3,2,1,0:T(8,128)(2,1)S(1)} %get-tuple-element.90.held, ...), custom_call_target="tpu_custom_call" | custom-call | flops 58720256 | bytes 1835008 | tf_op jit(solution)/shard_map/pallas_call | solution.py:183
  84.2 0.7 collective-permute-start.19
  85.0 4.9 %collective-permute-done.14.piece = bf16[64,7168]{1,0:T(8,128)(2,1)S(1)} collective-permute-done((bf16[64,7168]{1,0:T(8,128)(2,1)S(1)}, bf16[64,7168]{1,0:T(8,128)(2,1)S(1)}, u32[]{:S(2)}, u32[]{:S(2)}) %collective-permute-start.14) | collective-permute-done | bytes 917536 | tf_op jit(solution)/shard_map/ppermute | solution.py:307
  89.9 3.2 %shard_map.84 = (f32[1,64,512]{2,1,0:T(8,128)S(1)}, f32[1,64,512]{2,1,0:T(8,128)S(1)}, bf16[1,64,512]{2,1,0:T(8,128)(2,1)S(1)}, bf16[1,64,512]{2,1,0:T(8,128)(2,1)S(1)}) custom-call(s32[10]{0:T(128)S(1)} %pad_add_fusion.facts, bf16[64,7168]{1,0:T(8,128)(2,1)S(1)} %collective-permute-done.14.piece, bf16[2,7,1024,512]{3,2,1,0:T(8,128)(2,1)S(1)} %get-tuple-element.90.held, ...), custom_call_target="tpu_custom_call" | custom-call | flops 30064771072 | bytes 939524096 | tf_op jit(solution)/shard_map/pallas_call | solution.py:183
  93.2 1.2 %collective-permute-start.15 = (bf16[2,16,64]{2,1,0:T(8,128)(2,1)S(1)}, bf16[2,16,64]{2,1,0:T(8,128)(2,1)S(1)}, u32[]{:S(2)}, u32[]{:S(2)}) collective-permute-start(bf16[2,16,64]{2,1,0:T(8,128)(2,1)S(1)} %add_convert_fusion.2), channel_id=1, source_target_pairs={{0,4},{2,6},{4,0},{6,2},{8,12},{10,14},{12,8},{14,10},{16,20},{18,... | collective-permute-start | bytes 12296 | tf_op jit(solution)/shard_map/ppermute | solution.py:489
  94.4 1.0 collective-permute-start.16
  95.4 1.3 %collective-permute-start.17 = (bf16[2,16,64]{2,1,0:T(8,128)(2,1)S(1)}, bf16[2,16,64]{2,1,0:T(8,128)(2,1)S(1)}, u32[]{:S(2)}, u32[]{:S(2)}) collective-permute-start(bf16[2,16,64]{2,1,0:T(8,128)(2,1)S(1)} %add_convert_fusion.2), channel_id=1, source_target_pairs={{0,12},{2,14},{4,8},{6,10},{8,4},{10,6},{12,0},{14,2},{16,28},{18,... | collective-permute-start | bytes 12296 | tf_op jit(solution)/shard_map/ppermute | solution.py:489
  96.7 0.2 fusion.14
  96.9 1.6 %collective-permute-start.20 = (bf16[3,64,512]{2,1,0:T(8,128)(2,1)S(1)}, bf16[3,64,512]{2,1,0:T(8,128)(2,1)S(1)}, u32[]{:S(2)}, u32[]{:S(2)}) collective-permute-start(bf16[3,64,512]{2,1,0:T(8,128)(2,1)S(1)} %get-tuple-element.119), channel_id=1, source_target_pairs={{0,1},{1,0},{2,3},{3,2},{4,5},{5,4},{6,7},{7,6},{8,9},{9,8},{10,11... | collective-permute-start | bytes 589832 | tf_op jit(solution)/shard_map/ppermute | solution.py:503
  98.5 1.5 %collective-permute-done.17 = bf16[2,16,64]{2,1,0:T(8,128)(2,1)S(1)} collective-permute-done((bf16[2,16,64]{2,1,0:T(8,128)(2,1)S(1)}, bf16[2,16,64]{2,1,0:T(8,128)(2,1)S(1)}, u32[]{:S(2)}, u32[]{:S(2)}) %collective-permute-start.17) | collective-permute-done | bytes 4128 | tf_op jit(solution)/shard_map/ppermute | solution.py:489
  100.0 1.8 %collective-permute-start.18 = (bf16[8,16,64]{2,1,0:T(8,128)(2,1)S(1)}, bf16[8,16,64]{2,1,0:T(8,128)(2,1)S(1)}, u32[]{:S(2)}, u32[]{:S(2)}) collective-permute-start(bf16[8,16,64]{2,1,0:T(8,128)(2,1)S(1)} %pad_maximum_fusion.5), channel_id=1, source_target_pairs={{0,16},{2,18},{4,20},{6,22},{8,24},{10,26},{12,28},{14,30},{16,0},... | collective-permute-start | bytes 49160 | tf_op jit(solution)/shard_map/ppermute | solution.py:489
  101.8 1.5 %collective-permute-start.22 = (bf16[1,64,512]{2,1,0:T(8,128)(2,1)S(1)}, bf16[1,64,512]{2,1,0:T(8,128)(2,1)S(1)}, u32[]{:S(2)}, u32[]{:S(2)}) collective-permute-start(bf16[1,64,512]{2,1,0:T(8,128)(2,1)S(1)} %get-tuple-element.113), channel_id=1, source_target_pairs={{0,1},{1,0},{2,3},{3,2},{4,5},{5,4},{6,7},{7,6},{8,9},{9,8},{10,11... | collective-permute-start | bytes 196616 | tf_op jit(solution)/shard_map/ppermute | solution.py:317
  103.3 0.4 collective-permute-start.23
  103.6 1.3 %collective-permute-done.18 = bf16[8,16,64]{2,1,0:T(8,128)(2,1)S(1)} collective-permute-done((bf16[8,16,64]{2,1,0:T(8,128)(2,1)S(1)}, bf16[8,16,64]{2,1,0:T(8,128)(2,1)S(1)}, u32[]{:S(2)}, u32[]{:S(2)}) %collective-permute-start.18) | collective-permute-done | bytes 16416 | tf_op jit(solution)/shard_map/ppermute | solution.py:489
  104.9 1.3 %shard_map.86.rest = f32[4,64,512]{2,1,0:T(8,128)S(1)} custom-call(s32[10]{0:T(128)S(1)} %pad_add_fusion.facts, bf16[256,64]{1,0:T(8,128)(2,1)S(1)} %bitcast.26, bf16[256,256]{1,0:T(8,128)(2,1)S(1)} %fusion.12.spots, bf16[256,1024]{1,0:T(8,128)(2,1)S(1)} %compare_convert_fusion.mask, bf16[64,1024]{1,0:T(8,128)(2,1)S(1)} %fusion.13.copies, ...), custom_call_target="tpu_custom_call" | custom-call | flops 8388608 | bytes 262144 | tf_op jit(solution)/shard_map/pallas_call | solution.py:183
  106.3 1.1 collective-permute-done.23.got_both
  107.4 1.3 %shard_map.87 = bf16[4,64,512]{2,1,0:T(8,128)(2,1)} custom-call(s32[10]{0:T(128)S(1)} %pad_add_fusion.facts, f32[4,64,512]{2,1,0:T(8,128)S(1)} %shard_map.86.rest, f32[1,64,512]{2,1,0:T(8,128)S(1)} %get-tuple-element.111.kept, f32[1,64,512]{2,1,0:T(8,128)S(1)} %collective-permute-done.21.got_sib, bf16[1,64,512]{2,1,0:T(8,128)(2,1)S(1)} %collective-permute-done.22.got_mp, ...), custom_call_target="tpu_custom_call" | custom-call | flops 4096 | bytes 128 | tf_op jit(solution)/shard_map/pallas_call | solution.py:183
  (71 shorter events, 2.6 us)
Async XLA Ops:
  1.4 5.5 %copy-start.1 = (bf16[16,32,512]{2,1,0:T(8,128)(2,1)S(1)}, bf16[16,32,512]{2,1,0:T(8,128)(2,1)}, u32[]{:S(2)}) copy-start(bf16[16,32,512]{2,1,0:T(8,128)(2,1)} %param.12) | copy-start | bytes 1572868
  1.4 2.0 %collective-permute-start = (bf16[32,7168]{1,0:T(8,128)(2,1)S(1)}, bf16[32,7168]{1,0:T(8,128)(2,1)S(1)}, u32[]{:S(2)}, u32[]{:S(2)}) collective-permute-start(bf16[32,7168]{1,0:T(8,128)(2,1)S(1)} %fusion.9), channel_id=1, source_target_pairs={{0,2},{2,0},{8,10},{10,8},{16,18},{18,16},{24,26},{26,24},{28,30},... | collective-permute-start | bytes 1376264 | tf_op jit(solution)/shard_map/ppermute | solution.py:301
  3.4 18.1 %copy-start.2 = (s32[512,1]{0,1:T(1,128)S(1)}, s32[512,1]{0,1:T(1,128)}, u32[]{:S(2)}) copy-start(s32[512,1]{0,1:T(1,128)} %param.13) | copy-start | bytes 6148
  3.4 18.1 %copy-start.3 = (s32[16]{0:T(128)S(1)}, s32[16]{0:T(128)}, u32[]{:S(2)}) copy-start(s32[16]{0:T(128)} %param.14) | copy-start | bytes 196
  3.5 54.1 %collective-permute-start.10 = (bf16[14336,512]{1,0:T(8,128)(2,1)}, bf16[14336,512]{1,0:T(8,128)(2,1)}, u32[]{:S(2)}, u32[]{:S(2)}) collective-permute-start(bf16[14336,512]{1,0:T(8,128)(2,1)} %refs_7_), channel_id=1, source_target_pairs={{0,2},{2,0},{8,10},{10,8},{16,18},{18,16},{24,26},{26,24},{28,30},... | collective-permute-start | bytes 44040200 | tf_op jit(solution)/shard_map/ppermute | solution.py:301
  4.0 28.1 %collective-permute-start.3 = (bf16[64,7168]{1,0:T(8,128)(2,1)S(1)}, bf16[64,7168]{1,0:T(8,128)(2,1)S(1)}, u32[]{:S(2)}, u32[]{:S(2)}) collective-permute-start(bf16[64,7168]{1,0:T(8,128)(2,1)S(1)} %pad_maximum_fusion.2.refs_0_), channel_id=1, source_target_pairs={{0,8},{8,16},{16,24},{24,28},{28,20},{20,12},{12,4},{4,0},{2,6},{1... | collective-permute-start | bytes 2752520 | tf_op jit(solution)/shard_map/ppermute | solution.py:307
  6.8 25.4 %collective-permute-start.5 = (bf16[64,7168]{1,0:T(8,128)(2,1)S(1)}, bf16[64,7168]{1,0:T(8,128)(2,1)S(1)}, u32[]{:S(2)}, u32[]{:S(2)}) collective-permute-start(bf16[64,7168]{1,0:T(8,128)(2,1)S(1)} %pad_maximum_fusion.2.refs_0_), channel_id=1, source_target_pairs={{0,4},{8,0},{16,8},{24,16},{28,24},{20,28},{12,20},{4,12},{2,10},{... | collective-permute-start | bytes 2752520 | tf_op jit(solution)/shard_map/ppermute | solution.py:307
  6.8 49.4 %collective-permute-start.9 = (bf16[64,14336]{1,0:T(8,128)(2,1)}, bf16[64,14336]{1,0:T(8,128)(2,1)}, u32[]{:S(2)}, u32[]{:S(2)}) collective-permute-start(bf16[64,14336]{1,0:T(8,128)(2,1)} %bitcast.28), channel_id=1, source_target_pairs={{0,2},{2,0},{8,10},{10,8},{16,18},{18,16},{24,26},{26,24},{28,30},... | collective-permute-start | bytes 5505032 | tf_op jit(solution)/shard_map/ppermute | solution.py:301
  7.0 14.5 %collective-permute-start.1 = (bf16[16,32,512]{2,1,0:T(8,128)(2,1)S(1)}, bf16[16,32,512]{2,1,0:T(8,128)(2,1)}, u32[]{:S(2)}, u32[]{:S(2)}) collective-permute-start(bf16[16,32,512]{2,1,0:T(8,128)(2,1)S(1)} %copy-done.1), channel_id=1, source_target_pairs={{0,1},{1,0},{2,3},{3,2},{4,5},{5,4},{6,7},{7,6},{8,9},{9,8},{10,11... | collective-permute-start | bytes 1572872 | tf_op jit(solution)/shard_map/ppermute | solution.py:330
  24.2 13.5 %collective-permute-start.2 = (bf16[8,7168]{1,0:T(8,128)(2,1)}, bf16[8,7168]{1,0:T(8,128)(2,1)}, u32[]{:S(2)}, u32[]{:S(2)}) collective-permute-start(bf16[8,7168]{1,0:T(8,128)(2,1)} %convolution_convert_fusion), channel_id=1, source_target_pairs={{0,28},{2,30},{8,20},{10,22},{16,12},{18,14},{24,4},{26,6},{28,0},... | collective-permute-start | bytes 344072 | tf_op jit(solution)/shard_map/ppermute | solution.py:301
  32.1 22.1 %collective-permute-start.4 = (bf16[64,7168]{1,0:T(8,128)(2,1)S(1)}, bf16[64,7168]{1,0:T(8,128)(2,1)}, u32[]{:S(2)}, u32[]{:S(2)}) collective-permute-start(bf16[64,7168]{1,0:T(8,128)(2,1)S(1)} %collective-permute-done.3.refs_1_), channel_id=1, source_target_pairs={{0,8},{8,16},{16,24},{24,28},{28,20},{20,12},{12,4},{4,0},{2,6},{1... | collective-permute-start | bytes 2752520 | tf_op jit(solution)/shard_map/ppermute | solution.py:307
  32.2 22.0 %collective-permute-start.6 = (bf16[64,7168]{1,0:T(8,128)(2,1)S(1)}, bf16[64,7168]{1,0:T(8,128)(2,1)}, u32[]{:S(2)}, u32[]{:S(2)}) collective-permute-start(bf16[64,7168]{1,0:T(8,128)(2,1)S(1)} %collective-permute-done.5.refs_2_), channel_id=1, source_target_pairs={{0,4},{8,0},{16,8},{24,16},{28,24},{20,28},{12,20},{4,12},{2,10},{... | collective-permute-start | bytes 2752520 | tf_op jit(solution)/shard_map/ppermute | solution.py:307
  37.7 19.8 %copy-start = (bf16[64,7168]{1,0:T(8,128)(2,1)S(1)}, bf16[64,7168]{1,0:T(8,128)(2,1)}, u32[]{:S(2)}) copy-start(bf16[64,7168]{1,0:T(8,128)(2,1)} %constant_dynamic-slice_fusion) | copy-start | bytes 2752516
  54.2 22.3 %collective-permute-start.7 = (bf16[64,7168]{1,0:T(8,128)(2,1)}, bf16[64,7168]{1,0:T(8,128)(2,1)S(1)}, u32[]{:S(2)}, u32[]{:S(2)}) collective-permute-start(bf16[64,7168]{1,0:T(8,128)(2,1)} %collective-permute-done.4.refs_3_), channel_id=1, source_target_pairs={{0,8},{8,16},{16,24},{24,28},{28,20},{20,12},{12,4},{4,0},{2,6},{1... | collective-permute-start | bytes 2752520 | tf_op jit(solution)/shard_map/ppermute | solution.py:307
  55.3 21.3 %collective-permute-start.8 = (bf16[64,7168]{1,0:T(8,128)(2,1)}, bf16[64,7168]{1,0:T(8,128)(2,1)S(1)}, u32[]{:S(2)}, u32[]{:S(2)}) collective-permute-start(bf16[64,7168]{1,0:T(8,128)(2,1)} %collective-permute-done.6.refs_4_), channel_id=1, source_target_pairs={{0,4},{8,0},{16,8},{24,16},{28,24},{20,28},{12,20},{4,12},{2,10},{... | collective-permute-start | bytes 2752520 | tf_op jit(solution)/shard_map/ppermute | solution.py:307
  76.5 13.4 %collective-permute-start.14 = (bf16[64,7168]{1,0:T(8,128)(2,1)S(1)}, bf16[64,7168]{1,0:T(8,128)(2,1)S(1)}, u32[]{:S(2)}, u32[]{:S(2)}) collective-permute-start(bf16[64,7168]{1,0:T(8,128)(2,1)S(1)} %collective-permute-done.7.piece), channel_id=1, source_target_pairs={{0,8},{8,16},{16,24},{24,28},{28,20},{20,12},{12,4},{4,0},{2,6},{1... | collective-permute-start | bytes 2752520 | tf_op jit(solution)/shard_map/ppermute | solution.py:307
  80.1 13.1 %collective-permute-start.12 = (f32[2,16,64]{2,1,0:T(8,128)S(1)}, f32[2,16,64]{2,1,0:T(8,128)S(1)}, u32[]{:S(2)}, u32[]{:S(2)}) collective-permute-start(f32[2,16,64]{2,1,0:T(8,128)S(1)} %get-tuple-element.89), channel_id=1, source_target_pairs={{0,1},{1,0},{2,3},{3,2},{4,5},{5,4},{6,7},{7,6},{8,9},{9,8},{10,11... | collective-permute-start | bytes 24584 | tf_op jit(solution)/shard_map/ppermute | solution.py:317
  81.6 11.6 %collective-permute-start.13 = (f32[2,16,64]{2,1,0:T(8,128)S(1)}, f32[2,16,64]{2,1,0:T(8,128)S(1)}, u32[]{:S(2)}, u32[]{:S(2)}) collective-permute-start(f32[2,16,64]{2,1,0:T(8,128)S(1)} %get-tuple-element.89), channel_id=1, source_target_pairs={{0,3},{1,2},{2,1},{3,0},{4,7},{5,6},{6,5},{7,4},{8,11},{9,10},{10,... | collective-permute-start | bytes 24584 | tf_op jit(solution)/shard_map/ppermute | solution.py:318
  84.2 12.5 %collective-permute-start.19 = (f32[2,3,64,512]{3,2,1,0:T(8,128)S(1)}, f32[2,3,64,512]{3,2,1,0:T(8,128)S(1)}, u32[]{:S(2)}, u32[]{:S(2)}) collective-permute-start(f32[2,3,64,512]{3,2,1,0:T(8,128)S(1)} %get-tuple-element.110), channel_id=1, source_target_pairs={{0,2},{2,0},{8,10},{10,8},{16,18},{18,16},{24,26},{26,24},{28,30},... | collective-permute-start | bytes 2359304 | tf_op jit(solution)/shard_map/ppermute | solution.py:301
  85.0 8.2 %collective-permute-start.11 = (f32[2,16,64]{2,1,0:T(8,128)S(1)}, f32[2,16,64]{2,1,0:T(8,128)S(1)}, u32[]{:S(2)}, u32[]{:S(2)}) collective-permute-start(f32[2,16,64]{2,1,0:T(8,128)S(1)} %get-tuple-element.88), channel_id=1, source_target_pairs={{0,2},{2,0},{8,10},{10,8},{16,18},{18,16},{24,26},{26,24},{28,30},... | collective-permute-start | bytes 24584 | tf_op jit(solution)/shard_map/ppermute | solution.py:301
  93.2 5.3 %collective-permute-start.15 = (bf16[2,16,64]{2,1,0:T(8,128)(2,1)S(1)}, bf16[2,16,64]{2,1,0:T(8,128)(2,1)S(1)}, u32[]{:S(2)}, u32[]{:S(2)}) collective-permute-start(bf16[2,16,64]{2,1,0:T(8,128)(2,1)S(1)} %add_convert_fusion.2), channel_id=1, source_target_pairs={{0,4},{2,6},{4,0},{6,2},{8,12},{10,14},{12,8},{14,10},{16,20},{18,... | collective-permute-start | bytes 12296 | tf_op jit(solution)/shard_map/ppermute | solution.py:489
  94.4 4.1 %collective-permute-start.16 = (bf16[2,16,64]{2,1,0:T(8,128)(2,1)S(1)}, bf16[2,16,64]{2,1,0:T(8,128)(2,1)S(1)}, u32[]{:S(2)}, u32[]{:S(2)}) collective-permute-start(bf16[2,16,64]{2,1,0:T(8,128)(2,1)S(1)} %add_convert_fusion.2), channel_id=1, source_target_pairs={{0,8},{2,10},{4,12},{6,14},{8,0},{10,2},{12,4},{14,6},{16,24},{18,... | collective-permute-start | bytes 12296 | tf_op jit(solution)/shard_map/ppermute | solution.py:489
  95.4 4.5 %collective-permute-start.17 = (bf16[2,16,64]{2,1,0:T(8,128)(2,1)S(1)}, bf16[2,16,64]{2,1,0:T(8,128)(2,1)S(1)}, u32[]{:S(2)}, u32[]{:S(2)}) collective-permute-start(bf16[2,16,64]{2,1,0:T(8,128)(2,1)S(1)} %add_convert_fusion.2), channel_id=1, source_target_pairs={{0,12},{2,14},{4,8},{6,10},{8,4},{10,6},{12,0},{14,2},{16,28},{18,... | collective-permute-start | bytes 12296 | tf_op jit(solution)/shard_map/ppermute | solution.py:489
  96.9 8.0 %collective-permute-start.20 = (bf16[3,64,512]{2,1,0:T(8,128)(2,1)S(1)}, bf16[3,64,512]{2,1,0:T(8,128)(2,1)S(1)}, u32[]{:S(2)}, u32[]{:S(2)}) collective-permute-start(bf16[3,64,512]{2,1,0:T(8,128)(2,1)S(1)} %get-tuple-element.119), channel_id=1, source_target_pairs={{0,1},{1,0},{2,3},{3,2},{4,5},{5,4},{6,7},{7,6},{8,9},{9,8},{10,11... | collective-permute-start | bytes 589832 | tf_op jit(solution)/shard_map/ppermute | solution.py:503
  100.0 4.9 %collective-permute-start.18 = (bf16[8,16,64]{2,1,0:T(8,128)(2,1)S(1)}, bf16[8,16,64]{2,1,0:T(8,128)(2,1)S(1)}, u32[]{:S(2)}, u32[]{:S(2)}) collective-permute-start(bf16[8,16,64]{2,1,0:T(8,128)(2,1)S(1)} %pad_maximum_fusion.5), channel_id=1, source_target_pairs={{0,16},{2,18},{4,20},{6,22},{8,24},{10,26},{12,28},{14,30},{16,0},... | collective-permute-start | bytes 49160 | tf_op jit(solution)/shard_map/ppermute | solution.py:489
  101.8 5.6 %collective-permute-start.21 = (f32[1,64,512]{2,1,0:T(8,128)S(1)}, f32[1,64,512]{2,1,0:T(8,128)S(1)}, u32[]{:S(2)}, u32[]{:S(2)}) collective-permute-start(f32[1,64,512]{2,1,0:T(8,128)S(1)} %get-tuple-element.112), channel_id=1, source_target_pairs={{0,2},{2,0},{8,10},{10,8},{16,18},{18,16},{24,26},{26,24},{28,30},... | collective-permute-start | bytes 393224 | tf_op jit(solution)/shard_map/ppermute | solution.py:301
  101.8 4.5 %collective-permute-start.22 = (bf16[1,64,512]{2,1,0:T(8,128)(2,1)S(1)}, bf16[1,64,512]{2,1,0:T(8,128)(2,1)S(1)}, u32[]{:S(2)}, u32[]{:S(2)}) collective-permute-start(bf16[1,64,512]{2,1,0:T(8,128)(2,1)S(1)} %get-tuple-element.113), channel_id=1, source_target_pairs={{0,1},{1,0},{2,3},{3,2},{4,5},{5,4},{6,7},{7,6},{8,9},{9,8},{10,11... | collective-permute-start | bytes 196616 | tf_op jit(solution)/shard_map/ppermute | solution.py:317
  103.3 4.1 %collective-permute-start.23 = (bf16[1,64,512]{2,1,0:T(8,128)(2,1)S(1)}, bf16[1,64,512]{2,1,0:T(8,128)(2,1)S(1)}, u32[]{:S(2)}, u32[]{:S(2)}) collective-permute-start(bf16[1,64,512]{2,1,0:T(8,128)(2,1)S(1)} %get-tuple-element.114), channel_id=1, source_target_pairs={{0,3},{1,2},{2,1},{3,0},{4,7},{5,6},{6,5},{7,4},{8,11},{9,10},{10,... | collective-permute-start | bytes 196616 | tf_op jit(solution)/shard_map/ppermute | solution.py:318

commit v17 on v15

--- a/solution.py
+++ b/solution.py
@@ -36,7 +36,7 @@
     return started(sources, places, ready)
 
 
-def weight_products(rows_of, held, sums, copies=None):
+def weight_products(rows_of, held, sums, copies=None, first=0):
     tiles, tile = held.shape[1:3]
     for total in sums:
         total[...] = jnp.zeros_like(total)
@@ -45,7 +45,7 @@
         for which, total in enumerate(sums):
             if copies:
                 copies[2 * index + which].wait()
-            total[...] += jnp.dot(rows, held[which, index], preferred_element_type=jnp.float32)
+            total[...] += jnp.dot(rows, held[first + which, index], preferred_element_type=jnp.float32)
 
 
 def factor_products(rows_of, table, low):
@@ -151,29 +151,29 @@
         sent[which] = jnp.where(facts[1] == 0, total[half:], total[:half])
 
 
-def last_kernel(facts, piece, held, base, base_sib, *refs):
-    outs, sums = refs[:4], refs[4:]
-    weight_products(lambda here: piece[:, here], held, sums)
-    away = [in_lanes(facts[0], total, 0, piece.shape[0] // 2) for total in sums]
-    share(facts[2], (base[0], base_sib[0]), away, outs, 0)
-
-
-def delta_kernel(pairs, facts, low, spots, mask, copies, second, kept, got, out):
+def last_kernel(which, facts, piece, held, base, mine, others, total):
+    weight_products(lambda here: piece[:, here], held, [total], first=which)
+    away = in_lanes(facts[0], total, 0, piece.shape[0] // 2)
+    mine[0] = jnp.where(facts[2] == 1, base[0], away)
+    others[0] = jnp.where(facts[2] == 1, away, base[0]).astype(others.dtype)
+
+
+def delta_kernel(facts, low, spots, mask, copies, second, out):
     f32 = jnp.float32
     own = jnp.dot(spots[...], low[...], preferred_element_type=f32).astype(jnp.bfloat16)
     spread = jnp.dot(own, copies[...], preferred_element_type=f32).astype(jnp.bfloat16) * mask[...]
     out[...] = jnp.dot(spread, second[...], preferred_element_type=f32).reshape(out.shape)
-    for pair in range(1, pairs):
+
+
+def final_kernel(pairs, facts, delta, kept_more, got_more, kept, got_sib, got_mp, got_both, out):
+    f32 = jnp.float32
+    for pair in range(pairs):
+        if pair:
+            value = kept_more[pair - 1] + got_more[pair - 1].astype(f32)
+        else:
+            value = kept[0] + got_sib[0] + (got_mp[0].astype(f32) + got_both[0].astype(f32))
         place = facts[2 + pairs + pair]
-        out[place] = out[place] + (kept[pair - 1] + got[pair - 1].astype(f32))
-
-
-def final_kernel(pairs, facts, rest, kept, got_sib, got_mp, got_both, out):
-    f32 = jnp.float32
-    value = kept[0] + got_sib[0] + (got_mp[0].astype(f32) + got_both[0].astype(f32))
-    for place in range(out.shape[0]):
-        there = jnp.where(facts[2 + pairs] == place, value, 0)
-        out[place] = (rest[place] + there).astype(out.dtype)
+        out[place] = (value + delta[place]).astype(out.dtype)
 
 
 def kernel_call(kernel, facts, arrays, shapes, scratch, flops, weights=(), grant=12):
@@ -449,10 +449,6 @@
 
     last = turn(one_way, 1)
 
-    def shares(pairs):
-        shape = (pairs, group_rows, width)
-        return [(shape, f32)] * 2 + [(shape, bf16)] * 2
-
     kept, sent = kernel_call(
         low_kernel,
         facts,
@@ -473,40 +469,43 @@
         sums(2 * group_rows, False),
         flops(2 * group_rows, 2 * width),
     )
-    kept_more, out_more = [a + b for a, b in zip(own_more, send(sib_more, 0, 1))]
-    out_more = out_more.astype(bf16)
-
-    kept_one, *one = kernel_call(
-        last_kernel,
-        facts,
-        (last, held, early[0], early[1]),
-        shares(1),
-        sums(group_rows, False),
-        1024 * flops(group_rows, 2 * width),
-    )
+    got_sib = send(sib_more, 0, 1)
+
+    def last_rows(which, rows, base, cost):
+        shape = (1, group_rows, width)
+        return kernel_call(
+            functools.partial(last_kernel, which),
+            facts,
+            (rows, held, base),
+            [(shape, f32), (shape, bf16)],
+            [pltpu.VMEM((group_rows, width), f32)],
+            cost * flops(group_rows, width),
+        )
+
+    to_sib, to_both = last_rows(1, last, early[1], 1024)
+    got, got_sib, to_sib, to_both = lax.optimization_barrier((got, got_sib, to_sib, to_both))
+    kept_more, out_more = [a + b for a, b in zip(own_more, got_sib)]
+    low = (kept + got[1] + (got[0] + got[2])[::-1]).astype(bf16)
+    low, last = lax.optimization_barrier((low, last))
 
     def from_node(value, gap):
         return lax.ppermute(value, "wide", [(w, w ^ (2 * gap)) for w in range(owners)])
 
-    def gather(value, gap, reach):
-        parts = [from_node(value, gap * k) for k in range(1, reach)]
-        return jnp.concatenate([value] + parts, axis=0)
-
-    got, one = lax.optimization_barrier((got, one))
-    low = (kept + got[1] + (got[0] + got[2])[::-1]).astype(bf16)
     gap = 1
     while gap < nodes:
         reach = min(4, nodes // gap)
-        low = gather(low, gap, reach)
+        parts = [from_node(low, gap * k) for k in range(1, reach)]
+        low = jnp.concatenate([low] + parts, axis=0)
         gap *= reach
-    got_more = lax.ppermute(out_more, INNER, SWAP)
-    got_one = to_three(*one)
+    got_more = lax.ppermute(out_more.astype(bf16), INNER, SWAP)
+    kept_one, to_mp = last_rows(0, last, early[0], 1)
+    got_one = to_three(to_sib, to_mp, to_both)
 
     shape = (own_nodes, group_rows, width)
-    rest = kernel_call(
-        functools.partial(delta_kernel, far),
+    delta = kernel_call(
+        delta_kernel,
         facts,
-        (low.reshape(owners * half, rank), spots, mask, copies, second, kept_more, got_more),
+        (low.reshape(owners * half, rank), spots, mask, copies, second),
         [(shape, f32)],
         [],
         2 * here * owners * rank * width,
@@ -514,7 +513,7 @@
     out = kernel_call(
         functools.partial(final_kernel, far),
         facts,
-        (rest, kept_one, *got_one),
+        (delta, kept_more, got_more, kept_one, *got_one),
         [(shape, bf16)],
         [],
         here * width,

time: 109 us -> 110 us (level)
    pallas_call x6 -> x7, Pallas kernels: 20.8 us -> 21.4 us  [kernel_call(): pl.pallas_call(kernel, in_specs=[pl.BlockSpec(memory_space=pltpu.SMEM)] +...]
where the time goes in v17:
time: 110 us; the launch traced here: 109 us
  waiting for transfers between devices  42.9 us (39%)
  starting transfers between devices  27.1 us (25%)
  Pallas kernels  21.4 us (19%)
  other arithmetic  9.12 us (8%)
  local copies, waits for them, and re-layouts  7.39 us (7%)
    ppermute x7, waiting for transfers between devices, turn(): return lax.ppermute(value, 'wide', pairs)  28.9 us
    pallas_call x7, Pallas kernels, kernel_call(): pl.pallas_call(kernel, in_specs=[pl.BlockSpec(memory_space=pltpu.SMEM)] +...  21.4 us
    ppermute x1, waiting for transfers between devices, ringed(): other_second = lax.ppermute(second_factor_table, INNER, SWAP)  10.5 us
    ppermute x7, starting transfers between devices, turn(): return lax.ppermute(value, 'wide', pairs)  8.19 us
    ppermute x7, starting transfers between devices, send(): return lax.ppermute(value, 'wide', moved(shift, cross))  6.69 us
    ppermute x4, starting transfers between devices, from_node(): lax.ppermute(value, 'wide', [(w, w ^ 2 * gap) for w in range(owners)])  5.15 us
    ppermute x4, waiting for transfers between devices, from_node(): lax.ppermute(value, 'wide', [(w, w ^ 2 * gap) for w in range(owners)])  3.46 us
    dynamic_slice x2, local copies, waits for them, and re-layouts, half_of(): return lax.dynamic_slice_in_dim(value, which * depth, depth, axis)  3.42 us
  transfers between devices with their start and end apart: 24, of which 5 were waited for; matrix products, arithmetic and copies ran while one was open for 15% of the time, Pallas kernels for 18%

profile of v17, /device:TPU:0, one launch (start us, length us, event | category | flops | bytes accessed | tf_op | source)
XLA Modules:
  0.0 109.1 jit_solution(5791387822437139979)
XLA Ops:
  0.0 1.4 %fusion.9 = bf16[32,7168]{1,0:T(8,128)(2,1)S(1)} fusion(bf16[32,14336]{1,0:T(8,128)(2,1)} %param.9, s32[]{:T(128)S(6)} %select_n.105, bf16[32,14336]{1,0:T(8,128)(2,1)} %param.8), kind=kLoop, calls=%fused_computation.18 | loop fusion | flops 1835008 | bytes 1376260 | tf_op jit(solution)/shard_map/convert_element_type | solution.py:199
  1.4 0.5 collective-permute-start
  2.0 1.4 %fusion.8 = bf16[32,7168]{1,0:T(8,128)(2,1)S(1)} fusion(bf16[32,14336]{1,0:T(8,128)(2,1)} %param.9, s32[]{:T(128)S(6)} %select_n.106, bf16[32,14336]{1,0:T(8,128)(2,1)} %param.8), kind=kLoop, calls=%fused_computation.17 | loop fusion | flops 1835008 | bytes 1376260 | tf_op jit(solution)/shard_map/convert_element_type | solution.py:199
  3.5 0.4 collective-permute-start.10
  4.0 2.8 %collective-permute-start.3 = (bf16[64,7168]{1,0:T(8,128)(2,1)S(1)}, bf16[64,7168]{1,0:T(8,128)(2,1)S(1)}, u32[]{:S(2)}, u32[]{:S(2)}) collective-permute-start(bf16[64,7168]{1,0:T(8,128)(2,1)S(1)} %pad_maximum_fusion.2.refs_0_), channel_id=1, source_target_pairs={{0,8},{8,16},{16,24},{24,28},{28,20},{20,12},{12,4},{4,0},{2,6},{1... | collective-permute-start | bytes 2752520 | tf_op jit(solution)/shard_map/ppermute | solution.py:307
  6.8 0.1 collective-permute-start.9
  7.0 1.8 %collective-permute-start.1 = (bf16[16,32,512]{2,1,0:T(8,128)(2,1)S(1)}, bf16[16,32,512]{2,1,0:T(8,128)(2,1)}, u32[]{:S(2)}, u32[]{:S(2)}) collective-permute-start(bf16[16,32,512]{2,1,0:T(8,128)(2,1)S(1)} %copy-done.1), channel_id=1, source_target_pairs={{0,1},{1,0},{2,3},{3,2},{4,5},{5,4},{6,7},{7,6},{8,9},{9,8},{10,11... | collective-permute-start | bytes 1572872 | tf_op jit(solution)/shard_map/ppermute | solution.py:330
  8.8 2.2 %constant_dynamic-slice_fusion = bf16[64,7168]{1,0:T(8,128)(2,1)} fusion(bf16[64,14336]{1,0:T(8,128)(2,1)} %bitcast.29, s32[]{:T(128)S(6)} %select_n.124), kind=kLoop, calls=%fused_computation.78 | loop fusion | bytes 1835012 | tf_op jit(solution)/shard_map/dynamic_slice | solution.py:310
  10.9 10.5 %collective-permute-done.1 = bf16[16,32,512]{2,1,0:T(8,128)(2,1)} collective-permute-done((bf16[16,32,512]{2,1,0:T(8,128)(2,1)S(1)}, bf16[16,32,512]{2,1,0:T(8,128)(2,1)}, u32[]{:S(2)}, u32[]{:S(2)}) %collective-permute-start.1) | collective-permute-done | bytes 524320 | tf_op jit(solution)/shard_map/ppermute | solution.py:330
  21.6 0.7 constant_dynamic-slice_fusion.4
  22.3 0.5 convert_reduce_fusion
  23.3 0.9 convolution_convert_fusion
  24.2 4.8 %collective-permute-start.2 = (bf16[8,7168]{1,0:T(8,128)(2,1)}, bf16[8,7168]{1,0:T(8,128)(2,1)}, u32[]{:S(2)}, u32[]{:S(2)}) collective-permute-start(bf16[8,7168]{1,0:T(8,128)(2,1)} %convolution_convert_fusion), channel_id=1, source_target_pairs={{0,28},{2,30},{8,20},{10,22},{16,12},{18,14},{24,4},{26,6},{28,0},... | collective-permute-start | bytes 344072 | tf_op jit(solution)/shard_map/ppermute | solution.py:301
  29.6 0.7 add_convert_fusion.2
  30.3 0.6 add_convert_fusion.1
  31.3 0.7 and_convert_fusion
  32.2 2.0 %collective-permute-start.6 = (bf16[64,7168]{1,0:T(8,128)(2,1)S(1)}, bf16[64,7168]{1,0:T(8,128)(2,1)}, u32[]{:S(2)}, u32[]{:S(2)}) collective-permute-start(bf16[64,7168]{1,0:T(8,128)(2,1)S(1)} %collective-permute-done.5.refs_2_), channel_id=1, source_target_pairs={{0,4},{8,0},{16,8},{24,16},{28,24},{20,28},{12,20},{4,12},{2,10},{... | collective-permute-start | bytes 2752520 | tf_op jit(solution)/shard_map/ppermute | solution.py:307
  34.2 0.2 compare_convert_fusion.mask
  34.5 1.0 reshape.433
  35.4 0.7 copy.11
  36.1 0.8 slice.39.refs_6_
  36.9 0.7 pad_maximum_fusion.3.choices
  37.7 1.3 %pad_maximum_fusion.1.second = bf16[1024,512]{1,0:T(8,128)(2,1)S(1)} fusion(bf16[512,512]{1,0:T(8,128)(2,1)} %bitcast.9, bf16[512,512]{1,0:T(8,128)(2,1)} %bitcast.27), kind=kLoop, calls=%fused_computation.6 | loop fusion | flops 2097152 | bytes 2097152 | tf_op jit(solution)/shard_map/concatenate | solution.py:418
  39.0 15.2 %collective-permute-done.4.refs_3_ = bf16[64,7168]{1,0:T(8,128)(2,1)} collective-permute-done((bf16[64,7168]{1,0:T(8,128)(2,1)S(1)}, bf16[64,7168]{1,0:T(8,128)(2,1)}, u32[]{:S(2)}, u32[]{:S(2)}) %collective-permute-start.4) | collective-permute-done | bytes 917536 | tf_op jit(solution)/shard_map/ppermute | solution.py:307
  54.2 1.1 collective-permute-start.7
  55.3 0.9 collective-permute-start.8
  56.2 1.2 %constant_dynamic-slice_fusion.1 = bf16[64,7168]{1,0:T(8,128)(2,1)S(1)} fusion(bf16[64,14336]{1,0:T(8,128)(2,1)} %collective-permute-done.9, s32[]{:T(128)S(6)} %select_n.124), kind=kLoop, calls=%fused_computation.79 | loop fusion | bytes 1835012 | tf_op jit(solution)/shard_map/dynamic_slice | solution.py:310
  57.6 10.1 %shard_map.82 = (f32[1,64,512]{2,1,0:T(8,128)S(1)}, f32[1,64,512]{2,1,0:T(8,128)S(1)}, f32[4,64,512]{2,1,0:T(8,128)S(1)}, f32[4,64,512]{2,1,0:T(8,128)S(1)}, f32...) custom-call(s32[10]{0:T(128)S(1)} %pad_add_fusion.facts, bf16[64,7168]{1,0:T(8,128)(2,1)S(1)} %pad_maximum_fusion.2.refs_0_, ...), custom_call_target="tpu_custom_call" | custom-call | flops 165150720 | bytes 5160960 | tf_op jit(solution)/shard_map/pallas_call | solution.py:183
  67.7 8.9 %collective-permute-done.7.piece = bf16[64,7168]{1,0:T(8,128)(2,1)S(1)} collective-permute-done((bf16[64,7168]{1,0:T(8,128)(2,1)}, bf16[64,7168]{1,0:T(8,128)(2,1)S(1)}, u32[]{:S(2)}, u32[]{:S(2)}) %collective-permute-start.7) | collective-permute-done | bytes 917536 | tf_op jit(solution)/shard_map/ppermute | solution.py:307
  76.5 1.3 %collective-permute-start.15 = (bf16[64,7168]{1,0:T(8,128)(2,1)S(1)}, bf16[64,7168]{1,0:T(8,128)(2,1)S(1)}, u32[]{:S(2)}, u32[]{:S(2)}) collective-permute-start(bf16[64,7168]{1,0:T(8,128)(2,1)S(1)} %collective-permute-done.7.piece), channel_id=1, source_target_pairs={{0,8},{8,16},{16,24},{24,28},{28,20},{20,12},{12,4},{4,0},{2,6},{1... | collective-permute-start | bytes 2752520 | tf_op jit(solution)/shard_map/ppermute | solution.py:307
  77.9 2.2 %shard_map.83 = (f32[2,16,64]{2,1,0:T(8,128)S(1)}, f32[2,16,64]{2,1,0:T(8,128)S(1)}) custom-call(s32[10]{0:T(128)S(1)} %pad_add_fusion.facts, bf16[64,7168]{1,0:T(8,128)(2,1)S(1)} %collective-permute-done.7.piece, bf16[64,7168]{1,0:T(8,128)(2,1)S(1)} %collective-permute-done.8.other, bf16[8,7168]{1,0:T(8,128)(2,1)} %collective-permute-done.2.far_rows, ...), custom_call_target="tpu_custom_call" | custom-call | flops 7340032 | bytes 229376 | tf_op jit(solution)/shard_map/pallas_call | solution.py:183
  80.1 1.5 %collective-permute-start.12 = (f32[2,16,64]{2,1,0:T(8,128)S(1)}, f32[2,16,64]{2,1,0:T(8,128)S(1)}, u32[]{:S(2)}, u32[]{:S(2)}) collective-permute-start(f32[2,16,64]{2,1,0:T(8,128)S(1)} %get-tuple-element.89), channel_id=1, source_target_pairs={{0,1},{1,0},{2,3},{3,2},{4,5},{5,4},{6,7},{7,6},{8,9},{9,8},{10,11... | collective-permute-start | bytes 24584 | tf_op jit(solution)/shard_map/ppermute | solution.py:317
  81.6 2.6 %shard_map.84 = (f32[2,3,64,512]{3,2,1,0:T(8,128)S(1)}, f32[2,3,64,512]{3,2,1,0:T(8,128)S(1)}) custom-call(s32[10]{0:T(128)S(1)} %pad_add_fusion.facts, bf16[64,7168]{1,0:T(8,128)(2,1)S(1)} %collective-permute-done.7.piece, bf16[64,7168]{1,0:T(8,128)(2,1)S(1)} %collective-permute-done.8.other, bf16[2,7,1024,512]{3,2,1,0:T(8,128)(2,1)S(1)} %get-tuple-element.92.held, ...), custom_call_target="tpu_custom_call" | custom-call | flops 58720256 | bytes 1835008 | tf_op jit(solution)/shard_map/pallas_call | solution.py:183
  84.2 0.7 collective-permute-start.14
  85.0 4.9 %collective-permute-done.15.piece = bf16[64,7168]{1,0:T(8,128)(2,1)S(1)} collective-permute-done((bf16[64,7168]{1,0:T(8,128)(2,1)S(1)}, bf16[64,7168]{1,0:T(8,128)(2,1)S(1)}, u32[]{:S(2)}, u32[]{:S(2)}) %collective-permute-start.15) | collective-permute-done | bytes 917536 | tf_op jit(solution)/shard_map/ppermute | solution.py:307
  89.9 1.9 %shard_map.85 = (f32[1,64,512]{2,1,0:T(8,128)S(1)}, bf16[1,64,512]{2,1,0:T(8,128)(2,1)S(1)}) custom-call(s32[10]{0:T(128)S(1)} %pad_add_fusion.facts, bf16[64,7168]{1,0:T(8,128)(2,1)S(1)} %collective-permute-done.15.piece, bf16[2,7,1024,512]{3,2,1,0:T(8,128)(2,1)S(1)} %get-tuple-element.92.held, f32[1,64,512]{2,1,0:T(8,128)S(1)} %get-tuple-element.96.base), custom_call_target="tpu_custom_call" | custom-call | flops 15032385536 | bytes 469762048 | tf_op jit(solution)/shard_map/pallas_call | solution.py:183
  91.9 1.2 %collective-permute-start.16 = (bf16[2,16,64]{2,1,0:T(8,128)(2,1)S(1)}, bf16[2,16,64]{2,1,0:T(8,128)(2,1)S(1)}, u32[]{:S(2)}, u32[]{:S(2)}) collective-permute-start(bf16[2,16,64]{2,1,0:T(8,128)(2,1)S(1)} %add_convert_fusion.3), channel_id=1, source_target_pairs={{0,4},{2,6},{4,0},{6,2},{8,12},{10,14},{12,8},{14,10},{16,20},{18,... | collective-permute-start | bytes 12296 | tf_op jit(solution)/shard_map/ppermute | solution.py:492
  93.1 1.1 collective-permute-start.17
  94.2 1.3 %collective-permute-start.18 = (bf16[2,16,64]{2,1,0:T(8,128)(2,1)S(1)}, bf16[2,16,64]{2,1,0:T(8,128)(2,1)S(1)}, u32[]{:S(2)}, u32[]{:S(2)}) collective-permute-start(bf16[2,16,64]{2,1,0:T(8,128)(2,1)S(1)} %add_convert_fusion.3), channel_id=1, source_target_pairs={{0,12},{2,14},{4,8},{6,10},{8,4},{10,6},{12,0},{14,2},{16,28},{18,... | collective-permute-start | bytes 12296 | tf_op jit(solution)/shard_map/ppermute | solution.py:492
  95.5 1.9 %shard_map.87 = (f32[1,64,512]{2,1,0:T(8,128)S(1)}, bf16[1,64,512]{2,1,0:T(8,128)(2,1)S(1)}) custom-call(s32[10]{0:T(128)S(1)} %pad_add_fusion.facts, bf16[64,7168]{1,0:T(8,128)(2,1)S(1)} %collective-permute-done.15.piece, bf16[2,7,1024,512]{3,2,1,0:T(8,128)(2,1)S(1)} %get-tuple-element.92.held, f32[1,64,512]{2,1,0:T(8,128)S(1)} %get-tuple-element.110.base), custom_call_target="tpu_custom_call" | custom-call | flops 14680064 | bytes 458752 | tf_op jit(solution)/shard_map/pallas_call | solution.py:183
  97.4 1.6 %collective-permute-start.22 = (bf16[1,64,512]{2,1,0:T(8,128)(2,1)S(1)}, bf16[1,64,512]{2,1,0:T(8,128)(2,1)S(1)}, u32[]{:S(2)}, u32[]{:S(2)}) collective-permute-start(bf16[1,64,512]{2,1,0:T(8,128)(2,1)S(1)} %get-tuple-element.113), channel_id=1, source_target_pairs={{0,1},{1,0},{2,3},{3,2},{4,5},{5,4},{6,7},{7,6},{8,9},{9,8},{10,11... | collective-permute-start | bytes 196616 | tf_op jit(solution)/shard_map/ppermute | solution.py:317
  99.0 0.2 fusion.12
  99.1 0.6 collective-permute-start.20
  99.8 1.6 %collective-permute-start.23 = (bf16[1,64,512]{2,1,0:T(8,128)(2,1)S(1)}, bf16[1,64,512]{2,1,0:T(8,128)(2,1)S(1)}, u32[]{:S(2)}, u32[]{:S(2)}) collective-permute-start(bf16[1,64,512]{2,1,0:T(8,128)(2,1)S(1)} %get-tuple-element.114), channel_id=1, source_target_pairs={{0,3},{1,2},{2,1},{3,0},{4,7},{5,6},{6,5},{7,4},{8,11},{9,10},{10,... | collective-permute-start | bytes 196616 | tf_op jit(solution)/shard_map/ppermute | solution.py:318
  101.4 1.6 %collective-permute-start.19 = (bf16[8,16,64]{2,1,0:T(8,128)(2,1)S(1)}, bf16[8,16,64]{2,1,0:T(8,128)(2,1)S(1)}, u32[]{:S(2)}, u32[]{:S(2)}) collective-permute-start(bf16[8,16,64]{2,1,0:T(8,128)(2,1)S(1)} %pad_maximum_fusion.4), channel_id=1, source_target_pairs={{0,16},{2,18},{4,20},{6,22},{8,24},{10,26},{12,28},{14,30},{16,0},... | collective-permute-start | bytes 49160 | tf_op jit(solution)/shard_map/ppermute | solution.py:492
  103.0 3.5 %collective-permute-done.19 = bf16[8,16,64]{2,1,0:T(8,128)(2,1)S(1)} collective-permute-done((bf16[8,16,64]{2,1,0:T(8,128)(2,1)S(1)}, bf16[8,16,64]{2,1,0:T(8,128)(2,1)S(1)}, u32[]{:S(2)}, u32[]{:S(2)}) %collective-permute-start.19) | collective-permute-done | bytes 16416 | tf_op jit(solution)/shard_map/ppermute | solution.py:492
  106.5 1.3 %shard_map.86.delta = f32[4,64,512]{2,1,0:T(8,128)S(1)} custom-call(s32[10]{0:T(128)S(1)} %pad_add_fusion.facts, bf16[256,64]{1,0:T(8,128)(2,1)S(1)} %bitcast.26, bf16[256,256]{1,0:T(8,128)(2,1)S(1)} %fusion.10.spots, bf16[256,1024]{1,0:T(8,128)(2,1)S(1)} %compare_convert_fusion.mask, bf16[64,1024]{1,0:T(8,128)(2,1)S(1)} %fusion.11.copies, ...), custom_call_target="tpu_custom_call" | custom-call | flops 8388608 | bytes 262144 | tf_op jit(solution)/shard_map/pallas_call | solution.py:183
  107.8 1.3 %shard_map.88 = bf16[4,64,512]{2,1,0:T(8,128)(2,1)} custom-call(s32[10]{0:T(128)S(1)} %pad_add_fusion.facts, f32[4,64,512]{2,1,0:T(8,128)S(1)} %shard_map.86.delta, f32[3,64,512]{2,1,0:T(8,128)S(1)} %get-tuple-element.120.kept_more, bf16[3,64,512]{2,1,0:T(8,128)(2,1)S(1)} %collective-permute-done.20.got_more, f32[1,64,512]{2,1,0:T(8,128)S(1)} %get-tuple-element.111.kept, ...), custom_call_target="tpu_custom_call" | custom-call | flops 4096 | bytes 128 | tf_op jit(solution)/shard_map/pallas_call | solution.py:183
  (76 shorter events, 2.4 us)
Async XLA Ops:
  1.4 5.5 %copy-start.1 = (bf16[16,32,512]{2,1,0:T(8,128)(2,1)S(1)}, bf16[16,32,512]{2,1,0:T(8,128)(2,1)}, u32[]{:S(2)}) copy-start(bf16[16,32,512]{2,1,0:T(8,128)(2,1)} %param.12) | copy-start | bytes 1572868
  1.4 2.0 %collective-permute-start = (bf16[32,7168]{1,0:T(8,128)(2,1)S(1)}, bf16[32,7168]{1,0:T(8,128)(2,1)S(1)}, u32[]{:S(2)}, u32[]{:S(2)}) collective-permute-start(bf16[32,7168]{1,0:T(8,128)(2,1)S(1)} %fusion.9), channel_id=1, source_target_pairs={{0,2},{2,0},{8,10},{10,8},{16,18},{18,16},{24,26},{26,24},{28,30},... | collective-permute-start | bytes 1376264 | tf_op jit(solution)/shard_map/ppermute | solution.py:301
  3.4 18.1 %copy-start.2 = (s32[512,1]{0,1:T(1,128)S(1)}, s32[512,1]{0,1:T(1,128)}, u32[]{:S(2)}) copy-start(s32[512,1]{0,1:T(1,128)} %param.13) | copy-start | bytes 6148
  3.4 18.1 %copy-start.3 = (s32[16]{0:T(128)S(1)}, s32[16]{0:T(128)}, u32[]{:S(2)}) copy-start(s32[16]{0:T(128)} %param.14) | copy-start | bytes 196
  3.5 54.1 %collective-permute-start.10 = (bf16[14336,512]{1,0:T(8,128)(2,1)}, bf16[14336,512]{1,0:T(8,128)(2,1)}, u32[]{:S(2)}, u32[]{:S(2)}) collective-permute-start(bf16[14336,512]{1,0:T(8,128)(2,1)} %refs_7_), channel_id=1, source_target_pairs={{0,2},{2,0},{8,10},{10,8},{16,18},{18,16},{24,26},{26,24},{28,30},... | collective-permute-start | bytes 44040200 | tf_op jit(solution)/shard_map/ppermute | solution.py:301
  4.0 28.1 %collective-permute-start.3 = (bf16[64,7168]{1,0:T(8,128)(2,1)S(1)}, bf16[64,7168]{1,0:T(8,128)(2,1)S(1)}, u32[]{:S(2)}, u32[]{:S(2)}) collective-permute-start(bf16[64,7168]{1,0:T(8,128)(2,1)S(1)} %pad_maximum_fusion.2.refs_0_), channel_id=1, source_target_pairs={{0,8},{8,16},{16,24},{24,28},{28,20},{20,12},{12,4},{4,0},{2,6},{1... | collective-permute-start | bytes 2752520 | tf_op jit(solution)/shard_map/ppermute | solution.py:307
  6.8 25.4 %collective-permute-start.5 = (bf16[64,7168]{1,0:T(8,128)(2,1)S(1)}, bf16[64,7168]{1,0:T(8,128)(2,1)S(1)}, u32[]{:S(2)}, u32[]{:S(2)}) collective-permute-start(bf16[64,7168]{1,0:T(8,128)(2,1)S(1)} %pad_maximum_fusion.2.refs_0_), channel_id=1, source_target_pairs={{0,4},{8,0},{16,8},{24,16},{28,24},{20,28},{12,20},{4,12},{2,10},{... | collective-permute-start | bytes 2752520 | tf_op jit(solution)/shard_map/ppermute | solution.py:307
  6.8 49.4 %collective-permute-start.9 = (bf16[64,14336]{1,0:T(8,128)(2,1)}, bf16[64,14336]{1,0:T(8,128)(2,1)}, u32[]{:S(2)}, u32[]{:S(2)}) collective-permute-start(bf16[64,14336]{1,0:T(8,128)(2,1)} %bitcast.28), channel_id=1, source_target_pairs={{0,2},{2,0},{8,10},{10,8},{16,18},{18,16},{24,26},{26,24},{28,30},... | collective-permute-start | bytes 5505032 | tf_op jit(solution)/shard_map/ppermute | solution.py:301
  7.0 14.5 %collective-permute-start.1 = (bf16[16,32,512]{2,1,0:T(8,128)(2,1)S(1)}, bf16[16,32,512]{2,1,0:T(8,128)(2,1)}, u32[]{:S(2)}, u32[]{:S(2)}) collective-permute-start(bf16[16,32,512]{2,1,0:T(8,128)(2,1)S(1)} %copy-done.1), channel_id=1, source_target_pairs={{0,1},{1,0},{2,3},{3,2},{4,5},{5,4},{6,7},{7,6},{8,9},{9,8},{10,11... | collective-permute-start | bytes 1572872 | tf_op jit(solution)/shard_map/ppermute | solution.py:330
  24.2 13.5 %collective-permute-start.2 = (bf16[8,7168]{1,0:T(8,128)(2,1)}, bf16[8,7168]{1,0:T(8,128)(2,1)}, u32[]{:S(2)}, u32[]{:S(2)}) collective-permute-start(bf16[8,7168]{1,0:T(8,128)(2,1)} %convolution_convert_fusion), channel_id=1, source_target_pairs={{0,28},{2,30},{8,20},{10,22},{16,12},{18,14},{24,4},{26,6},{28,0},... | collective-permute-start | bytes 344072 | tf_op jit(solution)/shard_map/ppermute | solution.py:301
  32.1 22.1 %collective-permute-start.4 = (bf16[64,7168]{1,0:T(8,128)(2,1)S(1)}, bf16[64,7168]{1,0:T(8,128)(2,1)}, u32[]{:S(2)}, u32[]{:S(2)}) collective-permute-start(bf16[64,7168]{1,0:T(8,128)(2,1)S(1)} %collective-permute-done.3.refs_1_), channel_id=1, source_target_pairs={{0,8},{8,16},{16,24},{24,28},{28,20},{20,12},{12,4},{4,0},{2,6},{1... | collective-permute-start | bytes 2752520 | tf_op jit(solution)/shard_map/ppermute | solution.py:307
  32.2 22.0 %collective-permute-start.6 = (bf16[64,7168]{1,0:T(8,128)(2,1)S(1)}, bf16[64,7168]{1,0:T(8,128)(2,1)}, u32[]{:S(2)}, u32[]{:S(2)}) collective-permute-start(bf16[64,7168]{1,0:T(8,128)(2,1)S(1)} %collective-permute-done.5.refs_2_), channel_id=1, source_target_pairs={{0,4},{8,0},{16,8},{24,16},{28,24},{20,28},{12,20},{4,12},{2,10},{... | collective-permute-start | bytes 2752520 | tf_op jit(solution)/shard_map/ppermute | solution.py:307
  37.7 19.8 %copy-start = (bf16[64,7168]{1,0:T(8,128)(2,1)S(1)}, bf16[64,7168]{1,0:T(8,128)(2,1)}, u32[]{:S(2)}) copy-start(bf16[64,7168]{1,0:T(8,128)(2,1)} %constant_dynamic-slice_fusion) | copy-start | bytes 2752516
  54.2 22.4 %collective-permute-start.7 = (bf16[64,7168]{1,0:T(8,128)(2,1)}, bf16[64,7168]{1,0:T(8,128)(2,1)S(1)}, u32[]{:S(2)}, u32[]{:S(2)}) collective-permute-start(bf16[64,7168]{1,0:T(8,128)(2,1)} %collective-permute-done.4.refs_3_), channel_id=1, source_target_pairs={{0,8},{8,16},{16,24},{24,28},{28,20},{20,12},{12,4},{4,0},{2,6},{1... | collective-permute-start | bytes 2752520 | tf_op jit(solution)/shard_map/ppermute | solution.py:307
  55.3 21.3 %collective-permute-start.8 = (bf16[64,7168]{1,0:T(8,128)(2,1)}, bf16[64,7168]{1,0:T(8,128)(2,1)S(1)}, u32[]{:S(2)}, u32[]{:S(2)}) collective-permute-start(bf16[64,7168]{1,0:T(8,128)(2,1)} %collective-permute-done.6.refs_4_), channel_id=1, source_target_pairs={{0,4},{8,0},{16,8},{24,16},{28,24},{20,28},{12,20},{4,12},{2,10},{... | collective-permute-start | bytes 2752520 | tf_op jit(solution)/shard_map/ppermute | solution.py:307
  76.5 13.4 %collective-permute-start.15 = (bf16[64,7168]{1,0:T(8,128)(2,1)S(1)}, bf16[64,7168]{1,0:T(8,128)(2,1)S(1)}, u32[]{:S(2)}, u32[]{:S(2)}) collective-permute-start(bf16[64,7168]{1,0:T(8,128)(2,1)S(1)} %collective-permute-done.7.piece), channel_id=1, source_target_pairs={{0,8},{8,16},{16,24},{24,28},{28,20},{20,12},{12,4},{4,0},{2,6},{1... | collective-permute-start | bytes 2752520 | tf_op jit(solution)/shard_map/ppermute | solution.py:307
  80.1 11.8 %collective-permute-start.12 = (f32[2,16,64]{2,1,0:T(8,128)S(1)}, f32[2,16,64]{2,1,0:T(8,128)S(1)}, u32[]{:S(2)}, u32[]{:S(2)}) collective-permute-start(f32[2,16,64]{2,1,0:T(8,128)S(1)} %get-tuple-element.89), channel_id=1, source_target_pairs={{0,1},{1,0},{2,3},{3,2},{4,5},{5,4},{6,7},{7,6},{8,9},{9,8},{10,11... | collective-permute-start | bytes 24584 | tf_op jit(solution)/shard_map/ppermute | solution.py:317
  81.6 10.3 %collective-permute-start.13 = (f32[2,16,64]{2,1,0:T(8,128)S(1)}, f32[2,16,64]{2,1,0:T(8,128)S(1)}, u32[]{:S(2)}, u32[]{:S(2)}) collective-permute-start(f32[2,16,64]{2,1,0:T(8,128)S(1)} %get-tuple-element.89), channel_id=1, source_target_pairs={{0,3},{1,2},{2,1},{3,0},{4,7},{5,6},{6,5},{7,4},{8,11},{9,10},{10,... | collective-permute-start | bytes 24584 | tf_op jit(solution)/shard_map/ppermute | solution.py:318
  84.2 7.7 %collective-permute-start.14 = (f32[2,3,64,512]{3,2,1,0:T(8,128)S(1)}, f32[2,3,64,512]{3,2,1,0:T(8,128)S(1)}, u32[]{:S(2)}, u32[]{:S(2)}) collective-permute-start(f32[2,3,64,512]{3,2,1,0:T(8,128)S(1)} %get-tuple-element.95), channel_id=1, source_target_pairs={{0,2},{2,0},{8,10},{10,8},{16,18},{18,16},{24,26},{26,24},{28,30},... | collective-permute-start | bytes 2359304 | tf_op jit(solution)/shard_map/ppermute | solution.py:301
  85.0 6.9 %collective-permute-start.11 = (f32[2,16,64]{2,1,0:T(8,128)S(1)}, f32[2,16,64]{2,1,0:T(8,128)S(1)}, u32[]{:S(2)}, u32[]{:S(2)}) collective-permute-start(f32[2,16,64]{2,1,0:T(8,128)S(1)} %get-tuple-element.88), channel_id=1, source_target_pairs={{0,2},{2,0},{8,10},{10,8},{16,18},{18,16},{24,26},{26,24},{28,30},... | collective-permute-start | bytes 24584 | tf_op jit(solution)/shard_map/ppermute | solution.py:301
  91.9 7.8 %collective-permute-start.16 = (bf16[2,16,64]{2,1,0:T(8,128)(2,1)S(1)}, bf16[2,16,64]{2,1,0:T(8,128)(2,1)S(1)}, u32[]{:S(2)}, u32[]{:S(2)}) collective-permute-start(bf16[2,16,64]{2,1,0:T(8,128)(2,1)S(1)} %add_convert_fusion.3), channel_id=1, source_target_pairs={{0,4},{2,6},{4,0},{6,2},{8,12},{10,14},{12,8},{14,10},{16,20},{18,... | collective-permute-start | bytes 12296 | tf_op jit(solution)/shard_map/ppermute | solution.py:492
  93.1 6.6 %collective-permute-start.17 = (bf16[2,16,64]{2,1,0:T(8,128)(2,1)S(1)}, bf16[2,16,64]{2,1,0:T(8,128)(2,1)S(1)}, u32[]{:S(2)}, u32[]{:S(2)}) collective-permute-start(bf16[2,16,64]{2,1,0:T(8,128)(2,1)S(1)} %add_convert_fusion.3), channel_id=1, source_target_pairs={{0,8},{2,10},{4,12},{6,14},{8,0},{10,2},{12,4},{14,6},{16,24},{18,... | collective-permute-start | bytes 12296 | tf_op jit(solution)/shard_map/ppermute | solution.py:492
  94.2 7.2 %collective-permute-start.18 = (bf16[2,16,64]{2,1,0:T(8,128)(2,1)S(1)}, bf16[2,16,64]{2,1,0:T(8,128)(2,1)S(1)}, u32[]{:S(2)}, u32[]{:S(2)}) collective-permute-start(bf16[2,16,64]{2,1,0:T(8,128)(2,1)S(1)} %add_convert_fusion.3), channel_id=1, source_target_pairs={{0,12},{2,14},{4,8},{6,10},{8,4},{10,6},{12,0},{14,2},{16,28},{18,... | collective-permute-start | bytes 12296 | tf_op jit(solution)/shard_map/ppermute | solution.py:492
  97.4 10.3 %collective-permute-start.22 = (bf16[1,64,512]{2,1,0:T(8,128)(2,1)S(1)}, bf16[1,64,512]{2,1,0:T(8,128)(2,1)S(1)}, u32[]{:S(2)}, u32[]{:S(2)}) collective-permute-start(bf16[1,64,512]{2,1,0:T(8,128)(2,1)S(1)} %get-tuple-element.113), channel_id=1, source_target_pairs={{0,1},{1,0},{2,3},{3,2},{4,5},{5,4},{6,7},{7,6},{8,9},{9,8},{10,11... | collective-permute-start | bytes 196616 | tf_op jit(solution)/shard_map/ppermute | solution.py:317
  99.1 8.7 %collective-permute-start.20 = (bf16[3,64,512]{2,1,0:T(8,128)(2,1)S(1)}, bf16[3,64,512]{2,1,0:T(8,128)(2,1)S(1)}, u32[]{:S(2)}, u32[]{:S(2)}) collective-permute-start(bf16[3,64,512]{2,1,0:T(8,128)(2,1)S(1)} %get-tuple-element.119), channel_id=1, source_target_pairs={{0,1},{1,0},{2,3},{3,2},{4,5},{5,4},{6,7},{7,6},{8,9},{9,8},{10,11... | collective-permute-start | bytes 589832 | tf_op jit(solution)/shard_map/ppermute | solution.py:500
  99.7 8.0 %collective-permute-start.21 = (f32[1,64,512]{2,1,0:T(8,128)S(1)}, f32[1,64,512]{2,1,0:T(8,128)S(1)}, u32[]{:S(2)}, u32[]{:S(2)}) collective-permute-start(f32[1,64,512]{2,1,0:T(8,128)S(1)} %get-tuple-element.112), channel_id=1, source_target_pairs={{0,2},{2,0},{8,10},{10,8},{16,18},{18,16},{24,26},{26,24},{28,30},... | collective-permute-start | bytes 393224 | tf_op jit(solution)/shard_map/ppermute | solution.py:301
  99.8 8.0 %collective-permute-start.23 = (bf16[1,64,512]{2,1,0:T(8,128)(2,1)S(1)}, bf16[1,64,512]{2,1,0:T(8,128)(2,1)S(1)}, u32[]{:S(2)}, u32[]{:S(2)}) collective-permute-start(bf16[1,64,512]{2,1,0:T(8,128)(2,1)S(1)} %get-tuple-element.114), channel_id=1, source_target_pairs={{0,3},{1,2},{2,1},{3,0},{4,7},{5,6},{6,5},{7,4},{8,11},{9,10},{10,... | collective-permute-start | bytes 196616 | tf_op jit(solution)/shard_map/ppermute | solution.py:318
  101.4 5.1 %collective-permute-start.19 = (bf16[8,16,64]{2,1,0:T(8,128)(2,1)S(1)}, bf16[8,16,64]{2,1,0:T(8,128)(2,1)S(1)}, u32[]{:S(2)}, u32[]{:S(2)}) collective-permute-start(bf16[8,16,64]{2,1,0:T(8,128)(2,1)S(1)} %pad_maximum_fusion.4), channel_id=1, source_target_pairs={{0,16},{2,18},{4,20},{6,22},{8,24},{10,26},{12,28},{14,30},{16,0},... | collective-permute-start | bytes 49160 | tf_op jit(solution)/shard_map/ppermute | solution.py:492

commit v18 on v17

--- a/solution.py
+++ b/solution.py
@@ -491,12 +491,15 @@
     def from_node(value, gap):
         return lax.ppermute(value, "wide", [(w, w ^ (2 * gap)) for w in range(owners)])
 
-    gap = 1
-    while gap < nodes:
-        reach = min(4, nodes // gap)
-        parts = [from_node(low, gap * k) for k in range(1, reach)]
-        low = jnp.concatenate([low] + parts, axis=0)
-        gap *= reach
+    def gather(value, gap, reach):
+        parts = [from_node(value, gap * k) for k in range(1, reach)]
+        return jnp.concatenate([value] + parts, axis=0)
+
+    reach = min(4, nodes)
+    low, to_sib = lax.optimization_barrier((gather(low, 1, reach), to_sib))
+    while reach < nodes:
+        low = gather(low, reach, 2)
+        reach *= 2
     got_more = lax.ppermute(out_more.astype(bf16), INNER, SWAP)
     kept_one, to_mp = last_rows(0, last, early[0], 1)
     got_one = to_three(to_sib, to_mp, to_both)

time: 110 us -> 110 us (level)
    ppermute x4, waiting for transfers between devices: 3.46 us -> 1.53 us  [from_node(): lax.ppermute(value, 'wide', [(w, w ^ 2 * gap) for w in range(owners)])]
    ppermute x2, waiting for transfers between devices: 0.01 us -> 1.36 us  [to_three(): lax.ppermute(to_mp, INNER, SWAP)]
    ppermute x2, starting transfers between devices: 1.6 us -> 0.37 us  [to_three(): lax.ppermute(to_both, ('wide',) + INNER, crossed)]
  transfers between devices with their start and end apart: 24 -> 24, of which waited for: 5 -> 7; matrix products, arithmetic and copies ran while one was open for 15% -> 14% of each run, Pallas kernels for 18% -> 18%
where the time goes in v18:
time: 110 us; the launch traced here: 109 us
  waiting for transfers between devices  43.4 us (39%)
  starting transfers between devices  27 us (25%)
  Pallas kernels  21.4 us (19%)
  other arithmetic  9.13 us (8%)
  local copies, waits for them, and re-layouts  7.35 us (7%)
    ppermute x7, waiting for transfers between devices, turn(): return lax.ppermute(value, 'wide', pairs)  28.9 us
    pallas_call x7, Pallas kernels, kernel_call(): pl.pallas_call(kernel, in_specs=[pl.BlockSpec(memory_space=pltpu.SMEM)] +...  21.4 us
    ppermute x1, waiting for transfers between devices, ringed(): other_second = lax.ppermute(second_factor_table, INNER, SWAP)  10.5 us
    ppermute x7, starting transfers between devices, turn(): return lax.ppermute(value, 'wide', pairs)  8.19 us
    ppermute x7, starting transfers between devices, send(): return lax.ppermute(value, 'wide', moved(shift, cross))  6.69 us
    ppermute x4, starting transfers between devices, from_node(): lax.ppermute(value, 'wide', [(w, w ^ 2 * gap) for w in range(owners)])  5.32 us
    dynamic_slice x2, local copies, waits for them, and re-layouts, half_of(): return lax.dynamic_slice_in_dim(value, which * depth, depth, axis)  3.42 us
    ppermute x2, starting transfers between devices, to_three(): lax.ppermute(to_mp, INNER, SWAP)  3.06 us
  transfers between devices with their start and end apart: 24, of which 7 were waited for; matrix products, arithmetic and copies ran while one was open for 14% of the time, Pallas kernels for 18%

profile of v18, /device:TPU:0, one launch (start us, length us, event | category | flops | bytes accessed | tf_op | source)
XLA Modules:
  0.0 109.5 jit_solution(9616689481154159042)
XLA Ops:
  0.0 1.4 %fusion.9 = bf16[32,7168]{1,0:T(8,128)(2,1)S(1)} fusion(bf16[32,14336]{1,0:T(8,128)(2,1)} %param.9, s32[]{:T(128)S(6)} %select_n.105, bf16[32,14336]{1,0:T(8,128)(2,1)} %param.8), kind=kLoop, calls=%fused_computation.18 | loop fusion | flops 1835008 | bytes 1376260 | tf_op jit(solution)/shard_map/convert_element_type | solution.py:199
  1.4 0.5 collective-permute-start
  2.0 1.4 %fusion.8 = bf16[32,7168]{1,0:T(8,128)(2,1)S(1)} fusion(bf16[32,14336]{1,0:T(8,128)(2,1)} %param.9, s32[]{:T(128)S(6)} %select_n.106, bf16[32,14336]{1,0:T(8,128)(2,1)} %param.8), kind=kLoop, calls=%fused_computation.17 | loop fusion | flops 1835008 | bytes 1376260 | tf_op jit(solution)/shard_map/convert_element_type | solution.py:199
  3.5 0.4 collective-permute-start.10
  4.0 2.8 %collective-permute-start.3 = (bf16[64,7168]{1,0:T(8,128)(2,1)S(1)}, bf16[64,7168]{1,0:T(8,128)(2,1)S(1)}, u32[]{:S(2)}, u32[]{:S(2)}) collective-permute-start(bf16[64,7168]{1,0:T(8,128)(2,1)S(1)} %pad_maximum_fusion.2.refs_0_), channel_id=1, source_target_pairs={{0,8},{8,16},{16,24},{24,28},{28,20},{20,12},{12,4},{4,0},{2,6},{1... | collective-permute-start | bytes 2752520 | tf_op jit(solution)/shard_map/ppermute | solution.py:307
  7.0 1.8 %collective-permute-start.1 = (bf16[16,32,512]{2,1,0:T(8,128)(2,1)S(1)}, bf16[16,32,512]{2,1,0:T(8,128)(2,1)}, u32[]{:S(2)}, u32[]{:S(2)}) collective-permute-start(bf16[16,32,512]{2,1,0:T(8,128)(2,1)S(1)} %copy-done.1), channel_id=1, source_target_pairs={{0,1},{1,0},{2,3},{3,2},{4,5},{5,4},{6,7},{7,6},{8,9},{9,8},{10,11... | collective-permute-start | bytes 1572872 | tf_op jit(solution)/shard_map/ppermute | solution.py:330
  8.8 2.2 %constant_dynamic-slice_fusion = bf16[64,7168]{1,0:T(8,128)(2,1)} fusion(bf16[64,14336]{1,0:T(8,128)(2,1)} %bitcast.29, s32[]{:T(128)S(6)} %select_n.124), kind=kLoop, calls=%fused_computation.74 | loop fusion | bytes 1835012 | tf_op jit(solution)/shard_map/dynamic_slice | solution.py:310
  10.9 10.5 %collective-permute-done.1 = bf16[16,32,512]{2,1,0:T(8,128)(2,1)} collective-permute-done((bf16[16,32,512]{2,1,0:T(8,128)(2,1)S(1)}, bf16[16,32,512]{2,1,0:T(8,128)(2,1)}, u32[]{:S(2)}, u32[]{:S(2)}) %collective-permute-start.1) | collective-permute-done | bytes 524320 | tf_op jit(solution)/shard_map/ppermute | solution.py:330
  21.6 0.7 constant_dynamic-slice_fusion.4
  22.3 0.5 convert_reduce_fusion
  23.3 0.9 convolution_convert_fusion
  24.2 4.8 %collective-permute-start.2 = (bf16[8,7168]{1,0:T(8,128)(2,1)}, bf16[8,7168]{1,0:T(8,128)(2,1)}, u32[]{:S(2)}, u32[]{:S(2)}) collective-permute-start(bf16[8,7168]{1,0:T(8,128)(2,1)} %convolution_convert_fusion), channel_id=1, source_target_pairs={{0,28},{2,30},{8,20},{10,22},{16,12},{18,14},{24,4},{26,6},{28,0},... | collective-permute-start | bytes 344072 | tf_op jit(solution)/shard_map/ppermute | solution.py:301
  29.6 0.7 add_convert_fusion.2
  30.3 0.6 add_convert_fusion.1
  31.3 0.7 and_convert_fusion
  32.2 2.0 %collective-permute-start.6 = (bf16[64,7168]{1,0:T(8,128)(2,1)S(1)}, bf16[64,7168]{1,0:T(8,128)(2,1)}, u32[]{:S(2)}, u32[]{:S(2)}) collective-permute-start(bf16[64,7168]{1,0:T(8,128)(2,1)S(1)} %collective-permute-done.5.refs_2_), channel_id=1, source_target_pairs={{0,4},{8,0},{16,8},{24,16},{28,24},{20,28},{12,20},{4,12},{2,10},{... | collective-permute-start | bytes 2752520 | tf_op jit(solution)/shard_map/ppermute | solution.py:307
  34.5 1.0 reshape.433
  35.4 0.7 copy.11
  36.1 0.8 slice.39.refs_6_
  36.9 0.7 pad_maximum_fusion.4.choices
  37.7 1.3 %pad_maximum_fusion.1.second = bf16[1024,512]{1,0:T(8,128)(2,1)S(1)} fusion(bf16[512,512]{1,0:T(8,128)(2,1)} %bitcast.9, bf16[512,512]{1,0:T(8,128)(2,1)} %bitcast.27), kind=kLoop, calls=%fused_computation.6 | loop fusion | flops 2097152 | bytes 2097152 | tf_op jit(solution)/shard_map/concatenate | solution.py:418
  39.0 15.2 %collective-permute-done.4.refs_3_ = bf16[64,7168]{1,0:T(8,128)(2,1)} collective-permute-done((bf16[64,7168]{1,0:T(8,128)(2,1)S(1)}, bf16[64,7168]{1,0:T(8,128)(2,1)}, u32[]{:S(2)}, u32[]{:S(2)}) %collective-permute-start.4) | collective-permute-done | bytes 917536 | tf_op jit(solution)/shard_map/ppermute | solution.py:307
  54.2 1.1 collective-permute-start.7
  55.3 0.9 collective-permute-start.8
  56.2 1.2 %constant_dynamic-slice_fusion.1 = bf16[64,7168]{1,0:T(8,128)(2,1)S(1)} fusion(bf16[64,14336]{1,0:T(8,128)(2,1)} %collective-permute-done.9, s32[]{:T(128)S(6)} %select_n.124), kind=kLoop, calls=%fused_computation.75 | loop fusion | bytes 1835012 | tf_op jit(solution)/shard_map/dynamic_slice | solution.py:310
  57.6 10.1 %shard_map.82 = (f32[1,64,512]{2,1,0:T(8,128)S(1)}, f32[1,64,512]{2,1,0:T(8,128)S(1)}, f32[4,64,512]{2,1,0:T(8,128)S(1)}, f32[4,64,512]{2,1,0:T(8,128)S(1)}, f32...) custom-call(s32[10]{0:T(128)S(1)} %pad_add_fusion.facts, bf16[64,7168]{1,0:T(8,128)(2,1)S(1)} %pad_maximum_fusion.2.refs_0_, ...), custom_call_target="tpu_custom_call" | custom-call | flops 165150720 | bytes 5160960 | tf_op jit(solution)/shard_map/pallas_call | solution.py:183
  67.7 8.9 %collective-permute-done.7.piece = bf16[64,7168]{1,0:T(8,128)(2,1)S(1)} collective-permute-done((bf16[64,7168]{1,0:T(8,128)(2,1)}, bf16[64,7168]{1,0:T(8,128)(2,1)S(1)}, u32[]{:S(2)}, u32[]{:S(2)}) %collective-permute-start.7) | collective-permute-done | bytes 917536 | tf_op jit(solution)/shard_map/ppermute | solution.py:307
  76.5 1.3 %collective-permute-start.15 = (bf16[64,7168]{1,0:T(8,128)(2,1)S(1)}, bf16[64,7168]{1,0:T(8,128)(2,1)S(1)}, u32[]{:S(2)}, u32[]{:S(2)}) collective-permute-start(bf16[64,7168]{1,0:T(8,128)(2,1)S(1)} %collective-permute-done.7.piece), channel_id=1, source_target_pairs={{0,8},{8,16},{16,24},{24,28},{28,20},{20,12},{12,4},{4,0},{2,6},{1... | collective-permute-start | bytes 2752520 | tf_op jit(solution)/shard_map/ppermute | solution.py:307
  77.9 2.2 %shard_map.83 = (f32[2,16,64]{2,1,0:T(8,128)S(1)}, f32[2,16,64]{2,1,0:T(8,128)S(1)}) custom-call(s32[10]{0:T(128)S(1)} %pad_add_fusion.facts, bf16[64,7168]{1,0:T(8,128)(2,1)S(1)} %collective-permute-done.7.piece, bf16[64,7168]{1,0:T(8,128)(2,1)S(1)} %collective-permute-done.8.other, bf16[8,7168]{1,0:T(8,128)(2,1)} %collective-permute-done.2.far_rows, ...), custom_call_target="tpu_custom_call" | custom-call | flops 7340032 | bytes 229376 | tf_op jit(solution)/shard_map/pallas_call | solution.py:183
  80.1 1.5 %collective-permute-start.12 = (f32[2,16,64]{2,1,0:T(8,128)S(1)}, f32[2,16,64]{2,1,0:T(8,128)S(1)}, u32[]{:S(2)}, u32[]{:S(2)}) collective-permute-start(f32[2,16,64]{2,1,0:T(8,128)S(1)} %get-tuple-element.91), channel_id=1, source_target_pairs={{0,1},{1,0},{2,3},{3,2},{4,5},{5,4},{6,7},{7,6},{8,9},{9,8},{10,11... | collective-permute-start | bytes 24584 | tf_op jit(solution)/shard_map/ppermute | solution.py:317
  81.6 2.6 %shard_map.84 = (f32[2,3,64,512]{3,2,1,0:T(8,128)S(1)}, f32[2,3,64,512]{3,2,1,0:T(8,128)S(1)}) custom-call(s32[10]{0:T(128)S(1)} %pad_add_fusion.facts, bf16[64,7168]{1,0:T(8,128)(2,1)S(1)} %collective-permute-done.7.piece, bf16[64,7168]{1,0:T(8,128)(2,1)S(1)} %collective-permute-done.8.other, bf16[2,7,1024,512]{3,2,1,0:T(8,128)(2,1)S(1)} %get-tuple-element.94.held, ...), custom_call_target="tpu_custom_call" | custom-call | flops 58720256 | bytes 1835008 | tf_op jit(solution)/shard_map/pallas_call | solution.py:183
  84.2 0.7 collective-permute-start.14
  85.0 4.9 %collective-permute-done.15.piece = bf16[64,7168]{1,0:T(8,128)(2,1)S(1)} collective-permute-done((bf16[64,7168]{1,0:T(8,128)(2,1)S(1)}, bf16[64,7168]{1,0:T(8,128)(2,1)S(1)}, u32[]{:S(2)}, u32[]{:S(2)}) %collective-permute-start.15) | collective-permute-done | bytes 917536 | tf_op jit(solution)/shard_map/ppermute | solution.py:307
  89.9 1.9 %shard_map.85 = (f32[1,64,512]{2,1,0:T(8,128)S(1)}, bf16[1,64,512]{2,1,0:T(8,128)(2,1)S(1)}) custom-call(s32[10]{0:T(128)S(1)} %pad_add_fusion.facts, bf16[64,7168]{1,0:T(8,128)(2,1)S(1)} %collective-permute-done.15.piece, bf16[2,7,1024,512]{3,2,1,0:T(8,128)(2,1)S(1)} %get-tuple-element.94.held, f32[1,64,512]{2,1,0:T(8,128)S(1)} %get-tuple-element.98.base), custom_call_target="tpu_custom_call" | custom-call | flops 15032385536 | bytes 469762048 | tf_op jit(solution)/shard_map/pallas_call | solution.py:183
  91.9 1.2 %collective-permute-start.16 = (bf16[2,16,64]{2,1,0:T(8,128)(2,1)S(1)}, bf16[2,16,64]{2,1,0:T(8,128)(2,1)S(1)}, u32[]{:S(2)}, u32[]{:S(2)}) collective-permute-start(bf16[2,16,64]{2,1,0:T(8,128)(2,1)S(1)} %add_convert_fusion.3), channel_id=1, source_target_pairs={{0,4},{2,6},{4,0},{6,2},{8,12},{10,14},{12,8},{14,10},{16,20},{18,... | collective-permute-start | bytes 12296 | tf_op jit(solution)/shard_map/ppermute | solution.py:492
  93.1 1.1 collective-permute-start.17
  94.2 1.3 %collective-permute-start.18 = (bf16[2,16,64]{2,1,0:T(8,128)(2,1)S(1)}, bf16[2,16,64]{2,1,0:T(8,128)(2,1)S(1)}, u32[]{:S(2)}, u32[]{:S(2)}) collective-permute-start(bf16[2,16,64]{2,1,0:T(8,128)(2,1)S(1)} %add_convert_fusion.3), channel_id=1, source_target_pairs={{0,12},{2,14},{4,8},{6,10},{8,4},{10,6},{12,0},{14,2},{16,28},{18,... | collective-permute-start | bytes 12296 | tf_op jit(solution)/shard_map/ppermute | solution.py:492
  95.5 0.2 fusion.12
  95.7 1.6 %collective-permute-start.20 = (bf16[3,64,512]{2,1,0:T(8,128)(2,1)S(1)}, bf16[3,64,512]{2,1,0:T(8,128)(2,1)S(1)}, u32[]{:S(2)}, u32[]{:S(2)}) collective-permute-start(bf16[3,64,512]{2,1,0:T(8,128)(2,1)S(1)} %get-tuple-element.123), channel_id=1, source_target_pairs={{0,1},{1,0},{2,3},{3,2},{4,5},{5,4},{6,7},{7,6},{8,9},{9,8},{10,11... | collective-permute-start | bytes 589832 | tf_op jit(solution)/shard_map/ppermute | solution.py:503
  97.2 1.5 %collective-permute-done.18 = bf16[2,16,64]{2,1,0:T(8,128)(2,1)S(1)} collective-permute-done((bf16[2,16,64]{2,1,0:T(8,128)(2,1)S(1)}, bf16[2,16,64]{2,1,0:T(8,128)(2,1)S(1)}, u32[]{:S(2)}, u32[]{:S(2)}) %collective-permute-start.18) | collective-permute-done | bytes 4128 | tf_op jit(solution)/shard_map/ppermute | solution.py:492
  98.8 1.8 %collective-permute-start.19 = (bf16[8,16,64]{2,1,0:T(8,128)(2,1)S(1)}, bf16[8,16,64]{2,1,0:T(8,128)(2,1)S(1)}, u32[]{:S(2)}, u32[]{:S(2)}) collective-permute-start(bf16[8,16,64]{2,1,0:T(8,128)(2,1)S(1)} %pad_maximum_fusion.5), channel_id=1, source_target_pairs={{0,16},{2,18},{4,20},{6,22},{8,24},{10,26},{12,28},{14,30},{16,0},... | collective-permute-start | bytes 49160 | tf_op jit(solution)/shard_map/ppermute | solution.py:492
  100.5 1.9 %shard_map.87 = (f32[1,64,512]{2,1,0:T(8,128)S(1)}, bf16[1,64,512]{2,1,0:T(8,128)(2,1)S(1)}) custom-call(s32[10]{0:T(128)S(1)} %pad_add_fusion.facts, bf16[64,7168]{1,0:T(8,128)(2,1)S(1)} %collective-permute-done.15.piece, bf16[2,7,1024,512]{3,2,1,0:T(8,128)(2,1)S(1)} %get-tuple-element.94.held, f32[1,64,512]{2,1,0:T(8,128)S(1)} %get-tuple-element.114.base), custom_call_target="tpu_custom_call" | custom-call | flops 14680064 | bytes 458752 | tf_op jit(solution)/shard_map/pallas_call | solution.py:183
  102.5 1.6 %collective-permute-start.22 = (bf16[1,64,512]{2,1,0:T(8,128)(2,1)S(1)}, bf16[1,64,512]{2,1,0:T(8,128)(2,1)S(1)}, u32[]{:S(2)}, u32[]{:S(2)}) collective-permute-start(bf16[1,64,512]{2,1,0:T(8,128)(2,1)S(1)} %get-tuple-element.117), channel_id=1, source_target_pairs={{0,1},{1,0},{2,3},{3,2},{4,5},{5,4},{6,7},{7,6},{8,9},{9,8},{10,11... | collective-permute-start | bytes 196616 | tf_op jit(solution)/shard_map/ppermute | solution.py:317
  104.0 0.4 collective-permute-start.23
  104.4 1.3 %shard_map.86.delta = f32[4,64,512]{2,1,0:T(8,128)S(1)} custom-call(s32[10]{0:T(128)S(1)} %pad_add_fusion.facts, bf16[256,64]{1,0:T(8,128)(2,1)S(1)} %bitcast.26, bf16[256,256]{1,0:T(8,128)(2,1)S(1)} %fusion.10.spots, bf16[256,1024]{1,0:T(8,128)(2,1)S(1)} %compare_convert_fusion.mask, bf16[64,1024]{1,0:T(8,128)(2,1)S(1)} %fusion.11.copies, ...), custom_call_target="tpu_custom_call" | custom-call | flops 8388608 | bytes 262144 | tf_op jit(solution)/shard_map/pallas_call | solution.py:183
  105.7 1.4 %collective-permute-done.22.got_mp = bf16[1,64,512]{2,1,0:T(8,128)(2,1)S(1)} collective-permute-done((bf16[1,64,512]{2,1,0:T(8,128)(2,1)S(1)}, bf16[1,64,512]{2,1,0:T(8,128)(2,1)S(1)}, u32[]{:S(2)}, u32[]{:S(2)}) %collective-permute-start.22) | collective-permute-done | bytes 65568 | tf_op jit(solution)/shard_map/ppermute | solution.py:317
  107.1 1.1 collective-permute-done.23.got_both
  108.1 1.3 %shard_map.88 = bf16[4,64,512]{2,1,0:T(8,128)(2,1)} custom-call(s32[10]{0:T(128)S(1)} %pad_add_fusion.facts, f32[4,64,512]{2,1,0:T(8,128)S(1)} %shard_map.86.delta, f32[3,64,512]{2,1,0:T(8,128)S(1)} %get-tuple-element.124.kept_more, bf16[3,64,512]{2,1,0:T(8,128)(2,1)S(1)} %collective-permute-done.20.got_more, f32[1,64,512]{2,1,0:T(8,128)S(1)} %get-tuple-element.115.kept, ...), custom_call_target="tpu_custom_call" | custom-call | flops 4096 | bytes 128 | tf_op jit(solution)/shard_map/pallas_call | solution.py:183
  (72 shorter events, 2.7 us)
Async XLA Ops:
  1.4 5.5 %copy-start.1 = (bf16[16,32,512]{2,1,0:T(8,128)(2,1)S(1)}, bf16[16,32,512]{2,1,0:T(8,128)(2,1)}, u32[]{:S(2)}) copy-start(bf16[16,32,512]{2,1,0:T(8,128)(2,1)} %param.12) | copy-start | bytes 1572868
  1.4 2.0 %collective-permute-start = (bf16[32,7168]{1,0:T(8,128)(2,1)S(1)}, bf16[32,7168]{1,0:T(8,128)(2,1)S(1)}, u32[]{:S(2)}, u32[]{:S(2)}) collective-permute-start(bf16[32,7168]{1,0:T(8,128)(2,1)S(1)} %fusion.9), channel_id=1, source_target_pairs={{0,2},{2,0},{8,10},{10,8},{16,18},{18,16},{24,26},{26,24},{28,30},... | collective-permute-start | bytes 1376264 | tf_op jit(solution)/shard_map/ppermute | solution.py:301
  3.4 18.1 %copy-start.2 = (s32[512,1]{0,1:T(1,128)S(1)}, s32[512,1]{0,1:T(1,128)}, u32[]{:S(2)}) copy-start(s32[512,1]{0,1:T(1,128)} %param.13) | copy-start | bytes 6148
  3.4 18.1 %copy-start.3 = (s32[16]{0:T(128)S(1)}, s32[16]{0:T(128)}, u32[]{:S(2)}) copy-start(s32[16]{0:T(128)} %param.14) | copy-start | bytes 196
  3.5 54.1 %collective-permute-start.10 = (bf16[14336,512]{1,0:T(8,128)(2,1)}, bf16[14336,512]{1,0:T(8,128)(2,1)}, u32[]{:S(2)}, u32[]{:S(2)}) collective-permute-start(bf16[14336,512]{1,0:T(8,128)(2,1)} %refs_7_), channel_id=1, source_target_pairs={{0,2},{2,0},{8,10},{10,8},{16,18},{18,16},{24,26},{26,24},{28,30},... | collective-permute-start | bytes 44040200 | tf_op jit(solution)/shard_map/ppermute | solution.py:301
  4.0 28.1 %collective-permute-start.3 = (bf16[64,7168]{1,0:T(8,128)(2,1)S(1)}, bf16[64,7168]{1,0:T(8,128)(2,1)S(1)}, u32[]{:S(2)}, u32[]{:S(2)}) collective-permute-start(bf16[64,7168]{1,0:T(8,128)(2,1)S(1)} %pad_maximum_fusion.2.refs_0_), channel_id=1, source_target_pairs={{0,8},{8,16},{16,24},{24,28},{28,20},{20,12},{12,4},{4,0},{2,6},{1... | collective-permute-start | bytes 2752520 | tf_op jit(solution)/shard_map/ppermute | solution.py:307
  6.8 25.4 %collective-permute-start.5 = (bf16[64,7168]{1,0:T(8,128)(2,1)S(1)}, bf16[64,7168]{1,0:T(8,128)(2,1)S(1)}, u32[]{:S(2)}, u32[]{:S(2)}) collective-permute-start(bf16[64,7168]{1,0:T(8,128)(2,1)S(1)} %pad_maximum_fusion.2.refs_0_), channel_id=1, source_target_pairs={{0,4},{8,0},{16,8},{24,16},{28,24},{20,28},{12,20},{4,12},{2,10},{... | collective-permute-start | bytes 2752520 | tf_op jit(solution)/shard_map/ppermute | solution.py:307
  6.8 49.4 %collective-permute-start.9 = (bf16[64,14336]{1,0:T(8,128)(2,1)}, bf16[64,14336]{1,0:T(8,128)(2,1)}, u32[]{:S(2)}, u32[]{:S(2)}) collective-permute-start(bf16[64,14336]{1,0:T(8,128)(2,1)} %bitcast.28), channel_id=1, source_target_pairs={{0,2},{2,0},{8,10},{10,8},{16,18},{18,16},{24,26},{26,24},{28,30},... | collective-permute-start | bytes 5505032 | tf_op jit(solution)/shard_map/ppermute | solution.py:301
  7.0 14.5 %collective-permute-start.1 = (bf16[16,32,512]{2,1,0:T(8,128)(2,1)S(1)}, bf16[16,32,512]{2,1,0:T(8,128)(2,1)}, u32[]{:S(2)}, u32[]{:S(2)}) collective-permute-start(bf16[16,32,512]{2,1,0:T(8,128)(2,1)S(1)} %copy-done.1), channel_id=1, source_target_pairs={{0,1},{1,0},{2,3},{3,2},{4,5},{5,4},{6,7},{7,6},{8,9},{9,8},{10,11... | collective-permute-start | bytes 1572872 | tf_op jit(solution)/shard_map/ppermute | solution.py:330
  24.2 13.5 %collective-permute-start.2 = (bf16[8,7168]{1,0:T(8,128)(2,1)}, bf16[8,7168]{1,0:T(8,128)(2,1)}, u32[]{:S(2)}, u32[]{:S(2)}) collective-permute-start(bf16[8,7168]{1,0:T(8,128)(2,1)} %convolution_convert_fusion), channel_id=1, source_target_pairs={{0,28},{2,30},{8,20},{10,22},{16,12},{18,14},{24,4},{26,6},{28,0},... | collective-permute-start | bytes 344072 | tf_op jit(solution)/shard_map/ppermute | solution.py:301
  32.1 22.1 %collective-permute-start.4 = (bf16[64,7168]{1,0:T(8,128)(2,1)S(1)}, bf16[64,7168]{1,0:T(8,128)(2,1)}, u32[]{:S(2)}, u32[]{:S(2)}) collective-permute-start(bf16[64,7168]{1,0:T(8,128)(2,1)S(1)} %collective-permute-done.3.refs_1_), channel_id=1, source_target_pairs={{0,8},{8,16},{16,24},{24,28},{28,20},{20,12},{12,4},{4,0},{2,6},{1... | collective-permute-start | bytes 2752520 | tf_op jit(solution)/shard_map/ppermute | solution.py:307
  32.2 22.0 %collective-permute-start.6 = (bf16[64,7168]{1,0:T(8,128)(2,1)S(1)}, bf16[64,7168]{1,0:T(8,128)(2,1)}, u32[]{:S(2)}, u32[]{:S(2)}) collective-permute-start(bf16[64,7168]{1,0:T(8,128)(2,1)S(1)} %collective-permute-done.5.refs_2_), channel_id=1, source_target_pairs={{0,4},{8,0},{16,8},{24,16},{28,24},{20,28},{12,20},{4,12},{2,10},{... | collective-permute-start | bytes 2752520 | tf_op jit(solution)/shard_map/ppermute | solution.py:307
  37.7 19.8 %copy-start = (bf16[64,7168]{1,0:T(8,128)(2,1)S(1)}, bf16[64,7168]{1,0:T(8,128)(2,1)}, u32[]{:S(2)}) copy-start(bf16[64,7168]{1,0:T(8,128)(2,1)} %constant_dynamic-slice_fusion) | copy-start | bytes 2752516
  54.2 22.4 %collective-permute-start.7 = (bf16[64,7168]{1,0:T(8,128)(2,1)}, bf16[64,7168]{1,0:T(8,128)(2,1)S(1)}, u32[]{:S(2)}, u32[]{:S(2)}) collective-permute-start(bf16[64,7168]{1,0:T(8,128)(2,1)} %collective-permute-done.4.refs_3_), channel_id=1, source_target_pairs={{0,8},{8,16},{16,24},{24,28},{28,20},{20,12},{12,4},{4,0},{2,6},{1... | collective-permute-start | bytes 2752520 | tf_op jit(solution)/shard_map/ppermute | solution.py:307
  55.3 21.3 %collective-permute-start.8 = (bf16[64,7168]{1,0:T(8,128)(2,1)}, bf16[64,7168]{1,0:T(8,128)(2,1)S(1)}, u32[]{:S(2)}, u32[]{:S(2)}) collective-permute-start(bf16[64,7168]{1,0:T(8,128)(2,1)} %collective-permute-done.6.refs_4_), channel_id=1, source_target_pairs={{0,4},{8,0},{16,8},{24,16},{28,24},{20,28},{12,20},{4,12},{2,10},{... | collective-permute-start | bytes 2752520 | tf_op jit(solution)/shard_map/ppermute | solution.py:307
  76.5 13.4 %collective-permute-start.15 = (bf16[64,7168]{1,0:T(8,128)(2,1)S(1)}, bf16[64,7168]{1,0:T(8,128)(2,1)S(1)}, u32[]{:S(2)}, u32[]{:S(2)}) collective-permute-start(bf16[64,7168]{1,0:T(8,128)(2,1)S(1)} %collective-permute-done.7.piece), channel_id=1, source_target_pairs={{0,8},{8,16},{16,24},{24,28},{28,20},{20,12},{12,4},{4,0},{2,6},{1... | collective-permute-start | bytes 2752520 | tf_op jit(solution)/shard_map/ppermute | solution.py:307
  80.1 11.8 %collective-permute-start.12 = (f32[2,16,64]{2,1,0:T(8,128)S(1)}, f32[2,16,64]{2,1,0:T(8,128)S(1)}, u32[]{:S(2)}, u32[]{:S(2)}) collective-permute-start(f32[2,16,64]{2,1,0:T(8,128)S(1)} %get-tuple-element.91), channel_id=1, source_target_pairs={{0,1},{1,0},{2,3},{3,2},{4,5},{5,4},{6,7},{7,6},{8,9},{9,8},{10,11... | collective-permute-start | bytes 24584 | tf_op jit(solution)/shard_map/ppermute | solution.py:317
  81.6 10.3 %collective-permute-start.13 = (f32[2,16,64]{2,1,0:T(8,128)S(1)}, f32[2,16,64]{2,1,0:T(8,128)S(1)}, u32[]{:S(2)}, u32[]{:S(2)}) collective-permute-start(f32[2,16,64]{2,1,0:T(8,128)S(1)} %get-tuple-element.91), channel_id=1, source_target_pairs={{0,3},{1,2},{2,1},{3,0},{4,7},{5,6},{6,5},{7,4},{8,11},{9,10},{10,... | collective-permute-start | bytes 24584 | tf_op jit(solution)/shard_map/ppermute | solution.py:318
  84.2 7.7 %collective-permute-start.14 = (f32[2,3,64,512]{3,2,1,0:T(8,128)S(1)}, f32[2,3,64,512]{3,2,1,0:T(8,128)S(1)}, u32[]{:S(2)}, u32[]{:S(2)}) collective-permute-start(f32[2,3,64,512]{3,2,1,0:T(8,128)S(1)} %get-tuple-element.97), channel_id=1, source_target_pairs={{0,2},{2,0},{8,10},{10,8},{16,18},{18,16},{24,26},{26,24},{28,30},... | collective-permute-start | bytes 2359304 | tf_op jit(solution)/shard_map/ppermute | solution.py:301
  85.0 6.9 %collective-permute-start.11 = (f32[2,16,64]{2,1,0:T(8,128)S(1)}, f32[2,16,64]{2,1,0:T(8,128)S(1)}, u32[]{:S(2)}, u32[]{:S(2)}) collective-permute-start(f32[2,16,64]{2,1,0:T(8,128)S(1)} %get-tuple-element.90), channel_id=1, source_target_pairs={{0,2},{2,0},{8,10},{10,8},{16,18},{18,16},{24,26},{26,24},{28,30},... | collective-permute-start | bytes 24584 | tf_op jit(solution)/shard_map/ppermute | solution.py:301
  91.9 5.3 %collective-permute-start.16 = (bf16[2,16,64]{2,1,0:T(8,128)(2,1)S(1)}, bf16[2,16,64]{2,1,0:T(8,128)(2,1)S(1)}, u32[]{:S(2)}, u32[]{:S(2)}) collective-permute-start(bf16[2,16,64]{2,1,0:T(8,128)(2,1)S(1)} %add_convert_fusion.3), channel_id=1, source_target_pairs={{0,4},{2,6},{4,0},{6,2},{8,12},{10,14},{12,8},{14,10},{16,20},{18,... | collective-permute-start | bytes 12296 | tf_op jit(solution)/shard_map/ppermute | solution.py:492
  93.1 4.1 %collective-permute-start.17 = (bf16[2,16,64]{2,1,0:T(8,128)(2,1)S(1)}, bf16[2,16,64]{2,1,0:T(8,128)(2,1)S(1)}, u32[]{:S(2)}, u32[]{:S(2)}) collective-permute-start(bf16[2,16,64]{2,1,0:T(8,128)(2,1)S(1)} %add_convert_fusion.3), channel_id=1, source_target_pairs={{0,8},{2,10},{4,12},{6,14},{8,0},{10,2},{12,4},{14,6},{16,24},{18,... | collective-permute-start | bytes 12296 | tf_op jit(solution)/shard_map/ppermute | solution.py:492
  94.2 4.5 %collective-permute-start.18 = (bf16[2,16,64]{2,1,0:T(8,128)(2,1)S(1)}, bf16[2,16,64]{2,1,0:T(8,128)(2,1)S(1)}, u32[]{:S(2)}, u32[]{:S(2)}) collective-permute-start(bf16[2,16,64]{2,1,0:T(8,128)(2,1)S(1)} %add_convert_fusion.3), channel_id=1, source_target_pairs={{0,12},{2,14},{4,8},{6,10},{8,4},{10,6},{12,0},{14,2},{16,28},{18,... | collective-permute-start | bytes 12296 | tf_op jit(solution)/shard_map/ppermute | solution.py:492
  95.7 12.5 %collective-permute-start.20 = (bf16[3,64,512]{2,1,0:T(8,128)(2,1)S(1)}, bf16[3,64,512]{2,1,0:T(8,128)(2,1)S(1)}, u32[]{:S(2)}, u32[]{:S(2)}) collective-permute-start(bf16[3,64,512]{2,1,0:T(8,128)(2,1)S(1)} %get-tuple-element.123), channel_id=1, source_target_pairs={{0,1},{1,0},{2,3},{3,2},{4,5},{5,4},{6,7},{7,6},{8,9},{9,8},{10,11... | collective-permute-start | bytes 589832 | tf_op jit(solution)/shard_map/ppermute | solution.py:503
  98.8 5.6 %collective-permute-start.19 = (bf16[8,16,64]{2,1,0:T(8,128)(2,1)S(1)}, bf16[8,16,64]{2,1,0:T(8,128)(2,1)S(1)}, u32[]{:S(2)}, u32[]{:S(2)}) collective-permute-start(bf16[8,16,64]{2,1,0:T(8,128)(2,1)S(1)} %pad_maximum_fusion.5), channel_id=1, source_target_pairs={{0,16},{2,18},{4,20},{6,22},{8,24},{10,26},{12,28},{14,30},{16,0},... | collective-permute-start | bytes 49160 | tf_op jit(solution)/shard_map/ppermute | solution.py:492
  100.5 7.6 %collective-permute-start.21 = (f32[1,64,512]{2,1,0:T(8,128)S(1)}, f32[1,64,512]{2,1,0:T(8,128)S(1)}, u32[]{:S(2)}, u32[]{:S(2)}) collective-permute-start(f32[1,64,512]{2,1,0:T(8,128)S(1)} %get-tuple-element.116), channel_id=1, source_target_pairs={{0,2},{2,0},{8,10},{10,8},{16,18},{18,16},{24,26},{26,24},{28,30},... | collective-permute-start | bytes 393224 | tf_op jit(solution)/shard_map/ppermute | solution.py:301
  102.5 4.6 %collective-permute-start.22 = (bf16[1,64,512]{2,1,0:T(8,128)(2,1)S(1)}, bf16[1,64,512]{2,1,0:T(8,128)(2,1)S(1)}, u32[]{:S(2)}, u32[]{:S(2)}) collective-permute-start(bf16[1,64,512]{2,1,0:T(8,128)(2,1)S(1)} %get-tuple-element.117), channel_id=1, source_target_pairs={{0,1},{1,0},{2,3},{3,2},{4,5},{5,4},{6,7},{7,6},{8,9},{9,8},{10,11... | collective-permute-start | bytes 196616 | tf_op jit(solution)/shard_map/ppermute | solution.py:317
  104.0 4.1 %collective-permute-start.23 = (bf16[1,64,512]{2,1,0:T(8,128)(2,1)S(1)}, bf16[1,64,512]{2,1,0:T(8,128)(2,1)S(1)}, u32[]{:S(2)}, u32[]{:S(2)}) collective-permute-start(bf16[1,64,512]{2,1,0:T(8,128)(2,1)S(1)} %get-tuple-element.118), channel_id=1, source_target_pairs={{0,3},{1,2},{2,1},{3,0},{4,7},{5,6},{6,5},{7,4},{8,11},{9,10},{10,... | collective-permute-start | bytes 196616 | tf_op jit(solution)/shard_map/ppermute | solution.py:318

commit v19 on v18

--- a/solution.py
+++ b/solution.py
@@ -496,12 +496,12 @@
         return jnp.concatenate([value] + parts, axis=0)
 
     reach = min(4, nodes)
-    low, to_sib = lax.optimization_barrier((gather(low, 1, reach), to_sib))
+    kept_one, to_mp = last_rows(0, last, early[0], 1)
+    low, to_sib, to_mp = lax.optimization_barrier((gather(low, 1, reach), to_sib, to_mp))
     while reach < nodes:
         low = gather(low, reach, 2)
         reach *= 2
     got_more = lax.ppermute(out_more.astype(bf16), INNER, SWAP)
-    kept_one, to_mp = last_rows(0, last, early[0], 1)
     got_one = to_three(to_sib, to_mp, to_both)
 
     shape = (own_nodes, group_rows, width)

time: 110 us -> 108 us (0.982)
  waiting for transfers between devices: 43.4 us -> 41.8 us
  transfers between devices with their start and end apart: 24 -> 24, of which waited for: 7 -> 6; matrix products, arithmetic and copies ran while one was open for 14% -> 15% of each run, Pallas kernels for 18% -> 19%
where the time goes in v19:
time: 108 us
  waiting for transfers between devices  41.8 us (39%)
  starting transfers between devices  27 us (25%)
  Pallas kernels  21.4 us (20%)
  other arithmetic  9.14 us (8%)
  local copies, waits for them, and re-layouts  7.35 us (7%)
    ppermute x7, waiting for transfers between devices, turn(): return lax.ppermute(value, 'wide', pairs)  28.9 us
    pallas_call x7, Pallas kernels, kernel_call(): pl.pallas_call(kernel, in_specs=[pl.BlockSpec(memory_space=pltpu.SMEM)] +...  21.4 us
    ppermute x1, waiting for transfers between devices, ringed(): other_second = lax.ppermute(second_factor_table, INNER, SWAP)  10.5 us
    ppermute x7, starting transfers between devices, turn(): return lax.ppermute(value, 'wide', pairs)  8.19 us
    ppermute x7, starting transfers between devices, send(): return lax.ppermute(value, 'wide', moved(shift, cross))  6.69 us
    ppermute x4, starting transfers between devices, from_node(): lax.ppermute(value, 'wide', [(w, w ^ 2 * gap) for w in range(owners)])  5.15 us
    dynamic_slice x2, local copies, waits for them, and re-layouts, half_of(): return lax.dynamic_slice_in_dim(value, which * depth, depth, axis)  3.42 us
    convert_element_type x2, other arithmetic, hidden_of(): (jax.nn.silu(gate.astype(jnp.float32)) * up.astype(jnp.float32)).astype(j...  2.85 us
  transfers between devices with their start and end apart: 24, of which 6 were waited for; matrix products, arithmetic and copies ran while one was open for 15% of the time, Pallas kernels for 19%

profile of v19, /device:TPU:0, one launch (start us, length us, event | category | flops | bytes accessed | tf_op | source)
XLA Modules:
  0.0 107.9 jit_solution(14088081197611910552)
XLA Ops:
  0.0 1.4 %fusion.9 = bf16[32,7168]{1,0:T(8,128)(2,1)S(1)} fusion(bf16[32,14336]{1,0:T(8,128)(2,1)} %param.9, s32[]{:T(128)S(6)} %select_n.105, bf16[32,14336]{1,0:T(8,128)(2,1)} %param.8), kind=kLoop, calls=%fused_computation.18 | loop fusion | flops 1835008 | bytes 1376260 | tf_op jit(solution)/shard_map/convert_element_type | solution.py:199
  1.4 0.5 collective-permute-start
  2.0 1.4 %fusion.8 = bf16[32,7168]{1,0:T(8,128)(2,1)S(1)} fusion(bf16[32,14336]{1,0:T(8,128)(2,1)} %param.9, s32[]{:T(128)S(6)} %select_n.106, bf16[32,14336]{1,0:T(8,128)(2,1)} %param.8), kind=kLoop, calls=%fused_computation.17 | loop fusion | flops 1835008 | bytes 1376260 | tf_op jit(solution)/shard_map/convert_element_type | solution.py:199
  3.5 0.4 collective-permute-start.10
  4.0 2.8 %collective-permute-start.3 = (bf16[64,7168]{1,0:T(8,128)(2,1)S(1)}, bf16[64,7168]{1,0:T(8,128)(2,1)S(1)}, u32[]{:S(2)}, u32[]{:S(2)}) collective-permute-start(bf16[64,7168]{1,0:T(8,128)(2,1)S(1)} %pad_maximum_fusion.2.refs_0_), channel_id=1, source_target_pairs={{0,8},{8,16},{16,24},{24,28},{28,20},{20,12},{12,4},{4,0},{2,6},{1... | collective-permute-start | bytes 2752520 | tf_op jit(solution)/shard_map/ppermute | solution.py:307
  7.0 1.8 %collective-permute-start.1 = (bf16[16,32,512]{2,1,0:T(8,128)(2,1)S(1)}, bf16[16,32,512]{2,1,0:T(8,128)(2,1)}, u32[]{:S(2)}, u32[]{:S(2)}) collective-permute-start(bf16[16,32,512]{2,1,0:T(8,128)(2,1)S(1)} %copy-done.1), channel_id=1, source_target_pairs={{0,1},{1,0},{2,3},{3,2},{4,5},{5,4},{6,7},{7,6},{8,9},{9,8},{10,11... | collective-permute-start | bytes 1572872 | tf_op jit(solution)/shard_map/ppermute | solution.py:330
  8.8 2.2 %constant_dynamic-slice_fusion = bf16[64,7168]{1,0:T(8,128)(2,1)} fusion(bf16[64,14336]{1,0:T(8,128)(2,1)} %bitcast.29, s32[]{:T(128)S(6)} %select_n.124), kind=kLoop, calls=%fused_computation.74 | loop fusion | bytes 1835012 | tf_op jit(solution)/shard_map/dynamic_slice | solution.py:310
  10.9 10.5 %collective-permute-done.1 = bf16[16,32,512]{2,1,0:T(8,128)(2,1)} collective-permute-done((bf16[16,32,512]{2,1,0:T(8,128)(2,1)S(1)}, bf16[16,32,512]{2,1,0:T(8,128)(2,1)}, u32[]{:S(2)}, u32[]{:S(2)}) %collective-permute-start.1) | collective-permute-done | bytes 524320 | tf_op jit(solution)/shard_map/ppermute | solution.py:330
  21.6 0.7 constant_dynamic-slice_fusion.4
  22.3 0.5 convert_reduce_fusion
  23.3 0.9 convolution_convert_fusion
  24.2 4.8 %collective-permute-start.2 = (bf16[8,7168]{1,0:T(8,128)(2,1)}, bf16[8,7168]{1,0:T(8,128)(2,1)}, u32[]{:S(2)}, u32[]{:S(2)}) collective-permute-start(bf16[8,7168]{1,0:T(8,128)(2,1)} %convolution_convert_fusion), channel_id=1, source_target_pairs={{0,28},{2,30},{8,20},{10,22},{16,12},{18,14},{24,4},{26,6},{28,0},... | collective-permute-start | bytes 344072 | tf_op jit(solution)/shard_map/ppermute | solution.py:301
  29.6 0.7 add_convert_fusion.2
  30.3 0.6 add_convert_fusion.1
  31.3 0.7 and_convert_fusion
  32.2 2.0 %collective-permute-start.6 = (bf16[64,7168]{1,0:T(8,128)(2,1)S(1)}, bf16[64,7168]{1,0:T(8,128)(2,1)}, u32[]{:S(2)}, u32[]{:S(2)}) collective-permute-start(bf16[64,7168]{1,0:T(8,128)(2,1)S(1)} %collective-permute-done.5.refs_2_), channel_id=1, source_target_pairs={{0,4},{8,0},{16,8},{24,16},{28,24},{20,28},{12,20},{4,12},{2,10},{... | collective-permute-start | bytes 2752520 | tf_op jit(solution)/shard_map/ppermute | solution.py:307
  34.2 0.2 compare_convert_fusion.mask
  34.5 1.0 reshape.433
  35.4 0.7 copy.11
  36.1 0.8 slice.39.refs_6_
  36.9 0.7 pad_maximum_fusion.4.choices
  37.7 1.3 %pad_maximum_fusion.1.second = bf16[1024,512]{1,0:T(8,128)(2,1)S(1)} fusion(bf16[512,512]{1,0:T(8,128)(2,1)} %bitcast.9, bf16[512,512]{1,0:T(8,128)(2,1)} %bitcast.27), kind=kLoop, calls=%fused_computation.6 | loop fusion | flops 2097152 | bytes 2097152 | tf_op jit(solution)/shard_map/concatenate | solution.py:418
  39.0 15.2 %collective-permute-done.4.refs_3_ = bf16[64,7168]{1,0:T(8,128)(2,1)} collective-permute-done((bf16[64,7168]{1,0:T(8,128)(2,1)S(1)}, bf16[64,7168]{1,0:T(8,128)(2,1)}, u32[]{:S(2)}, u32[]{:S(2)}) %collective-permute-start.4) | collective-permute-done | bytes 917536 | tf_op jit(solution)/shard_map/ppermute | solution.py:307
  54.2 1.1 %collective-permute-start.7 = (bf16[64,7168]{1,0:T(8,128)(2,1)}, bf16[64,7168]{1,0:T(8,128)(2,1)S(1)}, u32[]{:S(2)}, u32[]{:S(2)}) collective-permute-start(bf16[64,7168]{1,0:T(8,128)(2,1)} %collective-permute-done.4.refs_3_), channel_id=1, source_target_pairs={{0,8},{8,16},{16,24},{24,28},{28,20},{20,12},{12,4},{4,0},{2,6},{1... | collective-permute-start | bytes 2752520 | tf_op jit(solution)/shard_map/ppermute | solution.py:307
  55.3 0.9 collective-permute-start.8
  56.2 1.2 %constant_dynamic-slice_fusion.1 = bf16[64,7168]{1,0:T(8,128)(2,1)S(1)} fusion(bf16[64,14336]{1,0:T(8,128)(2,1)} %collective-permute-done.9, s32[]{:T(128)S(6)} %select_n.124), kind=kLoop, calls=%fused_computation.75 | loop fusion | bytes 1835012 | tf_op jit(solution)/shard_map/dynamic_slice | solution.py:310
  57.6 10.1 %shard_map.82 = (f32[1,64,512]{2,1,0:T(8,128)S(1)}, f32[1,64,512]{2,1,0:T(8,128)S(1)}, f32[4,64,512]{2,1,0:T(8,128)S(1)}, f32[4,64,512]{2,1,0:T(8,128)S(1)}, f32...) custom-call(s32[10]{0:T(128)S(1)} %pad_add_fusion.facts, bf16[64,7168]{1,0:T(8,128)(2,1)S(1)} %pad_maximum_fusion.2.refs_0_, ...), custom_call_target="tpu_custom_call" | custom-call | flops 165150720 | bytes 5160960 | tf_op jit(solution)/shard_map/pallas_call | solution.py:183
  67.7 8.9 %collective-permute-done.7.piece = bf16[64,7168]{1,0:T(8,128)(2,1)S(1)} collective-permute-done((bf16[64,7168]{1,0:T(8,128)(2,1)}, bf16[64,7168]{1,0:T(8,128)(2,1)S(1)}, u32[]{:S(2)}, u32[]{:S(2)}) %collective-permute-start.7) | collective-permute-done | bytes 917536 | tf_op jit(solution)/shard_map/ppermute | solution.py:307
  76.5 1.3 %collective-permute-start.15 = (bf16[64,7168]{1,0:T(8,128)(2,1)S(1)}, bf16[64,7168]{1,0:T(8,128)(2,1)S(1)}, u32[]{:S(2)}, u32[]{:S(2)}) collective-permute-start(bf16[64,7168]{1,0:T(8,128)(2,1)S(1)} %collective-permute-done.7.piece), channel_id=1, source_target_pairs={{0,8},{8,16},{16,24},{24,28},{28,20},{20,12},{12,4},{4,0},{2,6},{1... | collective-permute-start | bytes 2752520 | tf_op jit(solution)/shard_map/ppermute | solution.py:307
  77.9 2.2 %shard_map.83 = (f32[2,16,64]{2,1,0:T(8,128)S(1)}, f32[2,16,64]{2,1,0:T(8,128)S(1)}) custom-call(s32[10]{0:T(128)S(1)} %pad_add_fusion.facts, bf16[64,7168]{1,0:T(8,128)(2,1)S(1)} %collective-permute-done.7.piece, bf16[64,7168]{1,0:T(8,128)(2,1)S(1)} %collective-permute-done.8.other, bf16[8,7168]{1,0:T(8,128)(2,1)} %collective-permute-done.2.far_rows, ...), custom_call_target="tpu_custom_call" | custom-call | flops 7340032 | bytes 229376 | tf_op jit(solution)/shard_map/pallas_call | solution.py:183
  80.1 1.5 %collective-permute-start.12 = (f32[2,16,64]{2,1,0:T(8,128)S(1)}, f32[2,16,64]{2,1,0:T(8,128)S(1)}, u32[]{:S(2)}, u32[]{:S(2)}) collective-permute-start(f32[2,16,64]{2,1,0:T(8,128)S(1)} %get-tuple-element.92), channel_id=1, source_target_pairs={{0,1},{1,0},{2,3},{3,2},{4,5},{5,4},{6,7},{7,6},{8,9},{9,8},{10,11... | collective-permute-start | bytes 24584 | tf_op jit(solution)/shard_map/ppermute | solution.py:317
  81.6 2.6 %shard_map.84 = (f32[2,3,64,512]{3,2,1,0:T(8,128)S(1)}, f32[2,3,64,512]{3,2,1,0:T(8,128)S(1)}) custom-call(s32[10]{0:T(128)S(1)} %pad_add_fusion.facts, bf16[64,7168]{1,0:T(8,128)(2,1)S(1)} %collective-permute-done.7.piece, bf16[64,7168]{1,0:T(8,128)(2,1)S(1)} %collective-permute-done.8.other, bf16[2,7,1024,512]{3,2,1,0:T(8,128)(2,1)S(1)} %get-tuple-element.95.held, ...), custom_call_target="tpu_custom_call" | custom-call | flops 58720256 | bytes 1835008 | tf_op jit(solution)/shard_map/pallas_call | solution.py:183
  84.2 0.7 collective-permute-start.14
  85.0 4.9 %collective-permute-done.15.piece = bf16[64,7168]{1,0:T(8,128)(2,1)S(1)} collective-permute-done((bf16[64,7168]{1,0:T(8,128)(2,1)S(1)}, bf16[64,7168]{1,0:T(8,128)(2,1)S(1)}, u32[]{:S(2)}, u32[]{:S(2)}) %collective-permute-start.15) | collective-permute-done | bytes 917536 | tf_op jit(solution)/shard_map/ppermute | solution.py:307
  89.9 1.9 %shard_map.85 = (f32[1,64,512]{2,1,0:T(8,128)S(1)}, bf16[1,64,512]{2,1,0:T(8,128)(2,1)S(1)}) custom-call(s32[10]{0:T(128)S(1)} %pad_add_fusion.facts, bf16[64,7168]{1,0:T(8,128)(2,1)S(1)} %collective-permute-done.15.piece, bf16[2,7,1024,512]{3,2,1,0:T(8,128)(2,1)S(1)} %get-tuple-element.95.held, f32[1,64,512]{2,1,0:T(8,128)S(1)} %get-tuple-element.99.base), custom_call_target="tpu_custom_call" | custom-call | flops 15032385536 | bytes 469762048 | tf_op jit(solution)/shard_map/pallas_call | solution.py:183
  91.9 1.2 %collective-permute-start.16 = (bf16[2,16,64]{2,1,0:T(8,128)(2,1)S(1)}, bf16[2,16,64]{2,1,0:T(8,128)(2,1)S(1)}, u32[]{:S(2)}, u32[]{:S(2)}) collective-permute-start(bf16[2,16,64]{2,1,0:T(8,128)(2,1)S(1)} %add_convert_fusion.3), channel_id=1, source_target_pairs={{0,4},{2,6},{4,0},{6,2},{8,12},{10,14},{12,8},{14,10},{16,20},{18,... | collective-permute-start | bytes 12296 | tf_op jit(solution)/shard_map/ppermute | solution.py:492
  93.1 1.1 collective-permute-start.17
  94.2 1.3 %collective-permute-start.18 = (bf16[2,16,64]{2,1,0:T(8,128)(2,1)S(1)}, bf16[2,16,64]{2,1,0:T(8,128)(2,1)S(1)}, u32[]{:S(2)}, u32[]{:S(2)}) collective-permute-start(bf16[2,16,64]{2,1,0:T(8,128)(2,1)S(1)} %add_convert_fusion.3), channel_id=1, source_target_pairs={{0,12},{2,14},{4,8},{6,10},{8,4},{10,6},{12,0},{14,2},{16,28},{18,... | collective-permute-start | bytes 12296 | tf_op jit(solution)/shard_map/ppermute | solution.py:492
  95.5 0.2 fusion.12
  95.7 1.6 %collective-permute-start.20 = (bf16[3,64,512]{2,1,0:T(8,128)(2,1)S(1)}, bf16[3,64,512]{2,1,0:T(8,128)(2,1)S(1)}, u32[]{:S(2)}, u32[]{:S(2)}) collective-permute-start(bf16[3,64,512]{2,1,0:T(8,128)(2,1)S(1)} %get-tuple-element.125), channel_id=1, source_target_pairs={{0,1},{1,0},{2,3},{3,2},{4,5},{5,4},{6,7},{7,6},{8,9},{9,8},{10,11... | collective-permute-start | bytes 589832 | tf_op jit(solution)/shard_map/ppermute | solution.py:504
  97.2 1.9 %shard_map.86 = (f32[1,64,512]{2,1,0:T(8,128)S(1)}, bf16[1,64,512]{2,1,0:T(8,128)(2,1)S(1)}) custom-call(s32[10]{0:T(128)S(1)} %pad_add_fusion.facts, bf16[64,7168]{1,0:T(8,128)(2,1)S(1)} %collective-permute-done.15.piece, bf16[2,7,1024,512]{3,2,1,0:T(8,128)(2,1)S(1)} %get-tuple-element.95.held, f32[1,64,512]{2,1,0:T(8,128)S(1)} %get-tuple-element.108.base), custom_call_target="tpu_custom_call" | custom-call | flops 14680064 | bytes 458752 | tf_op jit(solution)/shard_map/pallas_call | solution.py:183
  99.2 1.6 %collective-permute-start.19 = (bf16[8,16,64]{2,1,0:T(8,128)(2,1)S(1)}, bf16[8,16,64]{2,1,0:T(8,128)(2,1)S(1)}, u32[]{:S(2)}, u32[]{:S(2)}) collective-permute-start(bf16[8,16,64]{2,1,0:T(8,128)(2,1)S(1)} %pad_maximum_fusion.5), channel_id=1, source_target_pairs={{0,16},{2,18},{4,20},{6,22},{8,24},{10,26},{12,28},{14,30},{16,0},... | collective-permute-start | bytes 49160 | tf_op jit(solution)/shard_map/ppermute | solution.py:492
  100.8 1.3 %collective-permute-start.23 = (bf16[1,64,512]{2,1,0:T(8,128)(2,1)S(1)}, bf16[1,64,512]{2,1,0:T(8,128)(2,1)S(1)}, u32[]{:S(2)}, u32[]{:S(2)}) collective-permute-start(bf16[1,64,512]{2,1,0:T(8,128)(2,1)S(1)} %get-tuple-element.120), channel_id=1, source_target_pairs={{0,3},{1,2},{2,1},{3,0},{4,7},{5,6},{6,5},{7,4},{8,11},{9,10},{10,... | collective-permute-start | bytes 196616 | tf_op jit(solution)/shard_map/ppermute | solution.py:318
  102.1 0.8 collective-permute-start.22
  102.9 1.1 %collective-permute-done.19 = bf16[8,16,64]{2,1,0:T(8,128)(2,1)S(1)} collective-permute-done((bf16[8,16,64]{2,1,0:T(8,128)(2,1)S(1)}, bf16[8,16,64]{2,1,0:T(8,128)(2,1)S(1)}, u32[]{:S(2)}, u32[]{:S(2)}) %collective-permute-start.19) | collective-permute-done | bytes 16416 | tf_op jit(solution)/shard_map/ppermute | solution.py:492
  104.1 1.3 %shard_map.87.delta = f32[4,64,512]{2,1,0:T(8,128)S(1)} custom-call(s32[10]{0:T(128)S(1)} %pad_add_fusion.facts, bf16[256,64]{1,0:T(8,128)(2,1)S(1)} %bitcast.26, bf16[256,256]{1,0:T(8,128)(2,1)S(1)} %fusion.10.spots, bf16[256,1024]{1,0:T(8,128)(2,1)S(1)} %compare_convert_fusion.mask, bf16[64,1024]{1,0:T(8,128)(2,1)S(1)} %fusion.11.copies, ...), custom_call_target="tpu_custom_call" | custom-call | flops 8388608 | bytes 262144 | tf_op jit(solution)/shard_map/pallas_call | solution.py:183
  105.4 1.2 %collective-permute-done.22.got_mp = bf16[1,64,512]{2,1,0:T(8,128)(2,1)S(1)} collective-permute-done((bf16[1,64,512]{2,1,0:T(8,128)(2,1)S(1)}, bf16[1,64,512]{2,1,0:T(8,128)(2,1)S(1)}, u32[]{:S(2)}, u32[]{:S(2)}) %collective-permute-start.22) | collective-permute-done | bytes 65568 | tf_op jit(solution)/shard_map/ppermute | solution.py:317
  106.6 1.3 %shard_map.88 = bf16[4,64,512]{2,1,0:T(8,128)(2,1)} custom-call(s32[10]{0:T(128)S(1)} %pad_add_fusion.facts, f32[4,64,512]{2,1,0:T(8,128)S(1)} %shard_map.87.delta, f32[3,64,512]{2,1,0:T(8,128)S(1)} %get-tuple-element.126.kept_more, bf16[3,64,512]{2,1,0:T(8,128)(2,1)S(1)} %collective-permute-done.20.got_more, f32[1,64,512]{2,1,0:T(8,128)S(1)} %get-tuple-element.117.kept, ...), custom_call_target="tpu_custom_call" | custom-call | flops 4096 | bytes 128 | tf_op jit(solution)/shard_map/pallas_call | solution.py:183
  (72 shorter events, 2.5 us)
Async XLA Ops:
  1.4 5.5 %copy-start.1 = (bf16[16,32,512]{2,1,0:T(8,128)(2,1)S(1)}, bf16[16,32,512]{2,1,0:T(8,128)(2,1)}, u32[]{:S(2)}) copy-start(bf16[16,32,512]{2,1,0:T(8,128)(2,1)} %param.12) | copy-start | bytes 1572868
  1.4 2.0 %collective-permute-start = (bf16[32,7168]{1,0:T(8,128)(2,1)S(1)}, bf16[32,7168]{1,0:T(8,128)(2,1)S(1)}, u32[]{:S(2)}, u32[]{:S(2)}) collective-permute-start(bf16[32,7168]{1,0:T(8,128)(2,1)S(1)} %fusion.9), channel_id=1, source_target_pairs={{0,2},{2,0},{8,10},{10,8},{16,18},{18,16},{24,26},{26,24},{28,30},... | collective-permute-start | bytes 1376264 | tf_op jit(solution)/shard_map/ppermute | solution.py:301
  3.4 18.1 %copy-start.2 = (s32[512,1]{0,1:T(1,128)S(1)}, s32[512,1]{0,1:T(1,128)}, u32[]{:S(2)}) copy-start(s32[512,1]{0,1:T(1,128)} %param.13) | copy-start | bytes 6148
  3.4 18.1 %copy-start.3 = (s32[16]{0:T(128)S(1)}, s32[16]{0:T(128)}, u32[]{:S(2)}) copy-start(s32[16]{0:T(128)} %param.14) | copy-start | bytes 196
  3.5 54.1 %collective-permute-start.10 = (bf16[14336,512]{1,0:T(8,128)(2,1)}, bf16[14336,512]{1,0:T(8,128)(2,1)}, u32[]{:S(2)}, u32[]{:S(2)}) collective-permute-start(bf16[14336,512]{1,0:T(8,128)(2,1)} %refs_7_), channel_id=1, source_target_pairs={{0,2},{2,0},{8,10},{10,8},{16,18},{18,16},{24,26},{26,24},{28,30},... | collective-permute-start | bytes 44040200 | tf_op jit(solution)/shard_map/ppermute | solution.py:301
  4.0 28.1 %collective-permute-start.3 = (bf16[64,7168]{1,0:T(8,128)(2,1)S(1)}, bf16[64,7168]{1,0:T(8,128)(2,1)S(1)}, u32[]{:S(2)}, u32[]{:S(2)}) collective-permute-start(bf16[64,7168]{1,0:T(8,128)(2,1)S(1)} %pad_maximum_fusion.2.refs_0_), channel_id=1, source_target_pairs={{0,8},{8,16},{16,24},{24,28},{28,20},{20,12},{12,4},{4,0},{2,6},{1... | collective-permute-start | bytes 2752520 | tf_op jit(solution)/shard_map/ppermute | solution.py:307
  6.8 25.4 %collective-permute-start.5 = (bf16[64,7168]{1,0:T(8,128)(2,1)S(1)}, bf16[64,7168]{1,0:T(8,128)(2,1)S(1)}, u32[]{:S(2)}, u32[]{:S(2)}) collective-permute-start(bf16[64,7168]{1,0:T(8,128)(2,1)S(1)} %pad_maximum_fusion.2.refs_0_), channel_id=1, source_target_pairs={{0,4},{8,0},{16,8},{24,16},{28,24},{20,28},{12,20},{4,12},{2,10},{... | collective-permute-start | bytes 2752520 | tf_op jit(solution)/shard_map/ppermute | solution.py:307
  6.8 49.4 %collective-permute-start.9 = (bf16[64,14336]{1,0:T(8,128)(2,1)}, bf16[64,14336]{1,0:T(8,128)(2,1)}, u32[]{:S(2)}, u32[]{:S(2)}) collective-permute-start(bf16[64,14336]{1,0:T(8,128)(2,1)} %bitcast.28), channel_id=1, source_target_pairs={{0,2},{2,0},{8,10},{10,8},{16,18},{18,16},{24,26},{26,24},{28,30},... | collective-permute-start | bytes 5505032 | tf_op jit(solution)/shard_map/ppermute | solution.py:301
  7.0 14.5 %collective-permute-start.1 = (bf16[16,32,512]{2,1,0:T(8,128)(2,1)S(1)}, bf16[16,32,512]{2,1,0:T(8,128)(2,1)}, u32[]{:S(2)}, u32[]{:S(2)}) collective-permute-start(bf16[16,32,512]{2,1,0:T(8,128)(2,1)S(1)} %copy-done.1), channel_id=1, source_target_pairs={{0,1},{1,0},{2,3},{3,2},{4,5},{5,4},{6,7},{7,6},{8,9},{9,8},{10,11... | collective-permute-start | bytes 1572872 | tf_op jit(solution)/shard_map/ppermute | solution.py:330
  24.2 13.5 %collective-permute-start.2 = (bf16[8,7168]{1,0:T(8,128)(2,1)}, bf16[8,7168]{1,0:T(8,128)(2,1)}, u32[]{:S(2)}, u32[]{:S(2)}) collective-permute-start(bf16[8,7168]{1,0:T(8,128)(2,1)} %convolution_convert_fusion), channel_id=1, source_target_pairs={{0,28},{2,30},{8,20},{10,22},{16,12},{18,14},{24,4},{26,6},{28,0},... | collective-permute-start | bytes 344072 | tf_op jit(solution)/shard_map/ppermute | solution.py:301
  32.1 22.1 %collective-permute-start.4 = (bf16[64,7168]{1,0:T(8,128)(2,1)S(1)}, bf16[64,7168]{1,0:T(8,128)(2,1)}, u32[]{:S(2)}, u32[]{:S(2)}) collective-permute-start(bf16[64,7168]{1,0:T(8,128)(2,1)S(1)} %collective-permute-done.3.refs_1_), channel_id=1, source_target_pairs={{0,8},{8,16},{16,24},{24,28},{28,20},{20,12},{12,4},{4,0},{2,6},{1... | collective-permute-start | bytes 2752520 | tf_op jit(solution)/shard_map/ppermute | solution.py:307
  32.2 22.0 %collective-permute-start.6 = (bf16[64,7168]{1,0:T(8,128)(2,1)S(1)}, bf16[64,7168]{1,0:T(8,128)(2,1)}, u32[]{:S(2)}, u32[]{:S(2)}) collective-permute-start(bf16[64,7168]{1,0:T(8,128)(2,1)S(1)} %collective-permute-done.5.refs_2_), channel_id=1, source_target_pairs={{0,4},{8,0},{16,8},{24,16},{28,24},{20,28},{12,20},{4,12},{2,10},{... | collective-permute-start | bytes 2752520 | tf_op jit(solution)/shard_map/ppermute | solution.py:307
  37.7 19.8 %copy-start = (bf16[64,7168]{1,0:T(8,128)(2,1)S(1)}, bf16[64,7168]{1,0:T(8,128)(2,1)}, u32[]{:S(2)}) copy-start(bf16[64,7168]{1,0:T(8,128)(2,1)} %constant_dynamic-slice_fusion) | copy-start | bytes 2752516
  54.2 22.4 %collective-permute-start.7 = (bf16[64,7168]{1,0:T(8,128)(2,1)}, bf16[64,7168]{1,0:T(8,128)(2,1)S(1)}, u32[]{:S(2)}, u32[]{:S(2)}) collective-permute-start(bf16[64,7168]{1,0:T(8,128)(2,1)} %collective-permute-done.4.refs_3_), channel_id=1, source_target_pairs={{0,8},{8,16},{16,24},{24,28},{28,20},{20,12},{12,4},{4,0},{2,6},{1... | collective-permute-start | bytes 2752520 | tf_op jit(solution)/shard_map/ppermute | solution.py:307
  55.3 21.3 %collective-permute-start.8 = (bf16[64,7168]{1,0:T(8,128)(2,1)}, bf16[64,7168]{1,0:T(8,128)(2,1)S(1)}, u32[]{:S(2)}, u32[]{:S(2)}) collective-permute-start(bf16[64,7168]{1,0:T(8,128)(2,1)} %collective-permute-done.6.refs_4_), channel_id=1, source_target_pairs={{0,4},{8,0},{16,8},{24,16},{28,24},{20,28},{12,20},{4,12},{2,10},{... | collective-permute-start | bytes 2752520 | tf_op jit(solution)/shard_map/ppermute | solution.py:307
  76.5 13.4 %collective-permute-start.15 = (bf16[64,7168]{1,0:T(8,128)(2,1)S(1)}, bf16[64,7168]{1,0:T(8,128)(2,1)S(1)}, u32[]{:S(2)}, u32[]{:S(2)}) collective-permute-start(bf16[64,7168]{1,0:T(8,128)(2,1)S(1)} %collective-permute-done.7.piece), channel_id=1, source_target_pairs={{0,8},{8,16},{16,24},{24,28},{28,20},{20,12},{12,4},{4,0},{2,6},{1... | collective-permute-start | bytes 2752520 | tf_op jit(solution)/shard_map/ppermute | solution.py:307
  80.1 11.8 %collective-permute-start.12 = (f32[2,16,64]{2,1,0:T(8,128)S(1)}, f32[2,16,64]{2,1,0:T(8,128)S(1)}, u32[]{:S(2)}, u32[]{:S(2)}) collective-permute-start(f32[2,16,64]{2,1,0:T(8,128)S(1)} %get-tuple-element.92), channel_id=1, source_target_pairs={{0,1},{1,0},{2,3},{3,2},{4,5},{5,4},{6,7},{7,6},{8,9},{9,8},{10,11... | collective-permute-start | bytes 24584 | tf_op jit(solution)/shard_map/ppermute | solution.py:317
  81.6 10.3 %collective-permute-start.13 = (f32[2,16,64]{2,1,0:T(8,128)S(1)}, f32[2,16,64]{2,1,0:T(8,128)S(1)}, u32[]{:S(2)}, u32[]{:S(2)}) collective-permute-start(f32[2,16,64]{2,1,0:T(8,128)S(1)} %get-tuple-element.92), channel_id=1, source_target_pairs={{0,3},{1,2},{2,1},{3,0},{4,7},{5,6},{6,5},{7,4},{8,11},{9,10},{10,... | collective-permute-start | bytes 24584 | tf_op jit(solution)/shard_map/ppermute | solution.py:318
  84.2 7.7 %collective-permute-start.14 = (f32[2,3,64,512]{3,2,1,0:T(8,128)S(1)}, f32[2,3,64,512]{3,2,1,0:T(8,128)S(1)}, u32[]{:S(2)}, u32[]{:S(2)}) collective-permute-start(f32[2,3,64,512]{3,2,1,0:T(8,128)S(1)} %get-tuple-element.98), channel_id=1, source_target_pairs={{0,2},{2,0},{8,10},{10,8},{16,18},{18,16},{24,26},{26,24},{28,30},... | collective-permute-start | bytes 2359304 | tf_op jit(solution)/shard_map/ppermute | solution.py:301
  85.0 6.9 %collective-permute-start.11 = (f32[2,16,64]{2,1,0:T(8,128)S(1)}, f32[2,16,64]{2,1,0:T(8,128)S(1)}, u32[]{:S(2)}, u32[]{:S(2)}) collective-permute-start(f32[2,16,64]{2,1,0:T(8,128)S(1)} %get-tuple-element.91), channel_id=1, source_target_pairs={{0,2},{2,0},{8,10},{10,8},{16,18},{18,16},{24,26},{26,24},{28,30},... | collective-permute-start | bytes 24584 | tf_op jit(solution)/shard_map/ppermute | solution.py:301
  91.9 7.2 %collective-permute-start.16 = (bf16[2,16,64]{2,1,0:T(8,128)(2,1)S(1)}, bf16[2,16,64]{2,1,0:T(8,128)(2,1)S(1)}, u32[]{:S(2)}, u32[]{:S(2)}) collective-permute-start(bf16[2,16,64]{2,1,0:T(8,128)(2,1)S(1)} %add_convert_fusion.3), channel_id=1, source_target_pairs={{0,4},{2,6},{4,0},{6,2},{8,12},{10,14},{12,8},{14,10},{16,20},{18,... | collective-permute-start | bytes 12296 | tf_op jit(solution)/shard_map/ppermute | solution.py:492
  93.1 6.0 %collective-permute-start.17 = (bf16[2,16,64]{2,1,0:T(8,128)(2,1)S(1)}, bf16[2,16,64]{2,1,0:T(8,128)(2,1)S(1)}, u32[]{:S(2)}, u32[]{:S(2)}) collective-permute-start(bf16[2,16,64]{2,1,0:T(8,128)(2,1)S(1)} %add_convert_fusion.3), channel_id=1, source_target_pairs={{0,8},{2,10},{4,12},{6,14},{8,0},{10,2},{12,4},{14,6},{16,24},{18,... | collective-permute-start | bytes 12296 | tf_op jit(solution)/shard_map/ppermute | solution.py:492
  94.2 5.0 %collective-permute-start.18 = (bf16[2,16,64]{2,1,0:T(8,128)(2,1)S(1)}, bf16[2,16,64]{2,1,0:T(8,128)(2,1)S(1)}, u32[]{:S(2)}, u32[]{:S(2)}) collective-permute-start(bf16[2,16,64]{2,1,0:T(8,128)(2,1)S(1)} %add_convert_fusion.3), channel_id=1, source_target_pairs={{0,12},{2,14},{4,8},{6,10},{8,4},{10,6},{12,0},{14,2},{16,28},{18,... | collective-permute-start | bytes 12296 | tf_op jit(solution)/shard_map/ppermute | solution.py:492
  95.7 10.9 %collective-permute-start.20 = (bf16[3,64,512]{2,1,0:T(8,128)(2,1)S(1)}, bf16[3,64,512]{2,1,0:T(8,128)(2,1)S(1)}, u32[]{:S(2)}, u32[]{:S(2)}) collective-permute-start(bf16[3,64,512]{2,1,0:T(8,128)(2,1)S(1)} %get-tuple-element.125), channel_id=1, source_target_pairs={{0,1},{1,0},{2,3},{3,2},{4,5},{5,4},{6,7},{7,6},{8,9},{9,8},{10,11... | collective-permute-start | bytes 589832 | tf_op jit(solution)/shard_map/ppermute | solution.py:504
  99.2 4.9 %collective-permute-start.19 = (bf16[8,16,64]{2,1,0:T(8,128)(2,1)S(1)}, bf16[8,16,64]{2,1,0:T(8,128)(2,1)S(1)}, u32[]{:S(2)}, u32[]{:S(2)}) collective-permute-start(bf16[8,16,64]{2,1,0:T(8,128)(2,1)S(1)} %pad_maximum_fusion.5), channel_id=1, source_target_pairs={{0,16},{2,18},{4,20},{6,22},{8,24},{10,26},{12,28},{14,30},{16,0},... | collective-permute-start | bytes 49160 | tf_op jit(solution)/shard_map/ppermute | solution.py:492
  100.8 5.8 %collective-permute-start.21 = (f32[1,64,512]{2,1,0:T(8,128)S(1)}, f32[1,64,512]{2,1,0:T(8,128)S(1)}, u32[]{:S(2)}, u32[]{:S(2)}) collective-permute-start(f32[1,64,512]{2,1,0:T(8,128)S(1)} %get-tuple-element.118), channel_id=1, source_target_pairs={{0,2},{2,0},{8,10},{10,8},{16,18},{18,16},{24,26},{26,24},{28,30},... | collective-permute-start | bytes 393224 | tf_op jit(solution)/shard_map/ppermute | solution.py:301
  100.8 4.6 %collective-permute-start.23 = (bf16[1,64,512]{2,1,0:T(8,128)(2,1)S(1)}, bf16[1,64,512]{2,1,0:T(8,128)(2,1)S(1)}, u32[]{:S(2)}, u32[]{:S(2)}) collective-permute-start(bf16[1,64,512]{2,1,0:T(8,128)(2,1)S(1)} %get-tuple-element.120), channel_id=1, source_target_pairs={{0,3},{1,2},{2,1},{3,0},{4,7},{5,6},{6,5},{7,4},{8,11},{9,10},{10,... | collective-permute-start | bytes 196616 | tf_op jit(solution)/shard_map/ppermute | solution.py:318
  102.1 4.5 %collective-permute-start.22 = (bf16[1,64,512]{2,1,0:T(8,128)(2,1)S(1)}, bf16[1,64,512]{2,1,0:T(8,128)(2,1)S(1)}, u32[]{:S(2)}, u32[]{:S(2)}) collective-permute-start(bf16[1,64,512]{2,1,0:T(8,128)(2,1)S(1)} %get-tuple-element.119), channel_id=1, source_target_pairs={{0,1},{1,0},{2,3},{3,2},{4,5},{5,4},{6,7},{7,6},{8,9},{9,8},{10,11... | collective-permute-start | bytes 196616 | tf_op jit(solution)/shard_map/ppermute | solution.py:317
